TPU v7x, 32 devices: a whole 2x2x4 slice. The times are simulated.
32 devices in a mesh: tp: 2 (over y), dp: 16 (over z, x, core).
Axes of the slice: x: 2, y: 2, z: 4, core: 2. Of those that a mesh axis runs over, the one named last changes fastest.
Arguments:
- activations: bfloat16 [4, 2048, 8192], P(None, 'dp', 'tp'), may hold values from -6 to 6
- value_weight: bfloat16 [8192, 1024], P('tp'), may hold values from -0.0625 to 0.0625
- shrink_store: bfloat16 [8192, 8192], P('tp', 'dp'), may hold values from -0.0625 to 0.0625
- expand_store: bfloat16 [8192, 1024], P('dp', 'tp'), may hold values from -0.75 to 0.75
- adapter_row: int32 [128], replicated, may hold values from 0 to 127, as said below
- token_adapter: int32 [4, 2048], P(None, 'dp'), may hold values from 0 to 132, as said below
- hot_ids: int32 [4, 4], replicated, may hold values from 0 to 127, as said below
Outputs:
- adapted: bfloat16 [4, 2048, 1024], P(None, 'dp', 'tp')
Inputs may be any that keep to these rules, and one draw needn't show every extreme that they name: `token_adapter`: code 128 + 4 means no adapter. In each step, of the tokens of one device's aligned block of 128, at most 16 name adapters stored by one owner (rows owner * 8 to owner * 8 + 7), and at most 2 do so by a code of 4 or more. `hot_ids`: the 4 adapters of a step are different. `adapter_row`: A permutation of the stored rows.
All inputs are finite; a program needn't handle non-finite values.
Results may differ from a plain program's by a relative error of at most 0.0047.
Values may be sent and summed in bfloat16 or wider, within the bound.
No kernel may reach another device: no remote copies, remote signals or barrier semaphores. Data moves between devices by JAX's collectives and lax.ppermute only.
A program may use at most 128 MiB of HBM per device.

v0:
```python
import jax
import jax.numpy as jnp
from jax import lax
from jax.sharding import PartitionSpec as P

R = 64
CAP = 2


def from_root(block, axis, source):
    block = jnp.where(lax.axis_index(axis) == source, block, jnp.zeros_like(block))
    return lax.psum(block, axis)


def owner_delta(tokens_now, send_mask, owner_dev, local_slot, capacity, shrink_store, expand_store):
    dp_count = lax.axis_size("dp")
    token_count, width_part = tokens_now.shape
    per_dev = expand_store.shape[0] // R
    head_part = expand_store.shape[1]
    owner_hits = (
        (owner_dev[:, None] == jnp.arange(dp_count)[None, :]) & send_mask[:, None]
    ).astype(jnp.int32)
    running = jnp.cumsum(owner_hits, axis=0) - 1
    slot_index = jnp.sum(jnp.where(owner_hits > 0, running, 0), axis=1)
    target = jnp.where(send_mask, owner_dev * capacity + slot_index, dp_count * capacity)
    rows_out = (
        jnp.zeros((dp_count * capacity, width_part), jnp.bfloat16)
        .at[target]
        .set(tokens_now, mode="drop")
    )
    rows_out = rows_out.reshape(dp_count, capacity, width_part)
    tag_rows = (
        jnp.full((dp_count * capacity,), per_dev, jnp.bfloat16)
        .at[target]
        .set(local_slot.astype(jnp.bfloat16), mode="drop")
    )
    tag_rows = tag_rows.reshape(dp_count, capacity)
    rows_in = lax.all_to_all(rows_out, "dp", split_axis=0, concat_axis=0, tiled=True)
    tags_in = lax.all_to_all(tag_rows, "dp", split_axis=0, concat_axis=0, tiled=True)
    item_count = rows_in.shape[1]
    flat_rows = rows_in.reshape(-1, width_part)
    row_count = flat_rows.shape[0]
    chooser = (
        tags_in.reshape(-1)[:, None] == jnp.arange(per_dev).astype(jnp.bfloat16)[None, :]
    ).astype(jnp.float32)
    partial_value = jnp.dot(flat_rows, shrink_store, preferred_element_type=jnp.float32).reshape(
        row_count, per_dev, R
    )
    z_part = jnp.einsum("mar,ma->mr", partial_value, chooser)
    z_rows = lax.psum(z_part, "tp").astype(jnp.bfloat16)
    spread = (chooser.astype(jnp.bfloat16)[:, :, None] * z_rows[:, None, :]).reshape(
        row_count, per_dev * R
    )
    answer = jnp.dot(spread, expand_store, preferred_element_type=jnp.float32).astype(jnp.bfloat16)
    answers = answer.reshape(dp_count, item_count, head_part)
    returned = lax.all_to_all(answers, "dp", split_axis=0, concat_axis=0, tiled=True).reshape(
        dp_count * capacity, head_part
    )
    gathered = returned[jnp.clip(target, 0, dp_count * capacity - 1)]
    return jnp.where(send_mask[:, None], gathered, jnp.zeros_like(gathered))


def hot_delta(tokens_now, is_hot, route_now, hot_now, adapter_row, shrink_store, expand_store):
    token_count, width_part = tokens_now.shape
    per_dev = expand_store.shape[0] // R
    hot_count = hot_now.shape[0]
    pieces_shrink = []
    pieces_expand = []
    for entry in range(hot_count):
        row_here = adapter_row[hot_now[entry]]
        owner_root = row_here // per_dev
        slot_here = row_here % per_dev
        shrink_piece = lax.dynamic_slice_in_dim(shrink_store, slot_here * R, R, 1).reshape(-1, 128)
        expand_piece = lax.dynamic_slice_in_dim(expand_store, slot_here * R, R, 0)
        shrink_got, expand_got = (
            from_root(shrink_piece, "dp", owner_root),
            from_root(expand_piece, "dp", owner_root),
        )
        pieces_shrink.append(shrink_got.reshape(width_part, R))
        pieces_expand.append(expand_got)
    shrink_hot = jnp.concatenate(pieces_shrink, axis=1)
    expand_hot = jnp.concatenate(pieces_expand, axis=0)
    chooser = ((route_now[:, None] == jnp.arange(hot_count)[None, :]) & is_hot[:, None]).astype(
        jnp.float32
    )
    partial_value = jnp.dot(tokens_now, shrink_hot, preferred_element_type=jnp.float32).reshape(
        token_count, hot_count, R
    )
    z_part = jnp.einsum("thr,th->tr", partial_value, chooser)
    z_rows = lax.psum(z_part, "tp").astype(jnp.bfloat16)
    spread = (chooser.astype(jnp.bfloat16)[:, :, None] * z_rows[:, None, :]).reshape(
        token_count, hot_count * R
    )
    return jnp.dot(spread, expand_hot, preferred_element_type=jnp.float32).astype(jnp.bfloat16)


def on_device(
    activations, value_weight, shrink_store, expand_store, adapter_row, token_adapter, hot_ids
):
    step_count = activations.shape[0]
    adapter_count = adapter_row.shape[0]
    hot_count = hot_ids.shape[1]
    per_dev = expand_store.shape[0] // R
    none_code = adapter_count + hot_count
    results = []
    for step in range(step_count):
        tokens_now = activations[step]
        route_now = token_adapter[step]
        hot_now = hot_ids[step]
        is_live = route_now < none_code
        picked = hot_now[jnp.clip(route_now, 0, hot_count - 1)]
        adapter = jnp.clip(
            jnp.where(route_now < hot_count, picked, route_now - hot_count), 0, adapter_count - 1
        )
        store_row = adapter_row[adapter]
        owner_dev = store_row // per_dev
        local_slot = store_row % per_dev
        base_part = lax.psum_scatter(
            jnp.dot(tokens_now, value_weight, preferred_element_type=jnp.float32),
            "tp",
            scatter_dimension=1,
            tiled=True,
        )
        is_hot = is_live & (route_now < hot_count)
        delta_hot = hot_delta(
            tokens_now, is_hot, route_now, hot_now, adapter_row, shrink_store, expand_store
        )
        delta_cold = owner_delta(
            tokens_now,
            is_live & jnp.logical_not(is_hot),
            owner_dev,
            local_slot,
            CAP,
            shrink_store,
            expand_store,
        )
        delta_rows = delta_hot + delta_cold
        delta_rows = lax.optimization_barrier(delta_rows)
        results.append((base_part + delta_rows.astype(jnp.float32)).astype(jnp.bfloat16))
    return jnp.stack(results)


def solution(mesh):
    placed = (
        P(None, "dp", "tp"),
        P("tp", None),
        P("tp", "dp"),
        P("dp", "tp"),
        P(),
        P(None, "dp"),
        P(),
    )
    return jax.shard_map(
        on_device, mesh=mesh, in_specs=placed, out_specs=P(None, "dp", "tp"), check_vma=False
    )
```

profile of v0, /device:TPU:0, one launch (start us, length us, event | category | flops | bytes accessed | tf_op | source)
XLA Modules:
  0.0 595.6 jit_solution(5157469115122608343)
XLA Ops:
  7.4 1.9 fusion.188
  38.5 2.0 fusion.189
  81.2 2.0 dynamic-slice_select_fusion.31
  83.2 8.3 %dynamic-slice_select_fusion.15 = (bf16[4096,64]{1,0:T(8,128)(2,1)}, bf16[4096,64]{1,0:T(8,128)(2,1)}, bf16[4096,64]{1,0:T(8,128)(2,1)}, bf16[4096,64]{1,0:T(8,1...) fusion(bf16[4096,512]{1,0:T(8,128)(2,1)} %param.9, ...), kind=kLoop, calls=%fused_computation.95 | loop fusion | flops 2359296 | bytes 9437229 | tf_op jit(solution)/shard_map/jit(_where)/select_n | solution.py:11
  92.3 5.7 dynamic-slice_select_fusion.14
  98.1 5.8 fusion.54
  103.9 6.4 %fusion.49 = f32[128,1024]{1,0:T(8,128)} fusion(bf16[4096,1024]{1,0:T(8,128)(2,1)} %param.8, bf16[4,128,4096]{2,1,0:T(8,128)(2,1)} %param.7), kind=kOutput, calls=%fused_computation.73 | convolution fusion | flops 1073741824 | bytes 9961472 | tf_op jit(solution)/shard_map/dot_general | solution.py:119
  110.6 6.1 %fusion.44 = f32[128,1024]{1,0:T(8,128)} fusion(bf16[4096,1024]{1,0:T(8,128)(2,1)} %param.8, bf16[4,128,4096]{2,1,0:T(8,128)(2,1)} %param.7), kind=kOutput, calls=%fused_computation.68 | convolution fusion | flops 1073741824 | bytes 9961472 | tf_op jit(solution)/shard_map/dot_general | solution.py:119
  116.8 7.3 %fusion.152 = (s32[128]{0:T(128)S(1)}, s32[128]{0:T(128)S(1)}, s32[128]{0:T(128)S(1)}) fusion(s32[]{:T(128)} %bitcast.8, s32[]{:T(128)} %bitcast.6, s32[]{:T(128)} %bitcast.2, s32[]{:T(128)} %bitcast.4, s32[4,128]{1,0:T(4,128)S(1)} %copy-done.4, s32[]{:T(128)} %bitcast.30, s32[]{:T(128)} %bitcast.32, s32[]{:T(128)} %bitcast.34, s32[]{:T(128)} %bitcast.36, ...), kind=kLoop, calls=%fused_computation.333 | loop fusion | flops 6528 | bytes 3120 | tf_op jit(solution)/shard_map/select_n | solution.py:115
  124.1 2.5 fusion.161
  135.5 7.7 %all-to-all-start = ((bf16[16,1,2]{2,1,0:T(2,128)(2,1)}), bf16[16,1,2]{2,1,0:T(2,128)(2,1)S(1)}, u32[]{:S(2)}, u32[]{:S(2)}) async-start(bf16[16,1,2]{2,1,0:T(2,128)(2,1)} %all_to_all.64), calls=%async_computation.1 | async-start | bytes 16384 | tf_op jit(solution)/shard_map/all_to_all | solution.py:39
  143.3 6.0 %fusion.39 = f32[128,1024]{1,0:T(8,128)} fusion(bf16[4096,1024]{1,0:T(8,128)(2,1)} %param.8, bf16[4,128,4096]{2,1,0:T(8,128)(2,1)} %param.7), kind=kOutput, calls=%fused_computation.63 | convolution fusion | flops 1073741824 | bytes 9961472 | tf_op jit(solution)/shard_map/dot_general | solution.py:119
  151.5 6.0 %all-to-all-start.3 = ((bf16[16,1,2]{2,1,0:T(2,128)(2,1)}), bf16[16,1,2]{2,1,0:T(2,128)(2,1)S(1)}, u32[]{:S(2)}, u32[]{:S(2)}) async-start(bf16[16,1,2]{2,1,0:T(2,128)(2,1)} %all_to_all.65), calls=%async_computation.5 | async-start | bytes 16384 | tf_op jit(solution)/shard_map/all_to_all | solution.py:39
  159.6 4.5 all-to-all-done.3
  164.1 3.5 all-to-all-start.6
  169.6 4.4 all-to-all-done.6
  174.0 3.5 all-to-all-start.9
  177.5 2.7 scatter_custom_fusion.1
  181.1 3.0 all-to-all-done.9
  184.0 3.7 all-to-all-start.1
  187.8 6.5 %copy.10 = bf16[4096,512]{0,1:T(8,128)(2,1)} copy(bf16[4096,512]{1,0:T(8,128)(2,1)} %param.9) | data formatting | bytes 8388608 | tf_op args[2]
  194.3 2.7 scatter_custom_fusion.3
  196.9 2.7 scatter_custom_fusion.5
  199.6 2.7 scatter_custom_fusion.7
  205.6 6.1 %all-to-all-start.4 = ((bf16[16,2,4096]{2,1,0:T(2,128)(2,1)}), bf16[16,2,4096]{2,1,0:T(2,128)(2,1)S(1)}, u32[]{:S(2)}, u32[]{:S(2)}) async-start(bf16[16,2,4096]{2,1,0:T(2,128)(2,1)} %reshape.1378), calls=%async_computation.6 | async-start | bytes 524288 | tf_op jit(solution)/shard_map/all_to_all | solution.py:38
  211.9 4.2 fusion.190
  216.3 10.1 %all-to-all-done.4 = bf16[16,2,4096]{2,1,0:T(2,128)(2,1)S(1)} async-done(((bf16[16,2,4096]{2,1,0:T(2,128)(2,1)}), bf16[16,2,4096]{2,1,0:T(2,128)(2,1)S(1)}, u32[]{:S(2)}, u32[]{:S(2)}) %all-to-all-start.4) | async-done | bytes 262176 | tf_op jit(solution)/shard_map/all_to_all | solution.py:38
  226.5 3.5 all-to-all-start.7
  230.1 4.3 fusion.191
  234.6 6.5 %all-to-all-done.7 = bf16[16,2,4096]{2,1,0:T(2,128)(2,1)S(1)} async-done(((bf16[16,2,4096]{2,1,0:T(2,128)(2,1)}), bf16[16,2,4096]{2,1,0:T(2,128)(2,1)S(1)}, u32[]{:S(2)}, u32[]{:S(2)}) %all-to-all-start.7) | async-done | bytes 262176 | tf_op jit(solution)/shard_map/all_to_all | solution.py:38
  241.1 4.2 all-to-all-start.10
  245.4 4.4 fusion.192
  250.0 9.5 %all-to-all-done.10 = bf16[16,2,4096]{2,1,0:T(2,128)(2,1)S(1)} async-done(((bf16[16,2,4096]{2,1,0:T(2,128)(2,1)}), bf16[16,2,4096]{2,1,0:T(2,128)(2,1)S(1)}, u32[]{:S(2)}, u32[]{:S(2)}) %all-to-all-start.10) | async-done | bytes 262176 | tf_op jit(solution)/shard_map/all_to_all | solution.py:38
  259.7 4.2 fusion.193
  264.1 252.1 %all-reduce.5.cloned.1.call-done = (bf16[4096,64]{1,0:T(8,128)(2,1)}, bf16[4096,64]{1,0:T(8,128)(2,1)}, bf16[4096,64]{1,0:T(8,128)(2,1)}, bf16[4096,64]{1,0:T(8,...) async-done(((bf16[4096,64]{1,0:T(8,128)(2,1)}, ...) | async-done | bytes 9437200 | tf_op jit(solution)/shard_map/psum | solution.py:12
  516.3 4.5 fusion
  521.2 2.0 fusion.8
  523.4 2.0 fusion.16
  525.6 2.0 fusion.24
  527.6 11.6 %all-reduce.6 = (bf16[128,64]{0,1:T(8,128)(2,1)S(1)}, bf16[32,64]{1,0:T(8,128)(2,1)S(1)}, bf16[128,64]{0,1:T(8,128)(2,1)S(1)}, bf16[32,64]{1,0:T(8,128)(2,1)S(1)...) all-reduce(f32[128,64]{0,1:T(8,128)S(1)} %multiply_reduce_fusion, ...), channel_id=1, replica_groups=mesh['tp'=2,'dp'=16] {'tp'}, use_global_device_ids=true, to_apply=%region_50.51 | all-reduce | flops 40960 | bytes 245760 | tf_op jit(solution)/shard_map/psum | solution.py:90
  540.3 3.9 all-to-all-start.2
  546.2 4.7 all-to-all-done.2
  550.9 3.8 all-to-all-start.5
  555.3 5.9 all-to-all-done.5
  561.3 3.5 all-to-all-start.8
  567.2 4.2 all-to-all-done.8
  571.4 3.5 all-to-all-start.11
  576.5 4.9 all-to-all-done.11
  (189 shorter events, 35.7 us)
Async XLA Ops:
  7.4 508.9 %all-reduce.5.cloned.1.call-start = ((), (), s32[]{:S(2)}) async-start(), calls=%async_computation.20 | async-start | bytes 35651584 | tf_op jit(solution)/shard_map/psum | solution.py:12
  83.2 8.3 %copy-start.3 = (bf16[512,512]{1,0:T(8,128)(2,1)S(1)}, bf16[512,512]{1,0:T(8,128)(2,1)}, u32[]{:S(2)}) copy-start(bf16[512,512]{1,0:T(8,128)(2,1)} %param.10) | copy-start | bytes 1572868
  83.2 9.2 %copy-start.1 = (bf16[4096,512]{1,0:T(8,128)(2,1)S(1)}, bf16[4096,512]{1,0:T(8,128)(2,1)}, u32[]{:S(2)}) copy-start(bf16[4096,512]{1,0:T(8,128)(2,1)} %param.9) | copy-start | bytes 12582916
  98.0 484.6 %reduce-scatter.5.cloned.1.call-start = ((), (), s32[]{:S(2)}) async-start(), calls=%async_computation.16 | async-start | bytes 786432 | tf_op jit(solution)/shard_map/reduce_scatter | solution.py:118
  103.9 479.8 %reduce-scatter.7.cloned.1.call-start = ((), (), s32[]{:S(2)}) async-start(), calls=%async_computation.17 | async-start | bytes 786432 | tf_op jit(solution)/shard_map/reduce_scatter | solution.py:118
  110.4 6.4 %copy-start.4 = (s32[4,128]{1,0:T(4,128)S(1)}, s32[4,128]{1,0:T(4,128)}, u32[]{:S(2)}) copy-start(s32[4,128]{1,0:T(4,128)} %param.12) | copy-start | bytes 6148
  110.4 16.2 %copy-start = (s32[128]{0:T(128)S(1)}, s32[128]{0:T(128)}, u32[]{:S(2)}) copy-start(s32[128]{0:T(128)} %param.11) | copy-start | bytes 1540
  110.4 474.3 %reduce-scatter.9.cloned.1.call-start = ((), (), s32[]{:S(2)}) async-start(), calls=%async_computation.18 | async-start | bytes 786432 | tf_op jit(solution)/shard_map/reduce_scatter | solution.py:118
  135.5 16.0 %all-to-all-start = ((bf16[16,1,2]{2,1,0:T(2,128)(2,1)}), bf16[16,1,2]{2,1,0:T(2,128)(2,1)S(1)}, u32[]{:S(2)}, u32[]{:S(2)}) async-start(bf16[16,1,2]{2,1,0:T(2,128)(2,1)} %all_to_all.64), calls=%async_computation.1 | async-start | bytes 16384 | tf_op jit(solution)/shard_map/all_to_all | solution.py:39
  143.2 442.5 %reduce-scatter.11.cloned.1.call-start = ((), (), s32[]{:S(2)}) async-start(), calls=%async_computation.19 | async-start | bytes 786432 | tf_op jit(solution)/shard_map/reduce_scatter | solution.py:118
  151.5 12.6 %all-to-all-start.3 = ((bf16[16,1,2]{2,1,0:T(2,128)(2,1)}), bf16[16,1,2]{2,1,0:T(2,128)(2,1)S(1)}, u32[]{:S(2)}, u32[]{:S(2)}) async-start(bf16[16,1,2]{2,1,0:T(2,128)(2,1)} %all_to_all.65), calls=%async_computation.5 | async-start | bytes 16384 | tf_op jit(solution)/shard_map/all_to_all | solution.py:39
  164.1 9.9 %all-to-all-start.6 = ((bf16[16,1,2]{2,1,0:T(2,128)(2,1)}), bf16[16,1,2]{2,1,0:T(2,128)(2,1)S(1)}, u32[]{:S(2)}, u32[]{:S(2)}) async-start(bf16[16,1,2]{2,1,0:T(2,128)(2,1)} %all_to_all.66), calls=%async_computation.9 | async-start | bytes 16384 | tf_op jit(solution)/shard_map/all_to_all | solution.py:39
  174.0 10.0 %all-to-all-start.9 = ((bf16[16,1,2]{2,1,0:T(2,128)(2,1)}), bf16[16,1,2]{2,1,0:T(2,128)(2,1)S(1)}, u32[]{:S(2)}, u32[]{:S(2)}) async-start(bf16[16,1,2]{2,1,0:T(2,128)(2,1)} %all_to_all.67), calls=%async_computation.13 | async-start | bytes 16384 | tf_op jit(solution)/shard_map/all_to_all | solution.py:39
  184.0 21.6 %all-to-all-start.1 = ((bf16[16,2,4096]{2,1,0:T(2,128)(2,1)}), bf16[16,2,4096]{2,1,0:T(2,128)(2,1)S(1)}, u32[]{:S(2)}, u32[]{:S(2)}) async-start(bf16[16,2,4096]{2,1,0:T(2,128)(2,1)} %reshape.1369), calls=%async_computation.2 | async-start | bytes 524288 | tf_op jit(solution)/shard_map/all_to_all | solution.py:38
  205.6 20.8 %all-to-all-start.4 = ((bf16[16,2,4096]{2,1,0:T(2,128)(2,1)}), bf16[16,2,4096]{2,1,0:T(2,128)(2,1)S(1)}, u32[]{:S(2)}, u32[]{:S(2)}) async-start(bf16[16,2,4096]{2,1,0:T(2,128)(2,1)} %reshape.1378), calls=%async_computation.6 | async-start | bytes 524288 | tf_op jit(solution)/shard_map/all_to_all | solution.py:38
  226.5 14.6 %all-to-all-start.7 = ((bf16[16,2,4096]{2,1,0:T(2,128)(2,1)}), bf16[16,2,4096]{2,1,0:T(2,128)(2,1)S(1)}, u32[]{:S(2)}, u32[]{:S(2)}) async-start(bf16[16,2,4096]{2,1,0:T(2,128)(2,1)} %reshape.1387), calls=%async_computation.10 | async-start | bytes 524288 | tf_op jit(solution)/shard_map/all_to_all | solution.py:38
  241.1 18.5 %all-to-all-start.10 = ((bf16[16,2,4096]{2,1,0:T(2,128)(2,1)}), bf16[16,2,4096]{2,1,0:T(2,128)(2,1)S(1)}, u32[]{:S(2)}, u32[]{:S(2)}) async-start(bf16[16,2,4096]{2,1,0:T(2,128)(2,1)} %reshape.1396), calls=%async_computation.14 | async-start | bytes 524288 | tf_op jit(solution)/shard_map/all_to_all | solution.py:38
  516.2 4.6 copy-start.2
  516.3 4.6 copy-start.13
  516.3 4.6 copy-start.14
  516.3 4.7 copy-start.15
  516.3 5.0 copy-start.16
  521.2 2.1 copy-start.10
  521.2 2.1 copy-start.11
  521.2 2.2 copy-start.12
  523.4 2.1 copy-start.6
  523.4 2.1 copy-start.7
  523.4 2.2 copy-start.8
  527.6 48.2 %copy-start.29 = (bf16[64,512]{1,0:T(8,128)(2,1)S(1)}, bf16[64,512]{1,0:T(8,128)(2,1)}, u32[]{:S(2)}) copy-start(bf16[64,512]{1,0:T(8,128)(2,1)} %get-tuple-element.41) | copy-start | bytes 196612
  527.6 48.2 %copy-start.30 = (bf16[64,512]{1,0:T(8,128)(2,1)S(1)}, bf16[64,512]{1,0:T(8,128)(2,1)}, u32[]{:S(2)}) copy-start(bf16[64,512]{1,0:T(8,128)(2,1)} %get-tuple-element.42) | copy-start | bytes 196612
  527.6 48.2 %copy-start.31 = (bf16[64,512]{1,0:T(8,128)(2,1)S(1)}, bf16[64,512]{1,0:T(8,128)(2,1)}, u32[]{:S(2)}) copy-start(bf16[64,512]{1,0:T(8,128)(2,1)} %get-tuple-element.43) | copy-start | bytes 196612
  527.6 48.2 %copy-start.32 = (bf16[64,512]{1,0:T(8,128)(2,1)S(1)}, bf16[64,512]{1,0:T(8,128)(2,1)}, u32[]{:S(2)}) copy-start(bf16[64,512]{1,0:T(8,128)(2,1)} %get-tuple-element.44) | copy-start | bytes 196612
  539.7 36.3 %copy-start.25 = (bf16[64,512]{1,0:T(8,128)(2,1)S(1)}, bf16[64,512]{1,0:T(8,128)(2,1)}, u32[]{:S(2)}) copy-start(bf16[64,512]{1,0:T(8,128)(2,1)} %get-tuple-element.37) | copy-start | bytes 196612
  539.7 36.4 %copy-start.26 = (bf16[64,512]{1,0:T(8,128)(2,1)S(1)}, bf16[64,512]{1,0:T(8,128)(2,1)}, u32[]{:S(2)}) copy-start(bf16[64,512]{1,0:T(8,128)(2,1)} %get-tuple-element.38) | copy-start | bytes 196612
  539.7 36.3 %copy-start.27 = (bf16[64,512]{1,0:T(8,128)(2,1)S(1)}, bf16[64,512]{1,0:T(8,128)(2,1)}, u32[]{:S(2)}) copy-start(bf16[64,512]{1,0:T(8,128)(2,1)} %get-tuple-element.39) | copy-start | bytes 196612
  539.7 36.3 %copy-start.28 = (bf16[64,512]{1,0:T(8,128)(2,1)S(1)}, bf16[64,512]{1,0:T(8,128)(2,1)}, u32[]{:S(2)}) copy-start(bf16[64,512]{1,0:T(8,128)(2,1)} %get-tuple-element.40) | copy-start | bytes 196612
  540.3 10.5 %all-to-all-start.2 = ((bf16[16,2,512]{2,1,0:T(2,128)(2,1)}), bf16[16,2,512]{2,1,0:T(2,128)(2,1)S(1)}, u32[]{:S(2)}, u32[]{:S(2)}) async-start(bf16[16,2,512]{2,1,0:T(2,128)(2,1)} %reshape.1371), calls=%async_computation.3 | async-start | bytes 65536 | tf_op jit(solution)/shard_map/all_to_all | solution.py:56
  544.8 31.5 %copy-start.21 = (bf16[64,512]{1,0:T(8,128)(2,1)S(1)}, bf16[64,512]{1,0:T(8,128)(2,1)}, u32[]{:S(2)}) copy-start(bf16[64,512]{1,0:T(8,128)(2,1)} %get-tuple-element.33) | copy-start | bytes 196612
  544.8 31.5 %copy-start.22 = (bf16[64,512]{1,0:T(8,128)(2,1)S(1)}, bf16[64,512]{1,0:T(8,128)(2,1)}, u32[]{:S(2)}) copy-start(bf16[64,512]{1,0:T(8,128)(2,1)} %get-tuple-element.34) | copy-start | bytes 196612
  544.8 31.5 %copy-start.23 = (bf16[64,512]{1,0:T(8,128)(2,1)S(1)}, bf16[64,512]{1,0:T(8,128)(2,1)}, u32[]{:S(2)}) copy-start(bf16[64,512]{1,0:T(8,128)(2,1)} %get-tuple-element.35) | copy-start | bytes 196612
  544.8 31.5 %copy-start.24 = (bf16[64,512]{1,0:T(8,128)(2,1)S(1)}, bf16[64,512]{1,0:T(8,128)(2,1)}, u32[]{:S(2)}) copy-start(bf16[64,512]{1,0:T(8,128)(2,1)} %get-tuple-element.36) | copy-start | bytes 196612
  550.9 10.4 %all-to-all-start.5 = ((bf16[16,2,512]{2,1,0:T(2,128)(2,1)}), bf16[16,2,512]{2,1,0:T(2,128)(2,1)S(1)}, u32[]{:S(2)}, u32[]{:S(2)}) async-start(bf16[16,2,512]{2,1,0:T(2,128)(2,1)} %reshape.1380), calls=%async_computation.7 | async-start | bytes 65536 | tf_op jit(solution)/shard_map/all_to_all | solution.py:56
  561.3 10.1 %all-to-all-start.8 = ((bf16[16,2,512]{2,1,0:T(2,128)(2,1)}), bf16[16,2,512]{2,1,0:T(2,128)(2,1)S(1)}, u32[]{:S(2)}, u32[]{:S(2)}) async-start(bf16[16,2,512]{2,1,0:T(2,128)(2,1)} %reshape.1389), calls=%async_computation.11 | async-start | bytes 65536 | tf_op jit(solution)/shard_map/all_to_all | solution.py:56
  565.4 16.9 %copy-start.17 = (bf16[64,512]{1,0:T(8,128)(2,1)S(1)}, bf16[64,512]{1,0:T(8,128)(2,1)}, u32[]{:S(2)}) copy-start(bf16[64,512]{1,0:T(8,128)(2,1)} %get-tuple-element.29) | copy-start | bytes 196612
  565.5 16.9 %copy-start.18 = (bf16[64,512]{1,0:T(8,128)(2,1)S(1)}, bf16[64,512]{1,0:T(8,128)(2,1)}, u32[]{:S(2)}) copy-start(bf16[64,512]{1,0:T(8,128)(2,1)} %get-tuple-element.30) | copy-start | bytes 196612
  565.5 16.9 %copy-start.19 = (bf16[64,512]{1,0:T(8,128)(2,1)S(1)}, bf16[64,512]{1,0:T(8,128)(2,1)}, u32[]{:S(2)}) copy-start(bf16[64,512]{1,0:T(8,128)(2,1)} %get-tuple-element.31) | copy-start | bytes 196612
  565.5 16.9 %copy-start.20 = (bf16[64,512]{1,0:T(8,128)(2,1)S(1)}, bf16[64,512]{1,0:T(8,128)(2,1)}, u32[]{:S(2)}) copy-start(bf16[64,512]{1,0:T(8,128)(2,1)} %get-tuple-element.32) | copy-start | bytes 196612
  571.4 10.1 %all-to-all-start.11 = ((bf16[16,2,512]{2,1,0:T(2,128)(2,1)}), bf16[16,2,512]{2,1,0:T(2,128)(2,1)S(1)}, u32[]{:S(2)}, u32[]{:S(2)}) async-start(bf16[16,2,512]{2,1,0:T(2,128)(2,1)} %reshape.1398), calls=%async_computation.15 | async-start | bytes 65536 | tf_op jit(solution)/shard_map/all_to_all | solution.py:56
  (2 other events, 4.1 us)
Sparse Core Ops, SparseCore 0:
  98.2 418.0 all-reduce.4
Sparse Core Ops, SparseCore 1:
  103.9 17.2 reduce-scatter.4
  123.4 14.5 reduce-scatter.6
  140.0 14.5 reduce-scatter.8
  156.9 14.5 reduce-scatter.10
where the time goes:
time: 605 us; the launch traced here: 596 us
  waiting for transfers between devices  310 us (51%)
  between operations  86.5 us (14%)
  matrix products  54.3 us (9%)
  starting transfers between devices  53.3 us (9%)
  local copies, waits for them, and re-layouts  45.7 us (8%)
  other arithmetic  34.1 us (6%)
  blocking collectives  11.6 us (2%)
    psum x1, waiting for transfers between devices, from_root(): return lax.psum(block, axis)  252 us
    all_to_all x4, waiting for transfers between devices, owner_delta(): lax.all_to_all(rows_out, 'dp', split_axis=0, concat_axis=0, tiled=True)  26.1 us
    dot_general x4, matrix products, on_device(): jnp.dot(tokens_now, value_weight, preferred_element_type=jnp.float32)  24.3 us
    all_to_all x4, starting transfers between devices, owner_delta(): lax.all_to_all(tag_rows, 'dp', split_axis=0, concat_axis=0, tiled=True)  20.6 us
    all_to_all x4, waiting for transfers between devices, owner_delta(): lax.all_to_all(answers, 'dp', split_axis=0, concat_axis=0, tiled=True)  19.7 us
    all_to_all x4, starting transfers between devices, owner_delta(): lax.all_to_all(rows_out, 'dp', split_axis=0, concat_axis=0, tiled=True)  17.7 us
    dot_general x4, matrix products, owner_delta(): jnp.dot(flat_rows, shrink_store, preferred_element_type=jnp.float32)  17.2 us
    select_n x4, other arithmetic, from_root(): jnp.where(lax.axis_index(axis) == source, block, jnp.zeros_like(block))  16.8 us
  transfers between devices with their start and end apart: 17, of which 11 were waited for; matrix products, arithmetic and copies ran while one was open for 18% of the time, Pallas kernels for 0%

commit v1 on v0

v1 whole, which is shorter than its diff:
```python
import jax
import jax.numpy as jnp
from jax import lax
from jax.sharding import Mesh, PartitionSpec as P

R = 64
CAP = 2
HCAP = 16
DP = ("z", "x", "core")
LAYER = ("x", "core")


def pick(flags):
    return flags.astype(jnp.bfloat16)


def matmul(a, b):
    return jnp.dot(a, b, preferred_element_type=jnp.float32)


def sum_over_tp(part):
    if lax.axis_size("tp") == 2:
        return part + lax.ppermute(part, "tp", [(0, 1), (1, 0)])
    return lax.psum(part, "tp")


def line_stages(n):
    half = n // 2
    stages = [([(k, k + 1), (n - 1 - k, n - 2 - k)], None) for k in range(half - 1)]
    stages.append(([(half - 1, half), (half, half - 1)], None))
    stages += [([(k + 1, k), (n - 2 - k, n - 1 - k)], k) for k in reversed(range(half - 1))]
    return stages


def hot_factors(store, selector, step_count):
    x_at, core_at, z_at = lax.axis_index("x"), lax.axis_index("core"), lax.axis_index("z")
    depth, width = store.shape
    quarter = depth // 4
    cols = selector.shape[1] // step_count
    halves = store.reshape(2, 2, quarter, width)
    other = lax.dynamic_index_in_dim(halves, 1 - core_at, 1, keepdims=False).reshape(2 * quarter, width)
    mine = lax.dynamic_index_in_dim(halves, core_at, 1, keepdims=False).reshape(2 * quarter, width)
    swap = [(0, 1), (1, 0)]
    z_count = lax.axis_size("z")
    stages = line_stages(z_count)
    stage_count = 2 + len(stages)
    picked = [selector[:, s * cols:(s + 1) * cols] for s in range(step_count)]
    sends = [matmul(other, p).astype(jnp.bfloat16) for p in picked]
    keeps = [matmul(mine, p).astype(jnp.bfloat16) for p in picked]
    held = [None] * step_count
    for wave in range(step_count + stage_count - 1):
        active = [s for s in range(step_count) if 0 <= wave - s < stage_count]
        got = []
        for s in active:
            stage = wave - s
            if stage == 0:
                got.append(lax.ppermute(sends[s], "core", swap))
            elif stage == 1:
                got.append(lax.ppermute(sends[s], "x", swap))
            else:
                got.append(lax.ppermute(held[s], "z", stages[stage - 2][0]))
        nxt = wave + 1
        if nxt < step_count:
            *got, sends[nxt] = lax.optimization_barrier((*got, sends[nxt]))
        else:
            got = lax.optimization_barrier(tuple(got))
        for s, piece in zip(active, got):
            stage = wave - s
            if stage == 0:
                total = (keeps[s] + piece).reshape(2, quarter, cols)
                sends[s] = lax.dynamic_index_in_dim(total, 1 - x_at, 0, keepdims=False)
                held[s] = lax.dynamic_index_in_dim(total, x_at, 0, keepdims=False)
            elif stage == 1 or stages[stage - 2][1] is None:
                held[s] = held[s] + piece
            else:
                k = stages[stage - 2][1]
                held[s] = jnp.where((z_at == k) | (z_at == z_count - 1 - k), piece, held[s])
    return held


def on_device(
    activations, value_weight, shrink_store, expand_store, adapter_row, token_adapter, hot_ids
):
    step_count, token_count, depth = activations.shape
    adapter_count = adapter_row.shape[0]
    hot_count = hot_ids.shape[1]
    per_dev = expand_store.shape[0] // R
    head_part = expand_store.shape[1]
    dp_count = lax.axis_size("z") * lax.axis_size("x") * lax.axis_size("core")
    layer_count = 4
    tp_count = lax.axis_size("tp")
    me = lax.axis_index(DP)
    none_code = adapter_count + hot_count
    tokens_all = step_count * token_count
    rows = activations.reshape(tokens_all, depth)

    names = jnp.arange(adapter_count, dtype=jnp.int32)
    hot_row = jnp.sum(jnp.where(hot_ids[:, :, None] == names, adapter_row, 0), axis=-1)
    hot_first = jnp.where(hot_row // per_dev == me, (hot_row % per_dev) * R, -R * per_dev)
    cold_row = jnp.sum(jnp.where((token_adapter - hot_count)[:, :, None] == names, adapter_row, 0), axis=-1)
    is_hot = token_adapter < hot_count
    is_cold = (token_adapter < none_code) & jnp.logical_not(is_hot)
    owner = cold_row // per_dev
    group = jnp.where(is_hot, token_adapter, jnp.where(is_cold, hot_count + owner, -1))
    at = jnp.arange(token_count, dtype=jnp.int32)
    before = (group[:, :, None] == group[:, None, :]) & (at[None, :] < at[:, None])
    rank = jnp.sum(before.astype(jnp.int32), axis=-1)
    step_at = jnp.arange(step_count, dtype=jnp.int32)[:, None]
    hot_rows = step_count * hot_count * HCAP
    cold_rows = dp_count * step_count * CAP
    hot_target = (step_at * hot_count + token_adapter) * HCAP + rank
    cold_target = (owner * step_count + step_at) * CAP + rank
    hot_target = jnp.where(is_hot, hot_target, -1).reshape(-1)
    cold_target = jnp.where(is_cold, cold_target, -1).reshape(-1)
    place_hot = pick(jnp.arange(hot_rows, dtype=jnp.int32)[:, None] == hot_target)
    cold_hit = jnp.arange(cold_rows, dtype=jnp.int32)[:, None] == cold_target
    place_cold = pick(cold_hit)
    tag = jnp.sum(jnp.where(cold_hit, (cold_row % per_dev + 1).reshape(-1), 0), axis=-1)

    column = jnp.arange(per_dev * R, dtype=jnp.int32)
    lane = jnp.arange(R, dtype=jnp.int32)
    wanted = (hot_first.reshape(-1)[:, None] + lane).reshape(-1)
    shrink_hot = hot_factors(shrink_store, pick(column[:, None] == wanted), step_count)
    expand_hot = lax.psum(
        matmul(pick(wanted[:, None] == column), expand_store).astype(jnp.bfloat16), DP
    )

    rows_out = matmul(place_cold, rows).astype(jnp.bfloat16)
    tag_out = jnp.broadcast_to(tag.astype(jnp.bfloat16)[:, None], (cold_rows, 128))
    packet = jnp.concatenate([rows_out, tag_out], axis=1).reshape(dp_count, step_count * CAP, depth + 128)
    packet = lax.all_to_all(packet, DP, split_axis=0, concat_axis=0, tiled=True)
    packet = packet.reshape(cold_rows, depth + 128)
    tag_in = packet[:, depth:depth + 1].astype(jnp.int32)
    chosen = (column // R + 1)[None, :] == tag_in
    z_cold = sum_over_tp(jnp.where(chosen, matmul(packet[:, :depth], shrink_store), 0.0))
    delta_cold = matmul(z_cold.astype(jnp.bfloat16), expand_store).astype(jnp.bfloat16)
    delta_cold = lax.all_to_all(
        delta_cold.reshape(dp_count, step_count * CAP, head_part), DP, split_axis=0, concat_axis=0, tiled=True
    ).reshape(cold_rows, head_part)

    quarter = depth // layer_count
    hot_out = jnp.stack(
        [matmul(place_hot, rows[:, q * quarter:(q + 1) * quarter]).astype(jnp.bfloat16) for q in range(layer_count)]
    )
    hot_in = lax.all_to_all(hot_out, LAYER, split_axis=0, concat_axis=0, tiled=True)
    hot_in = hot_in.reshape(layer_count, step_count, hot_count * HCAP, quarter)
    pairs = hot_count // 2
    low = (jnp.arange(2 * R) < R)[None, None, :]
    z_parts = []
    for s in range(step_count):
        dense = matmul(hot_in[:, s].reshape(-1, quarter), shrink_hot[s])
        dense = dense.reshape(layer_count, pairs, 2, HCAP, pairs, 2 * R)
        z_parts.append(
            jnp.stack(
                [jnp.where(low, dense[:, p, 0, :, p], dense[:, p, 1, :, p]) for p in range(pairs)], axis=1
            )
        )
    z_part = jnp.stack(z_parts, axis=1).reshape(layer_count, step_count * pairs * HCAP, 2 * R)
    z_part = jnp.broadcast_to(z_part[None], (tp_count, *z_part.shape)).reshape(-1, *z_part.shape[1:])
    z_hot = lax.all_to_all(z_part, ("tp", *LAYER), split_axis=0, concat_axis=0, tiled=True)
    z_hot = jnp.sum(z_hot, axis=0).astype(jnp.bfloat16)
    groups = step_count * pairs
    spread = jnp.where(
        (jnp.arange(groups)[:, None, None, None, None] == jnp.arange(groups)[:, None])
        & (jnp.arange(2)[:, None, None, None] == (jnp.arange(2 * R) // R)),
        z_hot.reshape(groups, 1, HCAP, 1, 2 * R),
        jnp.zeros((), jnp.bfloat16),
    ).reshape(hot_rows, groups * 2 * R)
    delta_hot = matmul(spread, expand_hot).astype(jnp.bfloat16)

    base = lax.psum_scatter(matmul(rows, value_weight), "tp", scatter_dimension=1, tiled=True)
    place = jnp.concatenate([place_hot, place_cold], axis=0)
    delta = lax.dot_general(
        place,
        jnp.concatenate([delta_hot, delta_cold], axis=0),
        (((0,), (0,)), ((), ())),
        preferred_element_type=jnp.float32,
    )
    return (base + delta).astype(jnp.bfloat16).reshape(step_count, token_count, head_part)


def solution(mesh):
    tp_count, dp_count = mesh.shape["tp"], mesh.shape["dp"]
    fine = Mesh(mesh.devices.reshape(tp_count, dp_count // 4, 2, 2), ("tp", *DP))
    placed = (
        P(None, DP, "tp"),
        P("tp", None),
        P("tp", DP),
        P(DP, "tp"),
        P(),
        P(None, DP),
        P(),
    )
    return jax.shard_map(
        on_device, mesh=fine, in_specs=placed, out_specs=P(None, DP, "tp"), check_vma=False
    )
```

time: 605 us -> 257 us (0.42); the launches traced: 596 us -> 255 us
  waiting for transfers between devices: 310 us -> 95.6 us
  between operations: 86.5 us -> 15.6 us
  local copies, waits for them, and re-layouts: 45.7 us -> 11.2 us
  blocking collectives: 11.6 us -> 0 us
  other arithmetic: 34.1 us -> 26.1 us
    psum x1, waiting for transfers between devices: 252 us -> 0.02 us  [on_device(): lax.psum(matmul(pick(wanted[:, None] == column), expand_store).astype(jnp...]
    ppermute x0 -> x21, waiting for transfers between devices: none -> 81.8 us  [the longest x12 59.1 us: hot_factors(): got.append(lax.ppermute(held[s], 'z', stages[stage - 2][0]))]
    all_to_all x12 -> x4, waiting for transfers between devices: 57.8 us -> 13.8 us  [the longest x1 7.66 us: on_device(): lax.all_to_all(z_part, ('tp', *LAYER), split_axis=0, concat_axis=0, tiled...]
    ppermute x0 -> x21, starting transfers between devices: none -> 41.1 us  [the longest x12 31.7 us: hot_factors(): got.append(lax.ppermute(held[s], 'z', stages[stage - 2][0]))]
    all_to_all x12 -> x4, starting transfers between devices: 53 us -> 16.9 us  [the longest x1 5.99 us: on_device(): packet = lax.all_to_all(packet, DP, split_axis=0, concat_axis=0, tiled=True)]
    select_n x11 -> x5, other arithmetic: 26.6 us -> 0.13 us  [the longest x1 0.06 us: on_device(): jnp.where((jnp.arange(groups)[:, None, None, None, None] == jnp.arange(gr...]
    add x0 -> x19, other arithmetic: none -> 16.8 us  [the longest x12 9.74 us: hot_factors(): held[s] = held[s] + piece]
    scatter x8 -> x0, local copies, waits for them, and re-layouts: 16.1 us -> none  [the longest x4 10.7 us: owner_delta(): rows_out = jnp.zeros((dp_count * capacity, width_part), jnp.bfloat16).at[...]
  transfers between devices with their start and end apart: 17 -> 27, of which waited for: 11 -> 12; matrix products, arithmetic and copies ran while one was open for 18% -> 29% of each run, Pallas kernels for 0% -> 0%
where the time goes in v1:
time: 257 us; the launch traced here: 255 us
  waiting for transfers between devices  95.6 us (37%)
  starting transfers between devices  58.2 us (23%)
  matrix products  48.6 us (19%)
  other arithmetic  26.1 us (10%)
  between operations  15.6 us (6%)
  local copies, waits for them, and re-layouts  11.2 us (4%)
    ppermute x12, waiting for transfers between devices, hot_factors(): got.append(lax.ppermute(held[s], 'z', stages[stage - 2][0]))  59.1 us
    dot_general x22, matrix products, matmul(): return jnp.dot(a, b, preferred_element_type=jnp.float32)  46.1 us
    ppermute x12, starting transfers between devices, hot_factors(): got.append(lax.ppermute(held[s], 'z', stages[stage - 2][0]))  31.7 us
    ppermute x4, waiting for transfers between devices, hot_factors(): got.append(lax.ppermute(sends[s], 'x', swap))  22.8 us
    add x12, other arithmetic, hot_factors(): held[s] = held[s] + piece  9.74 us
    all_to_all x1, waiting for transfers between devices, on_device(): lax.all_to_all(z_part, ('tp', *LAYER), split_axis=0, concat_axis=0, tiled...  7.66 us
    add x4, other arithmetic, hot_factors(): total = (keeps[s] + piece).reshape(2, quarter, cols)  6.94 us
    ppermute x4, starting transfers between devices, hot_factors(): got.append(lax.ppermute(sends[s], 'x', swap))  6.75 us
  transfers between devices with their start and end apart: 27, of which 12 were waited for; matrix products, arithmetic and copies ran while one was open for 29% of the time, Pallas kernels for 0%

profile of v1, /device:TPU:0, one launch (start us, length us, event | category | flops | bytes accessed | tf_op | source)
XLA Modules:
  0.0 255.3 jit_solution(12082705997971993256)
XLA Ops:
  8.9 4.1 %constant_dynamic-slice_fusion = (bf16[2,1,1024,512]{3,2,1,0:T(8,128)(2,1)S(1)}, bf16[2,1,1024,512]{3,2,1,0:T(8,128)(2,1)}) fusion(bf16[2,2,1024,512]{3,2,1,0:T(8,128)(2,1)} %bitcast.196, s32[]{:T(128)S(6)} %select_n.229, s32[]{:T(128)S(6)} %select_n.224), kind=kLoop, calls=%fused_computation.129 | loop fusion | bytes 8388616 | tf_op jit(solution)/shard_map/jit(dynamic_index_in_dim)/dynamic_slice | solution.py:41
  13.0 1.8 convolution_convert_fusion.7
  17.7 1.6 pad_maximum_fusion
  19.4 3.9 %all-to-all-start = ((bf16[4,256,1024]{2,1,0:T(8,128)(2,1)}), bf16[4,256,1024]{2,1,0:T(8,128)(2,1)S(1)}, u32[]{:S(2)}, u32[]{:S(2)}) async-start(bf16[4,256,1024]{2,1,0:T(8,128)(2,1)} %pad_maximum_fusion), calls=%async_computation.1 | async-start | bytes 4194304 | tf_op jit(solution)/shard_map/all_to_all | solution.py:145
  23.2 1.7 fusion.1
  25.2 10.5 %fusion.61 = f32[512,1024]{1,0:T(8,128)} fusion(bf16[512,4096]{1,0:T(8,128)(2,1)} %bitcast.200, bf16[4096,1024]{1,0:T(8,128)(2,1)} %param.8), kind=kOutput, calls=%fused_computation.163 | convolution fusion | flops 4294967296 | bytes 14680064 | tf_op jit(solution)/shard_map/dot_general | solution.py:18
  35.7 3.5 %convolution_convert_fusion.6 = bf16[2048,256]{1,0:T(8,128)(2,1)} fusion(bf16[2048,512]{1,0:T(8,128)(2,1)} %bitcast.217, pred[512,1024]{1,0:T(32,128)(4,1)S(1)} %iota_compare_fusion.1), kind=kOutput, calls=%fused_computation.6 | convolution fusion | flops 537395200 | bytes 3276800 | tf_op jit(solution)/shard_map/dot_general | solution.py:18
  39.3 1.7 convolution_convert_fusion.5
  41.0 1.8 convolution_convert_fusion.8
  43.3 1.7 convolution_convert_fusion.4
  45.0 3.5 %convolution_convert_fusion.3 = bf16[2048,256]{1,0:T(8,128)(2,1)} fusion(bf16[2048,512]{1,0:T(8,128)(2,1)} %bitcast.218, pred[512,1024]{1,0:T(32,128)(4,1)S(1)} %iota_compare_fusion.1), kind=kOutput, calls=%fused_computation.3 | convolution fusion | flops 537395200 | bytes 3276800 | tf_op jit(solution)/shard_map/dot_general | solution.py:18
  48.5 1.7 add.198
  50.2 2.4 collective-permute-start.1
  52.6 1.7 convolution_convert_fusion
  54.3 10.3 %collective-permute-done.1 = bf16[1024,256]{1,0:T(8,128)(2,1)S(1)} collective-permute-done((bf16[1024,256]{1,0:T(8,128)(2,1)S(1)}, bf16[1024,256]{1,0:T(8,128)(2,1)S(1)}, u32[]{:S(2)}, u32[]{:S(2)}) %collective-permute-start.1) | collective-permute-done | bytes 524320 | tf_op jit(solution)/shard_map/ppermute | solution.py:59
  65.6 1.9 add.202
  67.6 2.1 collective-permute-start.4
  69.7 4.6 %collective-permute-start.3 = (bf16[1024,256]{1,0:T(8,128)(2,1)S(1)}, bf16[1024,256]{1,0:T(8,128)(2,1)S(1)}, u32[]{:S(2)}, u32[]{:S(2)}) collective-permute-start(bf16[1024,256]{1,0:T(8,128)(2,1)S(1)} %bitcast_add_fusion.3), channel_id=1, source_target_pairs={{0,4},{12,8},{1,5},{13,9},{2,6},{14,10},{3,7},{15,11},{16,20},{28,... | collective-permute-start | bytes 1572872 | tf_op jit(solution)/shard_map/ppermute | solution.py:61
  75.5 6.8 %collective-permute-done.4 = bf16[1024,256]{1,0:T(8,128)(2,1)S(1)} collective-permute-done((bf16[1024,256]{1,0:T(8,128)(2,1)S(1)}, bf16[1024,256]{1,0:T(8,128)(2,1)S(1)}, u32[]{:S(2)}, u32[]{:S(2)}) %collective-permute-start.4) | collective-permute-done | bytes 524320 | tf_op jit(solution)/shard_map/ppermute | solution.py:59
  82.3 4.4 %collective-permute-done.3 = bf16[1024,256]{1,0:T(8,128)(2,1)S(1)} collective-permute-done((bf16[1024,256]{1,0:T(8,128)(2,1)S(1)}, bf16[1024,256]{1,0:T(8,128)(2,1)S(1)}, u32[]{:S(2)}, u32[]{:S(2)}) %collective-permute-start.3) | collective-permute-done | bytes 524320 | tf_op jit(solution)/shard_map/ppermute | solution.py:61
  87.5 2.5 convolution_convert_fusion.2
  90.0 1.8 add.205
  93.4 6.0 %all-to-all-start.2 = ((bf16[16,8,4224]{2,1,0:T(8,128)(2,1)}), bf16[16,8,4224]{2,1,0:T(8,128)(2,1)}, u32[]{:S(2)}, u32[]{:S(2)}) async-start(bf16[16,8,4224]{2,1,0:T(8,128)(2,1)} %maximum_bitcast_fusion), calls=%async_computation.3 | async-start | bytes 2162688 | tf_op jit(solution)/shard_map/all_to_all | solution.py:131
  100.9 3.8 %collective-permute-start.7 = (bf16[1024,256]{1,0:T(8,128)(2,1)S(1)}, bf16[1024,256]{1,0:T(8,128)(2,1)S(1)}, u32[]{:S(2)}, u32[]{:S(2)}) collective-permute-start(bf16[1024,256]{1,0:T(8,128)(2,1)S(1)} %bitcast_add_fusion.2), channel_id=1, source_target_pairs={{0,4},{12,8},{1,5},{13,9},{2,6},{14,10},{3,7},{15,11},{16,20},{28,... | collective-permute-start | bytes 1572872 | tf_op jit(solution)/shard_map/ppermute | solution.py:61
  106.8 1.6 convolution_convert_fusion.1
  108.4 5.6 %collective-permute-done.8 = bf16[1024,256]{1,0:T(8,128)(2,1)} collective-permute-done((bf16[1024,256]{1,0:T(8,128)(2,1)}, bf16[1024,256]{1,0:T(8,128)(2,1)}, u32[]{:S(2)}, u32[]{:S(2)}) %collective-permute-start.8) | collective-permute-done | bytes 524320 | tf_op jit(solution)/shard_map/ppermute | solution.py:59
  114.0 21.3 %collective-permute-done.7 = bf16[1024,256]{1,0:T(8,128)(2,1)S(1)} collective-permute-done((bf16[1024,256]{1,0:T(8,128)(2,1)S(1)}, bf16[1024,256]{1,0:T(8,128)(2,1)S(1)}, u32[]{:S(2)}, u32[]{:S(2)}) %collective-permute-start.7) | collective-permute-done | bytes 524320 | tf_op jit(solution)/shard_map/ppermute | solution.py:61
  135.3 1.5 add.209
  136.9 1.8 collective-permute-start.13
  139.9 11.1 %collective-permute-start.12 = (bf16[1024,256]{1,0:T(8,128)(2,1)S(1)}, bf16[1024,256]{1,0:T(8,128)(2,1)S(1)}, u32[]{:S(2)}, u32[]{:S(2)}) collective-permute-start(bf16[1024,256]{1,0:T(8,128)(2,1)S(1)} %bitcast_add_fusion.1), channel_id=1, source_target_pairs={{0,4},{12,8},{1,5},{13,9},{2,6},{14,10},{3,7},{15,11},{16,20},{28,... | collective-permute-start | bytes 1572872 | tf_op jit(solution)/shard_map/ppermute | solution.py:61
  153.4 8.4 %collective-permute-done.12 = bf16[1024,256]{1,0:T(8,128)(2,1)S(1)} collective-permute-done((bf16[1024,256]{1,0:T(8,128)(2,1)S(1)}, bf16[1024,256]{1,0:T(8,128)(2,1)S(1)}, u32[]{:S(2)}, u32[]{:S(2)}) %collective-permute-start.12) | collective-permute-done | bytes 524320 | tf_op jit(solution)/shard_map/ppermute | solution.py:61
  161.8 5.1 %collective-permute-done.10 = bf16[1024,256]{1,0:T(8,128)(2,1)S(1)} collective-permute-done((bf16[1024,256]{1,0:T(8,128)(2,1)S(1)}, bf16[1024,256]{1,0:T(8,128)(2,1)S(1)}, u32[]{:S(2)}, u32[]{:S(2)}) %collective-permute-start.10) | collective-permute-done | bytes 524320 | tf_op jit(solution)/shard_map/ppermute | solution.py:61
  167.9 2.3 collective-permute-start.16
  170.3 1.5 collective-permute-start.15
  176.3 3.2 %convolution_select_fusion = f32[128,512]{1,0:T(8,128)S(1)} fusion(bf16[4096,512]{1,0:T(8,128)(2,1)} %param.9, bf16[128,4224]{1,0:T(8,128)(2,1)} %bitcast.73, s32[512]{0:T(512)S(1)} %fusion.50, s32[128]{0:T(128)S(1)} %convert_reduce_fusion.1), kind=kOutput, calls=%fused_computation.25 | convolution fusion | flops 537001984 | bytes 5507584 | tf_op jit(solution)/shard_map/dot_general | solution.py:18
  179.6 1.8 collective-permute-start.20
  181.3 5.6 %collective-permute-done.14 = bf16[1024,256]{1,0:T(8,128)(2,1)} collective-permute-done((bf16[1024,256]{1,0:T(8,128)(2,1)}, bf16[1024,256]{1,0:T(8,128)(2,1)}, u32[]{:S(2)}, u32[]{:S(2)}) %collective-permute-start.14) | collective-permute-done | bytes 524320 | tf_op jit(solution)/shard_map/ppermute | solution.py:61
  192.5 2.1 fusion.62
  195.9 7.9 %collective-permute-done.17 = bf16[1024,256]{1,0:T(8,128)(2,1)S(1)} collective-permute-done((bf16[1024,256]{1,0:T(8,128)(2,1)S(1)}, bf16[1024,256]{1,0:T(8,128)(2,1)S(1)}, u32[]{:S(2)}, u32[]{:S(2)}) %collective-permute-start.17) | collective-permute-done | bytes 524320 | tf_op jit(solution)/shard_map/ppermute | solution.py:61
  207.3 2.1 fusion.23
  211.7 6.3 %collective-permute-done.19 = bf16[1024,256]{1,0:T(8,128)(2,1)} collective-permute-done((bf16[1024,256]{1,0:T(8,128)(2,1)S(1)}, bf16[1024,256]{1,0:T(8,128)(2,1)}, u32[]{:S(2)}, u32[]{:S(2)}) %collective-permute-start.19) | collective-permute-done | bytes 524320 | tf_op jit(solution)/shard_map/ppermute | solution.py:61
  220.8 3.5 %all-to-all-start.1 = ((f32[8,128,128]{2,1,0:T(8,128)}), f32[8,128,128]{2,1,0:T(8,128)S(1)}, u32[]{:S(2)}, u32[]{:S(2)}) async-start(f32[8,128,128]{2,1,0:T(8,128)} %bitcast.69), calls=%async_computation.2 | async-start | bytes 1048576 | tf_op jit(solution)/shard_map/all_to_all | solution.py:160
  224.5 1.8 fusion.7
  226.3 7.7 %all-to-all-done.1 = f32[8,128,128]{2,1,0:T(8,128)S(1)} async-done(((f32[8,128,128]{2,1,0:T(8,128)}), f32[8,128,128]{2,1,0:T(8,128)S(1)}, u32[]{:S(2)}, u32[]{:S(2)}) %all-to-all-start.1) | async-done | bytes 524320 | tf_op jit(solution)/shard_map/all_to_all | solution.py:160
  233.9 3.5 %all-to-all-start.3 = ((bf16[16,8,512]{2,1,0:T(8,128)(2,1)}), bf16[16,8,512]{2,1,0:T(8,128)(2,1)S(1)}, u32[]{:S(2)}, u32[]{:S(2)}) async-start(bf16[16,8,512]{2,1,0:T(8,128)(2,1)} %fusion.7), calls=%async_computation.4 | async-start | bytes 262144 | tf_op jit(solution)/shard_map/all_to_all | solution.py:137
  237.6 1.7 convolution_convert_fusion.13
  239.3 6.1 %all-to-all-done.3 = bf16[16,8,512]{2,1,0:T(8,128)(2,1)S(1)} async-done(((bf16[16,8,512]{2,1,0:T(8,128)(2,1)}), bf16[16,8,512]{2,1,0:T(8,128)(2,1)S(1)}, u32[]{:S(2)}, u32[]{:S(2)}) %all-to-all-start.3) | async-done | bytes 131104 | tf_op jit(solution)/shard_map/all_to_all | solution.py:137
  245.4 2.5 fusion.2
  (161 shorter events, 37.9 us)
Async XLA Ops:
  7.4 15.9 %copy-start = (bf16[512,512]{1,0:T(8,128)(2,1)S(1)}, bf16[512,512]{1,0:T(8,128)(2,1)}, u32[]{:S(2)}) copy-start(bf16[512,512]{1,0:T(8,128)(2,1)} %param.10) | copy-start | bytes 1572868
  8.9 36.1 %copy-start.23 = (pred[512,1024]{1,0:T(32,128)(4,1)}, pred[512,1024]{1,0:T(32,128)(4,1)S(1)}, u32[]{:S(2)}) copy-start(pred[512,1024]{1,0:T(32,128)(4,1)S(1)} %iota_compare_fusion.1) | copy-start | bytes 1572868
  8.9 7.0 %copy-start.4 = (bf16[4,128,4096]{2,1,0:T(8,128)(2,1)S(1)}, bf16[4,128,4096]{2,1,0:T(8,128)(2,1)}, u32[]{:S(2)}) copy-start(bf16[4,128,4096]{2,1,0:T(8,128)(2,1)} %param.7) | copy-start | bytes 12582916
  14.8 28.0 %collective-permute-start = (bf16[2048,256]{1,0:T(8,128)(2,1)}, bf16[2048,256]{1,0:T(8,128)(2,1)}, u32[]{:S(2)}, u32[]{:S(2)}) collective-permute-start(bf16[2048,256]{1,0:T(8,128)(2,1)} %convolution_convert_fusion.7), channel_id=1, source_target_pairs={{0,1},{1,0},{2,3},{3,2},{4,5},{5,4},{6,7},{7,6},{8,9},{9,8},{10,11... | collective-permute-start | bytes 3145736 | tf_op jit(solution)/shard_map/ppermute | solution.py:57
  19.4 74.1 %all-to-all-start = ((bf16[4,256,1024]{2,1,0:T(8,128)(2,1)}), bf16[4,256,1024]{2,1,0:T(8,128)(2,1)S(1)}, u32[]{:S(2)}, u32[]{:S(2)}) async-start(bf16[4,256,1024]{2,1,0:T(8,128)(2,1)} %pad_maximum_fusion), calls=%async_computation.1 | async-start | bytes 4194304 | tf_op jit(solution)/shard_map/all_to_all | solution.py:145
  23.2 214.4 %all-reduce.2.cloned.1.call-start = ((), (), s32[]{:S(2)}) async-start(), calls=%async_computation.6 | async-start | bytes 2097152 | tf_op jit(solution)/shard_map/psum | solution.py:124
  25.0 220.4 %reduce-scatter.2.cloned.1.call-start = ((), (), s32[]{:S(2)}) async-start(), calls=%async_computation.5 | async-start | bytes 3145728 | tf_op jit(solution)/shard_map/reduce_scatter | solution.py:171
  42.8 22.7 %collective-permute-start.2 = (bf16[2048,256]{1,0:T(8,128)(2,1)}, bf16[2048,256]{1,0:T(8,128)(2,1)}, u32[]{:S(2)}, u32[]{:S(2)}) collective-permute-start(bf16[2048,256]{1,0:T(8,128)(2,1)} %convolution_convert_fusion.6), channel_id=1, source_target_pairs={{0,1},{1,0},{2,3},{3,2},{4,5},{5,4},{6,7},{7,6},{8,9},{9,8},{10,11... | collective-permute-start | bytes 3145736 | tf_op jit(solution)/shard_map/ppermute | solution.py:57
  48.5 4.1 %copy-start.5 = (bf16[4,128,4096]{2,1,0:T(8,128)(2,1)S(1)}, bf16[4,128,4096]{2,1,0:T(8,128)(2,1)}, u32[]{:S(2)}) copy-start(bf16[4,128,4096]{2,1,0:T(8,128)(2,1)} %param.7) | copy-start | bytes 12582916
  50.1 4.2 %copy-start.1 = (bf16[2048,256]{1,0:T(8,128)(2,1)}, bf16[2048,256]{1,0:T(8,128)(2,1)S(1)}, u32[]{:S(2)}) copy-start(bf16[2048,256]{1,0:T(8,128)(2,1)S(1)} %add.198) | copy-start | bytes 3145732
  50.2 14.4 %collective-permute-start.1 = (bf16[1024,256]{1,0:T(8,128)(2,1)S(1)}, bf16[1024,256]{1,0:T(8,128)(2,1)S(1)}, u32[]{:S(2)}, u32[]{:S(2)}) collective-permute-start(bf16[1024,256]{1,0:T(8,128)(2,1)S(1)} %dynamic-slice_bitcast_fusion.3), channel_id=1, source_target_pairs={{0,2},{2,0},{1,3},{3,1},{4,6},{6,4},{5,7},{7,5},{8,10},{10,8},{9,1... | collective-permute-start | bytes 1572872 | tf_op jit(solution)/shard_map/ppermute | solution.py:59
  65.4 22.0 %collective-permute-start.5 = (bf16[2048,256]{1,0:T(8,128)(2,1)}, bf16[2048,256]{1,0:T(8,128)(2,1)}, u32[]{:S(2)}, u32[]{:S(2)}) collective-permute-start(bf16[2048,256]{1,0:T(8,128)(2,1)} %convolution_convert_fusion.5), channel_id=1, source_target_pairs={{0,1},{1,0},{2,3},{3,2},{4,5},{5,4},{6,7},{7,6},{8,9},{9,8},{10,11... | collective-permute-start | bytes 3145736 | tf_op jit(solution)/shard_map/ppermute | solution.py:57
  65.6 4.1 %copy-start.2 = (bf16[2048,256]{1,0:T(8,128)(2,1)S(1)}, bf16[2048,256]{1,0:T(8,128)(2,1)}, u32[]{:S(2)}) copy-start(bf16[2048,256]{1,0:T(8,128)(2,1)} %copy-done.1) | copy-start | bytes 3145732
  67.5 8.0 %copy-start.6 = (bf16[2048,256]{1,0:T(8,128)(2,1)}, bf16[2048,256]{1,0:T(8,128)(2,1)S(1)}, u32[]{:S(2)}) copy-start(bf16[2048,256]{1,0:T(8,128)(2,1)S(1)} %add.202) | copy-start | bytes 3145732
  67.5 6.9 %copy-start.3 = (bf16[128,4096]{1,0:T(8,128)(2,1)S(1)}, bf16[128,4096]{1,0:T(8,128)(2,1)}, u32[]{:S(2)}) copy-start(bf16[128,4096]{1,0:T(8,128)(2,1)} %convolution_convert_fusion) | copy-start | bytes 3145732
  67.6 19.9 %copy-start.10 = (bf16[2,1,1024,512]{3,2,1,0:T(8,128)(2,1)S(1)}, bf16[2,1,1024,512]{3,2,1,0:T(8,128)(2,1)}, u32[]{:S(2)}) copy-start(bf16[2,1,1024,512]{3,2,1,0:T(8,128)(2,1)} %get-tuple-element.50) | copy-start | bytes 6291460
  67.6 14.7 %collective-permute-start.4 = (bf16[1024,256]{1,0:T(8,128)(2,1)S(1)}, bf16[1024,256]{1,0:T(8,128)(2,1)S(1)}, u32[]{:S(2)}, u32[]{:S(2)}) collective-permute-start(bf16[1024,256]{1,0:T(8,128)(2,1)S(1)} %dynamic-slice_bitcast_fusion.2), channel_id=1, source_target_pairs={{0,2},{2,0},{1,3},{3,1},{4,6},{6,4},{5,7},{7,5},{8,10},{10,8},{9,1... | collective-permute-start | bytes 1572872 | tf_op jit(solution)/shard_map/ppermute | solution.py:59
  69.7 16.9 %collective-permute-start.3 = (bf16[1024,256]{1,0:T(8,128)(2,1)S(1)}, bf16[1024,256]{1,0:T(8,128)(2,1)S(1)}, u32[]{:S(2)}, u32[]{:S(2)}) collective-permute-start(bf16[1024,256]{1,0:T(8,128)(2,1)S(1)} %bitcast_add_fusion.3), channel_id=1, source_target_pairs={{0,4},{12,8},{1,5},{13,9},{2,6},{14,10},{3,7},{15,11},{16,20},{28,... | collective-permute-start | bytes 1572872 | tf_op jit(solution)/shard_map/ppermute | solution.py:61
  82.3 5.2 %copy-start.26 = (bf16[1024,256]{1,0:T(8,128)(2,1)}, bf16[1024,256]{1,0:T(8,128)(2,1)S(1)}, u32[]{:S(2)}) copy-start(bf16[1024,256]{1,0:T(8,128)(2,1)S(1)} %collective-permute-done.4) | copy-start | bytes 1572868
  87.4 47.9 %collective-permute-start.9 = (bf16[2048,256]{1,0:T(8,128)(2,1)}, bf16[2048,256]{1,0:T(8,128)(2,1)}, u32[]{:S(2)}, u32[]{:S(2)}) collective-permute-start(bf16[2048,256]{1,0:T(8,128)(2,1)} %convolution_convert_fusion.3), channel_id=1, source_target_pairs={{0,1},{1,0},{2,3},{3,2},{4,5},{5,4},{6,7},{7,6},{8,9},{9,8},{10,11... | collective-permute-start | bytes 3145736 | tf_op jit(solution)/shard_map/ppermute | solution.py:57
  93.0 21.1 %collective-permute-start.8 = (bf16[1024,256]{1,0:T(8,128)(2,1)}, bf16[1024,256]{1,0:T(8,128)(2,1)}, u32[]{:S(2)}, u32[]{:S(2)}) collective-permute-start(bf16[1024,256]{1,0:T(8,128)(2,1)} %dynamic-slice_bitcast_fusion.1), channel_id=1, source_target_pairs={{0,2},{2,0},{1,3},{3,1},{4,6},{6,4},{5,7},{7,5},{8,10},{10,8},{9,1... | collective-permute-start | bytes 1572872 | tf_op jit(solution)/shard_map/ppermute | solution.py:59
  93.4 82.0 %all-to-all-start.2 = ((bf16[16,8,4224]{2,1,0:T(8,128)(2,1)}), bf16[16,8,4224]{2,1,0:T(8,128)(2,1)}, u32[]{:S(2)}, u32[]{:S(2)}) async-start(bf16[16,8,4224]{2,1,0:T(8,128)(2,1)} %maximum_bitcast_fusion), calls=%async_computation.3 | async-start | bytes 2162688 | tf_op jit(solution)/shard_map/all_to_all | solution.py:131
  99.4 7.4 %copy-start.11 = (bf16[2,1,1024,512]{3,2,1,0:T(8,128)(2,1)S(1)}, bf16[2,1,1024,512]{3,2,1,0:T(8,128)(2,1)}, u32[]{:S(2)}) copy-start(bf16[2,1,1024,512]{3,2,1,0:T(8,128)(2,1)} %get-tuple-element.50) | copy-start | bytes 6291460
  100.9 34.4 %collective-permute-start.7 = (bf16[1024,256]{1,0:T(8,128)(2,1)S(1)}, bf16[1024,256]{1,0:T(8,128)(2,1)S(1)}, u32[]{:S(2)}, u32[]{:S(2)}) collective-permute-start(bf16[1024,256]{1,0:T(8,128)(2,1)S(1)} %bitcast_add_fusion.2), channel_id=1, source_target_pairs={{0,4},{12,8},{1,5},{13,9},{2,6},{14,10},{3,7},{15,11},{16,20},{28,... | collective-permute-start | bytes 1572872 | tf_op jit(solution)/shard_map/ppermute | solution.py:61
  105.9 29.4 %collective-permute-start.6 = (bf16[1024,256]{1,0:T(8,128)(2,1)S(1)}, bf16[1024,256]{1,0:T(8,128)(2,1)S(1)}, u32[]{:S(2)}, u32[]{:S(2)}) collective-permute-start(bf16[1024,256]{1,0:T(8,128)(2,1)S(1)} %add.203), channel_id=1, source_target_pairs={{4,8},{8,4},{5,9},{9,5},{6,10},{10,6},{7,11},{11,7},{20,24},{24,20... | collective-permute-start | bytes 1572872 | tf_op jit(solution)/shard_map/ppermute | solution.py:61
  108.4 30.4 %copy-start.8 = (bf16[2048,256]{1,0:T(8,128)(2,1)S(1)}, bf16[2048,256]{1,0:T(8,128)(2,1)}, u32[]{:S(2)}) copy-start(bf16[2048,256]{1,0:T(8,128)(2,1)} %copy-done.7) | copy-start | bytes 3145732
  136.9 16.4 %collective-permute-start.13 = (bf16[1024,256]{1,0:T(8,128)(2,1)S(1)}, bf16[1024,256]{1,0:T(8,128)(2,1)S(1)}, u32[]{:S(2)}, u32[]{:S(2)}) collective-permute-start(bf16[1024,256]{1,0:T(8,128)(2,1)S(1)} %dynamic-slice_bitcast_fusion), channel_id=1, source_target_pairs={{0,2},{2,0},{1,3},{3,1},{4,6},{6,4},{5,7},{7,5},{8,10},{10,8},{9,1... | collective-permute-start | bytes 1572872 | tf_op jit(solution)/shard_map/ppermute | solution.py:59
  139.9 21.9 %collective-permute-start.12 = (bf16[1024,256]{1,0:T(8,128)(2,1)S(1)}, bf16[1024,256]{1,0:T(8,128)(2,1)S(1)}, u32[]{:S(2)}, u32[]{:S(2)}) collective-permute-start(bf16[1024,256]{1,0:T(8,128)(2,1)S(1)} %bitcast_add_fusion.1), channel_id=1, source_target_pairs={{0,4},{12,8},{1,5},{13,9},{2,6},{14,10},{3,7},{15,11},{16,20},{28,... | collective-permute-start | bytes 1572872 | tf_op jit(solution)/shard_map/ppermute | solution.py:61
  151.1 10.7 %collective-permute-start.11 = (bf16[1024,256]{1,0:T(8,128)(2,1)S(1)}, bf16[1024,256]{1,0:T(8,128)(2,1)S(1)}, u32[]{:S(2)}, u32[]{:S(2)}) collective-permute-start(bf16[1024,256]{1,0:T(8,128)(2,1)S(1)} %add.207), channel_id=1, source_target_pairs={{4,8},{8,4},{5,9},{9,5},{6,10},{10,6},{7,11},{11,7},{20,24},{24,20... | collective-permute-start | bytes 1572872 | tf_op jit(solution)/shard_map/ppermute | solution.py:61
  152.0 20.8 %copy-start.14 = (bf16[1024,256]{1,0:T(8,128)(2,1)}, bf16[1024,256]{1,0:T(8,128)(2,1)S(1)}, u32[]{:S(2)}) copy-start(bf16[1024,256]{1,0:T(8,128)(2,1)S(1)} %add.206) | copy-start | bytes 1572868
  152.0 14.9 %collective-permute-start.10 = (bf16[1024,256]{1,0:T(8,128)(2,1)S(1)}, bf16[1024,256]{1,0:T(8,128)(2,1)S(1)}, u32[]{:S(2)}, u32[]{:S(2)}) collective-permute-start(bf16[1024,256]{1,0:T(8,128)(2,1)S(1)} %add.206), channel_id=1, source_target_pairs={{4,0},{8,12},{5,1},{9,13},{6,2},{10,14},{7,3},{11,15},{20,16},{24,... | collective-permute-start | bytes 1572872 | tf_op jit(solution)/shard_map/ppermute | solution.py:61
  166.9 5.8 %copy-start.24 = (bf16[1024,256]{1,0:T(8,128)(2,1)}, bf16[1024,256]{1,0:T(8,128)(2,1)S(1)}, u32[]{:S(2)}) copy-start(bf16[1024,256]{1,0:T(8,128)(2,1)S(1)} %collective-permute-done.10) | copy-start | bytes 1572868
  167.9 13.5 %collective-permute-start.16 = (bf16[1024,256]{1,0:T(8,128)(2,1)}, bf16[1024,256]{1,0:T(8,128)(2,1)}, u32[]{:S(2)}, u32[]{:S(2)}) collective-permute-start(bf16[1024,256]{1,0:T(8,128)(2,1)} %bitcast_add_fusion), channel_id=1, source_target_pairs={{0,4},{12,8},{1,5},{13,9},{2,6},{14,10},{3,7},{15,11},{16,20},{28,... | collective-permute-start | bytes 1572872 | tf_op jit(solution)/shard_map/ppermute | solution.py:61
  170.3 11.1 %collective-permute-start.15 = (bf16[1024,256]{1,0:T(8,128)(2,1)S(1)}, bf16[1024,256]{1,0:T(8,128)(2,1)}, u32[]{:S(2)}, u32[]{:S(2)}) collective-permute-start(bf16[1024,256]{1,0:T(8,128)(2,1)S(1)} %add.211), channel_id=1, source_target_pairs={{4,8},{8,4},{5,9},{9,5},{6,10},{10,6},{7,11},{11,7},{20,24},{24,20... | collective-permute-start | bytes 1572872 | tf_op jit(solution)/shard_map/ppermute | solution.py:61
  172.7 14.2 %collective-permute-start.14 = (bf16[1024,256]{1,0:T(8,128)(2,1)}, bf16[1024,256]{1,0:T(8,128)(2,1)}, u32[]{:S(2)}, u32[]{:S(2)}) collective-permute-start(bf16[1024,256]{1,0:T(8,128)(2,1)} %add.210), channel_id=1, source_target_pairs={{4,0},{8,12},{5,1},{9,13},{6,2},{10,14},{7,3},{11,15},{20,16},{24,... | collective-permute-start | bytes 1572872 | tf_op jit(solution)/shard_map/ppermute | solution.py:61
  179.5 12.7 %copy-start.15 = (bf16[1024,256]{1,0:T(8,128)(2,1)S(1)}, bf16[1024,256]{1,0:T(8,128)(2,1)}, u32[]{:S(2)}) copy-start(bf16[1024,256]{1,0:T(8,128)(2,1)} %copy-done.14) | copy-start | bytes 1572868
  179.5 12.7 %copy-start.25 = (bf16[1024,256]{1,0:T(8,128)(2,1)S(1)}, bf16[1024,256]{1,0:T(8,128)(2,1)}, u32[]{:S(2)}) copy-start(bf16[1024,256]{1,0:T(8,128)(2,1)} %copy-done.24) | copy-start | bytes 1572868
  179.6 44.9 %collective-permute-start.20 = (f32[128,512]{1,0:T(8,128)S(1)}, f32[128,512]{1,0:T(8,128)}, u32[]{:S(2)}, u32[]{:S(2)}) collective-permute-start(f32[128,512]{1,0:T(8,128)S(1)} %convolution_select_fusion), channel_id=1, source_target_pairs={{0,16},{16,0},{1,17},{17,1},{2,18},{18,2},{3,19},{19,3},{4,20},{20... | collective-permute-start | bytes 786440 | tf_op jit(solution)/shard_map/ppermute | solution.py:23
  188.2 7.7 %collective-permute-start.18 = (bf16[1024,256]{1,0:T(8,128)(2,1)S(1)}, bf16[1024,256]{1,0:T(8,128)(2,1)}, u32[]{:S(2)}, u32[]{:S(2)}) collective-permute-start(bf16[1024,256]{1,0:T(8,128)(2,1)S(1)} %add.214), channel_id=1, source_target_pairs={{4,8},{8,4},{5,9},{9,5},{6,10},{10,6},{7,11},{11,7},{20,24},{24,20... | collective-permute-start | bytes 1572872 | tf_op jit(solution)/shard_map/ppermute | solution.py:61
  190.9 12.9 %collective-permute-start.17 = (bf16[1024,256]{1,0:T(8,128)(2,1)S(1)}, bf16[1024,256]{1,0:T(8,128)(2,1)S(1)}, u32[]{:S(2)}, u32[]{:S(2)}) collective-permute-start(bf16[1024,256]{1,0:T(8,128)(2,1)S(1)} %add.213), channel_id=1, source_target_pairs={{4,0},{8,12},{5,1},{9,13},{6,2},{10,14},{7,3},{11,15},{20,16},{24,... | collective-permute-start | bytes 1572872 | tf_op jit(solution)/shard_map/ppermute | solution.py:61
  205.8 4.9 %copy-start.17 = (bf16[4,1,64,1024]{3,2,1,0:T(8,128)(2,1)S(1)}, bf16[4,1,64,1024]{3,2,1,0:T(8,128)(2,1)}, u32[]{:S(2)}) copy-start(bf16[4,1,64,1024]{3,2,1,0:T(8,128)(2,1)} %get-tuple-element.53) | copy-start | bytes 1572868
  205.8 12.3 %collective-permute-start.19 = (bf16[1024,256]{1,0:T(8,128)(2,1)S(1)}, bf16[1024,256]{1,0:T(8,128)(2,1)}, u32[]{:S(2)}, u32[]{:S(2)}) collective-permute-start(bf16[1024,256]{1,0:T(8,128)(2,1)S(1)} %add.215), channel_id=1, source_target_pairs={{4,0},{8,12},{5,1},{9,13},{6,2},{10,14},{7,3},{11,15},{20,16},{24,... | collective-permute-start | bytes 1572872 | tf_op jit(solution)/shard_map/ppermute | solution.py:61
  210.7 8.7 %copy-start.16 = (bf16[4,1,64,1024]{3,2,1,0:T(8,128)(2,1)S(1)}, bf16[4,1,64,1024]{3,2,1,0:T(8,128)(2,1)}, u32[]{:S(2)}) copy-start(bf16[4,1,64,1024]{3,2,1,0:T(8,128)(2,1)} %get-tuple-element.52) | copy-start | bytes 1572868
  211.7 8.0 %copy-start.19 = (f32[4,2,2,16,2,128]{5,3,4,2,1,0:T(8,128)S(1)}, f32[4,2,2,16,2,128]{5,3,4,2,1,0:T(8,128)}, u32[]{:S(2)}) copy-start(f32[4,2,2,16,2,128]{5,3,4,2,1,0:T(8,128)} %fusion.62) | copy-start | bytes 786436
  211.7 8.0 %copy-start.20 = (f32[4,2,2,16,2,128]{5,3,0,4,2,1:T(8,128)S(1)}, f32[4,2,2,16,2,128]{5,3,0,4,2,1:T(8,128)}, u32[]{:S(2)}) copy-start(f32[4,2,2,16,2,128]{5,3,0,4,2,1:T(8,128)} %fusion.23) | copy-start | bytes 786436
  211.7 8.1 %copy-start.21 = (f32[4,2,2,16,2,128]{5,3,0,4,2,1:T(8,128)S(1)}, f32[4,2,2,16,2,128]{5,3,0,4,2,1:T(8,128)}, u32[]{:S(2)}) copy-start(f32[4,2,2,16,2,128]{5,3,0,4,2,1:T(8,128)} %fusion.21) | copy-start | bytes 786436
  220.8 13.2 %all-to-all-start.1 = ((f32[8,128,128]{2,1,0:T(8,128)}), f32[8,128,128]{2,1,0:T(8,128)S(1)}, u32[]{:S(2)}, u32[]{:S(2)}) async-start(f32[8,128,128]{2,1,0:T(8,128)} %bitcast.69), calls=%async_computation.2 | async-start | bytes 1048576 | tf_op jit(solution)/shard_map/all_to_all | solution.py:160
  233.9 11.4 %all-to-all-start.3 = ((bf16[16,8,512]{2,1,0:T(8,128)(2,1)}), bf16[16,8,512]{2,1,0:T(8,128)(2,1)S(1)}, u32[]{:S(2)}, u32[]{:S(2)}) async-start(bf16[16,8,512]{2,1,0:T(8,128)(2,1)} %fusion.7), calls=%async_computation.4 | async-start | bytes 262144 | tf_op jit(solution)/shard_map/all_to_all | solution.py:137
  (11 other events, 24.3 us)
Sparse Core Ops, SparseCore 0:
  27.9 105.8 all-reduce.1
Sparse Core Ops, SparseCore 1:
  35.8 34.2 reduce-scatter.1

commit v2 on v1

v2 whole, which is shorter than its diff:
```python
import jax
import jax.numpy as jnp
from jax import lax
from jax.sharding import Mesh, PartitionSpec as P

R = 64
CAP = 2
HCAP = 16
DP = ("z", "x", "core")
LAYER = ("x", "core")
SWAP = [(0, 1), (1, 0)]


def pick(flags):
    return flags.astype(jnp.bfloat16)


def matmul(a, b):
    return jnp.dot(a, b, preferred_element_type=jnp.float32)


def narrow(a, b):
    return matmul(a, b).astype(jnp.bfloat16)


def sum_over_tp(part):
    if lax.axis_size("tp") == 2:
        return part + lax.ppermute(part, "tp", SWAP)
    return lax.psum(part, "tp")


def after(value, *others):
    return lax.optimization_barrier((value, *others))[0]


def line_sum(held):
    n, z_at = lax.axis_size("z"), lax.axis_index("z")
    half = n // 2
    for k in range(half - 1):
        held = held + lax.ppermute(held, "z", [(k, k + 1), (n - 1 - k, n - 2 - k)])
    held = held + lax.ppermute(held, "z", [(half - 1, half), (half, half - 1)])
    pieces = [held]
    for k in reversed(range(half - 1)):
        got = lax.ppermute(held, "z", [(k + 1, k), (n - 2 - k, n - 1 - k)])
        here = (z_at == k) | (z_at == n - 1 - k)
        if k > 0:
            held = jnp.where(here, got, held)
        else:
            pieces = [jnp.where(here, jnp.zeros_like(held), held), got]
    return pieces


def on_device(
    activations, value_weight, shrink_store, expand_store, adapter_row, token_adapter, hot_ids
):
    step_count, token_count, depth = activations.shape
    adapter_count = adapter_row.shape[0]
    hot_count = hot_ids.shape[1]
    per_dev = expand_store.shape[0] // R
    head_part = expand_store.shape[1]
    dp_count = lax.axis_size("z") * lax.axis_size("x") * lax.axis_size("core")
    me = lax.axis_index(DP)
    x_at, core_at = lax.axis_index("x"), lax.axis_index("core")
    none_code = adapter_count + hot_count
    rows = activations.reshape(step_count * token_count, depth)

    names = jnp.arange(adapter_count, dtype=jnp.int32)
    hot_row = jnp.sum(jnp.where(hot_ids[:, :, None] == names, adapter_row, 0), axis=-1)
    hot_first = jnp.where(hot_row // per_dev == me, (hot_row % per_dev) * R, -R * per_dev)
    column = jnp.arange(per_dev * R, dtype=jnp.int32)
    lane = jnp.arange(R, dtype=jnp.int32)
    entry = jnp.arange(hot_count, dtype=jnp.int32)

    def wanted(core):
        order = [2 * x_at + core, 2 * (1 - x_at) + core]
        first = [jnp.sum(jnp.where(entry == e, hot_first, 0), axis=1) for e in order]
        return jnp.concatenate([(f[:, None] + lane).reshape(-1) for f in first])

    want_mine, want_other = wanted(core_at), wanted(1 - core_at)
    kept = step_count * R
    chunk_count = 4
    part = depth // chunk_count

    def gathered(other, mine, cut, previous):
        got = lax.ppermute(other, "core", SWAP)
        send = cut(mine, True) + cut(got, True)
        if previous is not None:
            send = after(send, previous)
        crossed = lax.ppermute(send, "x", SWAP)
        return line_sum(cut(mine) + cut(got) + crossed), send, crossed

    def cut_columns(block, last=False):
        return block[:, kept:] if last else block[:, :kept]

    def cut_rows(block, last=False):
        return block[kept:] if last else block[:kept]

    pick_mine, pick_other = lax.optimization_barrier(
        (pick(column[:, None] == want_mine), pick(column[:, None] == want_other))
    )
    shrink_hot, sent, over_x = [], [], []
    for c in range(chunk_count):
        store = shrink_store[c * part:(c + 1) * part]
        if c > 0:
            step_before = sent[0] if c == 1 else over_x[c - 2]
            pick_mine, pick_other = after(pick_mine, step_before), after(pick_other, step_before)
        pieces, send, crossed = gathered(
            narrow(store, pick_other), narrow(store, pick_mine), cut_columns, over_x[-1] if over_x else None
        )
        shrink_hot.append(pieces)
        sent.append(send)
        over_x.append(crossed)
    want_mine, want_other = after(want_mine, over_x[-2]), after(want_other, over_x[-2])
    expand_hot, _, _ = gathered(
        narrow(pick(want_other[:, None] == column), expand_store),
        narrow(pick(want_mine[:, None] == column), expand_store),
        cut_rows,
        over_x[-1],
    )
    expand_hot = sum(expand_hot[1:], expand_hot[0])

    token_adapter = after(token_adapter, sent[0])
    cold_row = jnp.sum(jnp.where((token_adapter - hot_count)[:, :, None] == names, adapter_row, 0), axis=-1)
    is_hot = token_adapter < hot_count
    is_cold = (token_adapter < none_code) & jnp.logical_not(is_hot)
    owner = cold_row // per_dev
    group = jnp.where(is_hot, token_adapter, jnp.where(is_cold, hot_count + owner, -1))
    at = jnp.arange(token_count, dtype=jnp.int32)
    before = (group[:, :, None] == group[:, None, :]) & (at[None, :] < at[:, None])
    rank = jnp.sum(before.astype(jnp.int32), axis=-1)
    step_at = jnp.arange(step_count, dtype=jnp.int32)[:, None]
    hot_rows = hot_count * step_count * HCAP
    cold_rows = dp_count * step_count * CAP
    hot_target = (token_adapter * step_count + step_at) * HCAP + rank
    cold_target = (owner * step_count + step_at) * CAP + rank
    hot_target = jnp.where(is_hot, hot_target, -1).reshape(-1)
    cold_target = jnp.where(is_cold, cold_target, -1).reshape(-1)
    place_hot = pick(jnp.arange(hot_rows, dtype=jnp.int32)[:, None] == hot_target)
    cold_hit = jnp.arange(cold_rows, dtype=jnp.int32)[:, None] == cold_target
    place_cold = pick(cold_hit)
    tag = jnp.sum(jnp.where(cold_hit, (cold_row % per_dev + 1).reshape(-1), 0), axis=-1)

    tag_out = jnp.broadcast_to(tag.astype(jnp.bfloat16)[:, None], (cold_rows, 128))
    packet = jnp.concatenate([narrow(place_cold, rows), tag_out], axis=1)
    packet = packet.reshape(dp_count, step_count * CAP, depth + 128)
    packet = lax.all_to_all(packet, DP, split_axis=0, concat_axis=0, tiled=True)
    packet = packet.reshape(cold_rows, depth + 128)
    tag_in = packet[:, depth:depth + 1].astype(jnp.int32)
    chosen = (column // R + 1)[None, :] == tag_in
    z_cold = sum_over_tp(jnp.where(chosen, matmul(packet[:, :depth], shrink_store), 0.0))
    delta_cold = narrow(z_cold.astype(jnp.bfloat16), expand_store)
    delta_cold = lax.all_to_all(
        delta_cold.reshape(dp_count, step_count * CAP, head_part), DP, split_axis=0, concat_axis=0, tiled=True
    ).reshape(cold_rows, head_part)

    base = lax.psum_scatter(
        matmul(rows, after(value_weight, over_x[0])), "tp", scatter_dimension=1, tiled=True
    )

    hot_out = after(narrow(after(place_hot, over_x[1]), rows), over_x[-1])
    hot_out = hot_out.reshape(hot_count, step_count * HCAP, depth)
    hot_in = lax.all_to_all(hot_out, LAYER, split_axis=0, concat_axis=0, tiled=True).reshape(hot_rows, depth)
    dense = None
    for c, pieces in enumerate(shrink_hot):
        for piece in pieces:
            product = matmul(hot_in[:, c * part:(c + 1) * part], piece)
            dense = product if dense is None else dense + product
    pairs = step_count // 2
    dense = dense.reshape(hot_count, pairs, 2, HCAP, pairs, 2 * R)
    low = (jnp.arange(2 * R) < R)[None, None, :]
    z_part = jnp.stack([jnp.where(low, dense[:, p, 0, :, p], dense[:, p, 1, :, p]) for p in range(pairs)], axis=1)
    z_part = after(z_part.reshape(hot_rows // 2, 2 * R), delta_cold)
    z_hot = sum_over_tp(z_part).astype(jnp.bfloat16)
    same_pair = jnp.arange(pairs)[:, None, None, None, None] == jnp.arange(pairs)[:, None]
    same_half = jnp.arange(2)[:, None, None, None] == jnp.arange(2 * R) // R
    spread = jnp.where(
        same_pair & same_half,
        z_hot.reshape(hot_count, pairs, 1, HCAP, 1, 2 * R),
        jnp.zeros((), jnp.bfloat16),
    ).reshape(hot_rows, kept)
    delta_hot = narrow(spread, expand_hot).reshape(hot_count, step_count * HCAP, head_part)
    delta_hot = lax.all_to_all(delta_hot, LAYER, split_axis=0, concat_axis=0, tiled=True)

    delta = lax.dot_general(
        jnp.concatenate([place_hot, place_cold], axis=0),
        jnp.concatenate([delta_hot.reshape(hot_rows, head_part), delta_cold], axis=0),
        (((0,), (0,)), ((), ())),
        preferred_element_type=jnp.float32,
    )
    return (base + delta).astype(jnp.bfloat16).reshape(step_count, token_count, head_part)


def solution(mesh):
    tp_count, dp_count = mesh.shape["tp"], mesh.shape["dp"]
    fine = Mesh(mesh.devices.reshape(tp_count, dp_count // 4, 2, 2), ("tp", *DP))
    placed = (
        P(None, DP, "tp"),
        P("tp", None),
        P("tp", DP),
        P(DP, "tp"),
        P(),
        P(None, DP),
        P(),
    )
    return jax.shard_map(
        on_device, mesh=fine, in_specs=placed, out_specs=P(None, DP, "tp"), check_vma=False
    )
```

time: 257 us -> 221 us (0.86)
  waiting for transfers between devices: 95.6 us -> 61.3 us
  starting transfers between devices: 58.2 us -> 72 us
  matrix products: 48.6 us -> 39.6 us
  local copies, waits for them, and re-layouts: 11.2 us -> 4.78 us
    ppermute x21 -> x27, waiting for transfers between devices: 81.8 us -> 55.3 us  [the longest x5 30.9 us: line_sum(): got = lax.ppermute(held, 'z', [(k + 1, k), (n - 2 - k, n - 1 - k)])]
    ppermute x21 -> x27, starting transfers between devices: 41.1 us -> 50.7 us  [the longest x5 26.9 us: line_sum(): held = held + lax.ppermute(held, 'z', [(k, k + 1), (n - 1 - k, n - 2 - k)])]
    dot_general x22 -> x24, matrix products: 46.1 us -> 39.1 us  [matmul(): return jnp.dot(a, b, preferred_element_type=jnp.float32)]
    all_to_all x1, waiting for transfers between devices: 6.1 us -> 0.01 us  [on_device(): lax.all_to_all(delta_cold.reshape(dp_count, step_count * CAP, head_part),...]
    all_to_all x1, starting transfers between devices: 3.51 us -> 9.28 us  [on_device(): lax.all_to_all(delta_cold.reshape(dp_count, step_count * CAP, head_part),...]
    add x17 -> x22, other arithmetic: 16.8 us -> 21.9 us  [the longest x5 7.87 us: gathered(): return (line_sum(cut(mine) + cut(got) + crossed), send, crossed)]
    dynamic_slice x1 -> x0, local copies, waits for them, and re-layouts: 4.07 us -> none  [hot_factors(): lax.dynamic_index_in_dim(halves, 1 - core_at, 1, keepdims=False)]
    dot_general x4 -> x0, other arithmetic: 3.35 us -> none  [matmul(): return jnp.dot(a, b, preferred_element_type=jnp.float32)]
  transfers between devices with their start and end apart: 27 -> 32, of which waited for: 12 -> 12; matrix products, arithmetic and copies ran while one was open for 29% -> 28% of each run, Pallas kernels for 0% -> 0%
where the time goes in v2:
time: 221 us; the launch traced here: 220 us
  starting transfers between devices  72 us (33%)
  waiting for transfers between devices  61.3 us (28%)
  matrix products  39.6 us (18%)
  other arithmetic  27.7 us (13%)
  between operations  14.3 us (6%)
  local copies, waits for them, and re-layouts  4.78 us (2%)
    dot_general x24, matrix products, matmul(): return jnp.dot(a, b, preferred_element_type=jnp.float32)  39.1 us
    ppermute x5, waiting for transfers between devices, line_sum(): got = lax.ppermute(held, 'z', [(k + 1, k), (n - 2 - k, n - 1 - k)])  30.9 us
    ppermute x5, starting transfers between devices, line_sum(): held = held + lax.ppermute(held, 'z', [(k, k + 1), (n - 1 - k, n - 2 - k)])  26.9 us
    ppermute x5, waiting for transfers between devices, gathered(): crossed = lax.ppermute(send, 'x', SWAP)  20.1 us
    all_to_all x1, starting transfers between devices, on_device(): lax.all_to_all(delta_cold.reshape(dp_count, step_count * CAP, head_part),...  9.28 us
    ppermute x5, starting transfers between devices, gathered(): crossed = lax.ppermute(send, 'x', SWAP)  9.07 us
    add x5, other arithmetic, gathered(): return (line_sum(cut(mine) + cut(got) + crossed), send, crossed)  7.87 us
    ppermute x5, starting transfers between devices, line_sum(): got = lax.ppermute(held, 'z', [(k + 1, k), (n - 2 - k, n - 1 - k)])  6.41 us
  transfers between devices with their start and end apart: 32, of which 12 were waited for; matrix products, arithmetic and copies ran while one was open for 28% of the time, Pallas kernels for 0%

profile of v2, /device:TPU:0, one launch (start us, length us, event | category | flops | bytes accessed | tf_op | source)
XLA Modules:
  0.0 219.6 jit_solution(4418091545847375836)
XLA Ops:
  9.4 2.0 fusion.1
  12.0 2.1 fusion
  14.6 2.9 %collective-permute-start.1 = (bf16[1024,256]{0,1:T(8,128)(2,1)S(1)}, bf16[1024,256]{0,1:T(8,128)(2,1)}, u32[]{:S(2)}, u32[]{:S(2)}) collective-permute-start(bf16[1024,256]{0,1:T(8,128)(2,1)S(1)} %slice_add_fusion.7), channel_id=1, source_target_pairs={{0,2},{2,0},{1,3},{3,1},{4,6},{6,4},{5,7},{7,5},{8,10},{10,8},{9,1... | collective-permute-start | bytes 1572872 | tf_op jit(solution)/shard_map/ppermute | solution.py:89
  19.9 5.0 %all-to-all-start.1 = ((bf16[16,8,4224]{2,1,0:T(8,128)(2,1)}), bf16[16,8,4224]{2,1,0:T(8,128)(2,1)S(1)}, u32[]{:S(2)}, u32[]{:S(2)}) async-start(bf16[16,8,4224]{2,1,0:T(8,128)(2,1)} %maximum_bitcast_fusion), calls=%async_computation.2 | async-start | bytes 2162688 | tf_op jit(solution)/shard_map/all_to_all | solution.py:146
  24.9 2.2 %fusion.3 = bf16[1024,512]{0,1:T(8,128)(2,1)S(1)} fusion(bf16[512,512]{1,0:T(8,128)(2,1)} %copy-done.20, bf16[4096,512]{1,0:T(8,128)(2,1)} %param.9), kind=kOutput, calls=%fused_computation.14 | convolution fusion | flops 537395200 | bytes 2621440 | tf_op jit(solution)/shard_map/dot_general | solution.py:19
  27.7 2.0 fusion.2
  29.8 2.6 %collective-permute-done.1 = bf16[1024,256]{0,1:T(8,128)(2,1)} collective-permute-done((bf16[1024,256]{0,1:T(8,128)(2,1)S(1)}, bf16[1024,256]{0,1:T(8,128)(2,1)}, u32[]{:S(2)}, u32[]{:S(2)}) %collective-permute-start.1) | collective-permute-done | bytes 524320 | tf_op jit(solution)/shard_map/ppermute | solution.py:89
  33.5 3.4 %collective-permute-start.8 = (bf16[1024,256]{0,1:T(8,128)(2,1)S(1)}, bf16[1024,256]{0,1:T(8,128)(2,1)}, u32[]{:S(2)}, u32[]{:S(2)}) collective-permute-start(bf16[1024,256]{0,1:T(8,128)(2,1)S(1)} %fusion.29), channel_id=1, source_target_pairs={{0,4},{12,8},{1,5},{13,9},{2,6},{14,10},{3,7},{15,11},{16,20},{28,... | collective-permute-start | bytes 1572872 | tf_op jit(solution)/shard_map/ppermute | solution.py:40
  37.0 3.0 %fusion.7 = bf16[1024,512]{0,1:T(8,128)(2,1)} fusion(bf16[512,512]{1,0:T(8,128)(2,1)S(1)} %copy-done.21, bf16[4096,512]{1,0:T(8,128)(2,1)} %param.9), kind=kOutput, calls=%fused_computation.18 | convolution fusion | flops 537395200 | bytes 2621440 | tf_op jit(solution)/shard_map/dot_general | solution.py:19
  41.9 2.6 %collective-permute-start.3 = (bf16[1024,256]{0,1:T(8,128)(2,1)}, bf16[1024,256]{0,1:T(8,128)(2,1)}, u32[]{:S(2)}, u32[]{:S(2)}) collective-permute-start(bf16[1024,256]{0,1:T(8,128)(2,1)} %slice_add_fusion.6), channel_id=1, source_target_pairs={{0,2},{2,0},{1,3},{3,1},{4,6},{6,4},{5,7},{7,5},{8,10},{10,8},{9,1... | collective-permute-start | bytes 1572872 | tf_op jit(solution)/shard_map/ppermute | solution.py:89
  44.5 8.4 %convolution_bitcast_fusion = f32[512,1024]{0,1:T(8,128)} fusion(bf16[4096,1024]{1,0:T(8,128)(2,1)} %param.8, bf16[512,4096]{1,0:T(8,128)(2,1)S(1)} %bitcast.89), kind=kOutput, calls=%fused_computation.2 | convolution fusion | flops 4294967296 | bytes 14680064 | tf_op jit(solution)/shard_map/dot_general | solution.py:19
  53.0 2.1 fusion.6
  56.4 1.6 collective-permute-start.9
  58.0 2.0 collective-permute-done.3
  60.0 1.8 fusion.5
  64.8 2.3 %fusion.28 = bf16[1024,256]{0,1:T(8,128)(2,1)} fusion(bf16[1024,256]{0,1:T(8,128)(2,1)} %collective-permute-done.3, bf16[1024,512]{0,1:T(8,128)(2,1)S(1)} %copy-done.9, bf16[1024,512]{0,1:T(8,128)(2,1)S(1)} %copy-done.11), kind=kLoop, calls=%fused_computation.54 | loop fusion | flops 524288 | bytes 2097152 | tf_op jit(solution)/shard_map/add | solution.py:90
  67.1 6.8 %collective-permute-start.11 = (bf16[1024,256]{0,1:T(8,128)(2,1)}, bf16[1024,256]{0,1:T(8,128)(2,1)}, u32[]{:S(2)}, u32[]{:S(2)}) collective-permute-start(bf16[1024,256]{0,1:T(8,128)(2,1)} %fusion.28), channel_id=1, source_target_pairs={{0,4},{12,8},{1,5},{13,9},{2,6},{14,10},{3,7},{15,11},{16,20},{28,... | collective-permute-start | bytes 1572872 | tf_op jit(solution)/shard_map/ppermute | solution.py:40
  73.9 2.6 %convolution_convert_fusion = bf16[256,4096]{1,0:T(8,128)(2,1)} fusion(bf16[256,512]{1,0:T(8,128)(2,1)S(1)} %fusion.39, bf16[512,4096]{1,0:T(8,128)(2,1)S(1)} %bitcast.90), kind=kOutput, calls=%fused_computation | convolution fusion | flops 1074790400 | bytes 6553600 | tf_op jit(solution)/shard_map/dot_general | solution.py:19
  79.6 2.0 fusion.27
  81.6 6.7 %collective-permute-start.14 = (bf16[1024,256]{0,1:T(8,128)(2,1)}, bf16[1024,256]{0,1:T(8,128)(2,1)}, u32[]{:S(2)}, u32[]{:S(2)}) collective-permute-start(bf16[1024,256]{0,1:T(8,128)(2,1)} %fusion.27), channel_id=1, source_target_pairs={{0,4},{12,8},{1,5},{13,9},{2,6},{14,10},{3,7},{15,11},{16,20},{28,... | collective-permute-start | bytes 1572872 | tf_op jit(solution)/shard_map/ppermute | solution.py:40
  88.3 3.1 %collective-permute-done.7 = bf16[1024,256]{0,1:T(8,128)(2,1)} collective-permute-done((bf16[1024,256]{0,1:T(8,128)(2,1)S(1)}, bf16[1024,256]{0,1:T(8,128)(2,1)}, u32[]{:S(2)}, u32[]{:S(2)}) %collective-permute-start.7) | collective-permute-done | bytes 524320 | tf_op jit(solution)/shard_map/ppermute | solution.py:89
  92.4 3.6 %all-to-all-start = ((bf16[4,64,4096]{2,1,0:T(8,128)(2,1)}), bf16[4,64,4096]{2,1,0:T(8,128)(2,1)S(1)}, u32[]{:S(2)}, u32[]{:S(2)}) async-start(bf16[4,64,4096]{2,1,0:T(8,128)(2,1)} %bitcast.91), calls=%async_computation.1 | async-start | bytes 4194304 | tf_op jit(solution)/shard_map/all_to_all | solution.py:162
  96.0 1.4 fusion.26
  97.4 5.0 %collective-permute-start.17 = (bf16[1024,256]{0,1:T(8,128)(2,1)S(1)}, bf16[1024,256]{0,1:T(8,128)(2,1)S(1)}, u32[]{:S(2)}, u32[]{:S(2)}) collective-permute-start(bf16[1024,256]{0,1:T(8,128)(2,1)S(1)} %fusion.26), channel_id=1, source_target_pairs={{0,4},{12,8},{1,5},{13,9},{2,6},{14,10},{3,7},{15,11},{16,20},{28,... | collective-permute-start | bytes 1572872 | tf_op jit(solution)/shard_map/ppermute | solution.py:40
  103.3 1.4 add.298
  106.0 1.6 add.304
  109.3 2.0 collective-permute-start.23
  111.4 2.9 %collective-permute-done.17 = bf16[1024,256]{0,1:T(8,128)(2,1)S(1)} collective-permute-done((bf16[1024,256]{0,1:T(8,128)(2,1)S(1)}, bf16[1024,256]{0,1:T(8,128)(2,1)S(1)}, u32[]{:S(2)}, u32[]{:S(2)}) %collective-permute-start.17) | collective-permute-done | bytes 524320 | tf_op jit(solution)/shard_map/ppermute | solution.py:40
  115.8 11.4 %collective-permute-done.23 = bf16[256,512]{1,0:T(8,128)(2,1)S(1)} collective-permute-done((bf16[256,512]{1,0:T(8,128)(2,1)S(1)}, bf16[256,512]{1,0:T(8,128)(2,1)S(1)}, u32[]{:S(2)}, u32[]{:S(2)}) %collective-permute-start.23) | collective-permute-done | bytes 262176 | tf_op jit(solution)/shard_map/ppermute | solution.py:89
  127.3 1.5 collective-permute-start.20
  129.8 5.0 %collective-permute-start.24 = (bf16[256,512]{1,0:T(8,128)(2,1)S(1)}, bf16[256,512]{1,0:T(8,128)(2,1)S(1)}, u32[]{:S(2)}, u32[]{:S(2)}) collective-permute-start(bf16[256,512]{1,0:T(8,128)(2,1)S(1)} %fusion.63), channel_id=1, source_target_pairs={{0,4},{12,8},{1,5},{13,9},{2,6},{14,10},{3,7},{15,11},{16,20},{28,... | collective-permute-start | bytes 786440 | tf_op jit(solution)/shard_map/ppermute | solution.py:40
  134.8 2.0 add.294
  136.9 1.3 collective-permute-start.10
  143.8 1.4 collective-permute-start.25
  147.5 9.3 %all-to-all-start.2 = ((bf16[16,8,512]{2,1,0:T(8,128)(2,1)}), bf16[16,8,512]{2,1,0:T(8,128)(2,1)S(1)}, u32[]{:S(2)}, u32[]{:S(2)}) async-start(bf16[16,8,512]{2,1,0:T(8,128)(2,1)} %fusion.14), calls=%async_computation.3 | async-start | bytes 262144 | tf_op jit(solution)/shard_map/all_to_all | solution.py:152
  157.9 1.4 fusion.53
  159.2 7.3 %collective-permute-done.13 = bf16[1024,256]{0,1:T(8,128)(2,1)} collective-permute-done((bf16[1024,256]{0,1:T(8,128)(2,1)}, bf16[1024,256]{0,1:T(8,128)(2,1)}, u32[]{:S(2)}, u32[]{:S(2)}) %collective-permute-start.13) | collective-permute-done | bytes 524320 | tf_op jit(solution)/shard_map/ppermute | solution.py:44
  166.6 1.4 fusion.50
  168.0 9.8 %collective-permute-done.16 = bf16[1024,256]{0,1:T(8,128)(2,1)} collective-permute-done((bf16[1024,256]{0,1:T(8,128)(2,1)}, bf16[1024,256]{0,1:T(8,128)(2,1)}, u32[]{:S(2)}, u32[]{:S(2)}) %collective-permute-start.16) | collective-permute-done | bytes 524320 | tf_op jit(solution)/shard_map/ppermute | solution.py:44
  177.8 1.4 fusion.47
  179.2 8.2 %collective-permute-done.19 = bf16[1024,256]{0,1:T(8,128)(2,1)} collective-permute-done((bf16[1024,256]{0,1:T(8,128)(2,1)}, bf16[1024,256]{0,1:T(8,128)(2,1)}, u32[]{:S(2)}, u32[]{:S(2)}) %collective-permute-start.19) | collective-permute-done | bytes 524320 | tf_op jit(solution)/shard_map/ppermute | solution.py:44
  187.4 1.4 fusion.44
  191.2 1.3 collective-permute-start.26
  192.5 1.4 collective-permute-done.21
  194.0 5.5 %collective-permute-done.26 = bf16[256,512]{1,0:T(8,128)(2,1)S(1)} collective-permute-done((bf16[256,512]{1,0:T(8,128)(2,1)S(1)}, bf16[256,512]{1,0:T(8,128)(2,1)S(1)}, u32[]{:S(2)}, u32[]{:S(2)}) %collective-permute-start.26) | collective-permute-done | bytes 262176 | tf_op jit(solution)/shard_map/ppermute | solution.py:44
  200.4 3.4 %all-to-all-start.3 = ((bf16[4,64,512]{2,1,0:T(8,128)(2,1)}), bf16[4,64,512]{2,1,0:T(8,128)(2,1)S(1)}, u32[]{:S(2)}, u32[]{:S(2)}) async-start(bf16[4,64,512]{2,1,0:T(8,128)(2,1)} %bitcast.25), calls=%async_computation.4 | async-start | bytes 524288 | tf_op jit(solution)/shard_map/all_to_all | solution.py:182
  203.9 6.0 %all-to-all-done.3 = bf16[4,64,512]{2,1,0:T(8,128)(2,1)S(1)} async-done(((bf16[4,64,512]{2,1,0:T(8,128)(2,1)}), bf16[4,64,512]{2,1,0:T(8,128)(2,1)S(1)}, u32[]{:S(2)}, u32[]{:S(2)}) %all-to-all-start.3) | async-done | bytes 262176 | tf_op jit(solution)/shard_map/all_to_all | solution.py:182
  210.3 1.4 add_convert_fusion
  (158 shorter events, 38.3 us)
Async XLA Ops:
  6.5 71.8 %copy-start = (bf16[512,512]{1,0:T(8,128)(2,1)S(1)}, bf16[512,512]{1,0:T(8,128)(2,1)}, u32[]{:S(2)}) copy-start(bf16[512,512]{1,0:T(8,128)(2,1)} %param.10) | copy-start | bytes 1572868
  8.4 5.8 %copy-start.16 = (bf16[512,512]{1,0:T(8,128)(2,1)}, bf16[512,512]{1,0:T(8,128)(2,1)S(1)}, u32[]{:S(2)}) copy-start(bf16[512,512]{1,0:T(8,128)(2,1)S(1)} %fusion.16) | copy-start | bytes 1572868
  11.4 2.8 %collective-permute-start = (bf16[1024,512]{0,1:T(8,128)(2,1)S(1)}, bf16[1024,512]{0,1:T(8,128)(2,1)S(1)}, u32[]{:S(2)}, u32[]{:S(2)}) collective-permute-start(bf16[1024,512]{0,1:T(8,128)(2,1)S(1)} %fusion.1), channel_id=1, source_target_pairs={{0,1},{1,0},{2,3},{3,2},{4,5},{5,4},{6,7},{7,6},{8,9},{9,8},{10,11... | collective-permute-start | bytes 3145736 | tf_op jit(solution)/shard_map/ppermute | solution.py:85
  12.0 5.9 %copy-start.3 = (bf16[4,128,4096]{2,1,0:T(8,128)(2,1)S(1)}, bf16[4,128,4096]{2,1,0:T(8,128)(2,1)}, u32[]{:S(2)}) copy-start(bf16[4,128,4096]{2,1,0:T(8,128)(2,1)} %param.7) | copy-start | bytes 12582916
  14.2 3.8 %copy-start.13 = (bf16[1024,512]{0,1:T(8,128)(2,1)}, bf16[1024,512]{0,1:T(8,128)(2,1)S(1)}, u32[]{:S(2)}) copy-start(bf16[1024,512]{0,1:T(8,128)(2,1)S(1)} %fusion) | copy-start | bytes 3145732
  14.6 17.8 %collective-permute-start.1 = (bf16[1024,256]{0,1:T(8,128)(2,1)S(1)}, bf16[1024,256]{0,1:T(8,128)(2,1)}, u32[]{:S(2)}, u32[]{:S(2)}) collective-permute-start(bf16[1024,256]{0,1:T(8,128)(2,1)S(1)} %slice_add_fusion.7), channel_id=1, source_target_pairs={{0,2},{2,0},{1,3},{3,1},{4,6},{6,4},{5,7},{7,5},{8,10},{10,8},{9,1... | collective-permute-start | bytes 1572872 | tf_op jit(solution)/shard_map/ppermute | solution.py:89
  19.9 71.5 %all-to-all-start.1 = ((bf16[16,8,4224]{2,1,0:T(8,128)(2,1)}), bf16[16,8,4224]{2,1,0:T(8,128)(2,1)S(1)}, u32[]{:S(2)}, u32[]{:S(2)}) async-start(bf16[16,8,4224]{2,1,0:T(8,128)(2,1)} %maximum_bitcast_fusion), calls=%async_computation.2 | async-start | bytes 2162688 | tf_op jit(solution)/shard_map/all_to_all | solution.py:146
  24.9 185.5 %reduce-scatter.2.cloned.1.call-start = ((), (), s32[]{:S(2)}) async-start(), calls=%async_computation.5 | async-start | bytes 3145728 | tf_op jit(solution)/shard_map/reduce_scatter | solution.py:156
  27.1 5.3 %copy-start.14 = (bf16[1024,512]{0,1:T(8,128)(2,1)S(1)}, bf16[1024,512]{0,1:T(8,128)(2,1)}, u32[]{:S(2)}) copy-start(bf16[1024,512]{0,1:T(8,128)(2,1)} %copy-done.13) | copy-start | bytes 3145732
  27.1 12.8 %collective-permute-start.2 = (bf16[1024,512]{0,1:T(8,128)(2,1)S(1)}, bf16[1024,512]{0,1:T(8,128)(2,1)S(1)}, u32[]{:S(2)}, u32[]{:S(2)}) collective-permute-start(bf16[1024,512]{0,1:T(8,128)(2,1)S(1)} %fusion.3), channel_id=1, source_target_pairs={{0,1},{1,0},{2,3},{3,2},{4,5},{5,4},{6,7},{7,6},{8,9},{9,8},{10,11... | collective-permute-start | bytes 3145736 | tf_op jit(solution)/shard_map/ppermute | solution.py:85
  27.7 9.3 %copy-start.21 = (bf16[512,512]{1,0:T(8,128)(2,1)S(1)}, bf16[512,512]{1,0:T(8,128)(2,1)}, u32[]{:S(2)}) copy-start(bf16[512,512]{1,0:T(8,128)(2,1)} %copy-done.20) | copy-start | bytes 1572868
  29.7 10.2 %copy-start.10 = (bf16[1024,512]{0,1:T(8,128)(2,1)}, bf16[1024,512]{0,1:T(8,128)(2,1)S(1)}, u32[]{:S(2)}) copy-start(bf16[1024,512]{0,1:T(8,128)(2,1)S(1)} %fusion.2) | copy-start | bytes 3145732
  33.5 11.0 %copy-start.4 = (bf16[4,128,4096]{2,1,0:T(8,128)(2,1)S(1)}, bf16[4,128,4096]{2,1,0:T(8,128)(2,1)}, u32[]{:S(2)}) copy-start(bf16[4,128,4096]{2,1,0:T(8,128)(2,1)} %param.7) | copy-start | bytes 12582916
  33.5 21.6 %collective-permute-start.8 = (bf16[1024,256]{0,1:T(8,128)(2,1)S(1)}, bf16[1024,256]{0,1:T(8,128)(2,1)}, u32[]{:S(2)}, u32[]{:S(2)}) collective-permute-start(bf16[1024,256]{0,1:T(8,128)(2,1)S(1)} %fusion.29), channel_id=1, source_target_pairs={{0,4},{12,8},{1,5},{13,9},{2,6},{14,10},{3,7},{15,11},{16,20},{28,... | collective-permute-start | bytes 1572872 | tf_op jit(solution)/shard_map/ppermute | solution.py:40
  39.9 22.0 %collective-permute-start.5 = (bf16[1024,512]{0,1:T(8,128)(2,1)}, bf16[1024,512]{0,1:T(8,128)(2,1)}, u32[]{:S(2)}, u32[]{:S(2)}) collective-permute-start(bf16[1024,512]{0,1:T(8,128)(2,1)} %fusion.7), channel_id=1, source_target_pairs={{0,1},{1,0},{2,3},{3,2},{4,5},{5,4},{6,7},{7,6},{8,9},{9,8},{10,11... | collective-permute-start | bytes 3145736 | tf_op jit(solution)/shard_map/ppermute | solution.py:85
  41.9 11.1 %copy-start.18 = (bf16[512,512]{1,0:T(8,128)(2,1)S(1)}, bf16[512,512]{1,0:T(8,128)(2,1)}, u32[]{:S(2)}) copy-start(bf16[512,512]{1,0:T(8,128)(2,1)} %copy-done.16) | copy-start | bytes 1572868
  41.9 18.1 %collective-permute-start.3 = (bf16[1024,256]{0,1:T(8,128)(2,1)}, bf16[1024,256]{0,1:T(8,128)(2,1)}, u32[]{:S(2)}, u32[]{:S(2)}) collective-permute-start(bf16[1024,256]{0,1:T(8,128)(2,1)} %slice_add_fusion.6), channel_id=1, source_target_pairs={{0,2},{2,0},{1,3},{3,1},{4,6},{6,4},{5,7},{7,5},{8,10},{10,8},{9,1... | collective-permute-start | bytes 1572872 | tf_op jit(solution)/shard_map/ppermute | solution.py:89
  53.0 7.0 %copy-start.6 = (bf16[4096,512]{1,0:T(8,128)(2,1)S(1)}, bf16[4096,512]{1,0:T(8,128)(2,1)}, u32[]{:S(2)}) copy-start(bf16[4096,512]{1,0:T(8,128)(2,1)} %param.9) | copy-start | bytes 12582916
  56.4 7.6 %copy-start.19 = (bf16[512,512]{1,0:T(8,128)(2,1)S(1)}, bf16[512,512]{1,0:T(8,128)(2,1)}, u32[]{:S(2)}) copy-start(bf16[512,512]{1,0:T(8,128)(2,1)} %copy-done.16) | copy-start | bytes 1572868
  56.4 73.4 %collective-permute-start.9 = (bf16[1024,256]{0,1:T(8,128)(2,1)S(1)}, bf16[1024,256]{0,1:T(8,128)(2,1)}, u32[]{:S(2)}, u32[]{:S(2)}) collective-permute-start(bf16[1024,256]{0,1:T(8,128)(2,1)S(1)} %add.293), channel_id=1, source_target_pairs={{4,8},{8,4},{5,9},{9,5},{6,10},{10,6},{7,11},{11,7},{20,24},{24,20... | collective-permute-start | bytes 1572872 | tf_op jit(solution)/shard_map/ppermute | solution.py:41
  61.8 15.7 %collective-permute-start.4 = (bf16[1024,512]{0,1:T(8,128)(2,1)S(1)}, bf16[1024,512]{0,1:T(8,128)(2,1)S(1)}, u32[]{:S(2)}, u32[]{:S(2)}) collective-permute-start(bf16[1024,512]{0,1:T(8,128)(2,1)S(1)} %fusion.5), channel_id=1, source_target_pairs={{0,1},{1,0},{2,3},{3,2},{4,5},{5,4},{6,7},{7,6},{8,9},{9,8},{10,11... | collective-permute-start | bytes 3145736 | tf_op jit(solution)/shard_map/ppermute | solution.py:85
  63.2 10.7 %copy-start.5 = (bf16[4,128,4096]{2,1,0:T(8,128)(2,1)S(1)}, bf16[4,128,4096]{2,1,0:T(8,128)(2,1)}, u32[]{:S(2)}) copy-start(bf16[4,128,4096]{2,1,0:T(8,128)(2,1)} %param.7) | copy-start | bytes 12582916
  63.2 14.3 %collective-permute-start.6 = (bf16[1024,256]{0,1:T(8,128)(2,1)S(1)}, bf16[1024,256]{0,1:T(8,128)(2,1)S(1)}, u32[]{:S(2)}, u32[]{:S(2)}) collective-permute-start(bf16[1024,256]{0,1:T(8,128)(2,1)S(1)} %slice_add_fusion.4), channel_id=1, source_target_pairs={{0,2},{2,0},{1,3},{3,1},{4,6},{6,4},{5,7},{7,5},{8,10},{10,8},{9,1... | collective-permute-start | bytes 1572872 | tf_op jit(solution)/shard_map/ppermute | solution.py:89
  64.8 12.7 %copy-start.15 = (bf16[1024,512]{0,1:T(8,128)(2,1)}, bf16[1024,512]{0,1:T(8,128)(2,1)S(1)}, u32[]{:S(2)}) copy-start(bf16[1024,512]{0,1:T(8,128)(2,1)S(1)} %fusion.4) | copy-start | bytes 3145732
  67.1 36.2 %collective-permute-start.11 = (bf16[1024,256]{0,1:T(8,128)(2,1)}, bf16[1024,256]{0,1:T(8,128)(2,1)}, u32[]{:S(2)}, u32[]{:S(2)}) collective-permute-start(bf16[1024,256]{0,1:T(8,128)(2,1)} %fusion.28), channel_id=1, source_target_pairs={{0,4},{12,8},{1,5},{13,9},{2,6},{14,10},{3,7},{15,11},{16,20},{28,... | collective-permute-start | bytes 1572872 | tf_op jit(solution)/shard_map/ppermute | solution.py:40
  77.5 4.0 %copy-start.12 = (bf16[1024,512]{0,1:T(8,128)(2,1)}, bf16[1024,512]{0,1:T(8,128)(2,1)S(1)}, u32[]{:S(2)}) copy-start(bf16[1024,512]{0,1:T(8,128)(2,1)S(1)} %collective-permute-done.4) | copy-start | bytes 3145732
  77.6 13.8 %collective-permute-start.7 = (bf16[1024,256]{0,1:T(8,128)(2,1)S(1)}, bf16[1024,256]{0,1:T(8,128)(2,1)}, u32[]{:S(2)}, u32[]{:S(2)}) collective-permute-start(bf16[1024,256]{0,1:T(8,128)(2,1)S(1)} %slice_add_fusion.5), channel_id=1, source_target_pairs={{0,2},{2,0},{1,3},{3,1},{4,6},{6,4},{5,7},{7,5},{8,10},{10,8},{9,1... | collective-permute-start | bytes 1572872 | tf_op jit(solution)/shard_map/ppermute | solution.py:89
  79.6 28.7 %collective-permute-start.22 = (bf16[512,512]{1,0:T(8,128)(2,1)}, bf16[512,512]{1,0:T(8,128)(2,1)}, u32[]{:S(2)}, u32[]{:S(2)}) collective-permute-start(bf16[512,512]{1,0:T(8,128)(2,1)} %convolution_convert_fusion.10), channel_id=1, source_target_pairs={{0,1},{1,0},{2,3},{3,2},{4,5},{5,4},{6,7},{7,6},{8,9},{9,8},{10,11... | collective-permute-start | bytes 1572872 | tf_op jit(solution)/shard_map/ppermute | solution.py:85
  81.6 24.4 %collective-permute-start.14 = (bf16[1024,256]{0,1:T(8,128)(2,1)}, bf16[1024,256]{0,1:T(8,128)(2,1)}, u32[]{:S(2)}, u32[]{:S(2)}) collective-permute-start(bf16[1024,256]{0,1:T(8,128)(2,1)} %fusion.27), channel_id=1, source_target_pairs={{0,4},{12,8},{1,5},{13,9},{2,6},{14,10},{3,7},{15,11},{16,20},{28,... | collective-permute-start | bytes 1572872 | tf_op jit(solution)/shard_map/ppermute | solution.py:40
  92.4 55.1 %all-to-all-start = ((bf16[4,64,4096]{2,1,0:T(8,128)(2,1)}), bf16[4,64,4096]{2,1,0:T(8,128)(2,1)S(1)}, u32[]{:S(2)}, u32[]{:S(2)}) async-start(bf16[4,64,4096]{2,1,0:T(8,128)(2,1)} %bitcast.91), calls=%async_computation.1 | async-start | bytes 4194304 | tf_op jit(solution)/shard_map/all_to_all | solution.py:162
  97.4 16.8 %collective-permute-start.17 = (bf16[1024,256]{0,1:T(8,128)(2,1)S(1)}, bf16[1024,256]{0,1:T(8,128)(2,1)S(1)}, u32[]{:S(2)}, u32[]{:S(2)}) collective-permute-start(bf16[1024,256]{0,1:T(8,128)(2,1)S(1)} %fusion.26), channel_id=1, source_target_pairs={{0,4},{12,8},{1,5},{13,9},{2,6},{14,10},{3,7},{15,11},{16,20},{28,... | collective-permute-start | bytes 1572872 | tf_op jit(solution)/shard_map/ppermute | solution.py:40
  104.7 34.3 %collective-permute-start.12 = (bf16[1024,256]{0,1:T(8,128)(2,1)S(1)}, bf16[1024,256]{0,1:T(8,128)(2,1)S(1)}, u32[]{:S(2)}, u32[]{:S(2)}) collective-permute-start(bf16[1024,256]{0,1:T(8,128)(2,1)S(1)} %add.298), channel_id=1, source_target_pairs={{4,8},{8,4},{5,9},{9,5},{6,10},{10,6},{7,11},{11,7},{20,24},{24,20... | collective-permute-start | bytes 1572872 | tf_op jit(solution)/shard_map/ppermute | solution.py:41
  105.4 9.7 %copy-start.7 = (bf16[4096,512]{1,0:T(8,128)(2,1)S(1)}, bf16[4096,512]{1,0:T(8,128)(2,1)}, u32[]{:S(2)}) copy-start(bf16[4096,512]{1,0:T(8,128)(2,1)} %param.9) | copy-start | bytes 12582916
  105.9 9.2 %copy-start.2 = (bf16[16,8,4224]{2,1,0:T(8,128)(2,1)S(1)}, bf16[16,8,4224]{2,1,0:T(8,128)(2,1)}, u32[]{:S(2)}) copy-start(bf16[16,8,4224]{2,1,0:T(8,128)(2,1)} %copy-done.1) | copy-start | bytes 3244036
  107.6 33.8 %collective-permute-start.15 = (bf16[1024,256]{0,1:T(8,128)(2,1)S(1)}, bf16[1024,256]{0,1:T(8,128)(2,1)S(1)}, u32[]{:S(2)}, u32[]{:S(2)}) collective-permute-start(bf16[1024,256]{0,1:T(8,128)(2,1)S(1)} %add.304), channel_id=1, source_target_pairs={{4,8},{8,4},{5,9},{9,5},{6,10},{10,6},{7,11},{11,7},{20,24},{24,20... | collective-permute-start | bytes 1572872 | tf_op jit(solution)/shard_map/ppermute | solution.py:41
  109.3 18.0 %collective-permute-start.23 = (bf16[256,512]{1,0:T(8,128)(2,1)S(1)}, bf16[256,512]{1,0:T(8,128)(2,1)S(1)}, u32[]{:S(2)}, u32[]{:S(2)}) collective-permute-start(bf16[256,512]{1,0:T(8,128)(2,1)S(1)} %slice_add_fusion.8), channel_id=1, source_target_pairs={{0,2},{2,0},{1,3},{3,1},{4,6},{6,4},{5,7},{7,5},{8,10},{10,8},{9,1... | collective-permute-start | bytes 786440 | tf_op jit(solution)/shard_map/ppermute | solution.py:89
  114.4 30.8 %collective-permute-start.18 = (bf16[1024,256]{0,1:T(8,128)(2,1)S(1)}, bf16[1024,256]{0,1:T(8,128)(2,1)S(1)}, u32[]{:S(2)}, u32[]{:S(2)}) collective-permute-start(bf16[1024,256]{0,1:T(8,128)(2,1)S(1)} %add.310), channel_id=1, source_target_pairs={{4,8},{8,4},{5,9},{9,5},{6,10},{10,6},{7,11},{11,7},{20,24},{24,20... | collective-permute-start | bytes 1572872 | tf_op jit(solution)/shard_map/ppermute | solution.py:41
  127.3 9.6 %collective-permute-start.20 = (f32[128,512]{1,0:T(8,128)S(1)}, f32[128,512]{1,0:T(8,128)S(1)}, u32[]{:S(2)}, u32[]{:S(2)}) collective-permute-start(f32[128,512]{1,0:T(8,128)S(1)} %convolution_select_fusion), channel_id=1, source_target_pairs={{0,16},{16,0},{1,17},{17,1},{2,18},{18,2},{3,19},{19,3},{4,20},{20... | collective-permute-start | bytes 786440 | tf_op jit(solution)/shard_map/ppermute | solution.py:28
  129.8 13.9 %collective-permute-start.24 = (bf16[256,512]{1,0:T(8,128)(2,1)S(1)}, bf16[256,512]{1,0:T(8,128)(2,1)S(1)}, u32[]{:S(2)}, u32[]{:S(2)}) collective-permute-start(bf16[256,512]{1,0:T(8,128)(2,1)S(1)} %fusion.63), channel_id=1, source_target_pairs={{0,4},{12,8},{1,5},{13,9},{2,6},{14,10},{3,7},{15,11},{16,20},{28,... | collective-permute-start | bytes 786440 | tf_op jit(solution)/shard_map/ppermute | solution.py:40
  136.9 21.0 %collective-permute-start.10 = (bf16[1024,256]{0,1:T(8,128)(2,1)}, bf16[1024,256]{0,1:T(8,128)(2,1)}, u32[]{:S(2)}, u32[]{:S(2)}) collective-permute-start(bf16[1024,256]{0,1:T(8,128)(2,1)} %add.294), channel_id=1, source_target_pairs={{4,0},{8,12},{5,1},{9,13},{6,2},{10,14},{7,3},{11,15},{20,16},{24,... | collective-permute-start | bytes 1572872 | tf_op jit(solution)/shard_map/ppermute | solution.py:44
  140.1 26.4 %collective-permute-start.13 = (bf16[1024,256]{0,1:T(8,128)(2,1)}, bf16[1024,256]{0,1:T(8,128)(2,1)}, u32[]{:S(2)}, u32[]{:S(2)}) collective-permute-start(bf16[1024,256]{0,1:T(8,128)(2,1)} %add.299), channel_id=1, source_target_pairs={{4,0},{8,12},{5,1},{9,13},{6,2},{10,14},{7,3},{11,15},{20,16},{24,... | collective-permute-start | bytes 1572872 | tf_op jit(solution)/shard_map/ppermute | solution.py:44
  142.4 35.4 %collective-permute-start.16 = (bf16[1024,256]{0,1:T(8,128)(2,1)}, bf16[1024,256]{0,1:T(8,128)(2,1)}, u32[]{:S(2)}, u32[]{:S(2)}) collective-permute-start(bf16[1024,256]{0,1:T(8,128)(2,1)} %add.305), channel_id=1, source_target_pairs={{4,0},{8,12},{5,1},{9,13},{6,2},{10,14},{7,3},{11,15},{20,16},{24,... | collective-permute-start | bytes 1572872 | tf_op jit(solution)/shard_map/ppermute | solution.py:44
  143.8 46.4 %collective-permute-start.25 = (bf16[256,512]{1,0:T(8,128)(2,1)S(1)}, bf16[256,512]{1,0:T(8,128)(2,1)}, u32[]{:S(2)}, u32[]{:S(2)}) collective-permute-start(bf16[256,512]{1,0:T(8,128)(2,1)S(1)} %add.322), channel_id=1, source_target_pairs={{4,8},{8,4},{5,9},{9,5},{6,10},{10,6},{7,11},{11,7},{20,24},{24,20... | collective-permute-start | bytes 786440 | tf_op jit(solution)/shard_map/ppermute | solution.py:41
  146.2 41.3 %collective-permute-start.19 = (bf16[1024,256]{0,1:T(8,128)(2,1)}, bf16[1024,256]{0,1:T(8,128)(2,1)}, u32[]{:S(2)}, u32[]{:S(2)}) collective-permute-start(bf16[1024,256]{0,1:T(8,128)(2,1)} %add.311), channel_id=1, source_target_pairs={{4,0},{8,12},{5,1},{9,13},{6,2},{10,14},{7,3},{11,15},{20,16},{24,... | collective-permute-start | bytes 1572872 | tf_op jit(solution)/shard_map/ppermute | solution.py:44
  147.5 42.1 %all-to-all-start.2 = ((bf16[16,8,512]{2,1,0:T(8,128)(2,1)}), bf16[16,8,512]{2,1,0:T(8,128)(2,1)S(1)}, u32[]{:S(2)}, u32[]{:S(2)}) async-start(bf16[16,8,512]{2,1,0:T(8,128)(2,1)} %fusion.14), calls=%async_computation.3 | async-start | bytes 262144 | tf_op jit(solution)/shard_map/all_to_all | solution.py:152
  189.5 4.3 %collective-permute-start.21 = (f32[128,128]{1,0:T(8,128)S(1)}, f32[128,128]{1,0:T(8,128)S(1)}, u32[]{:S(2)}, u32[]{:S(2)}) collective-permute-start(f32[128,128]{1,0:T(8,128)S(1)} %bitcast.94), channel_id=1, source_target_pairs={{0,16},{16,0},{1,17},{17,1},{2,18},{18,2},{3,19},{19,3},{4,20},{20... | collective-permute-start | bytes 196616 | tf_op jit(solution)/shard_map/ppermute | solution.py:28
  191.2 8.3 %collective-permute-start.26 = (bf16[256,512]{1,0:T(8,128)(2,1)S(1)}, bf16[256,512]{1,0:T(8,128)(2,1)S(1)}, u32[]{:S(2)}, u32[]{:S(2)}) collective-permute-start(bf16[256,512]{1,0:T(8,128)(2,1)S(1)} %add.323), channel_id=1, source_target_pairs={{4,0},{8,12},{5,1},{9,13},{6,2},{10,14},{7,3},{11,15},{20,16},{24,... | collective-permute-start | bytes 786440 | tf_op jit(solution)/shard_map/ppermute | solution.py:44
  200.4 9.4 %all-to-all-start.3 = ((bf16[4,64,512]{2,1,0:T(8,128)(2,1)}), bf16[4,64,512]{2,1,0:T(8,128)(2,1)S(1)}, u32[]{:S(2)}, u32[]{:S(2)}) async-start(bf16[4,64,512]{2,1,0:T(8,128)(2,1)} %bitcast.25), calls=%async_computation.4 | async-start | bytes 524288 | tf_op jit(solution)/shard_map/all_to_all | solution.py:182
  (8 other events, 16.3 us)
Sparse Core Ops, SparseCore 0:
  53.1 32.2 reduce-scatter.1

commit v3 on v2

--- a/solution.py
+++ b/solution.py
@@ -33,21 +33,24 @@
     return lax.optimization_barrier((value, *others))[0]
 
 
-def line_sum(held):
-    n, z_at = lax.axis_size("z"), lax.axis_index("z")
+class Chain:
+    def __init__(self):
+        self.last = None
+
+    def hold(self, value):
+        self.last = value if self.last is None else after(value, self.last)
+        return self.last
+
+    def permute(self, value, axis, pairs):
+        return lax.ppermute(self.hold(value), axis, pairs)
+
+
+def line_hops(n):
     half = n // 2
-    for k in range(half - 1):
-        held = held + lax.ppermute(held, "z", [(k, k + 1), (n - 1 - k, n - 2 - k)])
-    held = held + lax.ppermute(held, "z", [(half - 1, half), (half, half - 1)])
-    pieces = [held]
-    for k in reversed(range(half - 1)):
-        got = lax.ppermute(held, "z", [(k + 1, k), (n - 2 - k, n - 1 - k)])
-        here = (z_at == k) | (z_at == n - 1 - k)
-        if k > 0:
-            held = jnp.where(here, got, held)
-        else:
-            pieces = [jnp.where(here, jnp.zeros_like(held), held), got]
-    return pieces
+    hops = [([(k, k + 1), (n - 1 - k, n - 2 - k)], None) for k in range(half - 1)]
+    hops.append(([(half - 1, half), (half, half - 1)], None))
+    hops += [([(k + 1, k), (n - 2 - k, n - 1 - k)], k) for k in reversed(range(half - 1))]
+    return hops
 
 
 def on_device(
@@ -81,45 +84,20 @@
     chunk_count = 4
     part = depth // chunk_count
 
-    def gathered(other, mine, cut, previous):
-        got = lax.ppermute(other, "core", SWAP)
-        send = cut(mine, True) + cut(got, True)
-        if previous is not None:
-            send = after(send, previous)
-        crossed = lax.ppermute(send, "x", SWAP)
-        return line_sum(cut(mine) + cut(got) + crossed), send, crossed
-
-    def cut_columns(block, last=False):
-        return block[:, kept:] if last else block[:, :kept]
-
-    def cut_rows(block, last=False):
-        return block[kept:] if last else block[:kept]
-
+    chain = Chain()
     pick_mine, pick_other = lax.optimization_barrier(
         (pick(column[:, None] == want_mine), pick(column[:, None] == want_other))
     )
-    shrink_hot, sent, over_x = [], [], []
-    for c in range(chunk_count):
-        store = shrink_store[c * part:(c + 1) * part]
-        if c > 0:
-            step_before = sent[0] if c == 1 else over_x[c - 2]
-            pick_mine, pick_other = after(pick_mine, step_before), after(pick_other, step_before)
-        pieces, send, crossed = gathered(
-            narrow(store, pick_other), narrow(store, pick_mine), cut_columns, over_x[-1] if over_x else None
-        )
-        shrink_hot.append(pieces)
-        sent.append(send)
-        over_x.append(crossed)
-    want_mine, want_other = after(want_mine, over_x[-2]), after(want_other, over_x[-2])
-    expand_hot, _, _ = gathered(
-        narrow(pick(want_other[:, None] == column), expand_store),
-        narrow(pick(want_mine[:, None] == column), expand_store),
-        cut_rows,
-        over_x[-1],
-    )
-    expand_hot = sum(expand_hot[1:], expand_hot[0])
-
-    token_adapter = after(token_adapter, sent[0])
+    z_at, z_count = lax.axis_index("z"), lax.axis_size("z")
+    hops = line_hops(z_count)
+
+    swapped = [lax.ppermute(chain.hold(narrow(shrink_store[:part], pick_other)), "core", SWAP)]
+    mine_all = narrow(after(shrink_store, chain.last), pick_mine)
+    mine = [mine_all[:part]]
+    crossed = [chain.permute(mine[0][:, kept:] + swapped[0][:, kept:], "x", SWAP)]
+    rest = lax.ppermute(chain.hold(narrow(shrink_store[part:], after(pick_other, chain.last))), "core", SWAP)
+
+    token_adapter = after(token_adapter, chain.last)
     cold_row = jnp.sum(jnp.where((token_adapter - hot_count)[:, :, None] == names, adapter_row, 0), axis=-1)
     is_hot = token_adapter < hot_count
     is_cold = (token_adapter < none_code) & jnp.logical_not(is_hot)
@@ -142,24 +120,109 @@
 
     tag_out = jnp.broadcast_to(tag.astype(jnp.bfloat16)[:, None], (cold_rows, 128))
     packet = jnp.concatenate([narrow(place_cold, rows), tag_out], axis=1)
-    packet = packet.reshape(dp_count, step_count * CAP, depth + 128)
-    packet = lax.all_to_all(packet, DP, split_axis=0, concat_axis=0, tiled=True)
-    packet = packet.reshape(cold_rows, depth + 128)
-    tag_in = packet[:, depth:depth + 1].astype(jnp.int32)
-    chosen = (column // R + 1)[None, :] == tag_in
-    z_cold = sum_over_tp(jnp.where(chosen, matmul(packet[:, :depth], shrink_store), 0.0))
-    delta_cold = narrow(z_cold.astype(jnp.bfloat16), expand_store)
-    delta_cold = lax.all_to_all(
-        delta_cold.reshape(dp_count, step_count * CAP, head_part), DP, split_axis=0, concat_axis=0, tiled=True
-    ).reshape(cold_rows, head_part)
-
-    base = lax.psum_scatter(
-        matmul(rows, after(value_weight, over_x[0])), "tp", scatter_dimension=1, tiled=True
-    )
-
-    hot_out = after(narrow(after(place_hot, over_x[1]), rows), over_x[-1])
-    hot_out = hot_out.reshape(hot_count, step_count * HCAP, depth)
-    hot_in = lax.all_to_all(hot_out, LAYER, split_axis=0, concat_axis=0, tiled=True).reshape(hot_rows, depth)
+    packet = chain.hold(packet.reshape(dp_count, step_count * CAP, depth + 128))
+    packet = lax.all_to_all(packet, DP, split_axis=0, concat_axis=0, tiled=True).reshape(cold_rows, depth + 128)
+
+    done = {}
+
+    def expand_pick():
+        late_mine, late_other = after(want_mine, chain.last), after(want_other, chain.last)
+        done["expand_other"] = narrow(pick(late_other[:, None] == column), expand_store)
+        done["expand_mine"] = narrow(pick(late_mine[:, None] == column), expand_store)
+
+    def expand_over_core():
+        done["expand_swapped"] = chain.permute(done["expand_other"], "core", SWAP)
+
+    def hot_tokens_rows():
+        done["hot_out"] = narrow(after(place_hot, chain.last), rows)
+
+    def hot_tokens_out():
+        hot_out = chain.hold(done["hot_out"].reshape(hot_count, step_count * HCAP, depth))
+        hot_in = lax.all_to_all(hot_out, LAYER, split_axis=0, concat_axis=0, tiled=True)
+        done["hot_in"] = hot_in.reshape(hot_rows, depth)
+
+    def base_product():
+        done["whole"] = matmul(rows, after(value_weight, chain.last))
+
+    def base_over_tp():
+        whole = done["whole"]
+        if lax.axis_size("tp") == 2:
+            first = lax.axis_index("tp") == 0
+            halves = whole[:, :head_part], whole[:, head_part:]
+            other = jnp.where(first, halves[1], halves[0])
+            done["base"] = jnp.where(first, *halves), chain.permute(other, "tp", SWAP)
+        else:
+            base = lax.psum_scatter(chain.hold(whole), "tp", scatter_dimension=1, tiled=True)
+            done["base"] = base, jnp.zeros_like(base)
+
+    def cold_shrink():
+        tag_in = packet[:, depth:depth + 1].astype(jnp.int32)
+        chosen = (column // R + 1)[None, :] == tag_in
+        product = matmul(packet[:, :depth], after(shrink_store, chain.last))
+        done["z_part"] = jnp.where(chosen, product, 0.0)
+
+    def cold_over_tp():
+        done["z_cold"] = sum_over_tp(chain.hold(done["z_part"]))
+
+    def cold_expand():
+        done["delta"] = narrow(done["z_cold"].astype(jnp.bfloat16), after(expand_store, chain.last))
+
+    def cold_back():
+        delta = chain.hold(done["delta"].reshape(dp_count, step_count * CAP, head_part))
+        delta = lax.all_to_all(delta, DP, split_axis=0, concat_axis=0, tiled=True)
+        done["delta_cold"] = delta.reshape(cold_rows, head_part)
+
+    between = {
+        (1, "end"): [hot_tokens_rows, expand_pick],
+        (2, "end"): [expand_over_core, base_product],
+        (3, "end"): [cold_shrink],
+        (4, "x"): [hot_tokens_out],
+        (4, "end"): [base_over_tp, cold_over_tp],
+        (5, "end"): [cold_expand],
+        (6, "end"): [cold_back],
+    }
+    held = [None] * (chunk_count + 1)
+    factors = [None] * (chunk_count + 1)
+    for slot in range(1, chunk_count + 1 + len(hops)):
+        if slot <= chunk_count:
+            c = slot
+            if c < chunk_count:
+                at = slice(c * part, (c + 1) * part)
+                mine.append(after(mine_all, crossed[c - 1])[at])
+                swapped.append(after(rest, crossed[c - 1])[(c - 1) * part:c * part])
+                send = mine[c][:, kept:] + swapped[c][:, kept:]
+            else:
+                mine.append(done["expand_mine"])
+                swapped.append(done["expand_swapped"])
+                send = mine[c][kept:] + swapped[c][kept:]
+            crossed.append(chain.permute(after(send, crossed[c - 1]), "x", SWAP))
+        for work in between.get((slot, "x"), []):
+            work()
+        for stage, (hop, outward) in enumerate(hops):
+            c = slot - 1 - stage
+            if not 0 <= c <= chunk_count:
+                continue
+            if stage == 0:
+                own, got = mine[c], swapped[c]
+                own, got = (own[:, :kept], got[:, :kept]) if c < chunk_count else (own[:kept], got[:kept])
+                held[c] = own + got + crossed[c]
+            got = chain.permute(held[c], "z", hop)
+            if outward is None:
+                held[c] = held[c] + got
+                factors[c] = [held[c]]
+            else:
+                here = (z_at == outward) | (z_at == z_count - 1 - outward)
+                if outward > 0:
+                    held[c] = jnp.where(here, got, held[c])
+                else:
+                    factors[c] = [jnp.where(here, jnp.zeros_like(held[c]), held[c]), got]
+        for work in between.get((slot, "end"), []):
+            work()
+    *shrink_hot, expand_hot = factors
+    expand_hot = sum(expand_hot[1:], expand_hot[0])
+    hot_in, delta_cold = done["hot_in"], done["delta_cold"]
+    base_kept, base_got = done["base"]
+
     dense = None
     for c, pieces in enumerate(shrink_hot):
         for piece in pieces:
@@ -169,7 +232,7 @@
     dense = dense.reshape(hot_count, pairs, 2, HCAP, pairs, 2 * R)
     low = (jnp.arange(2 * R) < R)[None, None, :]
     z_part = jnp.stack([jnp.where(low, dense[:, p, 0, :, p], dense[:, p, 1, :, p]) for p in range(pairs)], axis=1)
-    z_part = after(z_part.reshape(hot_rows // 2, 2 * R), delta_cold)
+    z_part = after(z_part.reshape(hot_rows // 2, 2 * R), delta_cold, base_got)
     z_hot = sum_over_tp(z_part).astype(jnp.bfloat16)
     same_pair = jnp.arange(pairs)[:, None, None, None, None] == jnp.arange(pairs)[:, None]
     same_half = jnp.arange(2)[:, None, None, None] == jnp.arange(2 * R) // R
@@ -187,7 +250,7 @@
         (((0,), (0,)), ((), ())),
         preferred_element_type=jnp.float32,
     )
-    return (base + delta).astype(jnp.bfloat16).reshape(step_count, token_count, head_part)
+    return (base_kept + base_got + delta).astype(jnp.bfloat16).reshape(step_count, token_count, head_part)
 
 
 def solution(mesh):

time: 221 us -> 218 us (0.986)
  waiting for transfers between devices: 61.3 us -> 81.8 us
  between operations: 14.3 us -> 0.74 us
  starting transfers between devices: 72 us -> 63.8 us
    ppermute x25 -> x24, waiting for transfers between devices: 54 us -> 75.5 us  [the longest x22 75.5 us: permute(): return lax.ppermute(self.hold(value), axis, pairs)]
    ppermute x25 -> x24, starting transfers between devices: 48.6 us -> 37.1 us  [the longest x22 36.4 us: permute(): return lax.ppermute(self.hold(value), axis, pairs)]
    select_n x0 -> x1, other arithmetic: none -> 2.88 us  [base_over_tp(): other = jnp.where(first, halves[1], halves[0])]
    add x21, other arithmetic: 21.7 us -> 19.2 us  [the longest x10 9.78 us: on_device(): held[c] = held[c] + got]
    all_to_all x3, starting transfers between devices: 17.9 us -> 20.2 us  [the longest x1 9.55 us: cold_back(): delta = lax.all_to_all(delta, DP, split_axis=0, concat_axis=0, tiled=True)]
    dot_general x24 -> x19, matrix products: 39.1 us -> 38.3 us  [matmul(): return jnp.dot(a, b, preferred_element_type=jnp.float32)]
  transfers between devices with their start and end apart: 32 -> 30, of which waited for: 12 -> 11; matrix products, arithmetic and copies ran while one was open for 28% -> 26% of each run, Pallas kernels for 0% -> 0%
where the time goes in v3:
time: 218 us; the launch traced here: 217 us
  waiting for transfers between devices  81.8 us (38%)
  starting transfers between devices  63.8 us (29%)
  matrix products  40.9 us (19%)
  other arithmetic  25.8 us (12%)
  local copies, waits for them, and re-layouts  3.81 us (2%)
    ppermute x22, waiting for transfers between devices, permute(): return lax.ppermute(self.hold(value), axis, pairs)  75.5 us
    dot_general x19, matrix products, matmul(): return jnp.dot(a, b, preferred_element_type=jnp.float32)  38.3 us
    ppermute x22, starting transfers between devices, permute(): return lax.ppermute(self.hold(value), axis, pairs)  36.4 us
    add x10, other arithmetic, on_device(): held[c] = held[c] + got  9.78 us
    all_to_all x1, starting transfers between devices, cold_back(): delta = lax.all_to_all(delta, DP, split_axis=0, concat_axis=0, tiled=True)  9.55 us
    all_to_all x1, starting transfers between devices, on_device(): lax.all_to_all(packet, DP, split_axis=0, concat_axis=0, tiled=True)  7.07 us
    all_to_all x1, waiting for transfers between devices, on_device(): lax.all_to_all(delta_hot, LAYER, split_axis=0, concat_axis=0, tiled=True)  5.97 us
    add x5, other arithmetic, on_device(): held[c] = own + got + crossed[c]  5.65 us
  transfers between devices with their start and end apart: 30, of which 11 were waited for; matrix products, arithmetic and copies ran while one was open for 26% of the time, Pallas kernels for 0%

profile of v3, /device:TPU:0, one launch (start us, length us, event | category | flops | bytes accessed | tf_op | source)
XLA Modules:
  0.0 216.9 jit_solution(14847261578022385165)
XLA Ops:
  2.0 2.0 fusion.2
  4.6 4.7 %convolution_convert_fusion = bf16[4096,512]{0,1:T(8,128)(2,1)S(1)} fusion(bf16[4096,512]{1,0:T(8,128)(2,1)} %param.9, bf16[512,512]{1,0:T(8,128)(2,1)S(1)} %fusion.12), kind=kOutput, calls=%fused_computation | convolution fusion | flops 2149580800 | bytes 8912896 | tf_op jit(solution)/shard_map/dot_general | solution.py:19
  9.4 3.6 %fusion = bf16[3072,512]{0,1:T(8,128)(2,1)} fusion(bf16[512,512]{1,0:T(8,128)(2,1)S(1)} %fusion.13, bf16[4096,512]{1,0:T(8,128)(2,1)S(1)} %copy-done.5), kind=kOutput, calls=%fused_computation.4 | convolution fusion | flops 1612185600 | bytes 6815744 | tf_op jit(solution)/shard_map/dot_general | solution.py:19
  16.1 7.1 %all-to-all-start.1 = ((bf16[16,8,4224]{2,1,0:T(8,128)(2,1)}), bf16[16,8,4224]{2,1,0:T(8,128)(2,1)S(1)}, u32[]{:S(2)}, u32[]{:S(2)}) async-start(bf16[16,8,4224]{2,1,0:T(8,128)(2,1)} %maximum_bitcast_fusion), calls=%async_computation.1 | async-start | bytes 2162688 | tf_op jit(solution)/shard_map/all_to_all | solution.py:124
  23.2 1.9 collective-permute-start.1
  25.2 24.1 %collective-permute-done.1 = bf16[1024,256]{0,1:T(8,128)(2,1)} collective-permute-done((bf16[1024,256]{0,1:T(8,128)(2,1)S(1)}, bf16[1024,256]{0,1:T(8,128)(2,1)}, u32[]{:S(2)}, u32[]{:S(2)}) %collective-permute-start.1) | collective-permute-done | bytes 524320 | tf_op jit(solution)/shard_map/ppermute | solution.py:45
  50.6 1.5 slice_add_fusion.4
  52.2 2.4 %collective-permute-start.3 = (bf16[1024,256]{0,1:T(8,128)(2,1)S(1)}, bf16[1024,256]{0,1:T(8,128)(2,1)S(1)}, u32[]{:S(2)}, u32[]{:S(2)}) collective-permute-start(bf16[1024,256]{0,1:T(8,128)(2,1)S(1)} %fusion.14), channel_id=1, source_target_pairs={{0,4},{12,8},{1,5},{13,9},{2,6},{14,10},{3,7},{15,11},{16,20},{28,... | collective-permute-start | bytes 1572872 | tf_op jit(solution)/shard_map/ppermute | solution.py:45
  56.2 5.0 %convolution_convert_fusion.1 = bf16[256,4096]{1,0:T(8,128)(2,1)} fusion(bf16[256,512]{1,0:T(8,128)(2,1)S(1)} %fusion.24, bf16[512,4096]{1,0:T(8,128)(2,1)} %bitcast.72), kind=kOutput, calls=%fused_computation.1 | convolution fusion | flops 1074790400 | bytes 6553600 | tf_op jit(solution)/shard_map/dot_general | solution.py:19
  61.2 6.8 %collective-permute-done.4 = bf16[1024,256]{0,1:T(8,128)(2,1)S(1)} collective-permute-done((bf16[1024,256]{0,1:T(8,128)(2,1)S(1)}, bf16[1024,256]{0,1:T(8,128)(2,1)S(1)}, u32[]{:S(2)}, u32[]{:S(2)}) %collective-permute-start.4) | collective-permute-done | bytes 524320 | tf_op jit(solution)/shard_map/ppermute | solution.py:45
  69.1 1.6 collective-permute-start.6
  72.4 1.6 collective-permute-start.5
  75.1 6.9 %collective-permute-done.6 = bf16[1024,256]{0,1:T(8,128)(2,1)S(1)} collective-permute-done((bf16[1024,256]{0,1:T(8,128)(2,1)S(1)}, bf16[1024,256]{0,1:T(8,128)(2,1)S(1)}, u32[]{:S(2)}, u32[]{:S(2)}) %collective-permute-start.6) | collective-permute-done | bytes 524320 | tf_op jit(solution)/shard_map/ppermute | solution.py:45
  83.1 1.8 collective-permute-start.9
  84.9 8.3 %convolution_bitcast_fusion = f32[512,1024]{1,0:T(8,128)} fusion(bf16[512,4096]{1,0:T(8,128)(2,1)S(1)} %bitcast.74, bf16[4096,1024]{1,0:T(8,128)(2,1)} %param.8), kind=kOutput, calls=%fused_computation.6 | convolution fusion | flops 4294967296 | bytes 14680064 | tf_op jit(solution)/shard_map/dot_general | solution.py:19
  93.2 1.9 add_add_fusion.1
  97.9 3.6 %all-to-all-start = ((bf16[4,64,4096]{2,1,0:T(8,128)(2,1)}), bf16[4,64,4096]{2,1,0:T(8,128)(2,1)S(1)}, u32[]{:S(2)}, u32[]{:S(2)}) async-start(bf16[4,64,4096]{2,1,0:T(8,128)(2,1)} %bitcast.75), calls=%async_computation | async-start | bytes 4194304 | tf_op jit(solution)/shard_map/all_to_all | solution.py:141
  101.5 2.9 %slice_select_fusion = f32[512,512]{1,0:T(8,128)} fusion(f32[512,1024]{1,0:T(8,128)} %convolution_bitcast_fusion, pred[]{:T(512)S(6)} %eq.227), kind=kLoop, calls=%fused_computation.32 | loop fusion | flops 262144 | bytes 3145729 | tf_op jit(solution)/shard_map/jit(_where)/select_n | solution.py:152
  105.1 3.6 %collective-permute-start.8 = (bf16[1024,256]{0,1:T(8,128)(2,1)S(1)}, bf16[1024,256]{0,1:T(8,128)(2,1)S(1)}, u32[]{:S(2)}, u32[]{:S(2)}) collective-permute-start(bf16[1024,256]{0,1:T(8,128)(2,1)S(1)} %copy-done.10), channel_id=1, source_target_pairs={{0,4},{12,8},{1,5},{13,9},{2,6},{14,10},{3,7},{15,11},{16,20},{28,... | collective-permute-start | bytes 1572872 | tf_op jit(solution)/shard_map/ppermute | solution.py:45
  108.8 2.0 collective-permute-start.17
  112.1 1.5 collective-permute-start.16
  113.6 3.6 %convolution_select_fusion = f32[128,512]{1,0:T(8,128)} fusion(bf16[4096,512]{1,0:T(8,128)(2,1)} %param.9, bf16[128,4224]{1,0:T(8,128)(2,1)S(1)} %bitcast.71, s32[512]{0:T(512)S(1)} %fusion.69, s32[128]{0:T(128)S(1)} %convert_reduce_fusion.1), kind=kOutput, calls=%fused_computation.19 | convolution fusion | flops 537001984 | bytes 5507584 | tf_op jit(solution)/shard_map/dot_general | solution.py:19
  117.2 3.8 %collective-permute-done.8 = bf16[1024,256]{0,1:T(8,128)(2,1)S(1)} collective-permute-done((bf16[1024,256]{0,1:T(8,128)(2,1)S(1)}, bf16[1024,256]{0,1:T(8,128)(2,1)S(1)}, u32[]{:S(2)}, u32[]{:S(2)}) %collective-permute-start.8) | collective-permute-done | bytes 524320 | tf_op jit(solution)/shard_map/ppermute | solution.py:45
  122.0 1.4 collective-permute-start.15
  124.4 1.5 collective-permute-start.22
  126.0 6.9 %collective-permute-done.17 = bf16[256,512]{1,0:T(8,128)(2,1)S(1)} collective-permute-done((bf16[256,512]{1,0:T(8,128)(2,1)S(1)}, bf16[256,512]{1,0:T(8,128)(2,1)S(1)}, u32[]{:S(2)}, u32[]{:S(2)}) %collective-permute-start.17) | collective-permute-done | bytes 262176 | tf_op jit(solution)/shard_map/ppermute | solution.py:45
  133.1 1.5 collective-permute-start.19
  134.6 5.0 %collective-permute-start.20 = (bf16[256,512]{1,0:T(8,128)(2,1)S(1)}, bf16[256,512]{1,0:T(8,128)(2,1)S(1)}, u32[]{:S(2)}, u32[]{:S(2)}) collective-permute-start(bf16[256,512]{1,0:T(8,128)(2,1)S(1)} %fusion.50), channel_id=1, source_target_pairs={{0,4},{12,8},{1,5},{13,9},{2,6},{14,10},{3,7},{15,11},{16,20},{28,... | collective-permute-start | bytes 786440 | tf_op jit(solution)/shard_map/ppermute | solution.py:45
  139.5 1.3 collective-permute-start.13
  140.9 1.3 collective-permute-start.14
  142.2 2.2 %add.312 = bf16[1024,256]{0,1:T(8,128)(2,1)} add(bf16[1024,256]{0,1:T(8,128)(2,1)} %add.300, bf16[1024,256]{0,1:T(8,128)(2,1)} %collective-permute-done.15) | non-fusion elementwise | flops 262144 | bytes 1572864 | tf_op jit(solution)/shard_map/add | solution.py:211
  144.3 1.5 collective-permute-start.12
  145.9 1.9 fusion.9
  150.1 1.4 collective-permute-start.24
  151.5 2.0 add.319
  153.5 9.5 %all-to-all-start.2 = ((bf16[16,8,512]{2,1,0:T(8,128)(2,1)}), bf16[16,8,512]{2,1,0:T(8,128)(2,1)}, u32[]{:S(2)}, u32[]{:S(2)}) async-start(bf16[16,8,512]{2,1,0:T(8,128)(2,1)} %fusion.9), calls=%async_computation.2 | async-start | bytes 262144 | tf_op jit(solution)/shard_map/all_to_all | solution.py:172
  164.2 1.3 collective-permute-start.21
  165.5 1.4 fusion.38
  166.9 1.7 collective-permute-done.14
  168.6 1.4 fusion.35
  169.9 10.6 %collective-permute-done.18 = bf16[1024,256]{0,1:T(8,128)(2,1)} collective-permute-done((bf16[1024,256]{0,1:T(8,128)(2,1)}, bf16[1024,256]{0,1:T(8,128)(2,1)}, u32[]{:S(2)}, u32[]{:S(2)}) %collective-permute-start.18) | collective-permute-done | bytes 524320 | tf_op jit(solution)/shard_map/ppermute | solution.py:45
  180.5 1.4 fusion.32
  181.9 8.3 %collective-permute-done.21 = bf16[1024,256]{0,1:T(8,128)(2,1)S(1)} collective-permute-done((bf16[1024,256]{0,1:T(8,128)(2,1)}, bf16[1024,256]{0,1:T(8,128)(2,1)S(1)}, u32[]{:S(2)}, u32[]{:S(2)}) %collective-permute-start.21) | collective-permute-done | bytes 524320 | tf_op jit(solution)/shard_map/ppermute | solution.py:45
  193.0 1.6 collective-permute-start.23
  197.5 6.5 %collective-permute-done.25 = bf16[256,512]{1,0:T(8,128)(2,1)S(1)} collective-permute-done((bf16[256,512]{1,0:T(8,128)(2,1)S(1)}, bf16[256,512]{1,0:T(8,128)(2,1)S(1)}, u32[]{:S(2)}, u32[]{:S(2)}) %collective-permute-start.25) | collective-permute-done | bytes 262176 | tf_op jit(solution)/shard_map/ppermute | solution.py:45
  204.9 3.4 %all-to-all-start.3 = ((bf16[4,64,512]{2,1,0:T(8,128)(2,1)}), bf16[4,64,512]{2,1,0:T(8,128)(2,1)S(1)}, u32[]{:S(2)}, u32[]{:S(2)}) async-start(bf16[4,64,512]{2,1,0:T(8,128)(2,1)} %bitcast.19), calls=%async_computation.3 | async-start | bytes 524288 | tf_op jit(solution)/shard_map/all_to_all | solution.py:245
  208.4 6.0 %all-to-all-done.3 = bf16[4,64,512]{2,1,0:T(8,128)(2,1)S(1)} async-done(((bf16[4,64,512]{2,1,0:T(8,128)(2,1)}), bf16[4,64,512]{2,1,0:T(8,128)(2,1)S(1)}, u32[]{:S(2)}, u32[]{:S(2)}) %all-to-all-start.3) | async-done | bytes 262176 | tf_op jit(solution)/shard_map/all_to_all | solution.py:245
  214.3 2.6 %add_convert_fusion = bf16[512,512]{1,0:T(8,128)(2,1)} fusion(f32[512,512]{1,0:T(8,128)} %collective-permute-done.12, f32[512,1024]{1,0:T(8,128)S(1)} %copy-done.8, pred[]{:T(512)S(6)} %eq.227, bf16[128,512]{1,0:T(8,128)(2,1)S(1)} %fusion.57, bf16[256,512]{1,0:T(8,128)(2,1)S(1)} %copy-done.19, bf16[128,512]{1,0:T(8,128)(2,1)} %bitcast.17, ...), kind=kOutput, calls=%fused_computation.24 | convolution fusion | flops 203948032 | bytes 4456449 | tf_op jit(solution)/shard_map/dot_general | solution.py:247
  (143 shorter events, 30.6 us)
Async XLA Ops:
  0.0 55.7 %copy-start = (bf16[512,512]{1,0:T(8,128)(2,1)S(1)}, bf16[512,512]{1,0:T(8,128)(2,1)}, u32[]{:S(2)}) copy-start(bf16[512,512]{1,0:T(8,128)(2,1)} %param.10) | copy-start | bytes 1572868
  4.0 5.3 %collective-permute-start = (bf16[1024,512]{0,1:T(8,128)(2,1)S(1)}, bf16[1024,512]{0,1:T(8,128)(2,1)S(1)}, u32[]{:S(2)}, u32[]{:S(2)}) collective-permute-start(bf16[1024,512]{0,1:T(8,128)(2,1)S(1)} %fusion.2), channel_id=1, source_target_pairs={{0,1},{1,0},{2,3},{3,2},{4,5},{5,4},{6,7},{7,6},{8,9},{9,8},{10,11... | collective-permute-start | bytes 3145736 | tf_op jit(solution)/shard_map/ppermute | solution.py:94
  4.6 4.8 %copy-start.5 = (bf16[4096,512]{1,0:T(8,128)(2,1)S(1)}, bf16[4096,512]{1,0:T(8,128)(2,1)}, u32[]{:S(2)}) copy-start(bf16[4096,512]{1,0:T(8,128)(2,1)} %param.9) | copy-start | bytes 12582916
  9.3 3.7 %copy-start.6 = (bf16[4096,512]{0,1:T(8,128)(2,1)}, bf16[4096,512]{0,1:T(8,128)(2,1)S(1)}, u32[]{:S(2)}) copy-start(bf16[4096,512]{0,1:T(8,128)(2,1)S(1)} %convolution_convert_fusion) | copy-start | bytes 12582916
  9.4 3.6 %copy-start.20 = (s32[4,128]{1,0:T(4,128)S(1)}, s32[4,128]{1,0:T(4,128)}, u32[]{:S(2)}) copy-start(s32[4,128]{1,0:T(4,128)} %param.12) | copy-start | bytes 6148
  9.4 4.8 %copy-start.3 = (bf16[4,128,4096]{2,1,0:T(8,128)(2,1)S(1)}, bf16[4,128,4096]{2,1,0:T(8,128)(2,1)}, u32[]{:S(2)}) copy-start(bf16[4,128,4096]{2,1,0:T(8,128)(2,1)} %param.7) | copy-start | bytes 12582916
  13.3 37.3 %collective-permute-start.2 = (bf16[3072,512]{0,1:T(8,128)(2,1)}, bf16[3072,512]{0,1:T(8,128)(2,1)}, u32[]{:S(2)}, u32[]{:S(2)}) collective-permute-start(bf16[3072,512]{0,1:T(8,128)(2,1)} %fusion), channel_id=1, source_target_pairs={{0,1},{1,0},{2,3},{3,2},{4,5},{5,4},{6,7},{7,6},{8,9},{9,8},{10,11... | collective-permute-start | bytes 9437192 | tf_op jit(solution)/shard_map/ppermute | solution.py:98
  16.1 34.4 %all-to-all-start.1 = ((bf16[16,8,4224]{2,1,0:T(8,128)(2,1)}), bf16[16,8,4224]{2,1,0:T(8,128)(2,1)S(1)}, u32[]{:S(2)}, u32[]{:S(2)}) async-start(bf16[16,8,4224]{2,1,0:T(8,128)(2,1)} %maximum_bitcast_fusion), calls=%async_computation.1 | async-start | bytes 2162688 | tf_op jit(solution)/shard_map/all_to_all | solution.py:124
  23.2 26.1 %collective-permute-start.1 = (bf16[1024,256]{0,1:T(8,128)(2,1)S(1)}, bf16[1024,256]{0,1:T(8,128)(2,1)}, u32[]{:S(2)}, u32[]{:S(2)}) collective-permute-start(bf16[1024,256]{0,1:T(8,128)(2,1)S(1)} %slice_add_fusion), channel_id=1, source_target_pairs={{0,2},{2,0},{1,3},{3,1},{4,6},{6,4},{5,7},{7,5},{8,10},{10,8},{9,1... | collective-permute-start | bytes 1572872 | tf_op jit(solution)/shard_map/ppermute | solution.py:45
  25.1 36.1 %copy-start.18 = (bf16[256,512]{1,0:T(8,128)(2,1)}, bf16[256,512]{1,0:T(8,128)(2,1)S(1)}, u32[]{:S(2)}) copy-start(bf16[256,512]{1,0:T(8,128)(2,1)S(1)} %fusion.24) | copy-start | bytes 786436
  50.5 10.7 %copy-start.1 = (bf16[16,8,4224]{2,1,0:T(8,128)(2,1)}, bf16[16,8,4224]{2,1,0:T(8,128)(2,1)S(1)}, u32[]{:S(2)}) copy-start(bf16[16,8,4224]{2,1,0:T(8,128)(2,1)S(1)} %all-to-all-done.1) | copy-start | bytes 3244036
  52.2 21.8 %collective-permute-start.3 = (bf16[1024,256]{0,1:T(8,128)(2,1)S(1)}, bf16[1024,256]{0,1:T(8,128)(2,1)S(1)}, u32[]{:S(2)}, u32[]{:S(2)}) collective-permute-start(bf16[1024,256]{0,1:T(8,128)(2,1)S(1)} %fusion.14), channel_id=1, source_target_pairs={{0,4},{12,8},{1,5},{13,9},{2,6},{14,10},{3,7},{15,11},{16,20},{28,... | collective-permute-start | bytes 1572872 | tf_op jit(solution)/shard_map/ppermute | solution.py:45
  54.6 13.4 %collective-permute-start.4 = (bf16[1024,256]{0,1:T(8,128)(2,1)S(1)}, bf16[1024,256]{0,1:T(8,128)(2,1)S(1)}, u32[]{:S(2)}, u32[]{:S(2)}) collective-permute-start(bf16[1024,256]{0,1:T(8,128)(2,1)S(1)} %slice_add_fusion.4), channel_id=1, source_target_pairs={{0,2},{2,0},{1,3},{3,1},{4,6},{6,4},{5,7},{7,5},{8,10},{10,8},{9,1... | collective-permute-start | bytes 1572872 | tf_op jit(solution)/shard_map/ppermute | solution.py:45
  56.2 40.1 %copy-start.12 = (bf16[512,512]{1,0:T(8,128)(2,1)}, bf16[512,512]{1,0:T(8,128)(2,1)S(1)}, u32[]{:S(2)}) copy-start(bf16[512,512]{1,0:T(8,128)(2,1)S(1)} %convolution_convert_fusion.5) | copy-start | bytes 1572868
  56.2 11.8 %copy-start.7 = (bf16[4096,512]{0,1:T(8,128)(2,1)S(1)}, bf16[4096,512]{0,1:T(8,128)(2,1)}, u32[]{:S(2)}) copy-start(bf16[4096,512]{0,1:T(8,128)(2,1)} %copy-done.6) | copy-start | bytes 12582916
  69.1 15.8 %copy-start.4 = (bf16[4,128,4096]{2,1,0:T(8,128)(2,1)S(1)}, bf16[4,128,4096]{2,1,0:T(8,128)(2,1)}, u32[]{:S(2)}) copy-start(bf16[4,128,4096]{2,1,0:T(8,128)(2,1)} %param.7) | copy-start | bytes 12582916
  69.1 12.9 %collective-permute-start.6 = (bf16[1024,256]{0,1:T(8,128)(2,1)S(1)}, bf16[1024,256]{0,1:T(8,128)(2,1)S(1)}, u32[]{:S(2)}, u32[]{:S(2)}) collective-permute-start(bf16[1024,256]{0,1:T(8,128)(2,1)S(1)} %slice_add_fusion.3), channel_id=1, source_target_pairs={{0,2},{2,0},{1,3},{3,1},{4,6},{6,4},{5,7},{7,5},{8,10},{10,8},{9,1... | collective-permute-start | bytes 1572872 | tf_op jit(solution)/shard_map/ppermute | solution.py:45
  72.4 22.8 %collective-permute-start.5 = (bf16[1024,256]{0,1:T(8,128)(2,1)S(1)}, bf16[1024,256]{0,1:T(8,128)(2,1)S(1)}, u32[]{:S(2)}, u32[]{:S(2)}) collective-permute-start(bf16[1024,256]{0,1:T(8,128)(2,1)S(1)} %add_add_fusion.2), channel_id=1, source_target_pairs={{0,4},{12,8},{1,5},{13,9},{2,6},{14,10},{3,7},{15,11},{16,20},{28,... | collective-permute-start | bytes 1572872 | tf_op jit(solution)/shard_map/ppermute | solution.py:45
  74.1 21.2 %collective-permute-start.11 = (bf16[1024,256]{0,1:T(8,128)(2,1)S(1)}, bf16[1024,256]{0,1:T(8,128)(2,1)S(1)}, u32[]{:S(2)}, u32[]{:S(2)}) collective-permute-start(bf16[1024,256]{0,1:T(8,128)(2,1)S(1)} %add.291), channel_id=1, source_target_pairs={{4,8},{8,4},{5,9},{9,5},{6,10},{10,6},{7,11},{11,7},{20,24},{24,20... | collective-permute-start | bytes 1572872 | tf_op jit(solution)/shard_map/ppermute | solution.py:45
  75.0 21.3 %collective-permute-start.10 = (bf16[512,512]{1,0:T(8,128)(2,1)S(1)}, bf16[512,512]{1,0:T(8,128)(2,1)S(1)}, u32[]{:S(2)}, u32[]{:S(2)}) collective-permute-start(bf16[512,512]{1,0:T(8,128)(2,1)S(1)} %convolution_convert_fusion.6), channel_id=1, source_target_pairs={{0,1},{1,0},{2,3},{3,2},{4,5},{5,4},{6,7},{7,6},{8,9},{9,8},{10,11... | collective-permute-start | bytes 1572872 | tf_op jit(solution)/shard_map/ppermute | solution.py:45
  83.1 13.3 %collective-permute-start.9 = (bf16[1024,256]{0,1:T(8,128)(2,1)S(1)}, bf16[1024,256]{0,1:T(8,128)(2,1)S(1)}, u32[]{:S(2)}, u32[]{:S(2)}) collective-permute-start(bf16[1024,256]{0,1:T(8,128)(2,1)S(1)} %slice_add_fusion.2), channel_id=1, source_target_pairs={{0,2},{2,0},{1,3},{3,1},{4,6},{6,4},{5,7},{7,5},{8,10},{10,8},{9,1... | collective-permute-start | bytes 1572872 | tf_op jit(solution)/shard_map/ppermute | solution.py:45
  97.9 55.6 %all-to-all-start = ((bf16[4,64,4096]{2,1,0:T(8,128)(2,1)}), bf16[4,64,4096]{2,1,0:T(8,128)(2,1)S(1)}, u32[]{:S(2)}, u32[]{:S(2)}) async-start(bf16[4,64,4096]{2,1,0:T(8,128)(2,1)} %bitcast.75), calls=%async_computation | async-start | bytes 4194304 | tf_op jit(solution)/shard_map/all_to_all | solution.py:141
  101.5 9.3 %copy-start.17 = (bf16[1024,256]{0,1:T(8,128)(2,1)S(1)}, bf16[1024,256]{0,1:T(8,128)(2,1)}, u32[]{:S(2)}) copy-start(bf16[1024,256]{0,1:T(8,128)(2,1)} %copy-done.16) | copy-start | bytes 1572868
  101.5 12.0 %copy-start.2 = (bf16[16,8,4224]{2,1,0:T(8,128)(2,1)S(1)}, bf16[16,8,4224]{2,1,0:T(8,128)(2,1)}, u32[]{:S(2)}) copy-start(bf16[16,8,4224]{2,1,0:T(8,128)(2,1)} %copy-done.1) | copy-start | bytes 3244036
  104.4 19.0 %collective-permute-start.7 = (bf16[1024,256]{0,1:T(8,128)(2,1)S(1)}, bf16[1024,256]{0,1:T(8,128)(2,1)S(1)}, u32[]{:S(2)}, u32[]{:S(2)}) collective-permute-start(bf16[1024,256]{0,1:T(8,128)(2,1)S(1)} %add.295), channel_id=1, source_target_pairs={{4,8},{8,4},{5,9},{9,5},{6,10},{10,6},{7,11},{11,7},{20,24},{24,20... | collective-permute-start | bytes 1572872 | tf_op jit(solution)/shard_map/ppermute | solution.py:45
  105.1 15.9 %collective-permute-start.8 = (bf16[1024,256]{0,1:T(8,128)(2,1)S(1)}, bf16[1024,256]{0,1:T(8,128)(2,1)S(1)}, u32[]{:S(2)}, u32[]{:S(2)}) collective-permute-start(bf16[1024,256]{0,1:T(8,128)(2,1)S(1)} %copy-done.10), channel_id=1, source_target_pairs={{0,4},{12,8},{1,5},{13,9},{2,6},{14,10},{3,7},{15,11},{16,20},{28,... | collective-permute-start | bytes 1572872 | tf_op jit(solution)/shard_map/ppermute | solution.py:45
  108.8 24.0 %collective-permute-start.17 = (bf16[256,512]{1,0:T(8,128)(2,1)S(1)}, bf16[256,512]{1,0:T(8,128)(2,1)S(1)}, u32[]{:S(2)}, u32[]{:S(2)}) collective-permute-start(bf16[256,512]{1,0:T(8,128)(2,1)S(1)} %slice_add_fusion.6), channel_id=1, source_target_pairs={{0,2},{2,0},{1,3},{3,1},{4,6},{6,4},{5,7},{7,5},{8,10},{10,8},{9,1... | collective-permute-start | bytes 786440 | tf_op jit(solution)/shard_map/ppermute | solution.py:45
  112.1 20.7 %copy-start.13 = (bf16[512,512]{1,0:T(8,128)(2,1)S(1)}, bf16[512,512]{1,0:T(8,128)(2,1)}, u32[]{:S(2)}) copy-start(bf16[512,512]{1,0:T(8,128)(2,1)} %copy-done.12) | copy-start | bytes 1572868
  112.1 20.7 %copy-start.15 = (bf16[512,512]{1,0:T(8,128)(2,1)S(1)}, bf16[512,512]{1,0:T(8,128)(2,1)}, u32[]{:S(2)}) copy-start(bf16[512,512]{1,0:T(8,128)(2,1)} %copy-done.14) | copy-start | bytes 1572868
  112.1 20.8 %collective-permute-start.16 = (bf16[1024,256]{0,1:T(8,128)(2,1)S(1)}, bf16[1024,256]{0,1:T(8,128)(2,1)S(1)}, u32[]{:S(2)}, u32[]{:S(2)}) collective-permute-start(bf16[1024,256]{0,1:T(8,128)(2,1)S(1)} %add_add_fusion), channel_id=1, source_target_pairs={{0,4},{12,8},{1,5},{13,9},{2,6},{14,10},{3,7},{15,11},{16,20},{28,... | collective-permute-start | bytes 1572872 | tf_op jit(solution)/shard_map/ppermute | solution.py:45
  122.0 18.8 %collective-permute-start.15 = (bf16[1024,256]{0,1:T(8,128)(2,1)}, bf16[1024,256]{0,1:T(8,128)(2,1)}, u32[]{:S(2)}, u32[]{:S(2)}) collective-permute-start(bf16[1024,256]{0,1:T(8,128)(2,1)} %add.300), channel_id=1, source_target_pairs={{4,8},{8,4},{5,9},{9,5},{6,10},{10,6},{7,11},{11,7},{20,24},{24,20... | collective-permute-start | bytes 1572872 | tf_op jit(solution)/shard_map/ppermute | solution.py:45
  124.4 19.9 %collective-permute-start.22 = (f32[128,512]{1,0:T(8,128)}, f32[128,512]{1,0:T(8,128)}, u32[]{:S(2)}, u32[]{:S(2)}) collective-permute-start(f32[128,512]{1,0:T(8,128)} %convolution_select_fusion), channel_id=1, source_target_pairs={{0,16},{16,0},{1,17},{17,1},{2,18},{18,2},{3,19},{19,3},{4,20},{20... | collective-permute-start | bytes 786440 | tf_op jit(solution)/shard_map/ppermute | solution.py:28
  132.9 14.9 %copy-start.11 = (bf16[256,512]{1,0:T(8,128)(2,1)}, bf16[256,512]{1,0:T(8,128)(2,1)S(1)}, u32[]{:S(2)}) copy-start(bf16[256,512]{1,0:T(8,128)(2,1)S(1)} %fusion.50) | copy-start | bytes 786436
  133.1 17.0 %collective-permute-start.19 = (bf16[1024,256]{0,1:T(8,128)(2,1)S(1)}, bf16[1024,256]{0,1:T(8,128)(2,1)}, u32[]{:S(2)}, u32[]{:S(2)}) collective-permute-start(bf16[1024,256]{0,1:T(8,128)(2,1)S(1)} %add.314), channel_id=1, source_target_pairs={{4,8},{8,4},{5,9},{9,5},{6,10},{10,6},{7,11},{11,7},{20,24},{24,20... | collective-permute-start | bytes 1572872 | tf_op jit(solution)/shard_map/ppermute | solution.py:45
  134.6 13.2 %collective-permute-start.20 = (bf16[256,512]{1,0:T(8,128)(2,1)S(1)}, bf16[256,512]{1,0:T(8,128)(2,1)S(1)}, u32[]{:S(2)}, u32[]{:S(2)}) collective-permute-start(bf16[256,512]{1,0:T(8,128)(2,1)S(1)} %fusion.50), channel_id=1, source_target_pairs={{0,4},{12,8},{1,5},{13,9},{2,6},{14,10},{3,7},{15,11},{16,20},{28,... | collective-permute-start | bytes 786440 | tf_op jit(solution)/shard_map/ppermute | solution.py:45
  139.5 24.6 %collective-permute-start.13 = (bf16[1024,256]{0,1:T(8,128)(2,1)}, bf16[1024,256]{0,1:T(8,128)(2,1)}, u32[]{:S(2)}, u32[]{:S(2)}) collective-permute-start(bf16[1024,256]{0,1:T(8,128)(2,1)} %add.307), channel_id=1, source_target_pairs={{4,0},{8,12},{5,1},{9,13},{6,2},{10,14},{7,3},{11,15},{20,16},{24,... | collective-permute-start | bytes 1572872 | tf_op jit(solution)/shard_map/ppermute | solution.py:45
  140.9 27.7 %collective-permute-start.14 = (bf16[1024,256]{0,1:T(8,128)(2,1)}, bf16[1024,256]{0,1:T(8,128)(2,1)}, u32[]{:S(2)}, u32[]{:S(2)}) collective-permute-start(bf16[1024,256]{0,1:T(8,128)(2,1)} %add.299), channel_id=1, source_target_pairs={{4,0},{8,12},{5,1},{9,13},{6,2},{10,14},{7,3},{11,15},{20,16},{24,... | collective-permute-start | bytes 1572872 | tf_op jit(solution)/shard_map/ppermute | solution.py:45
  144.3 48.7 %collective-permute-start.12 = (f32[512,512]{1,0:T(8,128)}, f32[512,512]{1,0:T(8,128)}, u32[]{:S(2)}, u32[]{:S(2)}) collective-permute-start(f32[512,512]{1,0:T(8,128)} %slice_select_fusion), channel_id=1, source_target_pairs={{0,16},{16,0},{1,17},{17,1},{2,18},{18,2},{3,19},{19,3},{4,20},{20... | collective-permute-start | bytes 3145736 | tf_op jit(solution)/shard_map/ppermute | solution.py:45
  147.8 32.7 %collective-permute-start.18 = (bf16[1024,256]{0,1:T(8,128)(2,1)}, bf16[1024,256]{0,1:T(8,128)(2,1)}, u32[]{:S(2)}, u32[]{:S(2)}) collective-permute-start(bf16[1024,256]{0,1:T(8,128)(2,1)} %add.312), channel_id=1, source_target_pairs={{4,0},{8,12},{5,1},{9,13},{6,2},{10,14},{7,3},{11,15},{20,16},{24,... | collective-permute-start | bytes 1572872 | tf_op jit(solution)/shard_map/ppermute | solution.py:45
  150.1 44.6 %collective-permute-start.24 = (bf16[256,512]{1,0:T(8,128)(2,1)S(1)}, bf16[256,512]{1,0:T(8,128)(2,1)}, u32[]{:S(2)}, u32[]{:S(2)}) collective-permute-start(bf16[256,512]{1,0:T(8,128)(2,1)S(1)} %add.321), channel_id=1, source_target_pairs={{4,8},{8,4},{5,9},{9,5},{6,10},{10,6},{7,11},{11,7},{20,24},{24,20... | collective-permute-start | bytes 786440 | tf_op jit(solution)/shard_map/ppermute | solution.py:45
  153.5 39.5 %all-to-all-start.2 = ((bf16[16,8,512]{2,1,0:T(8,128)(2,1)}), bf16[16,8,512]{2,1,0:T(8,128)(2,1)}, u32[]{:S(2)}, u32[]{:S(2)}) async-start(bf16[16,8,512]{2,1,0:T(8,128)(2,1)} %fusion.9), calls=%async_computation.2 | async-start | bytes 262144 | tf_op jit(solution)/shard_map/all_to_all | solution.py:172
  163.8 26.7 %copy-start.9 = (bf16[1024,256]{0,1:T(8,128)(2,1)S(1)}, bf16[1024,256]{0,1:T(8,128)(2,1)}, u32[]{:S(2)}) copy-start(bf16[1024,256]{0,1:T(8,128)(2,1)} %add.307) | copy-start | bytes 1572868
  164.2 26.0 %collective-permute-start.21 = (bf16[1024,256]{0,1:T(8,128)(2,1)}, bf16[1024,256]{0,1:T(8,128)(2,1)S(1)}, u32[]{:S(2)}, u32[]{:S(2)}) collective-permute-start(bf16[1024,256]{0,1:T(8,128)(2,1)} %add.319), channel_id=1, source_target_pairs={{4,0},{8,12},{5,1},{9,13},{6,2},{10,14},{7,3},{11,15},{20,16},{24,... | collective-permute-start | bytes 1572872 | tf_op jit(solution)/shard_map/ppermute | solution.py:45
  191.6 22.7 %copy-start.8 = (f32[512,1024]{1,0:T(8,128)S(1)}, f32[512,1024]{1,0:T(8,128)}, u32[]{:S(2)}) copy-start(f32[512,1024]{1,0:T(8,128)} %convolution_bitcast_fusion) | copy-start | bytes 6291460
  191.6 22.7 %copy-start.19 = (bf16[256,512]{1,0:T(8,128)(2,1)S(1)}, bf16[256,512]{1,0:T(8,128)(2,1)}, u32[]{:S(2)}) copy-start(bf16[256,512]{1,0:T(8,128)(2,1)} %copy-done.18) | copy-start | bytes 786436
  193.0 4.3 %collective-permute-start.23 = (f32[128,128]{1,0:T(8,128)S(1)}, f32[128,128]{1,0:T(8,128)S(1)}, u32[]{:S(2)}, u32[]{:S(2)}) collective-permute-start(f32[128,128]{1,0:T(8,128)S(1)} %bitcast.77), channel_id=1, source_target_pairs={{0,16},{16,0},{1,17},{17,1},{2,18},{18,2},{3,19},{19,3},{4,20},{20... | collective-permute-start | bytes 196616 | tf_op jit(solution)/shard_map/ppermute | solution.py:28
  195.7 8.3 %collective-permute-start.25 = (bf16[256,512]{1,0:T(8,128)(2,1)S(1)}, bf16[256,512]{1,0:T(8,128)(2,1)S(1)}, u32[]{:S(2)}, u32[]{:S(2)}) collective-permute-start(bf16[256,512]{1,0:T(8,128)(2,1)S(1)} %add.325), channel_id=1, source_target_pairs={{4,0},{8,12},{5,1},{9,13},{6,2},{10,14},{7,3},{11,15},{20,16},{24,... | collective-permute-start | bytes 786440 | tf_op jit(solution)/shard_map/ppermute | solution.py:45
  204.9 9.4 %all-to-all-start.3 = ((bf16[4,64,512]{2,1,0:T(8,128)(2,1)}), bf16[4,64,512]{2,1,0:T(8,128)(2,1)S(1)}, u32[]{:S(2)}, u32[]{:S(2)}) async-start(bf16[4,64,512]{2,1,0:T(8,128)(2,1)} %bitcast.19), calls=%async_computation.3 | async-start | bytes 524288 | tf_op jit(solution)/shard_map/all_to_all | solution.py:245
  (4 other events, 8.8 us)

commit v4 on v3

v4 whole, which is shorter than its diff:
```python
import jax
import jax.numpy as jnp
from jax import lax
from jax.sharding import Mesh, PartitionSpec as P

R = 64
CAP = 2
HCAP = 16
DP = ("z_high", "z_low", "x", "core")
GROUP = ("z_low", "x", "core")
SWAP = [(0, 1), (1, 0)]


def pick(flags):
    return flags.astype(jnp.bfloat16)


def matmul(a, b):
    return jnp.dot(a, b, preferred_element_type=jnp.float32)


def narrow(a, b):
    return matmul(a, b).astype(jnp.bfloat16)


def sum_over_tp(part):
    if lax.axis_size("tp") == 2:
        return part + lax.ppermute(part, "tp", SWAP)
    return lax.psum(part, "tp")


def after(value, *others):
    return lax.optimization_barrier((value, *others))[0]


class Chain:
    def __init__(self):
        self.last = None

    def hold(self, value):
        self.last = value if self.last is None else after(value, self.last)
        return self.last

    def permute(self, value, axis, pairs):
        return lax.ppermute(self.hold(value), axis, pairs)


def on_device(
    activations, value_weight, shrink_store, expand_store, adapter_row, token_adapter, hot_ids
):
    step_count, token_count, depth = activations.shape
    adapter_count = adapter_row.shape[0]
    hot_count = hot_ids.shape[1]
    per_dev = expand_store.shape[0] // R
    head_part = expand_store.shape[1]
    far_count = lax.axis_size("z_high")
    group_count = 8
    dp_count = far_count * group_count
    me = lax.axis_index(DP)
    z_at, x_at, core_at = lax.axis_index("z_low"), lax.axis_index("x"), lax.axis_index("core")
    none_code = adapter_count + hot_count
    rows = activations.reshape(step_count * token_count, depth)

    names = jnp.arange(adapter_count, dtype=jnp.int32)
    hot_row = jnp.sum(jnp.where(hot_ids[:, :, None] == names, adapter_row, 0), axis=-1)
    hot_first = jnp.where(hot_row // per_dev == me, (hot_row % per_dev) * R, -R * per_dev)
    column = jnp.arange(per_dev * R, dtype=jnp.int32)
    lane = jnp.arange(R, dtype=jnp.int32)
    entry = jnp.arange(hot_count, dtype=jnp.int32)
    near = step_count // 2

    def wanted(core):
        firsts = []
        for x in (x_at, 1 - x_at):
            of_steps = jnp.sum(jnp.where(entry == 2 * x + core, hot_first, 0), axis=1)
            firsts += [jnp.where(z_at == 0, of_steps[:near], of_steps[near:])]
            firsts += [jnp.where(z_at == 0, of_steps[near:], of_steps[:near])]
        return jnp.concatenate([(f[:, None] + lane).reshape(-1) for f in firsts])

    want_mine, want_other = wanted(core_at), wanted(1 - core_at)
    kept = near * R
    chunk_count = 4
    part = depth // chunk_count

    chain = Chain()
    pick_mine, pick_other = lax.optimization_barrier(
        (pick(column[:, None] == want_mine), pick(column[:, None] == want_other))
    )
    hops = [("x", SWAP), ("z_low", SWAP)]
    bit = 1
    while bit < far_count:
        hops.append(("z_high", [(i, i ^ bit) for i in range(far_count)]))
        bit *= 2

    def cut(block, c, first, last):
        return block[:, first * kept:last * kept] if c < chunk_count else block[first * kept:last * kept]

    swapped = [lax.ppermute(chain.hold(narrow(shrink_store[:part], pick_other)), "core", SWAP)]
    mine_all = narrow(after(shrink_store, chain.last), pick_mine)
    mine = [mine_all[:part]]
    rest = None
    got = {}
    held = {}

    def send(c, stage):
        if stage == 0:
            value = cut(mine[c], c, 2, 4) + cut(swapped[c], c, 2, 4)
        elif stage == 1:
            value = cut(mine[c], c, 1, 2) + cut(swapped[c], c, 1, 2) + cut(got[c, 0], c, 1, 2)
        elif stage == 2:
            value = cut(mine[c], c, 0, 1) + cut(swapped[c], c, 0, 1) + cut(got[c, 0], c, 0, 1) + got[c, 1]
            held[c] = value
        else:
            value = held[c] = held[c] + got[c, stage - 1]
        if c > 0:
            value = after(value, got[c - 1, stage])
        got[c, stage] = chain.permute(value, *hops[stage])

    send(0, 0)
    rest = lax.ppermute(chain.hold(narrow(shrink_store[part:], after(pick_other, chain.last))), "core", SWAP)

    token_adapter = after(token_adapter, chain.last)
    cold_row = jnp.sum(jnp.where((token_adapter - hot_count)[:, :, None] == names, adapter_row, 0), axis=-1)
    is_hot = token_adapter < hot_count
    is_cold = (token_adapter < none_code) & jnp.logical_not(is_hot)
    owner = cold_row // per_dev
    group = jnp.where(is_hot, token_adapter, jnp.where(is_cold, hot_count + owner, -1))
    at = jnp.arange(token_count, dtype=jnp.int32)
    before = (group[:, :, None] == group[:, None, :]) & (at[None, :] < at[:, None])
    rank = jnp.sum(before.astype(jnp.int32), axis=-1)
    step_at = jnp.arange(step_count, dtype=jnp.int32)[:, None]
    hot_rows = hot_count * step_count * HCAP
    cold_rows = dp_count * step_count * CAP
    hot_target = (((step_at // near) * hot_count + token_adapter) * near + step_at % near) * HCAP + rank
    cold_target = (owner * step_count + step_at) * CAP + rank
    hot_target = jnp.where(is_hot, hot_target, -1).reshape(-1)
    cold_target = jnp.where(is_cold, cold_target, -1).reshape(-1)
    place_hot = pick(jnp.arange(hot_rows, dtype=jnp.int32)[:, None] == hot_target)
    cold_hit = jnp.arange(cold_rows, dtype=jnp.int32)[:, None] == cold_target
    place_cold = pick(cold_hit)
    tag = jnp.sum(jnp.where(cold_hit, (cold_row % per_dev + 1).reshape(-1), 0), axis=-1)

    tag_out = jnp.broadcast_to(tag.astype(jnp.bfloat16)[:, None], (cold_rows, 128))
    packet = jnp.concatenate([narrow(place_cold, rows), tag_out], axis=1)
    packet = chain.hold(packet.reshape(dp_count, step_count * CAP, depth + 128))
    packet = lax.all_to_all(packet, DP, split_axis=0, concat_axis=0, tiled=True).reshape(cold_rows, depth + 128)

    done = {"hot_out": narrow(after(place_hot, chain.last), rows)}

    def expand_pick():
        late_mine, late_other = after(want_mine, chain.last), after(want_other, chain.last)
        done["expand_other"] = narrow(pick(late_other[:, None] == column), expand_store)
        done["expand_mine"] = narrow(pick(late_mine[:, None] == column), expand_store)

    def expand_over_core():
        done["expand_swapped"] = chain.permute(done["expand_other"], "core", SWAP)

    def hot_tokens_out():
        hot_out = chain.hold(done["hot_out"].reshape(group_count, near * HCAP, depth))
        hot_in = lax.all_to_all(hot_out, GROUP, split_axis=0, concat_axis=0, tiled=True)
        done["hot_in"] = hot_in.reshape(hot_rows, depth)

    def base_product():
        done["whole"] = matmul(rows, after(value_weight, chain.last))

    def base_over_tp():
        whole = done["whole"]
        if lax.axis_size("tp") == 2:
            first = lax.axis_index("tp") == 0
            halves = whole[:, :head_part], whole[:, head_part:]
            other = jnp.where(first, halves[1], halves[0])
            done["base"] = jnp.where(first, *halves), chain.permute(other, "tp", SWAP)
        else:
            base = lax.psum_scatter(chain.hold(whole), "tp", scatter_dimension=1, tiled=True)
            done["base"] = base, jnp.zeros_like(base)

    def cold_shrink():
        tag_in = packet[:, depth:depth + 1].astype(jnp.int32)
        chosen = (column // R + 1)[None, :] == tag_in
        product = matmul(packet[:, :depth], after(shrink_store, chain.last))
        done["z_part"] = jnp.where(chosen, product, 0.0)

    def cold_over_tp():
        done["z_cold"] = sum_over_tp(chain.hold(done["z_part"]))

    def cold_expand():
        done["delta"] = narrow(done["z_cold"].astype(jnp.bfloat16), after(expand_store, chain.last))

    def cold_back():
        delta = chain.hold(done["delta"].reshape(dp_count, step_count * CAP, head_part))
        delta = lax.all_to_all(delta, DP, split_axis=0, concat_axis=0, tiled=True)
        done["delta_cold"] = delta.reshape(cold_rows, head_part)

    between = {
        (1, "end"): [expand_pick, base_product],
        (2, "end"): [expand_over_core, cold_shrink],
        (3, "end"): [base_over_tp, cold_over_tp],
        (4, "x"): [hot_tokens_out],
        (4, "end"): [cold_expand],
        (5, "end"): [cold_back],
    }
    for slot in range(1, chunk_count + 1 + len(hops) - 1):
        c = slot
        if c < chunk_count:
            mine.append(after(mine_all, got[c - 1, 0])[c * part:(c + 1) * part])
            swapped.append(after(rest, got[c - 1, 0])[(c - 1) * part:c * part])
        elif c == chunk_count:
            mine.append(done["expand_mine"])
            swapped.append(done["expand_swapped"])
        for stage in range(len(hops)):
            if 0 <= slot - stage <= chunk_count:
                send(slot - stage, stage)
            if stage == 0:
                for work in between.get((slot, "x"), []):
                    work()
        for work in between.get((slot, "end"), []):
            work()
    *shrink_hot, expand_hot = [(held[c], got[c, len(hops) - 1]) for c in range(chunk_count + 1)]
    expand_hot = expand_hot[0] + expand_hot[1]
    hot_in, delta_cold = done["hot_in"], done["delta_cold"]
    base_kept, base_got = done["base"]

    dense = None
    for c, pieces in enumerate(shrink_hot):
        for piece in pieces:
            product = matmul(hot_in[:, c * part:(c + 1) * part], piece)
            dense = product if dense is None else dense + product
    dense = dense.reshape(group_count, near, HCAP, kept)
    at_step = jnp.arange(kept) // R
    z_part = sum(jnp.where(at_step == i, dense[:, i], 0.0) for i in range(near))
    z_part = after(z_part.reshape(group_count * HCAP, kept), delta_cold, base_got)
    z_hot = sum_over_tp(z_part).astype(jnp.bfloat16).reshape(group_count, 1, HCAP, kept)
    same_step = jnp.arange(near)[:, None, None] == at_step
    spread = jnp.where(same_step, z_hot, jnp.zeros((), jnp.bfloat16)).reshape(hot_rows, kept)
    delta_hot = narrow(spread, expand_hot).reshape(group_count, near * HCAP, head_part)
    delta_hot = lax.all_to_all(delta_hot, GROUP, split_axis=0, concat_axis=0, tiled=True)

    delta = lax.dot_general(
        jnp.concatenate([place_hot, place_cold], axis=0),
        jnp.concatenate([delta_hot.reshape(hot_rows, head_part), delta_cold], axis=0),
        (((0,), (0,)), ((), ())),
        preferred_element_type=jnp.float32,
    )
    return (base_kept + base_got + delta).astype(jnp.bfloat16).reshape(step_count, token_count, head_part)


def solution(mesh):
    tp_count, dp_count = mesh.shape["tp"], mesh.shape["dp"]
    fine = Mesh(mesh.devices.reshape(tp_count, dp_count // 8, 2, 2, 2), ("tp", *DP))
    placed = (
        P(None, DP, "tp"),
        P("tp", None),
        P("tp", DP),
        P(DP, "tp"),
        P(),
        P(None, DP),
        P(),
    )
    return jax.shard_map(
        on_device, mesh=fine, in_specs=placed, out_specs=P(None, DP, "tp"), check_vma=False
    )
```

time: 218 us -> 198 us (0.908)
  starting transfers between devices: 63.8 us -> 41.6 us
  waiting for transfers between devices: 81.8 us -> 90.8 us
  matrix products: 40.9 us -> 36.9 us
  other arithmetic: 25.8 us -> 22.3 us
    ppermute x22 -> x17, starting transfers between devices: 36.4 us -> 19.6 us  [permute(): return lax.ppermute(self.hold(value), axis, pairs)]
    ppermute x22 -> x17, waiting for transfers between devices: 75.5 us -> 83.7 us  [permute(): return lax.ppermute(self.hold(value), axis, pairs)]
    all_to_all x1, starting transfers between devices: 9.55 us -> 4.17 us  [cold_back(): delta = lax.all_to_all(delta, DP, split_axis=0, concat_axis=0, tiled=True)]
    dot_general x19, matrix products: 38.3 us -> 33.8 us  [matmul(): return jnp.dot(a, b, preferred_element_type=jnp.float32)]
    unnamed x46 -> x54, local copies, waits for them, and re-layouts: 2.01 us -> 4.39 us
    add x22 -> x24, other arithmetic: 19.4 us -> 17.5 us  [the longest x5 6.68 us: send(): cut(mine[c], c, 1, 2) + cut(swapped[c], c, 1, 2) + cut(got[c, 0], c, 1, 2)]
  transfers between devices with their start and end apart: 30 -> 25, of which waited for: 11 -> 11; matrix products, arithmetic and copies ran while one was open for 26% -> 23% of each run, Pallas kernels for 0% -> 0%
where the time goes in v4:
time: 198 us; the launch traced here: 197 us
  waiting for transfers between devices  90.8 us (46%)
  starting transfers between devices  41.6 us (21%)
  matrix products  36.9 us (19%)
  other arithmetic  22.3 us (11%)
  local copies, waits for them, and re-layouts  5.19 us (3%)
    ppermute x17, waiting for transfers between devices, permute(): return lax.ppermute(self.hold(value), axis, pairs)  83.7 us
    dot_general x19, matrix products, matmul(): return jnp.dot(a, b, preferred_element_type=jnp.float32)  33.8 us
    ppermute x17, starting transfers between devices, permute(): return lax.ppermute(self.hold(value), axis, pairs)  19.6 us
    all_to_all x1, starting transfers between devices, on_device(): lax.all_to_all(packet, DP, split_axis=0, concat_axis=0, tiled=True)  7.03 us
    add x5, other arithmetic, send(): cut(mine[c], c, 1, 2) + cut(swapped[c], c, 1, 2) + cut(got[c, 0], c, 1, 2)  6.68 us
    all_to_all x1, waiting for transfers between devices, on_device(): lax.all_to_all(delta_hot, GROUP, split_axis=0, concat_axis=0, tiled=True)  5.94 us
    add x5, other arithmetic, send(): cut(mine[c], c, 0, 1) + cut(swapped[c], c, 0, 1) + cut(got[c, 0], c, 0, 1)  5.67 us
    add x5, other arithmetic, send(): value = cut(mine[c], c, 2, 4) + cut(swapped[c], c, 2, 4)  4.54 us
  transfers between devices with their start and end apart: 25, of which 11 were waited for; matrix products, arithmetic and copies ran while one was open for 23% of the time, Pallas kernels for 0%

profile of v4, /device:TPU:0, one launch (start us, length us, event | category | flops | bytes accessed | tf_op | source)
XLA Modules:
  0.0 197.5 jit_solution(11168808077185100293)
XLA Ops:
  3.0 2.0 %fusion.2 = bf16[1024,512]{0,1:T(8,128)(2,1)S(1)} fusion(bf16[512,512]{1,0:T(8,128)(2,1)S(1)} %fusion.13, bf16[4096,512]{1,0:T(8,128)(2,1)} %param.9), kind=kOutput, calls=%fused_computation.8 | convolution fusion | flops 537395200 | bytes 2621440 | tf_op jit(solution)/shard_map/dot_general | solution.py:19
  5.6 4.7 %convolution_convert_fusion = bf16[4096,512]{0,1:T(8,128)(2,1)S(1)} fusion(bf16[4096,512]{1,0:T(8,128)(2,1)} %param.9, bf16[512,512]{1,0:T(8,128)(2,1)S(1)} %fusion.12), kind=kOutput, calls=%fused_computation | convolution fusion | flops 2149580800 | bytes 8912896 | tf_op jit(solution)/shard_map/dot_general | solution.py:19
  10.4 3.6 %fusion = bf16[3072,512]{0,1:T(8,128)(2,1)} fusion(bf16[512,512]{1,0:T(8,128)(2,1)S(1)} %fusion.13, bf16[4096,512]{1,0:T(8,128)(2,1)S(1)} %copy-done.4), kind=kOutput, calls=%fused_computation.4 | convolution fusion | flops 1612185600 | bytes 6815744 | tf_op jit(solution)/shard_map/dot_general | solution.py:19
  16.3 1.1 maximum_bitcast_fusion
  17.4 7.0 %all-to-all-start = ((bf16[16,8,4224]{2,1,0:T(8,128)(2,1)}), bf16[16,8,4224]{2,1,0:T(8,128)(2,1)S(1)}, u32[]{:S(2)}, u32[]{:S(2)}) async-start(bf16[16,8,4224]{2,1,0:T(8,128)(2,1)} %maximum_bitcast_fusion), calls=%async_computation | async-start | bytes 2162688 | tf_op jit(solution)/shard_map/all_to_all | solution.py:146
  24.4 2.0 collective-permute-start.1
  26.5 4.9 %convolution_convert_fusion.1 = bf16[256,4096]{1,0:T(8,128)(2,1)} fusion(bf16[256,512]{1,0:T(8,128)(2,1)S(1)} %fusion.16, bf16[512,4096]{1,0:T(8,128)(2,1)} %bitcast.61), kind=kOutput, calls=%fused_computation.1 | convolution fusion | flops 1074790400 | bytes 6553600 | tf_op jit(solution)/shard_map/dot_general | solution.py:19
  31.4 19.0 %collective-permute-done.1 = bf16[1024,256]{0,1:T(8,128)(2,1)S(1)} collective-permute-done((bf16[1024,256]{0,1:T(8,128)(2,1)S(1)}, bf16[1024,256]{0,1:T(8,128)(2,1)S(1)}, u32[]{:S(2)}, u32[]{:S(2)}) %collective-permute-start.1) | collective-permute-done | bytes 524320 | tf_op jit(solution)/shard_map/ppermute | solution.py:45
  52.3 1.3 slice_add_fusion.3
  54.8 8.1 %convolution_bitcast_fusion = f32[512,1024]{1,0:T(8,128)S(1)} fusion(bf16[512,4096]{1,0:T(8,128)(2,1)} %bitcast.62, bf16[4096,1024]{1,0:T(8,128)(2,1)} %param.8), kind=kOutput, calls=%fused_computation.6 | convolution fusion | flops 4294967296 | bytes 14680064 | tf_op jit(solution)/shard_map/dot_general | solution.py:19
  62.9 1.2 slice_select_fusion
  65.2 1.3 copy-done.2
  66.5 1.3 fusion.43
  67.9 1.1 slice_add_fusion.2
  69.0 1.5 collective-permute-start.7
  71.5 1.6 collective-permute-start.5
  73.1 1.9 collective-permute-start.6
  75.7 7.0 %collective-permute-done.7 = bf16[1024,256]{0,1:T(8,128)(2,1)S(1)} collective-permute-done((bf16[1024,256]{0,1:T(8,128)(2,1)S(1)}, bf16[1024,256]{0,1:T(8,128)(2,1)S(1)}, u32[]{:S(2)}, u32[]{:S(2)}) %collective-permute-start.7) | collective-permute-done | bytes 524320 | tf_op jit(solution)/shard_map/ppermute | solution.py:45
  82.6 1.3 slice_add_fusion.1
  85.6 1.8 slice_add_fusion.8
  88.2 8.5 %collective-permute-done.10 = bf16[1024,256]{0,1:T(8,128)(2,1)S(1)} collective-permute-done((bf16[1024,256]{0,1:T(8,128)(2,1)S(1)}, bf16[1024,256]{0,1:T(8,128)(2,1)S(1)}, u32[]{:S(2)}, u32[]{:S(2)}) %collective-permute-start.10) | collective-permute-done | bytes 524320 | tf_op jit(solution)/shard_map/ppermute | solution.py:45
  97.5 3.6 %all-to-all-start.1 = ((bf16[8,32,4096]{2,1,0:T(8,128)(2,1)}), bf16[8,32,4096]{2,1,0:T(8,128)(2,1)S(1)}, u32[]{:S(2)}, u32[]{:S(2)}) async-start(bf16[8,32,4096]{2,1,0:T(8,128)(2,1)} %bitcast.72), calls=%async_computation.1 | async-start | bytes 4194304 | tf_op jit(solution)/shard_map/all_to_all | solution.py:160
  101.1 2.0 %collective-permute-start.12 = (bf16[1024,128]{0,1:T(8,128)(2,1)}, bf16[1024,128]{0,1:T(8,128)(2,1)S(1)}, u32[]{:S(2)}, u32[]{:S(2)}) collective-permute-start(bf16[1024,128]{0,1:T(8,128)(2,1)} %slice_add_fusion.8), channel_id=1, source_target_pairs={{0,4},{4,0},{1,5},{5,1},{2,6},{6,2},{3,7},{7,3},{8,12},{12,8},{9,1... | collective-permute-start | bytes 786440 | tf_op jit(solution)/shard_map/ppermute | solution.py:45
  103.1 2.0 %collective-permute-start.11 = (bf16[1024,128]{0,1:T(8,128)(2,1)S(1)}, bf16[1024,128]{0,1:T(8,128)(2,1)}, u32[]{:S(2)}, u32[]{:S(2)}) collective-permute-start(bf16[1024,128]{0,1:T(8,128)(2,1)S(1)} %fusion.44), channel_id=1, source_target_pairs={{0,8},{8,0},{1,9},{9,1},{2,10},{10,2},{3,11},{11,3},{4,12},{12,4},... | collective-permute-start | bytes 786440 | tf_op jit(solution)/shard_map/ppermute | solution.py:45
  105.1 1.5 collective-permute-start.17
  107.1 30.9 %collective-permute-done.12 = bf16[1024,128]{0,1:T(8,128)(2,1)S(1)} collective-permute-done((bf16[1024,128]{0,1:T(8,128)(2,1)}, bf16[1024,128]{0,1:T(8,128)(2,1)S(1)}, u32[]{:S(2)}, u32[]{:S(2)}) %collective-permute-start.12) | collective-permute-done | bytes 262176 | tf_op jit(solution)/shard_map/ppermute | solution.py:45
  138.0 1.2 fusion.42
  139.2 1.5 collective-permute-start.15
  140.7 1.1 slice_add_fusion.5
  142.7 1.7 collective-permute-start.13
  145.4 2.0 collective-permute-done.15
  147.3 1.7 slice_add_fusion.17
  149.1 4.9 %collective-permute-done.14 = bf16[1024,128]{0,1:T(8,128)(2,1)S(1)} collective-permute-done((bf16[1024,128]{0,1:T(8,128)(2,1)S(1)}, bf16[1024,128]{0,1:T(8,128)(2,1)S(1)}, u32[]{:S(2)}, u32[]{:S(2)}) %collective-permute-start.14) | collective-permute-done | bytes 262176 | tf_op jit(solution)/shard_map/ppermute | solution.py:45
  154.0 1.1 fusion.41
  155.1 1.6 collective-permute-done.13
  157.4 1.8 collective-permute-start.16
  159.2 4.2 %all-to-all-start.2 = ((bf16[16,8,512]{2,1,0:T(8,128)(2,1)}), bf16[16,8,512]{2,1,0:T(8,128)(2,1)}, u32[]{:S(2)}, u32[]{:S(2)}) async-start(bf16[16,8,512]{2,1,0:T(8,128)(2,1)} %fusion.3), calls=%async_computation.2 | async-start | bytes 262144 | tf_op jit(solution)/shard_map/all_to_all | solution.py:191
  163.7 1.2 fusion.23
  165.3 1.2 fusion.29
  166.5 1.2 fusion.25
  168.1 4.1 %collective-permute-done.16 = bf16[1024,128]{0,1:T(8,128)(2,1)} collective-permute-done((bf16[1024,128]{0,1:T(8,128)(2,1)S(1)}, bf16[1024,128]{0,1:T(8,128)(2,1)}, u32[]{:S(2)}, u32[]{:S(2)}) %collective-permute-start.16) | collective-permute-done | bytes 262176 | tf_op jit(solution)/shard_map/ppermute | solution.py:45
  172.2 1.2 fusion.17
  173.9 1.6 collective-permute-start.18
  177.1 1.1 collective-permute-done.18
  178.2 5.8 %collective-permute-done.20 = bf16[128,512]{1,0:T(8,128)(2,1)S(1)} collective-permute-done((bf16[128,512]{1,0:T(8,128)(2,1)S(1)}, bf16[128,512]{1,0:T(8,128)(2,1)S(1)}, u32[]{:S(2)}, u32[]{:S(2)}) %collective-permute-start.20) | collective-permute-done | bytes 131104 | tf_op jit(solution)/shard_map/ppermute | solution.py:45
  184.9 3.4 %all-to-all-start.3 = ((bf16[8,32,512]{2,1,0:T(8,128)(2,1)}), bf16[8,32,512]{2,1,0:T(8,128)(2,1)S(1)}, u32[]{:S(2)}, u32[]{:S(2)}) async-start(bf16[8,32,512]{2,1,0:T(8,128)(2,1)} %bitcast.18), calls=%async_computation.3 | async-start | bytes 524288 | tf_op jit(solution)/shard_map/all_to_all | solution.py:236
  188.4 5.9 %all-to-all-done.3 = bf16[8,32,512]{2,1,0:T(8,128)(2,1)S(1)} async-done(((bf16[8,32,512]{2,1,0:T(8,128)(2,1)}), bf16[8,32,512]{2,1,0:T(8,128)(2,1)S(1)}, u32[]{:S(2)}, u32[]{:S(2)}) %all-to-all-start.3) | async-done | bytes 262176 | tf_op jit(solution)/shard_map/all_to_all | solution.py:236
  194.3 3.2 %add_convert_fusion = bf16[512,512]{1,0:T(8,128)(2,1)} fusion(f32[512,512]{1,0:T(8,128)} %collective-permute-done.8, f32[512,1024]{1,0:T(8,128)} %copy-done.6, pred[]{:T(512)S(6)} %eq.212, bf16[128,512]{1,0:T(8,128)(2,1)S(1)} %fusion.45, bf16[256,512]{1,0:T(8,128)(2,1)S(1)} %copy-done.17, bf16[128,512]{1,0:T(8,128)(2,1)} %bitcast.15, ...), kind=kOutput, calls=%fused_computation.24 | convolution fusion | flops 203948032 | bytes 4456449 | tf_op jit(solution)/shard_map/dot_general | solution.py:238
  (145 shorter events, 21.8 us)
Async XLA Ops:
  0.0 64.2 %copy-start = (bf16[512,512]{1,0:T(8,128)(2,1)S(1)}, bf16[512,512]{1,0:T(8,128)(2,1)}, u32[]{:S(2)}) copy-start(bf16[512,512]{1,0:T(8,128)(2,1)} %param.10) | copy-start | bytes 1572868
  5.0 5.3 %collective-permute-start = (bf16[1024,512]{0,1:T(8,128)(2,1)S(1)}, bf16[1024,512]{0,1:T(8,128)(2,1)S(1)}, u32[]{:S(2)}, u32[]{:S(2)}) collective-permute-start(bf16[1024,512]{0,1:T(8,128)(2,1)S(1)} %fusion.2), channel_id=1, source_target_pairs={{0,1},{1,0},{2,3},{3,2},{4,5},{5,4},{6,7},{7,6},{8,9},{9,8},{10,11... | collective-permute-start | bytes 3145736 | tf_op jit(solution)/shard_map/ppermute | solution.py:98
  5.6 4.8 %copy-start.4 = (bf16[4096,512]{1,0:T(8,128)(2,1)S(1)}, bf16[4096,512]{1,0:T(8,128)(2,1)}, u32[]{:S(2)}) copy-start(bf16[4096,512]{1,0:T(8,128)(2,1)} %param.9) | copy-start | bytes 12582916
  10.3 3.8 %copy-start.1 = (bf16[4096,512]{0,1:T(8,128)(2,1)}, bf16[4096,512]{0,1:T(8,128)(2,1)S(1)}, u32[]{:S(2)}) copy-start(bf16[4096,512]{0,1:T(8,128)(2,1)S(1)} %convolution_convert_fusion) | copy-start | bytes 12582916
  10.3 40.0 %copy-start.7 = (bf16[1024,512]{0,1:T(8,128)(2,1)}, bf16[1024,512]{0,1:T(8,128)(2,1)S(1)}, u32[]{:S(2)}) copy-start(bf16[1024,512]{0,1:T(8,128)(2,1)S(1)} %collective-permute-done) | copy-start | bytes 3145732
  10.4 3.7 %copy-start.19 = (s32[4,128]{1,0:T(4,128)S(1)}, s32[4,128]{1,0:T(4,128)}, u32[]{:S(2)}) copy-start(s32[4,128]{1,0:T(4,128)} %param.12) | copy-start | bytes 6148
  10.4 3.6 %copy-start.20 = (s32[128]{0:T(128)S(1)}, s32[128]{0:T(128)}, u32[]{:S(2)}) copy-start(s32[128]{0:T(128)} %param.11) | copy-start | bytes 1540
  10.4 5.0 %copy-start.3 = (bf16[4,128,4096]{2,1,0:T(8,128)(2,1)S(1)}, bf16[4,128,4096]{2,1,0:T(8,128)(2,1)}, u32[]{:S(2)}) copy-start(bf16[4,128,4096]{2,1,0:T(8,128)(2,1)} %param.7) | copy-start | bytes 12582916
  14.4 37.9 %collective-permute-start.2 = (bf16[3072,512]{0,1:T(8,128)(2,1)}, bf16[3072,512]{0,1:T(8,128)(2,1)}, u32[]{:S(2)}, u32[]{:S(2)}) collective-permute-start(bf16[3072,512]{0,1:T(8,128)(2,1)} %fusion), channel_id=1, source_target_pairs={{0,1},{1,0},{2,3},{3,2},{4,5},{5,4},{6,7},{7,6},{8,9},{9,8},{10,11... | collective-permute-start | bytes 9437192 | tf_op jit(solution)/shard_map/ppermute | solution.py:120
  17.4 34.8 %all-to-all-start = ((bf16[16,8,4224]{2,1,0:T(8,128)(2,1)}), bf16[16,8,4224]{2,1,0:T(8,128)(2,1)S(1)}, u32[]{:S(2)}, u32[]{:S(2)}) async-start(bf16[16,8,4224]{2,1,0:T(8,128)(2,1)} %maximum_bitcast_fusion), calls=%async_computation | async-start | bytes 2162688 | tf_op jit(solution)/shard_map/all_to_all | solution.py:146
  24.4 25.9 %collective-permute-start.1 = (bf16[1024,256]{0,1:T(8,128)(2,1)S(1)}, bf16[1024,256]{0,1:T(8,128)(2,1)S(1)}, u32[]{:S(2)}, u32[]{:S(2)}) collective-permute-start(bf16[1024,256]{0,1:T(8,128)(2,1)S(1)} %slice_add_fusion), channel_id=1, source_target_pairs={{0,2},{2,0},{1,3},{3,1},{4,6},{6,4},{5,7},{7,5},{8,10},{10,8},{9,1... | collective-permute-start | bytes 1572872 | tf_op jit(solution)/shard_map/ppermute | solution.py:45
  26.5 4.9 %copy-start.16 = (bf16[256,512]{1,0:T(8,128)(2,1)}, bf16[256,512]{1,0:T(8,128)(2,1)S(1)}, u32[]{:S(2)}) copy-start(bf16[256,512]{1,0:T(8,128)(2,1)S(1)} %fusion.16) | copy-start | bytes 786436
  50.4 0.8 copy-start.13
  53.6 14.3 %collective-permute-start.3 = (bf16[1024,256]{0,1:T(8,128)(2,1)S(1)}, bf16[1024,256]{0,1:T(8,128)(2,1)S(1)}, u32[]{:S(2)}, u32[]{:S(2)}) collective-permute-start(bf16[1024,256]{0,1:T(8,128)(2,1)S(1)} %slice_add_fusion.3), channel_id=1, source_target_pairs={{0,2},{2,0},{1,3},{3,1},{4,6},{6,4},{5,7},{7,5},{8,10},{10,8},{9,1... | collective-permute-start | bytes 1572872 | tf_op jit(solution)/shard_map/ppermute | solution.py:45
  54.0 11.2 %collective-permute-start.4 = (bf16[1024,128]{0,1:T(8,128)(2,1)S(1)}, bf16[1024,128]{0,1:T(8,128)(2,1)S(1)}, u32[]{:S(2)}, u32[]{:S(2)}) collective-permute-start(bf16[1024,128]{0,1:T(8,128)(2,1)S(1)} %slice_add_fusion.13), channel_id=1, source_target_pairs={{0,4},{4,0},{1,5},{5,1},{2,6},{6,2},{3,7},{7,3},{8,12},{12,8},{9,1... | collective-permute-start | bytes 786440 | tf_op jit(solution)/shard_map/ppermute | solution.py:45
  62.9 5.0 %copy-start.6 = (f32[512,1024]{1,0:T(8,128)}, f32[512,1024]{1,0:T(8,128)S(1)}, u32[]{:S(2)}) copy-start(f32[512,1024]{1,0:T(8,128)S(1)} %convolution_bitcast_fusion) | copy-start | bytes 6291460
  62.9 3.5 %copy-start.2 = (bf16[4096,512]{0,1:T(8,128)(2,1)S(1)}, bf16[4096,512]{0,1:T(8,128)(2,1)}, u32[]{:S(2)}) copy-start(bf16[4096,512]{0,1:T(8,128)(2,1)} %copy-done.1) | copy-start | bytes 12582916
  62.9 3.6 %copy-start.14 = (bf16[1024,256]{0,1:T(8,128)(2,1)S(1)}, bf16[1024,256]{0,1:T(8,128)(2,1)}, u32[]{:S(2)}) copy-start(bf16[1024,256]{0,1:T(8,128)(2,1)} %copy-done.13) | copy-start | bytes 1572868
  64.2 10.8 %copy-start.5 = (bf16[4096,512]{1,0:T(8,128)(2,1)S(1)}, bf16[4096,512]{1,0:T(8,128)(2,1)}, u32[]{:S(2)}) copy-start(bf16[4096,512]{1,0:T(8,128)(2,1)} %param.9) | copy-start | bytes 12582916
  65.1 22.2 %copy-start.8 = (bf16[512,512]{1,0:T(8,128)(2,1)}, bf16[512,512]{1,0:T(8,128)(2,1)S(1)}, u32[]{:S(2)}) copy-start(bf16[512,512]{1,0:T(8,128)(2,1)S(1)} %convolution_convert_fusion.5) | copy-start | bytes 1572868
  69.0 13.6 %collective-permute-start.7 = (bf16[1024,256]{0,1:T(8,128)(2,1)S(1)}, bf16[1024,256]{0,1:T(8,128)(2,1)S(1)}, u32[]{:S(2)}, u32[]{:S(2)}) collective-permute-start(bf16[1024,256]{0,1:T(8,128)(2,1)S(1)} %slice_add_fusion.2), channel_id=1, source_target_pairs={{0,2},{2,0},{1,3},{3,1},{4,6},{6,4},{5,7},{7,5},{8,10},{10,8},{9,1... | collective-permute-start | bytes 1572872 | tf_op jit(solution)/shard_map/ppermute | solution.py:45
  71.5 13.1 %collective-permute-start.5 = (bf16[1024,128]{0,1:T(8,128)(2,1)S(1)}, bf16[1024,128]{0,1:T(8,128)(2,1)S(1)}, u32[]{:S(2)}, u32[]{:S(2)}) collective-permute-start(bf16[1024,128]{0,1:T(8,128)(2,1)S(1)} %slice_add_fusion.11), channel_id=1, source_target_pairs={{0,4},{4,0},{1,5},{5,1},{2,6},{6,2},{3,7},{7,3},{8,12},{12,8},{9,1... | collective-permute-start | bytes 786440 | tf_op jit(solution)/shard_map/ppermute | solution.py:45
  73.1 12.5 %collective-permute-start.6 = (bf16[1024,128]{0,1:T(8,128)(2,1)S(1)}, bf16[1024,128]{0,1:T(8,128)(2,1)S(1)}, u32[]{:S(2)}, u32[]{:S(2)}) collective-permute-start(bf16[1024,128]{0,1:T(8,128)(2,1)S(1)} %fusion.43), channel_id=1, source_target_pairs={{0,8},{8,0},{1,9},{9,1},{2,10},{10,2},{3,11},{11,3},{4,12},{12,4},... | collective-permute-start | bytes 786440 | tf_op jit(solution)/shard_map/ppermute | solution.py:45
  74.9 12.4 %collective-permute-start.9 = (bf16[512,512]{1,0:T(8,128)(2,1)S(1)}, bf16[512,512]{1,0:T(8,128)(2,1)S(1)}, u32[]{:S(2)}, u32[]{:S(2)}) collective-permute-start(bf16[512,512]{1,0:T(8,128)(2,1)S(1)} %convolution_convert_fusion.6), channel_id=1, source_target_pairs={{0,1},{1,0},{2,3},{3,2},{4,5},{5,4},{6,7},{7,6},{8,9},{9,8},{10,11... | collective-permute-start | bytes 1572872 | tf_op jit(solution)/shard_map/ppermute | solution.py:45
  82.6 14.1 %copy-start.12 = (bf16[1024,256]{0,1:T(8,128)(2,1)}, bf16[1024,256]{0,1:T(8,128)(2,1)S(1)}, u32[]{:S(2)}) copy-start(bf16[1024,256]{0,1:T(8,128)(2,1)S(1)} %collective-permute-done.7) | copy-start | bytes 1572868
  83.9 12.7 %collective-permute-start.10 = (bf16[1024,256]{0,1:T(8,128)(2,1)S(1)}, bf16[1024,256]{0,1:T(8,128)(2,1)S(1)}, u32[]{:S(2)}, u32[]{:S(2)}) collective-permute-start(bf16[1024,256]{0,1:T(8,128)(2,1)S(1)} %slice_add_fusion.1), channel_id=1, source_target_pairs={{0,2},{2,0},{1,3},{3,1},{4,6},{6,4},{5,7},{7,5},{8,10},{10,8},{9,1... | collective-permute-start | bytes 1572872 | tf_op jit(solution)/shard_map/ppermute | solution.py:45
  85.6 11.1 %copy-start.21 = (bf16[1024,128]{0,1:T(8,128)(2,1)}, bf16[1024,128]{0,1:T(8,128)(2,1)S(1)}, u32[]{:S(2)}) copy-start(bf16[1024,128]{0,1:T(8,128)(2,1)S(1)} %collective-permute-done.6) | copy-start | bytes 786436
  87.4 9.3 %copy-start.9 = (bf16[512,512]{1,0:T(8,128)(2,1)}, bf16[512,512]{1,0:T(8,128)(2,1)S(1)}, u32[]{:S(2)}) copy-start(bf16[512,512]{1,0:T(8,128)(2,1)S(1)} %collective-permute-done.9) | copy-start | bytes 1572868
  96.7 0.8 copy-start.10
  97.5 61.7 %all-to-all-start.1 = ((bf16[8,32,4096]{2,1,0:T(8,128)(2,1)}), bf16[8,32,4096]{2,1,0:T(8,128)(2,1)S(1)}, u32[]{:S(2)}, u32[]{:S(2)}) async-start(bf16[8,32,4096]{2,1,0:T(8,128)(2,1)} %bitcast.72), calls=%async_computation.1 | async-start | bytes 4194304 | tf_op jit(solution)/shard_map/all_to_all | solution.py:160
  101.1 52.9 %copy-start.11 = (bf16[1024,256]{0,1:T(8,128)(2,1)S(1)}, bf16[1024,256]{0,1:T(8,128)(2,1)}, u32[]{:S(2)}) copy-start(bf16[1024,256]{0,1:T(8,128)(2,1)} %copy-done.10) | copy-start | bytes 1572868
  101.1 36.9 %collective-permute-start.12 = (bf16[1024,128]{0,1:T(8,128)(2,1)}, bf16[1024,128]{0,1:T(8,128)(2,1)S(1)}, u32[]{:S(2)}, u32[]{:S(2)}) collective-permute-start(bf16[1024,128]{0,1:T(8,128)(2,1)} %slice_add_fusion.8), channel_id=1, source_target_pairs={{0,4},{4,0},{1,5},{5,1},{2,6},{6,2},{3,7},{7,3},{8,12},{12,8},{9,1... | collective-permute-start | bytes 786440 | tf_op jit(solution)/shard_map/ppermute | solution.py:45
  103.1 36.1 %collective-permute-start.11 = (bf16[1024,128]{0,1:T(8,128)(2,1)S(1)}, bf16[1024,128]{0,1:T(8,128)(2,1)}, u32[]{:S(2)}, u32[]{:S(2)}) collective-permute-start(bf16[1024,128]{0,1:T(8,128)(2,1)S(1)} %fusion.44), channel_id=1, source_target_pairs={{0,8},{8,0},{1,9},{9,1},{2,10},{10,2},{3,11},{11,3},{4,12},{12,4},... | collective-permute-start | bytes 786440 | tf_op jit(solution)/shard_map/ppermute | solution.py:45
  105.1 39.4 %collective-permute-start.17 = (f32[128,512]{1,0:T(8,128)S(1)}, f32[128,512]{1,0:T(8,128)S(1)}, u32[]{:S(2)}, u32[]{:S(2)}) collective-permute-start(f32[128,512]{1,0:T(8,128)S(1)} %convolution_select_fusion), channel_id=1, source_target_pairs={{0,16},{16,0},{1,17},{17,1},{2,18},{18,2},{3,19},{19,3},{4,20},{20... | collective-permute-start | bytes 786440 | tf_op jit(solution)/shard_map/ppermute | solution.py:28
  106.6 67.2 %collective-permute-start.8 = (f32[512,512]{1,0:T(8,128)}, f32[512,512]{1,0:T(8,128)}, u32[]{:S(2)}, u32[]{:S(2)}) collective-permute-start(f32[512,512]{1,0:T(8,128)} %slice_select_fusion), channel_id=1, source_target_pairs={{0,16},{16,0},{1,17},{17,1},{2,18},{18,2},{3,19},{19,3},{4,20},{20... | collective-permute-start | bytes 3145736 | tf_op jit(solution)/shard_map/ppermute | solution.py:45
  139.2 17.5 %copy-start.15 = (bf16[1024,128]{0,1:T(8,128)(2,1)}, bf16[1024,128]{0,1:T(8,128)(2,1)S(1)}, u32[]{:S(2)}) copy-start(bf16[1024,128]{0,1:T(8,128)(2,1)S(1)} %fusion.42) | copy-start | bytes 786436
  139.2 8.1 %collective-permute-start.15 = (bf16[256,512]{1,0:T(8,128)(2,1)}, bf16[256,512]{1,0:T(8,128)(2,1)S(1)}, u32[]{:S(2)}, u32[]{:S(2)}) collective-permute-start(bf16[256,512]{1,0:T(8,128)(2,1)} %slice_add_fusion.7), channel_id=1, source_target_pairs={{0,2},{2,0},{1,3},{3,1},{4,6},{6,4},{5,7},{7,5},{8,10},{10,8},{9,1... | collective-permute-start | bytes 786440 | tf_op jit(solution)/shard_map/ppermute | solution.py:45
  141.9 12.1 %collective-permute-start.14 = (bf16[1024,128]{0,1:T(8,128)(2,1)S(1)}, bf16[1024,128]{0,1:T(8,128)(2,1)S(1)}, u32[]{:S(2)}, u32[]{:S(2)}) collective-permute-start(bf16[1024,128]{0,1:T(8,128)(2,1)S(1)} %slice_add_fusion.5), channel_id=1, source_target_pairs={{0,4},{4,0},{1,5},{5,1},{2,6},{6,2},{3,7},{7,3},{8,12},{12,8},{9,1... | collective-permute-start | bytes 786440 | tf_op jit(solution)/shard_map/ppermute | solution.py:45
  142.7 14.0 %collective-permute-start.13 = (bf16[1024,128]{0,1:T(8,128)(2,1)S(1)}, bf16[1024,128]{0,1:T(8,128)(2,1)S(1)}, u32[]{:S(2)}, u32[]{:S(2)}) collective-permute-start(bf16[1024,128]{0,1:T(8,128)(2,1)S(1)} %fusion.42), channel_id=1, source_target_pairs={{0,8},{8,0},{1,9},{9,1},{2,10},{10,2},{3,11},{11,3},{4,12},{12,4},... | collective-permute-start | bytes 786440 | tf_op jit(solution)/shard_map/ppermute | solution.py:45
  147.3 9.4 %copy-start.18 = (bf16[256,512]{1,0:T(8,128)(2,1)}, bf16[256,512]{1,0:T(8,128)(2,1)S(1)}, u32[]{:S(2)}) copy-start(bf16[256,512]{1,0:T(8,128)(2,1)S(1)} %collective-permute-done.15) | copy-start | bytes 786436
  154.0 21.4 %collective-permute-start.19 = (bf16[128,512]{1,0:T(8,128)(2,1)}, bf16[128,512]{1,0:T(8,128)(2,1)S(1)}, u32[]{:S(2)}, u32[]{:S(2)}) collective-permute-start(bf16[128,512]{1,0:T(8,128)(2,1)} %slice_add_fusion.17), channel_id=1, source_target_pairs={{0,4},{4,0},{1,5},{5,1},{2,6},{6,2},{3,7},{7,3},{8,12},{12,8},{9,1... | collective-permute-start | bytes 393224 | tf_op jit(solution)/shard_map/ppermute | solution.py:45
  157.4 14.8 %collective-permute-start.16 = (bf16[1024,128]{0,1:T(8,128)(2,1)S(1)}, bf16[1024,128]{0,1:T(8,128)(2,1)}, u32[]{:S(2)}, u32[]{:S(2)}) collective-permute-start(bf16[1024,128]{0,1:T(8,128)(2,1)S(1)} %fusion.41), channel_id=1, source_target_pairs={{0,8},{8,0},{1,9},{9,1},{2,10},{10,2},{3,11},{11,3},{4,12},{12,4},... | collective-permute-start | bytes 786440 | tf_op jit(solution)/shard_map/ppermute | solution.py:45
  159.2 14.6 %all-to-all-start.2 = ((bf16[16,8,512]{2,1,0:T(8,128)(2,1)}), bf16[16,8,512]{2,1,0:T(8,128)(2,1)}, u32[]{:S(2)}, u32[]{:S(2)}) async-start(bf16[16,8,512]{2,1,0:T(8,128)(2,1)} %fusion.3), calls=%async_computation.2 | async-start | bytes 262144 | tf_op jit(solution)/shard_map/all_to_all | solution.py:191
  163.4 4.4 %copy-start.23 = (bf16[1024,128]{0,1:T(8,128)(2,1)S(1)}, bf16[1024,128]{0,1:T(8,128)(2,1)}, u32[]{:S(2)}) copy-start(bf16[1024,128]{0,1:T(8,128)(2,1)} %copy-done.22) | copy-start | bytes 786436
  167.8 26.5 %copy-start.17 = (bf16[256,512]{1,0:T(8,128)(2,1)S(1)}, bf16[256,512]{1,0:T(8,128)(2,1)}, u32[]{:S(2)}) copy-start(bf16[256,512]{1,0:T(8,128)(2,1)} %copy-done.16) | copy-start | bytes 786436
  173.9 4.3 %collective-permute-start.18 = (f32[128,128]{1,0:T(8,128)S(1)}, f32[128,128]{1,0:T(8,128)S(1)}, u32[]{:S(2)}, u32[]{:S(2)}) collective-permute-start(f32[128,128]{1,0:T(8,128)S(1)} %fusion.49), channel_id=1, source_target_pairs={{0,16},{16,0},{1,17},{17,1},{2,18},{18,2},{3,19},{19,3},{4,20},{20... | collective-permute-start | bytes 196616 | tf_op jit(solution)/shard_map/ppermute | solution.py:28
  176.5 7.5 %collective-permute-start.20 = (bf16[128,512]{1,0:T(8,128)(2,1)S(1)}, bf16[128,512]{1,0:T(8,128)(2,1)S(1)}, u32[]{:S(2)}, u32[]{:S(2)}) collective-permute-start(bf16[128,512]{1,0:T(8,128)(2,1)S(1)} %fusion.46), channel_id=1, source_target_pairs={{0,8},{8,0},{1,9},{9,1},{2,10},{10,2},{3,11},{11,3},{4,12},{12,4},... | collective-permute-start | bytes 393224 | tf_op jit(solution)/shard_map/ppermute | solution.py:45
  184.9 9.4 %all-to-all-start.3 = ((bf16[8,32,512]{2,1,0:T(8,128)(2,1)}), bf16[8,32,512]{2,1,0:T(8,128)(2,1)S(1)}, u32[]{:S(2)}, u32[]{:S(2)}) async-start(bf16[8,32,512]{2,1,0:T(8,128)(2,1)} %bitcast.18), calls=%async_computation.3 | async-start | bytes 524288 | tf_op jit(solution)/shard_map/all_to_all | solution.py:236
  (1 other events, 0.7 us)

commit v5 on v4

v5 whole, which is shorter than its diff:
```python
import jax
import jax.numpy as jnp
from jax import lax
from jax.experimental import pallas as pl
from jax.experimental.pallas import tpu as pltpu
from jax.sharding import Mesh, PartitionSpec as P

R = 64
CAP = 2
HCAP = 16
TAG = 128
DP = ("z_high", "z_low", "x", "core")
GROUP = ("z_low", "x", "core")
SWAP = [(0, 1), (1, 0)]


def pick(flags):
    return flags.astype(jnp.bfloat16)


def matmul(a, b):
    return jnp.dot(a, b, preferred_element_type=jnp.float32)


def narrow(a, b):
    return matmul(a, b).astype(jnp.bfloat16)


def sum_over_tp(part):
    if lax.axis_size("tp") == 2:
        return part + lax.ppermute(part, "tp", SWAP)
    return lax.psum(part, "tp")


def after(value, *others):
    return lax.optimization_barrier((value, *others))[0]


class Chain:
    def __init__(self):
        self.last = None

    def hold(self, value):
        self.last = value if self.last is None else after(value, self.last)
        return self.last

    def permute(self, value, axis, pairs):
        return lax.ppermute(self.hold(value), axis, pairs)

    def wait(self, *arrived):
        self.last = after(self.last, *arrived)


def kernel_params():
    return dict(
        compiler_params=pltpu.CompilerParams(vmem_limit_bytes=40 * 2**20),
        cost_estimate=pl.CostEstimate(flops=1, bytes_accessed=1, transcendentals=0),
    )


def pick_columns(store, want_mine, want_other):
    depth, width = store.shape
    count = want_mine.shape[0]
    blocks = 8
    rows = depth // blocks

    def kernel(mine_at, other_at, store_ref, mine_ref, first_ref, rest_ref, pick_mine, pick_other):
        step = pl.program_id(0)

        @pl.when(step == 0)
        def _():
            column = lax.broadcasted_iota(jnp.int32, (width, count), 0)
            pick_mine[...] = (column == mine_at[...]).astype(jnp.float32).astype(jnp.bfloat16)
            pick_other[...] = (column == other_at[...]).astype(jnp.float32).astype(jnp.bfloat16)

        block = store_ref[...]
        other = narrow(block, pick_other[...])

        @pl.when(step < blocks // 4)
        def _():
            first_ref[...] = other

        @pl.when(step >= blocks // 4)
        def _():
            rest_ref[...] = other

        mine_ref[...] = narrow(block, pick_mine[...])

    out = lambda part: jax.ShapeDtypeStruct((depth * part // 4, count), jnp.bfloat16)
    index = pl.BlockSpec((1, count), lambda i: (0, 0))
    return pl.pallas_call(
        kernel,
        grid=(blocks,),
        in_specs=[index, index, pl.BlockSpec((rows, width), lambda i: (i, 0))],
        out_specs=[
            pl.BlockSpec((rows, count), lambda i: (i, 0)),
            pl.BlockSpec((rows, count), lambda i: (jnp.minimum(i, blocks // 4 - 1), 0)),
            pl.BlockSpec((rows, count), lambda i: (jnp.maximum(i - blocks // 4, 0), 0)),
        ],
        out_shape=[out(4), out(1), out(3)],
        scratch_shapes=[pltpu.VMEM((width, count), jnp.bfloat16)] * 2,
        **kernel_params(),
    )(want_mine[None], want_other[None], store)


def place_rows(rows, hot_target, cold_target, tag, hot_rows, cold_rows):
    count, depth = rows.shape
    blocks = 4
    width = depth // blocks

    def kernel(hot_at, cold_at, tag_at, rows_ref, hot_ref, cold_ref, place_hot, place_cold):
        step = pl.program_id(0)

        @pl.when(step == 0)
        def _():
            hot_hit = lax.broadcasted_iota(jnp.int32, (hot_rows, count), 0) == hot_at[...]
            cold_hit = lax.broadcasted_iota(jnp.int32, (cold_rows, count), 0) == cold_at[...]
            place_hot[...] = hot_hit.astype(jnp.float32).astype(jnp.bfloat16)
            place_cold[...] = cold_hit.astype(jnp.float32).astype(jnp.bfloat16)
            tags = jnp.sum(jnp.where(cold_hit, tag_at[...].astype(jnp.float32), 0.0), axis=1, keepdims=True)
            cold_ref[:, depth:] = jnp.broadcast_to(tags, (cold_rows, TAG)).astype(jnp.bfloat16)

        block = rows_ref[...]
        hot_ref[...] = narrow(place_hot[...], block)
        cold_ref[:, pl.ds(pl.multiple_of(step * width, 128), width)] = narrow(place_cold[...], block)

    index = pl.BlockSpec((1, count), lambda j: (0, 0))
    return pl.pallas_call(
        kernel,
        grid=(blocks,),
        in_specs=[index, index, index, pl.BlockSpec((count, width), lambda j: (0, j))],
        out_specs=[
            pl.BlockSpec((hot_rows, width), lambda j: (0, j)),
            pl.BlockSpec((cold_rows, depth + TAG), lambda j: (0, 0)),
        ],
        out_shape=[
            jax.ShapeDtypeStruct((hot_rows, depth), jnp.bfloat16),
            jax.ShapeDtypeStruct((cold_rows, depth + TAG), jnp.bfloat16),
        ],
        scratch_shapes=[pltpu.VMEM((hot_rows, count), jnp.bfloat16), pltpu.VMEM((cold_rows, count), jnp.bfloat16)],
        **kernel_params(),
    )(hot_target[None], cold_target[None], tag[None], rows)


def base_halves(rows, weight):
    count, depth = rows.shape
    width = weight.shape[1]
    half = width // 2
    blocks = 8
    part = depth // blocks

    def kernel(tp_at, rows_ref, weight_ref, own_ref, other_ref, total):
        step = pl.program_id(0)
        product = matmul(rows_ref[...], weight_ref[...])

        @pl.when(step == 0)
        def _():
            total[...] = product

        @pl.when(step > 0)
        def _():
            total[...] += product

        @pl.when(step == blocks - 1)
        def _():
            first = pl.multiple_of(tp_at[0] * half, 128)
            second = pl.multiple_of((1 - tp_at[0]) * half, 128)
            own_ref[...] = total[:, pl.ds(first, half)]
            other_ref[...] = total[:, pl.ds(second, half)]

    out = pl.BlockSpec((count, half), lambda k, at: (0, 0))
    return pl.pallas_call(
        kernel,
        grid_spec=pltpu.PrefetchScalarGridSpec(
            num_scalar_prefetch=1,
            grid=(blocks,),
            in_specs=[
                pl.BlockSpec((count, part), lambda k, at: (0, k)),
                pl.BlockSpec((part, width), lambda k, at: (k, 0)),
            ],
            out_specs=[out, out],
            scratch_shapes=[pltpu.VMEM((count, width), jnp.float32)],
        ),
        out_shape=[jax.ShapeDtypeStruct((count, half), jnp.float32)] * 2,
        **kernel_params(),
    )(lax.axis_index("tp").astype(jnp.int32)[None], rows, weight)


def hot_shrink(blocks, factors, before=None):
    near = factors[0][1][0].shape[1] // R
    served, kept = blocks[0].shape[0], near * R
    count = len(blocks)
    pieces = [piece for _, pair in factors for piece in pair]

    def kernel(*refs):
        *in_refs, out_ref = refs
        rows = in_refs[:count]
        piece_refs = in_refs[count:count + len(pieces)]
        total = in_refs[-1][...] if before is not None else None
        for n, (first, pair) in enumerate(factors):
            depth = pair[0].shape[0]
            factor = piece_refs[2 * n][...] + piece_refs[2 * n + 1][...]
            block = jnp.concatenate([row[:, first:first + depth] for row in rows], axis=0)
            product = matmul(block, factor)
            total = product if total is None else total + product
        if before is None:
            out_ref[...] = total
            return
        total = total.reshape(count, near, HCAP, kept)
        at_step = lax.broadcasted_iota(jnp.int32, (count, HCAP, kept), 2) // R
        z = sum(jnp.where(at_step == i, total[:, i], 0.0) for i in range(near))
        out_ref[...] = z.reshape(count * HCAP, kept)

    out_rows = count * (served if before is None else HCAP)
    return pl.pallas_call(
        kernel,
        out_shape=jax.ShapeDtypeStruct((out_rows, kept), jnp.float32),
        **kernel_params(),
    )(*blocks, *pieces, *(() if before is None else (before,)))


def hot_expand(z_own, z_got, expand):
    kept, head = expand[0].shape
    near = kept // R
    count = z_own.shape[0] // HCAP

    def kernel(own_ref, got_ref, first_ref, second_ref, *out_refs):
        z = (own_ref[...] + got_ref[...]).astype(jnp.bfloat16).astype(jnp.float32).reshape(count, 1, HCAP, kept)
        shape = (count, near, HCAP, kept)
        same = lax.broadcasted_iota(jnp.int32, shape, 3) // R == lax.broadcasted_iota(jnp.int32, shape, 1)
        spread = jnp.where(same, jnp.broadcast_to(z, shape), 0.0).astype(jnp.bfloat16)
        factor = first_ref[...] + second_ref[...]
        delta = narrow(spread.reshape(count * near * HCAP, kept), factor)
        for k, out_ref in enumerate(out_refs):
            out_ref[...] = delta[k * near * HCAP:(k + 1) * near * HCAP]

    return pl.pallas_call(
        kernel,
        out_shape=[jax.ShapeDtypeStruct((near * HCAP, head), jnp.bfloat16)] * count,
        **kernel_params(),
    )(z_own, z_got, *expand)


def add_hot(partial, target, blocks):
    count = partial.shape[0]
    hot_rows = len(blocks) * blocks[0].shape[0]

    def kernel(partial_ref, target_ref, *refs):
        *block_refs, out_ref = refs
        hit = lax.broadcasted_iota(jnp.int32, (count, hot_rows), 1) == target_ref[...]
        place = hit.astype(jnp.float32).astype(jnp.bfloat16)
        delta = matmul(place, jnp.concatenate([ref[...] for ref in block_refs], axis=0))
        out_ref[...] = (partial_ref[...] + delta).astype(jnp.bfloat16)

    return pl.pallas_call(
        kernel,
        out_shape=jax.ShapeDtypeStruct(partial.shape, jnp.bfloat16),
        **kernel_params(),
    )(partial, target[:, None], *blocks)


def on_device(
    activations, value_weight, shrink_store, expand_store, adapter_row, token_adapter, hot_ids
):
    step_count, token_count, depth = activations.shape
    adapter_count = adapter_row.shape[0]
    hot_count = hot_ids.shape[1]
    per_dev = expand_store.shape[0] // R
    head_part = expand_store.shape[1]
    far_count = lax.axis_size("z_high")
    group_count = 8
    dp_count = far_count * group_count
    me = lax.axis_index(DP)
    group_at = lax.axis_index(GROUP)
    z_at, x_at, core_at = lax.axis_index("z_low"), lax.axis_index("x"), lax.axis_index("core")
    none_code = adapter_count + hot_count
    rows = activations.reshape(step_count * token_count, depth)

    names = jnp.arange(adapter_count, dtype=jnp.int32)
    hot_row = jnp.sum(jnp.where(hot_ids[:, :, None] == names, adapter_row, 0), axis=-1)
    hot_first = jnp.where(hot_row // per_dev == me, (hot_row % per_dev) * R, -R * per_dev)
    column = jnp.arange(per_dev * R, dtype=jnp.int32)
    lane = jnp.arange(R, dtype=jnp.int32)
    entry = jnp.arange(hot_count, dtype=jnp.int32)
    near = step_count // 2

    def wanted(core):
        firsts = []
        for x in (x_at, 1 - x_at):
            of_steps = jnp.sum(jnp.where(entry == 2 * x + core, hot_first, 0), axis=1)
            firsts += [jnp.where(z_at == 0, of_steps[:near], of_steps[near:])]
            firsts += [jnp.where(z_at == 0, of_steps[near:], of_steps[:near])]
        return jnp.concatenate([(f[:, None] + lane).reshape(-1) for f in firsts])

    want_mine, want_other = wanted(core_at), wanted(1 - core_at)
    kept = near * R
    chunk_count = 4
    part = depth // chunk_count

    chain = Chain()
    hops = [("x", SWAP), ("z_low", SWAP)]
    bit = 1
    while bit < far_count:
        hops.append(("z_high", [(i, i ^ bit) for i in range(far_count)]))
        bit *= 2

    def cut(block, c, first, last):
        return block[:, first * kept:last * kept] if c > 0 else block[first * kept:last * kept]

    mine, swapped, got, held = {}, {}, {}, {}

    def operand(c, stage):
        if stage == 0:
            return cut(mine[c], c, 2, 4) + cut(swapped[c], c, 2, 4)
        if stage == 1:
            return cut(mine[c], c, 1, 2) + cut(swapped[c], c, 1, 2) + cut(got[c, 0], c, 1, 2)
        if stage == 2:
            held[c] = cut(mine[c], c, 0, 1) + cut(swapped[c], c, 0, 1) + cut(got[c, 0], c, 0, 1) + got[c, 1]
        else:
            held[c] = held[c] + got[c, stage - 1]
        return held[c]

    def send(c, stage, value=None):
        value = operand(c, stage) if value is None else value
        if c > 0:
            value = after(value, got[c - 1, stage])
        got[c, stage] = chain.permute(value, *hops[stage])

    swapped[0] = chain.permute(narrow(pick(want_other[:, None] == column), expand_store), "core", SWAP)
    mine[0] = narrow(pick(want_mine[:, None] == column), expand_store)
    mine_all, other_first, other_rest = pick_columns(after(shrink_store, chain.last), want_mine, want_other)
    send(0, 0)
    first_swapped = chain.permute(other_first, "core", SWAP)
    rest_swapped = chain.permute(other_rest, "core", SWAP)
    mine[1], swapped[1] = mine_all[:part], first_swapped

    token_adapter = after(token_adapter, chain.last)
    cold_row = jnp.sum(jnp.where((token_adapter - hot_count)[:, :, None] == names, adapter_row, 0), axis=-1)
    is_hot = token_adapter < hot_count
    is_cold = (token_adapter < none_code) & jnp.logical_not(is_hot)
    owner = cold_row // per_dev
    group = jnp.where(is_hot, token_adapter, jnp.where(is_cold, hot_count + owner, -1))
    at = jnp.arange(token_count, dtype=jnp.int32)
    before = (group[:, :, None] == group[:, None, :]) & (at[None, :] < at[:, None])
    rank = jnp.sum(before.astype(jnp.int32), axis=-1)
    step_at = jnp.arange(step_count, dtype=jnp.int32)[:, None]
    hot_rows = hot_count * step_count * HCAP
    cold_rows = dp_count * step_count * CAP
    server = ((step_at // near) * hot_count + token_adapter) ^ group_at
    hot_target = (server * near + step_at % near) * HCAP + rank
    cold_target = (owner * step_count + step_at) * CAP + rank
    hot_target = jnp.where(is_hot, hot_target, -1).reshape(-1)
    cold_target = jnp.where(is_cold, cold_target, -1).reshape(-1)
    hot_out, packet = place_rows(
        rows, hot_target, cold_target, (cold_row % per_dev + 1).reshape(-1), hot_rows, cold_rows
    )
    served = near * HCAP

    done = {}

    def cold_tokens_out():
        sent = chain.hold(packet.reshape(dp_count, step_count * CAP, depth + TAG))
        sent = lax.all_to_all(sent, DP, split_axis=0, concat_axis=0, tiled=True)
        done["packet"] = sent.reshape(cold_rows, depth + TAG)

    hot_in = [hot_out[:served]] + [None] * (group_count - 1)

    def hot_tokens_out(*blocks):
        def work():
            for k in blocks:
                pairs = [(i, i ^ k) for i in range(group_count)]
                hot_in[k] = chain.permute(hot_out[k * served:(k + 1) * served], GROUP, pairs)
        return work

    def base_product():
        if lax.axis_size("tp") == 2:
            done["base"] = base_halves(rows, after(value_weight, chain.last))
        else:
            done["base"] = matmul(rows, after(value_weight, chain.last)), None

    def hot_tokens_in(*blocks):
        return lambda: chain.wait(*[hot_in[k] for k in blocks])

    def base_over_tp():
        own, other = done["base"]
        if other is None:
            done["base"] = lax.psum_scatter(chain.hold(own), "tp", scatter_dimension=1, tiled=True)
            done["base_got"] = done["base"]
        else:
            done["base_got"] = chain.permute(other, "tp", SWAP)
            done["base"] = own + done["base_got"]

    def cold_shrink():
        tag_in = done["packet"][:, depth:depth + 1].astype(jnp.int32)
        chosen = (column // R + 1)[None, :] == tag_in
        product = matmul(done["packet"][:, :depth], after(shrink_store, chain.last))
        done["z_part"] = jnp.where(chosen, product, 0.0)

    def cold_over_tp():
        done["z_cold"] = sum_over_tp(chain.hold(done["z_part"]))

    def cold_expand():
        done["delta"] = narrow(done["z_cold"].astype(jnp.bfloat16), after(expand_store, chain.last))

    def cold_back():
        delta = chain.hold(done["delta"].reshape(dp_count, step_count * CAP, head_part))
        delta = lax.all_to_all(delta, DP, split_axis=0, concat_axis=0, tiled=True)
        done["delta_cold"] = delta.reshape(cold_rows, head_part)

    between = {
        (1, "x"): [cold_tokens_out],
        (2, "end"): [hot_tokens_out(1, 4), base_product],
        (3, "end"): [hot_tokens_out(5), cold_shrink],
        (4, "x"): [hot_tokens_out(2, 3), base_over_tp],
        (4, "end"): [hot_tokens_in(1, 4), cold_over_tp],
        (5, "x"): [hot_tokens_out(6, 7)],
        (5, "end"): [hot_tokens_in(5, 2, 3), cold_expand],
        (6, "x"): [cold_back],
    }
    ready = operand(1, 0)
    for slot in range(1, chunk_count + 1 + len(hops) - 1):
        for stage in range(len(hops)):
            c = slot - stage
            if 0 <= c <= chunk_count:
                send(c, stage, ready if stage == 0 else None)
                if stage == 0 and c < chunk_count:
                    mine[c + 1] = after(mine_all, chain.last)[c * part:(c + 1) * part]
                    swapped[c + 1] = after(rest_swapped, chain.last)[(c - 1) * part:c * part]
                    ready = chain.hold(operand(c + 1, 0))
            if stage == 0:
                for work in between.get((slot, "x"), []):
                    work()
        for work in between.get((slot, "end"), []):
            work()
    chain.wait(hot_in[6], hot_in[7], done["base_got"])
    expand_hot, *shrink_hot = [(held[c], got[c, len(hops) - 1]) for c in range(chunk_count + 1)]
    shrink_hot = [(c * part, pair) for c, pair in enumerate(shrink_hot)]

    place_cold = pick(jnp.arange(cold_rows, dtype=jnp.int32)[:, None] == cold_target)
    partial = done["base"] + lax.dot_general(
        place_cold, done["delta_cold"], (((0,), (0,)), ((), ())), preferred_element_type=jnp.float32
    )

    dense = hot_shrink(hot_in, shrink_hot[:-1])
    z_part = hot_shrink(hot_in, shrink_hot[-1:], dense)
    z_part, partial = lax.optimization_barrier((z_part, partial))
    if lax.axis_size("tp") == 2:
        z_got = lax.ppermute(z_part, "tp", SWAP)
    else:
        z_part = lax.psum(z_part, "tp")
        z_got = jnp.zeros_like(z_part)
    delta_hot = list(hot_expand(z_part, z_got, expand_hot))
    for k in range(1, group_count):
        delta_hot[k] = lax.ppermute(delta_hot[k], GROUP, [(i, i ^ k) for i in range(group_count)])
    added = add_hot(partial, hot_target, delta_hot)
    return added.reshape(step_count, token_count, head_part)


def solution(mesh):
    tp_count, dp_count = mesh.shape["tp"], mesh.shape["dp"]
    fine = Mesh(mesh.devices.reshape(tp_count, dp_count // 8, 2, 2, 2), ("tp", *DP))
    placed = (
        P(None, DP, "tp"),
        P("tp", None),
        P("tp", DP),
        P(DP, "tp"),
        P(),
        P(None, DP),
        P(),
    )
    return jax.shard_map(
        on_device, mesh=fine, in_specs=placed, out_specs=P(None, DP, "tp"), check_vma=False
    )
```

time: 198 us -> 194 us (0.980)
  matrix products: 36.9 us -> 6.76 us
  Pallas kernels: 0 us -> 27.7 us
  waiting for transfers between devices: 90.8 us -> 66.9 us
  local copies, waits for them, and re-layouts: 5.19 us -> 23 us
  starting transfers between devices: 41.6 us -> 46.4 us
    ppermute x17 -> x26, waiting for transfers between devices: 83.7 us -> 41.7 us  [permute(): return lax.ppermute(self.hold(value), axis, pairs)]
    dot_general x19 -> x4, matrix products: 33.8 us -> 5.1 us  [matmul(): return jnp.dot(a, b, preferred_element_type=jnp.float32)]
    pallas_call x0 -> x7, Pallas kernels: none -> 27.7 us  [the longest x1 11 us: base_halves(): pl.pallas_call(kernel, grid_spec=pltpu.PrefetchScalarGridSpec(num_scalar_...]
    ppermute x2 -> x1, waiting for transfers between devices: 1.14 us -> 19.3 us  [sum_over_tp(): return part + lax.ppermute(part, 'tp', SWAP)]
    unnamed x54 -> x70, local copies, waits for them, and re-layouts: 4.39 us -> 20.9 us
    all_to_all x3 -> x1, starting transfers between devices: 14 us -> 4.68 us  [cold_tokens_out(): sent = lax.all_to_all(sent, DP, split_axis=0, concat_axis=0, tiled=True)]
    ppermute x17 -> x26, starting transfers between devices: 19.6 us -> 28.9 us  [permute(): return lax.ppermute(self.hold(value), axis, pairs)]
    ppermute x2 -> x8, starting transfers between devices: 0.64 us -> 7.95 us  [the longest x7 6.36 us: on_device(): lax.ppermute(delta_hot[k], GROUP, [(i, i ^ k) for i in range(group_count)])]
  transfers between devices with their start and end apart: 25 -> 37, of which waited for: 11 -> 12; matrix products, arithmetic and copies ran while one was open for 23% -> 14% of each run, Pallas kernels for 0% -> 13%
where the time goes in v5:
time: 194 us; the launch traced here: 193 us
  waiting for transfers between devices  66.9 us (34%)
  starting transfers between devices  46.4 us (24%)
  Pallas kernels  27.7 us (14%)
  local copies, waits for them, and re-layouts  23 us (12%)
  other arithmetic  21.9 us (11%)
  matrix products  6.76 us (3%)
    ppermute x26, waiting for transfers between devices, permute(): return lax.ppermute(self.hold(value), axis, pairs)  41.7 us
    ppermute x26, starting transfers between devices, permute(): return lax.ppermute(self.hold(value), axis, pairs)  28.9 us
    unnamed x70, local copies, waits for them, and re-layouts  20.9 us
    ppermute x1, waiting for transfers between devices, sum_over_tp(): return part + lax.ppermute(part, 'tp', SWAP)  19.3 us
    pallas_call x1, Pallas kernels, base_halves(): pl.pallas_call(kernel, grid_spec=pltpu.PrefetchScalarGridSpec(num_scalar_...  11 us
    pallas_call x1, Pallas kernels, pick_columns(): pl.pallas_call(kernel, grid=(blocks,), in_specs=[index, index, pl.BlockSp...  8.06 us
    add x5, other arithmetic, operand(): cut(mine[c], c, 1, 2) + cut(swapped[c], c, 1, 2) + cut(got[c, 0], c, 1, 2)  7.11 us
    ppermute x7, starting transfers between devices, on_device(): lax.ppermute(delta_hot[k], GROUP, [(i, i ^ k) for i in range(group_count)])  6.36 us
  transfers between devices with their start and end apart: 37, of which 12 were waited for; matrix products, arithmetic and copies ran while one was open for 14% of the time, Pallas kernels for 13%

profile of v5, /device:TPU:0, one launch (start us, length us, event | category | flops | bytes accessed | tf_op | source)
XLA Modules:
  0.0 193.0 jit_solution(3489569758301935124)
XLA Ops:
  3.8 2.2 %copy-done.3 = bf16[4096,512]{1,0:T(8,128)(2,1)S(1)} copy-done((bf16[4096,512]{1,0:T(8,128)(2,1)S(1)}, bf16[4096,512]{1,0:T(8,128)(2,1)}, u32[]{:S(2)}) %copy-start.3) | copy-done | bytes 4194328
  6.0 8.1 %shard_map.73 = (bf16[4096,512]{1,0:T(8,128)(2,1)S(1)}, bf16[1024,512]{1,0:T(8,128)(2,1)S(1)}, bf16[3072,512]{1,0:T(8,128)(2,1)}) custom-call(s32[1,512]{1,0:T(1,128)S(1)} %bitcast.28, s32[1,512]{1,0:T(1,128)S(1)} %bitcast.27, bf16[4096,512]{1,0:T(8,128)(2,1)S(1)} %copy-done.3), custom_call_target="tpu_custom_call" | custom-call | flops 1 | bytes 1 | tf_op jit(solution)/shard_map/pallas_call | solution.py:91
  14.1 2.0 %copy-done.4 = bf16[4096,512]{1,0:T(8,128)(2,1)} copy-done((bf16[4096,512]{1,0:T(8,128)(2,1)}, bf16[4096,512]{1,0:T(8,128)(2,1)S(1)}, u32[]{:S(2)}) %copy-start.4) | copy-done | bytes 4194328
  18.0 2.6 %collective-permute-start.1 = (bf16[256,512]{1,0:T(8,128)(2,1)}, bf16[256,512]{1,0:T(8,128)(2,1)S(1)}, u32[]{:S(2)}, u32[]{:S(2)}) collective-permute-start(bf16[256,512]{1,0:T(8,128)(2,1)} %slice_add_fusion.14), channel_id=1, source_target_pairs={{0,2},{2,0},{1,3},{3,1},{4,6},{6,4},{5,7},{7,5},{8,10},{10,8},{9,1... | collective-permute-start | bytes 786440 | tf_op jit(solution)/shard_map/ppermute | solution.py:48
  21.2 2.2 %copy-done.1 = bf16[4,128,4096]{2,1,0:T(8,128)(2,1)S(1)} copy-done((bf16[4,128,4096]{2,1,0:T(8,128)(2,1)S(1)}, bf16[4,128,4096]{2,1,0:T(8,128)(2,1)}, u32[]{:S(2)}) %copy-start.1) | copy-done | bytes 4194328
  23.4 3.9 %shard_map.74 = (bf16[256,4096]{1,0:T(8,128)(2,1)S(1)}, bf16[128,4224]{1,0:T(8,128)(2,1)}) custom-call(s32[1,512]{1,0:T(1,128)S(1)} %bitcast.23, s32[1,512]{1,0:T(1,128)S(1)} %bitcast.25, s32[1,512]{1,0:T(1,128)S(1)} %fusion.19.tag_at, bf16[512,4096]{1,0:T(8,128)(2,1)S(1)} %bitcast.21), custom_call_target="tpu_custom_call" | custom-call | flops 1 | bytes 1 | tf_op jit(solution)/shard_map/pallas_call | solution.py:128
  27.3 1.4 slice_add_fusion
  29.4 1.2 fusion.26
  30.7 1.6 slice_add_fusion.15
  32.2 1.3 slice_add_fusion.3
  33.5 9.3 %collective-permute-done.5 = bf16[1024,256]{1,0:T(8,128)(2,1)S(1)} collective-permute-done((bf16[1024,256]{1,0:T(8,128)(2,1)S(1)}, bf16[1024,256]{1,0:T(8,128)(2,1)S(1)}, u32[]{:S(2)}, u32[]{:S(2)}) %collective-permute-start.5) | collective-permute-done | bytes 524320 | tf_op jit(solution)/shard_map/ppermute | solution.py:48
  43.6 1.7 slice_add_fusion.12
  45.4 1.6 collective-permute-start.4
  46.9 4.7 %all-to-all-start = ((bf16[16,8,4224]{2,1,0:T(8,128)(2,1)}), bf16[16,8,4224]{2,1,0:T(8,128)(2,1)}, u32[]{:S(2)}, u32[]{:S(2)}) async-start(bf16[16,8,4224]{2,1,0:T(8,128)(2,1)} %bitcast.6), calls=%async_computation | async-start | bytes 2162688 | tf_op jit(solution)/shard_map/all_to_all | solution.py:363
  51.6 1.3 slice_add_fusion.2
  53.5 1.9 collective-permute-start.9
  56.5 2.4 %collective-permute-start.10 = (bf16[128,512]{1,0:T(8,128)(2,1)S(1)}, bf16[128,512]{1,0:T(8,128)(2,1)S(1)}, u32[]{:S(2)}, u32[]{:S(2)}) collective-permute-start(bf16[128,512]{1,0:T(8,128)(2,1)S(1)} %fusion.9.first_ref), channel_id=1, source_target_pairs={{0,8},{8,0},{1,9},{9,1},{2,10},{10,2},{3,11},{11,3},{4,12},{12,4},... | collective-permute-start | bytes 393224 | tf_op jit(solution)/shard_map/ppermute | solution.py:48
  58.9 2.2 %copy-done.2 = bf16[4,128,4096]{2,1,0:T(8,128)(2,1)S(1)} copy-done((bf16[4,128,4096]{2,1,0:T(8,128)(2,1)S(1)}, bf16[4,128,4096]{2,1,0:T(8,128)(2,1)}, u32[]{:S(2)}) %copy-start.2) | copy-done | bytes 4194328
  61.1 11.0 %shard_map.75 = (f32[512,512]{1,0:T(8,128)S(1)}, f32[512,512]{1,0:T(8,128)}) custom-call(s32[1]{0:T(128)} %bitcast.8.tp_at, bf16[512,4096]{1,0:T(8,128)(2,1)S(1)} %bitcast.22, bf16[4096,1024]{1,0:T(8,128)(2,1)} %weight_ref), custom_call_target="tpu_custom_call" | custom-call | flops 1 | bytes 1 | tf_op jit(solution)/shard_map/pallas_call | solution.py:172
  72.1 1.5 collective-permute-start.8
  74.6 3.1 %collective-permute-done.9 = bf16[1024,128]{1,0:T(8,128)(2,1)S(1)} collective-permute-done((bf16[1024,128]{1,0:T(8,128)(2,1)}, bf16[1024,128]{1,0:T(8,128)(2,1)S(1)}, u32[]{:S(2)}, u32[]{:S(2)}) %collective-permute-start.9) | collective-permute-done | bytes 262176 | tf_op jit(solution)/shard_map/ppermute | solution.py:48
  80.8 3.9 %collective-permute-done.10.second_ref = bf16[128,512]{1,0:T(8,128)(2,1)S(1)} collective-permute-done((bf16[128,512]{1,0:T(8,128)(2,1)S(1)}, bf16[128,512]{1,0:T(8,128)(2,1)S(1)}, u32[]{:S(2)}, u32[]{:S(2)}) %collective-permute-start.10) | collective-permute-done | bytes 131104 | tf_op jit(solution)/shard_map/ppermute | solution.py:48
  84.6 2.2 %collective-permute-done.8 = bf16[1024,256]{1,0:T(8,128)(2,1)S(1)} collective-permute-done((bf16[1024,256]{1,0:T(8,128)(2,1)S(1)}, bf16[1024,256]{1,0:T(8,128)(2,1)S(1)}, u32[]{:S(2)}, u32[]{:S(2)}) %collective-permute-start.8) | collective-permute-done | bytes 524320 | tf_op jit(solution)/shard_map/ppermute | solution.py:48
  86.8 1.5 collective-permute-start.17
  91.2 7.5 %collective-permute-done.21.refs_9_ = bf16[1024,128]{1,0:T(8,128)(2,1)S(1)} collective-permute-done((bf16[1024,128]{1,0:T(8,128)(2,1)S(1)}, bf16[1024,128]{1,0:T(8,128)(2,1)S(1)}, u32[]{:S(2)}, u32[]{:S(2)}) %collective-permute-start.21) | collective-permute-done | bytes 262176 | tf_op jit(solution)/shard_map/ppermute | solution.py:48
  100.4 2.5 %collective-permute-start.12 = (bf16[32,4096]{1,0:T(8,128)(2,1)}, bf16[32,4096]{1,0:T(8,128)(2,1)S(1)}, u32[]{:S(2)}, u32[]{:S(2)}) collective-permute-start(bf16[32,4096]{1,0:T(8,128)(2,1)} %get-tuple-element.116), channel_id=1, source_target_pairs={{0,3},{1,2},{2,1},{3,0},{4,7},{5,6},{6,5},{7,4},{8,11},{9,10},{10,... | collective-permute-start | bytes 786440 | tf_op jit(solution)/shard_map/ppermute | solution.py:48
  104.5 8.2 %collective-permute-done.22.refs_11_ = bf16[1024,128]{1,0:T(8,128)(2,1)S(1)} collective-permute-done((bf16[1024,128]{1,0:T(8,128)(2,1)S(1)}, bf16[1024,128]{1,0:T(8,128)(2,1)S(1)}, u32[]{:S(2)}, u32[]{:S(2)}) %collective-permute-start.22) | collective-permute-done | bytes 262176 | tf_op jit(solution)/shard_map/ppermute | solution.py:48
  113.4 1.5 collective-permute-start.26
  115.7 1.7 slice_add_fusion.7
  118.3 3.2 %convolution_select_fusion = f32[128,512]{1,0:T(8,128)S(1)} fusion(bf16[4096,512]{1,0:T(8,128)(2,1)} %store_ref, bf16[128,4224]{1,0:T(8,128)(2,1)} %bitcast.7, s32[512]{0:T(512)S(1)} %fusion.16, s32[128]{0:T(128)S(1)} %convert_reduce_fusion.1), kind=kOutput, calls=%fused_computation.2 | convolution fusion | flops 537001984 | bytes 5507584 | tf_op jit(solution)/shard_map/dot_general | solution.py:22
  122.2 2.7 %collective-permute-start.20 = (bf16[1024,128]{1,0:T(8,128)(2,1)S(1)}, bf16[1024,128]{1,0:T(8,128)(2,1)}, u32[]{:S(2)}, u32[]{:S(2)}) collective-permute-start(bf16[1024,128]{1,0:T(8,128)(2,1)S(1)} %copy-done.28), channel_id=1, source_target_pairs={{0,4},{4,0},{1,5},{5,1},{2,6},{6,2},{3,7},{7,3},{8,12},{12,8},{9,1... | collective-permute-start | bytes 786440 | tf_op jit(solution)/shard_map/ppermute | solution.py:48
  124.9 19.3 %collective-permute-done.24 = f32[128,512]{1,0:T(8,128)S(1)} collective-permute-done((f32[128,512]{1,0:T(8,128)S(1)}, f32[128,512]{1,0:T(8,128)S(1)}, u32[]{:S(2)}, u32[]{:S(2)}) %collective-permute-start.24) | collective-permute-done | bytes 262176 | tf_op jit(solution)/shard_map/ppermute | solution.py:31
  145.1 2.9 %collective-permute-start.15 = (bf16[32,4096]{1,0:T(8,128)(2,1)}, bf16[32,4096]{1,0:T(8,128)(2,1)}, u32[]{:S(2)}, u32[]{:S(2)}) collective-permute-start(bf16[32,4096]{1,0:T(8,128)(2,1)} %get-tuple-element.118), channel_id=1, source_target_pairs={{0,6},{1,7},{2,4},{3,5},{4,2},{5,3},{6,0},{7,1},{8,14},{9,15},{10,... | collective-permute-start | bytes 786440 | tf_op jit(solution)/shard_map/ppermute | solution.py:48
  148.9 4.3 %all-to-all-start.1 = ((bf16[16,8,512]{2,1,0:T(8,128)(2,1)}), bf16[16,8,512]{2,1,0:T(8,128)(2,1)}, u32[]{:S(2)}, u32[]{:S(2)}) async-start(bf16[16,8,512]{2,1,0:T(8,128)(2,1)} %fusion), calls=%async_computation.1 | async-start | bytes 262144 | tf_op jit(solution)/shard_map/all_to_all | solution.py:407
  153.2 1.3 fusion.6.refs_8_
  154.5 2.8 %collective-permute-start.25 = (bf16[1024,128]{1,0:T(8,128)(2,1)S(1)}, bf16[1024,128]{1,0:T(8,128)(2,1)}, u32[]{:S(2)}, u32[]{:S(2)}) collective-permute-start(bf16[1024,128]{1,0:T(8,128)(2,1)S(1)} %fusion.6.refs_8_), channel_id=1, source_target_pairs={{0,8},{8,0},{1,9},{9,1},{2,10},{10,2},{3,11},{11,3},{4,12},{12,4},... | collective-permute-start | bytes 786440 | tf_op jit(solution)/shard_map/ppermute | solution.py:48
  157.3 7.1 %collective-permute-done.15.refs_6_ = bf16[32,4096]{1,0:T(8,128)(2,1)} collective-permute-done((bf16[32,4096]{1,0:T(8,128)(2,1)}, bf16[32,4096]{1,0:T(8,128)(2,1)}, u32[]{:S(2)}, u32[]{:S(2)}) %collective-permute-start.15) | collective-permute-done | bytes 262176 | tf_op jit(solution)/shard_map/ppermute | solution.py:48
  168.2 1.8 shard_map.76.refs_10_
  170.6 1.7 add_add_fusion.partial_ref
  175.1 1.6 shard_map.77.own_ref
  176.7 1.6 collective-permute-start.27
  178.3 2.7 %collective-permute-done.27.got_ref = f32[128,128]{1,0:T(8,128)S(1)} collective-permute-done((f32[128,128]{1,0:T(8,128)S(1)}, f32[128,128]{1,0:T(8,128)S(1)}, u32[]{:S(2)}, u32[]{:S(2)}) %collective-permute-start.27) | collective-permute-done | bytes 65568 | tf_op jit(solution)/shard_map/ppermute | solution.py:448
  182.2 1.8 collective-permute-start.29
  184.1 1.7 collective-permute-start.32
  185.8 1.5 collective-permute-start.33
  187.3 1.2 collective-permute-start.34
  188.7 1.9 collective-permute-done.33.refs_6_
  190.6 1.3 collective-permute-done.34.refs_7_
  (163 shorter events, 34.2 us)
Async XLA Ops:
  0.0 20.6 %copy-start.31 = (s32[128]{0:T(128)S(1)}, s32[128]{0:T(128)}, u32[]{:S(2)}) copy-start(s32[128]{0:T(128)} %param.11) | copy-start | bytes 1540
  0.0 20.6 %copy-start.30 = (s32[4,128]{1,0:T(4,128)S(1)}, s32[4,128]{1,0:T(4,128)}, u32[]{:S(2)}) copy-start(s32[4,128]{1,0:T(4,128)} %param.12) | copy-start | bytes 6148
  2.5 14.1 %collective-permute-start = (bf16[512,512]{1,0:T(8,128)(2,1)S(1)}, bf16[512,512]{1,0:T(8,128)(2,1)S(1)}, u32[]{:S(2)}, u32[]{:S(2)}) collective-permute-start(bf16[512,512]{1,0:T(8,128)(2,1)S(1)} %convolution_convert_fusion.1), channel_id=1, source_target_pairs={{0,1},{1,0},{2,3},{3,2},{4,5},{5,4},{6,7},{7,6},{8,9},{9,8},{10,11... | collective-permute-start | bytes 1572872 | tf_op jit(solution)/shard_map/ppermute | solution.py:48
  17.4 14.9 %collective-permute-start.3 = (bf16[3072,512]{1,0:T(8,128)(2,1)}, bf16[3072,512]{1,0:T(8,128)(2,1)}, u32[]{:S(2)}, u32[]{:S(2)}) collective-permute-start(bf16[3072,512]{1,0:T(8,128)(2,1)} %get-tuple-element.81), channel_id=1, source_target_pairs={{0,1},{1,0},{2,3},{3,2},{4,5},{5,4},{6,7},{7,6},{8,9},{9,8},{10,11... | collective-permute-start | bytes 9437192 | tf_op jit(solution)/shard_map/ppermute | solution.py:48
  17.4 9.9 %collective-permute-start.2 = (bf16[1024,512]{1,0:T(8,128)(2,1)S(1)}, bf16[1024,512]{1,0:T(8,128)(2,1)S(1)}, u32[]{:S(2)}, u32[]{:S(2)}) collective-permute-start(bf16[1024,512]{1,0:T(8,128)(2,1)S(1)} %get-tuple-element.80), channel_id=1, source_target_pairs={{0,1},{1,0},{2,3},{3,2},{4,5},{5,4},{6,7},{7,6},{8,9},{9,8},{10,11... | collective-permute-start | bytes 3145736 | tf_op jit(solution)/shard_map/ppermute | solution.py:48
  18.0 10.8 %collective-permute-start.1 = (bf16[256,512]{1,0:T(8,128)(2,1)}, bf16[256,512]{1,0:T(8,128)(2,1)S(1)}, u32[]{:S(2)}, u32[]{:S(2)}) collective-permute-start(bf16[256,512]{1,0:T(8,128)(2,1)} %slice_add_fusion.14), channel_id=1, source_target_pairs={{0,2},{2,0},{1,3},{3,1},{4,6},{6,4},{5,7},{7,5},{8,10},{10,8},{9,1... | collective-permute-start | bytes 786440 | tf_op jit(solution)/shard_map/ppermute | solution.py:48
  27.3 18.0 %copy-start.21 = (bf16[1024,512]{1,0:T(8,128)(2,1)}, bf16[1024,512]{1,0:T(8,128)(2,1)S(1)}, u32[]{:S(2)}) copy-start(bf16[1024,512]{1,0:T(8,128)(2,1)S(1)} %collective-permute-done.2) | copy-start | bytes 3145732
  28.8 16.6 %copy-start.27 = (bf16[256,512]{1,0:T(8,128)(2,1)}, bf16[256,512]{1,0:T(8,128)(2,1)S(1)}, u32[]{:S(2)}) copy-start(bf16[256,512]{1,0:T(8,128)(2,1)S(1)} %collective-permute-done.1) | copy-start | bytes 786436
  28.8 14.1 %collective-permute-start.5 = (bf16[1024,256]{1,0:T(8,128)(2,1)S(1)}, bf16[1024,256]{1,0:T(8,128)(2,1)S(1)}, u32[]{:S(2)}, u32[]{:S(2)}) collective-permute-start(bf16[1024,256]{1,0:T(8,128)(2,1)S(1)} %slice_add_fusion), channel_id=1, source_target_pairs={{0,2},{2,0},{1,3},{3,1},{4,6},{6,4},{5,7},{7,5},{8,10},{10,8},{9,1... | collective-permute-start | bytes 1572872 | tf_op jit(solution)/shard_map/ppermute | solution.py:48
  42.8 29.3 %collective-permute-start.7 = (bf16[1024,256]{1,0:T(8,128)(2,1)S(1)}, bf16[1024,256]{1,0:T(8,128)(2,1)S(1)}, u32[]{:S(2)}, u32[]{:S(2)}) collective-permute-start(bf16[1024,256]{1,0:T(8,128)(2,1)S(1)} %slice_add_fusion.3), channel_id=1, source_target_pairs={{0,2},{2,0},{1,3},{3,1},{4,6},{6,4},{5,7},{7,5},{8,10},{10,8},{9,1... | collective-permute-start | bytes 1572872 | tf_op jit(solution)/shard_map/ppermute | solution.py:48
  45.4 7.5 %collective-permute-start.4 = (bf16[128,512]{1,0:T(8,128)(2,1)}, bf16[128,512]{1,0:T(8,128)(2,1)S(1)}, u32[]{:S(2)}, u32[]{:S(2)}) collective-permute-start(bf16[128,512]{1,0:T(8,128)(2,1)} %slice_add_fusion.15), channel_id=1, source_target_pairs={{0,4},{4,0},{1,5},{5,1},{2,6},{6,2},{3,7},{7,3},{8,12},{12,8},{9,1... | collective-permute-start | bytes 393224 | tf_op jit(solution)/shard_map/ppermute | solution.py:48
  46.9 70.5 %all-to-all-start = ((bf16[16,8,4224]{2,1,0:T(8,128)(2,1)}), bf16[16,8,4224]{2,1,0:T(8,128)(2,1)}, u32[]{:S(2)}, u32[]{:S(2)}) async-start(bf16[16,8,4224]{2,1,0:T(8,128)(2,1)} %bitcast.6), calls=%async_computation | async-start | bytes 2162688 | tf_op jit(solution)/shard_map/all_to_all | solution.py:363
  53.5 24.2 %collective-permute-start.9 = (bf16[1024,128]{1,0:T(8,128)(2,1)}, bf16[1024,128]{1,0:T(8,128)(2,1)S(1)}, u32[]{:S(2)}, u32[]{:S(2)}) collective-permute-start(bf16[1024,128]{1,0:T(8,128)(2,1)} %slice_add_fusion.12), channel_id=1, source_target_pairs={{0,4},{4,0},{1,5},{5,1},{2,6},{6,2},{3,7},{7,3},{8,12},{12,8},{9,1... | collective-permute-start | bytes 786440 | tf_op jit(solution)/shard_map/ppermute | solution.py:48
  56.5 28.2 %collective-permute-start.10 = (bf16[128,512]{1,0:T(8,128)(2,1)S(1)}, bf16[128,512]{1,0:T(8,128)(2,1)S(1)}, u32[]{:S(2)}, u32[]{:S(2)}) collective-permute-start(bf16[128,512]{1,0:T(8,128)(2,1)S(1)} %fusion.9.first_ref), channel_id=1, source_target_pairs={{0,8},{8,0},{1,9},{9,1},{2,10},{10,2},{3,11},{11,3},{4,12},{12,4},... | collective-permute-start | bytes 393224 | tf_op jit(solution)/shard_map/ppermute | solution.py:48
  61.1 12.5 %copy-start.5 = (bf16[4096,512]{1,0:T(8,128)(2,1)S(1)}, bf16[4096,512]{1,0:T(8,128)(2,1)}, u32[]{:S(2)}) copy-start(bf16[4096,512]{1,0:T(8,128)(2,1)} %copy-done.4) | copy-start | bytes 12582916
  61.1 18.6 %copy-start.26 = (bf16[1024,256]{1,0:T(8,128)(2,1)S(1)}, bf16[1024,256]{1,0:T(8,128)(2,1)}, u32[]{:S(2)}) copy-start(bf16[1024,256]{1,0:T(8,128)(2,1)} %copy-done.25) | copy-start | bytes 1572868
  72.1 8.7 %copy-start.24 = (bf16[1024,256]{1,0:T(8,128)(2,1)}, bf16[1024,256]{1,0:T(8,128)(2,1)S(1)}, u32[]{:S(2)}) copy-start(bf16[1024,256]{1,0:T(8,128)(2,1)S(1)} %collective-permute-done.7) | copy-start | bytes 1572868
  72.1 14.8 %collective-permute-start.8 = (bf16[1024,256]{1,0:T(8,128)(2,1)S(1)}, bf16[1024,256]{1,0:T(8,128)(2,1)S(1)}, u32[]{:S(2)}, u32[]{:S(2)}) collective-permute-start(bf16[1024,256]{1,0:T(8,128)(2,1)S(1)} %slice_add_fusion.2), channel_id=1, source_target_pairs={{0,2},{2,0},{1,3},{3,1},{4,6},{6,4},{5,7},{7,5},{8,10},{10,8},{9,1... | collective-permute-start | bytes 1572872 | tf_op jit(solution)/shard_map/ppermute | solution.py:48
  78.8 10.9 %collective-permute-start.18 = (bf16[1024,128]{1,0:T(8,128)(2,1)S(1)}, bf16[1024,128]{1,0:T(8,128)(2,1)S(1)}, u32[]{:S(2)}, u32[]{:S(2)}) collective-permute-start(bf16[1024,128]{1,0:T(8,128)(2,1)S(1)} %slice_add_fusion.9), channel_id=1, source_target_pairs={{0,4},{4,0},{1,5},{5,1},{2,6},{6,2},{3,7},{7,3},{8,12},{12,8},{9,1... | collective-permute-start | bytes 786440 | tf_op jit(solution)/shard_map/ppermute | solution.py:48
  84.6 18.2 %copy-start.19 = (bf16[128,512]{1,0:T(8,128)(2,1)}, bf16[128,512]{1,0:T(8,128)(2,1)S(1)}, u32[]{:S(2)}) copy-start(bf16[128,512]{1,0:T(8,128)(2,1)S(1)} %collective-permute-done.10.second_ref) | copy-start | bytes 393220
  84.6 14.1 %collective-permute-start.21 = (bf16[1024,128]{1,0:T(8,128)(2,1)S(1)}, bf16[1024,128]{1,0:T(8,128)(2,1)S(1)}, u32[]{:S(2)}, u32[]{:S(2)}) collective-permute-start(bf16[1024,128]{1,0:T(8,128)(2,1)S(1)} %fusion.7.refs_8_), channel_id=1, source_target_pairs={{0,8},{8,0},{1,9},{9,1},{2,10},{10,2},{3,11},{11,3},{4,12},{12,4},... | collective-permute-start | bytes 786440 | tf_op jit(solution)/shard_map/ppermute | solution.py:48
  86.8 28.0 %collective-permute-start.17 = (bf16[1024,256]{1,0:T(8,128)(2,1)S(1)}, bf16[1024,256]{1,0:T(8,128)(2,1)S(1)}, u32[]{:S(2)}, u32[]{:S(2)}) collective-permute-start(bf16[1024,256]{1,0:T(8,128)(2,1)S(1)} %slice_add_fusion.1), channel_id=1, source_target_pairs={{0,2},{2,0},{1,3},{3,1},{4,6},{6,4},{5,7},{7,5},{8,10},{10,8},{9,1... | collective-permute-start | bytes 1572872 | tf_op jit(solution)/shard_map/ppermute | solution.py:48
  89.7 13.1 %collective-permute-start.19 = (bf16[1024,128]{1,0:T(8,128)(2,1)S(1)}, bf16[1024,128]{1,0:T(8,128)(2,1)S(1)}, u32[]{:S(2)}, u32[]{:S(2)}) collective-permute-start(bf16[1024,128]{1,0:T(8,128)(2,1)S(1)} %slice_add_fusion.6), channel_id=1, source_target_pairs={{0,4},{4,0},{1,5},{5,1},{2,6},{6,2},{3,7},{7,3},{8,12},{12,8},{9,1... | collective-permute-start | bytes 786440 | tf_op jit(solution)/shard_map/ppermute | solution.py:48
  99.4 13.3 %collective-permute-start.22 = (bf16[1024,128]{1,0:T(8,128)(2,1)S(1)}, bf16[1024,128]{1,0:T(8,128)(2,1)S(1)}, u32[]{:S(2)}, u32[]{:S(2)}) collective-permute-start(bf16[1024,128]{1,0:T(8,128)(2,1)S(1)} %fusion.4.refs_10_), channel_id=1, source_target_pairs={{0,8},{8,0},{1,9},{9,1},{2,10},{10,2},{3,11},{11,3},{4,12},{12,4},... | collective-permute-start | bytes 786440 | tf_op jit(solution)/shard_map/ppermute | solution.py:48
  99.4 22.8 %collective-permute-start.14 = (bf16[32,4096]{1,0:T(8,128)(2,1)}, bf16[32,4096]{1,0:T(8,128)(2,1)S(1)}, u32[]{:S(2)}, u32[]{:S(2)}) collective-permute-start(bf16[32,4096]{1,0:T(8,128)(2,1)} %get-tuple-element.113), channel_id=1, source_target_pairs={{0,5},{1,4},{2,7},{3,6},{4,1},{5,0},{6,3},{7,2},{8,13},{9,12},{10,... | collective-permute-start | bytes 786440 | tf_op jit(solution)/shard_map/ppermute | solution.py:48
  100.4 21.8 %collective-permute-start.12 = (bf16[32,4096]{1,0:T(8,128)(2,1)}, bf16[32,4096]{1,0:T(8,128)(2,1)S(1)}, u32[]{:S(2)}, u32[]{:S(2)}) collective-permute-start(bf16[32,4096]{1,0:T(8,128)(2,1)} %get-tuple-element.116), channel_id=1, source_target_pairs={{0,3},{1,2},{2,1},{3,0},{4,7},{5,6},{6,5},{7,4},{8,11},{9,10},{10,... | collective-permute-start | bytes 786440 | tf_op jit(solution)/shard_map/ppermute | solution.py:48
  102.9 22.0 %collective-permute-start.11 = (bf16[32,4096]{1,0:T(8,128)(2,1)}, bf16[32,4096]{1,0:T(8,128)(2,1)S(1)}, u32[]{:S(2)}, u32[]{:S(2)}) collective-permute-start(bf16[32,4096]{1,0:T(8,128)(2,1)} %get-tuple-element.115), channel_id=1, source_target_pairs={{0,2},{1,3},{2,0},{3,1},{4,6},{5,7},{6,4},{7,5},{8,10},{9,11},{10,... | collective-permute-start | bytes 786440 | tf_op jit(solution)/shard_map/ppermute | solution.py:48
  113.4 57.3 %collective-permute-start.26 = (f32[512,512]{1,0:T(8,128)}, f32[512,512]{1,0:T(8,128)}, u32[]{:S(2)}, u32[]{:S(2)}) collective-permute-start(f32[512,512]{1,0:T(8,128)} %get-tuple-element.123), channel_id=1, source_target_pairs={{0,16},{16,0},{1,17},{17,1},{2,18},{18,2},{3,19},{19,3},{4,20},{20... | collective-permute-start | bytes 3145736 | tf_op jit(solution)/shard_map/ppermute | solution.py:48
  117.4 4.7 %copy-start.28 = (bf16[1024,128]{1,0:T(8,128)(2,1)S(1)}, bf16[1024,128]{1,0:T(8,128)(2,1)}, u32[]{:S(2)}) copy-start(bf16[1024,128]{1,0:T(8,128)(2,1)} %slice_add_fusion.7) | copy-start | bytes 786436
  121.6 22.6 %collective-permute-start.24 = (f32[128,512]{1,0:T(8,128)S(1)}, f32[128,512]{1,0:T(8,128)S(1)}, u32[]{:S(2)}, u32[]{:S(2)}) collective-permute-start(f32[128,512]{1,0:T(8,128)S(1)} %convolution_select_fusion), channel_id=1, source_target_pairs={{0,16},{16,0},{1,17},{17,1},{2,18},{18,2},{3,19},{19,3},{4,20},{20... | collective-permute-start | bytes 786440 | tf_op jit(solution)/shard_map/ppermute | solution.py:31
  122.2 22.0 %collective-permute-start.23 = (bf16[1024,128]{1,0:T(8,128)(2,1)S(1)}, bf16[1024,128]{1,0:T(8,128)(2,1)S(1)}, u32[]{:S(2)}, u32[]{:S(2)}) collective-permute-start(bf16[1024,128]{1,0:T(8,128)(2,1)S(1)} %fusion.5.refs_12_), channel_id=1, source_target_pairs={{0,8},{8,0},{1,9},{9,1},{2,10},{10,2},{3,11},{11,3},{4,12},{12,4},... | collective-permute-start | bytes 786440 | tf_op jit(solution)/shard_map/ppermute | solution.py:48
  122.2 48.5 %copy-start.6 = (bf16[32,4096]{1,0:T(8,128)(2,1)}, bf16[32,4096]{1,0:T(8,128)(2,1)S(1)}, u32[]{:S(2)}) copy-start(bf16[32,4096]{1,0:T(8,128)(2,1)S(1)} %collective-permute-done.12.refs_3_) | copy-start | bytes 786436
  122.2 22.9 %collective-permute-start.20 = (bf16[1024,128]{1,0:T(8,128)(2,1)S(1)}, bf16[1024,128]{1,0:T(8,128)(2,1)}, u32[]{:S(2)}, u32[]{:S(2)}) collective-permute-start(bf16[1024,128]{1,0:T(8,128)(2,1)S(1)} %copy-done.28), channel_id=1, source_target_pairs={{0,4},{4,0},{1,5},{5,1},{2,6},{6,2},{3,7},{7,3},{8,12},{12,8},{9,1... | collective-permute-start | bytes 786440 | tf_op jit(solution)/shard_map/ppermute | solution.py:48
  124.9 24.0 %copy-start.8 = (bf16[32,4096]{1,0:T(8,128)(2,1)}, bf16[32,4096]{1,0:T(8,128)(2,1)S(1)}, u32[]{:S(2)}) copy-start(bf16[32,4096]{1,0:T(8,128)(2,1)S(1)} %collective-permute-done.11.refs_2_) | copy-start | bytes 786436
  124.9 29.6 %collective-permute-start.13 = (bf16[32,4096]{1,0:T(8,128)(2,1)}, bf16[32,4096]{1,0:T(8,128)(2,1)}, u32[]{:S(2)}, u32[]{:S(2)}) collective-permute-start(bf16[32,4096]{1,0:T(8,128)(2,1)} %get-tuple-element.103), channel_id=1, source_target_pairs={{0,4},{1,5},{2,6},{3,7},{4,0},{5,1},{6,2},{7,3},{8,12},{9,13},{10,... | collective-permute-start | bytes 786440 | tf_op jit(solution)/shard_map/ppermute | solution.py:48
  144.2 13.1 %collective-permute-start.6 = (bf16[32,4096]{1,0:T(8,128)(2,1)}, bf16[32,4096]{1,0:T(8,128)(2,1)}, u32[]{:S(2)}, u32[]{:S(2)}) collective-permute-start(bf16[32,4096]{1,0:T(8,128)(2,1)} %get-tuple-element.101), channel_id=1, source_target_pairs={{0,1},{1,0},{2,3},{3,2},{4,5},{5,4},{6,7},{7,6},{8,9},{9,8},{10,11... | collective-permute-start | bytes 786440 | tf_op jit(solution)/shard_map/ppermute | solution.py:48
  144.9 12.4 %collective-permute-start.16 = (bf16[32,4096]{1,0:T(8,128)(2,1)}, bf16[32,4096]{1,0:T(8,128)(2,1)}, u32[]{:S(2)}, u32[]{:S(2)}) collective-permute-start(bf16[32,4096]{1,0:T(8,128)(2,1)} %get-tuple-element.119), channel_id=1, source_target_pairs={{0,7},{1,6},{2,5},{3,4},{4,3},{5,2},{6,1},{7,0},{8,15},{9,14},{10,... | collective-permute-start | bytes 786440 | tf_op jit(solution)/shard_map/ppermute | solution.py:48
  145.1 19.3 %collective-permute-start.15 = (bf16[32,4096]{1,0:T(8,128)(2,1)}, bf16[32,4096]{1,0:T(8,128)(2,1)}, u32[]{:S(2)}, u32[]{:S(2)}) collective-permute-start(bf16[32,4096]{1,0:T(8,128)(2,1)} %get-tuple-element.118), channel_id=1, source_target_pairs={{0,6},{1,7},{2,4},{3,5},{4,2},{5,3},{6,0},{7,1},{8,14},{9,15},{10,... | collective-permute-start | bytes 786440 | tf_op jit(solution)/shard_map/ppermute | solution.py:48
  148.9 21.8 %all-to-all-start.1 = ((bf16[16,8,512]{2,1,0:T(8,128)(2,1)}), bf16[16,8,512]{2,1,0:T(8,128)(2,1)}, u32[]{:S(2)}, u32[]{:S(2)}) async-start(bf16[16,8,512]{2,1,0:T(8,128)(2,1)} %fusion), calls=%async_computation.1 | async-start | bytes 262144 | tf_op jit(solution)/shard_map/all_to_all | solution.py:407
  154.5 17.9 %collective-permute-start.25 = (bf16[1024,128]{1,0:T(8,128)(2,1)S(1)}, bf16[1024,128]{1,0:T(8,128)(2,1)}, u32[]{:S(2)}, u32[]{:S(2)}) collective-permute-start(bf16[1024,128]{1,0:T(8,128)(2,1)S(1)} %fusion.6.refs_8_), channel_id=1, source_target_pairs={{0,8},{8,0},{1,9},{9,1},{2,10},{10,2},{3,11},{11,3},{4,12},{12,4},... | collective-permute-start | bytes 786440 | tf_op jit(solution)/shard_map/ppermute | solution.py:48
  176.7 4.3 %collective-permute-start.27 = (f32[128,128]{1,0:T(8,128)S(1)}, f32[128,128]{1,0:T(8,128)S(1)}, u32[]{:S(2)}, u32[]{:S(2)}) collective-permute-start(f32[128,128]{1,0:T(8,128)S(1)} %shard_map.77.own_ref), channel_id=1, source_target_pairs={{0,16},{16,0},{1,17},{17,1},{2,18},{18,2},{3,19},{19,3},{4,20},{20... | collective-permute-start | bytes 196616 | tf_op jit(solution)/shard_map/ppermute | solution.py:448
  182.1 3.6 %collective-permute-start.28 = (bf16[32,512]{1,0:T(8,128)(2,1)S(1)}, bf16[32,512]{1,0:T(8,128)(2,1)S(1)}, u32[]{:S(2)}, u32[]{:S(2)}) collective-permute-start(bf16[32,512]{1,0:T(8,128)(2,1)S(1)} %get-tuple-element.140), channel_id=1, source_target_pairs={{0,1},{1,0},{2,3},{3,2},{4,5},{5,4},{6,7},{7,6},{8,9},{9,8},{10,11... | collective-permute-start | bytes 98312 | tf_op jit(solution)/shard_map/ppermute | solution.py:454
  182.2 5.1 %collective-permute-start.29 = (bf16[32,512]{1,0:T(8,128)(2,1)S(1)}, bf16[32,512]{1,0:T(8,128)(2,1)S(1)}, u32[]{:S(2)}, u32[]{:S(2)}) collective-permute-start(bf16[32,512]{1,0:T(8,128)(2,1)S(1)} %get-tuple-element.141), channel_id=1, source_target_pairs={{0,2},{1,3},{2,0},{3,1},{4,6},{5,7},{6,4},{7,5},{8,10},{9,11},{10,... | collective-permute-start | bytes 98312 | tf_op jit(solution)/shard_map/ppermute | solution.py:454
  184.0 4.6 %collective-permute-start.30 = (bf16[32,512]{1,0:T(8,128)(2,1)S(1)}, bf16[32,512]{1,0:T(8,128)(2,1)S(1)}, u32[]{:S(2)}, u32[]{:S(2)}) collective-permute-start(bf16[32,512]{1,0:T(8,128)(2,1)S(1)} %get-tuple-element.142), channel_id=1, source_target_pairs={{0,3},{1,2},{2,1},{3,0},{4,7},{5,6},{6,5},{7,4},{8,11},{9,10},{10,... | collective-permute-start | bytes 98312 | tf_op jit(solution)/shard_map/ppermute | solution.py:454
  184.1 4.6 %collective-permute-start.31 = (bf16[32,512]{1,0:T(8,128)(2,1)S(1)}, bf16[32,512]{1,0:T(8,128)(2,1)S(1)}, u32[]{:S(2)}, u32[]{:S(2)}) collective-permute-start(bf16[32,512]{1,0:T(8,128)(2,1)S(1)} %get-tuple-element.143), channel_id=1, source_target_pairs={{0,4},{1,5},{2,6},{3,7},{4,0},{5,1},{6,2},{7,3},{8,12},{9,13},{10,... | collective-permute-start | bytes 98312 | tf_op jit(solution)/shard_map/ppermute | solution.py:454
  184.1 4.6 %collective-permute-start.32 = (bf16[32,512]{1,0:T(8,128)(2,1)S(1)}, bf16[32,512]{1,0:T(8,128)(2,1)S(1)}, u32[]{:S(2)}, u32[]{:S(2)}) collective-permute-start(bf16[32,512]{1,0:T(8,128)(2,1)S(1)} %get-tuple-element.144), channel_id=1, source_target_pairs={{0,5},{1,4},{2,7},{3,6},{4,1},{5,0},{6,3},{7,2},{8,13},{9,12},{10,... | collective-permute-start | bytes 98312 | tf_op jit(solution)/shard_map/ppermute | solution.py:454
  185.8 4.8 %collective-permute-start.33 = (bf16[32,512]{1,0:T(8,128)(2,1)S(1)}, bf16[32,512]{1,0:T(8,128)(2,1)S(1)}, u32[]{:S(2)}, u32[]{:S(2)}) collective-permute-start(bf16[32,512]{1,0:T(8,128)(2,1)S(1)} %get-tuple-element.145), channel_id=1, source_target_pairs={{0,6},{1,7},{2,4},{3,5},{4,2},{5,3},{6,0},{7,1},{8,14},{9,15},{10,... | collective-permute-start | bytes 98312 | tf_op jit(solution)/shard_map/ppermute | solution.py:454
  187.3 4.6 %collective-permute-start.34 = (bf16[32,512]{1,0:T(8,128)(2,1)S(1)}, bf16[32,512]{1,0:T(8,128)(2,1)S(1)}, u32[]{:S(2)}, u32[]{:S(2)}) collective-permute-start(bf16[32,512]{1,0:T(8,128)(2,1)S(1)} %get-tuple-element.146), channel_id=1, source_target_pairs={{0,7},{1,6},{2,5},{3,4},{4,3},{5,2},{6,1},{7,0},{8,15},{9,14},{10,... | collective-permute-start | bytes 98312 | tf_op jit(solution)/shard_map/ppermute | solution.py:454
  (21 other events, 23.9 us)

commit v6 on v5

--- a/solution.py
+++ b/solution.py
@@ -58,13 +58,13 @@
     )
 
 
-def pick_columns(store, want_mine, want_other):
+def pick_columns(store, want_mine, want_other, first_blocks):
     depth, width = store.shape
-    count = want_mine.shape[0]
-    blocks = 8
-    rows = depth // blocks
-
-    def kernel(mine_at, other_at, store_ref, mine_ref, first_ref, rest_ref, pick_mine, pick_other):
+    groups, lanes = want_mine.shape
+    count = groups * lanes
+    rows = depth // 8
+
+    def kernel(mine_held, other_held, mine_at, other_at, store_ref, mine_ref, first_ref, rest_ref, pick_mine, pick_other):
         step = pl.program_id(0)
 
         @pl.when(step == 0)
@@ -73,34 +73,52 @@
             pick_mine[...] = (column == mine_at[...]).astype(jnp.float32).astype(jnp.bfloat16)
             pick_other[...] = (column == other_at[...]).astype(jnp.float32).astype(jnp.bfloat16)
 
-        block = store_ref[...]
-        other = narrow(block, pick_other[...])
-
-        @pl.when(step < blocks // 4)
-        def _():
-            first_ref[...] = other
-
-        @pl.when(step >= blocks // 4)
-        def _():
-            rest_ref[...] = other
-
-        mine_ref[...] = narrow(block, pick_mine[...])
-
-    out = lambda part: jax.ShapeDtypeStruct((depth * part // 4, count), jnp.bfloat16)
-    index = pl.BlockSpec((1, count), lambda i: (0, 0))
+        def fill(out_ref, held, picker):
+            for g in range(groups):
+                at = slice(g * lanes, (g + 1) * lanes)
+
+                @pl.when(held[g] > 0)
+                def _():
+                    out_ref[:, at] = narrow(store_ref[...], picker[:, at])
+
+                @pl.when(held[g] == 0)
+                def _():
+                    out_ref[:, at] = jnp.zeros((rows, lanes), jnp.bfloat16)
+
+        fill(mine_ref, mine_held, pick_mine)
+
+        @pl.when(step < first_blocks)
+        def _():
+            fill(first_ref, other_held, pick_other)
+
+        @pl.when(step >= first_blocks)
+        def _():
+            fill(rest_ref, other_held, pick_other)
+
+    out = lambda blocks: jax.ShapeDtypeStruct((rows * blocks, count), jnp.bfloat16)
+    index = pl.BlockSpec((1, count), lambda i, *held: (0, 0))
     return pl.pallas_call(
         kernel,
-        grid=(blocks,),
-        in_specs=[index, index, pl.BlockSpec((rows, width), lambda i: (i, 0))],
-        out_specs=[
-            pl.BlockSpec((rows, count), lambda i: (i, 0)),
-            pl.BlockSpec((rows, count), lambda i: (jnp.minimum(i, blocks // 4 - 1), 0)),
-            pl.BlockSpec((rows, count), lambda i: (jnp.maximum(i - blocks // 4, 0), 0)),
-        ],
-        out_shape=[out(4), out(1), out(3)],
-        scratch_shapes=[pltpu.VMEM((width, count), jnp.bfloat16)] * 2,
+        grid_spec=pltpu.PrefetchScalarGridSpec(
+            num_scalar_prefetch=2,
+            grid=(8,),
+            in_specs=[index, index, pl.BlockSpec((rows, width), lambda i, *held: (i, 0))],
+            out_specs=[
+                pl.BlockSpec((rows, count), lambda i, *held: (i, 0)),
+                pl.BlockSpec((rows, count), lambda i, *held: (jnp.minimum(i, first_blocks - 1), 0)),
+                pl.BlockSpec((rows, count), lambda i, *held: (jnp.maximum(i - first_blocks, 0), 0)),
+            ],
+            scratch_shapes=[pltpu.VMEM((width, count), jnp.bfloat16)] * 2,
+        ),
+        out_shape=[out(8), out(first_blocks), out(8 - first_blocks)],
         **kernel_params(),
-    )(want_mine[None], want_other[None], store)
+    )(
+        jnp.any(want_mine >= 0, axis=1).astype(jnp.int32),
+        jnp.any(want_other >= 0, axis=1).astype(jnp.int32),
+        want_mine.reshape(1, -1),
+        want_other.reshape(1, -1),
+        store,
+    )
 
 
 def place_rows(rows, hot_target, cold_target, tag, hot_rows, cold_rows):
@@ -186,51 +204,17 @@
     )(lax.axis_index("tp").astype(jnp.int32)[None], rows, weight)
 
 
-def hot_shrink(blocks, factors, before=None):
-    near = factors[0][1][0].shape[1] // R
-    served, kept = blocks[0].shape[0], near * R
-    count = len(blocks)
-    pieces = [piece for _, pair in factors for piece in pair]
-
-    def kernel(*refs):
-        *in_refs, out_ref = refs
-        rows = in_refs[:count]
-        piece_refs = in_refs[count:count + len(pieces)]
-        total = in_refs[-1][...] if before is not None else None
-        for n, (first, pair) in enumerate(factors):
-            depth = pair[0].shape[0]
-            factor = piece_refs[2 * n][...] + piece_refs[2 * n + 1][...]
-            block = jnp.concatenate([row[:, first:first + depth] for row in rows], axis=0)
-            product = matmul(block, factor)
-            total = product if total is None else total + product
-        if before is None:
-            out_ref[...] = total
-            return
-        total = total.reshape(count, near, HCAP, kept)
-        at_step = lax.broadcasted_iota(jnp.int32, (count, HCAP, kept), 2) // R
-        z = sum(jnp.where(at_step == i, total[:, i], 0.0) for i in range(near))
-        out_ref[...] = z.reshape(count * HCAP, kept)
-
-    out_rows = count * (served if before is None else HCAP)
-    return pl.pallas_call(
-        kernel,
-        out_shape=jax.ShapeDtypeStruct((out_rows, kept), jnp.float32),
-        **kernel_params(),
-    )(*blocks, *pieces, *(() if before is None else (before,)))
-
-
 def hot_expand(z_own, z_got, expand):
-    kept, head = expand[0].shape
+    kept, head = expand.shape
     near = kept // R
     count = z_own.shape[0] // HCAP
 
-    def kernel(own_ref, got_ref, first_ref, second_ref, *out_refs):
+    def kernel(own_ref, got_ref, expand_ref, *out_refs):
         z = (own_ref[...] + got_ref[...]).astype(jnp.bfloat16).astype(jnp.float32).reshape(count, 1, HCAP, kept)
         shape = (count, near, HCAP, kept)
         same = lax.broadcasted_iota(jnp.int32, shape, 3) // R == lax.broadcasted_iota(jnp.int32, shape, 1)
         spread = jnp.where(same, jnp.broadcast_to(z, shape), 0.0).astype(jnp.bfloat16)
-        factor = first_ref[...] + second_ref[...]
-        delta = narrow(spread.reshape(count * near * HCAP, kept), factor)
+        delta = narrow(spread.reshape(count * near * HCAP, kept), expand_ref[...])
         for k, out_ref in enumerate(out_refs):
             out_ref[...] = delta[k * near * HCAP:(k + 1) * near * HCAP]
 
@@ -238,7 +222,7 @@
         kernel,
         out_shape=[jax.ShapeDtypeStruct((near * HCAP, head), jnp.bfloat16)] * count,
         **kernel_params(),
-    )(z_own, z_got, *expand)
+    )(z_own, z_got, expand)
 
 
 def add_hot(partial, target, blocks):
@@ -290,12 +274,13 @@
             of_steps = jnp.sum(jnp.where(entry == 2 * x + core, hot_first, 0), axis=1)
             firsts += [jnp.where(z_at == 0, of_steps[:near], of_steps[near:])]
             firsts += [jnp.where(z_at == 0, of_steps[near:], of_steps[:near])]
-        return jnp.concatenate([(f[:, None] + lane).reshape(-1) for f in firsts])
+        return jnp.stack([(f[:, None] + lane).reshape(-1) for f in firsts])
 
     want_mine, want_other = wanted(core_at), wanted(1 - core_at)
     kept = near * R
-    chunk_count = 4
-    part = depth // chunk_count
+    eighth = depth // 8
+    edges = [0, 3 * eighth, 6 * eighth, depth]
+    chunk_count = len(edges) - 1
 
     chain = Chain()
     hops = [("x", SWAP), ("z_low", SWAP)]
@@ -303,36 +288,31 @@
     while bit < far_count:
         hops.append(("z_high", [(i, i ^ bit) for i in range(far_count)]))
         bit *= 2
-
-    def cut(block, c, first, last):
-        return block[:, first * kept:last * kept] if c > 0 else block[first * kept:last * kept]
-
     mine, swapped, got, held = {}, {}, {}, {}
 
     def operand(c, stage):
         if stage == 0:
-            return cut(mine[c], c, 2, 4) + cut(swapped[c], c, 2, 4)
+            return mine[c][:, 2 * kept:] + swapped[c][:, 2 * kept:]
         if stage == 1:
-            return cut(mine[c], c, 1, 2) + cut(swapped[c], c, 1, 2) + cut(got[c, 0], c, 1, 2)
+            return mine[c][:, kept:2 * kept] + swapped[c][:, kept:2 * kept] + got[c, 0][:, kept:]
         if stage == 2:
-            held[c] = cut(mine[c], c, 0, 1) + cut(swapped[c], c, 0, 1) + cut(got[c, 0], c, 0, 1) + got[c, 1]
+            held[c] = mine[c][:, :kept] + swapped[c][:, :kept] + got[c, 0][:, :kept] + got[c, 1]
         else:
             held[c] = held[c] + got[c, stage - 1]
         return held[c]
 
     def send(c, stage, value=None):
-        value = operand(c, stage) if value is None else value
-        if c > 0:
-            value = after(value, got[c - 1, stage])
-        got[c, stage] = chain.permute(value, *hops[stage])
-
-    swapped[0] = chain.permute(narrow(pick(want_other[:, None] == column), expand_store), "core", SWAP)
-    mine[0] = narrow(pick(want_mine[:, None] == column), expand_store)
-    mine_all, other_first, other_rest = pick_columns(after(shrink_store, chain.last), want_mine, want_other)
+        got[c, stage] = chain.permute(operand(c, stage) if value is None else value, *hops[stage])
+
+    mine_all, other_first, other_rest = pick_columns(shrink_store, want_mine, want_other, 3)
+    mine[0], swapped[0] = mine_all[:edges[1]], chain.permute(other_first, "core", SWAP)
+    rest_swapped = chain.permute(other_rest, "core", SWAP)
     send(0, 0)
-    first_swapped = chain.permute(other_first, "core", SWAP)
-    rest_swapped = chain.permute(other_rest, "core", SWAP)
-    mine[1], swapped[1] = mine_all[:part], first_swapped
+
+    by_server = hot_first.reshape(2, near, hot_count).transpose(0, 2, 1)
+    by_server = (by_server[..., None] + lane).reshape(-1)
+    expand_hot = narrow(pick(after(by_server, chain.last)[:, None] == column), expand_store)
+    expand_part = lax.psum_scatter(expand_hot, GROUP, scatter_dimension=0, tiled=True)
 
     token_adapter = after(token_adapter, chain.last)
     cold_row = jnp.sum(jnp.where((token_adapter - hot_count)[:, :, None] == names, adapter_row, 0), axis=-1)
@@ -363,13 +343,13 @@
         sent = lax.all_to_all(sent, DP, split_axis=0, concat_axis=0, tiled=True)
         done["packet"] = sent.reshape(cold_rows, depth + TAG)
 
-    hot_in = [hot_out[:served]] + [None] * (group_count - 1)
+    done["hot_0"] = hot_out[:served]
 
     def hot_tokens_out(*blocks):
         def work():
             for k in blocks:
                 pairs = [(i, i ^ k) for i in range(group_count)]
-                hot_in[k] = chain.permute(hot_out[k * served:(k + 1) * served], GROUP, pairs)
+                done[f"hot_{k}"] = chain.permute(hot_out[k * served:(k + 1) * served], GROUP, pairs)
         return work
 
     def base_product():
@@ -378,17 +358,20 @@
         else:
             done["base"] = matmul(rows, after(value_weight, chain.last)), None
 
-    def hot_tokens_in(*blocks):
-        return lambda: chain.wait(*[hot_in[k] for k in blocks])
-
     def base_over_tp():
         own, other = done["base"]
         if other is None:
-            done["base"] = lax.psum_scatter(chain.hold(own), "tp", scatter_dimension=1, tiled=True)
-            done["base_got"] = done["base"]
+            done["base_own"] = None
+            done["base_got"] = lax.psum_scatter(chain.hold(own), "tp", scatter_dimension=1, tiled=True)
         else:
-            done["base_got"] = chain.permute(other, "tp", SWAP)
-            done["base"] = own + done["base_got"]
+            done["base_own"], done["base_got"] = own, chain.permute(other, "tp", SWAP)
+
+    def expand_over_far():
+        own = after(expand_part, chain.last)
+        if far_count == 2:
+            done["expand_own"], done["expand_got"] = own, chain.permute(own, "z_high", SWAP)
+        else:
+            done["expand_own"], done["expand_got"] = jnp.zeros_like(own), lax.psum(chain.hold(own), "z_high")
 
     def cold_shrink():
         tag_in = done["packet"][:, depth:depth + 1].astype(jnp.int32)
@@ -407,42 +390,57 @@
         delta = lax.all_to_all(delta, DP, split_axis=0, concat_axis=0, tiled=True)
         done["delta_cold"] = delta.reshape(cold_rows, head_part)
 
+    cold_tokens_out()
+    base_product()
     between = {
-        (1, "x"): [cold_tokens_out],
-        (2, "end"): [hot_tokens_out(1, 4), base_product],
-        (3, "end"): [hot_tokens_out(5), cold_shrink],
-        (4, "x"): [hot_tokens_out(2, 3), base_over_tp],
-        (4, "end"): [hot_tokens_in(1, 4), cold_over_tp],
-        (5, "x"): [hot_tokens_out(6, 7)],
-        (5, "end"): [hot_tokens_in(5, 2, 3), cold_expand],
-        (6, "x"): [cold_back],
+        1: [hot_tokens_out(4, 5, 1)],
+        2: [cold_shrink, cold_over_tp, base_over_tp],
+        3: [hot_tokens_out(6, 7, 2, 3), expand_over_far, cold_expand, cold_back],
     }
-    ready = operand(1, 0)
-    for slot in range(1, chunk_count + 1 + len(hops) - 1):
-        for stage in range(len(hops)):
-            c = slot - stage
-            if 0 <= c <= chunk_count:
-                send(c, stage, ready if stage == 0 else None)
-                if stage == 0 and c < chunk_count:
-                    mine[c + 1] = after(mine_all, chain.last)[c * part:(c + 1) * part]
-                    swapped[c + 1] = after(rest_swapped, chain.last)[(c - 1) * part:c * part]
-                    ready = chain.hold(operand(c + 1, 0))
-            if stage == 0:
-                for work in between.get((slot, "x"), []):
-                    work()
-        for work in between.get((slot, "end"), []):
+    awaited = {
+        1: ["packet", "hot_4", "hot_5", "hot_1"],
+        2: ["z_cold"],
+        3: ["hot_6", "hot_7", "hot_2", "hot_3", "expand_got", "base_got"],
+        4: ["delta_cold"],
+    }
+    ready = None
+    for slot in range(chunk_count + len(hops) - 1):
+        if slot > 0:
+            for stage in sorted(range(len(hops)), key=lambda stage: stage == 1):
+                if 0 <= slot - stage < chunk_count:
+                    send(slot - stage, stage, ready if stage == 0 else None)
+        for work in between.get(slot, []):
             work()
-    chain.wait(hot_in[6], hot_in[7], done["base_got"])
-    expand_hot, *shrink_hot = [(held[c], got[c, len(hops) - 1]) for c in range(chunk_count + 1)]
-    shrink_hot = [(c * part, pair) for c, pair in enumerate(shrink_hot)]
+        c = slot + 1
+        if c < chunk_count:
+            mine[c] = after(mine_all, chain.last)[edges[c]:edges[c + 1]]
+            swapped[c] = after(rest_swapped, chain.last)[edges[c] - edges[1]:edges[c + 1] - edges[1]]
+            ready = chain.hold(operand(c, 0))
+        here = [(slot - stage, stage) for stage in range(len(hops)) if 0 <= slot - stage < chunk_count]
+        names_here = awaited.get(slot, [])
+        arrived = lax.optimization_barrier(
+            (chain.last, *[got[at] for at in here], *[done[name] for name in names_here])
+        )
+        chain.last = arrived[0]
+        got.update(zip(here, arrived[1:]))
+        done.update(zip(names_here, arrived[1 + len(here):]))
+    base = done["base_own"] + done["base_got"] if done["base_own"] is not None else done["base_got"]
+    expand_hot = done["expand_own"] + done["expand_got"]
 
     place_cold = pick(jnp.arange(cold_rows, dtype=jnp.int32)[:, None] == cold_target)
-    partial = done["base"] + lax.dot_general(
+    partial = base + lax.dot_general(
         place_cold, done["delta_cold"], (((0,), (0,)), ((), ())), preferred_element_type=jnp.float32
     )
 
-    dense = hot_shrink(hot_in, shrink_hot[:-1])
-    z_part = hot_shrink(hot_in, shrink_hot[-1:], dense)
+    hot_in = jnp.concatenate([done[f"hot_{k}"] for k in range(group_count)], axis=0)
+    dense = None
+    for c in range(chunk_count):
+        for piece in (held[c], got[c, len(hops) - 1]):
+            product = matmul(hot_in[:, edges[c]:edges[c + 1]], piece)
+            dense = product if dense is None else dense + product
+    dense = dense.reshape(group_count, near, HCAP, kept)
+    at_step = jnp.arange(kept) // R
+    z_part = sum(jnp.where(at_step == i, dense[:, i], 0.0) for i in range(near)).reshape(group_count * HCAP, kept)
     z_part, partial = lax.optimization_barrier((z_part, partial))
     if lax.axis_size("tp") == 2:
         z_got = lax.ppermute(z_part, "tp", SWAP)

time: 194 us -> 222 us (1.14)
  between operations: 0.41 us -> 13.9 us
  waiting for transfers between devices: 66.9 us -> 79.7 us
  matrix products: 6.76 us -> 14 us
  Pallas kernels: 27.7 us -> 20.6 us
    ppermute x26 -> x20, waiting for transfers between devices: 41.7 us -> 74.7 us  [permute(): return lax.ppermute(self.hold(value), axis, pairs)]
    ppermute x1, waiting for transfers between devices: 19.3 us -> 0.01 us  [sum_over_tp(): return part + lax.ppermute(part, 'tp', SWAP)]
    dot_general x4 -> x9, matrix products: 5.1 us -> 12.3 us  [matmul(): return jnp.dot(a, b, preferred_element_type=jnp.float32)]
    pallas_call x3 -> x1, Pallas kernels: 11.4 us -> 6.31 us  [pick_columns(): pl.pallas_call(kernel, grid_spec=pltpu.PrefetchScalarGridSpec(num_scalar_...]
    add x23 -> x21, other arithmetic: 19.1 us -> 17.7 us  [the longest x3 5.93 us: operand(): mine[c][:, :kept] + swapped[c][:, :kept] + got[c, 0][:, :kept] + got[c, 1]]
    ppermute x26 -> x20, starting transfers between devices: 28.9 us -> 27.9 us  [permute(): return lax.ppermute(self.hold(value), axis, pairs)]
    unnamed x70 -> x51, local copies, waits for them, and re-layouts: 20.9 us -> 21.6 us
  transfers between devices with their start and end apart: 37 -> 32, of which waited for: 12 -> 12; matrix products, arithmetic and copies ran while one was open for 14% -> 19% of each run, Pallas kernels for 13% -> 6%
where the time goes in v6:
time: 222 us; the launch traced here: 221 us
  waiting for transfers between devices  79.7 us (36%)
  starting transfers between devices  48.3 us (22%)
  local copies, waits for them, and re-layouts  24.3 us (11%)
  other arithmetic  20.8 us (9%)
  Pallas kernels  20.6 us (9%)
  matrix products  14 us (6%)
  between operations  13.9 us (6%)
    ppermute x20, waiting for transfers between devices, permute(): return lax.ppermute(self.hold(value), axis, pairs)  74.7 us
    ppermute x20, starting transfers between devices, permute(): return lax.ppermute(self.hold(value), axis, pairs)  27.9 us
    unnamed x51, local copies, waits for them, and re-layouts  21.6 us
    dot_general x9, matrix products, matmul(): return jnp.dot(a, b, preferred_element_type=jnp.float32)  12.3 us
    pallas_call x1, Pallas kernels, base_halves(): pl.pallas_call(kernel, grid_spec=pltpu.PrefetchScalarGridSpec(num_scalar_...  9.96 us
    ppermute x7, starting transfers between devices, on_device(): lax.ppermute(delta_hot[k], GROUP, [(i, i ^ k) for i in range(group_count)])  6.34 us
    pallas_call x1, Pallas kernels, pick_columns(): pl.pallas_call(kernel, grid_spec=pltpu.PrefetchScalarGridSpec(num_scalar_...  6.31 us
    add x3, other arithmetic, operand(): mine[c][:, :kept] + swapped[c][:, :kept] + got[c, 0][:, :kept] + got[c, 1]  5.93 us
  transfers between devices with their start and end apart: 32, of which 12 were waited for; matrix products, arithmetic and copies ran while one was open for 19% of the time, Pallas kernels for 6%

profile of v6, /device:TPU:0, one launch (start us, length us, event | category | flops | bytes accessed | tf_op | source)
XLA Modules:
  0.0 221.4 jit_solution(11597633131101906417)
XLA Ops:
  9.4 2.2 copy-done.1
  11.6 6.3 %shard_map.73 = (bf16[4096,512]{1,0:T(8,128)(2,1)S(1)}, bf16[1536,512]{1,0:T(8,128)(2,1)S(1)}, bf16[2560,512]{1,0:T(8,128)(2,1)}) custom-call(s32[4]{0:T(128)S(1)} %convert_element_type.21.mine_held, s32[4]{0:T(128)S(1)} %convert_element_type.22.other_held, s32[1,512]{1,0:T(1,128)S(1)} %bitcast.49, s32[1,512]{1,0:T(1,128)S(1)} %bitcast.50, ...), custom_call_target="tpu_custom_call" | custom-call | flops 1 | bytes 1 | tf_op jit(solution)/shard_map/pallas_call | solution.py:100
  17.9 2.0 copy-done.4
  20.7 4.3 %collective-permute-done = bf16[1536,512]{1,0:T(8,128)(2,1)} collective-permute-done((bf16[1536,512]{1,0:T(8,128)(2,1)S(1)}, bf16[1536,512]{1,0:T(8,128)(2,1)}, u32[]{:S(2)}, u32[]{:S(2)}) %collective-permute-start) | collective-permute-done | bytes 1572896 | tf_op jit(solution)/shard_map/ppermute | solution.py:48
  25.0 1.5 slice_add_fusion
  26.5 3.6 %collective-permute-start.2 = (bf16[1536,256]{1,0:T(8,128)(2,1)S(1)}, bf16[1536,256]{1,0:T(8,128)(2,1)}, u32[]{:S(2)}, u32[]{:S(2)}) collective-permute-start(bf16[1536,256]{1,0:T(8,128)(2,1)S(1)} %slice_add_fusion), channel_id=1, source_target_pairs={{0,2},{2,0},{1,3},{3,1},{4,6},{6,4},{5,7},{7,5},{8,10},{10,8},{9,1... | collective-permute-start | bytes 2359304 | tf_op jit(solution)/shard_map/ppermute | solution.py:48
  30.7 2.2 copy-done.2
  32.9 2.9 %shard_map.74 = (bf16[256,4096]{1,0:T(8,128)(2,1)S(1)}, bf16[128,4224]{1,0:T(8,128)(2,1)S(1)}) custom-call(s32[1,512]{1,0:T(1,128)S(1)} %bitcast.45, s32[1,512]{1,0:T(1,128)S(1)} %bitcast.47, s32[1,512]{1,0:T(1,128)S(1)} %fusion.29.tag_at, bf16[512,4096]{1,0:T(8,128)(2,1)S(1)} %bitcast.42), custom_call_target="tpu_custom_call" | custom-call | flops 1 | bytes 1 | tf_op jit(solution)/shard_map/pallas_call | solution.py:146
  36.9 5.7 %all-to-all-start = ((bf16[16,8,4224]{2,1,0:T(8,128)(2,1)}), bf16[16,8,4224]{2,1,0:T(8,128)(2,1)}, u32[]{:S(2)}, u32[]{:S(2)}) async-start(bf16[16,8,4224]{2,1,0:T(8,128)(2,1)} %bitcast.44), calls=%async_computation | async-start | bytes 2162688 | tf_op jit(solution)/shard_map/all_to_all | solution.py:343
  42.7 1.7 fusion.1
  44.5 1.5 slice_add_fusion.1
  45.9 4.8 %collective-permute-done.2 = bf16[1536,256]{1,0:T(8,128)(2,1)} collective-permute-done((bf16[1536,256]{1,0:T(8,128)(2,1)S(1)}, bf16[1536,256]{1,0:T(8,128)(2,1)}, u32[]{:S(2)}, u32[]{:S(2)}) %collective-permute-start.2) | collective-permute-done | bytes 786464 | tf_op jit(solution)/shard_map/ppermute | solution.py:48
  52.2 2.8 %collective-permute-start.4 = (bf16[1536,128]{1,0:T(8,128)(2,1)S(1)}, bf16[1536,128]{1,0:T(8,128)(2,1)S(1)}, u32[]{:S(2)}, u32[]{:S(2)}) collective-permute-start(bf16[1536,128]{1,0:T(8,128)(2,1)S(1)} %fusion.16), channel_id=1, source_target_pairs={{0,4},{4,0},{1,5},{5,1},{2,6},{6,2},{3,7},{7,3},{8,12},{12,8},{9,1... | collective-permute-start | bytes 1179656 | tf_op jit(solution)/shard_map/ppermute | solution.py:48
  56.2 2.0 collective-permute-start.5
  58.2 2.0 slice_add_fusion.2
  60.2 21.1 %collective-permute-done.6 = bf16[32,4096]{1,0:T(8,128)(2,1)S(1)} collective-permute-done((bf16[32,4096]{1,0:T(8,128)(2,1)S(1)}, bf16[32,4096]{1,0:T(8,128)(2,1)S(1)}, u32[]{:S(2)}, u32[]{:S(2)}) %collective-permute-start.6) | collective-permute-done | bytes 262176 | tf_op jit(solution)/shard_map/ppermute | solution.py:48
  81.3 6.4 %collective-permute-done.5 = bf16[32,4096]{1,0:T(8,128)(2,1)S(1)} collective-permute-done((bf16[32,4096]{1,0:T(8,128)(2,1)S(1)}, bf16[32,4096]{1,0:T(8,128)(2,1)S(1)}, u32[]{:S(2)}, u32[]{:S(2)}) %collective-permute-start.5) | collective-permute-done | bytes 262176 | tf_op jit(solution)/shard_map/ppermute | solution.py:48
  88.5 2.5 %fusion.15 = bf16[1536,128]{1,0:T(8,128)(2,1)} fusion(bf16[1536,128]{1,0:T(8,128)(2,1)} %copy-done.10, bf16[1536,512]{1,0:T(8,128)(2,1)} %collective-permute-done, bf16[1536,256]{1,0:T(8,128)(2,1)} %collective-permute-done.2, bf16[4096,512]{1,0:T(8,128)(2,1)} %copy-done.4), kind=kLoop, calls=%fused_computation.27 | loop fusion | flops 589824 | bytes 1966080 | tf_op jit(solution)/shard_map/add | solution.py:299
  91.0 2.0 slice_add_fusion.5
  93.6 2.5 %collective-permute-start.10 = (bf16[1536,128]{1,0:T(8,128)(2,1)}, bf16[1536,128]{1,0:T(8,128)(2,1)}, u32[]{:S(2)}, u32[]{:S(2)}) collective-permute-start(bf16[1536,128]{1,0:T(8,128)(2,1)} %fusion.15), channel_id=1, source_target_pairs={{0,8},{8,0},{1,9},{9,1},{2,10},{10,2},{3,11},{11,3},{4,12},{12,4},... | collective-permute-start | bytes 1179656 | tf_op jit(solution)/shard_map/ppermute | solution.py:48
  96.9 3.2 %convolution_select_fusion = f32[128,512]{1,0:T(8,128)S(1)} fusion(bf16[4096,512]{1,0:T(8,128)(2,1)} %store_ref.1, bf16[128,4224]{1,0:T(8,128)(2,1)} %bitcast.7, s32[512]{0:T(512)S(1)} %fusion.25, s32[128]{0:T(128)S(1)} %convert_reduce_fusion.1), kind=kOutput, calls=%fused_computation.3 | convolution fusion | flops 537001984 | bytes 5507584 | tf_op jit(solution)/shard_map/dot_general | solution.py:22
  100.2 1.6 collective-permute-start.11
  101.8 2.2 copy-done.3
  103.9 10.0 %shard_map.75 = (f32[512,512]{1,0:T(8,128)S(1)}, f32[512,512]{1,0:T(8,128)S(1)}) custom-call(s32[1]{0:T(128)} %bitcast.8.tp_at, bf16[512,4096]{1,0:T(8,128)(2,1)S(1)} %bitcast.43, bf16[4096,1024]{1,0:T(8,128)(2,1)} %weight_ref), custom_call_target="tpu_custom_call" | custom-call | flops 1 | bytes 1 | tf_op jit(solution)/shard_map/pallas_call | solution.py:190
  115.6 2.1 add_add_fusion.1
  117.7 1.9 slice_add_fusion.6
  121.5 2.1 collective-permute-start.15
  123.7 7.2 %collective-permute-done.18 = bf16[128,512]{1,0:T(8,128)(2,1)S(1)} collective-permute-done((bf16[128,512]{1,0:T(8,128)(2,1)}, bf16[128,512]{1,0:T(8,128)(2,1)S(1)}, u32[]{:S(2)}, u32[]{:S(2)}) %collective-permute-start.18) | collective-permute-done | bytes 131104 | tf_op jit(solution)/shard_map/ppermute | solution.py:48
  131.1 10.2 %collective-permute-start.12 = (bf16[1024,128]{1,0:T(8,128)(2,1)}, bf16[1024,128]{1,0:T(8,128)(2,1)}, u32[]{:S(2)}, u32[]{:S(2)}) collective-permute-start(bf16[1024,128]{1,0:T(8,128)(2,1)} %slice_add_fusion.6), channel_id=1, source_target_pairs={{0,4},{4,0},{1,5},{5,1},{2,6},{6,2},{3,7},{7,3},{8,12},{12,8},{9,1... | collective-permute-start | bytes 786440 | tf_op jit(solution)/shard_map/ppermute | solution.py:48
  141.3 3.5 %collective-permute-done.16 = bf16[32,4096]{1,0:T(8,128)(2,1)} collective-permute-done((bf16[32,4096]{1,0:T(8,128)(2,1)S(1)}, bf16[32,4096]{1,0:T(8,128)(2,1)}, u32[]{:S(2)}, u32[]{:S(2)}) %collective-permute-start.16) | collective-permute-done | bytes 262176 | tf_op jit(solution)/shard_map/ppermute | solution.py:48
  145.5 1.7 constant_dynamic-update-slice_fusion.6
  148.1 5.0 %all-to-all-start.1 = ((bf16[16,8,512]{2,1,0:T(8,128)(2,1)}), bf16[16,8,512]{2,1,0:T(8,128)(2,1)S(1)}, u32[]{:S(2)}, u32[]{:S(2)}) async-start(bf16[16,8,512]{2,1,0:T(8,128)(2,1)} %fusion.2), calls=%async_computation.2 | async-start | bytes 262144 | tf_op jit(solution)/shard_map/all_to_all | solution.py:390
  153.1 14.6 %collective-permute-done.13 = bf16[1536,128]{1,0:T(8,128)(2,1)S(1)} collective-permute-done((bf16[1536,128]{1,0:T(8,128)(2,1)}, bf16[1536,128]{1,0:T(8,128)(2,1)S(1)}, u32[]{:S(2)}, u32[]{:S(2)}) %collective-permute-start.13) | collective-permute-done | bytes 393248 | tf_op jit(solution)/shard_map/ppermute | solution.py:48
  169.1 1.7 constant_dynamic-update-slice_fusion.5
  170.7 1.7 constant_dynamic-update-slice_fusion.4
  172.5 1.7 constant_dynamic-update-slice_fusion.3
  174.2 1.7 constant_dynamic-update-slice_fusion.2
  175.8 1.7 constant_dynamic-update-slice_fusion.1
  177.5 1.7 constant_dynamic-update-slice_fusion
  179.3 1.5 fusion.12
  180.7 1.6 fusion.8
  184.5 12.5 %collective-permute-done.20 = bf16[1024,128]{1,0:T(8,128)(2,1)S(1)} collective-permute-done((bf16[1024,128]{1,0:T(8,128)(2,1)S(1)}, bf16[1024,128]{1,0:T(8,128)(2,1)S(1)}, u32[]{:S(2)}, u32[]{:S(2)}) %collective-permute-start.20) | collective-permute-done | bytes 262176 | tf_op jit(solution)/shard_map/ppermute | solution.py:48
  198.4 1.7 add_add_fusion.partial_ref
  200.1 1.6 collective-permute-start.21
  201.7 2.7 %collective-permute-done.21.got_ref = f32[128,128]{1,0:T(8,128)S(1)} collective-permute-done((f32[128,128]{1,0:T(8,128)S(1)}, f32[128,128]{1,0:T(8,128)S(1)}, u32[]{:S(2)}, u32[]{:S(2)}) %collective-permute-start.21) | collective-permute-done | bytes 65568 | tf_op jit(solution)/shard_map/ppermute | solution.py:446
  206.6 1.7 collective-permute-start.26
  208.9 2.1 collective-permute-start.28
  211.2 2.2 %collective-permute-done.27.refs_6_ = bf16[32,512]{1,0:T(8,128)(2,1)S(1)} collective-permute-done((bf16[32,512]{1,0:T(8,128)(2,1)S(1)}, bf16[32,512]{1,0:T(8,128)(2,1)S(1)}, u32[]{:S(2)}, u32[]{:S(2)}) %collective-permute-start.27) | collective-permute-done | bytes 32800 | tf_op jit(solution)/shard_map/ppermute | solution.py:452
  (141 shorter events, 24.7 us)
Async XLA Ops:
  6.5 36.2 %copy-start = (bf16[512,512]{1,0:T(8,128)(2,1)S(1)}, bf16[512,512]{1,0:T(8,128)(2,1)}, u32[]{:S(2)}) copy-start(bf16[512,512]{1,0:T(8,128)(2,1)} %param.10) | copy-start | bytes 1572868
  19.9 10.2 %copy-start.20 = (s32[4,128]{1,0:T(4,128)S(1)}, s32[4,128]{1,0:T(4,128)}, u32[]{:S(2)}) copy-start(s32[4,128]{1,0:T(4,128)} %param.12) | copy-start | bytes 6148
  19.9 10.2 %copy-start.21 = (s32[128]{0:T(128)S(1)}, s32[128]{0:T(128)}, u32[]{:S(2)}) copy-start(s32[128]{0:T(128)} %param.11) | copy-start | bytes 1540
  19.9 5.1 %collective-permute-start = (bf16[1536,512]{1,0:T(8,128)(2,1)S(1)}, bf16[1536,512]{1,0:T(8,128)(2,1)}, u32[]{:S(2)}, u32[]{:S(2)}) collective-permute-start(bf16[1536,512]{1,0:T(8,128)(2,1)S(1)} %get-tuple-element.74), channel_id=1, source_target_pairs={{0,1},{1,0},{2,3},{3,2},{4,5},{5,4},{6,7},{7,6},{8,9},{9,8},{10,11... | collective-permute-start | bytes 4718600 | tf_op jit(solution)/shard_map/ppermute | solution.py:48
  20.3 24.2 %collective-permute-start.1 = (bf16[2560,512]{1,0:T(8,128)(2,1)}, bf16[2560,512]{1,0:T(8,128)(2,1)}, u32[]{:S(2)}, u32[]{:S(2)}) collective-permute-start(bf16[2560,512]{1,0:T(8,128)(2,1)} %get-tuple-element.76), channel_id=1, source_target_pairs={{0,1},{1,0},{2,3},{3,2},{4,5},{5,4},{6,7},{7,6},{8,9},{9,8},{10,11... | collective-permute-start | bytes 7864328 | tf_op jit(solution)/shard_map/ppermute | solution.py:48
  26.5 24.3 %collective-permute-start.2 = (bf16[1536,256]{1,0:T(8,128)(2,1)S(1)}, bf16[1536,256]{1,0:T(8,128)(2,1)}, u32[]{:S(2)}, u32[]{:S(2)}) collective-permute-start(bf16[1536,256]{1,0:T(8,128)(2,1)S(1)} %slice_add_fusion), channel_id=1, source_target_pairs={{0,2},{2,0},{1,3},{3,1},{4,6},{6,4},{5,7},{7,5},{8,10},{10,8},{9,1... | collective-permute-start | bytes 2359304 | tf_op jit(solution)/shard_map/ppermute | solution.py:48
  36.9 51.6 %all-to-all-start = ((bf16[16,8,4224]{2,1,0:T(8,128)(2,1)}), bf16[16,8,4224]{2,1,0:T(8,128)(2,1)}, u32[]{:S(2)}, u32[]{:S(2)}) async-start(bf16[16,8,4224]{2,1,0:T(8,128)(2,1)} %bitcast.44), calls=%async_computation | async-start | bytes 2162688 | tf_op jit(solution)/shard_map/all_to_all | solution.py:343
  42.6 78.3 %reduce-scatter.2.cloned.1.call-start = ((), (), s32[]{:S(2)}) async-start(), calls=%async_computation.3 | async-start | bytes 1179648 | tf_op jit(solution)/shard_map/reduce_scatter | solution.py:315
  50.7 37.8 %collective-permute-start.3 = (bf16[1536,256]{1,0:T(8,128)(2,1)S(1)}, bf16[1536,256]{1,0:T(8,128)(2,1)S(1)}, u32[]{:S(2)}, u32[]{:S(2)}) collective-permute-start(bf16[1536,256]{1,0:T(8,128)(2,1)S(1)} %slice_add_fusion.1), channel_id=1, source_target_pairs={{0,2},{2,0},{1,3},{3,1},{4,6},{6,4},{5,7},{7,5},{8,10},{10,8},{9,1... | collective-permute-start | bytes 2359304 | tf_op jit(solution)/shard_map/ppermute | solution.py:48
  52.2 35.5 %collective-permute-start.4 = (bf16[1536,128]{1,0:T(8,128)(2,1)S(1)}, bf16[1536,128]{1,0:T(8,128)(2,1)S(1)}, u32[]{:S(2)}, u32[]{:S(2)}) collective-permute-start(bf16[1536,128]{1,0:T(8,128)(2,1)S(1)} %fusion.16), channel_id=1, source_target_pairs={{0,4},{4,0},{1,5},{5,1},{2,6},{6,2},{3,7},{7,3},{8,12},{12,8},{9,1... | collective-permute-start | bytes 1179656 | tf_op jit(solution)/shard_map/ppermute | solution.py:48
  56.0 4.2 %collective-permute-start.7 = (bf16[32,4096]{1,0:T(8,128)(2,1)S(1)}, bf16[32,4096]{1,0:T(8,128)(2,1)S(1)}, u32[]{:S(2)}, u32[]{:S(2)}) collective-permute-start(bf16[32,4096]{1,0:T(8,128)(2,1)S(1)} %get-tuple-element.89), channel_id=1, source_target_pairs={{0,1},{1,0},{2,3},{3,2},{4,5},{5,4},{6,7},{7,6},{8,9},{9,8},{10,11... | collective-permute-start | bytes 786440 | tf_op jit(solution)/shard_map/ppermute | solution.py:48
  56.0 25.3 %collective-permute-start.6 = (bf16[32,4096]{1,0:T(8,128)(2,1)S(1)}, bf16[32,4096]{1,0:T(8,128)(2,1)S(1)}, u32[]{:S(2)}, u32[]{:S(2)}) collective-permute-start(bf16[32,4096]{1,0:T(8,128)(2,1)S(1)} %get-tuple-element.88), channel_id=1, source_target_pairs={{0,5},{1,4},{2,7},{3,6},{4,1},{5,0},{6,3},{7,2},{8,13},{9,12},{10,... | collective-permute-start | bytes 786440 | tf_op jit(solution)/shard_map/ppermute | solution.py:48
  56.2 31.5 %collective-permute-start.5 = (bf16[32,4096]{1,0:T(8,128)(2,1)S(1)}, bf16[32,4096]{1,0:T(8,128)(2,1)S(1)}, u32[]{:S(2)}, u32[]{:S(2)}) collective-permute-start(bf16[32,4096]{1,0:T(8,128)(2,1)S(1)} %get-tuple-element.87), channel_id=1, source_target_pairs={{0,4},{1,5},{2,6},{3,7},{4,0},{5,1},{6,2},{7,3},{8,12},{9,13},{10,... | collective-permute-start | bytes 786440 | tf_op jit(solution)/shard_map/ppermute | solution.py:48
  60.2 41.5 %copy-start.15 = (bf16[32,4096]{1,0:T(8,128)(2,1)}, bf16[32,4096]{1,0:T(8,128)(2,1)S(1)}, u32[]{:S(2)}) copy-start(bf16[32,4096]{1,0:T(8,128)(2,1)S(1)} %collective-permute-done.7) | copy-start | bytes 786436
  60.2 55.3 %collective-permute-start.8 = (bf16[1024,256]{1,0:T(8,128)(2,1)}, bf16[1024,256]{1,0:T(8,128)(2,1)}, u32[]{:S(2)}, u32[]{:S(2)}) collective-permute-start(bf16[1024,256]{1,0:T(8,128)(2,1)} %slice_add_fusion.2), channel_id=1, source_target_pairs={{0,2},{2,0},{1,3},{3,1},{4,6},{6,4},{5,7},{7,5},{8,10},{10,8},{9,1... | collective-permute-start | bytes 1572872 | tf_op jit(solution)/shard_map/ppermute | solution.py:48
  81.3 20.5 %copy-start.13 = (bf16[32,4096]{1,0:T(8,128)(2,1)}, bf16[32,4096]{1,0:T(8,128)(2,1)S(1)}, u32[]{:S(2)}) copy-start(bf16[32,4096]{1,0:T(8,128)(2,1)S(1)} %collective-permute-done.6) | copy-start | bytes 786436
  87.7 14.1 %copy-start.14 = (bf16[32,4096]{1,0:T(8,128)(2,1)}, bf16[32,4096]{1,0:T(8,128)(2,1)S(1)}, u32[]{:S(2)}) copy-start(bf16[32,4096]{1,0:T(8,128)(2,1)S(1)} %collective-permute-done.5) | copy-start | bytes 786436
  88.5 7.6 %copy-start.7 = (bf16[1536,256]{1,0:T(8,128)(2,1)}, bf16[1536,256]{1,0:T(8,128)(2,1)S(1)}, u32[]{:S(2)}) copy-start(bf16[1536,256]{1,0:T(8,128)(2,1)S(1)} %collective-permute-done.3) | copy-start | bytes 2359300
  92.9 22.6 %collective-permute-start.9 = (bf16[1536,128]{1,0:T(8,128)(2,1)}, bf16[1536,128]{1,0:T(8,128)(2,1)}, u32[]{:S(2)}, u32[]{:S(2)}) collective-permute-start(bf16[1536,128]{1,0:T(8,128)(2,1)} %slice_add_fusion.5), channel_id=1, source_target_pairs={{0,4},{4,0},{1,5},{5,1},{2,6},{6,2},{3,7},{7,3},{8,12},{12,8},{9,1... | collective-permute-start | bytes 1179656 | tf_op jit(solution)/shard_map/ppermute | solution.py:48
  93.6 22.0 %collective-permute-start.10 = (bf16[1536,128]{1,0:T(8,128)(2,1)}, bf16[1536,128]{1,0:T(8,128)(2,1)}, u32[]{:S(2)}, u32[]{:S(2)}) collective-permute-start(bf16[1536,128]{1,0:T(8,128)(2,1)} %fusion.15), channel_id=1, source_target_pairs={{0,8},{8,0},{1,9},{9,1},{2,10},{10,2},{3,11},{11,3},{4,12},{12,4},... | collective-permute-start | bytes 1179656 | tf_op jit(solution)/shard_map/ppermute | solution.py:48
  100.2 14.3 %collective-permute-start.11 = (f32[128,512]{1,0:T(8,128)S(1)}, f32[128,512]{1,0:T(8,128)}, u32[]{:S(2)}, u32[]{:S(2)}) collective-permute-start(f32[128,512]{1,0:T(8,128)S(1)} %convolution_select_fusion), channel_id=1, source_target_pairs={{0,16},{16,0},{1,17},{17,1},{2,18},{18,2},{3,19},{19,3},{4,20},{20... | collective-permute-start | bytes 786440 | tf_op jit(solution)/shard_map/ppermute | solution.py:31
  103.9 11.6 %copy-start.8 = (bf16[1536,256]{1,0:T(8,128)(2,1)S(1)}, bf16[1536,256]{1,0:T(8,128)(2,1)}, u32[]{:S(2)}) copy-start(bf16[1536,256]{1,0:T(8,128)(2,1)} %copy-done.7) | copy-start | bytes 2359300
  113.9 5.6 %copy-start.12 = (bf16[32,4096]{1,0:T(8,128)(2,1)S(1)}, bf16[32,4096]{1,0:T(8,128)(2,1)}, u32[]{:S(2)}) copy-start(bf16[32,4096]{1,0:T(8,128)(2,1)} %get-tuple-element.112) | copy-start | bytes 786436
  113.9 5.6 %copy-start.11 = (bf16[32,4096]{1,0:T(8,128)(2,1)S(1)}, bf16[32,4096]{1,0:T(8,128)(2,1)}, u32[]{:S(2)}) copy-start(bf16[32,4096]{1,0:T(8,128)(2,1)} %get-tuple-element.111) | copy-start | bytes 786436
  113.9 53.8 %collective-permute-start.19 = (f32[512,512]{1,0:T(8,128)S(1)}, f32[512,512]{1,0:T(8,128)}, u32[]{:S(2)}, u32[]{:S(2)}) collective-permute-start(f32[512,512]{1,0:T(8,128)S(1)} %get-tuple-element.103), channel_id=1, source_target_pairs={{0,16},{16,0},{1,17},{17,1},{2,18},{18,2},{3,19},{19,3},{4,20},{20... | collective-permute-start | bytes 3145736 | tf_op jit(solution)/shard_map/ppermute | solution.py:48
  119.5 11.6 %collective-permute-start.17 = (bf16[32,4096]{1,0:T(8,128)(2,1)S(1)}, bf16[32,4096]{1,0:T(8,128)(2,1)S(1)}, u32[]{:S(2)}, u32[]{:S(2)}) collective-permute-start(bf16[32,4096]{1,0:T(8,128)(2,1)S(1)} %copy-done.12), channel_id=1, source_target_pairs={{0,3},{1,2},{2,1},{3,0},{4,7},{5,6},{6,5},{7,4},{8,11},{9,10},{10,... | collective-permute-start | bytes 786440 | tf_op jit(solution)/shard_map/ppermute | solution.py:48
  119.5 25.3 %collective-permute-start.16 = (bf16[32,4096]{1,0:T(8,128)(2,1)S(1)}, bf16[32,4096]{1,0:T(8,128)(2,1)}, u32[]{:S(2)}, u32[]{:S(2)}) collective-permute-start(bf16[32,4096]{1,0:T(8,128)(2,1)S(1)} %copy-done.11), channel_id=1, source_target_pairs={{0,2},{1,3},{2,0},{3,1},{4,6},{5,7},{6,4},{7,5},{8,10},{9,11},{10,... | collective-permute-start | bytes 786440 | tf_op jit(solution)/shard_map/ppermute | solution.py:48
  120.9 9.9 %collective-permute-start.18 = (bf16[128,512]{1,0:T(8,128)(2,1)}, bf16[128,512]{1,0:T(8,128)(2,1)S(1)}, u32[]{:S(2)}, u32[]{:S(2)}) collective-permute-start(bf16[128,512]{1,0:T(8,128)(2,1)} %reduce-scatter.2.cloned.1.call-done), channel_id=1, source_target_pairs={{0,8},{8,0},{1,9},{9,1},{2,10},{10,2},{3,11},{11,3},{4,12},{12,4},... | collective-permute-start | bytes 393224 | tf_op jit(solution)/shard_map/ppermute | solution.py:48
  121.5 31.5 %collective-permute-start.15 = (bf16[32,4096]{1,0:T(8,128)(2,1)}, bf16[32,4096]{1,0:T(8,128)(2,1)}, u32[]{:S(2)}, u32[]{:S(2)}) collective-permute-start(bf16[32,4096]{1,0:T(8,128)(2,1)} %get-tuple-element.110), channel_id=1, source_target_pairs={{0,7},{1,6},{2,5},{3,4},{4,3},{5,2},{6,1},{7,0},{8,15},{9,14},{10,... | collective-permute-start | bytes 786440 | tf_op jit(solution)/shard_map/ppermute | solution.py:48
  130.9 14.0 %copy-start.18 = (bf16[128,512]{1,0:T(8,128)(2,1)}, bf16[128,512]{1,0:T(8,128)(2,1)S(1)}, u32[]{:S(2)}) copy-start(bf16[128,512]{1,0:T(8,128)(2,1)S(1)} %collective-permute-done.18) | copy-start | bytes 393220
  130.9 22.2 %collective-permute-start.14 = (bf16[32,4096]{1,0:T(8,128)(2,1)}, bf16[32,4096]{1,0:T(8,128)(2,1)}, u32[]{:S(2)}, u32[]{:S(2)}) collective-permute-start(bf16[32,4096]{1,0:T(8,128)(2,1)} %get-tuple-element.109), channel_id=1, source_target_pairs={{0,6},{1,7},{2,4},{3,5},{4,2},{5,3},{6,0},{7,1},{8,14},{9,15},{10,... | collective-permute-start | bytes 786440 | tf_op jit(solution)/shard_map/ppermute | solution.py:48
  131.1 16.9 %copy-start.16 = (bf16[32,4096]{1,0:T(8,128)(2,1)}, bf16[32,4096]{1,0:T(8,128)(2,1)S(1)}, u32[]{:S(2)}) copy-start(bf16[32,4096]{1,0:T(8,128)(2,1)S(1)} %collective-permute-done.17) | copy-start | bytes 786436
  131.1 22.0 %collective-permute-start.12 = (bf16[1024,128]{1,0:T(8,128)(2,1)}, bf16[1024,128]{1,0:T(8,128)(2,1)}, u32[]{:S(2)}, u32[]{:S(2)}) collective-permute-start(bf16[1024,128]{1,0:T(8,128)(2,1)} %slice_add_fusion.6), channel_id=1, source_target_pairs={{0,4},{4,0},{1,5},{5,1},{2,6},{6,2},{3,7},{7,3},{8,12},{12,8},{9,1... | collective-permute-start | bytes 786440 | tf_op jit(solution)/shard_map/ppermute | solution.py:48
  144.9 22.9 %collective-permute-start.13 = (bf16[1536,128]{1,0:T(8,128)(2,1)}, bf16[1536,128]{1,0:T(8,128)(2,1)S(1)}, u32[]{:S(2)}, u32[]{:S(2)}) collective-permute-start(bf16[1536,128]{1,0:T(8,128)(2,1)} %add_add_fusion.1), channel_id=1, source_target_pairs={{0,8},{8,0},{1,9},{9,1},{2,10},{10,2},{3,11},{11,3},{4,12},{12,4},... | collective-permute-start | bytes 1179656 | tf_op jit(solution)/shard_map/ppermute | solution.py:48
  148.1 36.4 %all-to-all-start.1 = ((bf16[16,8,512]{2,1,0:T(8,128)(2,1)}), bf16[16,8,512]{2,1,0:T(8,128)(2,1)S(1)}, u32[]{:S(2)}, u32[]{:S(2)}) async-start(bf16[16,8,512]{2,1,0:T(8,128)(2,1)} %fusion.2), calls=%async_computation.2 | async-start | bytes 262144 | tf_op jit(solution)/shard_map/all_to_all | solution.py:390
  177.5 6.2 %copy-start.9 = (bf16[1536,128]{1,0:T(8,128)(2,1)S(1)}, bf16[1536,128]{1,0:T(8,128)(2,1)}, u32[]{:S(2)}) copy-start(bf16[1536,128]{1,0:T(8,128)(2,1)} %add_add_fusion.1) | copy-start | bytes 1179652
  179.3 3.1 %copy-start.6 = (bf16[256,4096]{1,0:T(8,128)(2,1)S(1)}, bf16[256,4096]{1,0:T(8,128)(2,1)}, u32[]{:S(2)}) copy-start(bf16[256,4096]{1,0:T(8,128)(2,1)} %constant_dynamic-update-slice_fusion) | copy-start | bytes 6291460
  184.1 12.9 %collective-permute-start.20 = (bf16[1024,128]{1,0:T(8,128)(2,1)S(1)}, bf16[1024,128]{1,0:T(8,128)(2,1)S(1)}, u32[]{:S(2)}, u32[]{:S(2)}) collective-permute-start(bf16[1024,128]{1,0:T(8,128)(2,1)S(1)} %add_add_fusion.2), channel_id=1, source_target_pairs={{0,8},{8,0},{1,9},{9,1},{2,10},{10,2},{3,11},{11,3},{4,12},{12,4},... | collective-permute-start | bytes 786440 | tf_op jit(solution)/shard_map/ppermute | solution.py:48
  198.3 3.4 %copy-start.17 = (bf16[128,512]{1,0:T(8,128)(2,1)S(1)}, bf16[128,512]{1,0:T(8,128)(2,1)}, u32[]{:S(2)}) copy-start(bf16[128,512]{1,0:T(8,128)(2,1)} %reduce-scatter.2.cloned.1.call-done) | copy-start | bytes 393220
  198.3 3.4 %copy-start.19 = (bf16[128,512]{1,0:T(8,128)(2,1)S(1)}, bf16[128,512]{1,0:T(8,128)(2,1)}, u32[]{:S(2)}) copy-start(bf16[128,512]{1,0:T(8,128)(2,1)} %copy-done.18) | copy-start | bytes 393220
  200.1 4.3 %collective-permute-start.21 = (f32[128,128]{1,0:T(8,128)S(1)}, f32[128,128]{1,0:T(8,128)S(1)}, u32[]{:S(2)}, u32[]{:S(2)}) collective-permute-start(f32[128,128]{1,0:T(8,128)S(1)} %fusion.20.own_ref), channel_id=1, source_target_pairs={{0,16},{16,0},{1,17},{17,1},{2,18},{18,2},{3,19},{19,3},{4,20},{20... | collective-permute-start | bytes 196616 | tf_op jit(solution)/shard_map/ppermute | solution.py:446
  204.6 3.6 %collective-permute-start.22 = (bf16[32,512]{1,0:T(8,128)(2,1)S(1)}, bf16[32,512]{1,0:T(8,128)(2,1)S(1)}, u32[]{:S(2)}, u32[]{:S(2)}) collective-permute-start(bf16[32,512]{1,0:T(8,128)(2,1)S(1)} %get-tuple-element.134), channel_id=1, source_target_pairs={{0,1},{1,0},{2,3},{3,2},{4,5},{5,4},{6,7},{7,6},{8,9},{9,8},{10,11... | collective-permute-start | bytes 98312 | tf_op jit(solution)/shard_map/ppermute | solution.py:452
  204.7 4.2 %collective-permute-start.23 = (bf16[32,512]{1,0:T(8,128)(2,1)S(1)}, bf16[32,512]{1,0:T(8,128)(2,1)S(1)}, u32[]{:S(2)}, u32[]{:S(2)}) collective-permute-start(bf16[32,512]{1,0:T(8,128)(2,1)S(1)} %get-tuple-element.135), channel_id=1, source_target_pairs={{0,2},{1,3},{2,0},{3,1},{4,6},{5,7},{6,4},{7,5},{8,10},{9,11},{10,... | collective-permute-start | bytes 98312 | tf_op jit(solution)/shard_map/ppermute | solution.py:452
  205.6 5.5 %collective-permute-start.24 = (bf16[32,512]{1,0:T(8,128)(2,1)S(1)}, bf16[32,512]{1,0:T(8,128)(2,1)S(1)}, u32[]{:S(2)}, u32[]{:S(2)}) collective-permute-start(bf16[32,512]{1,0:T(8,128)(2,1)S(1)} %get-tuple-element.136), channel_id=1, source_target_pairs={{0,3},{1,2},{2,1},{3,0},{4,7},{5,6},{6,5},{7,4},{8,11},{9,10},{10,... | collective-permute-start | bytes 98312 | tf_op jit(solution)/shard_map/ppermute | solution.py:452
  206.6 4.6 %collective-permute-start.25 = (bf16[32,512]{1,0:T(8,128)(2,1)S(1)}, bf16[32,512]{1,0:T(8,128)(2,1)S(1)}, u32[]{:S(2)}, u32[]{:S(2)}) collective-permute-start(bf16[32,512]{1,0:T(8,128)(2,1)S(1)} %get-tuple-element.137), channel_id=1, source_target_pairs={{0,4},{1,5},{2,6},{3,7},{4,0},{5,1},{6,2},{7,3},{8,12},{9,13},{10,... | collective-permute-start | bytes 98312 | tf_op jit(solution)/shard_map/ppermute | solution.py:452
  206.6 4.6 %collective-permute-start.26 = (bf16[32,512]{1,0:T(8,128)(2,1)S(1)}, bf16[32,512]{1,0:T(8,128)(2,1)S(1)}, u32[]{:S(2)}, u32[]{:S(2)}) collective-permute-start(bf16[32,512]{1,0:T(8,128)(2,1)S(1)} %get-tuple-element.138), channel_id=1, source_target_pairs={{0,5},{1,4},{2,7},{3,6},{4,1},{5,0},{6,3},{7,2},{8,13},{9,12},{10,... | collective-permute-start | bytes 98312 | tf_op jit(solution)/shard_map/ppermute | solution.py:452
  208.3 5.1 %collective-permute-start.27 = (bf16[32,512]{1,0:T(8,128)(2,1)S(1)}, bf16[32,512]{1,0:T(8,128)(2,1)S(1)}, u32[]{:S(2)}, u32[]{:S(2)}) collective-permute-start(bf16[32,512]{1,0:T(8,128)(2,1)S(1)} %get-tuple-element.139), channel_id=1, source_target_pairs={{0,6},{1,7},{2,4},{3,5},{4,2},{5,3},{6,0},{7,1},{8,14},{9,15},{10,... | collective-permute-start | bytes 98312 | tf_op jit(solution)/shard_map/ppermute | solution.py:452
  208.9 4.6 %collective-permute-start.28 = (bf16[32,512]{1,0:T(8,128)(2,1)S(1)}, bf16[32,512]{1,0:T(8,128)(2,1)S(1)}, u32[]{:S(2)}, u32[]{:S(2)}) collective-permute-start(bf16[32,512]{1,0:T(8,128)(2,1)S(1)} %get-tuple-element.140), channel_id=1, source_target_pairs={{0,7},{1,6},{2,5},{3,4},{4,3},{5,2},{6,1},{7,0},{8,15},{9,14},{10,... | collective-permute-start | bytes 98312 | tf_op jit(solution)/shard_map/ppermute | solution.py:452
  (6 other events, 10.4 us)
Sparse Core Ops, SparseCore 0:
  45.8 38.7 reduce-scatter.1

commit v7 on v6

--- a/solution.py
+++ b/solution.py
@@ -209,38 +209,34 @@
     near = kept // R
     count = z_own.shape[0] // HCAP
 
-    def kernel(own_ref, got_ref, expand_ref, *out_refs):
+    def kernel(own_ref, got_ref, expand_ref, out_ref):
         z = (own_ref[...] + got_ref[...]).astype(jnp.bfloat16).astype(jnp.float32).reshape(count, 1, HCAP, kept)
         shape = (count, near, HCAP, kept)
         same = lax.broadcasted_iota(jnp.int32, shape, 3) // R == lax.broadcasted_iota(jnp.int32, shape, 1)
         spread = jnp.where(same, jnp.broadcast_to(z, shape), 0.0).astype(jnp.bfloat16)
-        delta = narrow(spread.reshape(count * near * HCAP, kept), expand_ref[...])
-        for k, out_ref in enumerate(out_refs):
-            out_ref[...] = delta[k * near * HCAP:(k + 1) * near * HCAP]
+        out_ref[...] = narrow(spread.reshape(count * near * HCAP, kept), expand_ref[...])
 
     return pl.pallas_call(
         kernel,
-        out_shape=[jax.ShapeDtypeStruct((near * HCAP, head), jnp.bfloat16)] * count,
+        out_shape=jax.ShapeDtypeStruct((count * near * HCAP, head), jnp.bfloat16),
         **kernel_params(),
     )(z_own, z_got, expand)
 
 
-def add_hot(partial, target, blocks):
+def add_hot(partial, target, delta):
     count = partial.shape[0]
-    hot_rows = len(blocks) * blocks[0].shape[0]
-
-    def kernel(partial_ref, target_ref, *refs):
-        *block_refs, out_ref = refs
+    hot_rows = delta.shape[0]
+
+    def kernel(partial_ref, target_ref, delta_ref, out_ref):
         hit = lax.broadcasted_iota(jnp.int32, (count, hot_rows), 1) == target_ref[...]
         place = hit.astype(jnp.float32).astype(jnp.bfloat16)
-        delta = matmul(place, jnp.concatenate([ref[...] for ref in block_refs], axis=0))
-        out_ref[...] = (partial_ref[...] + delta).astype(jnp.bfloat16)
+        out_ref[...] = (partial_ref[...] + matmul(place, delta_ref[...])).astype(jnp.bfloat16)
 
     return pl.pallas_call(
         kernel,
         out_shape=jax.ShapeDtypeStruct(partial.shape, jnp.bfloat16),
         **kernel_params(),
-    )(partial, target[:, None], *blocks)
+    )(partial, target[:, None], delta)
 
 
 def on_device(
@@ -255,66 +251,12 @@
     group_count = 8
     dp_count = far_count * group_count
     me = lax.axis_index(DP)
-    group_at = lax.axis_index(GROUP)
     z_at, x_at, core_at = lax.axis_index("z_low"), lax.axis_index("x"), lax.axis_index("core")
     none_code = adapter_count + hot_count
     rows = activations.reshape(step_count * token_count, depth)
 
+    near = step_count // 2
     names = jnp.arange(adapter_count, dtype=jnp.int32)
-    hot_row = jnp.sum(jnp.where(hot_ids[:, :, None] == names, adapter_row, 0), axis=-1)
-    hot_first = jnp.where(hot_row // per_dev == me, (hot_row % per_dev) * R, -R * per_dev)
-    column = jnp.arange(per_dev * R, dtype=jnp.int32)
-    lane = jnp.arange(R, dtype=jnp.int32)
-    entry = jnp.arange(hot_count, dtype=jnp.int32)
-    near = step_count // 2
-
-    def wanted(core):
-        firsts = []
-        for x in (x_at, 1 - x_at):
-            of_steps = jnp.sum(jnp.where(entry == 2 * x + core, hot_first, 0), axis=1)
-            firsts += [jnp.where(z_at == 0, of_steps[:near], of_steps[near:])]
-            firsts += [jnp.where(z_at == 0, of_steps[near:], of_steps[:near])]
-        return jnp.stack([(f[:, None] + lane).reshape(-1) for f in firsts])
-
-    want_mine, want_other = wanted(core_at), wanted(1 - core_at)
-    kept = near * R
-    eighth = depth // 8
-    edges = [0, 3 * eighth, 6 * eighth, depth]
-    chunk_count = len(edges) - 1
-
-    chain = Chain()
-    hops = [("x", SWAP), ("z_low", SWAP)]
-    bit = 1
-    while bit < far_count:
-        hops.append(("z_high", [(i, i ^ bit) for i in range(far_count)]))
-        bit *= 2
-    mine, swapped, got, held = {}, {}, {}, {}
-
-    def operand(c, stage):
-        if stage == 0:
-            return mine[c][:, 2 * kept:] + swapped[c][:, 2 * kept:]
-        if stage == 1:
-            return mine[c][:, kept:2 * kept] + swapped[c][:, kept:2 * kept] + got[c, 0][:, kept:]
-        if stage == 2:
-            held[c] = mine[c][:, :kept] + swapped[c][:, :kept] + got[c, 0][:, :kept] + got[c, 1]
-        else:
-            held[c] = held[c] + got[c, stage - 1]
-        return held[c]
-
-    def send(c, stage, value=None):
-        got[c, stage] = chain.permute(operand(c, stage) if value is None else value, *hops[stage])
-
-    mine_all, other_first, other_rest = pick_columns(shrink_store, want_mine, want_other, 3)
-    mine[0], swapped[0] = mine_all[:edges[1]], chain.permute(other_first, "core", SWAP)
-    rest_swapped = chain.permute(other_rest, "core", SWAP)
-    send(0, 0)
-
-    by_server = hot_first.reshape(2, near, hot_count).transpose(0, 2, 1)
-    by_server = (by_server[..., None] + lane).reshape(-1)
-    expand_hot = narrow(pick(after(by_server, chain.last)[:, None] == column), expand_store)
-    expand_part = lax.psum_scatter(expand_hot, GROUP, scatter_dimension=0, tiled=True)
-
-    token_adapter = after(token_adapter, chain.last)
     cold_row = jnp.sum(jnp.where((token_adapter - hot_count)[:, :, None] == names, adapter_row, 0), axis=-1)
     is_hot = token_adapter < hot_count
     is_cold = (token_adapter < none_code) & jnp.logical_not(is_hot)
@@ -326,7 +268,7 @@
     step_at = jnp.arange(step_count, dtype=jnp.int32)[:, None]
     hot_rows = hot_count * step_count * HCAP
     cold_rows = dp_count * step_count * CAP
-    server = ((step_at // near) * hot_count + token_adapter) ^ group_at
+    server = (step_at // near) * hot_count + token_adapter
     hot_target = (server * near + step_at % near) * HCAP + rank
     cold_target = (owner * step_count + step_at) * CAP + rank
     hot_target = jnp.where(is_hot, hot_target, -1).reshape(-1)
@@ -334,7 +276,62 @@
     hot_out, packet = place_rows(
         rows, hot_target, cold_target, (cold_row % per_dev + 1).reshape(-1), hot_rows, cold_rows
     )
-    served = near * HCAP
+    chain = Chain()
+    hot_in = lax.all_to_all(
+        chain.hold(hot_out.reshape(group_count, near * HCAP, depth)), GROUP, split_axis=0, concat_axis=0, tiled=True
+    )
+
+    hot_row = jnp.sum(jnp.where(hot_ids[:, :, None] == names, adapter_row, 0), axis=-1)
+    hot_first = jnp.where(hot_row // per_dev == me, (hot_row % per_dev) * R, -R * per_dev)
+    column = jnp.arange(per_dev * R, dtype=jnp.int32)
+    lane = jnp.arange(R, dtype=jnp.int32)
+    entry = jnp.arange(hot_count, dtype=jnp.int32)
+
+    def wanted(core):
+        firsts = []
+        for x in (x_at, 1 - x_at):
+            of_steps = jnp.sum(jnp.where(entry == 2 * x + core, hot_first, 0), axis=1)
+            firsts += [jnp.where(z_at == 0, of_steps[:near], of_steps[near:])]
+            firsts += [jnp.where(z_at == 0, of_steps[near:], of_steps[:near])]
+        return jnp.stack([(f[:, None] + lane).reshape(-1) for f in firsts])
+
+    want_mine, want_other = wanted(core_at), wanted(1 - core_at)
+    kept = near * R
+    eighth = depth // 8
+    edges = [0, 3 * eighth, 6 * eighth, depth]
+    chunk_count = len(edges) - 1
+
+    hops = [("x", SWAP), ("z_low", SWAP)]
+    bit = 1
+    while bit < far_count:
+        hops.append(("z_high", [(i, i ^ bit) for i in range(far_count)]))
+        bit *= 2
+    mine, swapped, got, held = {}, {}, {}, {}
+
+    def operand(c, stage):
+        if stage == 0:
+            return mine[c][:, 2 * kept:] + swapped[c][:, 2 * kept:]
+        if stage == 1:
+            return mine[c][:, kept:2 * kept] + swapped[c][:, kept:2 * kept] + got[c, 0][:, kept:]
+        if stage == 2:
+            held[c] = mine[c][:, :kept] + swapped[c][:, :kept] + got[c, 0][:, :kept] + got[c, 1]
+        else:
+            held[c] = held[c] + got[c, stage - 1]
+        return held[c]
+
+    def send(c, stage, value=None):
+        got[c, stage] = chain.permute(operand(c, stage) if value is None else value, *hops[stage])
+
+    mine_all, other_first, other_rest = pick_columns(after(shrink_store, chain.last), want_mine, want_other, 3)
+    mine[0], swapped[0] = mine_all[:edges[1]], chain.permute(other_first, "core", SWAP)
+    rest_swapped = chain.permute(other_rest, "core", SWAP)
+    chain.last, hot_in, swapped[0] = lax.optimization_barrier((chain.last, hot_in, swapped[0]))
+    send(0, 0)
+
+    by_server = hot_first.reshape(2, near, hot_count).transpose(0, 2, 1)
+    by_server = (by_server[..., None] + lane).reshape(-1)
+    expand_hot = narrow(pick(after(by_server, chain.last)[:, None] == column), expand_store)
+    expand_part = lax.psum_scatter(expand_hot, GROUP, scatter_dimension=0, tiled=True)
 
     done = {}
 
@@ -342,15 +339,6 @@
         sent = chain.hold(packet.reshape(dp_count, step_count * CAP, depth + TAG))
         sent = lax.all_to_all(sent, DP, split_axis=0, concat_axis=0, tiled=True)
         done["packet"] = sent.reshape(cold_rows, depth + TAG)
-
-    done["hot_0"] = hot_out[:served]
-
-    def hot_tokens_out(*blocks):
-        def work():
-            for k in blocks:
-                pairs = [(i, i ^ k) for i in range(group_count)]
-                done[f"hot_{k}"] = chain.permute(hot_out[k * served:(k + 1) * served], GROUP, pairs)
-        return work
 
     def base_product():
         if lax.axis_size("tp") == 2:
@@ -391,18 +379,21 @@
         done["delta_cold"] = delta.reshape(cold_rows, head_part)
 
     cold_tokens_out()
-    base_product()
+    def all_but_hot():
+        place_cold = pick(jnp.arange(cold_rows, dtype=jnp.int32)[:, None] == cold_target)
+        partial = lax.dot_general(
+            place_cold, done["delta_cold"], (((0,), (0,)), ((), ())), preferred_element_type=jnp.float32
+        )
+        if done["base_own"] is not None:
+            partial = partial + done["base_own"]
+        done["partial"] = partial + done["base_got"]
+
     between = {
-        1: [hot_tokens_out(4, 5, 1)],
-        2: [cold_shrink, cold_over_tp, base_over_tp],
-        3: [hot_tokens_out(6, 7, 2, 3), expand_over_far, cold_expand, cold_back],
+        2: [cold_shrink, cold_over_tp, base_product],
+        3: [base_over_tp, expand_over_far, cold_expand, cold_back],
+        4: [all_but_hot],
     }
-    awaited = {
-        1: ["packet", "hot_4", "hot_5", "hot_1"],
-        2: ["z_cold"],
-        3: ["hot_6", "hot_7", "hot_2", "hot_3", "expand_got", "base_got"],
-        4: ["delta_cold"],
-    }
+    awaited = {1: ["packet"], 2: ["z_cold"], 3: ["expand_got"], 4: ["partial"]}
     ready = None
     for slot in range(chunk_count + len(hops) - 1):
         if slot > 0:
@@ -424,15 +415,10 @@
         chain.last = arrived[0]
         got.update(zip(here, arrived[1:]))
         done.update(zip(names_here, arrived[1 + len(here):]))
-    base = done["base_own"] + done["base_got"] if done["base_own"] is not None else done["base_got"]
     expand_hot = done["expand_own"] + done["expand_got"]
-
-    place_cold = pick(jnp.arange(cold_rows, dtype=jnp.int32)[:, None] == cold_target)
-    partial = base + lax.dot_general(
-        place_cold, done["delta_cold"], (((0,), (0,)), ((), ())), preferred_element_type=jnp.float32
-    )
-
-    hot_in = jnp.concatenate([done[f"hot_{k}"] for k in range(group_count)], axis=0)
+    partial = done["partial"]
+
+    hot_in = hot_in.reshape(hot_rows, depth)
     dense = None
     for c in range(chunk_count):
         for piece in (held[c], got[c, len(hops) - 1]):
@@ -441,16 +427,14 @@
     dense = dense.reshape(group_count, near, HCAP, kept)
     at_step = jnp.arange(kept) // R
     z_part = sum(jnp.where(at_step == i, dense[:, i], 0.0) for i in range(near)).reshape(group_count * HCAP, kept)
-    z_part, partial = lax.optimization_barrier((z_part, partial))
     if lax.axis_size("tp") == 2:
         z_got = lax.ppermute(z_part, "tp", SWAP)
     else:
         z_part = lax.psum(z_part, "tp")
         z_got = jnp.zeros_like(z_part)
-    delta_hot = list(hot_expand(z_part, z_got, expand_hot))
-    for k in range(1, group_count):
-        delta_hot[k] = lax.ppermute(delta_hot[k], GROUP, [(i, i ^ k) for i in range(group_count)])
-    added = add_hot(partial, hot_target, delta_hot)
+    delta_hot = hot_expand(z_part, z_got, expand_hot).reshape(group_count, near * HCAP, head_part)
+    delta_hot = lax.all_to_all(delta_hot, GROUP, split_axis=0, concat_axis=0, tiled=True)
+    added = add_hot(partial, hot_target, delta_hot.reshape(hot_rows, head_part))
     return added.reshape(step_count, token_count, head_part)
 
 

time: 222 us -> 201 us (0.905)
  local copies, waits for them, and re-layouts: 24.3 us -> 9.55 us
  starting transfers between devices: 48.3 us -> 35.6 us
  Pallas kernels: 20.6 us -> 23.9 us
  waiting for transfers between devices: 79.7 us -> 76.7 us
  other arithmetic: 20.8 us -> 23.7 us
    unnamed x51 -> x20, local copies, waits for them, and re-layouts: 21.6 us -> 8.54 us
    ppermute x20 -> x13, starting transfers between devices: 27.9 us -> 15 us  [permute(): return lax.ppermute(self.hold(value), axis, pairs)]
    ppermute x20 -> x13, waiting for transfers between devices: 74.7 us -> 62.2 us  [permute(): return lax.ppermute(self.hold(value), axis, pairs)]
    all_to_all x0 -> x2, waiting for transfers between devices: none -> 11.6 us  [the longest x1 5.83 us: on_device(): lax.all_to_all(delta_hot, GROUP, split_axis=0, concat_axis=0, tiled=True)]
    all_to_all x0 -> x2, starting transfers between devices: none -> 8.77 us  [the longest x1 5.36 us: on_device(): lax.all_to_all(chain.hold(hot_out.reshape(group_count, near * HCAP, depth...]
    ppermute x7 -> x0, starting transfers between devices: 6.34 us -> none  [on_device(): lax.ppermute(delta_hot[k], GROUP, [(i, i ^ k) for i in range(group_count)])]
    ppermute x7 -> x0, waiting for transfers between devices: 2.31 us -> none  [on_device(): lax.ppermute(delta_hot[k], GROUP, [(i, i ^ k) for i in range(group_count)])]
  transfers between devices with their start and end apart: 32 -> 20, of which waited for: 12 -> 8; matrix products, arithmetic and copies ran while one was open for 19% -> 18% of each run, Pallas kernels for 6% -> 9%
where the time goes in v7:
time: 201 us; the launch traced here: 199 us
  waiting for transfers between devices  76.7 us (38%)
  starting transfers between devices  35.6 us (18%)
  Pallas kernels  23.9 us (12%)
  other arithmetic  23.7 us (12%)
  matrix products  16.1 us (8%)
  between operations  13.7 us (7%)
  local copies, waits for them, and re-layouts  9.55 us (5%)
    ppermute x13, waiting for transfers between devices, permute(): return lax.ppermute(self.hold(value), axis, pairs)  62.2 us
    ppermute x13, starting transfers between devices, permute(): return lax.ppermute(self.hold(value), axis, pairs)  15 us
    dot_general x9, matrix products, matmul(): return jnp.dot(a, b, preferred_element_type=jnp.float32)  14.5 us
    pallas_call x1, Pallas kernels, base_halves(): pl.pallas_call(kernel, grid_spec=pltpu.PrefetchScalarGridSpec(num_scalar_...  9.91 us
    unnamed x20, local copies, waits for them, and re-layouts  8.54 us
    pallas_call x1, Pallas kernels, pick_columns(): pl.pallas_call(kernel, grid_spec=pltpu.PrefetchScalarGridSpec(num_scalar_...  8.01 us
    add x3, other arithmetic, operand(): return mine[c][:, 2 * kept:] + swapped[c][:, 2 * kept:]  6.52 us
    add x3, other arithmetic, operand(): mine[c][:, :kept] + swapped[c][:, :kept] + got[c, 0][:, :kept] + got[c, 1]  6.24 us
  transfers between devices with their start and end apart: 20, of which 8 were waited for; matrix products, arithmetic and copies ran while one was open for 18% of the time, Pallas kernels for 9%

profile of v7, /device:TPU:0, one launch (start us, length us, event | category | flops | bytes accessed | tf_op | source)
XLA Modules:
  0.0 199.3 jit_solution(4119915326075049961)
XLA Ops:
  9.9 2.2 %copy-done.2 = bf16[4,128,4096]{2,1,0:T(8,128)(2,1)S(1)} copy-done((bf16[4,128,4096]{2,1,0:T(8,128)(2,1)S(1)}, bf16[4,128,4096]{2,1,0:T(8,128)(2,1)}, u32[]{:S(2)}) %copy-start.2) | copy-done | bytes 4194328
  12.1 3.9 %shard_map.73 = (bf16[256,4096]{1,0:T(8,128)(2,1)}, bf16[128,4224]{1,0:T(8,128)(2,1)}) custom-call(s32[1,512]{1,0:T(1,128)S(1)} %bitcast.50, s32[1,512]{1,0:T(1,128)S(1)} %bitcast.52, s32[1,512]{1,0:T(1,128)S(1)} %fusion.27.tag_at, bf16[512,4096]{1,0:T(8,128)(2,1)S(1)} %bitcast.47), custom_call_target="tpu_custom_call" | custom-call | flops 1 | bytes 1 | tf_op jit(solution)/shard_map/pallas_call | solution.py:146
  16.0 5.4 %all-to-all-start = ((bf16[8,32,4096]{2,1,0:T(8,128)(2,1)}), bf16[8,32,4096]{2,1,0:T(8,128)(2,1)}, u32[]{:S(2)}, u32[]{:S(2)}) async-start(bf16[8,32,4096]{2,1,0:T(8,128)(2,1)} %bitcast.6), calls=%async_computation | async-start | bytes 4194304 | tf_op jit(solution)/shard_map/all_to_all | solution.py:280
  23.5 2.2 %copy-done.1 = bf16[4096,512]{1,0:T(8,128)(2,1)S(1)} copy-done((bf16[4096,512]{1,0:T(8,128)(2,1)S(1)}, bf16[4096,512]{1,0:T(8,128)(2,1)}, u32[]{:S(2)}) %copy-start.1) | copy-done | bytes 4194328
  25.7 8.0 %shard_map.74 = (bf16[4096,512]{1,0:T(8,128)(2,1)S(1)}, bf16[1536,512]{1,0:T(8,128)(2,1)S(1)}, bf16[2560,512]{1,0:T(8,128)(2,1)}) custom-call(s32[4]{0:T(128)S(1)} %convert_element_type.21.mine_held, s32[4]{0:T(128)S(1)} %convert_element_type.22.other_held, s32[1,512]{1,0:T(1,128)S(1)} %bitcast.54, s32[1,512]{1,0:T(1,128)S(1)} %bitcast.55, ...), custom_call_target="tpu_custom_call" | custom-call | flops 1 | bytes 1 | tf_op jit(solution)/shard_map/pallas_call | solution.py:100
  33.7 2.0 copy-done.4
  36.2 5.3 %collective-permute-done = bf16[1536,512]{1,0:T(8,128)(2,1)S(1)} collective-permute-done((bf16[1536,512]{1,0:T(8,128)(2,1)S(1)}, bf16[1536,512]{1,0:T(8,128)(2,1)S(1)}, u32[]{:S(2)}, u32[]{:S(2)}) %collective-permute-start) | collective-permute-done | bytes 1572896 | tf_op jit(solution)/shard_map/ppermute | solution.py:48
  41.5 5.7 %all-to-all-done = bf16[8,32,4096]{2,1,0:T(8,128)(2,1)} async-done(((bf16[8,32,4096]{2,1,0:T(8,128)(2,1)}), bf16[8,32,4096]{2,1,0:T(8,128)(2,1)}, u32[]{:S(2)}, u32[]{:S(2)}) %all-to-all-start) | async-done | bytes 2097184 | tf_op jit(solution)/shard_map/all_to_all | solution.py:280
  47.2 2.1 %slice_add_fusion.1 = bf16[1536,256]{1,0:T(8,128)(2,1)} fusion(bf16[1536,512]{1,0:T(8,128)(2,1)S(1)} %collective-permute-done, bf16[4096,512]{1,0:T(8,128)(2,1)} %copy-done.4), kind=kLoop, calls=%fused_computation.16 | loop fusion | flops 393216 | bytes 2359296 | tf_op jit(solution)/shard_map/add | solution.py:313
  49.4 5.4 %all-to-all-start.1 = ((bf16[16,8,4224]{2,1,0:T(8,128)(2,1)}), bf16[16,8,4224]{2,1,0:T(8,128)(2,1)S(1)}, u32[]{:S(2)}, u32[]{:S(2)}) async-start(bf16[16,8,4224]{2,1,0:T(8,128)(2,1)} %bitcast.7), calls=%async_computation.1 | async-start | bytes 2162688 | tf_op jit(solution)/shard_map/all_to_all | solution.py:340
  54.9 1.9 collective-permute-start.2
  57.0 2.3 %slice_add_fusion = bf16[1536,256]{1,0:T(8,128)(2,1)} fusion(bf16[2560,512]{1,0:T(8,128)(2,1)} %collective-permute-done.1, bf16[4096,512]{1,0:T(8,128)(2,1)} %copy-done.4), kind=kLoop, calls=%fused_computation.15 | loop fusion | flops 393216 | bytes 2359296 | tf_op jit(solution)/shard_map/add | solution.py:313
  59.4 27.5 %collective-permute-done.2 = bf16[1536,256]{1,0:T(8,128)(2,1)} collective-permute-done((bf16[1536,256]{1,0:T(8,128)(2,1)}, bf16[1536,256]{1,0:T(8,128)(2,1)}, u32[]{:S(2)}, u32[]{:S(2)}) %collective-permute-start.2) | collective-permute-done | bytes 786464 | tf_op jit(solution)/shard_map/ppermute | solution.py:48
  86.9 2.0 slice_add_fusion.4
  88.8 1.5 collective-permute-start.4
  90.3 1.8 fusion.1
  92.1 2.0 %slice_add_fusion.2 = bf16[1024,256]{1,0:T(8,128)(2,1)} fusion(bf16[2560,512]{1,0:T(8,128)(2,1)} %collective-permute-done.1, bf16[4096,512]{1,0:T(8,128)(2,1)} %copy-done.4), kind=kLoop, calls=%fused_computation.22 | loop fusion | flops 262144 | bytes 1572864 | tf_op jit(solution)/shard_map/add | solution.py:313
  94.7 12.4 %collective-permute-done.3 = bf16[1536,256]{1,0:T(8,128)(2,1)} collective-permute-done((bf16[1536,256]{1,0:T(8,128)(2,1)}, bf16[1536,256]{1,0:T(8,128)(2,1)}, u32[]{:S(2)}, u32[]{:S(2)}) %collective-permute-start.3) | collective-permute-done | bytes 786464 | tf_op jit(solution)/shard_map/ppermute | solution.py:48
  107.1 2.1 %add_add_fusion.1 = bf16[1536,128]{1,0:T(8,128)(2,1)} fusion(bf16[1536,128]{1,0:T(8,128)(2,1)} %collective-permute-done.4, bf16[1536,256]{1,0:T(8,128)(2,1)} %collective-permute-done.2, bf16[1536,512]{1,0:T(8,128)(2,1)S(1)} %collective-permute-done, bf16[4096,512]{1,0:T(8,128)(2,1)} %copy-done.4), kind=kLoop, calls=%fused_computation.27 | loop fusion | flops 589824 | bytes 1966080 | tf_op jit(solution)/shard_map/add | solution.py:317
  109.2 2.1 %slice_add_fusion.3 = bf16[1536,128]{1,0:T(8,128)(2,1)} fusion(bf16[1536,256]{1,0:T(8,128)(2,1)} %collective-permute-done.3, bf16[2560,512]{1,0:T(8,128)(2,1)} %collective-permute-done.1, bf16[4096,512]{1,0:T(8,128)(2,1)} %copy-done.4), kind=kLoop, calls=%fused_computation.28 | loop fusion | flops 393216 | bytes 1572864 | tf_op jit(solution)/shard_map/add | solution.py:315
  111.2 1.8 collective-permute-start.6
  113.0 2.4 %collective-permute-start.7 = (bf16[1536,128]{1,0:T(8,128)(2,1)}, bf16[1536,128]{1,0:T(8,128)(2,1)}, u32[]{:S(2)}, u32[]{:S(2)}) collective-permute-start(bf16[1536,128]{1,0:T(8,128)(2,1)} %add_add_fusion.1), channel_id=1, source_target_pairs={{0,8},{8,0},{1,9},{9,1},{2,10},{10,2},{3,11},{11,3},{4,12},{12,4},... | collective-permute-start | bytes 1179656 | tf_op jit(solution)/shard_map/ppermute | solution.py:48
  115.5 2.9 %convolution_select_fusion = f32[128,512]{1,0:T(8,128)S(1)} fusion(bf16[4096,512]{1,0:T(8,128)(2,1)} %store_ref, bf16[128,4224]{1,0:T(8,128)(2,1)S(1)} %bitcast.57, s32[512]{0:T(512)S(1)} %fusion.23, s32[128]{0:T(128)S(1)} %convert_reduce_fusion.1), kind=kOutput, calls=%fused_computation.5 | convolution fusion | flops 537001984 | bytes 5507584 | tf_op jit(solution)/shard_map/dot_general | solution.py:22
  118.4 1.6 collective-permute-start.8
  120.0 2.2 %copy-done.3 = bf16[4,128,4096]{2,1,0:T(8,128)(2,1)S(1)} copy-done((bf16[4,128,4096]{2,1,0:T(8,128)(2,1)S(1)}, bf16[4,128,4096]{2,1,0:T(8,128)(2,1)}, u32[]{:S(2)}) %copy-start.3) | copy-done | bytes 4194328
  122.2 9.9 %shard_map.75 = (f32[512,512]{1,0:T(8,128)S(1)}, f32[512,512]{1,0:T(8,128)S(1)}) custom-call(s32[1]{0:T(128)} %bitcast.11.tp_at, bf16[512,4096]{1,0:T(8,128)(2,1)S(1)} %bitcast.48, bf16[4096,1024]{1,0:T(8,128)(2,1)} %weight_ref), custom_call_target="tpu_custom_call" | custom-call | flops 1 | bytes 1 | tf_op jit(solution)/shard_map/pallas_call | solution.py:190
  132.2 2.2 %add_add_fusion = bf16[1536,128]{1,0:T(8,128)(2,1)} fusion(bf16[1536,128]{1,0:T(8,128)(2,1)} %collective-permute-done.6, bf16[1536,256]{1,0:T(8,128)(2,1)} %collective-permute-done.3, bf16[2560,512]{1,0:T(8,128)(2,1)} %collective-permute-done.1, bf16[4096,512]{1,0:T(8,128)(2,1)} %copy-done.4), kind=kLoop, calls=%fused_computation.26 | loop fusion | flops 589824 | bytes 1966080 | tf_op jit(solution)/shard_map/add | solution.py:317
  134.4 1.7 collective-permute-start.10
  136.0 1.9 slice_add_fusion.5
  137.9 1.5 collective-permute-start.9
  139.4 1.4 collective-permute-start.11
  140.8 1.7 collective-permute-start.13
  143.4 3.5 %all-to-all-start.2 = ((bf16[16,8,512]{2,1,0:T(8,128)(2,1)}), bf16[16,8,512]{2,1,0:T(8,128)(2,1)S(1)}, u32[]{:S(2)}, u32[]{:S(2)}) async-start(bf16[16,8,512]{2,1,0:T(8,128)(2,1)} %fusion.3), calls=%async_computation.3 | async-start | bytes 262144 | tf_op jit(solution)/shard_map/all_to_all | solution.py:378
  146.9 1.6 fusion.9
  148.5 1.6 convolution_add_fusion.4
  150.1 1.6 convolution_add_fusion.3
  151.7 9.0 %collective-permute-done.11 = bf16[128,512]{1,0:T(8,128)(2,1)S(1)} collective-permute-done((bf16[128,512]{1,0:T(8,128)(2,1)}, bf16[128,512]{1,0:T(8,128)(2,1)S(1)}, u32[]{:S(2)}, u32[]{:S(2)}) %collective-permute-start.11) | collective-permute-done | bytes 131104 | tf_op jit(solution)/shard_map/ppermute | solution.py:48
  160.7 1.9 add_add_fusion.2
  162.6 1.4 fusion.13
  164.0 1.5 fusion.4
  165.6 1.6 fusion.2.partial_ref
  167.2 8.1 %collective-permute-done.12 = bf16[1024,128]{1,0:T(8,128)(2,1)S(1)} collective-permute-done((bf16[1024,128]{1,0:T(8,128)(2,1)}, bf16[1024,128]{1,0:T(8,128)(2,1)S(1)}, u32[]{:S(2)}, u32[]{:S(2)}) %collective-permute-start.12) | collective-permute-done | bytes 262176 | tf_op jit(solution)/shard_map/ppermute | solution.py:48
  175.3 1.3 convolution_add_fusion.1
  176.7 1.4 collective-permute-start.14
  178.1 2.9 %collective-permute-done.14.got_ref = f32[128,128]{1,0:T(8,128)S(1)} collective-permute-done((f32[128,128]{1,0:T(8,128)S(1)}, f32[128,128]{1,0:T(8,128)S(1)}, u32[]{:S(2)}, u32[]{:S(2)}) %collective-permute-start.14) | collective-permute-done | bytes 65568 | tf_op jit(solution)/shard_map/ppermute | solution.py:431
  181.9 3.4 %all-to-all-start.3 = ((bf16[8,32,512]{2,1,0:T(8,128)(2,1)}), bf16[8,32,512]{2,1,0:T(8,128)(2,1)S(1)}, u32[]{:S(2)}, u32[]{:S(2)}) async-start(bf16[8,32,512]{2,1,0:T(8,128)(2,1)} %bitcast.20), calls=%async_computation.4 | async-start | bytes 524288 | tf_op jit(solution)/shard_map/all_to_all | solution.py:436
  185.5 5.8 %all-to-all-done.3 = bf16[8,32,512]{2,1,0:T(8,128)(2,1)S(1)} async-done(((bf16[8,32,512]{2,1,0:T(8,128)(2,1)}), bf16[8,32,512]{2,1,0:T(8,128)(2,1)S(1)}, u32[]{:S(2)}, u32[]{:S(2)}) %all-to-all-start.3) | async-done | bytes 262176 | tf_op jit(solution)/shard_map/all_to_all | solution.py:436
  191.3 1.1 shard_map.77
  (85 shorter events, 9.1 us)
Async XLA Ops:
  6.5 83.8 %copy-start = (bf16[512,512]{1,0:T(8,128)(2,1)S(1)}, bf16[512,512]{1,0:T(8,128)(2,1)}, u32[]{:S(2)}) copy-start(bf16[512,512]{1,0:T(8,128)(2,1)} %param.10) | copy-start | bytes 1572868
  9.9 2.2 %copy-start.2 = (bf16[4,128,4096]{2,1,0:T(8,128)(2,1)S(1)}, bf16[4,128,4096]{2,1,0:T(8,128)(2,1)}, u32[]{:S(2)}) copy-start(bf16[4,128,4096]{2,1,0:T(8,128)(2,1)} %param.7) | copy-start | bytes 12582916
  16.0 5.4 %copy-start.8 = (s32[128]{0:T(128)S(1)}, s32[128]{0:T(128)}, u32[]{:S(2)}) copy-start(s32[128]{0:T(128)} %param.11) | copy-start | bytes 1540
  16.0 5.4 %copy-start.9 = (s32[4,4]{1,0:T(4,128)S(1)}, s32[4,4]{1,0:T(4,128)}, u32[]{:S(2)}) copy-start(s32[4,4]{1,0:T(4,128)} %param.13) | copy-start | bytes 196
  16.0 31.2 %all-to-all-start = ((bf16[8,32,4096]{2,1,0:T(8,128)(2,1)}), bf16[8,32,4096]{2,1,0:T(8,128)(2,1)}, u32[]{:S(2)}, u32[]{:S(2)}) async-start(bf16[8,32,4096]{2,1,0:T(8,128)(2,1)} %bitcast.6), calls=%async_computation | async-start | bytes 4194304 | tf_op jit(solution)/shard_map/all_to_all | solution.py:280
  23.5 2.2 %copy-start.1 = (bf16[4096,512]{1,0:T(8,128)(2,1)S(1)}, bf16[4096,512]{1,0:T(8,128)(2,1)}, u32[]{:S(2)}) copy-start(bf16[4096,512]{1,0:T(8,128)(2,1)} %store_ref) | copy-start | bytes 12582916
  33.7 2.0 copy-start.4
  35.7 5.8 %collective-permute-start = (bf16[1536,512]{1,0:T(8,128)(2,1)S(1)}, bf16[1536,512]{1,0:T(8,128)(2,1)S(1)}, u32[]{:S(2)}, u32[]{:S(2)}) collective-permute-start(bf16[1536,512]{1,0:T(8,128)(2,1)S(1)} %get-tuple-element.55), channel_id=1, source_target_pairs={{0,1},{1,0},{2,3},{3,2},{4,5},{5,4},{6,7},{7,6},{8,9},{9,8},{10,11... | collective-permute-start | bytes 4718600 | tf_op jit(solution)/shard_map/ppermute | solution.py:48
  36.2 20.8 %collective-permute-start.1 = (bf16[2560,512]{1,0:T(8,128)(2,1)}, bf16[2560,512]{1,0:T(8,128)(2,1)}, u32[]{:S(2)}, u32[]{:S(2)}) collective-permute-start(bf16[2560,512]{1,0:T(8,128)(2,1)} %get-tuple-element.56), channel_id=1, source_target_pairs={{0,1},{1,0},{2,3},{3,2},{4,5},{5,4},{6,7},{7,6},{8,9},{9,8},{10,11... | collective-permute-start | bytes 7864328 | tf_op jit(solution)/shard_map/ppermute | solution.py:48
  49.4 57.7 %all-to-all-start.1 = ((bf16[16,8,4224]{2,1,0:T(8,128)(2,1)}), bf16[16,8,4224]{2,1,0:T(8,128)(2,1)S(1)}, u32[]{:S(2)}, u32[]{:S(2)}) async-start(bf16[16,8,4224]{2,1,0:T(8,128)(2,1)} %bitcast.7), calls=%async_computation.1 | async-start | bytes 2162688 | tf_op jit(solution)/shard_map/all_to_all | solution.py:340
  54.7 84.7 %reduce-scatter.2.cloned.1.call-start = ((), (), s32[]{:S(2)}) async-start(), calls=%async_computation.5 | async-start | bytes 1179648 | tf_op jit(solution)/shard_map/reduce_scatter | solution.py:334
  54.9 32.0 %collective-permute-start.2 = (bf16[1536,256]{1,0:T(8,128)(2,1)}, bf16[1536,256]{1,0:T(8,128)(2,1)}, u32[]{:S(2)}, u32[]{:S(2)}) collective-permute-start(bf16[1536,256]{1,0:T(8,128)(2,1)} %slice_add_fusion.1), channel_id=1, source_target_pairs={{0,2},{2,0},{1,3},{3,1},{4,6},{6,4},{5,7},{7,5},{8,10},{10,8},{9,1... | collective-permute-start | bytes 2359304 | tf_op jit(solution)/shard_map/ppermute | solution.py:48
  59.3 47.8 %collective-permute-start.3 = (bf16[1536,256]{1,0:T(8,128)(2,1)}, bf16[1536,256]{1,0:T(8,128)(2,1)}, u32[]{:S(2)}, u32[]{:S(2)}) collective-permute-start(bf16[1536,256]{1,0:T(8,128)(2,1)} %slice_add_fusion), channel_id=1, source_target_pairs={{0,2},{2,0},{1,3},{3,1},{4,6},{6,4},{5,7},{7,5},{8,10},{10,8},{9,1... | collective-permute-start | bytes 2359304 | tf_op jit(solution)/shard_map/ppermute | solution.py:48
  88.8 18.2 %collective-permute-start.4 = (bf16[1536,128]{1,0:T(8,128)(2,1)}, bf16[1536,128]{1,0:T(8,128)(2,1)}, u32[]{:S(2)}, u32[]{:S(2)}) collective-permute-start(bf16[1536,128]{1,0:T(8,128)(2,1)} %slice_add_fusion.4), channel_id=1, source_target_pairs={{0,4},{4,0},{1,5},{5,1},{2,6},{6,2},{3,7},{7,3},{8,12},{12,8},{9,1... | collective-permute-start | bytes 1179656 | tf_op jit(solution)/shard_map/ppermute | solution.py:48
  94.1 38.0 %collective-permute-start.5 = (bf16[1024,256]{1,0:T(8,128)(2,1)}, bf16[1024,256]{1,0:T(8,128)(2,1)}, u32[]{:S(2)}, u32[]{:S(2)}) collective-permute-start(bf16[1024,256]{1,0:T(8,128)(2,1)} %slice_add_fusion.2), channel_id=1, source_target_pairs={{0,2},{2,0},{1,3},{3,1},{4,6},{6,4},{5,7},{7,5},{8,10},{10,8},{9,1... | collective-permute-start | bytes 1572872 | tf_op jit(solution)/shard_map/ppermute | solution.py:48
  111.2 21.0 %collective-permute-start.6 = (bf16[1536,128]{1,0:T(8,128)(2,1)}, bf16[1536,128]{1,0:T(8,128)(2,1)}, u32[]{:S(2)}, u32[]{:S(2)}) collective-permute-start(bf16[1536,128]{1,0:T(8,128)(2,1)} %slice_add_fusion.3), channel_id=1, source_target_pairs={{0,4},{4,0},{1,5},{5,1},{2,6},{6,2},{3,7},{7,3},{8,12},{12,8},{9,1... | collective-permute-start | bytes 1179656 | tf_op jit(solution)/shard_map/ppermute | solution.py:48
  113.0 19.2 %collective-permute-start.7 = (bf16[1536,128]{1,0:T(8,128)(2,1)}, bf16[1536,128]{1,0:T(8,128)(2,1)}, u32[]{:S(2)}, u32[]{:S(2)}) collective-permute-start(bf16[1536,128]{1,0:T(8,128)(2,1)} %add_add_fusion.1), channel_id=1, source_target_pairs={{0,8},{8,0},{1,9},{9,1},{2,10},{10,2},{3,11},{11,3},{4,12},{12,4},... | collective-permute-start | bytes 1179656 | tf_op jit(solution)/shard_map/ppermute | solution.py:48
  118.4 13.7 %collective-permute-start.8 = (f32[128,512]{1,0:T(8,128)S(1)}, f32[128,512]{1,0:T(8,128)S(1)}, u32[]{:S(2)}, u32[]{:S(2)}) collective-permute-start(f32[128,512]{1,0:T(8,128)S(1)} %convolution_select_fusion), channel_id=1, source_target_pairs={{0,16},{16,0},{1,17},{17,1},{2,18},{18,2},{3,19},{19,3},{4,20},{20... | collective-permute-start | bytes 786440 | tf_op jit(solution)/shard_map/ppermute | solution.py:31
  120.0 2.2 %copy-start.3 = (bf16[4,128,4096]{2,1,0:T(8,128)(2,1)S(1)}, bf16[4,128,4096]{2,1,0:T(8,128)(2,1)}, u32[]{:S(2)}) copy-start(bf16[4,128,4096]{2,1,0:T(8,128)(2,1)} %param.7) | copy-start | bytes 12582916
  134.4 26.3 %collective-permute-start.10 = (bf16[1536,128]{1,0:T(8,128)(2,1)}, bf16[1536,128]{1,0:T(8,128)(2,1)S(1)}, u32[]{:S(2)}, u32[]{:S(2)}) collective-permute-start(bf16[1536,128]{1,0:T(8,128)(2,1)} %add_add_fusion), channel_id=1, source_target_pairs={{0,8},{8,0},{1,9},{9,1},{2,10},{10,2},{3,11},{11,3},{4,12},{12,4},... | collective-permute-start | bytes 1179656 | tf_op jit(solution)/shard_map/ppermute | solution.py:48
  137.9 22.8 %collective-permute-start.9 = (bf16[1024,128]{1,0:T(8,128)(2,1)}, bf16[1024,128]{1,0:T(8,128)(2,1)S(1)}, u32[]{:S(2)}, u32[]{:S(2)}) collective-permute-start(bf16[1024,128]{1,0:T(8,128)(2,1)} %slice_add_fusion.5), channel_id=1, source_target_pairs={{0,4},{4,0},{1,5},{5,1},{2,6},{6,2},{3,7},{7,3},{8,12},{12,8},{9,1... | collective-permute-start | bytes 786440 | tf_op jit(solution)/shard_map/ppermute | solution.py:48
  139.4 21.2 %collective-permute-start.11 = (bf16[128,512]{1,0:T(8,128)(2,1)}, bf16[128,512]{1,0:T(8,128)(2,1)S(1)}, u32[]{:S(2)}, u32[]{:S(2)}) collective-permute-start(bf16[128,512]{1,0:T(8,128)(2,1)} %reduce-scatter.2.cloned.1.call-done), channel_id=1, source_target_pairs={{0,8},{8,0},{1,9},{9,1},{2,10},{10,2},{3,11},{11,3},{4,12},{12,4},... | collective-permute-start | bytes 393224 | tf_op jit(solution)/shard_map/ppermute | solution.py:48
  140.8 24.8 %collective-permute-start.13 = (f32[512,512]{1,0:T(8,128)S(1)}, f32[512,512]{1,0:T(8,128)}, u32[]{:S(2)}, u32[]{:S(2)}) collective-permute-start(f32[512,512]{1,0:T(8,128)S(1)} %get-tuple-element.82), channel_id=1, source_target_pairs={{0,16},{16,0},{1,17},{17,1},{2,18},{18,2},{3,19},{19,3},{4,20},{20... | collective-permute-start | bytes 3145736 | tf_op jit(solution)/shard_map/ppermute | solution.py:48
  143.4 22.2 %all-to-all-start.2 = ((bf16[16,8,512]{2,1,0:T(8,128)(2,1)}), bf16[16,8,512]{2,1,0:T(8,128)(2,1)S(1)}, u32[]{:S(2)}, u32[]{:S(2)}) async-start(bf16[16,8,512]{2,1,0:T(8,128)(2,1)} %fusion.3), calls=%async_computation.3 | async-start | bytes 262144 | tf_op jit(solution)/shard_map/all_to_all | solution.py:378
  160.7 2.0 copy-start.6
  162.6 12.7 %collective-permute-start.12 = (bf16[1024,128]{1,0:T(8,128)(2,1)}, bf16[1024,128]{1,0:T(8,128)(2,1)S(1)}, u32[]{:S(2)}, u32[]{:S(2)}) collective-permute-start(bf16[1024,128]{1,0:T(8,128)(2,1)} %add_add_fusion.2), channel_id=1, source_target_pairs={{0,8},{8,0},{1,9},{9,1},{2,10},{10,2},{3,11},{11,3},{4,12},{12,4},... | collective-permute-start | bytes 786440 | tf_op jit(solution)/shard_map/ppermute | solution.py:48
  165.6 12.5 %copy-start.5 = (bf16[128,512]{1,0:T(8,128)(2,1)S(1)}, bf16[128,512]{1,0:T(8,128)(2,1)}, u32[]{:S(2)}) copy-start(bf16[128,512]{1,0:T(8,128)(2,1)} %reduce-scatter.2.cloned.1.call-done) | copy-start | bytes 393220
  165.6 12.5 %copy-start.7 = (bf16[128,512]{1,0:T(8,128)(2,1)S(1)}, bf16[128,512]{1,0:T(8,128)(2,1)}, u32[]{:S(2)}) copy-start(bf16[128,512]{1,0:T(8,128)(2,1)} %copy-done.6) | copy-start | bytes 393220
  176.7 4.3 %collective-permute-start.14 = (f32[128,128]{1,0:T(8,128)S(1)}, f32[128,128]{1,0:T(8,128)S(1)}, u32[]{:S(2)}, u32[]{:S(2)}) collective-permute-start(f32[128,128]{1,0:T(8,128)S(1)} %fusion.18.own_ref), channel_id=1, source_target_pairs={{0,16},{16,0},{1,17},{17,1},{2,18},{18,2},{3,19},{19,3},{4,20},{20... | collective-permute-start | bytes 196616 | tf_op jit(solution)/shard_map/ppermute | solution.py:431
  181.9 9.4 %all-to-all-start.3 = ((bf16[8,32,512]{2,1,0:T(8,128)(2,1)}), bf16[8,32,512]{2,1,0:T(8,128)(2,1)S(1)}, u32[]{:S(2)}, u32[]{:S(2)}) async-start(bf16[8,32,512]{2,1,0:T(8,128)(2,1)} %bitcast.20), calls=%async_computation.4 | async-start | bytes 524288 | tf_op jit(solution)/shard_map/all_to_all | solution.py:436
Sparse Core Ops, SparseCore 0:
  92.2 35.8 reduce-scatter.1

commit v8 on v7

--- a/solution.py
+++ b/solution.py
@@ -58,13 +58,14 @@
     )
 
 
-def pick_columns(store, want_mine, want_other, first_blocks):
+def pick_columns(store, expand, want_mine, want_other):
     depth, width = store.shape
     groups, lanes = want_mine.shape
     count = groups * lanes
-    rows = depth // 8
-
-    def kernel(mine_held, other_held, mine_at, other_at, store_ref, mine_ref, first_ref, rest_ref, pick_mine, pick_other):
+    blocks = 8
+    rows = depth // blocks
+
+    def kernel(mine_held, other_held, mine_at, other_at, store_ref, expand_ref, mine_ref, first_ref, rest_ref, pick_mine, pick_other):
         step = pl.program_id(0)
 
         @pl.when(step == 0)
@@ -77,9 +78,16 @@
             for g in range(groups):
                 at = slice(g * lanes, (g + 1) * lanes)
 
-                @pl.when(held[g] > 0)
+                @pl.when((held[g] > 0) & (step < blocks))
                 def _():
                     out_ref[:, at] = narrow(store_ref[...], picker[:, at])
+
+                @pl.when((held[g] > 0) & (step == blocks))
+                def _():
+                    product = lax.dot_general(
+                        expand_ref[...], picker[:, at], (((0,), (0,)), ((), ())), preferred_element_type=jnp.float32
+                    )
+                    out_ref[:, at] = product.astype(jnp.bfloat16)
 
                 @pl.when(held[g] == 0)
                 def _():
@@ -87,30 +95,35 @@
 
         fill(mine_ref, mine_held, pick_mine)
 
-        @pl.when(step < first_blocks)
+        @pl.when(step < 3)
         def _():
             fill(first_ref, other_held, pick_other)
 
-        @pl.when(step >= first_blocks)
+        @pl.when(step >= 3)
         def _():
             fill(rest_ref, other_held, pick_other)
 
-    out = lambda blocks: jax.ShapeDtypeStruct((rows * blocks, count), jnp.bfloat16)
+    out = lambda thirds: jax.ShapeDtypeStruct((3 * rows * thirds, count), jnp.bfloat16)
     index = pl.BlockSpec((1, count), lambda i, *held: (0, 0))
     return pl.pallas_call(
         kernel,
         grid_spec=pltpu.PrefetchScalarGridSpec(
             num_scalar_prefetch=2,
-            grid=(8,),
-            in_specs=[index, index, pl.BlockSpec((rows, width), lambda i, *held: (i, 0))],
+            grid=(blocks + 1,),
+            in_specs=[
+                index,
+                index,
+                pl.BlockSpec((rows, width), lambda i, *held: (jnp.minimum(i, blocks - 1), 0)),
+                pl.BlockSpec(expand.shape, lambda i, *held: (0, 0)),
+            ],
             out_specs=[
                 pl.BlockSpec((rows, count), lambda i, *held: (i, 0)),
-                pl.BlockSpec((rows, count), lambda i, *held: (jnp.minimum(i, first_blocks - 1), 0)),
-                pl.BlockSpec((rows, count), lambda i, *held: (jnp.maximum(i - first_blocks, 0), 0)),
+                pl.BlockSpec((rows, count), lambda i, *held: (jnp.minimum(i, 2), 0)),
+                pl.BlockSpec((rows, count), lambda i, *held: (jnp.maximum(i - 3, 0), 0)),
             ],
             scratch_shapes=[pltpu.VMEM((width, count), jnp.bfloat16)] * 2,
         ),
-        out_shape=[out(8), out(first_blocks), out(8 - first_blocks)],
+        out_shape=[out(3), out(1), out(2)],
         **kernel_params(),
     )(
         jnp.any(want_mine >= 0, axis=1).astype(jnp.int32),
@@ -118,46 +131,32 @@
         want_mine.reshape(1, -1),
         want_other.reshape(1, -1),
         store,
-    )
-
-
-def place_rows(rows, hot_target, cold_target, tag, hot_rows, cold_rows):
+        expand,
+    )
+
+
+def place_rows(rows, target, placed_rows):
     count, depth = rows.shape
     blocks = 4
     width = depth // blocks
 
-    def kernel(hot_at, cold_at, tag_at, rows_ref, hot_ref, cold_ref, place_hot, place_cold):
-        step = pl.program_id(0)
-
-        @pl.when(step == 0)
-        def _():
-            hot_hit = lax.broadcasted_iota(jnp.int32, (hot_rows, count), 0) == hot_at[...]
-            cold_hit = lax.broadcasted_iota(jnp.int32, (cold_rows, count), 0) == cold_at[...]
-            place_hot[...] = hot_hit.astype(jnp.float32).astype(jnp.bfloat16)
-            place_cold[...] = cold_hit.astype(jnp.float32).astype(jnp.bfloat16)
-            tags = jnp.sum(jnp.where(cold_hit, tag_at[...].astype(jnp.float32), 0.0), axis=1, keepdims=True)
-            cold_ref[:, depth:] = jnp.broadcast_to(tags, (cold_rows, TAG)).astype(jnp.bfloat16)
-
-        block = rows_ref[...]
-        hot_ref[...] = narrow(place_hot[...], block)
-        cold_ref[:, pl.ds(pl.multiple_of(step * width, 128), width)] = narrow(place_cold[...], block)
-
-    index = pl.BlockSpec((1, count), lambda j: (0, 0))
+    def kernel(target_at, rows_ref, out_ref, place):
+        @pl.when(pl.program_id(0) == 0)
+        def _():
+            hit = lax.broadcasted_iota(jnp.int32, (placed_rows, count), 0) == target_at[...]
+            place[...] = hit.astype(jnp.float32).astype(jnp.bfloat16)
+
+        out_ref[...] = narrow(place[...], rows_ref[...])
+
     return pl.pallas_call(
         kernel,
         grid=(blocks,),
-        in_specs=[index, index, index, pl.BlockSpec((count, width), lambda j: (0, j))],
-        out_specs=[
-            pl.BlockSpec((hot_rows, width), lambda j: (0, j)),
-            pl.BlockSpec((cold_rows, depth + TAG), lambda j: (0, 0)),
-        ],
-        out_shape=[
-            jax.ShapeDtypeStruct((hot_rows, depth), jnp.bfloat16),
-            jax.ShapeDtypeStruct((cold_rows, depth + TAG), jnp.bfloat16),
-        ],
-        scratch_shapes=[pltpu.VMEM((hot_rows, count), jnp.bfloat16), pltpu.VMEM((cold_rows, count), jnp.bfloat16)],
+        in_specs=[pl.BlockSpec((1, count), lambda j: (0, 0)), pl.BlockSpec((count, width), lambda j: (0, j))],
+        out_specs=pl.BlockSpec((placed_rows, width), lambda j: (0, j)),
+        out_shape=jax.ShapeDtypeStruct((placed_rows, depth), jnp.bfloat16),
+        scratch_shapes=[pltpu.VMEM((placed_rows, count), jnp.bfloat16)],
         **kernel_params(),
-    )(hot_target[None], cold_target[None], tag[None], rows)
+    )(target[None], rows)
 
 
 def base_halves(rows, weight):
@@ -204,23 +203,29 @@
     )(lax.axis_index("tp").astype(jnp.int32)[None], rows, weight)
 
 
-def hot_expand(z_own, z_got, expand):
-    kept, head = expand.shape
+def hot_expand(z_own, z_got, factors, head):
+    kept = factors[0].shape[1]
     near = kept // R
     count = z_own.shape[0] // HCAP
 
-    def kernel(own_ref, got_ref, expand_ref, out_ref):
+    def kernel(own_ref, got_ref, first_ref, second_ref, out_ref):
         z = (own_ref[...] + got_ref[...]).astype(jnp.bfloat16).astype(jnp.float32).reshape(count, 1, HCAP, kept)
         shape = (count, near, HCAP, kept)
         same = lax.broadcasted_iota(jnp.int32, shape, 3) // R == lax.broadcasted_iota(jnp.int32, shape, 1)
         spread = jnp.where(same, jnp.broadcast_to(z, shape), 0.0).astype(jnp.bfloat16)
-        out_ref[...] = narrow(spread.reshape(count * near * HCAP, kept), expand_ref[...])
+        product = lax.dot_general(
+            spread.reshape(count * near * HCAP, kept),
+            first_ref[-head:] + second_ref[-head:],
+            (((1,), (1,)), ((), ())),
+            preferred_element_type=jnp.float32,
+        )
+        out_ref[...] = product.astype(jnp.bfloat16)
 
     return pl.pallas_call(
         kernel,
         out_shape=jax.ShapeDtypeStruct((count * near * HCAP, head), jnp.bfloat16),
         **kernel_params(),
-    )(z_own, z_got, expand)
+    )(z_own, z_got, *factors)
 
 
 def add_hot(partial, target, delta):
@@ -273,9 +278,7 @@
     cold_target = (owner * step_count + step_at) * CAP + rank
     hot_target = jnp.where(is_hot, hot_target, -1).reshape(-1)
     cold_target = jnp.where(is_cold, cold_target, -1).reshape(-1)
-    hot_out, packet = place_rows(
-        rows, hot_target, cold_target, (cold_row % per_dev + 1).reshape(-1), hot_rows, cold_rows
-    )
+    hot_out = place_rows(rows, hot_target, hot_rows)
     chain = Chain()
     hot_in = lax.all_to_all(
         chain.hold(hot_out.reshape(group_count, near * HCAP, depth)), GROUP, split_axis=0, concat_axis=0, tiled=True
@@ -297,9 +300,8 @@
 
     want_mine, want_other = wanted(core_at), wanted(1 - core_at)
     kept = near * R
-    eighth = depth // 8
-    edges = [0, 3 * eighth, 6 * eighth, depth]
-    chunk_count = len(edges) - 1
+    chunk_count = 3
+    part = (depth + head_part) // chunk_count
 
     hops = [("x", SWAP), ("z_low", SWAP)]
     bit = 1
@@ -322,44 +324,37 @@
     def send(c, stage, value=None):
         got[c, stage] = chain.permute(operand(c, stage) if value is None else value, *hops[stage])
 
-    mine_all, other_first, other_rest = pick_columns(after(shrink_store, chain.last), want_mine, want_other, 3)
-    mine[0], swapped[0] = mine_all[:edges[1]], chain.permute(other_first, "core", SWAP)
+    mine_all, other_first, other_rest = pick_columns(
+        after(shrink_store, chain.last), expand_store, want_mine, want_other
+    )
+    mine[0], swapped[0] = mine_all[:part], chain.permute(other_first, "core", SWAP)
     rest_swapped = chain.permute(other_rest, "core", SWAP)
-    chain.last, hot_in, swapped[0] = lax.optimization_barrier((chain.last, hot_in, swapped[0]))
-    send(0, 0)
-
-    by_server = hot_first.reshape(2, near, hot_count).transpose(0, 2, 1)
-    by_server = (by_server[..., None] + lane).reshape(-1)
-    expand_hot = narrow(pick(after(by_server, chain.last)[:, None] == column), expand_store)
-    expand_part = lax.psum_scatter(expand_hot, GROUP, scatter_dimension=0, tiled=True)
-
-    done = {}
-
-    def cold_tokens_out():
-        sent = chain.hold(packet.reshape(dp_count, step_count * CAP, depth + TAG))
-        sent = lax.all_to_all(sent, DP, split_axis=0, concat_axis=0, tiled=True)
-        done["packet"] = sent.reshape(cold_rows, depth + TAG)
+    ready, hot_in = lax.optimization_barrier((operand(0, 0), hot_in))
+    send(0, 0, ready)
+
+    cold_at = after(cold_target, chain.last)
+    cold_hit = jnp.arange(cold_rows, dtype=jnp.int32)[:, None] == cold_at
+    tag = jnp.sum(jnp.where(cold_hit, (cold_row % per_dev + 1).reshape(-1), 0), axis=-1)
+    tag = jnp.broadcast_to(tag.astype(jnp.bfloat16)[:, None], (cold_rows, TAG))
+    packet = jnp.concatenate([narrow(pick(cold_hit), rows), tag], axis=1)
+    packet = chain.hold(packet.reshape(dp_count, step_count * CAP, depth + TAG))
+    packet = lax.all_to_all(packet, DP, split_axis=0, concat_axis=0, tiled=True).reshape(cold_rows, depth + TAG)
+
+    done = {"packet": packet}
 
     def base_product():
+        weight = after(value_weight, chain.last)
         if lax.axis_size("tp") == 2:
-            done["base"] = base_halves(rows, after(value_weight, chain.last))
+            done["base_own"], done["base_other"] = base_halves(rows, weight)
         else:
-            done["base"] = matmul(rows, after(value_weight, chain.last)), None
+            done["base_own"], done["base_other"] = jnp.zeros((1, 1), jnp.float32), matmul(rows, weight)
 
     def base_over_tp():
-        own, other = done["base"]
-        if other is None:
-            done["base_own"] = None
-            done["base_got"] = lax.psum_scatter(chain.hold(own), "tp", scatter_dimension=1, tiled=True)
+        if lax.axis_size("tp") == 2:
+            done["base_got"] = chain.permute(done["base_other"], "tp", SWAP)
         else:
-            done["base_own"], done["base_got"] = own, chain.permute(other, "tp", SWAP)
-
-    def expand_over_far():
-        own = after(expand_part, chain.last)
-        if far_count == 2:
-            done["expand_own"], done["expand_got"] = own, chain.permute(own, "z_high", SWAP)
-        else:
-            done["expand_own"], done["expand_got"] = jnp.zeros_like(own), lax.psum(chain.hold(own), "z_high")
+            whole = chain.hold(done["base_other"])
+            done["base_got"] = lax.psum_scatter(whole, "tp", scatter_dimension=1, tiled=True)
 
     def cold_shrink():
         tag_in = done["packet"][:, depth:depth + 1].astype(jnp.int32)
@@ -378,22 +373,20 @@
         delta = lax.all_to_all(delta, DP, split_axis=0, concat_axis=0, tiled=True)
         done["delta_cold"] = delta.reshape(cold_rows, head_part)
 
-    cold_tokens_out()
     def all_but_hot():
         place_cold = pick(jnp.arange(cold_rows, dtype=jnp.int32)[:, None] == cold_target)
         partial = lax.dot_general(
             place_cold, done["delta_cold"], (((0,), (0,)), ((), ())), preferred_element_type=jnp.float32
         )
-        if done["base_own"] is not None:
-            partial = partial + done["base_own"]
-        done["partial"] = partial + done["base_got"]
+        done["partial"] = partial + done["base_own"] + done["base_got"]
 
     between = {
-        2: [cold_shrink, cold_over_tp, base_product],
-        3: [base_over_tp, expand_over_far, cold_expand, cold_back],
+        1: [base_product],
+        2: [cold_shrink, cold_over_tp, base_over_tp],
+        3: [cold_expand, cold_back],
         4: [all_but_hot],
     }
-    awaited = {1: ["packet"], 2: ["z_cold"], 3: ["expand_got"], 4: ["partial"]}
+    awaited = {1: ["packet", "base_own", "base_other"], 2: ["z_cold"], 4: ["partial"]}
     ready = None
     for slot in range(chunk_count + len(hops) - 1):
         if slot > 0:
@@ -404,8 +397,8 @@
             work()
         c = slot + 1
         if c < chunk_count:
-            mine[c] = after(mine_all, chain.last)[edges[c]:edges[c + 1]]
-            swapped[c] = after(rest_swapped, chain.last)[edges[c] - edges[1]:edges[c + 1] - edges[1]]
+            mine[c] = after(mine_all, chain.last)[c * part:(c + 1) * part]
+            swapped[c] = after(rest_swapped, chain.last)[(c - 1) * part:c * part]
             ready = chain.hold(operand(c, 0))
         here = [(slot - stage, stage) for stage in range(len(hops)) if 0 <= slot - stage < chunk_count]
         names_here = awaited.get(slot, [])
@@ -415,14 +408,14 @@
         chain.last = arrived[0]
         got.update(zip(here, arrived[1:]))
         done.update(zip(names_here, arrived[1 + len(here):]))
-    expand_hot = done["expand_own"] + done["expand_got"]
     partial = done["partial"]
 
     hot_in = hot_in.reshape(hot_rows, depth)
     dense = None
     for c in range(chunk_count):
+        last = min((c + 1) * part, depth)
         for piece in (held[c], got[c, len(hops) - 1]):
-            product = matmul(hot_in[:, edges[c]:edges[c + 1]], piece)
+            product = matmul(hot_in[:, c * part:last], piece[:last - c * part])
             dense = product if dense is None else dense + product
     dense = dense.reshape(group_count, near, HCAP, kept)
     at_step = jnp.arange(kept) // R
@@ -432,7 +425,7 @@
     else:
         z_part = lax.psum(z_part, "tp")
         z_got = jnp.zeros_like(z_part)
-    delta_hot = hot_expand(z_part, z_got, expand_hot).reshape(group_count, near * HCAP, head_part)
+    delta_hot = hot_expand(z_part, z_got, (held[c], got[c, len(hops) - 1]), head_part).reshape(group_count, near * HCAP, head_part)
     delta_hot = lax.all_to_all(delta_hot, GROUP, split_axis=0, concat_axis=0, tiled=True)
     added = add_hot(partial, hot_target, delta_hot.reshape(hot_rows, head_part))
     return added.reshape(step_count, token_count, head_part)

time: 201 us -> 189 us (0.940)
  between operations: 13.7 us -> 0.34 us
  waiting for transfers between devices: 76.7 us -> 84.5 us
  other arithmetic: 23.7 us -> 20.5 us
  local copies, waits for them, and re-layouts: 9.55 us -> 6.4 us
    all_to_all x1, waiting for transfers between devices: 0.01 us -> 8.93 us  [cold_back(): delta = lax.all_to_all(delta, DP, split_axis=0, concat_axis=0, tiled=True)]
    ppermute x13 -> x12, waiting for transfers between devices: 62.2 us -> 53.8 us  [permute(): return lax.ppermute(self.hold(value), axis, pairs)]
    ppermute x1, waiting for transfers between devices: 0.01 us -> 7.21 us  [sum_over_tp(): return part + lax.ppermute(part, 'tp', SWAP)]
    add x3, other arithmetic: 6.52 us -> 3.16 us  [operand(): return mine[c][:, 2 * kept:] + swapped[c][:, 2 * kept:]]
    unnamed x20 -> x24, local copies, waits for them, and re-layouts: 8.54 us -> 5.49 us
    ppermute x13 -> x12, starting transfers between devices: 15 us -> 13.4 us  [permute(): return lax.ppermute(self.hold(value), axis, pairs)]
  transfers between devices with their start and end apart: 20 -> 18, of which waited for: 8 -> 11; matrix products, arithmetic and copies ran while one was open for 18% -> 18% of each run, Pallas kernels for 9% -> 10%
where the time goes in v8:
time: 189 us; the launch traced here: 187 us
  waiting for transfers between devices  84.5 us (45%)
  starting transfers between devices  34.3 us (18%)
  Pallas kernels  25 us (13%)
  other arithmetic  20.5 us (11%)
  matrix products  16.3 us (9%)
  local copies, waits for them, and re-layouts  6.4 us (3%)
    ppermute x12, waiting for transfers between devices, permute(): return lax.ppermute(self.hold(value), axis, pairs)  53.8 us
    dot_general x9, matrix products, matmul(): return jnp.dot(a, b, preferred_element_type=jnp.float32)  16 us
    ppermute x12, starting transfers between devices, permute(): return lax.ppermute(self.hold(value), axis, pairs)  13.4 us
    pallas_call x1, Pallas kernels, base_halves(): pl.pallas_call(kernel, grid_spec=pltpu.PrefetchScalarGridSpec(num_scalar_...  9.89 us
    pallas_call x1, Pallas kernels, pick_columns(): pl.pallas_call(kernel, grid_spec=pltpu.PrefetchScalarGridSpec(num_scalar_...  9.73 us
    all_to_all x1, waiting for transfers between devices, cold_back(): delta = lax.all_to_all(delta, DP, split_axis=0, concat_axis=0, tiled=True)  8.93 us
    ppermute x1, waiting for transfers between devices, sum_over_tp(): return part + lax.ppermute(part, 'tp', SWAP)  7.21 us
    all_to_all x1, waiting for transfers between devices, on_device(): lax.all_to_all(chain.hold(hot_out.reshape(group_count, near * HCAP, depth...  6 us
  transfers between devices with their start and end apart: 18, of which 11 were waited for; matrix products, arithmetic and copies ran while one was open for 18% of the time, Pallas kernels for 10%

profile of v8, /device:TPU:0, one launch (start us, length us, event | category | flops | bytes accessed | tf_op | source)
XLA Modules:
  0.0 187.2 jit_solution(4003422980298673573)
XLA Ops:
  3.3 2.2 %copy-done = bf16[4,128,4096]{2,1,0:T(8,128)(2,1)S(1)} copy-done((bf16[4,128,4096]{2,1,0:T(8,128)(2,1)S(1)}, bf16[4,128,4096]{2,1,0:T(8,128)(2,1)}, u32[]{:S(2)}) %copy-start) | copy-done | bytes 4194328
  5.5 3.3 %shard_map.73 = bf16[256,4096]{1,0:T(8,128)(2,1)} custom-call(s32[1,512]{1,0:T(1,128)S(1)} %bitcast.50, bf16[512,4096]{1,0:T(8,128)(2,1)S(1)} %bitcast.47), custom_call_target="tpu_custom_call" | custom-call | flops 1 | bytes 1 | tf_op jit(solution)/shard_map/pallas_call | solution.py:151
  8.8 5.4 %all-to-all-start = ((bf16[8,32,4096]{2,1,0:T(8,128)(2,1)}), bf16[8,32,4096]{2,1,0:T(8,128)(2,1)}, u32[]{:S(2)}, u32[]{:S(2)}) async-start(bf16[8,32,4096]{2,1,0:T(8,128)(2,1)} %bitcast.4), calls=%async_computation | async-start | bytes 4194304 | tf_op jit(solution)/shard_map/all_to_all | solution.py:283
  16.3 2.2 %copy-done.2 = bf16[4096,512]{1,0:T(8,128)(2,1)S(1)} copy-done((bf16[4096,512]{1,0:T(8,128)(2,1)S(1)}, bf16[4096,512]{1,0:T(8,128)(2,1)}, u32[]{:S(2)}) %copy-start.2) | copy-done | bytes 4194328
  18.5 9.7 %shard_map.74 = (bf16[4608,512]{1,0:T(8,128)(2,1)S(1)}, bf16[1536,512]{1,0:T(8,128)(2,1)S(1)}, bf16[3072,512]{1,0:T(8,128)(2,1)}) custom-call(s32[4]{0:T(128)S(1)} %convert_element_type.28.mine_held, s32[4]{0:T(128)S(1)} %convert_element_type.29.other_held, s32[1,512]{1,0:T(1,128)S(1)} %bitcast.52, s32[1,512]{1,0:T(1,128)S(1)} %bitcast.53, ...), custom_call_target="tpu_custom_call" | custom-call | flops 1 | bytes 1 | tf_op jit(solution)/shard_map/pallas_call | solution.py:108
  28.7 5.1 %collective-permute-done = bf16[1536,512]{1,0:T(8,128)(2,1)S(1)} collective-permute-done((bf16[1536,512]{1,0:T(8,128)(2,1)S(1)}, bf16[1536,512]{1,0:T(8,128)(2,1)S(1)}, u32[]{:S(2)}, u32[]{:S(2)}) %collective-permute-start) | collective-permute-done | bytes 1572896 | tf_op jit(solution)/shard_map/ppermute | solution.py:48
  33.9 6.0 %all-to-all-done = bf16[8,32,4096]{2,1,0:T(8,128)(2,1)} async-done(((bf16[8,32,4096]{2,1,0:T(8,128)(2,1)}), bf16[8,32,4096]{2,1,0:T(8,128)(2,1)}, u32[]{:S(2)}, u32[]{:S(2)}) %all-to-all-start) | async-done | bytes 2097184 | tf_op jit(solution)/shard_map/all_to_all | solution.py:283
  40.1 2.9 %convolution_convert_fusion = bf16[128,4096]{1,0:T(8,128)(2,1)S(1)} fusion(bf16[512,4096]{1,0:T(8,128)(2,1)} %bitcast.46, s32[512]{0:T(512)S(1)} %get-tuple-element.56), kind=kOutput, calls=%fused_computation | convolution fusion | flops 537460736 | bytes 5244928 | tf_op jit(solution)/shard_map/dot_general | solution.py:22
  43.1 1.1 maximum_bitcast_fusion
  44.2 5.4 %all-to-all-start.1 = ((bf16[16,8,4224]{2,1,0:T(8,128)(2,1)}), bf16[16,8,4224]{2,1,0:T(8,128)(2,1)}, u32[]{:S(2)}, u32[]{:S(2)}) async-start(bf16[16,8,4224]{2,1,0:T(8,128)(2,1)} %maximum_bitcast_fusion), calls=%async_computation.1 | async-start | bytes 2162688 | tf_op jit(solution)/shard_map/all_to_all | solution.py:341
  49.6 1.9 %collective-permute-start.2 = (bf16[1536,256]{1,0:T(8,128)(2,1)S(1)}, bf16[1536,256]{1,0:T(8,128)(2,1)}, u32[]{:S(2)}, u32[]{:S(2)}) collective-permute-start(bf16[1536,256]{1,0:T(8,128)(2,1)S(1)} %slice_add_fusion), channel_id=1, source_target_pairs={{0,2},{2,0},{1,3},{3,1},{4,6},{6,4},{5,7},{7,5},{8,10},{10,8},{9,1... | collective-permute-start | bytes 2359304 | tf_op jit(solution)/shard_map/ppermute | solution.py:48
  51.5 1.6 slice_add_fusion.2
  53.3 28.3 %collective-permute-done.2 = bf16[1536,256]{1,0:T(8,128)(2,1)} collective-permute-done((bf16[1536,256]{1,0:T(8,128)(2,1)S(1)}, bf16[1536,256]{1,0:T(8,128)(2,1)}, u32[]{:S(2)}, u32[]{:S(2)}) %collective-permute-start.2) | collective-permute-done | bytes 786464 | tf_op jit(solution)/shard_map/ppermute | solution.py:48
  81.7 1.2 fusion.13
  82.9 1.5 collective-permute-start.4
  84.4 1.5 slice_add_fusion.1
  86.5 9.9 %shard_map.75 = (f32[512,512]{1,0:T(8,128)S(1)}, f32[512,512]{1,0:T(8,128)S(1)}) custom-call(s32[1]{0:T(128)} %bitcast.9.tp_at, bf16[512,4096]{1,0:T(8,128)(2,1)S(1)} %bitcast.48, bf16[4096,1024]{1,0:T(8,128)(2,1)} %weight_ref), custom_call_target="tpu_custom_call" | custom-call | flops 1 | bytes 1 | tf_op jit(solution)/shard_map/pallas_call | solution.py:189
  96.4 2.0 %collective-permute-done.3 = bf16[1536,256]{1,0:T(8,128)(2,1)S(1)} collective-permute-done((bf16[1536,256]{1,0:T(8,128)(2,1)S(1)}, bf16[1536,256]{1,0:T(8,128)(2,1)S(1)}, u32[]{:S(2)}, u32[]{:S(2)}) %collective-permute-start.3) | collective-permute-done | bytes 786464 | tf_op jit(solution)/shard_map/ppermute | solution.py:48
  98.4 1.0 copy-done.6
  99.4 1.5 fusion.12
  101.0 1.3 slice_add_fusion.6
  102.4 1.5 collective-permute-start.6
  103.9 2.4 %collective-permute-start.7 = (bf16[1536,128]{1,0:T(8,128)(2,1)S(1)}, bf16[1536,128]{1,0:T(8,128)(2,1)S(1)}, u32[]{:S(2)}, u32[]{:S(2)}) collective-permute-start(bf16[1536,128]{1,0:T(8,128)(2,1)S(1)} %fusion.12), channel_id=1, source_target_pairs={{0,8},{8,0},{1,9},{9,1},{2,10},{10,2},{3,11},{11,3},{4,12},{12,4},... | collective-permute-start | bytes 1179656 | tf_op jit(solution)/shard_map/ppermute | solution.py:48
  107.1 3.2 %convolution_select_fusion = f32[128,512]{1,0:T(8,128)S(1)} fusion(bf16[4096,512]{1,0:T(8,128)(2,1)} %store_ref, bf16[128,4224]{1,0:T(8,128)(2,1)} %bitcast.8, s32[512]{0:T(512)S(1)} %fusion.28, s32[128]{0:T(128)S(1)} %convert_reduce_fusion.1), kind=kOutput, calls=%fused_computation.1 | convolution fusion | flops 537001984 | bytes 5507584 | tf_op jit(solution)/shard_map/dot_general | solution.py:22
  110.4 1.6 collective-permute-start.8
  112.5 7.2 %collective-permute-done.8 = f32[128,512]{1,0:T(8,128)S(1)} collective-permute-done((f32[128,512]{1,0:T(8,128)S(1)}, f32[128,512]{1,0:T(8,128)S(1)}, u32[]{:S(2)}, u32[]{:S(2)}) %collective-permute-start.8) | collective-permute-done | bytes 262176 | tf_op jit(solution)/shard_map/ppermute | solution.py:31
  119.7 1.1 collective-permute-done.6
  120.8 2.4 %collective-permute-done.7 = bf16[1536,128]{1,0:T(8,128)(2,1)S(1)} collective-permute-done((bf16[1536,128]{1,0:T(8,128)(2,1)S(1)}, bf16[1536,128]{1,0:T(8,128)(2,1)S(1)}, u32[]{:S(2)}, u32[]{:S(2)}) %collective-permute-start.7) | collective-permute-done | bytes 393248 | tf_op jit(solution)/shard_map/ppermute | solution.py:48
  123.2 1.4 slice_add_fusion.5
  124.6 1.9 %add_add_fusion.1 = bf16[1536,128]{1,0:T(8,128)(2,1)} fusion(bf16[1536,128]{1,0:T(8,128)(2,1)S(1)} %collective-permute-done.6, bf16[1536,256]{1,0:T(8,128)(2,1)S(1)} %copy-done.7, bf16[3072,512]{1,0:T(8,128)(2,1)} %collective-permute-done.1, bf16[4608,512]{1,0:T(8,128)(2,1)} %copy-done.3), kind=kLoop, calls=%fused_computation.28 | loop fusion | flops 589824 | bytes 1966080 | tf_op jit(solution)/shard_map/add | solution.py:319
  126.9 2.6 %collective-permute-start.10 = (bf16[1536,128]{1,0:T(8,128)(2,1)}, bf16[1536,128]{1,0:T(8,128)(2,1)S(1)}, u32[]{:S(2)}, u32[]{:S(2)}) collective-permute-start(bf16[1536,128]{1,0:T(8,128)(2,1)} %add_add_fusion.1), channel_id=1, source_target_pairs={{0,8},{8,0},{1,9},{9,1},{2,10},{10,2},{3,11},{11,3},{4,12},{12,4},... | collective-permute-start | bytes 1179656 | tf_op jit(solution)/shard_map/ppermute | solution.py:48
  130.4 3.5 %all-to-all-start.2 = ((bf16[16,8,512]{2,1,0:T(8,128)(2,1)}), bf16[16,8,512]{2,1,0:T(8,128)(2,1)S(1)}, u32[]{:S(2)}, u32[]{:S(2)}) async-start(bf16[16,8,512]{2,1,0:T(8,128)(2,1)} %fusion), calls=%async_computation.2 | async-start | bytes 262144 | tf_op jit(solution)/shard_map/all_to_all | solution.py:373
  133.9 1.6 fusion.5
  135.5 1.6 convolution_add_fusion.3
  137.1 1.6 convolution_add_fusion.2
  138.7 8.9 %all-to-all-done.2 = bf16[16,8,512]{2,1,0:T(8,128)(2,1)S(1)} async-done(((bf16[16,8,512]{2,1,0:T(8,128)(2,1)}), bf16[16,8,512]{2,1,0:T(8,128)(2,1)S(1)}, u32[]{:S(2)}, u32[]{:S(2)}) %all-to-all-start.2) | async-done | bytes 131104 | tf_op jit(solution)/shard_map/all_to_all | solution.py:373
  148.0 1.4 add_add_fusion.2.first_ref
  149.4 1.2 collective-permute-start.11
  150.7 1.3 fusion.9
  152.0 1.5 fusion.1
  153.5 1.6 add_add_fusion.partial_ref
  155.1 14.9 %collective-permute-done.11.second_ref = bf16[1536,128]{1,0:T(8,128)(2,1)S(1)} collective-permute-done((bf16[1536,128]{1,0:T(8,128)(2,1)S(1)}, bf16[1536,128]{1,0:T(8,128)(2,1)S(1)}, u32[]{:S(2)}, u32[]{:S(2)}) %collective-permute-start.11) | collective-permute-done | bytes 393248 | tf_op jit(solution)/shard_map/ppermute | solution.py:48
  170.0 1.3 convolution_add_fusion
  171.4 1.6 collective-permute-start.13
  173.0 2.7 %collective-permute-done.13.got_ref = f32[128,128]{1,0:T(8,128)S(1)} collective-permute-done((f32[128,128]{1,0:T(8,128)S(1)}, f32[128,128]{1,0:T(8,128)S(1)}, u32[]{:S(2)}, u32[]{:S(2)}) %collective-permute-start.13) | collective-permute-done | bytes 65568 | tf_op jit(solution)/shard_map/ppermute | solution.py:424
  176.7 3.4 %all-to-all-start.3 = ((bf16[8,32,512]{2,1,0:T(8,128)(2,1)}), bf16[8,32,512]{2,1,0:T(8,128)(2,1)S(1)}, u32[]{:S(2)}, u32[]{:S(2)}) async-start(bf16[8,32,512]{2,1,0:T(8,128)(2,1)} %bitcast.17), calls=%async_computation.3 | async-start | bytes 524288 | tf_op jit(solution)/shard_map/all_to_all | solution.py:429
  180.2 5.8 %all-to-all-done.3 = bf16[8,32,512]{2,1,0:T(8,128)(2,1)S(1)} async-done(((bf16[8,32,512]{2,1,0:T(8,128)(2,1)}), bf16[8,32,512]{2,1,0:T(8,128)(2,1)S(1)}, u32[]{:S(2)}, u32[]{:S(2)}) %all-to-all-start.3) | async-done | bytes 262176 | tf_op jit(solution)/shard_map/all_to_all | solution.py:429
  186.1 1.1 shard_map.77
  (84 shorter events, 11.3 us)
Async XLA Ops:
  3.3 2.2 %copy-start = (bf16[4,128,4096]{2,1,0:T(8,128)(2,1)S(1)}, bf16[4,128,4096]{2,1,0:T(8,128)(2,1)}, u32[]{:S(2)}) copy-start(bf16[4,128,4096]{2,1,0:T(8,128)(2,1)} %param.7) | copy-start | bytes 12582916
  8.8 5.4 %copy-start.9 = (s32[128]{0:T(128)S(1)}, s32[128]{0:T(128)}, u32[]{:S(2)}) copy-start(s32[128]{0:T(128)} %param.11) | copy-start | bytes 1540
  8.8 5.4 %copy-start.10 = (s32[4,4]{1,0:T(4,128)S(1)}, s32[4,4]{1,0:T(4,128)}, u32[]{:S(2)}) copy-start(s32[4,4]{1,0:T(4,128)} %param.13) | copy-start | bytes 196
  8.8 7.5 %copy-start.4 = (bf16[512,512]{1,0:T(8,128)(2,1)S(1)}, bf16[512,512]{1,0:T(8,128)(2,1)}, u32[]{:S(2)}) copy-start(bf16[512,512]{1,0:T(8,128)(2,1)} %expand_ref.1) | copy-start | bytes 1572868
  8.8 31.2 %all-to-all-start = ((bf16[8,32,4096]{2,1,0:T(8,128)(2,1)}), bf16[8,32,4096]{2,1,0:T(8,128)(2,1)}, u32[]{:S(2)}, u32[]{:S(2)}) async-start(bf16[8,32,4096]{2,1,0:T(8,128)(2,1)} %bitcast.4), calls=%async_computation | async-start | bytes 4194304 | tf_op jit(solution)/shard_map/all_to_all | solution.py:283
  16.3 2.2 %copy-start.2 = (bf16[4096,512]{1,0:T(8,128)(2,1)S(1)}, bf16[4096,512]{1,0:T(8,128)(2,1)}, u32[]{:S(2)}) copy-start(bf16[4096,512]{1,0:T(8,128)(2,1)} %store_ref) | copy-start | bytes 12582916
  28.2 5.6 %copy-start.3 = (bf16[4608,512]{1,0:T(8,128)(2,1)}, bf16[4608,512]{1,0:T(8,128)(2,1)S(1)}, u32[]{:S(2)}) copy-start(bf16[4608,512]{1,0:T(8,128)(2,1)S(1)} %get-tuple-element.63) | copy-start | bytes 14155780
  28.2 5.6 %collective-permute-start = (bf16[1536,512]{1,0:T(8,128)(2,1)S(1)}, bf16[1536,512]{1,0:T(8,128)(2,1)S(1)}, u32[]{:S(2)}, u32[]{:S(2)}) collective-permute-start(bf16[1536,512]{1,0:T(8,128)(2,1)S(1)} %get-tuple-element.51), channel_id=1, source_target_pairs={{0,1},{1,0},{2,3},{3,2},{4,5},{5,4},{6,7},{7,6},{8,9},{9,8},{10,11... | collective-permute-start | bytes 4718600 | tf_op jit(solution)/shard_map/ppermute | solution.py:48
  28.2 23.3 %collective-permute-start.1 = (bf16[3072,512]{1,0:T(8,128)(2,1)}, bf16[3072,512]{1,0:T(8,128)(2,1)}, u32[]{:S(2)}, u32[]{:S(2)}) collective-permute-start(bf16[3072,512]{1,0:T(8,128)(2,1)} %get-tuple-element.54), channel_id=1, source_target_pairs={{0,1},{1,0},{2,3},{3,2},{4,5},{5,4},{6,7},{7,6},{8,9},{9,8},{10,11... | collective-permute-start | bytes 9437192 | tf_op jit(solution)/shard_map/ppermute | solution.py:48
  33.8 47.8 %copy-start.5 = (bf16[1536,512]{1,0:T(8,128)(2,1)}, bf16[1536,512]{1,0:T(8,128)(2,1)S(1)}, u32[]{:S(2)}) copy-start(bf16[1536,512]{1,0:T(8,128)(2,1)S(1)} %collective-permute-done) | copy-start | bytes 4718596
  44.2 55.2 %all-to-all-start.1 = ((bf16[16,8,4224]{2,1,0:T(8,128)(2,1)}), bf16[16,8,4224]{2,1,0:T(8,128)(2,1)}, u32[]{:S(2)}, u32[]{:S(2)}) async-start(bf16[16,8,4224]{2,1,0:T(8,128)(2,1)} %maximum_bitcast_fusion), calls=%async_computation.1 | async-start | bytes 2162688 | tf_op jit(solution)/shard_map/all_to_all | solution.py:341
  49.6 32.1 %collective-permute-start.2 = (bf16[1536,256]{1,0:T(8,128)(2,1)S(1)}, bf16[1536,256]{1,0:T(8,128)(2,1)}, u32[]{:S(2)}, u32[]{:S(2)}) collective-permute-start(bf16[1536,256]{1,0:T(8,128)(2,1)S(1)} %slice_add_fusion), channel_id=1, source_target_pairs={{0,2},{2,0},{1,3},{3,1},{4,6},{6,4},{5,7},{7,5},{8,10},{10,8},{9,1... | collective-permute-start | bytes 2359304 | tf_op jit(solution)/shard_map/ppermute | solution.py:48
  51.5 35.0 %copy-start.1 = (bf16[4,128,4096]{2,1,0:T(8,128)(2,1)S(1)}, bf16[4,128,4096]{2,1,0:T(8,128)(2,1)}, u32[]{:S(2)}) copy-start(bf16[4,128,4096]{2,1,0:T(8,128)(2,1)} %param.7) | copy-start | bytes 12582916
  53.1 45.3 %collective-permute-start.3 = (bf16[1536,256]{1,0:T(8,128)(2,1)S(1)}, bf16[1536,256]{1,0:T(8,128)(2,1)S(1)}, u32[]{:S(2)}, u32[]{:S(2)}) collective-permute-start(bf16[1536,256]{1,0:T(8,128)(2,1)S(1)} %slice_add_fusion.2), channel_id=1, source_target_pairs={{0,2},{2,0},{1,3},{3,1},{4,6},{6,4},{5,7},{7,5},{8,10},{10,8},{9,1... | collective-permute-start | bytes 2359304 | tf_op jit(solution)/shard_map/ppermute | solution.py:48
  82.9 16.5 %collective-permute-start.4 = (bf16[1536,128]{1,0:T(8,128)(2,1)S(1)}, bf16[1536,128]{1,0:T(8,128)(2,1)}, u32[]{:S(2)}, u32[]{:S(2)}) collective-permute-start(bf16[1536,128]{1,0:T(8,128)(2,1)S(1)} %fusion.13), channel_id=1, source_target_pairs={{0,4},{4,0},{1,5},{5,1},{2,6},{6,2},{3,7},{7,3},{8,12},{12,8},{9,1... | collective-permute-start | bytes 1179656 | tf_op jit(solution)/shard_map/ppermute | solution.py:48
  85.9 33.9 %collective-permute-start.5 = (bf16[1536,256]{1,0:T(8,128)(2,1)S(1)}, bf16[1536,256]{1,0:T(8,128)(2,1)}, u32[]{:S(2)}, u32[]{:S(2)}) collective-permute-start(bf16[1536,256]{1,0:T(8,128)(2,1)S(1)} %slice_add_fusion.1), channel_id=1, source_target_pairs={{0,2},{2,0},{1,3},{3,1},{4,6},{6,4},{5,7},{7,5},{8,10},{10,8},{9,1... | collective-permute-start | bytes 2359304 | tf_op jit(solution)/shard_map/ppermute | solution.py:48
  98.4 1.0 copy-start.6
  99.4 1.6 copy-start.7
  101.0 9.3 %copy-start.8 = (bf16[1536,128]{1,0:T(8,128)(2,1)}, bf16[1536,128]{1,0:T(8,128)(2,1)S(1)}, u32[]{:S(2)}) copy-start(bf16[1536,128]{1,0:T(8,128)(2,1)S(1)} %fusion.12) | copy-start | bytes 1179652
  102.4 18.5 %collective-permute-start.6 = (bf16[1536,128]{1,0:T(8,128)(2,1)S(1)}, bf16[1536,128]{1,0:T(8,128)(2,1)S(1)}, u32[]{:S(2)}, u32[]{:S(2)}) collective-permute-start(bf16[1536,128]{1,0:T(8,128)(2,1)S(1)} %slice_add_fusion.6), channel_id=1, source_target_pairs={{0,4},{4,0},{1,5},{5,1},{2,6},{6,2},{3,7},{7,3},{8,12},{12,8},{9,1... | collective-permute-start | bytes 1179656 | tf_op jit(solution)/shard_map/ppermute | solution.py:48
  103.9 19.3 %collective-permute-start.7 = (bf16[1536,128]{1,0:T(8,128)(2,1)S(1)}, bf16[1536,128]{1,0:T(8,128)(2,1)S(1)}, u32[]{:S(2)}, u32[]{:S(2)}) collective-permute-start(bf16[1536,128]{1,0:T(8,128)(2,1)S(1)} %fusion.12), channel_id=1, source_target_pairs={{0,8},{8,0},{1,9},{9,1},{2,10},{10,2},{3,11},{11,3},{4,12},{12,4},... | collective-permute-start | bytes 1179656 | tf_op jit(solution)/shard_map/ppermute | solution.py:48
  110.4 9.3 %collective-permute-start.8 = (f32[128,512]{1,0:T(8,128)S(1)}, f32[128,512]{1,0:T(8,128)S(1)}, u32[]{:S(2)}, u32[]{:S(2)}) collective-permute-start(f32[128,512]{1,0:T(8,128)S(1)} %convolution_select_fusion), channel_id=1, source_target_pairs={{0,16},{16,0},{1,17},{17,1},{2,18},{18,2},{3,19},{19,3},{4,20},{20... | collective-permute-start | bytes 786440 | tf_op jit(solution)/shard_map/ppermute | solution.py:31
  112.0 41.5 %collective-permute-start.12 = (f32[512,512]{1,0:T(8,128)S(1)}, f32[512,512]{1,0:T(8,128)}, u32[]{:S(2)}, u32[]{:S(2)}) collective-permute-start(f32[512,512]{1,0:T(8,128)S(1)} %get-tuple-element.77), channel_id=1, source_target_pairs={{0,16},{16,0},{1,17},{17,1},{2,18},{18,2},{3,19},{19,3},{4,20},{20... | collective-permute-start | bytes 3145736 | tf_op jit(solution)/shard_map/ppermute | solution.py:48
  123.2 3.7 %copy-start.11 = (bf16[1536,128]{1,0:T(8,128)(2,1)}, bf16[1536,128]{1,0:T(8,128)(2,1)S(1)}, u32[]{:S(2)}) copy-start(bf16[1536,128]{1,0:T(8,128)(2,1)S(1)} %collective-permute-done.7) | copy-start | bytes 1179652
  126.6 21.4 %collective-permute-start.9 = (bf16[1536,128]{1,0:T(8,128)(2,1)S(1)}, bf16[1536,128]{1,0:T(8,128)(2,1)}, u32[]{:S(2)}, u32[]{:S(2)}) collective-permute-start(bf16[1536,128]{1,0:T(8,128)(2,1)S(1)} %slice_add_fusion.5), channel_id=1, source_target_pairs={{0,4},{4,0},{1,5},{5,1},{2,6},{6,2},{3,7},{7,3},{8,12},{12,8},{9,1... | collective-permute-start | bytes 1179656 | tf_op jit(solution)/shard_map/ppermute | solution.py:48
  126.9 21.1 %collective-permute-start.10 = (bf16[1536,128]{1,0:T(8,128)(2,1)}, bf16[1536,128]{1,0:T(8,128)(2,1)S(1)}, u32[]{:S(2)}, u32[]{:S(2)}) collective-permute-start(bf16[1536,128]{1,0:T(8,128)(2,1)} %add_add_fusion.1), channel_id=1, source_target_pairs={{0,8},{8,0},{1,9},{9,1},{2,10},{10,2},{3,11},{11,3},{4,12},{12,4},... | collective-permute-start | bytes 1179656 | tf_op jit(solution)/shard_map/ppermute | solution.py:48
  130.4 17.2 %all-to-all-start.2 = ((bf16[16,8,512]{2,1,0:T(8,128)(2,1)}), bf16[16,8,512]{2,1,0:T(8,128)(2,1)S(1)}, u32[]{:S(2)}, u32[]{:S(2)}) async-start(bf16[16,8,512]{2,1,0:T(8,128)(2,1)} %fusion), calls=%async_computation.2 | async-start | bytes 262144 | tf_op jit(solution)/shard_map/all_to_all | solution.py:373
  149.4 20.6 %collective-permute-start.11 = (bf16[1536,128]{1,0:T(8,128)(2,1)S(1)}, bf16[1536,128]{1,0:T(8,128)(2,1)S(1)}, u32[]{:S(2)}, u32[]{:S(2)}) collective-permute-start(bf16[1536,128]{1,0:T(8,128)(2,1)S(1)} %add_add_fusion.2.first_ref), channel_id=1, source_target_pairs={{0,8},{8,0},{1,9},{9,1},{2,10},{10,2},{3,11},{11,3},{4,12},{12,4},... | collective-permute-start | bytes 1179656 | tf_op jit(solution)/shard_map/ppermute | solution.py:48
  171.4 4.3 %collective-permute-start.13 = (f32[128,128]{1,0:T(8,128)S(1)}, f32[128,128]{1,0:T(8,128)S(1)}, u32[]{:S(2)}, u32[]{:S(2)}) collective-permute-start(f32[128,128]{1,0:T(8,128)S(1)} %fusion.21.own_ref), channel_id=1, source_target_pairs={{0,16},{16,0},{1,17},{17,1},{2,18},{18,2},{3,19},{19,3},{4,20},{20... | collective-permute-start | bytes 196616 | tf_op jit(solution)/shard_map/ppermute | solution.py:424
  176.7 9.4 %all-to-all-start.3 = ((bf16[8,32,512]{2,1,0:T(8,128)(2,1)}), bf16[8,32,512]{2,1,0:T(8,128)(2,1)S(1)}, u32[]{:S(2)}, u32[]{:S(2)}) async-start(bf16[8,32,512]{2,1,0:T(8,128)(2,1)} %bitcast.17), calls=%async_computation.3 | async-start | bytes 524288 | tf_op jit(solution)/shard_map/all_to_all | solution.py:429

commit v9 on v8

--- a/solution.py
+++ b/solution.py
@@ -51,10 +51,10 @@
         self.last = after(self.last, *arrived)
 
 
-def kernel_params():
+def kernel_params(flops=1, bytes_accessed=1):
     return dict(
         compiler_params=pltpu.CompilerParams(vmem_limit_bytes=40 * 2**20),
-        cost_estimate=pl.CostEstimate(flops=1, bytes_accessed=1, transcendentals=0),
+        cost_estimate=pl.CostEstimate(flops=flops, bytes_accessed=bytes_accessed, transcendentals=0),
     )
 
 
@@ -155,7 +155,7 @@
         out_specs=pl.BlockSpec((placed_rows, width), lambda j: (0, j)),
         out_shape=jax.ShapeDtypeStruct((placed_rows, depth), jnp.bfloat16),
         scratch_shapes=[pltpu.VMEM((placed_rows, count), jnp.bfloat16)],
-        **kernel_params(),
+        **kernel_params(2 * placed_rows * count * depth, 2 * (placed_rows + count) * depth),
     )(target[None], rows)
 
 
@@ -262,6 +262,56 @@
 
     near = step_count // 2
     names = jnp.arange(adapter_count, dtype=jnp.int32)
+    chain = Chain()
+
+    hot_row = jnp.sum(jnp.where(hot_ids[:, :, None] == names, adapter_row, 0), axis=-1)
+    hot_first = jnp.where(hot_row // per_dev == me, (hot_row % per_dev) * R, -R * per_dev)
+    column = jnp.arange(per_dev * R, dtype=jnp.int32)
+    lane = jnp.arange(R, dtype=jnp.int32)
+    entry = jnp.arange(hot_count, dtype=jnp.int32)
+
+    def wanted(core):
+        firsts = []
+        for x in (x_at, 1 - x_at):
+            of_steps = jnp.sum(jnp.where(entry == 2 * x + core, hot_first, 0), axis=1)
+            firsts += [jnp.where(z_at == 0, of_steps[:near], of_steps[near:])]
+            firsts += [jnp.where(z_at == 0, of_steps[near:], of_steps[:near])]
+        return jnp.stack([(f[:, None] + lane).reshape(-1) for f in firsts])
+
+    want_mine, want_other = wanted(core_at), wanted(1 - core_at)
+    kept = near * R
+    chunk_count = 3
+    part = (depth + head_part) // chunk_count
+
+    hops = [("x", SWAP), ("z_low", SWAP)]
+    bit = 1
+    while bit < far_count:
+        hops.append(("z_high", [(i, i ^ bit) for i in range(far_count)]))
+        bit *= 2
+    mine, swapped, got, held = {}, {}, {}, {}
+
+    def operand(c, stage):
+        if stage == 0:
+            return mine[c][:, 2 * kept:] + swapped[c][:, 2 * kept:]
+        if stage == 1:
+            return mine[c][:, kept:2 * kept] + swapped[c][:, kept:2 * kept] + got[c, 0][:, kept:]
+        if stage == 2:
+            held[c] = mine[c][:, :kept] + swapped[c][:, :kept] + got[c, 0][:, :kept] + got[c, 1]
+        else:
+            held[c] = held[c] + got[c, stage - 1]
+        return held[c]
+
+    def send(c, stage, value=None):
+        got[c, stage] = chain.permute(operand(c, stage) if value is None else value, *hops[stage])
+
+    mine_all, other_first, other_rest = pick_columns(
+        shrink_store, expand_store, want_mine, want_other
+    )
+    mine[0], swapped[0] = mine_all[:part], chain.permute(other_first, "core", SWAP)
+    rest_swapped = chain.permute(other_rest, "core", SWAP)
+    send(0, 0)
+
+    token_adapter = after(token_adapter, chain.last)
     cold_row = jnp.sum(jnp.where((token_adapter - hot_count)[:, :, None] == names, adapter_row, 0), axis=-1)
     is_hot = token_adapter < hot_count
     is_cold = (token_adapter < none_code) & jnp.logical_not(is_hot)
@@ -278,69 +328,20 @@
     cold_target = (owner * step_count + step_at) * CAP + rank
     hot_target = jnp.where(is_hot, hot_target, -1).reshape(-1)
     cold_target = jnp.where(is_cold, cold_target, -1).reshape(-1)
-    hot_out = place_rows(rows, hot_target, hot_rows)
-    chain = Chain()
-    hot_in = lax.all_to_all(
-        chain.hold(hot_out.reshape(group_count, near * HCAP, depth)), GROUP, split_axis=0, concat_axis=0, tiled=True
-    )
-
-    hot_row = jnp.sum(jnp.where(hot_ids[:, :, None] == names, adapter_row, 0), axis=-1)
-    hot_first = jnp.where(hot_row // per_dev == me, (hot_row % per_dev) * R, -R * per_dev)
-    column = jnp.arange(per_dev * R, dtype=jnp.int32)
-    lane = jnp.arange(R, dtype=jnp.int32)
-    entry = jnp.arange(hot_count, dtype=jnp.int32)
-
-    def wanted(core):
-        firsts = []
-        for x in (x_at, 1 - x_at):
-            of_steps = jnp.sum(jnp.where(entry == 2 * x + core, hot_first, 0), axis=1)
-            firsts += [jnp.where(z_at == 0, of_steps[:near], of_steps[near:])]
-            firsts += [jnp.where(z_at == 0, of_steps[near:], of_steps[:near])]
-        return jnp.stack([(f[:, None] + lane).reshape(-1) for f in firsts])
-
-    want_mine, want_other = wanted(core_at), wanted(1 - core_at)
-    kept = near * R
-    chunk_count = 3
-    part = (depth + head_part) // chunk_count
-
-    hops = [("x", SWAP), ("z_low", SWAP)]
-    bit = 1
-    while bit < far_count:
-        hops.append(("z_high", [(i, i ^ bit) for i in range(far_count)]))
-        bit *= 2
-    mine, swapped, got, held = {}, {}, {}, {}
-
-    def operand(c, stage):
-        if stage == 0:
-            return mine[c][:, 2 * kept:] + swapped[c][:, 2 * kept:]
-        if stage == 1:
-            return mine[c][:, kept:2 * kept] + swapped[c][:, kept:2 * kept] + got[c, 0][:, kept:]
-        if stage == 2:
-            held[c] = mine[c][:, :kept] + swapped[c][:, :kept] + got[c, 0][:, :kept] + got[c, 1]
-        else:
-            held[c] = held[c] + got[c, stage - 1]
-        return held[c]
-
-    def send(c, stage, value=None):
-        got[c, stage] = chain.permute(operand(c, stage) if value is None else value, *hops[stage])
-
-    mine_all, other_first, other_rest = pick_columns(
-        after(shrink_store, chain.last), expand_store, want_mine, want_other
-    )
-    mine[0], swapped[0] = mine_all[:part], chain.permute(other_first, "core", SWAP)
-    rest_swapped = chain.permute(other_rest, "core", SWAP)
-    ready, hot_in = lax.optimization_barrier((operand(0, 0), hot_in))
-    send(0, 0, ready)
-
-    cold_at = after(cold_target, chain.last)
-    cold_hit = jnp.arange(cold_rows, dtype=jnp.int32)[:, None] == cold_at
-    tag = jnp.sum(jnp.where(cold_hit, (cold_row % per_dev + 1).reshape(-1), 0), axis=-1)
-    tag = jnp.broadcast_to(tag.astype(jnp.bfloat16)[:, None], (cold_rows, TAG))
-    packet = jnp.concatenate([narrow(pick(cold_hit), rows), tag], axis=1)
-    packet = chain.hold(packet.reshape(dp_count, step_count * CAP, depth + TAG))
-    packet = lax.all_to_all(packet, DP, split_axis=0, concat_axis=0, tiled=True).reshape(cold_rows, depth + TAG)
-
-    done = {"packet": packet}
+
+    hot_out = place_rows(rows, after(hot_target, chain.last), hot_rows)
+    hot_out = chain.hold(hot_out.reshape(group_count, near * HCAP, depth))
+    done = {"hot_in": lax.all_to_all(hot_out, GROUP, split_axis=0, concat_axis=0, tiled=True)}
+
+    def cold_tokens_out():
+        cold_at = after(cold_target, chain.last)
+        cold_hit = jnp.arange(cold_rows, dtype=jnp.int32)[:, None] == cold_at
+        tag = jnp.sum(jnp.where(cold_hit, (cold_row % per_dev + 1).reshape(-1), 0), axis=-1)
+        tag = jnp.broadcast_to(tag.astype(jnp.bfloat16)[:, None], (cold_rows, TAG))
+        packet = jnp.concatenate([narrow(pick(cold_hit), rows), tag], axis=1)
+        packet = chain.hold(packet.reshape(dp_count, step_count * CAP, depth + TAG))
+        packet = lax.all_to_all(packet, DP, split_axis=0, concat_axis=0, tiled=True)
+        done["packet"] = packet.reshape(cold_rows, depth + TAG)
 
     def base_product():
         weight = after(value_weight, chain.last)
@@ -381,12 +382,12 @@
         done["partial"] = partial + done["base_own"] + done["base_got"]
 
     between = {
-        1: [base_product],
-        2: [cold_shrink, cold_over_tp, base_over_tp],
-        3: [cold_expand, cold_back],
-        4: [all_but_hot],
+        1: [cold_tokens_out, base_product],
+        2: [base_over_tp],
+        3: [cold_shrink, cold_over_tp],
+        4: [cold_expand, cold_back, all_but_hot],
     }
-    awaited = {1: ["packet", "base_own", "base_other"], 2: ["z_cold"], 4: ["partial"]}
+    awaited = {1: ["hot_in", "base_own", "base_other"], 2: ["packet"], 3: ["z_cold", "base_got"]}
     ready = None
     for slot in range(chunk_count + len(hops) - 1):
         if slot > 0:
@@ -410,7 +411,7 @@
         done.update(zip(names_here, arrived[1 + len(here):]))
     partial = done["partial"]
 
-    hot_in = hot_in.reshape(hot_rows, depth)
+    hot_in = done["hot_in"].reshape(hot_rows, depth)
     dense = None
     for c in range(chunk_count):
         last = min((c + 1) * part, depth)

time: 189 us -> 198 us (1.048)
  waiting for transfers between devices: 84.5 us -> 91.4 us
  starting transfers between devices: 34.3 us -> 41.1 us
  Pallas kernels: 25 us -> 22.7 us
    ppermute x12, waiting for transfers between devices: 53.8 us -> 82.9 us  [permute(): return lax.ppermute(self.hold(value), axis, pairs)]
    all_to_all x1, waiting for transfers between devices: 8.93 us -> 0.01 us  [cold_back(): delta = lax.all_to_all(delta, DP, split_axis=0, concat_axis=0, tiled=True)]
    all_to_all x2, waiting for transfers between devices: 6 us -> 0.01 us  [the longest x1 0.01 us: on_device(): lax.all_to_all(hot_out, GROUP, split_axis=0, concat_axis=0, tiled=True)]
    ppermute x1, waiting for transfers between devices: 7.21 us -> 1.77 us  [sum_over_tp(): return part + lax.ppermute(part, 'tp', SWAP)]
    ppermute x12, starting transfers between devices: 13.4 us -> 16.7 us  [permute(): return lax.ppermute(self.hold(value), axis, pairs)]
    pallas_call x1, Pallas kernels: 9.73 us -> 7.43 us  [pick_columns(): pl.pallas_call(kernel, grid_spec=pltpu.PrefetchScalarGridSpec(num_scalar_...]
    unnamed x24 -> x32, local copies, waits for them, and re-layouts: 5.49 us -> 6.7 us
  transfers between devices with their start and end apart: 18 -> 18, of which waited for: 11 -> 10; matrix products, arithmetic and copies ran while one was open for 18% -> 16% of each run, Pallas kernels for 10% -> 7%
where the time goes in v9:
time: 198 us
  waiting for transfers between devices  91.4 us (46%)
  starting transfers between devices  41.1 us (21%)
  Pallas kernels  22.7 us (11%)
  other arithmetic  19.7 us (10%)
  matrix products  14.8 us (7%)
  local copies, waits for them, and re-layouts  7.61 us (4%)
    ppermute x12, waiting for transfers between devices, permute(): return lax.ppermute(self.hold(value), axis, pairs)  82.9 us
    ppermute x12, starting transfers between devices, permute(): return lax.ppermute(self.hold(value), axis, pairs)  16.7 us
    dot_general x9, matrix products, matmul(): return jnp.dot(a, b, preferred_element_type=jnp.float32)  14.5 us
    pallas_call x1, Pallas kernels, base_halves(): pl.pallas_call(kernel, grid_spec=pltpu.PrefetchScalarGridSpec(num_scalar_...  9.96 us
    pallas_call x1, Pallas kernels, pick_columns(): pl.pallas_call(kernel, grid_spec=pltpu.PrefetchScalarGridSpec(num_scalar_...  7.43 us
    all_to_all x1, starting transfers between devices, on_device(): lax.all_to_all(hot_out, GROUP, split_axis=0, concat_axis=0, tiled=True)  7.39 us
    unnamed x32, local copies, waits for them, and re-layouts  6.7 us
    all_to_all x1, starting transfers between devices, cold_tokens_out(): packet = lax.all_to_all(packet, DP, split_axis=0, concat_axis=0, tiled=True)  5.27 us
  transfers between devices with their start and end apart: 18, of which 10 were waited for; matrix products, arithmetic and copies ran while one was open for 16% of the time, Pallas kernels for 7%

profile of v9, /device:TPU:0, one launch (start us, length us, event | category | flops | bytes accessed | tf_op | source)
XLA Modules:
  0.0 197.6 jit_solution(6408372956381310005)
XLA Ops:
  2.8 2.2 %copy-done.2 = bf16[4096,512]{1,0:T(8,128)(2,1)S(1)} copy-done((bf16[4096,512]{1,0:T(8,128)(2,1)S(1)}, bf16[4096,512]{1,0:T(8,128)(2,1)}, u32[]{:S(2)}) %copy-start.2) | copy-done | bytes 4194328
  5.0 1.0 copy-done.4
  6.0 7.4 %shard_map.73 = (bf16[4608,512]{1,0:T(8,128)(2,1)S(1)}, bf16[1536,512]{1,0:T(8,128)(2,1)S(1)}, bf16[3072,512]{1,0:T(8,128)(2,1)}) custom-call(s32[4]{0:T(128)S(1)} %convert_element_type.28.mine_held, s32[4]{0:T(128)S(1)} %convert_element_type.29.other_held, s32[1,512]{1,0:T(1,128)S(1)} %bitcast.53, s32[1,512]{1,0:T(1,128)S(1)} %bitcast.54, ...), custom_call_target="tpu_custom_call" | custom-call | flops 1 | bytes 1 | tf_op jit(solution)/shard_map/pallas_call | solution.py:108
  14.0 4.4 %collective-permute-done = bf16[1536,512]{1,0:T(8,128)(2,1)S(1)} collective-permute-done((bf16[1536,512]{1,0:T(8,128)(2,1)S(1)}, bf16[1536,512]{1,0:T(8,128)(2,1)S(1)}, u32[]{:S(2)}, u32[]{:S(2)}) %collective-permute-start) | collective-permute-done | bytes 1572896 | tf_op jit(solution)/shard_map/ppermute | solution.py:48
  19.7 3.3 %shard_map.74 = bf16[256,4096]{1,0:T(8,128)(2,1)} custom-call(s32[1,512]{1,0:T(1,128)S(1)} %bitcast.51, bf16[512,4096]{1,0:T(8,128)(2,1)S(1)} %bitcast.48), custom_call_target="tpu_custom_call" | custom-call | flops 1073741824 | bytes 6291456 | tf_op jit(solution)/shard_map/pallas_call | solution.py:151
  23.0 7.4 %all-to-all-start = ((bf16[8,32,4096]{2,1,0:T(8,128)(2,1)}), bf16[8,32,4096]{2,1,0:T(8,128)(2,1)S(1)}, u32[]{:S(2)}, u32[]{:S(2)}) async-start(bf16[8,32,4096]{2,1,0:T(8,128)(2,1)} %bitcast.6), calls=%async_computation | async-start | bytes 4194304 | tf_op jit(solution)/shard_map/all_to_all | solution.py:334
  30.4 2.0 %collective-permute-start.2 = (bf16[1536,256]{1,0:T(8,128)(2,1)S(1)}, bf16[1536,256]{1,0:T(8,128)(2,1)S(1)}, u32[]{:S(2)}, u32[]{:S(2)}) collective-permute-start(bf16[1536,256]{1,0:T(8,128)(2,1)S(1)} %slice_add_fusion), channel_id=1, source_target_pairs={{0,2},{2,0},{1,3},{3,1},{4,6},{6,4},{5,7},{7,5},{8,10},{10,8},{9,1... | collective-permute-start | bytes 2359304 | tf_op jit(solution)/shard_map/ppermute | solution.py:48
  32.4 2.3 %slice_add_fusion.2 = bf16[1536,256]{1,0:T(8,128)(2,1)} fusion(bf16[3072,512]{1,0:T(8,128)(2,1)} %collective-permute-done.1, bf16[4608,512]{1,0:T(8,128)(2,1)} %copy-done.3), kind=kLoop, calls=%fused_computation.14 | loop fusion | flops 393216 | bytes 2359296 | tf_op jit(solution)/shard_map/add | solution.py:295
  34.7 38.2 %collective-permute-done.2 = bf16[1536,256]{1,0:T(8,128)(2,1)S(1)} collective-permute-done((bf16[1536,256]{1,0:T(8,128)(2,1)S(1)}, bf16[1536,256]{1,0:T(8,128)(2,1)S(1)}, u32[]{:S(2)}, u32[]{:S(2)}) %collective-permute-start.2) | collective-permute-done | bytes 786464 | tf_op jit(solution)/shard_map/ppermute | solution.py:48
  73.3 1.2 fusion.13
  74.6 2.9 %convolution_convert_fusion = bf16[128,4096]{1,0:T(8,128)(2,1)S(1)} fusion(bf16[512,4096]{1,0:T(8,128)(2,1)} %bitcast.47, s32[512]{0:T(512)S(1)} %get-tuple-element.61), kind=kOutput, calls=%fused_computation | convolution fusion | flops 537460736 | bytes 5244928 | tf_op jit(solution)/shard_map/dot_general | solution.py:22
  77.6 1.1 maximum_bitcast_fusion
  78.7 5.3 %all-to-all-start.1 = ((bf16[16,8,4224]{2,1,0:T(8,128)(2,1)}), bf16[16,8,4224]{2,1,0:T(8,128)(2,1)}, u32[]{:S(2)}, u32[]{:S(2)}) async-start(bf16[16,8,4224]{2,1,0:T(8,128)(2,1)} %maximum_bitcast_fusion), calls=%async_computation.1 | async-start | bytes 2162688 | tf_op jit(solution)/shard_map/all_to_all | solution.py:343
  84.0 1.9 collective-permute-start.4
  85.9 1.5 slice_add_fusion.1
  87.4 1.5 collective-permute-start.5
  88.9 2.2 %copy-done.1 = bf16[4,128,4096]{2,1,0:T(8,128)(2,1)S(1)} copy-done((bf16[4,128,4096]{2,1,0:T(8,128)(2,1)S(1)}, bf16[4,128,4096]{2,1,0:T(8,128)(2,1)}, u32[]{:S(2)}) %copy-start.1) | copy-done | bytes 4194328
  91.1 10.0 %shard_map.75 = (f32[512,512]{1,0:T(8,128)S(1)}, f32[512,512]{1,0:T(8,128)S(1)}) custom-call(s32[1]{0:T(128)} %bitcast.9.tp_at, bf16[512,4096]{1,0:T(8,128)(2,1)S(1)} %bitcast.49, bf16[4096,1024]{1,0:T(8,128)(2,1)} %weight_ref), custom_call_target="tpu_custom_call" | custom-call | flops 1 | bytes 1 | tf_op jit(solution)/shard_map/pallas_call | solution.py:189
  101.1 11.8 %collective-permute-done.4 = bf16[1536,128]{1,0:T(8,128)(2,1)S(1)} collective-permute-done((bf16[1536,128]{1,0:T(8,128)(2,1)S(1)}, bf16[1536,128]{1,0:T(8,128)(2,1)S(1)}, u32[]{:S(2)}, u32[]{:S(2)}) %collective-permute-start.4) | collective-permute-done | bytes 393248 | tf_op jit(solution)/shard_map/ppermute | solution.py:48
  112.9 2.0 %fusion.12 = bf16[1536,128]{1,0:T(8,128)(2,1)} fusion(bf16[1536,128]{1,0:T(8,128)(2,1)S(1)} %collective-permute-done.4, bf16[1536,512]{1,0:T(8,128)(2,1)} %copy-done.8, bf16[1536,256]{1,0:T(8,128)(2,1)S(1)} %copy-done.11, bf16[4608,512]{1,0:T(8,128)(2,1)} %copy-done.3), kind=kLoop, calls=%fused_computation.25 | loop fusion | flops 589824 | bytes 1966080 | tf_op jit(solution)/shard_map/add | solution.py:299
  114.9 1.3 slice_add_fusion.6
  117.0 2.2 %collective-permute-start.7 = (bf16[1536,128]{1,0:T(8,128)(2,1)}, bf16[1536,128]{1,0:T(8,128)(2,1)}, u32[]{:S(2)}, u32[]{:S(2)}) collective-permute-start(bf16[1536,128]{1,0:T(8,128)(2,1)} %fusion.12), channel_id=1, source_target_pairs={{0,8},{8,0},{1,9},{9,1},{2,10},{10,2},{3,11},{11,3},{4,12},{12,4},... | collective-permute-start | bytes 1179656 | tf_op jit(solution)/shard_map/ppermute | solution.py:48
  119.7 1.5 collective-permute-start.11
  121.3 14.3 %collective-permute-done.6 = bf16[1536,128]{1,0:T(8,128)(2,1)} collective-permute-done((bf16[1536,128]{1,0:T(8,128)(2,1)S(1)}, bf16[1536,128]{1,0:T(8,128)(2,1)}, u32[]{:S(2)}, u32[]{:S(2)}) %collective-permute-start.6) | collective-permute-done | bytes 393248 | tf_op jit(solution)/shard_map/ppermute | solution.py:48
  135.6 1.3 slice_add_fusion.5
  136.9 1.4 add_add_fusion.2
  138.3 2.5 %collective-permute-start.8 = (bf16[1536,128]{1,0:T(8,128)(2,1)S(1)}, bf16[1536,128]{1,0:T(8,128)(2,1)S(1)}, u32[]{:S(2)}, u32[]{:S(2)}) collective-permute-start(bf16[1536,128]{1,0:T(8,128)(2,1)S(1)} %slice_add_fusion.5), channel_id=1, source_target_pairs={{0,4},{4,0},{1,5},{5,1},{2,6},{6,2},{3,7},{7,3},{8,12},{12,8},{9,1... | collective-permute-start | bytes 1179656 | tf_op jit(solution)/shard_map/ppermute | solution.py:48
  140.8 2.9 %collective-permute-start.9 = (bf16[1536,128]{1,0:T(8,128)(2,1)S(1)}, bf16[1536,128]{1,0:T(8,128)(2,1)S(1)}, u32[]{:S(2)}, u32[]{:S(2)}) collective-permute-start(bf16[1536,128]{1,0:T(8,128)(2,1)S(1)} %add_add_fusion.2), channel_id=1, source_target_pairs={{0,8},{8,0},{1,9},{9,1},{2,10},{10,2},{3,11},{11,3},{4,12},{12,4},... | collective-permute-start | bytes 1179656 | tf_op jit(solution)/shard_map/ppermute | solution.py:48
  144.6 3.4 %convolution_select_fusion = f32[128,512]{1,0:T(8,128)S(1)} fusion(bf16[4096,512]{1,0:T(8,128)(2,1)} %store_ref.1, bf16[128,4224]{1,0:T(8,128)(2,1)} %bitcast.10, s32[512]{0:T(512)S(1)} %fusion.26, s32[128]{0:T(128)S(1)} %convert_reduce_fusion.1), kind=kOutput, calls=%fused_computation.1 | convolution fusion | flops 537001984 | bytes 5507584 | tf_op jit(solution)/shard_map/dot_general | solution.py:22
  148.0 1.6 collective-permute-start.10
  149.6 1.3 fusion.5
  151.0 1.3 convolution_add_fusion.3
  152.7 1.8 collective-permute-done.10
  154.5 2.7 %collective-permute-done.8 = bf16[1536,128]{1,0:T(8,128)(2,1)S(1)} collective-permute-done((bf16[1536,128]{1,0:T(8,128)(2,1)S(1)}, bf16[1536,128]{1,0:T(8,128)(2,1)S(1)}, u32[]{:S(2)}, u32[]{:S(2)}) %collective-permute-start.8) | collective-permute-done | bytes 393248 | tf_op jit(solution)/shard_map/ppermute | solution.py:48
  157.2 2.6 %collective-permute-done.9 = bf16[1536,128]{1,0:T(8,128)(2,1)S(1)} collective-permute-done((bf16[1536,128]{1,0:T(8,128)(2,1)S(1)}, bf16[1536,128]{1,0:T(8,128)(2,1)S(1)}, u32[]{:S(2)}, u32[]{:S(2)}) %collective-permute-start.9) | collective-permute-done | bytes 393248 | tf_op jit(solution)/shard_map/ppermute | solution.py:48
  160.6 1.7 add_add_fusion.1.first_ref
  163.6 5.1 %all-to-all-start.2 = ((bf16[16,8,512]{2,1,0:T(8,128)(2,1)}), bf16[16,8,512]{2,1,0:T(8,128)(2,1)S(1)}, u32[]{:S(2)}, u32[]{:S(2)}) async-start(bf16[16,8,512]{2,1,0:T(8,128)(2,1)} %fusion), calls=%async_computation.2 | async-start | bytes 262144 | tf_op jit(solution)/shard_map/all_to_all | solution.py:374
  168.7 1.3 fusion.9
  170.0 1.6 fusion.1
  171.6 8.8 %collective-permute-done.12.second_ref = bf16[1536,128]{1,0:T(8,128)(2,1)S(1)} collective-permute-done((bf16[1536,128]{1,0:T(8,128)(2,1)S(1)}, bf16[1536,128]{1,0:T(8,128)(2,1)S(1)}, u32[]{:S(2)}, u32[]{:S(2)}) %collective-permute-start.12) | collective-permute-done | bytes 393248 | tf_op jit(solution)/shard_map/ppermute | solution.py:48
  180.4 1.3 convolution_add_fusion
  181.8 1.6 collective-permute-start.13
  183.5 2.6 %collective-permute-done.13.got_ref = f32[128,128]{1,0:T(8,128)S(1)} collective-permute-done((f32[128,128]{1,0:T(8,128)S(1)}, f32[128,128]{1,0:T(8,128)S(1)}, u32[]{:S(2)}, u32[]{:S(2)}) %collective-permute-start.13) | collective-permute-done | bytes 65568 | tf_op jit(solution)/shard_map/ppermute | solution.py:425
  186.1 0.9 shard_map.76
  187.1 3.4 %all-to-all-start.3 = ((bf16[8,32,512]{2,1,0:T(8,128)(2,1)}), bf16[8,32,512]{2,1,0:T(8,128)(2,1)S(1)}, u32[]{:S(2)}, u32[]{:S(2)}) async-start(bf16[8,32,512]{2,1,0:T(8,128)(2,1)} %bitcast.18), calls=%async_computation.3 | async-start | bytes 524288 | tf_op jit(solution)/shard_map/all_to_all | solution.py:430
  190.8 1.5 add_add_fusion.partial_ref
  192.4 4.1 %all-to-all-done.3 = bf16[8,32,512]{2,1,0:T(8,128)(2,1)S(1)} async-done(((bf16[8,32,512]{2,1,0:T(8,128)(2,1)}), bf16[8,32,512]{2,1,0:T(8,128)(2,1)S(1)}, u32[]{:S(2)}, u32[]{:S(2)}) %all-to-all-start.3) | async-done | bytes 262176 | tf_op jit(solution)/shard_map/all_to_all | solution.py:430
  196.5 1.1 shard_map.77
  (92 shorter events, 10.2 us)
Async XLA Ops:
  2.8 2.2 %copy-start.2 = (bf16[4096,512]{1,0:T(8,128)(2,1)S(1)}, bf16[4096,512]{1,0:T(8,128)(2,1)}, u32[]{:S(2)}) copy-start(bf16[4096,512]{1,0:T(8,128)(2,1)} %store_ref.1) | copy-start | bytes 12582916
  5.0 1.0 copy-start.4
  6.0 13.7 %copy-start = (bf16[4,128,4096]{2,1,0:T(8,128)(2,1)S(1)}, bf16[4,128,4096]{2,1,0:T(8,128)(2,1)}, u32[]{:S(2)}) copy-start(bf16[4,128,4096]{2,1,0:T(8,128)(2,1)} %param.7) | copy-start | bytes 12582916
  13.5 5.0 %copy-start.3 = (bf16[4608,512]{1,0:T(8,128)(2,1)}, bf16[4608,512]{1,0:T(8,128)(2,1)S(1)}, u32[]{:S(2)}) copy-start(bf16[4608,512]{1,0:T(8,128)(2,1)S(1)} %get-tuple-element.63) | copy-start | bytes 14155780
  13.5 5.1 %copy-start.13 = (s32[4,128]{1,0:T(4,128)S(1)}, s32[4,128]{1,0:T(4,128)}, u32[]{:S(2)}) copy-start(s32[4,128]{1,0:T(4,128)} %param.12) | copy-start | bytes 6148
  13.5 5.1 %copy-start.14 = (s32[128]{0:T(128)S(1)}, s32[128]{0:T(128)}, u32[]{:S(2)}) copy-start(s32[128]{0:T(128)} %param.11) | copy-start | bytes 1540
  13.5 5.0 %collective-permute-start = (bf16[1536,512]{1,0:T(8,128)(2,1)S(1)}, bf16[1536,512]{1,0:T(8,128)(2,1)S(1)}, u32[]{:S(2)}, u32[]{:S(2)}) collective-permute-start(bf16[1536,512]{1,0:T(8,128)(2,1)S(1)} %get-tuple-element.49), channel_id=1, source_target_pairs={{0,1},{1,0},{2,3},{3,2},{4,5},{5,4},{6,7},{7,6},{8,9},{9,8},{10,11... | collective-permute-start | bytes 4718600 | tf_op jit(solution)/shard_map/ppermute | solution.py:48
  13.9 18.5 %collective-permute-start.1 = (bf16[3072,512]{1,0:T(8,128)(2,1)}, bf16[3072,512]{1,0:T(8,128)(2,1)}, u32[]{:S(2)}, u32[]{:S(2)}) collective-permute-start(bf16[3072,512]{1,0:T(8,128)(2,1)} %get-tuple-element.51), channel_id=1, source_target_pairs={{0,1},{1,0},{2,3},{3,2},{4,5},{5,4},{6,7},{7,6},{8,9},{9,8},{10,11... | collective-permute-start | bytes 9437192 | tf_op jit(solution)/shard_map/ppermute | solution.py:48
  18.5 1.1 copy-start.8
  23.0 55.7 %all-to-all-start = ((bf16[8,32,4096]{2,1,0:T(8,128)(2,1)}), bf16[8,32,4096]{2,1,0:T(8,128)(2,1)S(1)}, u32[]{:S(2)}, u32[]{:S(2)}) async-start(bf16[8,32,4096]{2,1,0:T(8,128)(2,1)} %bitcast.6), calls=%async_computation | async-start | bytes 4194304 | tf_op jit(solution)/shard_map/all_to_all | solution.py:334
  30.4 42.5 %collective-permute-start.2 = (bf16[1536,256]{1,0:T(8,128)(2,1)S(1)}, bf16[1536,256]{1,0:T(8,128)(2,1)S(1)}, u32[]{:S(2)}, u32[]{:S(2)}) collective-permute-start(bf16[1536,256]{1,0:T(8,128)(2,1)S(1)} %slice_add_fusion), channel_id=1, source_target_pairs={{0,2},{2,0},{1,3},{3,1},{4,6},{6,4},{5,7},{7,5},{8,10},{10,8},{9,1... | collective-permute-start | bytes 2359304 | tf_op jit(solution)/shard_map/ppermute | solution.py:48
  72.9 1.7 copy-start.10
  72.9 40.0 %collective-permute-start.3 = (bf16[1536,256]{1,0:T(8,128)(2,1)}, bf16[1536,256]{1,0:T(8,128)(2,1)}, u32[]{:S(2)}, u32[]{:S(2)}) collective-permute-start(bf16[1536,256]{1,0:T(8,128)(2,1)} %slice_add_fusion.2), channel_id=1, source_target_pairs={{0,2},{2,0},{1,3},{3,1},{4,6},{6,4},{5,7},{7,5},{8,10},{10,8},{9,1... | collective-permute-start | bytes 2359304 | tf_op jit(solution)/shard_map/ppermute | solution.py:48
  78.7 8.7 %copy-start.6 = (bf16[8,32,4096]{2,1,0:T(8,128)(2,1)}, bf16[8,32,4096]{2,1,0:T(8,128)(2,1)S(1)}, u32[]{:S(2)}) copy-start(bf16[8,32,4096]{2,1,0:T(8,128)(2,1)S(1)} %all-to-all-done) | copy-start | bytes 6291460
  78.7 42.6 %all-to-all-start.1 = ((bf16[16,8,4224]{2,1,0:T(8,128)(2,1)}), bf16[16,8,4224]{2,1,0:T(8,128)(2,1)}, u32[]{:S(2)}, u32[]{:S(2)}) async-start(bf16[16,8,4224]{2,1,0:T(8,128)(2,1)} %maximum_bitcast_fusion), calls=%async_computation.1 | async-start | bytes 2162688 | tf_op jit(solution)/shard_map/all_to_all | solution.py:343
  84.0 28.9 %collective-permute-start.4 = (bf16[1536,128]{1,0:T(8,128)(2,1)S(1)}, bf16[1536,128]{1,0:T(8,128)(2,1)S(1)}, u32[]{:S(2)}, u32[]{:S(2)}) collective-permute-start(bf16[1536,128]{1,0:T(8,128)(2,1)S(1)} %fusion.13), channel_id=1, source_target_pairs={{0,4},{4,0},{1,5},{5,1},{2,6},{6,2},{3,7},{7,3},{8,12},{12,8},{9,1... | collective-permute-start | bytes 1179656 | tf_op jit(solution)/shard_map/ppermute | solution.py:48
  87.4 33.9 %collective-permute-start.5 = (bf16[1536,256]{1,0:T(8,128)(2,1)S(1)}, bf16[1536,256]{1,0:T(8,128)(2,1)}, u32[]{:S(2)}, u32[]{:S(2)}) collective-permute-start(bf16[1536,256]{1,0:T(8,128)(2,1)S(1)} %slice_add_fusion.1), channel_id=1, source_target_pairs={{0,2},{2,0},{1,3},{3,1},{4,6},{6,4},{5,7},{7,5},{8,10},{10,8},{9,1... | collective-permute-start | bytes 2359304 | tf_op jit(solution)/shard_map/ppermute | solution.py:48
  88.9 2.2 %copy-start.1 = (bf16[4,128,4096]{2,1,0:T(8,128)(2,1)S(1)}, bf16[4,128,4096]{2,1,0:T(8,128)(2,1)}, u32[]{:S(2)}) copy-start(bf16[4,128,4096]{2,1,0:T(8,128)(2,1)} %param.7) | copy-start | bytes 12582916
  91.1 21.8 %copy-start.11 = (bf16[1536,256]{1,0:T(8,128)(2,1)S(1)}, bf16[1536,256]{1,0:T(8,128)(2,1)}, u32[]{:S(2)}) copy-start(bf16[1536,256]{1,0:T(8,128)(2,1)} %copy-done.10) | copy-start | bytes 2359300
  116.2 19.4 %collective-permute-start.6 = (bf16[1536,128]{1,0:T(8,128)(2,1)S(1)}, bf16[1536,128]{1,0:T(8,128)(2,1)}, u32[]{:S(2)}, u32[]{:S(2)}) collective-permute-start(bf16[1536,128]{1,0:T(8,128)(2,1)S(1)} %slice_add_fusion.6), channel_id=1, source_target_pairs={{0,4},{4,0},{1,5},{5,1},{2,6},{6,2},{3,7},{7,3},{8,12},{12,8},{9,1... | collective-permute-start | bytes 1179656 | tf_op jit(solution)/shard_map/ppermute | solution.py:48
  117.0 18.6 %collective-permute-start.7 = (bf16[1536,128]{1,0:T(8,128)(2,1)}, bf16[1536,128]{1,0:T(8,128)(2,1)}, u32[]{:S(2)}, u32[]{:S(2)}) collective-permute-start(bf16[1536,128]{1,0:T(8,128)(2,1)} %fusion.12), channel_id=1, source_target_pairs={{0,8},{8,0},{1,9},{9,1},{2,10},{10,2},{3,11},{11,3},{4,12},{12,4},... | collective-permute-start | bytes 1179656 | tf_op jit(solution)/shard_map/ppermute | solution.py:48
  119.7 40.1 %collective-permute-start.11 = (f32[512,512]{1,0:T(8,128)S(1)}, f32[512,512]{1,0:T(8,128)S(1)}, u32[]{:S(2)}, u32[]{:S(2)}) collective-permute-start(f32[512,512]{1,0:T(8,128)S(1)} %get-tuple-element.74), channel_id=1, source_target_pairs={{0,16},{16,0},{1,17},{17,1},{2,18},{18,2},{3,19},{19,3},{4,20},{20... | collective-permute-start | bytes 3145736 | tf_op jit(solution)/shard_map/ppermute | solution.py:48
  138.3 18.9 %collective-permute-start.8 = (bf16[1536,128]{1,0:T(8,128)(2,1)S(1)}, bf16[1536,128]{1,0:T(8,128)(2,1)S(1)}, u32[]{:S(2)}, u32[]{:S(2)}) collective-permute-start(bf16[1536,128]{1,0:T(8,128)(2,1)S(1)} %slice_add_fusion.5), channel_id=1, source_target_pairs={{0,4},{4,0},{1,5},{5,1},{2,6},{6,2},{3,7},{7,3},{8,12},{12,8},{9,1... | collective-permute-start | bytes 1179656 | tf_op jit(solution)/shard_map/ppermute | solution.py:48
  140.8 19.0 %collective-permute-start.9 = (bf16[1536,128]{1,0:T(8,128)(2,1)S(1)}, bf16[1536,128]{1,0:T(8,128)(2,1)S(1)}, u32[]{:S(2)}, u32[]{:S(2)}) collective-permute-start(bf16[1536,128]{1,0:T(8,128)(2,1)S(1)} %add_add_fusion.2), channel_id=1, source_target_pairs={{0,8},{8,0},{1,9},{9,1},{2,10},{10,2},{3,11},{11,3},{4,12},{12,4},... | collective-permute-start | bytes 1179656 | tf_op jit(solution)/shard_map/ppermute | solution.py:48
  144.6 5.0 %copy-start.7 = (bf16[8,32,4096]{2,1,0:T(8,128)(2,1)S(1)}, bf16[8,32,4096]{2,1,0:T(8,128)(2,1)}, u32[]{:S(2)}) copy-start(bf16[8,32,4096]{2,1,0:T(8,128)(2,1)} %copy-done.6) | copy-start | bytes 6291460
  148.0 6.4 %collective-permute-start.10 = (f32[128,512]{1,0:T(8,128)S(1)}, f32[128,512]{1,0:T(8,128)S(1)}, u32[]{:S(2)}, u32[]{:S(2)}) collective-permute-start(f32[128,512]{1,0:T(8,128)S(1)} %convolution_select_fusion), channel_id=1, source_target_pairs={{0,16},{16,0},{1,17},{17,1},{2,18},{18,2},{3,19},{19,3},{4,20},{20... | collective-permute-start | bytes 786440 | tf_op jit(solution)/shard_map/ppermute | solution.py:31
  152.3 10.4 %copy-start.5 = (bf16[512,512]{1,0:T(8,128)(2,1)S(1)}, bf16[512,512]{1,0:T(8,128)(2,1)}, u32[]{:S(2)}) copy-start(bf16[512,512]{1,0:T(8,128)(2,1)} %expand_ref.1) | copy-start | bytes 1572868
  159.8 0.7 copy-start.12
  160.6 11.1 %copy-start.9 = (f32[512,512]{1,0:T(8,128)}, f32[512,512]{1,0:T(8,128)S(1)}, u32[]{:S(2)}) copy-start(f32[512,512]{1,0:T(8,128)S(1)} %collective-permute-done.11) | copy-start | bytes 3145732
  162.3 18.1 %collective-permute-start.12 = (bf16[1536,128]{1,0:T(8,128)(2,1)S(1)}, bf16[1536,128]{1,0:T(8,128)(2,1)S(1)}, u32[]{:S(2)}, u32[]{:S(2)}) collective-permute-start(bf16[1536,128]{1,0:T(8,128)(2,1)S(1)} %add_add_fusion.1.first_ref), channel_id=1, source_target_pairs={{0,8},{8,0},{1,9},{9,1},{2,10},{10,2},{3,11},{11,3},{4,12},{12,4},... | collective-permute-start | bytes 1179656 | tf_op jit(solution)/shard_map/ppermute | solution.py:48
  163.6 18.2 %copy-start.15 = (pred[128]{0:T(512)(128)(4,1)S(1)}, pred[128]{0:T(512)(128)(4,1)}, u32[]{:S(2)}) copy-start(pred[128]{0:T(512)(128)(4,1)} %get-tuple-element.118) | copy-start | bytes 388
  163.6 23.5 %all-to-all-start.2 = ((bf16[16,8,512]{2,1,0:T(8,128)(2,1)}), bf16[16,8,512]{2,1,0:T(8,128)(2,1)S(1)}, u32[]{:S(2)}, u32[]{:S(2)}) async-start(bf16[16,8,512]{2,1,0:T(8,128)(2,1)} %fusion), calls=%async_computation.2 | async-start | bytes 262144 | tf_op jit(solution)/shard_map/all_to_all | solution.py:374
  181.8 4.3 %collective-permute-start.13 = (f32[128,128]{1,0:T(8,128)S(1)}, f32[128,128]{1,0:T(8,128)S(1)}, u32[]{:S(2)}, u32[]{:S(2)}) collective-permute-start(f32[128,128]{1,0:T(8,128)S(1)} %fusion.21.own_ref), channel_id=1, source_target_pairs={{0,16},{16,0},{1,17},{17,1},{2,18},{18,2},{3,19},{19,3},{4,20},{20... | collective-permute-start | bytes 196616 | tf_op jit(solution)/shard_map/ppermute | solution.py:425
  187.1 9.4 %all-to-all-start.3 = ((bf16[8,32,512]{2,1,0:T(8,128)(2,1)}), bf16[8,32,512]{2,1,0:T(8,128)(2,1)S(1)}, u32[]{:S(2)}, u32[]{:S(2)}) async-start(bf16[8,32,512]{2,1,0:T(8,128)(2,1)} %bitcast.18), calls=%async_computation.3 | async-start | bytes 524288 | tf_op jit(solution)/shard_map/all_to_all | solution.py:430

commit v10 on v9

--- a/solution.py
+++ b/solution.py
@@ -301,8 +301,8 @@
             held[c] = held[c] + got[c, stage - 1]
         return held[c]
 
-    def send(c, stage, value=None):
-        got[c, stage] = chain.permute(operand(c, stage) if value is None else value, *hops[stage])
+    def send(c, stage):
+        got[c, stage] = chain.permute(operand(c, stage), *hops[stage])
 
     mine_all, other_first, other_rest = pick_columns(
         shrink_store, expand_store, want_mine, want_other
@@ -388,19 +388,16 @@
         4: [cold_expand, cold_back, all_but_hot],
     }
     awaited = {1: ["hot_in", "base_own", "base_other"], 2: ["packet"], 3: ["z_cold", "base_got"]}
-    ready = None
     for slot in range(chunk_count + len(hops) - 1):
         if slot > 0:
+            if slot < chunk_count:
+                mine[slot] = after(mine_all, chain.last)[slot * part:(slot + 1) * part]
+                swapped[slot] = after(rest_swapped, chain.last)[(slot - 1) * part:slot * part]
             for stage in sorted(range(len(hops)), key=lambda stage: stage == 1):
                 if 0 <= slot - stage < chunk_count:
-                    send(slot - stage, stage, ready if stage == 0 else None)
+                    send(slot - stage, stage)
         for work in between.get(slot, []):
             work()
-        c = slot + 1
-        if c < chunk_count:
-            mine[c] = after(mine_all, chain.last)[c * part:(c + 1) * part]
-            swapped[c] = after(rest_swapped, chain.last)[(c - 1) * part:c * part]
-            ready = chain.hold(operand(c, 0))
         here = [(slot - stage, stage) for stage in range(len(hops)) if 0 <= slot - stage < chunk_count]
         names_here = awaited.get(slot, [])
         arrived = lax.optimization_barrier(

time: 198 us -> 196 us (0.990); the launches traced: 198 us -> 194 us
  starting transfers between devices: 41.1 us -> 31.9 us
  Pallas kernels: 22.7 us -> 24.9 us
    ppermute x12, starting transfers between devices: 16.7 us -> 10.4 us  [permute(): return lax.ppermute(self.hold(value), axis, pairs)]
    all_to_all x1, starting transfers between devices: 7.39 us -> 5.12 us  [on_device(): lax.all_to_all(hot_out, GROUP, split_axis=0, concat_axis=0, tiled=True)]
    pallas_call x1, Pallas kernels: 7.43 us -> 9.65 us  [pick_columns(): pl.pallas_call(kernel, grid_spec=pltpu.PrefetchScalarGridSpec(num_scalar_...]
  transfers between devices with their start and end apart: 18 -> 18, of which waited for: 10 -> 11; matrix products, arithmetic and copies ran while one was open for 16% -> 17% of each run, Pallas kernels for 7% -> 7%
where the time goes in v10:
time: 196 us; the launch traced here: 194 us
  waiting for transfers between devices  92.8 us (47%)
  starting transfers between devices  31.9 us (16%)
  Pallas kernels  24.9 us (13%)
  other arithmetic  20.3 us (10%)
  matrix products  14.8 us (8%)
  local copies, waits for them, and re-layouts  8.52 us (4%)
    ppermute x12, waiting for transfers between devices, permute(): return lax.ppermute(self.hold(value), axis, pairs)  83.4 us
    dot_general x9, matrix products, matmul(): return jnp.dot(a, b, preferred_element_type=jnp.float32)  14.5 us
    ppermute x12, starting transfers between devices, permute(): return lax.ppermute(self.hold(value), axis, pairs)  10.4 us
    pallas_call x1, Pallas kernels, base_halves(): pl.pallas_call(kernel, grid_spec=pltpu.PrefetchScalarGridSpec(num_scalar_...  9.89 us
    pallas_call x1, Pallas kernels, pick_columns(): pl.pallas_call(kernel, grid_spec=pltpu.PrefetchScalarGridSpec(num_scalar_...  9.65 us
    unnamed x32, local copies, waits for them, and re-layouts  7.61 us
    all_to_all x1, starting transfers between devices, cold_back(): delta = lax.all_to_all(delta, DP, split_axis=0, concat_axis=0, tiled=True)  5.17 us
    all_to_all x1, starting transfers between devices, on_device(): lax.all_to_all(hot_out, GROUP, split_axis=0, concat_axis=0, tiled=True)  5.12 us
  transfers between devices with their start and end apart: 18, of which 11 were waited for; matrix products, arithmetic and copies ran while one was open for 17% of the time, Pallas kernels for 7%

profile of v10, /device:TPU:0, one launch (start us, length us, event | category | flops | bytes accessed | tf_op | source)
XLA Modules:
  0.0 193.6 jit_solution(15281995116703102953)
XLA Ops:
  0.1 0.9 select_reduce_fusion.2
  2.8 2.2 %copy-done.2 = bf16[4096,512]{1,0:T(8,128)(2,1)S(1)} copy-done((bf16[4096,512]{1,0:T(8,128)(2,1)S(1)}, bf16[4096,512]{1,0:T(8,128)(2,1)}, u32[]{:S(2)}) %copy-start.2) | copy-done | bytes 4194328
  5.0 1.0 copy-done.4
  6.0 9.7 %shard_map.73 = (bf16[4608,512]{1,0:T(8,128)(2,1)S(1)}, bf16[1536,512]{1,0:T(8,128)(2,1)S(1)}, bf16[3072,512]{1,0:T(8,128)(2,1)}) custom-call(s32[4]{0:T(128)S(1)} %convert_element_type.28.mine_held, s32[4]{0:T(128)S(1)} %convert_element_type.29.other_held, s32[1,512]{1,0:T(1,128)S(1)} %bitcast.53, s32[1,512]{1,0:T(1,128)S(1)} %bitcast.54, ...), custom_call_target="tpu_custom_call" | custom-call | flops 1 | bytes 1 | tf_op jit(solution)/shard_map/pallas_call | solution.py:108
  16.3 4.4 %collective-permute-done = bf16[1536,512]{1,0:T(8,128)(2,1)S(1)} collective-permute-done((bf16[1536,512]{1,0:T(8,128)(2,1)S(1)}, bf16[1536,512]{1,0:T(8,128)(2,1)S(1)}, u32[]{:S(2)}, u32[]{:S(2)}) %collective-permute-start) | collective-permute-done | bytes 1572896 | tf_op jit(solution)/shard_map/ppermute | solution.py:48
  22.0 3.3 %shard_map.74 = bf16[256,4096]{1,0:T(8,128)(2,1)} custom-call(s32[1,512]{1,0:T(1,128)S(1)} %bitcast.51, bf16[512,4096]{1,0:T(8,128)(2,1)S(1)} %bitcast.48), custom_call_target="tpu_custom_call" | custom-call | flops 1073741824 | bytes 6291456 | tf_op jit(solution)/shard_map/pallas_call | solution.py:151
  25.2 5.1 %all-to-all-start = ((bf16[8,32,4096]{2,1,0:T(8,128)(2,1)}), bf16[8,32,4096]{2,1,0:T(8,128)(2,1)S(1)}, u32[]{:S(2)}, u32[]{:S(2)}) async-start(bf16[8,32,4096]{2,1,0:T(8,128)(2,1)} %bitcast.6), calls=%async_computation | async-start | bytes 4194304 | tf_op jit(solution)/shard_map/all_to_all | solution.py:334
  30.4 2.0 %collective-permute-start.1 = (bf16[1536,256]{1,0:T(8,128)(2,1)S(1)}, bf16[1536,256]{1,0:T(8,128)(2,1)S(1)}, u32[]{:S(2)}, u32[]{:S(2)}) collective-permute-start(bf16[1536,256]{1,0:T(8,128)(2,1)S(1)} %slice_add_fusion), channel_id=1, source_target_pairs={{0,2},{2,0},{1,3},{3,1},{4,6},{6,4},{5,7},{7,5},{8,10},{10,8},{9,1... | collective-permute-start | bytes 2359304 | tf_op jit(solution)/shard_map/ppermute | solution.py:48
  32.4 40.5 %collective-permute-done.1 = bf16[1536,256]{1,0:T(8,128)(2,1)S(1)} collective-permute-done((bf16[1536,256]{1,0:T(8,128)(2,1)S(1)}, bf16[1536,256]{1,0:T(8,128)(2,1)S(1)}, u32[]{:S(2)}, u32[]{:S(2)}) %collective-permute-start.1) | collective-permute-done | bytes 786464 | tf_op jit(solution)/shard_map/ppermute | solution.py:48
  73.8 1.2 fusion.13
  75.0 2.3 %slice_add_fusion.2 = bf16[1536,256]{1,0:T(8,128)(2,1)} fusion(bf16[3072,512]{1,0:T(8,128)(2,1)} %collective-permute-done.2, bf16[4608,512]{1,0:T(8,128)(2,1)} %copy-done.3), kind=kLoop, calls=%fused_computation.14 | loop fusion | flops 393216 | bytes 2359296 | tf_op jit(solution)/shard_map/add | solution.py:295
  77.8 1.7 collective-permute-start.4
  79.4 2.9 %convolution_convert_fusion = bf16[128,4096]{1,0:T(8,128)(2,1)S(1)} fusion(bf16[512,4096]{1,0:T(8,128)(2,1)} %bitcast.47, s32[512]{0:T(512)S(1)} %get-tuple-element.64), kind=kOutput, calls=%fused_computation | convolution fusion | flops 537460736 | bytes 5244928 | tf_op jit(solution)/shard_map/dot_general | solution.py:22
  82.5 1.1 maximum_bitcast_fusion
  83.6 4.6 %all-to-all-start.1 = ((bf16[16,8,4224]{2,1,0:T(8,128)(2,1)}), bf16[16,8,4224]{2,1,0:T(8,128)(2,1)}, u32[]{:S(2)}, u32[]{:S(2)}) async-start(bf16[16,8,4224]{2,1,0:T(8,128)(2,1)} %maximum_bitcast_fusion), calls=%async_computation.1 | async-start | bytes 2162688 | tf_op jit(solution)/shard_map/all_to_all | solution.py:343
  88.2 2.2 %copy-done.1 = bf16[4,128,4096]{2,1,0:T(8,128)(2,1)S(1)} copy-done((bf16[4,128,4096]{2,1,0:T(8,128)(2,1)S(1)}, bf16[4,128,4096]{2,1,0:T(8,128)(2,1)}, u32[]{:S(2)}) %copy-start.1) | copy-done | bytes 4194328
  90.4 9.9 %shard_map.75 = (f32[512,512]{1,0:T(8,128)S(1)}, f32[512,512]{1,0:T(8,128)S(1)}) custom-call(s32[1]{0:T(128)} %bitcast.9.tp_at, bf16[512,4096]{1,0:T(8,128)(2,1)S(1)} %bitcast.49, bf16[4096,1024]{1,0:T(8,128)(2,1)} %weight_ref), custom_call_target="tpu_custom_call" | custom-call | flops 1 | bytes 1 | tf_op jit(solution)/shard_map/pallas_call | solution.py:189
  100.3 3.6 %collective-permute-done.3 = bf16[1536,256]{1,0:T(8,128)(2,1)} collective-permute-done((bf16[1536,256]{1,0:T(8,128)(2,1)}, bf16[1536,256]{1,0:T(8,128)(2,1)}, u32[]{:S(2)}, u32[]{:S(2)}) %collective-permute-start.3) | collective-permute-done | bytes 786464 | tf_op jit(solution)/shard_map/ppermute | solution.py:48
  104.0 2.3 %slice_add_fusion.1 = bf16[1536,256]{1,0:T(8,128)(2,1)} fusion(bf16[3072,512]{1,0:T(8,128)(2,1)} %collective-permute-done.2, bf16[4608,512]{1,0:T(8,128)(2,1)} %copy-done.3), kind=kLoop, calls=%fused_computation.13 | loop fusion | flops 393216 | bytes 2359296 | tf_op jit(solution)/shard_map/add | solution.py:295
  106.3 2.1 %fusion.12 = bf16[1536,128]{1,0:T(8,128)(2,1)} fusion(bf16[1536,128]{1,0:T(8,128)(2,1)} %collective-permute-done.4, bf16[1536,512]{1,0:T(8,128)(2,1)} %copy-done.8, bf16[1536,256]{1,0:T(8,128)(2,1)S(1)} %copy-done.11, bf16[4608,512]{1,0:T(8,128)(2,1)} %copy-done.3), kind=kLoop, calls=%fused_computation.25 | loop fusion | flops 589824 | bytes 1966080 | tf_op jit(solution)/shard_map/add | solution.py:299
  108.4 1.3 slice_add_fusion.6
  109.8 1.9 collective-permute-start.7
  112.2 1.5 collective-permute-start.11
  113.8 12.4 %collective-permute-done.6 = bf16[1536,128]{1,0:T(8,128)(2,1)} collective-permute-done((bf16[1536,128]{1,0:T(8,128)(2,1)S(1)}, bf16[1536,128]{1,0:T(8,128)(2,1)}, u32[]{:S(2)}, u32[]{:S(2)}) %collective-permute-start.6) | collective-permute-done | bytes 393248 | tf_op jit(solution)/shard_map/ppermute | solution.py:48
  126.2 6.0 %collective-permute-done.7 = bf16[1536,128]{1,0:T(8,128)(2,1)} collective-permute-done((bf16[1536,128]{1,0:T(8,128)(2,1)}, bf16[1536,128]{1,0:T(8,128)(2,1)}, u32[]{:S(2)}, u32[]{:S(2)}) %collective-permute-start.7) | collective-permute-done | bytes 393248 | tf_op jit(solution)/shard_map/ppermute | solution.py:48
  132.2 1.3 slice_add_fusion.5
  133.5 1.4 add_add_fusion.2
  135.0 1.9 collective-permute-start.9
  137.8 3.4 %convolution_select_fusion = f32[128,512]{1,0:T(8,128)S(1)} fusion(bf16[4096,512]{1,0:T(8,128)(2,1)} %store_ref.1, bf16[128,4224]{1,0:T(8,128)(2,1)} %bitcast.10, s32[512]{0:T(512)S(1)} %fusion.26, s32[128]{0:T(128)S(1)} %convert_reduce_fusion.1), kind=kOutput, calls=%fused_computation.1 | convolution fusion | flops 537001984 | bytes 5507584 | tf_op jit(solution)/shard_map/dot_general | solution.py:22
  141.2 1.6 collective-permute-start.10
  142.8 1.3 fusion.5
  144.2 1.3 convolution_add_fusion.3
  145.9 2.7 %collective-permute-done.10 = f32[128,512]{1,0:T(8,128)S(1)} collective-permute-done((f32[128,512]{1,0:T(8,128)S(1)}, f32[128,512]{1,0:T(8,128)S(1)}, u32[]{:S(2)}, u32[]{:S(2)}) %collective-permute-start.10) | collective-permute-done | bytes 262176 | tf_op jit(solution)/shard_map/ppermute | solution.py:31
  148.6 4.2 %collective-permute-done.8 = bf16[1536,128]{1,0:T(8,128)(2,1)S(1)} collective-permute-done((bf16[1536,128]{1,0:T(8,128)(2,1)S(1)}, bf16[1536,128]{1,0:T(8,128)(2,1)S(1)}, u32[]{:S(2)}, u32[]{:S(2)}) %collective-permute-start.8) | collective-permute-done | bytes 393248 | tf_op jit(solution)/shard_map/ppermute | solution.py:48
  152.8 2.3 %collective-permute-done.9 = bf16[1536,128]{1,0:T(8,128)(2,1)S(1)} collective-permute-done((bf16[1536,128]{1,0:T(8,128)(2,1)S(1)}, bf16[1536,128]{1,0:T(8,128)(2,1)S(1)}, u32[]{:S(2)}, u32[]{:S(2)}) %collective-permute-start.9) | collective-permute-done | bytes 393248 | tf_op jit(solution)/shard_map/ppermute | solution.py:48
  155.9 1.3 add_add_fusion.1.first_ref
  158.4 5.2 %all-to-all-start.2 = ((bf16[16,8,512]{2,1,0:T(8,128)(2,1)}), bf16[16,8,512]{2,1,0:T(8,128)(2,1)S(1)}, u32[]{:S(2)}, u32[]{:S(2)}) async-start(bf16[16,8,512]{2,1,0:T(8,128)(2,1)} %fusion), calls=%async_computation.2 | async-start | bytes 262144 | tf_op jit(solution)/shard_map/all_to_all | solution.py:374
  163.6 1.3 fusion.9
  164.9 1.6 fusion.1
  166.5 9.9 %collective-permute-done.12.second_ref = bf16[1536,128]{1,0:T(8,128)(2,1)S(1)} collective-permute-done((bf16[1536,128]{1,0:T(8,128)(2,1)S(1)}, bf16[1536,128]{1,0:T(8,128)(2,1)S(1)}, u32[]{:S(2)}, u32[]{:S(2)}) %collective-permute-start.12) | collective-permute-done | bytes 393248 | tf_op jit(solution)/shard_map/ppermute | solution.py:48
  176.4 1.3 convolution_add_fusion
  177.8 1.6 collective-permute-start.13
  179.6 2.6 %collective-permute-done.13.got_ref = f32[128,128]{1,0:T(8,128)S(1)} collective-permute-done((f32[128,128]{1,0:T(8,128)S(1)}, f32[128,128]{1,0:T(8,128)S(1)}, u32[]{:S(2)}, u32[]{:S(2)}) %collective-permute-start.13) | collective-permute-done | bytes 65568 | tf_op jit(solution)/shard_map/ppermute | solution.py:422
  182.1 0.9 shard_map.76
  183.1 3.4 %all-to-all-start.3 = ((bf16[8,32,512]{2,1,0:T(8,128)(2,1)}), bf16[8,32,512]{2,1,0:T(8,128)(2,1)S(1)}, u32[]{:S(2)}, u32[]{:S(2)}) async-start(bf16[8,32,512]{2,1,0:T(8,128)(2,1)} %bitcast.18), calls=%async_computation.3 | async-start | bytes 524288 | tf_op jit(solution)/shard_map/all_to_all | solution.py:427
  186.9 1.5 add_add_fusion.partial_ref
  188.4 4.1 %all-to-all-done.3 = bf16[8,32,512]{2,1,0:T(8,128)(2,1)S(1)} async-done(((bf16[8,32,512]{2,1,0:T(8,128)(2,1)}), bf16[8,32,512]{2,1,0:T(8,128)(2,1)S(1)}, u32[]{:S(2)}, u32[]{:S(2)}) %all-to-all-start.3) | async-done | bytes 262176 | tf_op jit(solution)/shard_map/all_to_all | solution.py:427
  192.5 1.1 shard_map.77
  (92 shorter events, 9.6 us)
Async XLA Ops:
  2.8 2.2 %copy-start.2 = (bf16[4096,512]{1,0:T(8,128)(2,1)S(1)}, bf16[4096,512]{1,0:T(8,128)(2,1)}, u32[]{:S(2)}) copy-start(bf16[4096,512]{1,0:T(8,128)(2,1)} %store_ref.1) | copy-start | bytes 12582916
  5.0 1.0 copy-start.4
  6.0 15.9 %copy-start = (bf16[4,128,4096]{2,1,0:T(8,128)(2,1)S(1)}, bf16[4,128,4096]{2,1,0:T(8,128)(2,1)}, u32[]{:S(2)}) copy-start(bf16[4,128,4096]{2,1,0:T(8,128)(2,1)} %param.7) | copy-start | bytes 12582916
  15.7 5.0 %copy-start.3 = (bf16[4608,512]{1,0:T(8,128)(2,1)}, bf16[4608,512]{1,0:T(8,128)(2,1)S(1)}, u32[]{:S(2)}) copy-start(bf16[4608,512]{1,0:T(8,128)(2,1)S(1)} %get-tuple-element.73) | copy-start | bytes 14155780
  15.7 5.1 %copy-start.13 = (s32[4,128]{1,0:T(4,128)S(1)}, s32[4,128]{1,0:T(4,128)}, u32[]{:S(2)}) copy-start(s32[4,128]{1,0:T(4,128)} %param.12) | copy-start | bytes 6148
  15.7 5.2 %copy-start.14 = (s32[128]{0:T(128)S(1)}, s32[128]{0:T(128)}, u32[]{:S(2)}) copy-start(s32[128]{0:T(128)} %param.11) | copy-start | bytes 1540
  15.7 5.0 %collective-permute-start = (bf16[1536,512]{1,0:T(8,128)(2,1)S(1)}, bf16[1536,512]{1,0:T(8,128)(2,1)S(1)}, u32[]{:S(2)}, u32[]{:S(2)}) collective-permute-start(bf16[1536,512]{1,0:T(8,128)(2,1)S(1)} %get-tuple-element.51), channel_id=1, source_target_pairs={{0,1},{1,0},{2,3},{3,2},{4,5},{5,4},{6,7},{7,6},{8,9},{9,8},{10,11... | collective-permute-start | bytes 4718600 | tf_op jit(solution)/shard_map/ppermute | solution.py:48
  16.2 58.9 %collective-permute-start.2 = (bf16[3072,512]{1,0:T(8,128)(2,1)}, bf16[3072,512]{1,0:T(8,128)(2,1)}, u32[]{:S(2)}, u32[]{:S(2)}) collective-permute-start(bf16[3072,512]{1,0:T(8,128)(2,1)} %get-tuple-element.53), channel_id=1, source_target_pairs={{0,1},{1,0},{2,3},{3,2},{4,5},{5,4},{6,7},{7,6},{8,9},{9,8},{10,11... | collective-permute-start | bytes 9437192 | tf_op jit(solution)/shard_map/ppermute | solution.py:48
  20.7 1.2 copy-start.8
  25.2 58.4 %all-to-all-start = ((bf16[8,32,4096]{2,1,0:T(8,128)(2,1)}), bf16[8,32,4096]{2,1,0:T(8,128)(2,1)S(1)}, u32[]{:S(2)}, u32[]{:S(2)}) async-start(bf16[8,32,4096]{2,1,0:T(8,128)(2,1)} %bitcast.6), calls=%async_computation | async-start | bytes 4194304 | tf_op jit(solution)/shard_map/all_to_all | solution.py:334
  30.4 42.5 %collective-permute-start.1 = (bf16[1536,256]{1,0:T(8,128)(2,1)S(1)}, bf16[1536,256]{1,0:T(8,128)(2,1)S(1)}, u32[]{:S(2)}, u32[]{:S(2)}) collective-permute-start(bf16[1536,256]{1,0:T(8,128)(2,1)S(1)} %slice_add_fusion), channel_id=1, source_target_pairs={{0,2},{2,0},{1,3},{3,1},{4,6},{6,4},{5,7},{7,5},{8,10},{10,8},{9,1... | collective-permute-start | bytes 2359304 | tf_op jit(solution)/shard_map/ppermute | solution.py:48
  72.9 0.9 copy-start.10
  77.4 26.6 %collective-permute-start.3 = (bf16[1536,256]{1,0:T(8,128)(2,1)}, bf16[1536,256]{1,0:T(8,128)(2,1)}, u32[]{:S(2)}, u32[]{:S(2)}) collective-permute-start(bf16[1536,256]{1,0:T(8,128)(2,1)} %slice_add_fusion.2), channel_id=1, source_target_pairs={{0,2},{2,0},{1,3},{3,1},{4,6},{6,4},{5,7},{7,5},{8,10},{10,8},{9,1... | collective-permute-start | bytes 2359304 | tf_op jit(solution)/shard_map/ppermute | solution.py:48
  77.8 22.6 %collective-permute-start.4 = (bf16[1536,128]{1,0:T(8,128)(2,1)S(1)}, bf16[1536,128]{1,0:T(8,128)(2,1)}, u32[]{:S(2)}, u32[]{:S(2)}) collective-permute-start(bf16[1536,128]{1,0:T(8,128)(2,1)S(1)} %fusion.13), channel_id=1, source_target_pairs={{0,4},{4,0},{1,5},{5,1},{2,6},{6,2},{3,7},{7,3},{8,12},{12,8},{9,1... | collective-permute-start | bytes 1179656 | tf_op jit(solution)/shard_map/ppermute | solution.py:48
  83.6 4.6 %copy-start.6 = (bf16[8,32,4096]{2,1,0:T(8,128)(2,1)}, bf16[8,32,4096]{2,1,0:T(8,128)(2,1)S(1)}, u32[]{:S(2)}) copy-start(bf16[8,32,4096]{2,1,0:T(8,128)(2,1)S(1)} %all-to-all-done) | copy-start | bytes 6291460
  83.6 30.1 %all-to-all-start.1 = ((bf16[16,8,4224]{2,1,0:T(8,128)(2,1)}), bf16[16,8,4224]{2,1,0:T(8,128)(2,1)}, u32[]{:S(2)}, u32[]{:S(2)}) async-start(bf16[16,8,4224]{2,1,0:T(8,128)(2,1)} %maximum_bitcast_fusion), calls=%async_computation.1 | async-start | bytes 2162688 | tf_op jit(solution)/shard_map/all_to_all | solution.py:343
  88.2 2.2 %copy-start.1 = (bf16[4,128,4096]{2,1,0:T(8,128)(2,1)S(1)}, bf16[4,128,4096]{2,1,0:T(8,128)(2,1)}, u32[]{:S(2)}) copy-start(bf16[4,128,4096]{2,1,0:T(8,128)(2,1)} %param.7) | copy-start | bytes 12582916
  100.3 6.0 %copy-start.11 = (bf16[1536,256]{1,0:T(8,128)(2,1)S(1)}, bf16[1536,256]{1,0:T(8,128)(2,1)}, u32[]{:S(2)}) copy-start(bf16[1536,256]{1,0:T(8,128)(2,1)} %copy-done.10) | copy-start | bytes 2359300
  106.3 25.9 %collective-permute-start.5 = (bf16[1536,256]{1,0:T(8,128)(2,1)}, bf16[1536,256]{1,0:T(8,128)(2,1)}, u32[]{:S(2)}, u32[]{:S(2)}) collective-permute-start(bf16[1536,256]{1,0:T(8,128)(2,1)} %slice_add_fusion.1), channel_id=1, source_target_pairs={{0,2},{2,0},{1,3},{3,1},{4,6},{6,4},{5,7},{7,5},{8,10},{10,8},{9,1... | collective-permute-start | bytes 2359304 | tf_op jit(solution)/shard_map/ppermute | solution.py:48
  109.7 16.5 %collective-permute-start.6 = (bf16[1536,128]{1,0:T(8,128)(2,1)S(1)}, bf16[1536,128]{1,0:T(8,128)(2,1)}, u32[]{:S(2)}, u32[]{:S(2)}) collective-permute-start(bf16[1536,128]{1,0:T(8,128)(2,1)S(1)} %slice_add_fusion.6), channel_id=1, source_target_pairs={{0,4},{4,0},{1,5},{5,1},{2,6},{6,2},{3,7},{7,3},{8,12},{12,8},{9,1... | collective-permute-start | bytes 1179656 | tf_op jit(solution)/shard_map/ppermute | solution.py:48
  109.8 22.4 %collective-permute-start.7 = (bf16[1536,128]{1,0:T(8,128)(2,1)}, bf16[1536,128]{1,0:T(8,128)(2,1)}, u32[]{:S(2)}, u32[]{:S(2)}) collective-permute-start(bf16[1536,128]{1,0:T(8,128)(2,1)} %fusion.12), channel_id=1, source_target_pairs={{0,8},{8,0},{1,9},{9,1},{2,10},{10,2},{3,11},{11,3},{4,12},{12,4},... | collective-permute-start | bytes 1179656 | tf_op jit(solution)/shard_map/ppermute | solution.py:48
  112.2 36.4 %collective-permute-start.11 = (f32[512,512]{1,0:T(8,128)S(1)}, f32[512,512]{1,0:T(8,128)S(1)}, u32[]{:S(2)}, u32[]{:S(2)}) collective-permute-start(f32[512,512]{1,0:T(8,128)S(1)} %get-tuple-element.78), channel_id=1, source_target_pairs={{0,16},{16,0},{1,17},{17,1},{2,18},{18,2},{3,19},{19,3},{4,20},{20... | collective-permute-start | bytes 3145736 | tf_op jit(solution)/shard_map/ppermute | solution.py:48
  134.9 17.9 %collective-permute-start.8 = (bf16[1536,128]{1,0:T(8,128)(2,1)S(1)}, bf16[1536,128]{1,0:T(8,128)(2,1)S(1)}, u32[]{:S(2)}, u32[]{:S(2)}) collective-permute-start(bf16[1536,128]{1,0:T(8,128)(2,1)S(1)} %slice_add_fusion.5), channel_id=1, source_target_pairs={{0,4},{4,0},{1,5},{5,1},{2,6},{6,2},{3,7},{7,3},{8,12},{12,8},{9,1... | collective-permute-start | bytes 1179656 | tf_op jit(solution)/shard_map/ppermute | solution.py:48
  135.0 20.1 %collective-permute-start.9 = (bf16[1536,128]{1,0:T(8,128)(2,1)S(1)}, bf16[1536,128]{1,0:T(8,128)(2,1)S(1)}, u32[]{:S(2)}, u32[]{:S(2)}) collective-permute-start(bf16[1536,128]{1,0:T(8,128)(2,1)S(1)} %add_add_fusion.2), channel_id=1, source_target_pairs={{0,8},{8,0},{1,9},{9,1},{2,10},{10,2},{3,11},{11,3},{4,12},{12,4},... | collective-permute-start | bytes 1179656 | tf_op jit(solution)/shard_map/ppermute | solution.py:48
  137.8 5.0 %copy-start.7 = (bf16[8,32,4096]{2,1,0:T(8,128)(2,1)S(1)}, bf16[8,32,4096]{2,1,0:T(8,128)(2,1)}, u32[]{:S(2)}) copy-start(bf16[8,32,4096]{2,1,0:T(8,128)(2,1)} %copy-done.6) | copy-start | bytes 6291460
  141.2 7.4 %collective-permute-start.10 = (f32[128,512]{1,0:T(8,128)S(1)}, f32[128,512]{1,0:T(8,128)S(1)}, u32[]{:S(2)}, u32[]{:S(2)}) collective-permute-start(f32[128,512]{1,0:T(8,128)S(1)} %convolution_select_fusion), channel_id=1, source_target_pairs={{0,16},{16,0},{1,17},{17,1},{2,18},{18,2},{3,19},{19,3},{4,20},{20... | collective-permute-start | bytes 786440 | tf_op jit(solution)/shard_map/ppermute | solution.py:31
  145.5 12.0 %copy-start.5 = (bf16[512,512]{1,0:T(8,128)(2,1)S(1)}, bf16[512,512]{1,0:T(8,128)(2,1)}, u32[]{:S(2)}) copy-start(bf16[512,512]{1,0:T(8,128)(2,1)} %expand_ref.1) | copy-start | bytes 1572868
  148.6 17.9 %copy-start.9 = (f32[512,512]{1,0:T(8,128)}, f32[512,512]{1,0:T(8,128)S(1)}, u32[]{:S(2)}) copy-start(f32[512,512]{1,0:T(8,128)S(1)} %collective-permute-done.11) | copy-start | bytes 3145732
  155.1 0.7 copy-start.12
  157.2 19.2 %collective-permute-start.12 = (bf16[1536,128]{1,0:T(8,128)(2,1)S(1)}, bf16[1536,128]{1,0:T(8,128)(2,1)S(1)}, u32[]{:S(2)}, u32[]{:S(2)}) collective-permute-start(bf16[1536,128]{1,0:T(8,128)(2,1)S(1)} %add_add_fusion.1.first_ref), channel_id=1, source_target_pairs={{0,8},{8,0},{1,9},{9,1},{2,10},{10,2},{3,11},{11,3},{4,12},{12,4},... | collective-permute-start | bytes 1179656 | tf_op jit(solution)/shard_map/ppermute | solution.py:48
  158.4 19.4 %copy-start.15 = (pred[128]{0:T(512)(128)(4,1)S(1)}, pred[128]{0:T(512)(128)(4,1)}, u32[]{:S(2)}) copy-start(pred[128]{0:T(512)(128)(4,1)} %get-tuple-element.122) | copy-start | bytes 388
  158.4 24.7 %all-to-all-start.2 = ((bf16[16,8,512]{2,1,0:T(8,128)(2,1)}), bf16[16,8,512]{2,1,0:T(8,128)(2,1)S(1)}, u32[]{:S(2)}, u32[]{:S(2)}) async-start(bf16[16,8,512]{2,1,0:T(8,128)(2,1)} %fusion), calls=%async_computation.2 | async-start | bytes 262144 | tf_op jit(solution)/shard_map/all_to_all | solution.py:374
  177.8 4.3 %collective-permute-start.13 = (f32[128,128]{1,0:T(8,128)S(1)}, f32[128,128]{1,0:T(8,128)S(1)}, u32[]{:S(2)}, u32[]{:S(2)}) collective-permute-start(f32[128,128]{1,0:T(8,128)S(1)} %fusion.21.own_ref), channel_id=1, source_target_pairs={{0,16},{16,0},{1,17},{17,1},{2,18},{18,2},{3,19},{19,3},{4,20},{20... | collective-permute-start | bytes 196616 | tf_op jit(solution)/shard_map/ppermute | solution.py:422
  183.1 9.4 %all-to-all-start.3 = ((bf16[8,32,512]{2,1,0:T(8,128)(2,1)}), bf16[8,32,512]{2,1,0:T(8,128)(2,1)S(1)}, u32[]{:S(2)}, u32[]{:S(2)}) async-start(bf16[8,32,512]{2,1,0:T(8,128)(2,1)} %bitcast.18), calls=%async_computation.3 | async-start | bytes 524288 | tf_op jit(solution)/shard_map/all_to_all | solution.py:427

commit v11 on v10

--- a/solution.py
+++ b/solution.py
@@ -264,54 +264,6 @@
     names = jnp.arange(adapter_count, dtype=jnp.int32)
     chain = Chain()
 
-    hot_row = jnp.sum(jnp.where(hot_ids[:, :, None] == names, adapter_row, 0), axis=-1)
-    hot_first = jnp.where(hot_row // per_dev == me, (hot_row % per_dev) * R, -R * per_dev)
-    column = jnp.arange(per_dev * R, dtype=jnp.int32)
-    lane = jnp.arange(R, dtype=jnp.int32)
-    entry = jnp.arange(hot_count, dtype=jnp.int32)
-
-    def wanted(core):
-        firsts = []
-        for x in (x_at, 1 - x_at):
-            of_steps = jnp.sum(jnp.where(entry == 2 * x + core, hot_first, 0), axis=1)
-            firsts += [jnp.where(z_at == 0, of_steps[:near], of_steps[near:])]
-            firsts += [jnp.where(z_at == 0, of_steps[near:], of_steps[:near])]
-        return jnp.stack([(f[:, None] + lane).reshape(-1) for f in firsts])
-
-    want_mine, want_other = wanted(core_at), wanted(1 - core_at)
-    kept = near * R
-    chunk_count = 3
-    part = (depth + head_part) // chunk_count
-
-    hops = [("x", SWAP), ("z_low", SWAP)]
-    bit = 1
-    while bit < far_count:
-        hops.append(("z_high", [(i, i ^ bit) for i in range(far_count)]))
-        bit *= 2
-    mine, swapped, got, held = {}, {}, {}, {}
-
-    def operand(c, stage):
-        if stage == 0:
-            return mine[c][:, 2 * kept:] + swapped[c][:, 2 * kept:]
-        if stage == 1:
-            return mine[c][:, kept:2 * kept] + swapped[c][:, kept:2 * kept] + got[c, 0][:, kept:]
-        if stage == 2:
-            held[c] = mine[c][:, :kept] + swapped[c][:, :kept] + got[c, 0][:, :kept] + got[c, 1]
-        else:
-            held[c] = held[c] + got[c, stage - 1]
-        return held[c]
-
-    def send(c, stage):
-        got[c, stage] = chain.permute(operand(c, stage), *hops[stage])
-
-    mine_all, other_first, other_rest = pick_columns(
-        shrink_store, expand_store, want_mine, want_other
-    )
-    mine[0], swapped[0] = mine_all[:part], chain.permute(other_first, "core", SWAP)
-    rest_swapped = chain.permute(other_rest, "core", SWAP)
-    send(0, 0)
-
-    token_adapter = after(token_adapter, chain.last)
     cold_row = jnp.sum(jnp.where((token_adapter - hot_count)[:, :, None] == names, adapter_row, 0), axis=-1)
     is_hot = token_adapter < hot_count
     is_cold = (token_adapter < none_code) & jnp.logical_not(is_hot)
@@ -329,9 +281,56 @@
     hot_target = jnp.where(is_hot, hot_target, -1).reshape(-1)
     cold_target = jnp.where(is_cold, cold_target, -1).reshape(-1)
 
-    hot_out = place_rows(rows, after(hot_target, chain.last), hot_rows)
+    hot_out = place_rows(rows, hot_target, hot_rows)
     hot_out = chain.hold(hot_out.reshape(group_count, near * HCAP, depth))
     done = {"hot_in": lax.all_to_all(hot_out, GROUP, split_axis=0, concat_axis=0, tiled=True)}
+
+    hot_row = jnp.sum(jnp.where(hot_ids[:, :, None] == names, adapter_row, 0), axis=-1)
+    hot_first = jnp.where(hot_row // per_dev == me, (hot_row % per_dev) * R, -R * per_dev)
+    column = jnp.arange(per_dev * R, dtype=jnp.int32)
+    lane = jnp.arange(R, dtype=jnp.int32)
+    entry = jnp.arange(hot_count, dtype=jnp.int32)
+
+    def wanted(core):
+        firsts = []
+        for x in (x_at, 1 - x_at):
+            of_steps = jnp.sum(jnp.where(entry == 2 * x + core, hot_first, 0), axis=1)
+            firsts += [jnp.where(z_at == 0, of_steps[:near], of_steps[near:])]
+            firsts += [jnp.where(z_at == 0, of_steps[near:], of_steps[:near])]
+        return jnp.stack([(f[:, None] + lane).reshape(-1) for f in firsts])
+
+    want_mine, want_other = wanted(core_at), wanted(1 - core_at)
+    kept = near * R
+    chunk_count = 3
+    part = (depth + head_part) // chunk_count
+
+    hops = [("x", SWAP), ("z_low", SWAP)]
+    bit = 1
+    while bit < far_count:
+        hops.append(("z_high", [(i, i ^ bit) for i in range(far_count)]))
+        bit *= 2
+    mine, swapped, got, held = {}, {}, {}, {}
+
+    def operand(c, stage):
+        if stage == 0:
+            return mine[c][:, 2 * kept:] + swapped[c][:, 2 * kept:]
+        if stage == 1:
+            return mine[c][:, kept:2 * kept] + swapped[c][:, kept:2 * kept] + got[c, 0][:, kept:]
+        if stage == 2:
+            held[c] = mine[c][:, :kept] + swapped[c][:, :kept] + got[c, 0][:, :kept] + got[c, 1]
+        else:
+            held[c] = held[c] + got[c, stage - 1]
+        return held[c]
+
+    def send(c, stage):
+        got[c, stage] = chain.permute(operand(c, stage), *hops[stage])
+
+    mine_all, other_first, other_rest = pick_columns(
+        after(shrink_store, chain.last), expand_store, want_mine, want_other
+    )
+    mine[0], swapped[0] = mine_all[:part], chain.permute(other_first, "core", SWAP)
+    rest_swapped = chain.permute(other_rest, "core", SWAP)
+    send(0, 0)
 
     def cold_tokens_out():
         cold_at = after(cold_target, chain.last)
@@ -382,12 +381,12 @@
         done["partial"] = partial + done["base_own"] + done["base_got"]
 
     between = {
-        1: [cold_tokens_out, base_product],
+        0: [cold_tokens_out, base_product],
         2: [base_over_tp],
         3: [cold_shrink, cold_over_tp],
         4: [cold_expand, cold_back, all_but_hot],
     }
-    awaited = {1: ["hot_in", "base_own", "base_other"], 2: ["packet"], 3: ["z_cold", "base_got"]}
+    awaited = {0: ["base_own", "base_other"], 2: ["packet"], 3: ["z_cold", "base_got"]}
     for slot in range(chunk_count + len(hops) - 1):
         if slot > 0:
             if slot < chunk_count:

time: 196 us -> 192 us (0.980)
  waiting for transfers between devices: 92.8 us -> 85.1 us
  starting transfers between devices: 31.9 us -> 39.4 us
  matrix products: 14.8 us -> 12.7 us
  other arithmetic: 20.3 us -> 22.4 us
    ppermute x12, waiting for transfers between devices: 83.4 us -> 77.9 us  [permute(): return lax.ppermute(self.hold(value), axis, pairs)]
    all_to_all x1, starting transfers between devices: 4.56 us -> 9.5 us  [cold_tokens_out(): packet = lax.all_to_all(packet, DP, split_axis=0, concat_axis=0, tiled=True)]
    ppermute x12, starting transfers between devices: 10.4 us -> 14.9 us  [permute(): return lax.ppermute(self.hold(value), axis, pairs)]
    ppermute x1, waiting for transfers between devices: 2.68 us -> 0.43 us  [sum_over_tp(): return part + lax.ppermute(part, 'tp', SWAP)]
    pallas_call x1, Pallas kernels: 9.65 us -> 7.43 us  [pick_columns(): pl.pallas_call(kernel, grid_spec=pltpu.PrefetchScalarGridSpec(num_scalar_...]
    dot_general x9, matrix products: 14.5 us -> 12.3 us  [matmul(): return jnp.dot(a, b, preferred_element_type=jnp.float32)]
    unnamed x32 -> x22, local copies, waits for them, and re-layouts: 7.61 us -> 6.09 us
  transfers between devices with their start and end apart: 18 -> 18, of which waited for: 11 -> 13; matrix products, arithmetic and copies ran while one was open for 17% -> 15% of each run, Pallas kernels for 7% -> 6%
where the time goes in v11:
time: 192 us; the launch traced here: 190 us
  waiting for transfers between devices  85.1 us (44%)
  starting transfers between devices  39.4 us (21%)
  Pallas kernels  23.6 us (12%)
  other arithmetic  22.4 us (12%)
  matrix products  12.7 us (7%)
  local copies, waits for them, and re-layouts  7 us (4%)
    ppermute x12, waiting for transfers between devices, permute(): return lax.ppermute(self.hold(value), axis, pairs)  77.9 us
    ppermute x12, starting transfers between devices, permute(): return lax.ppermute(self.hold(value), axis, pairs)  14.9 us
    dot_general x9, matrix products, matmul(): return jnp.dot(a, b, preferred_element_type=jnp.float32)  12.3 us
    pallas_call x1, Pallas kernels, base_halves(): pl.pallas_call(kernel, grid_spec=pltpu.PrefetchScalarGridSpec(num_scalar_...  10.9 us
    all_to_all x1, starting transfers between devices, cold_tokens_out(): packet = lax.all_to_all(packet, DP, split_axis=0, concat_axis=0, tiled=True)  9.5 us
    pallas_call x1, Pallas kernels, pick_columns(): pl.pallas_call(kernel, grid_spec=pltpu.PrefetchScalarGridSpec(num_scalar_...  7.43 us
    unnamed x22, local copies, waits for them, and re-layouts  6.09 us
    add x3, other arithmetic, operand(): mine[c][:, :kept] + swapped[c][:, :kept] + got[c, 0][:, :kept] + got[c, 1]  4.76 us
  transfers between devices with their start and end apart: 18, of which 13 were waited for; matrix products, arithmetic and copies ran while one was open for 15% of the time, Pallas kernels for 6%

profile of v11, /device:TPU:0, one launch (start us, length us, event | category | flops | bytes accessed | tf_op | source)
XLA Modules:
  0.0 190.5 jit_solution(684470711118201082)
XLA Ops:
  6.2 2.2 %copy-done = bf16[4,128,4096]{2,1,0:T(8,128)(2,1)S(1)} copy-done((bf16[4,128,4096]{2,1,0:T(8,128)(2,1)S(1)}, bf16[4,128,4096]{2,1,0:T(8,128)(2,1)}, u32[]{:S(2)}) %copy-start) | copy-done | bytes 4194328
  8.4 3.3 %shard_map.73 = bf16[256,4096]{1,0:T(8,128)(2,1)} custom-call(s32[1,512]{1,0:T(1,128)S(1)} %bitcast.50, bf16[512,4096]{1,0:T(8,128)(2,1)S(1)} %bitcast.46), custom_call_target="tpu_custom_call" | custom-call | flops 1073741824 | bytes 6291456 | tf_op jit(solution)/shard_map/pallas_call | solution.py:151
  11.6 7.4 %shard_map.74 = (bf16[4608,512]{1,0:T(8,128)(2,1)S(1)}, bf16[1536,512]{1,0:T(8,128)(2,1)S(1)}, bf16[3072,512]{1,0:T(8,128)(2,1)}) custom-call(s32[4]{0:T(128)S(1)} %convert_element_type.29.mine_held, s32[4]{0:T(128)S(1)} %convert_element_type.30.other_held, s32[1,512]{1,0:T(1,128)S(1)} %bitcast.53, s32[1,512]{1,0:T(1,128)S(1)} %bitcast.52, ...), custom_call_target="tpu_custom_call" | custom-call | flops 1 | bytes 1 | tf_op jit(solution)/shard_map/pallas_call | solution.py:108
  19.6 4.6 %collective-permute-done = bf16[1536,512]{1,0:T(8,128)(2,1)S(1)} collective-permute-done((bf16[1536,512]{1,0:T(8,128)(2,1)S(1)}, bf16[1536,512]{1,0:T(8,128)(2,1)S(1)}, u32[]{:S(2)}, u32[]{:S(2)}) %collective-permute-start) | collective-permute-done | bytes 1572896 | tf_op jit(solution)/shard_map/ppermute | solution.py:48
  26.2 1.1 maximum_bitcast_fusion
  27.3 9.5 %all-to-all-start = ((bf16[16,8,4224]{2,1,0:T(8,128)(2,1)}), bf16[16,8,4224]{2,1,0:T(8,128)(2,1)}, u32[]{:S(2)}, u32[]{:S(2)}) async-start(bf16[16,8,4224]{2,1,0:T(8,128)(2,1)} %maximum_bitcast_fusion), calls=%async_computation | async-start | bytes 2162688 | tf_op jit(solution)/shard_map/all_to_all | solution.py:342
  36.8 1.9 collective-permute-start.1
  38.7 2.2 %copy-done.2 = bf16[4,128,4096]{2,1,0:T(8,128)(2,1)S(1)} copy-done((bf16[4,128,4096]{2,1,0:T(8,128)(2,1)S(1)}, bf16[4,128,4096]{2,1,0:T(8,128)(2,1)}, u32[]{:S(2)}) %copy-start.2) | copy-done | bytes 4194328
  40.8 10.9 %shard_map.75 = (f32[512,512]{1,0:T(8,128)S(1)}, f32[512,512]{1,0:T(8,128)}) custom-call(s32[1]{0:T(128)} %bitcast.8.tp_at, bf16[512,4096]{1,0:T(8,128)(2,1)S(1)} %bitcast.48, bf16[4096,1024]{1,0:T(8,128)(2,1)} %weight_ref), custom_call_target="tpu_custom_call" | custom-call | flops 1 | bytes 1 | tf_op jit(solution)/shard_map/pallas_call | solution.py:189
  51.7 16.7 %collective-permute-done.1 = bf16[1536,256]{1,0:T(8,128)(2,1)} collective-permute-done((bf16[1536,256]{1,0:T(8,128)(2,1)S(1)}, bf16[1536,256]{1,0:T(8,128)(2,1)}, u32[]{:S(2)}, u32[]{:S(2)}) %collective-permute-start.1) | collective-permute-done | bytes 786464 | tf_op jit(solution)/shard_map/ppermute | solution.py:48
  68.4 1.5 slice_add_fusion.2
  70.3 1.3 fusion.13
  71.6 1.7 collective-permute-start.4
  73.3 4.5 %all-to-all-start.2 = ((bf16[8,32,4096]{2,1,0:T(8,128)(2,1)}), bf16[8,32,4096]{2,1,0:T(8,128)(2,1)}, u32[]{:S(2)}, u32[]{:S(2)}) async-start(bf16[8,32,4096]{2,1,0:T(8,128)(2,1)} %bitcast.5), calls=%async_computation.2 | async-start | bytes 4194304 | tf_op jit(solution)/shard_map/all_to_all | solution.py:286
  77.9 5.8 %collective-permute-done.4 = bf16[1536,128]{1,0:T(8,128)(2,1)S(1)} collective-permute-done((bf16[1536,128]{1,0:T(8,128)(2,1)S(1)}, bf16[1536,128]{1,0:T(8,128)(2,1)S(1)}, u32[]{:S(2)}, u32[]{:S(2)}) %collective-permute-start.4) | collective-permute-done | bytes 393248 | tf_op jit(solution)/shard_map/ppermute | solution.py:48
  83.7 18.0 %collective-permute-done.3 = bf16[1536,256]{1,0:T(8,128)(2,1)} collective-permute-done((bf16[1536,256]{1,0:T(8,128)(2,1)S(1)}, bf16[1536,256]{1,0:T(8,128)(2,1)}, u32[]{:S(2)}, u32[]{:S(2)}) %collective-permute-start.3) | collective-permute-done | bytes 786464 | tf_op jit(solution)/shard_map/ppermute | solution.py:48
  101.7 1.5 slice_add_fusion.1
  103.6 1.3 fusion.12
  104.9 1.5 slice_add_fusion.6
  106.4 1.8 collective-permute-start.6
  108.1 2.4 %collective-permute-start.7 = (bf16[1536,128]{1,0:T(8,128)(2,1)S(1)}, bf16[1536,128]{1,0:T(8,128)(2,1)S(1)}, u32[]{:S(2)}, u32[]{:S(2)}) collective-permute-start(bf16[1536,128]{1,0:T(8,128)(2,1)S(1)} %fusion.12), channel_id=1, source_target_pairs={{0,8},{8,0},{1,9},{9,1},{2,10},{10,2},{3,11},{11,3},{4,12},{12,4},... | collective-permute-start | bytes 1179656 | tf_op jit(solution)/shard_map/ppermute | solution.py:48
  110.5 1.6 collective-permute-start.11
  112.1 11.2 %collective-permute-done.6 = bf16[1536,128]{1,0:T(8,128)(2,1)S(1)} collective-permute-done((bf16[1536,128]{1,0:T(8,128)(2,1)S(1)}, bf16[1536,128]{1,0:T(8,128)(2,1)S(1)}, u32[]{:S(2)}, u32[]{:S(2)}) %collective-permute-start.6) | collective-permute-done | bytes 393248 | tf_op jit(solution)/shard_map/ppermute | solution.py:48
  123.3 2.1 %collective-permute-done.7 = bf16[1536,128]{1,0:T(8,128)(2,1)S(1)} collective-permute-done((bf16[1536,128]{1,0:T(8,128)(2,1)S(1)}, bf16[1536,128]{1,0:T(8,128)(2,1)S(1)}, u32[]{:S(2)}, u32[]{:S(2)}) %collective-permute-start.7) | collective-permute-done | bytes 393248 | tf_op jit(solution)/shard_map/ppermute | solution.py:48
  125.3 3.0 %collective-permute-done.5 = bf16[1536,256]{1,0:T(8,128)(2,1)S(1)} collective-permute-done((bf16[1536,256]{1,0:T(8,128)(2,1)S(1)}, bf16[1536,256]{1,0:T(8,128)(2,1)S(1)}, u32[]{:S(2)}, u32[]{:S(2)}) %collective-permute-start.5) | collective-permute-done | bytes 786464 | tf_op jit(solution)/shard_map/ppermute | solution.py:48
  128.3 2.1 %add_add_fusion.2 = bf16[1536,128]{1,0:T(8,128)(2,1)} fusion(bf16[1536,128]{1,0:T(8,128)(2,1)S(1)} %collective-permute-done.6, bf16[1536,256]{1,0:T(8,128)(2,1)} %collective-permute-done.3, bf16[3072,512]{1,0:T(8,128)(2,1)} %collective-permute-done.2, bf16[4608,512]{1,0:T(8,128)(2,1)} %copy-done.5), kind=kLoop, calls=%fused_computation.29 | loop fusion | flops 589824 | bytes 1966080 | tf_op jit(solution)/shard_map/add | solution.py:320
  130.5 1.9 %slice_add_fusion.5 = bf16[1536,128]{1,0:T(8,128)(2,1)} fusion(bf16[1536,256]{1,0:T(8,128)(2,1)S(1)} %collective-permute-done.5, bf16[3072,512]{1,0:T(8,128)(2,1)} %collective-permute-done.2, bf16[4608,512]{1,0:T(8,128)(2,1)} %copy-done.5), kind=kLoop, calls=%fused_computation.30 | loop fusion | flops 393216 | bytes 1572864 | tf_op jit(solution)/shard_map/add | solution.py:318
  132.4 1.5 collective-permute-start.8
  133.9 2.4 %collective-permute-start.9 = (bf16[1536,128]{1,0:T(8,128)(2,1)}, bf16[1536,128]{1,0:T(8,128)(2,1)S(1)}, u32[]{:S(2)}, u32[]{:S(2)}) collective-permute-start(bf16[1536,128]{1,0:T(8,128)(2,1)} %add_add_fusion.2), channel_id=1, source_target_pairs={{0,8},{8,0},{1,9},{9,1},{2,10},{10,2},{3,11},{11,3},{4,12},{12,4},... | collective-permute-start | bytes 1179656 | tf_op jit(solution)/shard_map/ppermute | solution.py:48
  137.1 1.9 %convolution_select_fusion = f32[128,512]{1,0:T(8,128)S(1)} fusion(bf16[4096,512]{1,0:T(8,128)(2,1)S(1)} %copy-done.4, bf16[128,4224]{1,0:T(8,128)(2,1)} %bitcast.9, s32[512]{0:T(512)S(1)} %fusion.23, s32[128]{0:T(128)S(1)} %convert_reduce_fusion.1), kind=kOutput, calls=%fused_computation.1 | convolution fusion | flops 537001984 | bytes 5507584 | tf_op jit(solution)/shard_map/dot_general | solution.py:22
  139.0 1.6 collective-permute-start.10
  140.6 1.6 fusion.5
  142.2 1.5 convolution_add_fusion.3
  143.7 1.6 convolution_add_fusion.2
  146.7 4.1 %collective-permute-done.8 = bf16[1536,128]{1,0:T(8,128)(2,1)} collective-permute-done((bf16[1536,128]{1,0:T(8,128)(2,1)}, bf16[1536,128]{1,0:T(8,128)(2,1)}, u32[]{:S(2)}, u32[]{:S(2)}) %collective-permute-start.8) | collective-permute-done | bytes 393248 | tf_op jit(solution)/shard_map/ppermute | solution.py:48
  150.8 2.2 %collective-permute-done.9 = bf16[1536,128]{1,0:T(8,128)(2,1)S(1)} collective-permute-done((bf16[1536,128]{1,0:T(8,128)(2,1)}, bf16[1536,128]{1,0:T(8,128)(2,1)S(1)}, u32[]{:S(2)}, u32[]{:S(2)}) %collective-permute-start.9) | collective-permute-done | bytes 393248 | tf_op jit(solution)/shard_map/ppermute | solution.py:48
  153.8 1.3 add_add_fusion.1.first_ref
  156.4 4.0 %all-to-all-start.1 = ((bf16[16,8,512]{2,1,0:T(8,128)(2,1)}), bf16[16,8,512]{2,1,0:T(8,128)(2,1)S(1)}, u32[]{:S(2)}, u32[]{:S(2)}) async-start(bf16[16,8,512]{2,1,0:T(8,128)(2,1)} %fusion), calls=%async_computation.1 | async-start | bytes 262144 | tf_op jit(solution)/shard_map/all_to_all | solution.py:373
  160.4 1.3 fusion.9
  161.7 1.5 fusion.1
  163.2 10.1 %collective-permute-done.12.second_ref = bf16[1536,128]{1,0:T(8,128)(2,1)S(1)} collective-permute-done((bf16[1536,128]{1,0:T(8,128)(2,1)S(1)}, bf16[1536,128]{1,0:T(8,128)(2,1)S(1)}, u32[]{:S(2)}, u32[]{:S(2)}) %collective-permute-start.12) | collective-permute-done | bytes 393248 | tf_op jit(solution)/shard_map/ppermute | solution.py:48
  173.3 1.3 convolution_add_fusion
  174.7 1.6 collective-permute-start.13
  176.4 2.6 %collective-permute-done.13.got_ref = f32[128,128]{1,0:T(8,128)S(1)} collective-permute-done((f32[128,128]{1,0:T(8,128)S(1)}, f32[128,128]{1,0:T(8,128)S(1)}, u32[]{:S(2)}, u32[]{:S(2)}) %collective-permute-start.13) | collective-permute-done | bytes 65568 | tf_op jit(solution)/shard_map/ppermute | solution.py:421
  179.9 3.4 %all-to-all-start.3 = ((bf16[8,32,512]{2,1,0:T(8,128)(2,1)}), bf16[8,32,512]{2,1,0:T(8,128)(2,1)S(1)}, u32[]{:S(2)}, u32[]{:S(2)}) async-start(bf16[8,32,512]{2,1,0:T(8,128)(2,1)} %bitcast.17), calls=%async_computation.3 | async-start | bytes 524288 | tf_op jit(solution)/shard_map/all_to_all | solution.py:426
  183.7 1.5 add_add_fusion.partial_ref
  185.2 4.1 %all-to-all-done.3 = bf16[8,32,512]{2,1,0:T(8,128)(2,1)S(1)} async-done(((bf16[8,32,512]{2,1,0:T(8,128)(2,1)}), bf16[8,32,512]{2,1,0:T(8,128)(2,1)S(1)}, u32[]{:S(2)}, u32[]{:S(2)}) %all-to-all-start.3) | async-done | bytes 262176 | tf_op jit(solution)/shard_map/all_to_all | solution.py:426
  189.3 1.1 shard_map.77
  (82 shorter events, 15.2 us)
Async XLA Ops:
  6.2 2.2 %copy-start = (bf16[4,128,4096]{2,1,0:T(8,128)(2,1)S(1)}, bf16[4,128,4096]{2,1,0:T(8,128)(2,1)}, u32[]{:S(2)}) copy-start(bf16[4,128,4096]{2,1,0:T(8,128)(2,1)} %param.7) | copy-start | bytes 12582916
  8.3 3.3 %copy-start.3 = (bf16[4096,512]{1,0:T(8,128)(2,1)S(1)}, bf16[4096,512]{1,0:T(8,128)(2,1)}, u32[]{:S(2)}) copy-start(bf16[4096,512]{1,0:T(8,128)(2,1)} %store_ref) | copy-start | bytes 12582916
  8.4 3.3 %copy-start.6 = (bf16[512,512]{1,0:T(8,128)(2,1)S(1)}, bf16[512,512]{1,0:T(8,128)(2,1)}, u32[]{:S(2)}) copy-start(bf16[512,512]{1,0:T(8,128)(2,1)} %expand_ref.1) | copy-start | bytes 1572868
  11.6 13.7 %copy-start.1 = (bf16[4,128,4096]{2,1,0:T(8,128)(2,1)S(1)}, bf16[4,128,4096]{2,1,0:T(8,128)(2,1)}, u32[]{:S(2)}) copy-start(bf16[4,128,4096]{2,1,0:T(8,128)(2,1)} %param.7) | copy-start | bytes 12582916
  19.1 7.0 %copy-start.5 = (bf16[4608,512]{1,0:T(8,128)(2,1)}, bf16[4608,512]{1,0:T(8,128)(2,1)S(1)}, u32[]{:S(2)}) copy-start(bf16[4608,512]{1,0:T(8,128)(2,1)S(1)} %get-tuple-element.70) | copy-start | bytes 14155780
  19.1 5.1 %collective-permute-start = (bf16[1536,512]{1,0:T(8,128)(2,1)S(1)}, bf16[1536,512]{1,0:T(8,128)(2,1)S(1)}, u32[]{:S(2)}, u32[]{:S(2)}) collective-permute-start(bf16[1536,512]{1,0:T(8,128)(2,1)S(1)} %get-tuple-element.51), channel_id=1, source_target_pairs={{0,1},{1,0},{2,3},{3,2},{4,5},{5,4},{6,7},{7,6},{8,9},{9,8},{10,11... | collective-permute-start | bytes 4718600 | tf_op jit(solution)/shard_map/ppermute | solution.py:48
  19.5 48.9 %collective-permute-start.2 = (bf16[3072,512]{1,0:T(8,128)(2,1)}, bf16[3072,512]{1,0:T(8,128)(2,1)}, u32[]{:S(2)}, u32[]{:S(2)}) collective-permute-start(bf16[3072,512]{1,0:T(8,128)(2,1)} %get-tuple-element.53), channel_id=1, source_target_pairs={{0,1},{1,0},{2,3},{3,2},{4,5},{5,4},{6,7},{7,6},{8,9},{9,8},{10,11... | collective-permute-start | bytes 9437192 | tf_op jit(solution)/shard_map/ppermute | solution.py:48
  24.2 1.2 copy-start.7
  27.3 46.1 %all-to-all-start = ((bf16[16,8,4224]{2,1,0:T(8,128)(2,1)}), bf16[16,8,4224]{2,1,0:T(8,128)(2,1)}, u32[]{:S(2)}, u32[]{:S(2)}) async-start(bf16[16,8,4224]{2,1,0:T(8,128)(2,1)} %maximum_bitcast_fusion), calls=%async_computation | async-start | bytes 2162688 | tf_op jit(solution)/shard_map/all_to_all | solution.py:342
  36.8 31.6 %collective-permute-start.1 = (bf16[1536,256]{1,0:T(8,128)(2,1)S(1)}, bf16[1536,256]{1,0:T(8,128)(2,1)}, u32[]{:S(2)}, u32[]{:S(2)}) collective-permute-start(bf16[1536,256]{1,0:T(8,128)(2,1)S(1)} %slice_add_fusion), channel_id=1, source_target_pairs={{0,2},{2,0},{1,3},{3,1},{4,6},{6,4},{5,7},{7,5},{8,10},{10,8},{9,1... | collective-permute-start | bytes 2359304 | tf_op jit(solution)/shard_map/ppermute | solution.py:48
  38.7 2.2 %copy-start.2 = (bf16[4,128,4096]{2,1,0:T(8,128)(2,1)S(1)}, bf16[4,128,4096]{2,1,0:T(8,128)(2,1)}, u32[]{:S(2)}) copy-start(bf16[4,128,4096]{2,1,0:T(8,128)(2,1)} %param.7) | copy-start | bytes 12582916
  69.9 31.9 %collective-permute-start.3 = (bf16[1536,256]{1,0:T(8,128)(2,1)S(1)}, bf16[1536,256]{1,0:T(8,128)(2,1)}, u32[]{:S(2)}, u32[]{:S(2)}) collective-permute-start(bf16[1536,256]{1,0:T(8,128)(2,1)S(1)} %slice_add_fusion.2), channel_id=1, source_target_pairs={{0,2},{2,0},{1,3},{3,1},{4,6},{6,4},{5,7},{7,5},{8,10},{10,8},{9,1... | collective-permute-start | bytes 2359304 | tf_op jit(solution)/shard_map/ppermute | solution.py:48
  71.6 12.1 %collective-permute-start.4 = (bf16[1536,128]{1,0:T(8,128)(2,1)S(1)}, bf16[1536,128]{1,0:T(8,128)(2,1)S(1)}, u32[]{:S(2)}, u32[]{:S(2)}) collective-permute-start(bf16[1536,128]{1,0:T(8,128)(2,1)S(1)} %fusion.13), channel_id=1, source_target_pairs={{0,4},{4,0},{1,5},{5,1},{2,6},{6,2},{3,7},{7,3},{8,12},{12,8},{9,1... | collective-permute-start | bytes 1179656 | tf_op jit(solution)/shard_map/ppermute | solution.py:48
  73.3 67.3 %all-to-all-start.2 = ((bf16[8,32,4096]{2,1,0:T(8,128)(2,1)}), bf16[8,32,4096]{2,1,0:T(8,128)(2,1)}, u32[]{:S(2)}, u32[]{:S(2)}) async-start(bf16[8,32,4096]{2,1,0:T(8,128)(2,1)} %bitcast.5), calls=%async_computation.2 | async-start | bytes 4194304 | tf_op jit(solution)/shard_map/all_to_all | solution.py:286
  103.2 25.2 %collective-permute-start.5 = (bf16[1536,256]{1,0:T(8,128)(2,1)S(1)}, bf16[1536,256]{1,0:T(8,128)(2,1)S(1)}, u32[]{:S(2)}, u32[]{:S(2)}) collective-permute-start(bf16[1536,256]{1,0:T(8,128)(2,1)S(1)} %slice_add_fusion.1), channel_id=1, source_target_pairs={{0,2},{2,0},{1,3},{3,1},{4,6},{6,4},{5,7},{7,5},{8,10},{10,8},{9,1... | collective-permute-start | bytes 2359304 | tf_op jit(solution)/shard_map/ppermute | solution.py:48
  104.9 32.2 %copy-start.4 = (bf16[4096,512]{1,0:T(8,128)(2,1)S(1)}, bf16[4096,512]{1,0:T(8,128)(2,1)}, u32[]{:S(2)}) copy-start(bf16[4096,512]{1,0:T(8,128)(2,1)} %store_ref) | copy-start | bytes 12582916
  106.4 16.9 %collective-permute-start.6 = (bf16[1536,128]{1,0:T(8,128)(2,1)S(1)}, bf16[1536,128]{1,0:T(8,128)(2,1)S(1)}, u32[]{:S(2)}, u32[]{:S(2)}) collective-permute-start(bf16[1536,128]{1,0:T(8,128)(2,1)S(1)} %slice_add_fusion.6), channel_id=1, source_target_pairs={{0,4},{4,0},{1,5},{5,1},{2,6},{6,2},{3,7},{7,3},{8,12},{12,8},{9,1... | collective-permute-start | bytes 1179656 | tf_op jit(solution)/shard_map/ppermute | solution.py:48
  108.1 17.2 %collective-permute-start.7 = (bf16[1536,128]{1,0:T(8,128)(2,1)S(1)}, bf16[1536,128]{1,0:T(8,128)(2,1)S(1)}, u32[]{:S(2)}, u32[]{:S(2)}) collective-permute-start(bf16[1536,128]{1,0:T(8,128)(2,1)S(1)} %fusion.12), channel_id=1, source_target_pairs={{0,8},{8,0},{1,9},{9,1},{2,10},{10,2},{3,11},{11,3},{4,12},{12,4},... | collective-permute-start | bytes 1179656 | tf_op jit(solution)/shard_map/ppermute | solution.py:48
  110.5 36.2 %collective-permute-start.11 = (f32[512,512]{1,0:T(8,128)}, f32[512,512]{1,0:T(8,128)}, u32[]{:S(2)}, u32[]{:S(2)}) collective-permute-start(f32[512,512]{1,0:T(8,128)} %get-tuple-element.75), channel_id=1, source_target_pairs={{0,16},{16,0},{1,17},{17,1},{2,18},{18,2},{3,19},{19,3},{4,20},{20... | collective-permute-start | bytes 3145736 | tf_op jit(solution)/shard_map/ppermute | solution.py:48
  125.3 3.0 %copy-start.10 = (bf16[1536,128]{1,0:T(8,128)(2,1)}, bf16[1536,128]{1,0:T(8,128)(2,1)S(1)}, u32[]{:S(2)}) copy-start(bf16[1536,128]{1,0:T(8,128)(2,1)S(1)} %collective-permute-done.7) | copy-start | bytes 1179652
  132.4 18.4 %collective-permute-start.8 = (bf16[1536,128]{1,0:T(8,128)(2,1)}, bf16[1536,128]{1,0:T(8,128)(2,1)}, u32[]{:S(2)}, u32[]{:S(2)}) collective-permute-start(bf16[1536,128]{1,0:T(8,128)(2,1)} %slice_add_fusion.5), channel_id=1, source_target_pairs={{0,4},{4,0},{1,5},{5,1},{2,6},{6,2},{3,7},{7,3},{8,12},{12,8},{9,1... | collective-permute-start | bytes 1179656 | tf_op jit(solution)/shard_map/ppermute | solution.py:48
  133.9 19.2 %collective-permute-start.9 = (bf16[1536,128]{1,0:T(8,128)(2,1)}, bf16[1536,128]{1,0:T(8,128)(2,1)S(1)}, u32[]{:S(2)}, u32[]{:S(2)}) collective-permute-start(bf16[1536,128]{1,0:T(8,128)(2,1)} %add_add_fusion.2), channel_id=1, source_target_pairs={{0,8},{8,0},{1,9},{9,1},{2,10},{10,2},{3,11},{11,3},{4,12},{12,4},... | collective-permute-start | bytes 1179656 | tf_op jit(solution)/shard_map/ppermute | solution.py:48
  139.0 6.7 %collective-permute-start.10 = (f32[128,512]{1,0:T(8,128)S(1)}, f32[128,512]{1,0:T(8,128)}, u32[]{:S(2)}, u32[]{:S(2)}) collective-permute-start(f32[128,512]{1,0:T(8,128)S(1)} %convolution_select_fusion), channel_id=1, source_target_pairs={{0,16},{16,0},{1,17},{17,1},{2,18},{18,2},{3,19},{19,3},{4,20},{20... | collective-permute-start | bytes 786440 | tf_op jit(solution)/shard_map/ppermute | solution.py:31
  153.0 0.7 copy-start.8
  155.1 6.6 %copy-start.9 = (bf16[1536,128]{1,0:T(8,128)(2,1)S(1)}, bf16[1536,128]{1,0:T(8,128)(2,1)}, u32[]{:S(2)}) copy-start(bf16[1536,128]{1,0:T(8,128)(2,1)} %copy-done.8) | copy-start | bytes 1179652
  155.1 18.2 %collective-permute-start.12 = (bf16[1536,128]{1,0:T(8,128)(2,1)S(1)}, bf16[1536,128]{1,0:T(8,128)(2,1)S(1)}, u32[]{:S(2)}, u32[]{:S(2)}) collective-permute-start(bf16[1536,128]{1,0:T(8,128)(2,1)S(1)} %add_add_fusion.1.first_ref), channel_id=1, source_target_pairs={{0,8},{8,0},{1,9},{9,1},{2,10},{10,2},{3,11},{11,3},{4,12},{12,4},... | collective-permute-start | bytes 1179656 | tf_op jit(solution)/shard_map/ppermute | solution.py:48
  156.4 23.6 %all-to-all-start.1 = ((bf16[16,8,512]{2,1,0:T(8,128)(2,1)}), bf16[16,8,512]{2,1,0:T(8,128)(2,1)S(1)}, u32[]{:S(2)}, u32[]{:S(2)}) async-start(bf16[16,8,512]{2,1,0:T(8,128)(2,1)} %fusion), calls=%async_computation.1 | async-start | bytes 262144 | tf_op jit(solution)/shard_map/all_to_all | solution.py:373
  174.7 4.3 %collective-permute-start.13 = (f32[128,128]{1,0:T(8,128)S(1)}, f32[128,128]{1,0:T(8,128)S(1)}, u32[]{:S(2)}, u32[]{:S(2)}) collective-permute-start(f32[128,128]{1,0:T(8,128)S(1)} %fusion.21.own_ref), channel_id=1, source_target_pairs={{0,16},{16,0},{1,17},{17,1},{2,18},{18,2},{3,19},{19,3},{4,20},{20... | collective-permute-start | bytes 196616 | tf_op jit(solution)/shard_map/ppermute | solution.py:421
  179.9 9.4 %all-to-all-start.3 = ((bf16[8,32,512]{2,1,0:T(8,128)(2,1)}), bf16[8,32,512]{2,1,0:T(8,128)(2,1)S(1)}, u32[]{:S(2)}, u32[]{:S(2)}) async-start(bf16[8,32,512]{2,1,0:T(8,128)(2,1)} %bitcast.17), calls=%async_computation.3 | async-start | bytes 524288 | tf_op jit(solution)/shard_map/all_to_all | solution.py:426

commit v12 on v11

--- a/solution.py
+++ b/solution.py
@@ -51,10 +51,10 @@
         self.last = after(self.last, *arrived)
 
 
-def kernel_params(flops=1, bytes_accessed=1):
+def kernel_params():
     return dict(
         compiler_params=pltpu.CompilerParams(vmem_limit_bytes=40 * 2**20),
-        cost_estimate=pl.CostEstimate(flops=flops, bytes_accessed=bytes_accessed, transcendentals=0),
+        cost_estimate=pl.CostEstimate(flops=1, bytes_accessed=1, transcendentals=0),
     )
 
 
@@ -140,22 +140,38 @@
     blocks = 4
     width = depth // blocks
 
-    def kernel(target_at, rows_ref, out_ref, place):
-        @pl.when(pl.program_id(0) == 0)
+    def kernel(target_at, rows_ref, early_ref, late_ref, place):
+        step = pl.program_id(0)
+
+        @pl.when(step == 0)
         def _():
             hit = lax.broadcasted_iota(jnp.int32, (placed_rows, count), 0) == target_at[...]
             place[...] = hit.astype(jnp.float32).astype(jnp.bfloat16)
 
-        out_ref[...] = narrow(place[...], rows_ref[...])
+        placed = narrow(place[...], rows_ref[...])
+
+        @pl.when(step < blocks - 1)
+        def _():
+            early_ref[...] = placed
+
+        @pl.when(step == blocks - 1)
+        def _():
+            late_ref[...] = placed
 
     return pl.pallas_call(
         kernel,
         grid=(blocks,),
         in_specs=[pl.BlockSpec((1, count), lambda j: (0, 0)), pl.BlockSpec((count, width), lambda j: (0, j))],
-        out_specs=pl.BlockSpec((placed_rows, width), lambda j: (0, j)),
-        out_shape=jax.ShapeDtypeStruct((placed_rows, depth), jnp.bfloat16),
+        out_specs=[
+            pl.BlockSpec((placed_rows, width), lambda j: (0, jnp.minimum(j, blocks - 2))),
+            pl.BlockSpec((placed_rows, width), lambda j: (0, 0)),
+        ],
+        out_shape=[
+            jax.ShapeDtypeStruct((placed_rows, depth - width), jnp.bfloat16),
+            jax.ShapeDtypeStruct((placed_rows, width), jnp.bfloat16),
+        ],
         scratch_shapes=[pltpu.VMEM((placed_rows, count), jnp.bfloat16)],
-        **kernel_params(2 * placed_rows * count * depth, 2 * (placed_rows + count) * depth),
+        **kernel_params(),
     )(target[None], rows)
 
 
@@ -281,9 +297,14 @@
     hot_target = jnp.where(is_hot, hot_target, -1).reshape(-1)
     cold_target = jnp.where(is_cold, cold_target, -1).reshape(-1)
 
-    hot_out = place_rows(rows, hot_target, hot_rows)
-    hot_out = chain.hold(hot_out.reshape(group_count, near * HCAP, depth))
-    done = {"hot_in": lax.all_to_all(hot_out, GROUP, split_axis=0, concat_axis=0, tiled=True)}
+    early = 3 * depth // 4
+
+    def exchange(block):
+        block = chain.hold(block.reshape(group_count, near * HCAP, -1))
+        return lax.all_to_all(block, GROUP, split_axis=0, concat_axis=0, tiled=True).reshape(hot_rows, -1)
+
+    hot_first_part, hot_last_part = place_rows(rows, hot_target, hot_rows)
+    hot_early = exchange(hot_first_part)
 
     hot_row = jnp.sum(jnp.where(hot_ids[:, :, None] == names, adapter_row, 0), axis=-1)
     hot_first = jnp.where(hot_row // per_dev == me, (hot_row % per_dev) * R, -R * per_dev)
@@ -330,7 +351,9 @@
     )
     mine[0], swapped[0] = mine_all[:part], chain.permute(other_first, "core", SWAP)
     rest_swapped = chain.permute(other_rest, "core", SWAP)
-    send(0, 0)
+    first, hot_early = lax.optimization_barrier((operand(0, 0), hot_early))
+    got[0, 0] = chain.permute(first, *hops[0])
+    done = {"hot_late": exchange(hot_last_part)}
 
     def cold_tokens_out():
         cold_at = after(cold_target, chain.last)
@@ -381,12 +404,12 @@
         done["partial"] = partial + done["base_own"] + done["base_got"]
 
     between = {
-        0: [cold_tokens_out, base_product],
+        1: [cold_tokens_out, base_product],
         2: [base_over_tp],
         3: [cold_shrink, cold_over_tp],
         4: [cold_expand, cold_back, all_but_hot],
     }
-    awaited = {0: ["base_own", "base_other"], 2: ["packet"], 3: ["z_cold", "base_got"]}
+    awaited = {1: ["hot_late", "base_own", "base_other"], 2: ["packet"], 3: ["z_cold", "base_got"]}
     for slot in range(chunk_count + len(hops) - 1):
         if slot > 0:
             if slot < chunk_count:
@@ -407,12 +430,12 @@
         done.update(zip(names_here, arrived[1 + len(here):]))
     partial = done["partial"]
 
-    hot_in = done["hot_in"].reshape(hot_rows, depth)
     dense = None
     for c in range(chunk_count):
         last = min((c + 1) * part, depth)
+        hot_in = hot_early[:, c * part:last] if last <= early else done["hot_late"]
         for piece in (held[c], got[c, len(hops) - 1]):
-            product = matmul(hot_in[:, c * part:last], piece[:last - c * part])
+            product = matmul(hot_in, piece[:last - c * part])
             dense = product if dense is None else dense + product
     dense = dense.reshape(group_count, near, HCAP, kept)
     at_step = jnp.arange(kept) // R

time: 192 us -> 183 us (0.953)
  waiting for transfers between devices: 85.1 us -> 71.6 us
  starting transfers between devices: 39.4 us -> 42.3 us
  local copies, waits for them, and re-layouts: 7 us -> 9.37 us
    ppermute x12, waiting for transfers between devices: 77.9 us -> 62.3 us  [permute(): return lax.ppermute(self.hold(value), axis, pairs)]
    all_to_all x1 -> x2, starting transfers between devices: 4.52 us -> 8.72 us  [exchange(): lax.all_to_all(block, GROUP, split_axis=0, concat_axis=0, tiled=True)]
    all_to_all x1, starting transfers between devices: 9.5 us -> 6.68 us  [cold_tokens_out(): packet = lax.all_to_all(packet, DP, split_axis=0, concat_axis=0, tiled=True)]
    unnamed x22 -> x26, local copies, waits for them, and re-layouts: 6.09 us -> 8.46 us
    ppermute x1, waiting for transfers between devices: 0.43 us -> 2.75 us  [sum_over_tp(): return part + lax.ppermute(part, 'tp', SWAP)]
  transfers between devices with their start and end apart: 18 -> 19, of which waited for: 13 -> 10; matrix products, arithmetic and copies ran while one was open for 15% -> 17% of each run, Pallas kernels for 6% -> 11%
where the time goes in v12:
time: 183 us; the launch traced here: 182 us
  waiting for transfers between devices  71.6 us (39%)
  starting transfers between devices  42.3 us (23%)
  Pallas kernels  24 us (13%)
  other arithmetic  20.9 us (11%)
  matrix products  13.9 us (8%)
  local copies, waits for them, and re-layouts  9.37 us (5%)
    ppermute x12, waiting for transfers between devices, permute(): return lax.ppermute(self.hold(value), axis, pairs)  62.3 us
    ppermute x12, starting transfers between devices, permute(): return lax.ppermute(self.hold(value), axis, pairs)  15.3 us
    dot_general x9, matrix products, matmul(): return jnp.dot(a, b, preferred_element_type=jnp.float32)  13.6 us
    pallas_call x1, Pallas kernels, base_halves(): pl.pallas_call(kernel, grid_spec=pltpu.PrefetchScalarGridSpec(num_scalar_...  10.9 us
    all_to_all x2, starting transfers between devices, exchange(): lax.all_to_all(block, GROUP, split_axis=0, concat_axis=0, tiled=True)  8.72 us
    unnamed x26, local copies, waits for them, and re-layouts  8.46 us
    pallas_call x1, Pallas kernels, pick_columns(): pl.pallas_call(kernel, grid_spec=pltpu.PrefetchScalarGridSpec(num_scalar_...  7.41 us
    all_to_all x1, starting transfers between devices, cold_tokens_out(): packet = lax.all_to_all(packet, DP, split_axis=0, concat_axis=0, tiled=True)  6.68 us
  transfers between devices with their start and end apart: 19, of which 10 were waited for; matrix products, arithmetic and copies ran while one was open for 17% of the time, Pallas kernels for 11%

profile of v12, /device:TPU:0, one launch (start us, length us, event | category | flops | bytes accessed | tf_op | source)
XLA Modules:
  0.0 182.4 jit_solution(16311085629292891910)
XLA Ops:
  3.3 2.2 %copy-done = bf16[4,128,4096]{2,1,0:T(8,128)(2,1)S(1)} copy-done((bf16[4,128,4096]{2,1,0:T(8,128)(2,1)S(1)}, bf16[4,128,4096]{2,1,0:T(8,128)(2,1)}, u32[]{:S(2)}) %copy-start) | copy-done | bytes 4194328
  5.5 3.6 %shard_map.73 = (bf16[256,3072]{1,0:T(8,128)(2,1)}, bf16[256,1024]{1,0:T(8,128)(2,1)}) custom-call(s32[1,512]{1,0:T(1,128)S(1)} %bitcast.54, bf16[512,4096]{1,0:T(8,128)(2,1)S(1)} %bitcast.51), custom_call_target="tpu_custom_call" | custom-call | flops 1 | bytes 1 | tf_op jit(solution)/shard_map/pallas_call | solution.py:161
  9.1 5.2 %all-to-all-start = ((bf16[8,32,3072]{2,1,0:T(8,128)(2,1)}), bf16[8,32,3072]{2,1,0:T(8,128)(2,1)}, u32[]{:S(2)}, u32[]{:S(2)}) async-start(bf16[8,32,3072]{2,1,0:T(8,128)(2,1)} %bitcast.5), calls=%async_computation | async-start | bytes 3145728 | tf_op jit(solution)/shard_map/all_to_all | solution.py:304
  16.5 2.2 %copy-done.2 = bf16[4096,512]{1,0:T(8,128)(2,1)S(1)} copy-done((bf16[4096,512]{1,0:T(8,128)(2,1)S(1)}, bf16[4096,512]{1,0:T(8,128)(2,1)}, u32[]{:S(2)}) %copy-start.2) | copy-done | bytes 4194328
  18.7 7.4 %shard_map.74 = (bf16[4608,512]{1,0:T(8,128)(2,1)S(1)}, bf16[1536,512]{1,0:T(8,128)(2,1)S(1)}, bf16[3072,512]{1,0:T(8,128)(2,1)}) custom-call(s32[4]{0:T(128)S(1)} %convert_element_type.29.mine_held, s32[4]{0:T(128)S(1)} %convert_element_type.30.other_held, s32[1,512]{1,0:T(1,128)S(1)} %bitcast.56, s32[1,512]{1,0:T(1,128)S(1)} %bitcast.57, ...), custom_call_target="tpu_custom_call" | custom-call | flops 1 | bytes 1 | tf_op jit(solution)/shard_map/pallas_call | solution.py:108
  26.6 7.4 %collective-permute-done = bf16[1536,512]{1,0:T(8,128)(2,1)S(1)} collective-permute-done((bf16[1536,512]{1,0:T(8,128)(2,1)S(1)}, bf16[1536,512]{1,0:T(8,128)(2,1)S(1)}, u32[]{:S(2)}, u32[]{:S(2)}) %collective-permute-start) | collective-permute-done | bytes 1572896 | tf_op jit(solution)/shard_map/ppermute | solution.py:48
  34.0 1.1 copy-done.5
  35.2 1.8 %collective-permute-start.1 = (bf16[1536,256]{1,0:T(8,128)(2,1)S(1)}, bf16[1536,256]{1,0:T(8,128)(2,1)S(1)}, u32[]{:S(2)}, u32[]{:S(2)}) collective-permute-start(bf16[1536,256]{1,0:T(8,128)(2,1)S(1)} %slice_add_fusion), channel_id=1, source_target_pairs={{0,2},{2,0},{1,3},{3,1},{4,6},{6,4},{5,7},{7,5},{8,10},{10,8},{9,1... | collective-permute-start | bytes 2359304 | tf_op jit(solution)/shard_map/ppermute | solution.py:48
  37.1 3.5 %all-to-all-start.1 = ((bf16[8,32,1024]{2,1,0:T(8,128)(2,1)}), bf16[8,32,1024]{2,1,0:T(8,128)(2,1)S(1)}, u32[]{:S(2)}, u32[]{:S(2)}) async-start(bf16[8,32,1024]{2,1,0:T(8,128)(2,1)} %bitcast.6), calls=%async_computation.1 | async-start | bytes 1048576 | tf_op jit(solution)/shard_map/all_to_all | solution.py:304
  40.6 17.9 %collective-permute-done.1 = bf16[1536,256]{1,0:T(8,128)(2,1)S(1)} collective-permute-done((bf16[1536,256]{1,0:T(8,128)(2,1)S(1)}, bf16[1536,256]{1,0:T(8,128)(2,1)S(1)}, u32[]{:S(2)}, u32[]{:S(2)}) %collective-permute-start.1) | collective-permute-done | bytes 786464 | tf_op jit(solution)/shard_map/ppermute | solution.py:48
  58.5 2.6 %slice_add_fusion.2 = bf16[1536,256]{1,0:T(8,128)(2,1)} fusion(bf16[3072,512]{1,0:T(8,128)(2,1)} %collective-permute-done.2, bf16[4608,512]{1,0:T(8,128)(2,1)} %copy-done.3), kind=kLoop, calls=%fused_computation.14 | loop fusion | flops 393216 | bytes 2359296 | tf_op jit(solution)/shard_map/add | solution.py:337
  61.1 1.8 collective-permute-start.3
  62.9 1.2 fusion.11
  64.0 1.4 collective-permute-start.4
  65.5 2.9 %convolution_convert_fusion = bf16[128,4096]{1,0:T(8,128)(2,1)S(1)} fusion(bf16[512,4096]{1,0:T(8,128)(2,1)} %bitcast.50, s32[512]{0:T(512)S(1)} %get-tuple-element.71), kind=kOutput, calls=%fused_computation | convolution fusion | flops 537460736 | bytes 5244928 | tf_op jit(solution)/shard_map/dot_general | solution.py:22
  69.7 6.7 %all-to-all-start.2 = ((bf16[16,8,4224]{2,1,0:T(8,128)(2,1)}), bf16[16,8,4224]{2,1,0:T(8,128)(2,1)}, u32[]{:S(2)}, u32[]{:S(2)}) async-start(bf16[16,8,4224]{2,1,0:T(8,128)(2,1)} %maximum_bitcast_fusion), calls=%async_computation.2 | async-start | bytes 2162688 | tf_op jit(solution)/shard_map/all_to_all | solution.py:365
  76.4 2.2 %copy-done.1 = bf16[4,128,4096]{2,1,0:T(8,128)(2,1)S(1)} copy-done((bf16[4,128,4096]{2,1,0:T(8,128)(2,1)S(1)}, bf16[4,128,4096]{2,1,0:T(8,128)(2,1)}, u32[]{:S(2)}) %copy-start.1) | copy-done | bytes 4194328
  78.6 10.9 %shard_map.75 = (f32[512,512]{1,0:T(8,128)S(1)}, f32[512,512]{1,0:T(8,128)}) custom-call(s32[1]{0:T(128)} %bitcast.11.tp_at, bf16[512,4096]{1,0:T(8,128)(2,1)S(1)} %bitcast.52, bf16[4096,1024]{1,0:T(8,128)(2,1)} %weight_ref), custom_call_target="tpu_custom_call" | custom-call | flops 1 | bytes 1 | tf_op jit(solution)/shard_map/pallas_call | solution.py:205
  89.5 1.5 slice_add_fusion.1
  90.9 1.9 %collective-permute-start.5 = (bf16[1536,256]{1,0:T(8,128)(2,1)S(1)}, bf16[1536,256]{1,0:T(8,128)(2,1)}, u32[]{:S(2)}, u32[]{:S(2)}) collective-permute-start(bf16[1536,256]{1,0:T(8,128)(2,1)S(1)} %slice_add_fusion.1), channel_id=1, source_target_pairs={{0,2},{2,0},{1,3},{3,1},{4,6},{6,4},{5,7},{7,5},{8,10},{10,8},{9,1... | collective-permute-start | bytes 2359304 | tf_op jit(solution)/shard_map/ppermute | solution.py:48
  92.9 1.2 fusion.10
  94.1 1.3 slice_add_fusion.6
  95.4 1.5 collective-permute-start.6
  97.0 2.4 %collective-permute-start.7 = (bf16[1536,128]{1,0:T(8,128)(2,1)S(1)}, bf16[1536,128]{1,0:T(8,128)(2,1)S(1)}, u32[]{:S(2)}, u32[]{:S(2)}) collective-permute-start(bf16[1536,128]{1,0:T(8,128)(2,1)S(1)} %fusion.10), channel_id=1, source_target_pairs={{0,8},{8,0},{1,9},{9,1},{2,10},{10,2},{3,11},{11,3},{4,12},{12,4},... | collective-permute-start | bytes 1179656 | tf_op jit(solution)/shard_map/ppermute | solution.py:48
  99.9 1.5 collective-permute-start.11
  101.5 12.1 %collective-permute-done.6 = bf16[1536,128]{1,0:T(8,128)(2,1)S(1)} collective-permute-done((bf16[1536,128]{1,0:T(8,128)(2,1)S(1)}, bf16[1536,128]{1,0:T(8,128)(2,1)S(1)}, u32[]{:S(2)}, u32[]{:S(2)}) %collective-permute-start.6) | collective-permute-done | bytes 393248 | tf_op jit(solution)/shard_map/ppermute | solution.py:48
  113.6 7.0 %collective-permute-done.7 = bf16[1536,128]{1,0:T(8,128)(2,1)S(1)} collective-permute-done((bf16[1536,128]{1,0:T(8,128)(2,1)S(1)}, bf16[1536,128]{1,0:T(8,128)(2,1)S(1)}, u32[]{:S(2)}, u32[]{:S(2)}) %collective-permute-start.7) | collective-permute-done | bytes 393248 | tf_op jit(solution)/shard_map/ppermute | solution.py:48
  121.3 1.3 add_add_fusion.2
  122.7 1.3 slice_add_fusion.5
  124.1 2.0 %collective-permute-start.9 = (bf16[1536,128]{1,0:T(8,128)(2,1)S(1)}, bf16[1536,128]{1,0:T(8,128)(2,1)S(1)}, u32[]{:S(2)}, u32[]{:S(2)}) collective-permute-start(bf16[1536,128]{1,0:T(8,128)(2,1)S(1)} %add_add_fusion.2), channel_id=1, source_target_pairs={{0,8},{8,0},{1,9},{9,1},{2,10},{10,2},{3,11},{11,3},{4,12},{12,4},... | collective-permute-start | bytes 1179656 | tf_op jit(solution)/shard_map/ppermute | solution.py:48
  126.9 3.2 %convolution_select_fusion = f32[128,512]{1,0:T(8,128)S(1)} fusion(bf16[4096,512]{1,0:T(8,128)(2,1)} %store_ref, bf16[128,4224]{1,0:T(8,128)(2,1)} %bitcast.12, s32[512]{0:T(512)S(1)} %fusion.23, s32[128]{0:T(128)S(1)} %convert_reduce_fusion.1), kind=kOutput, calls=%fused_computation.1 | convolution fusion | flops 537001984 | bytes 5507584 | tf_op jit(solution)/shard_map/dot_general | solution.py:22
  130.1 1.6 collective-permute-start.10
  131.7 1.5 fusion.6
  133.2 1.5 convolution_add_fusion.2
  134.7 2.8 %collective-permute-done.10 = f32[128,512]{1,0:T(8,128)S(1)} collective-permute-done((f32[128,512]{1,0:T(8,128)S(1)}, f32[128,512]{1,0:T(8,128)S(1)}, u32[]{:S(2)}, u32[]{:S(2)}) %collective-permute-start.10) | collective-permute-done | bytes 262176 | tf_op jit(solution)/shard_map/ppermute | solution.py:31
  137.5 4.3 %collective-permute-done.8 = bf16[1536,128]{1,0:T(8,128)(2,1)S(1)} collective-permute-done((bf16[1536,128]{1,0:T(8,128)(2,1)S(1)}, bf16[1536,128]{1,0:T(8,128)(2,1)S(1)}, u32[]{:S(2)}, u32[]{:S(2)}) %collective-permute-start.8) | collective-permute-done | bytes 393248 | tf_op jit(solution)/shard_map/ppermute | solution.py:48
  141.9 2.3 %collective-permute-done.9 = bf16[1536,128]{1,0:T(8,128)(2,1)S(1)} collective-permute-done((bf16[1536,128]{1,0:T(8,128)(2,1)S(1)}, bf16[1536,128]{1,0:T(8,128)(2,1)S(1)}, u32[]{:S(2)}, u32[]{:S(2)}) %collective-permute-start.9) | collective-permute-done | bytes 393248 | tf_op jit(solution)/shard_map/ppermute | solution.py:48
  144.1 1.3 add_add_fusion.1.first_ref
  145.8 1.5 convolution_add_fusion.1
  148.2 5.0 %all-to-all-start.3 = ((bf16[16,8,512]{2,1,0:T(8,128)(2,1)}), bf16[16,8,512]{2,1,0:T(8,128)(2,1)S(1)}, u32[]{:S(2)}, u32[]{:S(2)}) async-start(bf16[16,8,512]{2,1,0:T(8,128)(2,1)} %fusion), calls=%async_computation.3 | async-start | bytes 262144 | tf_op jit(solution)/shard_map/all_to_all | solution.py:396
  153.5 11.3 %collective-permute-done.12.second_ref = bf16[1536,128]{1,0:T(8,128)(2,1)S(1)} collective-permute-done((bf16[1536,128]{1,0:T(8,128)(2,1)S(1)}, bf16[1536,128]{1,0:T(8,128)(2,1)S(1)}, u32[]{:S(2)}, u32[]{:S(2)}) %collective-permute-start.12) | collective-permute-done | bytes 393248 | tf_op jit(solution)/shard_map/ppermute | solution.py:48
  165.1 1.5 fusion.2
  166.6 1.6 collective-permute-start.13
  168.4 2.6 %collective-permute-done.13.got_ref = f32[128,128]{1,0:T(8,128)S(1)} collective-permute-done((f32[128,128]{1,0:T(8,128)S(1)}, f32[128,128]{1,0:T(8,128)S(1)}, u32[]{:S(2)}, u32[]{:S(2)}) %collective-permute-start.13) | collective-permute-done | bytes 65568 | tf_op jit(solution)/shard_map/ppermute | solution.py:444
  171.9 3.4 %all-to-all-start.4 = ((bf16[8,32,512]{2,1,0:T(8,128)(2,1)}), bf16[8,32,512]{2,1,0:T(8,128)(2,1)S(1)}, u32[]{:S(2)}, u32[]{:S(2)}) async-start(bf16[8,32,512]{2,1,0:T(8,128)(2,1)} %bitcast.19), calls=%async_computation.4 | async-start | bytes 524288 | tf_op jit(solution)/shard_map/all_to_all | solution.py:449
  175.7 1.6 add_add_fusion.partial_ref
  177.3 4.0 %all-to-all-done.4 = bf16[8,32,512]{2,1,0:T(8,128)(2,1)S(1)} async-done(((bf16[8,32,512]{2,1,0:T(8,128)(2,1)}), bf16[8,32,512]{2,1,0:T(8,128)(2,1)S(1)}, u32[]{:S(2)}, u32[]{:S(2)}) %all-to-all-start.4) | async-done | bytes 262176 | tf_op jit(solution)/shard_map/all_to_all | solution.py:449
  181.3 1.1 shard_map.77
  (88 shorter events, 12.9 us)
Async XLA Ops:
  3.3 2.2 %copy-start = (bf16[4,128,4096]{2,1,0:T(8,128)(2,1)S(1)}, bf16[4,128,4096]{2,1,0:T(8,128)(2,1)}, u32[]{:S(2)}) copy-start(bf16[4,128,4096]{2,1,0:T(8,128)(2,1)} %param.7) | copy-start | bytes 12582916
  5.5 8.9 %copy-start.8 = (s32[128]{0:T(128)S(1)}, s32[128]{0:T(128)}, u32[]{:S(2)}) copy-start(s32[128]{0:T(128)} %param.11) | copy-start | bytes 1540
  5.5 8.9 %copy-start.9 = (s32[4,4]{1,0:T(4,128)S(1)}, s32[4,4]{1,0:T(4,128)}, u32[]{:S(2)}) copy-start(s32[4,4]{1,0:T(4,128)} %param.13) | copy-start | bytes 196
  5.5 10.9 %copy-start.4 = (bf16[512,512]{1,0:T(8,128)(2,1)S(1)}, bf16[512,512]{1,0:T(8,128)(2,1)}, u32[]{:S(2)}) copy-start(bf16[512,512]{1,0:T(8,128)(2,1)} %expand_ref.1) | copy-start | bytes 1572868
  9.1 26.1 %all-to-all-start = ((bf16[8,32,3072]{2,1,0:T(8,128)(2,1)}), bf16[8,32,3072]{2,1,0:T(8,128)(2,1)}, u32[]{:S(2)}, u32[]{:S(2)}) async-start(bf16[8,32,3072]{2,1,0:T(8,128)(2,1)} %bitcast.5), calls=%async_computation | async-start | bytes 3145728 | tf_op jit(solution)/shard_map/all_to_all | solution.py:304
  16.5 2.2 %copy-start.2 = (bf16[4096,512]{1,0:T(8,128)(2,1)S(1)}, bf16[4096,512]{1,0:T(8,128)(2,1)}, u32[]{:S(2)}) copy-start(bf16[4096,512]{1,0:T(8,128)(2,1)} %store_ref) | copy-start | bytes 12582916
  26.1 7.9 %copy-start.3 = (bf16[4608,512]{1,0:T(8,128)(2,1)}, bf16[4608,512]{1,0:T(8,128)(2,1)S(1)}, u32[]{:S(2)}) copy-start(bf16[4608,512]{1,0:T(8,128)(2,1)S(1)} %get-tuple-element.80) | copy-start | bytes 14155780
  26.1 32.4 %collective-permute-start.2 = (bf16[3072,512]{1,0:T(8,128)(2,1)}, bf16[3072,512]{1,0:T(8,128)(2,1)}, u32[]{:S(2)}, u32[]{:S(2)}) collective-permute-start(bf16[3072,512]{1,0:T(8,128)(2,1)} %get-tuple-element.62), channel_id=1, source_target_pairs={{0,1},{1,0},{2,3},{3,2},{4,5},{5,4},{6,7},{7,6},{8,9},{9,8},{10,11... | collective-permute-start | bytes 9437192 | tf_op jit(solution)/shard_map/ppermute | solution.py:48
  26.6 7.4 %collective-permute-start = (bf16[1536,512]{1,0:T(8,128)(2,1)S(1)}, bf16[1536,512]{1,0:T(8,128)(2,1)S(1)}, u32[]{:S(2)}, u32[]{:S(2)}) collective-permute-start(bf16[1536,512]{1,0:T(8,128)(2,1)S(1)} %get-tuple-element.58), channel_id=1, source_target_pairs={{0,1},{1,0},{2,3},{3,2},{4,5},{5,4},{6,7},{7,6},{8,9},{9,8},{10,11... | collective-permute-start | bytes 4718600 | tf_op jit(solution)/shard_map/ppermute | solution.py:48
  34.0 1.1 copy-start.5
  35.2 23.2 %collective-permute-start.1 = (bf16[1536,256]{1,0:T(8,128)(2,1)S(1)}, bf16[1536,256]{1,0:T(8,128)(2,1)S(1)}, u32[]{:S(2)}, u32[]{:S(2)}) collective-permute-start(bf16[1536,256]{1,0:T(8,128)(2,1)S(1)} %slice_add_fusion), channel_id=1, source_target_pairs={{0,2},{2,0},{1,3},{3,1},{4,6},{6,4},{5,7},{7,5},{8,10},{10,8},{9,1... | collective-permute-start | bytes 2359304 | tf_op jit(solution)/shard_map/ppermute | solution.py:48
  37.1 32.6 %all-to-all-start.1 = ((bf16[8,32,1024]{2,1,0:T(8,128)(2,1)}), bf16[8,32,1024]{2,1,0:T(8,128)(2,1)S(1)}, u32[]{:S(2)}, u32[]{:S(2)}) async-start(bf16[8,32,1024]{2,1,0:T(8,128)(2,1)} %bitcast.6), calls=%async_computation.1 | async-start | bytes 1048576 | tf_op jit(solution)/shard_map/all_to_all | solution.py:304
  58.5 7.0 %copy-start.6 = (bf16[1536,256]{1,0:T(8,128)(2,1)}, bf16[1536,256]{1,0:T(8,128)(2,1)S(1)}, u32[]{:S(2)}) copy-start(bf16[1536,256]{1,0:T(8,128)(2,1)S(1)} %collective-permute-done.1) | copy-start | bytes 2359300
  61.1 28.4 %collective-permute-start.3 = (bf16[1536,256]{1,0:T(8,128)(2,1)}, bf16[1536,256]{1,0:T(8,128)(2,1)}, u32[]{:S(2)}, u32[]{:S(2)}) collective-permute-start(bf16[1536,256]{1,0:T(8,128)(2,1)} %slice_add_fusion.2), channel_id=1, source_target_pairs={{0,2},{2,0},{1,3},{3,1},{4,6},{6,4},{5,7},{7,5},{8,10},{10,8},{9,1... | collective-permute-start | bytes 2359304 | tf_op jit(solution)/shard_map/ppermute | solution.py:48
  64.0 25.4 %collective-permute-start.4 = (bf16[1536,128]{1,0:T(8,128)(2,1)S(1)}, bf16[1536,128]{1,0:T(8,128)(2,1)S(1)}, u32[]{:S(2)}, u32[]{:S(2)}) collective-permute-start(bf16[1536,128]{1,0:T(8,128)(2,1)S(1)} %fusion.11), channel_id=1, source_target_pairs={{0,4},{4,0},{1,5},{5,1},{2,6},{6,2},{3,7},{7,3},{8,12},{12,8},{9,1... | collective-permute-start | bytes 1179656 | tf_op jit(solution)/shard_map/ppermute | solution.py:48
  69.7 51.6 %all-to-all-start.2 = ((bf16[16,8,4224]{2,1,0:T(8,128)(2,1)}), bf16[16,8,4224]{2,1,0:T(8,128)(2,1)}, u32[]{:S(2)}, u32[]{:S(2)}) async-start(bf16[16,8,4224]{2,1,0:T(8,128)(2,1)} %maximum_bitcast_fusion), calls=%async_computation.2 | async-start | bytes 2162688 | tf_op jit(solution)/shard_map/all_to_all | solution.py:365
  76.4 2.2 %copy-start.1 = (bf16[4,128,4096]{2,1,0:T(8,128)(2,1)S(1)}, bf16[4,128,4096]{2,1,0:T(8,128)(2,1)}, u32[]{:S(2)}) copy-start(bf16[4,128,4096]{2,1,0:T(8,128)(2,1)} %param.7) | copy-start | bytes 12582916
  78.6 14.3 %copy-start.7 = (bf16[1536,256]{1,0:T(8,128)(2,1)S(1)}, bf16[1536,256]{1,0:T(8,128)(2,1)}, u32[]{:S(2)}) copy-start(bf16[1536,256]{1,0:T(8,128)(2,1)} %copy-done.6) | copy-start | bytes 2359300
  90.9 30.4 %collective-permute-start.5 = (bf16[1536,256]{1,0:T(8,128)(2,1)S(1)}, bf16[1536,256]{1,0:T(8,128)(2,1)}, u32[]{:S(2)}, u32[]{:S(2)}) collective-permute-start(bf16[1536,256]{1,0:T(8,128)(2,1)S(1)} %slice_add_fusion.1), channel_id=1, source_target_pairs={{0,2},{2,0},{1,3},{3,1},{4,6},{6,4},{5,7},{7,5},{8,10},{10,8},{9,1... | collective-permute-start | bytes 2359304 | tf_op jit(solution)/shard_map/ppermute | solution.py:48
  95.4 18.1 %collective-permute-start.6 = (bf16[1536,128]{1,0:T(8,128)(2,1)S(1)}, bf16[1536,128]{1,0:T(8,128)(2,1)S(1)}, u32[]{:S(2)}, u32[]{:S(2)}) collective-permute-start(bf16[1536,128]{1,0:T(8,128)(2,1)S(1)} %slice_add_fusion.6), channel_id=1, source_target_pairs={{0,4},{4,0},{1,5},{5,1},{2,6},{6,2},{3,7},{7,3},{8,12},{12,8},{9,1... | collective-permute-start | bytes 1179656 | tf_op jit(solution)/shard_map/ppermute | solution.py:48
  97.0 23.6 %collective-permute-start.7 = (bf16[1536,128]{1,0:T(8,128)(2,1)S(1)}, bf16[1536,128]{1,0:T(8,128)(2,1)S(1)}, u32[]{:S(2)}, u32[]{:S(2)}) collective-permute-start(bf16[1536,128]{1,0:T(8,128)(2,1)S(1)} %fusion.10), channel_id=1, source_target_pairs={{0,8},{8,0},{1,9},{9,1},{2,10},{10,2},{3,11},{11,3},{4,12},{12,4},... | collective-permute-start | bytes 1179656 | tf_op jit(solution)/shard_map/ppermute | solution.py:48
  99.9 37.6 %collective-permute-start.11 = (f32[512,512]{1,0:T(8,128)}, f32[512,512]{1,0:T(8,128)}, u32[]{:S(2)}, u32[]{:S(2)}) collective-permute-start(f32[512,512]{1,0:T(8,128)} %get-tuple-element.85), channel_id=1, source_target_pairs={{0,16},{16,0},{1,17},{17,1},{2,18},{18,2},{3,19},{19,3},{4,20},{20... | collective-permute-start | bytes 3145736 | tf_op jit(solution)/shard_map/ppermute | solution.py:48
  120.6 0.7 copy-start.11
  124.0 7.8 %copy-start.12 = (bf16[1536,128]{1,0:T(8,128)(2,1)S(1)}, bf16[1536,128]{1,0:T(8,128)(2,1)}, u32[]{:S(2)}) copy-start(bf16[1536,128]{1,0:T(8,128)(2,1)} %copy-done.11) | copy-start | bytes 1179652
  124.0 17.9 %collective-permute-start.8 = (bf16[1536,128]{1,0:T(8,128)(2,1)S(1)}, bf16[1536,128]{1,0:T(8,128)(2,1)S(1)}, u32[]{:S(2)}, u32[]{:S(2)}) collective-permute-start(bf16[1536,128]{1,0:T(8,128)(2,1)S(1)} %slice_add_fusion.5), channel_id=1, source_target_pairs={{0,4},{4,0},{1,5},{5,1},{2,6},{6,2},{3,7},{7,3},{8,12},{12,8},{9,1... | collective-permute-start | bytes 1179656 | tf_op jit(solution)/shard_map/ppermute | solution.py:48
  124.1 20.1 %collective-permute-start.9 = (bf16[1536,128]{1,0:T(8,128)(2,1)S(1)}, bf16[1536,128]{1,0:T(8,128)(2,1)S(1)}, u32[]{:S(2)}, u32[]{:S(2)}) collective-permute-start(bf16[1536,128]{1,0:T(8,128)(2,1)S(1)} %add_add_fusion.2), channel_id=1, source_target_pairs={{0,8},{8,0},{1,9},{9,1},{2,10},{10,2},{3,11},{11,3},{4,12},{12,4},... | collective-permute-start | bytes 1179656 | tf_op jit(solution)/shard_map/ppermute | solution.py:48
  130.1 7.3 %collective-permute-start.10 = (f32[128,512]{1,0:T(8,128)S(1)}, f32[128,512]{1,0:T(8,128)S(1)}, u32[]{:S(2)}, u32[]{:S(2)}) collective-permute-start(f32[128,512]{1,0:T(8,128)S(1)} %convolution_select_fusion), channel_id=1, source_target_pairs={{0,16},{16,0},{1,17},{17,1},{2,18},{18,2},{3,19},{19,3},{4,20},{20... | collective-permute-start | bytes 786440 | tf_op jit(solution)/shard_map/ppermute | solution.py:31
  145.5 21.1 %copy-start.10 = (pred[128]{0:T(512)(128)(4,1)S(1)}, pred[128]{0:T(512)(128)(4,1)}, u32[]{:S(2)}) copy-start(pred[128]{0:T(512)(128)(4,1)} %get-tuple-element.130) | copy-start | bytes 388
  145.5 19.3 %collective-permute-start.12 = (bf16[1536,128]{1,0:T(8,128)(2,1)S(1)}, bf16[1536,128]{1,0:T(8,128)(2,1)S(1)}, u32[]{:S(2)}, u32[]{:S(2)}) collective-permute-start(bf16[1536,128]{1,0:T(8,128)(2,1)S(1)} %add_add_fusion.1.first_ref), channel_id=1, source_target_pairs={{0,8},{8,0},{1,9},{9,1},{2,10},{10,2},{3,11},{11,3},{4,12},{12,4},... | collective-permute-start | bytes 1179656 | tf_op jit(solution)/shard_map/ppermute | solution.py:48
  148.2 23.7 %all-to-all-start.3 = ((bf16[16,8,512]{2,1,0:T(8,128)(2,1)}), bf16[16,8,512]{2,1,0:T(8,128)(2,1)S(1)}, u32[]{:S(2)}, u32[]{:S(2)}) async-start(bf16[16,8,512]{2,1,0:T(8,128)(2,1)} %fusion), calls=%async_computation.3 | async-start | bytes 262144 | tf_op jit(solution)/shard_map/all_to_all | solution.py:396
  166.6 4.3 %collective-permute-start.13 = (f32[128,128]{1,0:T(8,128)S(1)}, f32[128,128]{1,0:T(8,128)S(1)}, u32[]{:S(2)}, u32[]{:S(2)}) collective-permute-start(f32[128,128]{1,0:T(8,128)S(1)} %fusion.21.own_ref), channel_id=1, source_target_pairs={{0,16},{16,0},{1,17},{17,1},{2,18},{18,2},{3,19},{19,3},{4,20},{20... | collective-permute-start | bytes 196616 | tf_op jit(solution)/shard_map/ppermute | solution.py:444
  171.9 9.4 %all-to-all-start.4 = ((bf16[8,32,512]{2,1,0:T(8,128)(2,1)}), bf16[8,32,512]{2,1,0:T(8,128)(2,1)S(1)}, u32[]{:S(2)}, u32[]{:S(2)}) async-start(bf16[8,32,512]{2,1,0:T(8,128)(2,1)} %bitcast.19), calls=%async_computation.4 | async-start | bytes 524288 | tf_op jit(solution)/shard_map/all_to_all | solution.py:449

commit v13 on v12

--- a/solution.py
+++ b/solution.py
@@ -135,20 +135,26 @@
     )
 
 
-def place_rows(rows, target, placed_rows):
+def place_rows(rows, hot_target, cold_target, tag, hot_rows, cold_rows):
     count, depth = rows.shape
     blocks = 4
     width = depth // blocks
 
-    def kernel(target_at, rows_ref, early_ref, late_ref, place):
+    def kernel(hot_at, cold_at, tag_at, rows_ref, early_ref, late_ref, cold_ref, place_hot, place_cold):
         step = pl.program_id(0)
 
         @pl.when(step == 0)
         def _():
-            hit = lax.broadcasted_iota(jnp.int32, (placed_rows, count), 0) == target_at[...]
-            place[...] = hit.astype(jnp.float32).astype(jnp.bfloat16)
-
-        placed = narrow(place[...], rows_ref[...])
+            hot_hit = lax.broadcasted_iota(jnp.int32, (hot_rows, count), 0) == hot_at[...]
+            cold_hit = lax.broadcasted_iota(jnp.int32, (cold_rows, count), 0) == cold_at[...]
+            place_hot[...] = hot_hit.astype(jnp.float32).astype(jnp.bfloat16)
+            place_cold[...] = cold_hit.astype(jnp.float32).astype(jnp.bfloat16)
+            tags = jnp.sum(jnp.where(cold_hit, tag_at[...].astype(jnp.float32), 0.0), axis=1, keepdims=True)
+            cold_ref[:, depth:] = jnp.broadcast_to(tags, (cold_rows, TAG)).astype(jnp.bfloat16)
+
+        block = rows_ref[...]
+        placed = narrow(place_hot[...], block)
+        cold_ref[:, pl.ds(pl.multiple_of(step * width, 128), width)] = narrow(place_cold[...], block)
 
         @pl.when(step < blocks - 1)
         def _():
@@ -158,21 +164,24 @@
         def _():
             late_ref[...] = placed
 
+    index = pl.BlockSpec((1, count), lambda j: (0, 0))
     return pl.pallas_call(
         kernel,
         grid=(blocks,),
-        in_specs=[pl.BlockSpec((1, count), lambda j: (0, 0)), pl.BlockSpec((count, width), lambda j: (0, j))],
+        in_specs=[index, index, index, pl.BlockSpec((count, width), lambda j: (0, j))],
         out_specs=[
-            pl.BlockSpec((placed_rows, width), lambda j: (0, jnp.minimum(j, blocks - 2))),
-            pl.BlockSpec((placed_rows, width), lambda j: (0, 0)),
+            pl.BlockSpec((hot_rows, width), lambda j: (0, jnp.minimum(j, blocks - 2))),
+            pl.BlockSpec((hot_rows, width), lambda j: (0, 0)),
+            pl.BlockSpec((cold_rows, depth + TAG), lambda j: (0, 0)),
         ],
         out_shape=[
-            jax.ShapeDtypeStruct((placed_rows, depth - width), jnp.bfloat16),
-            jax.ShapeDtypeStruct((placed_rows, width), jnp.bfloat16),
+            jax.ShapeDtypeStruct((hot_rows, depth - width), jnp.bfloat16),
+            jax.ShapeDtypeStruct((hot_rows, width), jnp.bfloat16),
+            jax.ShapeDtypeStruct((cold_rows, depth + TAG), jnp.bfloat16),
         ],
-        scratch_shapes=[pltpu.VMEM((placed_rows, count), jnp.bfloat16)],
+        scratch_shapes=[pltpu.VMEM((hot_rows, count), jnp.bfloat16), pltpu.VMEM((cold_rows, count), jnp.bfloat16)],
         **kernel_params(),
-    )(target[None], rows)
+    )(hot_target[None], cold_target[None], tag[None], rows)
 
 
 def base_halves(rows, weight):
@@ -303,7 +312,9 @@
         block = chain.hold(block.reshape(group_count, near * HCAP, -1))
         return lax.all_to_all(block, GROUP, split_axis=0, concat_axis=0, tiled=True).reshape(hot_rows, -1)
 
-    hot_first_part, hot_last_part = place_rows(rows, hot_target, hot_rows)
+    hot_first_part, hot_last_part, packet = place_rows(
+        rows, hot_target, cold_target, (cold_row % per_dev + 1).reshape(-1), hot_rows, cold_rows
+    )
     hot_early = exchange(hot_first_part)
 
     hot_row = jnp.sum(jnp.where(hot_ids[:, :, None] == names, adapter_row, 0), axis=-1)
@@ -356,14 +367,9 @@
     done = {"hot_late": exchange(hot_last_part)}
 
     def cold_tokens_out():
-        cold_at = after(cold_target, chain.last)
-        cold_hit = jnp.arange(cold_rows, dtype=jnp.int32)[:, None] == cold_at
-        tag = jnp.sum(jnp.where(cold_hit, (cold_row % per_dev + 1).reshape(-1), 0), axis=-1)
-        tag = jnp.broadcast_to(tag.astype(jnp.bfloat16)[:, None], (cold_rows, TAG))
-        packet = jnp.concatenate([narrow(pick(cold_hit), rows), tag], axis=1)
-        packet = chain.hold(packet.reshape(dp_count, step_count * CAP, depth + TAG))
-        packet = lax.all_to_all(packet, DP, split_axis=0, concat_axis=0, tiled=True)
-        done["packet"] = packet.reshape(cold_rows, depth + TAG)
+        sent = chain.hold(packet.reshape(dp_count, step_count * CAP, depth + TAG))
+        sent = lax.all_to_all(sent, DP, split_axis=0, concat_axis=0, tiled=True)
+        done["packet"] = sent.reshape(cold_rows, depth + TAG)
 
     def base_product():
         weight = after(value_weight, chain.last)
@@ -404,12 +410,13 @@
         done["partial"] = partial + done["base_own"] + done["base_got"]
 
     between = {
-        1: [cold_tokens_out, base_product],
+        0: [base_product],
+        1: [cold_tokens_out],
         2: [base_over_tp],
         3: [cold_shrink, cold_over_tp],
         4: [cold_expand, cold_back, all_but_hot],
     }
-    awaited = {1: ["hot_late", "base_own", "base_other"], 2: ["packet"], 3: ["z_cold", "base_got"]}
+    awaited = {0: ["base_own", "base_other"], 1: ["hot_late"], 2: ["packet"], 3: ["z_cold", "base_got"]}
     for slot in range(chunk_count + len(hops) - 1):
         if slot > 0:
             if slot < chunk_count:

time: 183 us -> 181 us (0.989)
  starting transfers between devices: 42.3 us -> 52.9 us
  waiting for transfers between devices: 71.6 us -> 62.5 us
  matrix products: 13.9 us -> 11 us
  other arithmetic: 20.9 us -> 18.8 us
    ppermute x12, waiting for transfers between devices: 62.3 us -> 54 us  [permute(): return lax.ppermute(self.hold(value), axis, pairs)]
    ppermute x12, starting transfers between devices: 15.3 us -> 22.2 us  [permute(): return lax.ppermute(self.hold(value), axis, pairs)]
    all_to_all x1, starting transfers between devices: 6.68 us -> 10.4 us  [cold_tokens_out(): sent = lax.all_to_all(sent, DP, split_axis=0, concat_axis=0, tiled=True)]
    dot_general x9 -> x8, matrix products: 13.6 us -> 10.6 us  [matmul(): return jnp.dot(a, b, preferred_element_type=jnp.float32)]
    unnamed x26 -> x30, local copies, waits for them, and re-layouts: 8.46 us -> 9.26 us
  transfers between devices with their start and end apart: 19 -> 19, of which waited for: 10 -> 10; matrix products, arithmetic and copies ran while one was open for 17% -> 14% of each run, Pallas kernels for 11% -> 11%
where the time goes in v13:
time: 181 us
  waiting for transfers between devices  62.5 us (35%)
  starting transfers between devices  52.9 us (29%)
  Pallas kernels  24.9 us (14%)
  other arithmetic  18.8 us (10%)
  matrix products  11 us (6%)
  local copies, waits for them, and re-layouts  10.1 us (6%)
    ppermute x12, waiting for transfers between devices, permute(): return lax.ppermute(self.hold(value), axis, pairs)  54 us
    ppermute x12, starting transfers between devices, permute(): return lax.ppermute(self.hold(value), axis, pairs)  22.2 us
    pallas_call x1, Pallas kernels, base_halves(): pl.pallas_call(kernel, grid_spec=pltpu.PrefetchScalarGridSpec(num_scalar_...  10.9 us
    dot_general x8, matrix products, matmul(): return jnp.dot(a, b, preferred_element_type=jnp.float32)  10.6 us
    all_to_all x1, starting transfers between devices, cold_tokens_out(): sent = lax.all_to_all(sent, DP, split_axis=0, concat_axis=0, tiled=True)  10.4 us
    unnamed x30, local copies, waits for them, and re-layouts  9.26 us
    all_to_all x2, starting transfers between devices, exchange(): lax.all_to_all(block, GROUP, split_axis=0, concat_axis=0, tiled=True)  8.72 us
    pallas_call x1, Pallas kernels, pick_columns(): pl.pallas_call(kernel, grid_spec=pltpu.PrefetchScalarGridSpec(num_scalar_...  7.41 us
  transfers between devices with their start and end apart: 19, of which 10 were waited for; matrix products, arithmetic and copies ran while one was open for 14% of the time, Pallas kernels for 11%

profile of v13, /device:TPU:0, one launch (start us, length us, event | category | flops | bytes accessed | tf_op | source)
XLA Modules:
  0.0 180.5 jit_solution(15364947018511998602)
XLA Ops:
  0.7 0.9 select_reduce_fusion
  3.3 2.2 %copy-done = bf16[4,128,4096]{2,1,0:T(8,128)(2,1)S(1)} copy-done((bf16[4,128,4096]{2,1,0:T(8,128)(2,1)S(1)}, bf16[4,128,4096]{2,1,0:T(8,128)(2,1)}, u32[]{:S(2)}) %copy-start) | copy-done | bytes 4194328
  5.5 4.5 %shard_map.73 = (bf16[256,3072]{1,0:T(8,128)(2,1)}, bf16[256,1024]{1,0:T(8,128)(2,1)}, bf16[128,4224]{1,0:T(8,128)(2,1)}) custom-call(s32[1,512]{1,0:T(1,128)S(1)} %bitcast.50, s32[1,512]{1,0:T(1,128)S(1)} %bitcast.48, s32[1,512]{1,0:T(1,128)S(1)} %fusion.28.tag_at, bf16[512,4096]{1,0:T(8,128)(2,1)S(1)} %bitcast.45), custom_call_target="tpu_custom_call" | custom-call | flops 1 | bytes 1 | tf_op jit(solution)/shard_map/pallas_call | solution.py:168
  10.0 5.2 %all-to-all-start = ((bf16[8,32,3072]{2,1,0:T(8,128)(2,1)}), bf16[8,32,3072]{2,1,0:T(8,128)(2,1)}, u32[]{:S(2)}, u32[]{:S(2)}) async-start(bf16[8,32,3072]{2,1,0:T(8,128)(2,1)} %bitcast.8), calls=%async_computation | async-start | bytes 3145728 | tf_op jit(solution)/shard_map/all_to_all | solution.py:313
  17.4 2.2 %copy-done.2 = bf16[4096,512]{1,0:T(8,128)(2,1)S(1)} copy-done((bf16[4096,512]{1,0:T(8,128)(2,1)S(1)}, bf16[4096,512]{1,0:T(8,128)(2,1)}, u32[]{:S(2)}) %copy-start.2) | copy-done | bytes 4194328
  19.6 7.4 %shard_map.74 = (bf16[4608,512]{1,0:T(8,128)(2,1)S(1)}, bf16[1536,512]{1,0:T(8,128)(2,1)S(1)}, bf16[3072,512]{1,0:T(8,128)(2,1)}) custom-call(s32[4]{0:T(128)S(1)} %convert_element_type.18.mine_held, s32[4]{0:T(128)S(1)} %convert_element_type.19.other_held, s32[1,512]{1,0:T(1,128)S(1)} %bitcast.52, s32[1,512]{1,0:T(1,128)S(1)} %bitcast.53, ...), custom_call_target="tpu_custom_call" | custom-call | flops 1 | bytes 1 | tf_op jit(solution)/shard_map/pallas_call | solution.py:108
  27.5 7.4 %collective-permute-done = bf16[1536,512]{1,0:T(8,128)(2,1)S(1)} collective-permute-done((bf16[1536,512]{1,0:T(8,128)(2,1)S(1)}, bf16[1536,512]{1,0:T(8,128)(2,1)S(1)}, u32[]{:S(2)}, u32[]{:S(2)}) %collective-permute-start) | collective-permute-done | bytes 1572896 | tf_op jit(solution)/shard_map/ppermute | solution.py:48
  34.9 1.2 copy-done.5
  36.2 1.9 %collective-permute-start.1 = (bf16[1536,256]{1,0:T(8,128)(2,1)S(1)}, bf16[1536,256]{1,0:T(8,128)(2,1)}, u32[]{:S(2)}, u32[]{:S(2)}) collective-permute-start(bf16[1536,256]{1,0:T(8,128)(2,1)S(1)} %slice_add_fusion), channel_id=1, source_target_pairs={{0,2},{2,0},{1,3},{3,1},{4,6},{6,4},{5,7},{7,5},{8,10},{10,8},{9,1... | collective-permute-start | bytes 2359304 | tf_op jit(solution)/shard_map/ppermute | solution.py:48
  38.1 3.5 %all-to-all-start.1 = ((bf16[8,32,1024]{2,1,0:T(8,128)(2,1)}), bf16[8,32,1024]{2,1,0:T(8,128)(2,1)S(1)}, u32[]{:S(2)}, u32[]{:S(2)}) async-start(bf16[8,32,1024]{2,1,0:T(8,128)(2,1)} %bitcast.5), calls=%async_computation.1 | async-start | bytes 1048576 | tf_op jit(solution)/shard_map/all_to_all | solution.py:313
  41.6 2.2 %copy-done.1 = bf16[4,128,4096]{2,1,0:T(8,128)(2,1)S(1)} copy-done((bf16[4,128,4096]{2,1,0:T(8,128)(2,1)S(1)}, bf16[4,128,4096]{2,1,0:T(8,128)(2,1)}, u32[]{:S(2)}) %copy-start.1) | copy-done | bytes 4194328
  43.8 10.9 %shard_map.75 = (f32[512,512]{1,0:T(8,128)S(1)}, f32[512,512]{1,0:T(8,128)}) custom-call(s32[1]{0:T(128)} %bitcast.10.tp_at, bf16[512,4096]{1,0:T(8,128)(2,1)S(1)} %bitcast.46, bf16[4096,1024]{1,0:T(8,128)(2,1)} %weight_ref), custom_call_target="tpu_custom_call" | custom-call | flops 1 | bytes 1 | tf_op jit(solution)/shard_map/pallas_call | solution.py:214
  54.6 4.9 %collective-permute-done.1 = bf16[1536,256]{1,0:T(8,128)(2,1)} collective-permute-done((bf16[1536,256]{1,0:T(8,128)(2,1)S(1)}, bf16[1536,256]{1,0:T(8,128)(2,1)}, u32[]{:S(2)}, u32[]{:S(2)}) %collective-permute-start.1) | collective-permute-done | bytes 786464 | tf_op jit(solution)/shard_map/ppermute | solution.py:48
  59.5 1.5 slice_add_fusion.2
  61.0 1.9 %collective-permute-start.3 = (bf16[1536,256]{1,0:T(8,128)(2,1)S(1)}, bf16[1536,256]{1,0:T(8,128)(2,1)}, u32[]{:S(2)}, u32[]{:S(2)}) collective-permute-start(bf16[1536,256]{1,0:T(8,128)(2,1)S(1)} %slice_add_fusion.2), channel_id=1, source_target_pairs={{0,2},{2,0},{1,3},{3,1},{4,6},{6,4},{5,7},{7,5},{8,10},{10,8},{9,1... | collective-permute-start | bytes 2359304 | tf_op jit(solution)/shard_map/ppermute | solution.py:48
  62.9 1.3 fusion.11
  64.3 10.4 %all-to-all-start.2 = ((bf16[16,8,4224]{2,1,0:T(8,128)(2,1)}), bf16[16,8,4224]{2,1,0:T(8,128)(2,1)}, u32[]{:S(2)}, u32[]{:S(2)}) async-start(bf16[16,8,4224]{2,1,0:T(8,128)(2,1)} %bitcast.11), calls=%async_computation.2 | async-start | bytes 2162688 | tf_op jit(solution)/shard_map/all_to_all | solution.py:371
  74.7 9.7 %collective-permute-done.3 = bf16[1536,256]{1,0:T(8,128)(2,1)} collective-permute-done((bf16[1536,256]{1,0:T(8,128)(2,1)S(1)}, bf16[1536,256]{1,0:T(8,128)(2,1)}, u32[]{:S(2)}, u32[]{:S(2)}) %collective-permute-start.3) | collective-permute-done | bytes 786464 | tf_op jit(solution)/shard_map/ppermute | solution.py:48
  84.3 1.5 slice_add_fusion.1
  85.9 1.4 fusion.10
  87.3 1.3 slice_add_fusion.6
  88.7 13.8 %collective-permute-start.7 = (bf16[1536,128]{1,0:T(8,128)(2,1)S(1)}, bf16[1536,128]{1,0:T(8,128)(2,1)S(1)}, u32[]{:S(2)}, u32[]{:S(2)}) collective-permute-start(bf16[1536,128]{1,0:T(8,128)(2,1)S(1)} %fusion.10), channel_id=1, source_target_pairs={{0,8},{8,0},{1,9},{9,1},{2,10},{10,2},{3,11},{11,3},{4,12},{12,4},... | collective-permute-start | bytes 1179656 | tf_op jit(solution)/shard_map/ppermute | solution.py:48
  103.1 1.5 collective-permute-start.11
  104.6 14.2 %collective-permute-done.7 = bf16[1536,128]{1,0:T(8,128)(2,1)S(1)} collective-permute-done((bf16[1536,128]{1,0:T(8,128)(2,1)S(1)}, bf16[1536,128]{1,0:T(8,128)(2,1)S(1)}, u32[]{:S(2)}, u32[]{:S(2)}) %collective-permute-start.7) | collective-permute-done | bytes 393248 | tf_op jit(solution)/shard_map/ppermute | solution.py:48
  119.6 1.4 add_add_fusion.2
  121.0 1.3 slice_add_fusion.5
  122.4 2.0 %collective-permute-start.9 = (bf16[1536,128]{1,0:T(8,128)(2,1)S(1)}, bf16[1536,128]{1,0:T(8,128)(2,1)S(1)}, u32[]{:S(2)}, u32[]{:S(2)}) collective-permute-start(bf16[1536,128]{1,0:T(8,128)(2,1)S(1)} %add_add_fusion.2), channel_id=1, source_target_pairs={{0,8},{8,0},{1,9},{9,1},{2,10},{10,2},{3,11},{11,3},{4,12},{12,4},... | collective-permute-start | bytes 1179656 | tf_op jit(solution)/shard_map/ppermute | solution.py:48
  124.4 0.9 convert_reduce_fusion.1
  125.2 3.2 %convolution_select_fusion = f32[128,512]{1,0:T(8,128)S(1)} fusion(bf16[4096,512]{1,0:T(8,128)(2,1)} %store_ref, bf16[128,4224]{1,0:T(8,128)(2,1)} %bitcast.13, s32[512]{0:T(512)S(1)} %fusion.22, s32[128]{0:T(128)S(1)} %convert_reduce_fusion.1), kind=kOutput, calls=%fused_computation | convolution fusion | flops 537001984 | bytes 5507584 | tf_op jit(solution)/shard_map/dot_general | solution.py:22
  128.5 1.6 collective-permute-start.10
  130.1 1.5 fusion.6
  131.5 1.5 convolution_add_fusion.2
  133.0 1.9 %collective-permute-done.10 = f32[128,512]{1,0:T(8,128)S(1)} collective-permute-done((f32[128,512]{1,0:T(8,128)S(1)}, f32[128,512]{1,0:T(8,128)S(1)}, u32[]{:S(2)}, u32[]{:S(2)}) %collective-permute-start.10) | collective-permute-done | bytes 262176 | tf_op jit(solution)/shard_map/ppermute | solution.py:31
  135.0 4.6 %collective-permute-done.8 = bf16[1536,128]{1,0:T(8,128)(2,1)S(1)} collective-permute-done((bf16[1536,128]{1,0:T(8,128)(2,1)S(1)}, bf16[1536,128]{1,0:T(8,128)(2,1)S(1)}, u32[]{:S(2)}, u32[]{:S(2)}) %collective-permute-start.8) | collective-permute-done | bytes 393248 | tf_op jit(solution)/shard_map/ppermute | solution.py:48
  139.5 3.0 %collective-permute-done.9 = bf16[1536,128]{1,0:T(8,128)(2,1)S(1)} collective-permute-done((bf16[1536,128]{1,0:T(8,128)(2,1)S(1)}, bf16[1536,128]{1,0:T(8,128)(2,1)S(1)}, u32[]{:S(2)}, u32[]{:S(2)}) %collective-permute-start.9) | collective-permute-done | bytes 393248 | tf_op jit(solution)/shard_map/ppermute | solution.py:48
  143.2 1.4 add_add_fusion.1.first_ref
  145.0 1.5 convolution_add_fusion.1
  146.5 0.9 fusion
  147.3 5.0 %all-to-all-start.3 = ((bf16[16,8,512]{2,1,0:T(8,128)(2,1)}), bf16[16,8,512]{2,1,0:T(8,128)(2,1)S(1)}, u32[]{:S(2)}, u32[]{:S(2)}) async-start(bf16[16,8,512]{2,1,0:T(8,128)(2,1)} %fusion), calls=%async_computation.3 | async-start | bytes 262144 | tf_op jit(solution)/shard_map/all_to_all | solution.py:402
  152.6 10.3 %collective-permute-done.12.second_ref = bf16[1536,128]{1,0:T(8,128)(2,1)S(1)} collective-permute-done((bf16[1536,128]{1,0:T(8,128)(2,1)S(1)}, bf16[1536,128]{1,0:T(8,128)(2,1)S(1)}, u32[]{:S(2)}, u32[]{:S(2)}) %collective-permute-start.12) | collective-permute-done | bytes 393248 | tf_op jit(solution)/shard_map/ppermute | solution.py:48
  163.2 1.5 fusion.2
  164.7 1.6 collective-permute-start.13
  166.5 2.6 %collective-permute-done.13.got_ref = f32[128,128]{1,0:T(8,128)S(1)} collective-permute-done((f32[128,128]{1,0:T(8,128)S(1)}, f32[128,128]{1,0:T(8,128)S(1)}, u32[]{:S(2)}, u32[]{:S(2)}) %collective-permute-start.13) | collective-permute-done | bytes 65568 | tf_op jit(solution)/shard_map/ppermute | solution.py:451
  169.1 0.9 shard_map.76
  170.0 3.4 %all-to-all-start.4 = ((bf16[8,32,512]{2,1,0:T(8,128)(2,1)}), bf16[8,32,512]{2,1,0:T(8,128)(2,1)S(1)}, u32[]{:S(2)}, u32[]{:S(2)}) async-start(bf16[8,32,512]{2,1,0:T(8,128)(2,1)} %bitcast.20), calls=%async_computation.4 | async-start | bytes 524288 | tf_op jit(solution)/shard_map/all_to_all | solution.py:456
  173.8 1.5 add_add_fusion.partial_ref
  175.3 4.1 %all-to-all-done.4 = bf16[8,32,512]{2,1,0:T(8,128)(2,1)S(1)} async-done(((bf16[8,32,512]{2,1,0:T(8,128)(2,1)}), bf16[8,32,512]{2,1,0:T(8,128)(2,1)S(1)}, u32[]{:S(2)}, u32[]{:S(2)}) %all-to-all-start.4) | async-done | bytes 262176 | tf_op jit(solution)/shard_map/all_to_all | solution.py:456
  179.4 1.1 shard_map.77
  (87 shorter events, 8.9 us)
Async XLA Ops:
  3.3 2.2 %copy-start = (bf16[4,128,4096]{2,1,0:T(8,128)(2,1)S(1)}, bf16[4,128,4096]{2,1,0:T(8,128)(2,1)}, u32[]{:S(2)}) copy-start(bf16[4,128,4096]{2,1,0:T(8,128)(2,1)} %param.7) | copy-start | bytes 12582916
  5.5 9.8 %copy-start.10 = (s32[128]{0:T(128)S(1)}, s32[128]{0:T(128)}, u32[]{:S(2)}) copy-start(s32[128]{0:T(128)} %param.11) | copy-start | bytes 1540
  5.5 9.8 %copy-start.11 = (s32[4,4]{1,0:T(4,128)S(1)}, s32[4,4]{1,0:T(4,128)}, u32[]{:S(2)}) copy-start(s32[4,4]{1,0:T(4,128)} %param.13) | copy-start | bytes 196
  5.5 11.9 %copy-start.4 = (bf16[512,512]{1,0:T(8,128)(2,1)S(1)}, bf16[512,512]{1,0:T(8,128)(2,1)}, u32[]{:S(2)}) copy-start(bf16[512,512]{1,0:T(8,128)(2,1)} %expand_ref.1) | copy-start | bytes 1572868
  10.0 26.2 %all-to-all-start = ((bf16[8,32,3072]{2,1,0:T(8,128)(2,1)}), bf16[8,32,3072]{2,1,0:T(8,128)(2,1)}, u32[]{:S(2)}, u32[]{:S(2)}) async-start(bf16[8,32,3072]{2,1,0:T(8,128)(2,1)} %bitcast.8), calls=%async_computation | async-start | bytes 3145728 | tf_op jit(solution)/shard_map/all_to_all | solution.py:313
  17.4 2.2 %copy-start.2 = (bf16[4096,512]{1,0:T(8,128)(2,1)S(1)}, bf16[4096,512]{1,0:T(8,128)(2,1)}, u32[]{:S(2)}) copy-start(bf16[4096,512]{1,0:T(8,128)(2,1)} %store_ref) | copy-start | bytes 12582916
  27.0 7.9 %copy-start.3 = (bf16[4608,512]{1,0:T(8,128)(2,1)}, bf16[4608,512]{1,0:T(8,128)(2,1)S(1)}, u32[]{:S(2)}) copy-start(bf16[4608,512]{1,0:T(8,128)(2,1)S(1)} %get-tuple-element.80) | copy-start | bytes 14155780
  27.0 32.5 %collective-permute-start.2 = (bf16[3072,512]{1,0:T(8,128)(2,1)}, bf16[3072,512]{1,0:T(8,128)(2,1)}, u32[]{:S(2)}, u32[]{:S(2)}) collective-permute-start(bf16[3072,512]{1,0:T(8,128)(2,1)} %get-tuple-element.62), channel_id=1, source_target_pairs={{0,1},{1,0},{2,3},{3,2},{4,5},{5,4},{6,7},{7,6},{8,9},{9,8},{10,11... | collective-permute-start | bytes 9437192 | tf_op jit(solution)/shard_map/ppermute | solution.py:48
  27.5 7.4 %collective-permute-start = (bf16[1536,512]{1,0:T(8,128)(2,1)S(1)}, bf16[1536,512]{1,0:T(8,128)(2,1)S(1)}, u32[]{:S(2)}, u32[]{:S(2)}) collective-permute-start(bf16[1536,512]{1,0:T(8,128)(2,1)S(1)} %get-tuple-element.59), channel_id=1, source_target_pairs={{0,1},{1,0},{2,3},{3,2},{4,5},{5,4},{6,7},{7,6},{8,9},{9,8},{10,11... | collective-permute-start | bytes 4718600 | tf_op jit(solution)/shard_map/ppermute | solution.py:48
  34.9 1.2 copy-start.5
  36.2 23.3 %collective-permute-start.1 = (bf16[1536,256]{1,0:T(8,128)(2,1)S(1)}, bf16[1536,256]{1,0:T(8,128)(2,1)}, u32[]{:S(2)}, u32[]{:S(2)}) collective-permute-start(bf16[1536,256]{1,0:T(8,128)(2,1)S(1)} %slice_add_fusion), channel_id=1, source_target_pairs={{0,2},{2,0},{1,3},{3,1},{4,6},{6,4},{5,7},{7,5},{8,10},{10,8},{9,1... | collective-permute-start | bytes 2359304 | tf_op jit(solution)/shard_map/ppermute | solution.py:48
  38.1 26.2 %all-to-all-start.1 = ((bf16[8,32,1024]{2,1,0:T(8,128)(2,1)}), bf16[8,32,1024]{2,1,0:T(8,128)(2,1)S(1)}, u32[]{:S(2)}, u32[]{:S(2)}) async-start(bf16[8,32,1024]{2,1,0:T(8,128)(2,1)} %bitcast.5), calls=%async_computation.1 | async-start | bytes 1048576 | tf_op jit(solution)/shard_map/all_to_all | solution.py:313
  41.6 2.2 %copy-start.1 = (bf16[4,128,4096]{2,1,0:T(8,128)(2,1)S(1)}, bf16[4,128,4096]{2,1,0:T(8,128)(2,1)}, u32[]{:S(2)}) copy-start(bf16[4,128,4096]{2,1,0:T(8,128)(2,1)} %param.7) | copy-start | bytes 12582916
  61.0 23.4 %collective-permute-start.3 = (bf16[1536,256]{1,0:T(8,128)(2,1)S(1)}, bf16[1536,256]{1,0:T(8,128)(2,1)}, u32[]{:S(2)}, u32[]{:S(2)}) collective-permute-start(bf16[1536,256]{1,0:T(8,128)(2,1)S(1)} %slice_add_fusion.2), channel_id=1, source_target_pairs={{0,2},{2,0},{1,3},{3,1},{4,6},{6,4},{5,7},{7,5},{8,10},{10,8},{9,1... | collective-permute-start | bytes 2359304 | tf_op jit(solution)/shard_map/ppermute | solution.py:48
  64.2 10.5 %collective-permute-start.4 = (bf16[1536,128]{1,0:T(8,128)(2,1)S(1)}, bf16[1536,128]{1,0:T(8,128)(2,1)}, u32[]{:S(2)}, u32[]{:S(2)}) collective-permute-start(bf16[1536,128]{1,0:T(8,128)(2,1)S(1)} %fusion.11), channel_id=1, source_target_pairs={{0,4},{4,0},{1,5},{5,1},{2,6},{6,2},{3,7},{7,3},{8,12},{12,8},{9,1... | collective-permute-start | bytes 1179656 | tf_op jit(solution)/shard_map/ppermute | solution.py:48
  64.3 55.3 %all-to-all-start.2 = ((bf16[16,8,4224]{2,1,0:T(8,128)(2,1)}), bf16[16,8,4224]{2,1,0:T(8,128)(2,1)}, u32[]{:S(2)}, u32[]{:S(2)}) async-start(bf16[16,8,4224]{2,1,0:T(8,128)(2,1)} %bitcast.11), calls=%async_computation.2 | async-start | bytes 2162688 | tf_op jit(solution)/shard_map/all_to_all | solution.py:371
  85.8 33.8 %collective-permute-start.5 = (bf16[1536,256]{1,0:T(8,128)(2,1)S(1)}, bf16[1536,256]{1,0:T(8,128)(2,1)}, u32[]{:S(2)}, u32[]{:S(2)}) collective-permute-start(bf16[1536,256]{1,0:T(8,128)(2,1)S(1)} %slice_add_fusion.1), channel_id=1, source_target_pairs={{0,2},{2,0},{1,3},{3,1},{4,6},{6,4},{5,7},{7,5},{8,10},{10,8},{9,1... | collective-permute-start | bytes 2359304 | tf_op jit(solution)/shard_map/ppermute | solution.py:48
  88.6 16.0 %collective-permute-start.6 = (bf16[1536,128]{1,0:T(8,128)(2,1)S(1)}, bf16[1536,128]{1,0:T(8,128)(2,1)S(1)}, u32[]{:S(2)}, u32[]{:S(2)}) collective-permute-start(bf16[1536,128]{1,0:T(8,128)(2,1)S(1)} %slice_add_fusion.6), channel_id=1, source_target_pairs={{0,4},{4,0},{1,5},{5,1},{2,6},{6,2},{3,7},{7,3},{8,12},{12,8},{9,1... | collective-permute-start | bytes 1179656 | tf_op jit(solution)/shard_map/ppermute | solution.py:48
  88.7 30.1 %collective-permute-start.7 = (bf16[1536,128]{1,0:T(8,128)(2,1)S(1)}, bf16[1536,128]{1,0:T(8,128)(2,1)S(1)}, u32[]{:S(2)}, u32[]{:S(2)}) collective-permute-start(bf16[1536,128]{1,0:T(8,128)(2,1)S(1)} %fusion.10), channel_id=1, source_target_pairs={{0,8},{8,0},{1,9},{9,1},{2,10},{10,2},{3,11},{11,3},{4,12},{12,4},... | collective-permute-start | bytes 1179656 | tf_op jit(solution)/shard_map/ppermute | solution.py:48
  103.1 31.9 %collective-permute-start.11 = (f32[512,512]{1,0:T(8,128)}, f32[512,512]{1,0:T(8,128)S(1)}, u32[]{:S(2)}, u32[]{:S(2)}) collective-permute-start(f32[512,512]{1,0:T(8,128)} %get-tuple-element.85), channel_id=1, source_target_pairs={{0,16},{16,0},{1,17},{17,1},{2,18},{18,2},{3,19},{19,3},{4,20},{20... | collective-permute-start | bytes 3145736 | tf_op jit(solution)/shard_map/ppermute | solution.py:48
  104.6 14.2 %copy-start.9 = (bf16[1536,128]{1,0:T(8,128)(2,1)}, bf16[1536,128]{1,0:T(8,128)(2,1)S(1)}, u32[]{:S(2)}) copy-start(bf16[1536,128]{1,0:T(8,128)(2,1)S(1)} %collective-permute-done.6) | copy-start | bytes 1179652
  118.8 0.7 copy-start.13
  122.3 7.7 %copy-start.14 = (bf16[1536,128]{1,0:T(8,128)(2,1)S(1)}, bf16[1536,128]{1,0:T(8,128)(2,1)}, u32[]{:S(2)}) copy-start(bf16[1536,128]{1,0:T(8,128)(2,1)} %copy-done.13) | copy-start | bytes 1179652
  122.3 17.2 %collective-permute-start.8 = (bf16[1536,128]{1,0:T(8,128)(2,1)S(1)}, bf16[1536,128]{1,0:T(8,128)(2,1)S(1)}, u32[]{:S(2)}, u32[]{:S(2)}) collective-permute-start(bf16[1536,128]{1,0:T(8,128)(2,1)S(1)} %slice_add_fusion.5), channel_id=1, source_target_pairs={{0,4},{4,0},{1,5},{5,1},{2,6},{6,2},{3,7},{7,3},{8,12},{12,8},{9,1... | collective-permute-start | bytes 1179656 | tf_op jit(solution)/shard_map/ppermute | solution.py:48
  122.4 20.1 %collective-permute-start.9 = (bf16[1536,128]{1,0:T(8,128)(2,1)S(1)}, bf16[1536,128]{1,0:T(8,128)(2,1)S(1)}, u32[]{:S(2)}, u32[]{:S(2)}) collective-permute-start(bf16[1536,128]{1,0:T(8,128)(2,1)S(1)} %add_add_fusion.2), channel_id=1, source_target_pairs={{0,8},{8,0},{1,9},{9,1},{2,10},{10,2},{3,11},{11,3},{4,12},{12,4},... | collective-permute-start | bytes 1179656 | tf_op jit(solution)/shard_map/ppermute | solution.py:48
  128.5 6.4 %collective-permute-start.10 = (f32[128,512]{1,0:T(8,128)S(1)}, f32[128,512]{1,0:T(8,128)S(1)}, u32[]{:S(2)}, u32[]{:S(2)}) collective-permute-start(f32[128,512]{1,0:T(8,128)S(1)} %convolution_select_fusion), channel_id=1, source_target_pairs={{0,16},{16,0},{1,17},{17,1},{2,18},{18,2},{3,19},{19,3},{4,20},{20... | collective-permute-start | bytes 786440 | tf_op jit(solution)/shard_map/ppermute | solution.py:31
  135.0 4.6 %copy-start.6 = (f32[512,512]{1,0:T(8,128)}, f32[512,512]{1,0:T(8,128)S(1)}, u32[]{:S(2)}) copy-start(f32[512,512]{1,0:T(8,128)S(1)} %collective-permute-done.11) | copy-start | bytes 3145732
  142.5 0.7 copy-start.7
  144.6 18.6 %copy-start.8 = (bf16[1536,128]{1,0:T(8,128)(2,1)S(1)}, bf16[1536,128]{1,0:T(8,128)(2,1)}, u32[]{:S(2)}) copy-start(bf16[1536,128]{1,0:T(8,128)(2,1)} %copy-done.7) | copy-start | bytes 1179652
  144.6 20.1 %copy-start.12 = (pred[128]{0:T(512)(128)(4,1)S(1)}, pred[128]{0:T(512)(128)(4,1)}, u32[]{:S(2)}) copy-start(pred[128]{0:T(512)(128)(4,1)} %get-tuple-element.130) | copy-start | bytes 388
  144.6 18.3 %collective-permute-start.12 = (bf16[1536,128]{1,0:T(8,128)(2,1)S(1)}, bf16[1536,128]{1,0:T(8,128)(2,1)S(1)}, u32[]{:S(2)}, u32[]{:S(2)}) collective-permute-start(bf16[1536,128]{1,0:T(8,128)(2,1)S(1)} %add_add_fusion.1.first_ref), channel_id=1, source_target_pairs={{0,8},{8,0},{1,9},{9,1},{2,10},{10,2},{3,11},{11,3},{4,12},{12,4},... | collective-permute-start | bytes 1179656 | tf_op jit(solution)/shard_map/ppermute | solution.py:48
  147.3 22.7 %all-to-all-start.3 = ((bf16[16,8,512]{2,1,0:T(8,128)(2,1)}), bf16[16,8,512]{2,1,0:T(8,128)(2,1)S(1)}, u32[]{:S(2)}, u32[]{:S(2)}) async-start(bf16[16,8,512]{2,1,0:T(8,128)(2,1)} %fusion), calls=%async_computation.3 | async-start | bytes 262144 | tf_op jit(solution)/shard_map/all_to_all | solution.py:402
  164.7 4.3 %collective-permute-start.13 = (f32[128,128]{1,0:T(8,128)S(1)}, f32[128,128]{1,0:T(8,128)S(1)}, u32[]{:S(2)}, u32[]{:S(2)}) collective-permute-start(f32[128,128]{1,0:T(8,128)S(1)} %fusion.20.own_ref), channel_id=1, source_target_pairs={{0,16},{16,0},{1,17},{17,1},{2,18},{18,2},{3,19},{19,3},{4,20},{20... | collective-permute-start | bytes 196616 | tf_op jit(solution)/shard_map/ppermute | solution.py:451
  170.0 9.4 %all-to-all-start.4 = ((bf16[8,32,512]{2,1,0:T(8,128)(2,1)}), bf16[8,32,512]{2,1,0:T(8,128)(2,1)S(1)}, u32[]{:S(2)}, u32[]{:S(2)}) async-start(bf16[8,32,512]{2,1,0:T(8,128)(2,1)} %bitcast.20), calls=%async_computation.4 | async-start | bytes 524288 | tf_op jit(solution)/shard_map/all_to_all | solution.py:456

commit v14 on v13

--- a/solution.py
+++ b/solution.py
@@ -410,13 +410,13 @@
         done["partial"] = partial + done["base_own"] + done["base_got"]
 
     between = {
-        0: [base_product],
-        1: [cold_tokens_out],
-        2: [base_over_tp],
-        3: [cold_shrink, cold_over_tp],
-        4: [cold_expand, cold_back, all_but_hot],
+        0: [cold_tokens_out],
+        1: [base_product],
+        2: [cold_shrink, cold_over_tp, base_over_tp],
+        3: [cold_expand, cold_back],
+        4: [all_but_hot],
     }
-    awaited = {0: ["base_own", "base_other"], 1: ["hot_late"], 2: ["packet"], 3: ["z_cold", "base_got"]}
+    awaited = {0: ["hot_late"], 1: ["packet", "base_own", "base_other"], 2: ["z_cold"], 3: ["base_got"]}
     for slot in range(chunk_count + len(hops) - 1):
         if slot > 0:
             if slot < chunk_count:

time: 181 us -> 185 us (1.022)
  waiting for transfers between devices: 62.5 us -> 79.2 us
  starting transfers between devices: 52.9 us -> 38.4 us
  other arithmetic: 18.8 us -> 21.1 us
    ppermute x12, starting transfers between devices: 22.2 us -> 13.9 us  [permute(): return lax.ppermute(self.hold(value), axis, pairs)]
    all_to_all x2, waiting for transfers between devices: 0.01 us -> 7.19 us  [exchange(): lax.all_to_all(block, GROUP, split_axis=0, concat_axis=0, tiled=True)]
    ppermute x1, waiting for transfers between devices: 1.87 us -> 7.21 us  [sum_over_tp(): return part + lax.ppermute(part, 'tp', SWAP)]
    all_to_all x1, starting transfers between devices: 10.4 us -> 5.49 us  [cold_tokens_out(): sent = lax.all_to_all(sent, DP, split_axis=0, concat_axis=0, tiled=True)]
    ppermute x12, waiting for transfers between devices: 54 us -> 58.1 us  [permute(): return lax.ppermute(self.hold(value), axis, pairs)]
    pallas_call x1, Pallas kernels: 7.41 us -> 9.57 us  [pick_columns(): pl.pallas_call(kernel, grid_spec=pltpu.PrefetchScalarGridSpec(num_scalar_...]
    unnamed x30 -> x32, local copies, waits for them, and re-layouts: 9.26 us -> 8.93 us
  transfers between devices with their start and end apart: 19 -> 19, of which waited for: 10 -> 11; matrix products, arithmetic and copies ran while one was open for 14% -> 15% of each run, Pallas kernels for 11% -> 11%
where the time goes in v14:
time: 185 us
  waiting for transfers between devices  79.2 us (43%)
  starting transfers between devices  38.4 us (21%)
  Pallas kernels  26 us (14%)
  other arithmetic  21.1 us (11%)
  matrix products  9.83 us (5%)
  local copies, waits for them, and re-layouts  9.75 us (5%)
    ppermute x12, waiting for transfers between devices, permute(): return lax.ppermute(self.hold(value), axis, pairs)  58.1 us
    ppermute x12, starting transfers between devices, permute(): return lax.ppermute(self.hold(value), axis, pairs)  13.9 us
    pallas_call x1, Pallas kernels, base_halves(): pl.pallas_call(kernel, grid_spec=pltpu.PrefetchScalarGridSpec(num_scalar_...  9.89 us
    pallas_call x1, Pallas kernels, pick_columns(): pl.pallas_call(kernel, grid_spec=pltpu.PrefetchScalarGridSpec(num_scalar_...  9.57 us
    dot_general x8, matrix products, matmul(): return jnp.dot(a, b, preferred_element_type=jnp.float32)  9.49 us
    unnamed x32, local copies, waits for them, and re-layouts  8.93 us
    all_to_all x2, starting transfers between devices, exchange(): lax.all_to_all(block, GROUP, split_axis=0, concat_axis=0, tiled=True)  8.72 us
    ppermute x1, waiting for transfers between devices, sum_over_tp(): return part + lax.ppermute(part, 'tp', SWAP)  7.21 us
  transfers between devices with their start and end apart: 19, of which 11 were waited for; matrix products, arithmetic and copies ran while one was open for 15% of the time, Pallas kernels for 11%

profile of v14, /device:TPU:0, one launch (start us, length us, event | category | flops | bytes accessed | tf_op | source)
XLA Modules:
  0.0 184.7 jit_solution(11916430864840188782)
XLA Ops:
  3.3 2.2 %copy-done = bf16[4,128,4096]{2,1,0:T(8,128)(2,1)S(1)} copy-done((bf16[4,128,4096]{2,1,0:T(8,128)(2,1)S(1)}, bf16[4,128,4096]{2,1,0:T(8,128)(2,1)}, u32[]{:S(2)}) %copy-start) | copy-done | bytes 4194328
  5.5 4.5 %shard_map.73 = (bf16[256,3072]{1,0:T(8,128)(2,1)}, bf16[256,1024]{1,0:T(8,128)(2,1)}, bf16[128,4224]{1,0:T(8,128)(2,1)}) custom-call(s32[1,512]{1,0:T(1,128)S(1)} %bitcast.50, s32[1,512]{1,0:T(1,128)S(1)} %bitcast.48, s32[1,512]{1,0:T(1,128)S(1)} %fusion.28.tag_at, bf16[512,4096]{1,0:T(8,128)(2,1)S(1)} %bitcast.45), custom_call_target="tpu_custom_call" | custom-call | flops 1 | bytes 1 | tf_op jit(solution)/shard_map/pallas_call | solution.py:168
  10.0 5.2 %all-to-all-start = ((bf16[8,32,3072]{2,1,0:T(8,128)(2,1)}), bf16[8,32,3072]{2,1,0:T(8,128)(2,1)S(1)}, u32[]{:S(2)}, u32[]{:S(2)}) async-start(bf16[8,32,3072]{2,1,0:T(8,128)(2,1)} %bitcast.7), calls=%async_computation | async-start | bytes 3145728 | tf_op jit(solution)/shard_map/all_to_all | solution.py:313
  17.4 2.2 %copy-done.2 = bf16[4096,512]{1,0:T(8,128)(2,1)S(1)} copy-done((bf16[4096,512]{1,0:T(8,128)(2,1)S(1)}, bf16[4096,512]{1,0:T(8,128)(2,1)}, u32[]{:S(2)}) %copy-start.2) | copy-done | bytes 4194328
  19.6 9.6 %shard_map.74 = (bf16[4608,512]{1,0:T(8,128)(2,1)S(1)}, bf16[1536,512]{1,0:T(8,128)(2,1)S(1)}, bf16[3072,512]{1,0:T(8,128)(2,1)}) custom-call(s32[4]{0:T(128)S(1)} %convert_element_type.18.mine_held, s32[4]{0:T(128)S(1)} %convert_element_type.19.other_held, s32[1,512]{1,0:T(1,128)S(1)} %bitcast.52, s32[1,512]{1,0:T(1,128)S(1)} %bitcast.53, ...), custom_call_target="tpu_custom_call" | custom-call | flops 1 | bytes 1 | tf_op jit(solution)/shard_map/pallas_call | solution.py:108
  29.7 5.1 %collective-permute-done = bf16[1536,512]{1,0:T(8,128)(2,1)S(1)} collective-permute-done((bf16[1536,512]{1,0:T(8,128)(2,1)S(1)}, bf16[1536,512]{1,0:T(8,128)(2,1)S(1)}, u32[]{:S(2)}, u32[]{:S(2)}) %collective-permute-start) | collective-permute-done | bytes 1572896 | tf_op jit(solution)/shard_map/ppermute | solution.py:48
  34.8 1.2 copy-done.10
  36.1 1.2 copy-done.8
  37.2 3.5 %all-to-all-start.1 = ((bf16[8,32,1024]{2,1,0:T(8,128)(2,1)}), bf16[8,32,1024]{2,1,0:T(8,128)(2,1)S(1)}, u32[]{:S(2)}, u32[]{:S(2)}) async-start(bf16[8,32,1024]{2,1,0:T(8,128)(2,1)} %bitcast.9), calls=%async_computation.1 | async-start | bytes 1048576 | tf_op jit(solution)/shard_map/all_to_all | solution.py:313
  40.7 2.0 %collective-permute-start.1 = (bf16[1536,256]{1,0:T(8,128)(2,1)S(1)}, bf16[1536,256]{1,0:T(8,128)(2,1)S(1)}, u32[]{:S(2)}, u32[]{:S(2)}) collective-permute-start(bf16[1536,256]{1,0:T(8,128)(2,1)S(1)} %slice_add_fusion), channel_id=1, source_target_pairs={{0,2},{2,0},{1,3},{3,1},{4,6},{6,4},{5,7},{7,5},{8,10},{10,8},{9,1... | collective-permute-start | bytes 2359304 | tf_op jit(solution)/shard_map/ppermute | solution.py:48
  42.8 7.2 %all-to-all-done.1 = bf16[8,32,1024]{2,1,0:T(8,128)(2,1)S(1)} async-done(((bf16[8,32,1024]{2,1,0:T(8,128)(2,1)}), bf16[8,32,1024]{2,1,0:T(8,128)(2,1)S(1)}, u32[]{:S(2)}, u32[]{:S(2)}) %all-to-all-start.1) | async-done | bytes 524320 | tf_op jit(solution)/shard_map/all_to_all | solution.py:313
  50.0 5.5 %all-to-all-start.2 = ((bf16[16,8,4224]{2,1,0:T(8,128)(2,1)}), bf16[16,8,4224]{2,1,0:T(8,128)(2,1)}, u32[]{:S(2)}, u32[]{:S(2)}) async-start(bf16[16,8,4224]{2,1,0:T(8,128)(2,1)} %bitcast.8), calls=%async_computation.2 | async-start | bytes 2162688 | tf_op jit(solution)/shard_map/all_to_all | solution.py:371
  55.5 17.1 %collective-permute-done.1 = bf16[1536,256]{1,0:T(8,128)(2,1)S(1)} collective-permute-done((bf16[1536,256]{1,0:T(8,128)(2,1)S(1)}, bf16[1536,256]{1,0:T(8,128)(2,1)S(1)}, u32[]{:S(2)}, u32[]{:S(2)}) %collective-permute-start.1) | collective-permute-done | bytes 786464 | tf_op jit(solution)/shard_map/ppermute | solution.py:48
  72.6 1.7 slice_add_fusion.2
  74.4 2.0 %fusion.11 = bf16[1536,128]{1,0:T(8,128)(2,1)} fusion(bf16[1536,512]{1,0:T(8,128)(2,1)} %copy-done.10, bf16[1536,256]{1,0:T(8,128)(2,1)S(1)} %collective-permute-done.1, bf16[4608,512]{1,0:T(8,128)(2,1)} %copy-done.4), kind=kLoop, calls=%fused_computation.22 | loop fusion | flops 393216 | bytes 1572864 | tf_op jit(solution)/shard_map/add | solution.py:350
  76.8 2.2 %copy-done.1 = bf16[4,128,4096]{2,1,0:T(8,128)(2,1)S(1)} copy-done((bf16[4,128,4096]{2,1,0:T(8,128)(2,1)S(1)}, bf16[4,128,4096]{2,1,0:T(8,128)(2,1)}, u32[]{:S(2)}) %copy-start.1) | copy-done | bytes 4194328
  79.0 9.9 %shard_map.75 = (f32[512,512]{1,0:T(8,128)S(1)}, f32[512,512]{1,0:T(8,128)S(1)}) custom-call(s32[1]{0:T(128)} %bitcast.13.tp_at, bf16[512,4096]{1,0:T(8,128)(2,1)S(1)} %bitcast.46, bf16[4096,1024]{1,0:T(8,128)(2,1)} %weight_ref), custom_call_target="tpu_custom_call" | custom-call | flops 1 | bytes 1 | tf_op jit(solution)/shard_map/pallas_call | solution.py:214
  88.9 7.0 %collective-permute-done.3 = bf16[1536,256]{1,0:T(8,128)(2,1)} collective-permute-done((bf16[1536,256]{1,0:T(8,128)(2,1)S(1)}, bf16[1536,256]{1,0:T(8,128)(2,1)}, u32[]{:S(2)}, u32[]{:S(2)}) %collective-permute-start.3) | collective-permute-done | bytes 786464 | tf_op jit(solution)/shard_map/ppermute | solution.py:48
  95.9 1.6 slice_add_fusion.1
  97.6 1.5 fusion.10
  99.1 1.4 slice_add_fusion.6
  100.5 1.1 collective-permute-start.6
  101.6 4.0 %collective-permute-start.7 = (bf16[1536,128]{1,0:T(8,128)(2,1)S(1)}, bf16[1536,128]{1,0:T(8,128)(2,1)S(1)}, u32[]{:S(2)}, u32[]{:S(2)}) collective-permute-start(bf16[1536,128]{1,0:T(8,128)(2,1)S(1)} %fusion.10), channel_id=1, source_target_pairs={{0,8},{8,0},{1,9},{9,1},{2,10},{10,2},{3,11},{11,3},{4,12},{12,4},... | collective-permute-start | bytes 1179656 | tf_op jit(solution)/shard_map/ppermute | solution.py:48
  106.5 2.0 %convolution_select_fusion = f32[128,512]{1,0:T(8,128)S(1)} fusion(bf16[4096,512]{1,0:T(8,128)(2,1)S(1)} %copy-done.3, bf16[128,4224]{1,0:T(8,128)(2,1)} %bitcast.12, s32[512]{0:T(512)S(1)} %fusion.25, s32[128]{0:T(128)S(1)} %convert_reduce_fusion.1), kind=kOutput, calls=%fused_computation | convolution fusion | flops 537001984 | bytes 5507584 | tf_op jit(solution)/shard_map/dot_general | solution.py:22
  108.5 1.6 collective-permute-start.8
  110.6 7.2 %collective-permute-done.8 = f32[128,512]{1,0:T(8,128)S(1)} collective-permute-done((f32[128,512]{1,0:T(8,128)S(1)}, f32[128,512]{1,0:T(8,128)S(1)}, u32[]{:S(2)}, u32[]{:S(2)}) %collective-permute-start.8) | collective-permute-done | bytes 262176 | tf_op jit(solution)/shard_map/ppermute | solution.py:31
  117.8 1.8 collective-permute-done.6
  119.7 2.3 %add_add_fusion.2 = bf16[1536,128]{1,0:T(8,128)(2,1)} fusion(bf16[1536,128]{1,0:T(8,128)(2,1)S(1)} %collective-permute-done.6, bf16[1536,256]{1,0:T(8,128)(2,1)} %collective-permute-done.3, bf16[3072,512]{1,0:T(8,128)(2,1)} %collective-permute-done.2, bf16[4608,512]{1,0:T(8,128)(2,1)} %copy-done.4), kind=kLoop, calls=%fused_computation.24 | loop fusion | flops 589824 | bytes 1966080 | tf_op jit(solution)/shard_map/add | solution.py:352
  121.9 2.0 %slice_add_fusion.5 = bf16[1536,128]{1,0:T(8,128)(2,1)} fusion(bf16[1536,256]{1,0:T(8,128)(2,1)S(1)} %collective-permute-done.5, bf16[3072,512]{1,0:T(8,128)(2,1)} %collective-permute-done.2, bf16[4608,512]{1,0:T(8,128)(2,1)} %copy-done.4), kind=kLoop, calls=%fused_computation.25 | loop fusion | flops 393216 | bytes 1572864 | tf_op jit(solution)/shard_map/add | solution.py:350
  123.9 2.5 %collective-permute-start.9 = (bf16[1536,128]{1,0:T(8,128)(2,1)}, bf16[1536,128]{1,0:T(8,128)(2,1)}, u32[]{:S(2)}, u32[]{:S(2)}) collective-permute-start(bf16[1536,128]{1,0:T(8,128)(2,1)} %slice_add_fusion.5), channel_id=1, source_target_pairs={{0,4},{4,0},{1,5},{5,1},{2,6},{6,2},{3,7},{7,3},{8,12},{12,8},{9,1... | collective-permute-start | bytes 1179656 | tf_op jit(solution)/shard_map/ppermute | solution.py:48
  126.4 2.7 %collective-permute-start.10 = (bf16[1536,128]{1,0:T(8,128)(2,1)}, bf16[1536,128]{1,0:T(8,128)(2,1)}, u32[]{:S(2)}, u32[]{:S(2)}) collective-permute-start(bf16[1536,128]{1,0:T(8,128)(2,1)} %add_add_fusion.2), channel_id=1, source_target_pairs={{0,8},{8,0},{1,9},{9,1},{2,10},{10,2},{3,11},{11,3},{4,12},{12,4},... | collective-permute-start | bytes 1179656 | tf_op jit(solution)/shard_map/ppermute | solution.py:48
  129.1 0.9 fusion
  130.0 3.7 %all-to-all-start.3 = ((bf16[16,8,512]{2,1,0:T(8,128)(2,1)}), bf16[16,8,512]{2,1,0:T(8,128)(2,1)S(1)}, u32[]{:S(2)}, u32[]{:S(2)}) async-start(bf16[16,8,512]{2,1,0:T(8,128)(2,1)} %fusion), calls=%async_computation.3 | async-start | bytes 262144 | tf_op jit(solution)/shard_map/all_to_all | solution.py:402
  133.7 1.7 fusion.6
  135.4 1.6 convolution_add_fusion.2
  137.0 4.7 %collective-permute-done.9 = bf16[1536,128]{1,0:T(8,128)(2,1)} collective-permute-done((bf16[1536,128]{1,0:T(8,128)(2,1)}, bf16[1536,128]{1,0:T(8,128)(2,1)}, u32[]{:S(2)}, u32[]{:S(2)}) %collective-permute-start.9) | collective-permute-done | bytes 393248 | tf_op jit(solution)/shard_map/ppermute | solution.py:48
  141.8 15.3 %collective-permute-done.10 = bf16[1536,128]{1,0:T(8,128)(2,1)} collective-permute-done((bf16[1536,128]{1,0:T(8,128)(2,1)}, bf16[1536,128]{1,0:T(8,128)(2,1)}, u32[]{:S(2)}, u32[]{:S(2)}) %collective-permute-start.10) | collective-permute-done | bytes 393248 | tf_op jit(solution)/shard_map/ppermute | solution.py:48
  157.1 1.4 add_add_fusion.1.first_ref
  158.6 1.4 convolution_add_fusion.1
  160.2 7.0 %collective-permute-done.12.second_ref = bf16[1536,128]{1,0:T(8,128)(2,1)S(1)} collective-permute-done((bf16[1536,128]{1,0:T(8,128)(2,1)S(1)}, bf16[1536,128]{1,0:T(8,128)(2,1)S(1)}, u32[]{:S(2)}, u32[]{:S(2)}) %collective-permute-start.12) | collective-permute-done | bytes 393248 | tf_op jit(solution)/shard_map/ppermute | solution.py:48
  167.5 1.4 fusion.2
  168.9 1.6 collective-permute-start.13
  170.7 2.6 %collective-permute-done.13.got_ref = f32[128,128]{1,0:T(8,128)S(1)} collective-permute-done((f32[128,128]{1,0:T(8,128)S(1)}, f32[128,128]{1,0:T(8,128)S(1)}, u32[]{:S(2)}, u32[]{:S(2)}) %collective-permute-start.13) | collective-permute-done | bytes 65568 | tf_op jit(solution)/shard_map/ppermute | solution.py:451
  173.3 0.9 shard_map.76
  174.2 3.4 %all-to-all-start.4 = ((bf16[8,32,512]{2,1,0:T(8,128)(2,1)}), bf16[8,32,512]{2,1,0:T(8,128)(2,1)S(1)}, u32[]{:S(2)}, u32[]{:S(2)}) async-start(bf16[8,32,512]{2,1,0:T(8,128)(2,1)} %bitcast.20), calls=%async_computation.4 | async-start | bytes 524288 | tf_op jit(solution)/shard_map/all_to_all | solution.py:456
  178.0 1.5 add_add_fusion.partial_ref
  179.5 4.1 %all-to-all-done.4 = bf16[8,32,512]{2,1,0:T(8,128)(2,1)S(1)} async-done(((bf16[8,32,512]{2,1,0:T(8,128)(2,1)}), bf16[8,32,512]{2,1,0:T(8,128)(2,1)S(1)}, u32[]{:S(2)}, u32[]{:S(2)}) %all-to-all-start.4) | async-done | bytes 262176 | tf_op jit(solution)/shard_map/all_to_all | solution.py:456
  183.6 1.1 shard_map.77
  (89 shorter events, 9.1 us)
Async XLA Ops:
  3.3 2.2 %copy-start = (bf16[4,128,4096]{2,1,0:T(8,128)(2,1)S(1)}, bf16[4,128,4096]{2,1,0:T(8,128)(2,1)}, u32[]{:S(2)}) copy-start(bf16[4,128,4096]{2,1,0:T(8,128)(2,1)} %param.7) | copy-start | bytes 12582916
  5.5 9.8 %copy-start.13 = (s32[128]{0:T(128)S(1)}, s32[128]{0:T(128)}, u32[]{:S(2)}) copy-start(s32[128]{0:T(128)} %param.11) | copy-start | bytes 1540
  5.5 9.8 %copy-start.14 = (s32[4,4]{1,0:T(4,128)S(1)}, s32[4,4]{1,0:T(4,128)}, u32[]{:S(2)}) copy-start(s32[4,4]{1,0:T(4,128)} %param.13) | copy-start | bytes 196
  5.5 11.9 %copy-start.5 = (bf16[512,512]{1,0:T(8,128)(2,1)S(1)}, bf16[512,512]{1,0:T(8,128)(2,1)}, u32[]{:S(2)}) copy-start(bf16[512,512]{1,0:T(8,128)(2,1)} %expand_ref.1) | copy-start | bytes 1572868
  10.0 26.0 %all-to-all-start = ((bf16[8,32,3072]{2,1,0:T(8,128)(2,1)}), bf16[8,32,3072]{2,1,0:T(8,128)(2,1)S(1)}, u32[]{:S(2)}, u32[]{:S(2)}) async-start(bf16[8,32,3072]{2,1,0:T(8,128)(2,1)} %bitcast.7), calls=%async_computation | async-start | bytes 3145728 | tf_op jit(solution)/shard_map/all_to_all | solution.py:313
  17.4 2.2 %copy-start.2 = (bf16[4096,512]{1,0:T(8,128)(2,1)S(1)}, bf16[4096,512]{1,0:T(8,128)(2,1)}, u32[]{:S(2)}) copy-start(bf16[4096,512]{1,0:T(8,128)(2,1)} %store_ref) | copy-start | bytes 12582916
  29.2 5.6 %copy-start.4 = (bf16[4608,512]{1,0:T(8,128)(2,1)}, bf16[4608,512]{1,0:T(8,128)(2,1)S(1)}, u32[]{:S(2)}) copy-start(bf16[4608,512]{1,0:T(8,128)(2,1)S(1)} %get-tuple-element.81) | copy-start | bytes 14155780
  29.2 5.6 %collective-permute-start = (bf16[1536,512]{1,0:T(8,128)(2,1)S(1)}, bf16[1536,512]{1,0:T(8,128)(2,1)S(1)}, u32[]{:S(2)}, u32[]{:S(2)}) collective-permute-start(bf16[1536,512]{1,0:T(8,128)(2,1)S(1)} %get-tuple-element.58), channel_id=1, source_target_pairs={{0,1},{1,0},{2,3},{3,2},{4,5},{5,4},{6,7},{7,6},{8,9},{9,8},{10,11... | collective-permute-start | bytes 4718600 | tf_op jit(solution)/shard_map/ppermute | solution.py:48
  29.7 42.9 %collective-permute-start.2 = (bf16[3072,512]{1,0:T(8,128)(2,1)}, bf16[3072,512]{1,0:T(8,128)(2,1)}, u32[]{:S(2)}, u32[]{:S(2)}) collective-permute-start(bf16[3072,512]{1,0:T(8,128)(2,1)} %get-tuple-element.63), channel_id=1, source_target_pairs={{0,1},{1,0},{2,3},{3,2},{4,5},{5,4},{6,7},{7,6},{8,9},{9,8},{10,11... | collective-permute-start | bytes 9437192 | tf_op jit(solution)/shard_map/ppermute | solution.py:48
  34.8 1.2 copy-start.10
  36.1 1.2 copy-start.8
  37.2 12.7 %all-to-all-start.1 = ((bf16[8,32,1024]{2,1,0:T(8,128)(2,1)}), bf16[8,32,1024]{2,1,0:T(8,128)(2,1)S(1)}, u32[]{:S(2)}, u32[]{:S(2)}) async-start(bf16[8,32,1024]{2,1,0:T(8,128)(2,1)} %bitcast.9), calls=%async_computation.1 | async-start | bytes 1048576 | tf_op jit(solution)/shard_map/all_to_all | solution.py:313
  40.7 31.9 %collective-permute-start.1 = (bf16[1536,256]{1,0:T(8,128)(2,1)S(1)}, bf16[1536,256]{1,0:T(8,128)(2,1)S(1)}, u32[]{:S(2)}, u32[]{:S(2)}) collective-permute-start(bf16[1536,256]{1,0:T(8,128)(2,1)S(1)} %slice_add_fusion), channel_id=1, source_target_pairs={{0,2},{2,0},{1,3},{3,1},{4,6},{6,4},{5,7},{7,5},{8,10},{10,8},{9,1... | collective-permute-start | bytes 2359304 | tf_op jit(solution)/shard_map/ppermute | solution.py:48
  50.0 26.9 %copy-start.6 = (bf16[8,32,1024]{2,1,0:T(8,128)(2,1)}, bf16[8,32,1024]{2,1,0:T(8,128)(2,1)S(1)}, u32[]{:S(2)}) copy-start(bf16[8,32,1024]{2,1,0:T(8,128)(2,1)S(1)} %all-to-all-done.1) | copy-start | bytes 1572868
  50.0 46.0 %all-to-all-start.2 = ((bf16[16,8,4224]{2,1,0:T(8,128)(2,1)}), bf16[16,8,4224]{2,1,0:T(8,128)(2,1)}, u32[]{:S(2)}, u32[]{:S(2)}) async-start(bf16[16,8,4224]{2,1,0:T(8,128)(2,1)} %bitcast.8), calls=%async_computation.2 | async-start | bytes 2162688 | tf_op jit(solution)/shard_map/all_to_all | solution.py:371
  72.6 4.2 %copy-start.11 = (bf16[1536,256]{1,0:T(8,128)(2,1)}, bf16[1536,256]{1,0:T(8,128)(2,1)S(1)}, u32[]{:S(2)}) copy-start(bf16[1536,256]{1,0:T(8,128)(2,1)S(1)} %collective-permute-done.1) | copy-start | bytes 2359300
  74.3 21.6 %collective-permute-start.3 = (bf16[1536,256]{1,0:T(8,128)(2,1)S(1)}, bf16[1536,256]{1,0:T(8,128)(2,1)}, u32[]{:S(2)}, u32[]{:S(2)}) collective-permute-start(bf16[1536,256]{1,0:T(8,128)(2,1)S(1)} %slice_add_fusion.2), channel_id=1, source_target_pairs={{0,2},{2,0},{1,3},{3,1},{4,6},{6,4},{5,7},{7,5},{8,10},{10,8},{9,1... | collective-permute-start | bytes 2359304 | tf_op jit(solution)/shard_map/ppermute | solution.py:48
  76.4 12.5 %collective-permute-start.4 = (bf16[1536,128]{1,0:T(8,128)(2,1)}, bf16[1536,128]{1,0:T(8,128)(2,1)}, u32[]{:S(2)}, u32[]{:S(2)}) collective-permute-start(bf16[1536,128]{1,0:T(8,128)(2,1)} %fusion.11), channel_id=1, source_target_pairs={{0,4},{4,0},{1,5},{5,1},{2,6},{6,2},{3,7},{7,3},{8,12},{12,8},{9,1... | collective-permute-start | bytes 1179656 | tf_op jit(solution)/shard_map/ppermute | solution.py:48
  76.8 2.2 %copy-start.1 = (bf16[4,128,4096]{2,1,0:T(8,128)(2,1)S(1)}, bf16[4,128,4096]{2,1,0:T(8,128)(2,1)}, u32[]{:S(2)}) copy-start(bf16[4,128,4096]{2,1,0:T(8,128)(2,1)} %param.7) | copy-start | bytes 12582916
  95.9 10.5 %copy-start.3 = (bf16[4096,512]{1,0:T(8,128)(2,1)S(1)}, bf16[4096,512]{1,0:T(8,128)(2,1)}, u32[]{:S(2)}) copy-start(bf16[4096,512]{1,0:T(8,128)(2,1)} %store_ref) | copy-start | bytes 12582916
  97.5 22.1 %collective-permute-start.5 = (bf16[1536,256]{1,0:T(8,128)(2,1)S(1)}, bf16[1536,256]{1,0:T(8,128)(2,1)S(1)}, u32[]{:S(2)}, u32[]{:S(2)}) collective-permute-start(bf16[1536,256]{1,0:T(8,128)(2,1)S(1)} %slice_add_fusion.1), channel_id=1, source_target_pairs={{0,2},{2,0},{1,3},{3,1},{4,6},{6,4},{5,7},{7,5},{8,10},{10,8},{9,1... | collective-permute-start | bytes 2359304 | tf_op jit(solution)/shard_map/ppermute | solution.py:48
  99.1 9.4 %copy-start.12 = (bf16[1536,128]{1,0:T(8,128)(2,1)}, bf16[1536,128]{1,0:T(8,128)(2,1)S(1)}, u32[]{:S(2)}) copy-start(bf16[1536,128]{1,0:T(8,128)(2,1)S(1)} %fusion.10) | copy-start | bytes 1179652
  100.5 19.1 %collective-permute-start.6 = (bf16[1536,128]{1,0:T(8,128)(2,1)S(1)}, bf16[1536,128]{1,0:T(8,128)(2,1)S(1)}, u32[]{:S(2)}, u32[]{:S(2)}) collective-permute-start(bf16[1536,128]{1,0:T(8,128)(2,1)S(1)} %slice_add_fusion.6), channel_id=1, source_target_pairs={{0,4},{4,0},{1,5},{5,1},{2,6},{6,2},{3,7},{7,3},{8,12},{12,8},{9,1... | collective-permute-start | bytes 1179656 | tf_op jit(solution)/shard_map/ppermute | solution.py:48
  101.6 18.0 %collective-permute-start.7 = (bf16[1536,128]{1,0:T(8,128)(2,1)S(1)}, bf16[1536,128]{1,0:T(8,128)(2,1)S(1)}, u32[]{:S(2)}, u32[]{:S(2)}) collective-permute-start(bf16[1536,128]{1,0:T(8,128)(2,1)S(1)} %fusion.10), channel_id=1, source_target_pairs={{0,8},{8,0},{1,9},{9,1},{2,10},{10,2},{3,11},{11,3},{4,12},{12,4},... | collective-permute-start | bytes 1179656 | tf_op jit(solution)/shard_map/ppermute | solution.py:48
  108.5 9.3 %collective-permute-start.8 = (f32[128,512]{1,0:T(8,128)S(1)}, f32[128,512]{1,0:T(8,128)S(1)}, u32[]{:S(2)}, u32[]{:S(2)}) collective-permute-start(f32[128,512]{1,0:T(8,128)S(1)} %convolution_select_fusion), channel_id=1, source_target_pairs={{0,16},{16,0},{1,17},{17,1},{2,18},{18,2},{3,19},{19,3},{4,20},{20... | collective-permute-start | bytes 786440 | tf_op jit(solution)/shard_map/ppermute | solution.py:31
  110.1 27.0 %collective-permute-start.11 = (f32[512,512]{1,0:T(8,128)S(1)}, f32[512,512]{1,0:T(8,128)}, u32[]{:S(2)}, u32[]{:S(2)}) collective-permute-start(f32[512,512]{1,0:T(8,128)S(1)} %get-tuple-element.88), channel_id=1, source_target_pairs={{0,16},{16,0},{1,17},{17,1},{2,18},{18,2},{3,19},{19,3},{4,20},{20... | collective-permute-start | bytes 3145736 | tf_op jit(solution)/shard_map/ppermute | solution.py:48
  119.7 2.3 %copy-start.15 = (bf16[1536,128]{1,0:T(8,128)(2,1)}, bf16[1536,128]{1,0:T(8,128)(2,1)S(1)}, u32[]{:S(2)}) copy-start(bf16[1536,128]{1,0:T(8,128)(2,1)S(1)} %collective-permute-done.7) | copy-start | bytes 1179652
  123.9 17.9 %collective-permute-start.9 = (bf16[1536,128]{1,0:T(8,128)(2,1)}, bf16[1536,128]{1,0:T(8,128)(2,1)}, u32[]{:S(2)}, u32[]{:S(2)}) collective-permute-start(bf16[1536,128]{1,0:T(8,128)(2,1)} %slice_add_fusion.5), channel_id=1, source_target_pairs={{0,4},{4,0},{1,5},{5,1},{2,6},{6,2},{3,7},{7,3},{8,12},{12,8},{9,1... | collective-permute-start | bytes 1179656 | tf_op jit(solution)/shard_map/ppermute | solution.py:48
  126.4 30.7 %collective-permute-start.10 = (bf16[1536,128]{1,0:T(8,128)(2,1)}, bf16[1536,128]{1,0:T(8,128)(2,1)}, u32[]{:S(2)}, u32[]{:S(2)}) collective-permute-start(bf16[1536,128]{1,0:T(8,128)(2,1)} %add_add_fusion.2), channel_id=1, source_target_pairs={{0,8},{8,0},{1,9},{9,1},{2,10},{10,2},{3,11},{11,3},{4,12},{12,4},... | collective-permute-start | bytes 1179656 | tf_op jit(solution)/shard_map/ppermute | solution.py:48
  130.0 44.2 %all-to-all-start.3 = ((bf16[16,8,512]{2,1,0:T(8,128)(2,1)}), bf16[16,8,512]{2,1,0:T(8,128)(2,1)S(1)}, u32[]{:S(2)}, u32[]{:S(2)}) async-start(bf16[16,8,512]{2,1,0:T(8,128)(2,1)} %fusion), calls=%async_computation.3 | async-start | bytes 262144 | tf_op jit(solution)/shard_map/all_to_all | solution.py:402
  133.7 24.9 %copy-start.9 = (bf16[8,32,3072]{2,1,0:T(8,128)(2,1)S(1)}, bf16[8,32,3072]{2,1,0:T(8,128)(2,1)}, u32[]{:S(2)}) copy-start(bf16[8,32,3072]{2,1,0:T(8,128)(2,1)} %copy-done.8) | copy-start | bytes 4718596
  133.7 26.2 %copy-start.7 = (bf16[8,32,1024]{2,1,0:T(8,128)(2,1)S(1)}, bf16[8,32,1024]{2,1,0:T(8,128)(2,1)}, u32[]{:S(2)}) copy-start(bf16[8,32,1024]{2,1,0:T(8,128)(2,1)} %copy-done.6) | copy-start | bytes 1572868
  158.5 8.7 %collective-permute-start.12 = (bf16[1536,128]{1,0:T(8,128)(2,1)S(1)}, bf16[1536,128]{1,0:T(8,128)(2,1)S(1)}, u32[]{:S(2)}, u32[]{:S(2)}) collective-permute-start(bf16[1536,128]{1,0:T(8,128)(2,1)S(1)} %add_add_fusion.1.first_ref), channel_id=1, source_target_pairs={{0,8},{8,0},{1,9},{9,1},{2,10},{10,2},{3,11},{11,3},{4,12},{12,4},... | collective-permute-start | bytes 1179656 | tf_op jit(solution)/shard_map/ppermute | solution.py:48
  168.9 4.3 %collective-permute-start.13 = (f32[128,128]{1,0:T(8,128)S(1)}, f32[128,128]{1,0:T(8,128)S(1)}, u32[]{:S(2)}, u32[]{:S(2)}) collective-permute-start(f32[128,128]{1,0:T(8,128)S(1)} %fusion.20.own_ref), channel_id=1, source_target_pairs={{0,16},{16,0},{1,17},{17,1},{2,18},{18,2},{3,19},{19,3},{4,20},{20... | collective-permute-start | bytes 196616 | tf_op jit(solution)/shard_map/ppermute | solution.py:451
  174.2 9.4 %all-to-all-start.4 = ((bf16[8,32,512]{2,1,0:T(8,128)(2,1)}), bf16[8,32,512]{2,1,0:T(8,128)(2,1)S(1)}, u32[]{:S(2)}, u32[]{:S(2)}) async-start(bf16[8,32,512]{2,1,0:T(8,128)(2,1)} %bitcast.20), calls=%async_computation.4 | async-start | bytes 524288 | tf_op jit(solution)/shard_map/all_to_all | solution.py:456

commit v15 on v11

--- a/solution.py
+++ b/solution.py
@@ -51,10 +51,10 @@
         self.last = after(self.last, *arrived)
 
 
-def kernel_params(flops=1, bytes_accessed=1):
+def kernel_params():
     return dict(
         compiler_params=pltpu.CompilerParams(vmem_limit_bytes=40 * 2**20),
-        cost_estimate=pl.CostEstimate(flops=flops, bytes_accessed=bytes_accessed, transcendentals=0),
+        cost_estimate=pl.CostEstimate(flops=1, bytes_accessed=1, transcendentals=0),
     )
 
 
@@ -155,7 +155,7 @@
         out_specs=pl.BlockSpec((placed_rows, width), lambda j: (0, j)),
         out_shape=jax.ShapeDtypeStruct((placed_rows, depth), jnp.bfloat16),
         scratch_shapes=[pltpu.VMEM((placed_rows, count), jnp.bfloat16)],
-        **kernel_params(2 * placed_rows * count * depth, 2 * (placed_rows + count) * depth),
+        **kernel_params(),
     )(target[None], rows)
 
 
@@ -264,25 +264,20 @@
     names = jnp.arange(adapter_count, dtype=jnp.int32)
     chain = Chain()
 
-    cold_row = jnp.sum(jnp.where((token_adapter - hot_count)[:, :, None] == names, adapter_row, 0), axis=-1)
-    is_hot = token_adapter < hot_count
-    is_cold = (token_adapter < none_code) & jnp.logical_not(is_hot)
-    owner = cold_row // per_dev
-    group = jnp.where(is_hot, token_adapter, jnp.where(is_cold, hot_count + owner, -1))
-    at = jnp.arange(token_count, dtype=jnp.int32)
-    before = (group[:, :, None] == group[:, None, :]) & (at[None, :] < at[:, None])
-    rank = jnp.sum(before.astype(jnp.int32), axis=-1)
-    step_at = jnp.arange(step_count, dtype=jnp.int32)[:, None]
     hot_rows = hot_count * step_count * HCAP
     cold_rows = dp_count * step_count * CAP
+    step_at = jnp.arange(step_count, dtype=jnp.int32)[:, None]
+    at = jnp.arange(token_count, dtype=jnp.int32)
+
+    def rank_in(group):
+        before = (group[:, :, None] == group[:, None, :]) & (at[None, :] < at[:, None])
+        return jnp.sum(before.astype(jnp.int32), axis=-1)
+
+    is_hot = token_adapter < hot_count
     server = (step_at // near) * hot_count + token_adapter
-    hot_target = (server * near + step_at % near) * HCAP + rank
-    cold_target = (owner * step_count + step_at) * CAP + rank
+    hot_target = (server * near + step_at % near) * HCAP + rank_in(token_adapter)
     hot_target = jnp.where(is_hot, hot_target, -1).reshape(-1)
-    cold_target = jnp.where(is_cold, cold_target, -1).reshape(-1)
-
-    hot_out = place_rows(rows, hot_target, hot_rows)
-    hot_out = chain.hold(hot_out.reshape(group_count, near * HCAP, depth))
+    hot_out = chain.hold(place_rows(rows, hot_target, hot_rows).reshape(group_count, near * HCAP, depth))
     done = {"hot_in": lax.all_to_all(hot_out, GROUP, split_axis=0, concat_axis=0, tiled=True)}
 
     hot_row = jnp.sum(jnp.where(hot_ids[:, :, None] == names, adapter_row, 0), axis=-1)
@@ -332,9 +327,15 @@
     rest_swapped = chain.permute(other_rest, "core", SWAP)
     send(0, 0)
 
+    codes = after(token_adapter, chain.last)
+    cold_row = jnp.sum(jnp.where((codes - hot_count)[:, :, None] == names, adapter_row, 0), axis=-1)
+    is_cold = (codes < none_code) & (codes >= hot_count)
+    owner = cold_row // per_dev
+    cold_target = (owner * step_count + step_at) * CAP + rank_in(jnp.where(is_cold, owner, -1))
+    cold_target = jnp.where(is_cold, cold_target, -1).reshape(-1)
+
     def cold_tokens_out():
-        cold_at = after(cold_target, chain.last)
-        cold_hit = jnp.arange(cold_rows, dtype=jnp.int32)[:, None] == cold_at
+        cold_hit = jnp.arange(cold_rows, dtype=jnp.int32)[:, None] == cold_target
         tag = jnp.sum(jnp.where(cold_hit, (cold_row % per_dev + 1).reshape(-1), 0), axis=-1)
         tag = jnp.broadcast_to(tag.astype(jnp.bfloat16)[:, None], (cold_rows, TAG))
         packet = jnp.concatenate([narrow(pick(cold_hit), rows), tag], axis=1)
@@ -381,12 +382,12 @@
         done["partial"] = partial + done["base_own"] + done["base_got"]
 
     between = {
-        0: [cold_tokens_out, base_product],
-        2: [base_over_tp],
-        3: [cold_shrink, cold_over_tp],
+        0: [cold_tokens_out],
+        1: [base_product],
+        2: [cold_shrink, cold_over_tp, base_over_tp],
         4: [cold_expand, cold_back, all_but_hot],
     }
-    awaited = {0: ["base_own", "base_other"], 2: ["packet"], 3: ["z_cold", "base_got"]}
+    awaited = {0: ["hot_in"], 1: ["packet", "base_own", "base_other"], 2: ["z_cold"], 3: ["base_got"]}
     for slot in range(chunk_count + len(hops) - 1):
         if slot > 0:
             if slot < chunk_count:

time: 192 us -> 184 us (0.958)
  waiting for transfers between devices: 85.1 us -> 80.4 us
  starting transfers between devices: 39.4 us -> 36.4 us
  local copies, waits for them, and re-layouts: 7 us -> 9.21 us
  Pallas kernels: 23.6 us -> 21.4 us
  matrix products: 12.7 us -> 14.7 us
    ppermute x12, waiting for transfers between devices: 77.9 us -> 48.3 us  [permute(): return lax.ppermute(self.hold(value), axis, pairs)]
    all_to_all x1, waiting for transfers between devices: 0.01 us -> 17.8 us  [on_device(): lax.all_to_all(hot_out, GROUP, split_axis=0, concat_axis=0, tiled=True)]
    ppermute x1, waiting for transfers between devices: 0.43 us -> 7.21 us  [sum_over_tp(): return part + lax.ppermute(part, 'tp', SWAP)]
    all_to_all x1, starting transfers between devices: 9.5 us -> 5.04 us  [cold_tokens_out(): packet = lax.all_to_all(packet, DP, split_axis=0, concat_axis=0, tiled=True)]
    all_to_all x1, starting transfers between devices: 4.52 us -> 7.43 us  [on_device(): lax.all_to_all(hot_out, GROUP, split_axis=0, concat_axis=0, tiled=True)]
    unnamed x22 -> x24, local copies, waits for them, and re-layouts: 6.09 us -> 8.3 us
    dot_general x9, matrix products: 12.3 us -> 14.3 us  [matmul(): return jnp.dot(a, b, preferred_element_type=jnp.float32)]
  transfers between devices with their start and end apart: 18 -> 18, of which waited for: 13 -> 11; matrix products, arithmetic and copies ran while one was open for 15% -> 16% of each run, Pallas kernels for 6% -> 6%
where the time goes in v15:
time: 184 us
  waiting for transfers between devices  80.4 us (44%)
  starting transfers between devices  36.4 us (20%)
  Pallas kernels  21.4 us (12%)
  other arithmetic  21.2 us (12%)
  matrix products  14.7 us (8%)
  local copies, waits for them, and re-layouts  9.21 us (5%)
    ppermute x12, waiting for transfers between devices, permute(): return lax.ppermute(self.hold(value), axis, pairs)  48.3 us
    all_to_all x1, waiting for transfers between devices, on_device(): lax.all_to_all(hot_out, GROUP, split_axis=0, concat_axis=0, tiled=True)  17.8 us
    dot_general x9, matrix products, matmul(): return jnp.dot(a, b, preferred_element_type=jnp.float32)  14.3 us
    ppermute x12, starting transfers between devices, permute(): return lax.ppermute(self.hold(value), axis, pairs)  13.9 us
    pallas_call x1, Pallas kernels, base_halves(): pl.pallas_call(kernel, grid_spec=pltpu.PrefetchScalarGridSpec(num_scalar_...  9.89 us
    unnamed x24, local copies, waits for them, and re-layouts  8.3 us
    all_to_all x1, starting transfers between devices, on_device(): lax.all_to_all(hot_out, GROUP, split_axis=0, concat_axis=0, tiled=True)  7.43 us
    ppermute x1, waiting for transfers between devices, sum_over_tp(): return part + lax.ppermute(part, 'tp', SWAP)  7.21 us
  transfers between devices with their start and end apart: 18, of which 11 were waited for; matrix products, arithmetic and copies ran while one was open for 16% of the time, Pallas kernels for 6%

profile of v15, /device:TPU:0, one launch (start us, length us, event | category | flops | bytes accessed | tf_op | source)
XLA Modules:
  0.0 183.7 jit_solution(3404831193561176456)
XLA Ops:
  4.6 2.2 %copy-done = bf16[4,128,4096]{2,1,0:T(8,128)(2,1)S(1)} copy-done((bf16[4,128,4096]{2,1,0:T(8,128)(2,1)S(1)}, bf16[4,128,4096]{2,1,0:T(8,128)(2,1)}, u32[]{:S(2)}) %copy-start) | copy-done | bytes 4194328
  6.8 3.3 %shard_map.73 = bf16[256,4096]{1,0:T(8,128)(2,1)} custom-call(s32[1,512]{1,0:T(1,128)S(1)} %bitcast.50, bf16[512,4096]{1,0:T(8,128)(2,1)S(1)} %bitcast.47), custom_call_target="tpu_custom_call" | custom-call | flops 1 | bytes 1 | tf_op jit(solution)/shard_map/pallas_call | solution.py:151
  10.1 6.2 %shard_map.74 = (bf16[4608,512]{1,0:T(8,128)(2,1)S(1)}, bf16[1536,512]{1,0:T(8,128)(2,1)S(1)}, bf16[3072,512]{1,0:T(8,128)(2,1)S(1)}) custom-call(s32[4]{0:T(128)S(1)} %convert_element_type.31.mine_held, s32[4]{0:T(128)S(1)} %convert_element_type.32.other_held, s32[1,512]{1,0:T(1,128)S(1)} %bitcast.52, s32[1,512]{1,0:T(1,128)S(1)} %bitcast.53, ...), custom_call_target="tpu_custom_call" | custom-call | flops 1 | bytes 1 | tf_op jit(solution)/shard_map/pallas_call | solution.py:108
  16.3 2.1 %copy-done.4 = bf16[4608,512]{1,0:T(8,128)(2,1)} copy-done((bf16[4608,512]{1,0:T(8,128)(2,1)}, bf16[4608,512]{1,0:T(8,128)(2,1)S(1)}, u32[]{:S(2)}) %copy-start.4) | copy-done | bytes 4718616
  18.4 1.8 copy-done.6
  20.7 7.4 %all-to-all-start = ((bf16[8,32,4096]{2,1,0:T(8,128)(2,1)}), bf16[8,32,4096]{2,1,0:T(8,128)(2,1)}, u32[]{:S(2)}, u32[]{:S(2)}) async-start(bf16[8,32,4096]{2,1,0:T(8,128)(2,1)} %bitcast.4), calls=%async_computation | async-start | bytes 4194304 | tf_op jit(solution)/shard_map/all_to_all | solution.py:281
  28.6 1.5 slice_add_fusion
  30.0 1.7 collective-permute-start.1
  32.5 2.9 %convolution_convert_fusion = bf16[128,4096]{1,0:T(8,128)(2,1)S(1)} fusion(bf16[512,4096]{1,0:T(8,128)(2,1)} %bitcast.46, s32[512]{0:T(512)S(1)} %select_bitcast_fusion), kind=kOutput, calls=%fused_computation | convolution fusion | flops 537460736 | bytes 5244928 | tf_op jit(solution)/shard_map/dot_general | solution.py:22
  36.5 17.8 %all-to-all-done = bf16[8,32,4096]{2,1,0:T(8,128)(2,1)} async-done(((bf16[8,32,4096]{2,1,0:T(8,128)(2,1)}), bf16[8,32,4096]{2,1,0:T(8,128)(2,1)}, u32[]{:S(2)}, u32[]{:S(2)}) %all-to-all-start) | async-done | bytes 2097184 | tf_op jit(solution)/shard_map/all_to_all | solution.py:281
  54.4 5.0 %all-to-all-start.1 = ((bf16[16,8,4224]{2,1,0:T(8,128)(2,1)}), bf16[16,8,4224]{2,1,0:T(8,128)(2,1)}, u32[]{:S(2)}, u32[]{:S(2)}) async-start(bf16[16,8,4224]{2,1,0:T(8,128)(2,1)} %maximum_bitcast_fusion), calls=%async_computation.1 | async-start | bytes 2162688 | tf_op jit(solution)/shard_map/all_to_all | solution.py:343
  59.4 17.5 %collective-permute-done.1 = bf16[1536,256]{1,0:T(8,128)(2,1)S(1)} collective-permute-done((bf16[1536,256]{1,0:T(8,128)(2,1)S(1)}, bf16[1536,256]{1,0:T(8,128)(2,1)S(1)}, u32[]{:S(2)}, u32[]{:S(2)}) %collective-permute-start.1) | collective-permute-done | bytes 786464 | tf_op jit(solution)/shard_map/ppermute | solution.py:48
  76.9 1.7 slice_add_fusion.2
  78.7 2.0 %fusion.13 = bf16[1536,128]{1,0:T(8,128)(2,1)} fusion(bf16[1536,512]{1,0:T(8,128)(2,1)} %collective-permute-done, bf16[1536,256]{1,0:T(8,128)(2,1)S(1)} %collective-permute-done.1, bf16[4608,512]{1,0:T(8,128)(2,1)} %copy-done.4), kind=kLoop, calls=%fused_computation.27 | loop fusion | flops 393216 | bytes 1572864 | tf_op jit(solution)/shard_map/add | solution.py:313
  81.7 2.2 %copy-done.1 = bf16[4,128,4096]{2,1,0:T(8,128)(2,1)S(1)} copy-done((bf16[4,128,4096]{2,1,0:T(8,128)(2,1)S(1)}, bf16[4,128,4096]{2,1,0:T(8,128)(2,1)}, u32[]{:S(2)}) %copy-start.1) | copy-done | bytes 4194328
  83.9 9.9 %shard_map.75 = (f32[512,512]{1,0:T(8,128)S(1)}, f32[512,512]{1,0:T(8,128)S(1)}) custom-call(s32[1]{0:T(128)} %bitcast.9.tp_at, bf16[512,4096]{1,0:T(8,128)(2,1)S(1)} %bitcast.48, bf16[4096,1024]{1,0:T(8,128)(2,1)} %weight_ref), custom_call_target="tpu_custom_call" | custom-call | flops 1 | bytes 1 | tf_op jit(solution)/shard_map/pallas_call | solution.py:189
  93.8 6.2 %collective-permute-done.3 = bf16[1536,256]{1,0:T(8,128)(2,1)} collective-permute-done((bf16[1536,256]{1,0:T(8,128)(2,1)S(1)}, bf16[1536,256]{1,0:T(8,128)(2,1)}, u32[]{:S(2)}, u32[]{:S(2)}) %collective-permute-start.3) | collective-permute-done | bytes 786464 | tf_op jit(solution)/shard_map/ppermute | solution.py:48
  100.0 1.6 slice_add_fusion.1
  101.7 1.4 fusion.12
  103.1 1.3 slice_add_fusion.6
  104.4 1.2 collective-permute-start.6
  105.6 4.1 %collective-permute-start.7 = (bf16[1536,128]{1,0:T(8,128)(2,1)S(1)}, bf16[1536,128]{1,0:T(8,128)(2,1)S(1)}, u32[]{:S(2)}, u32[]{:S(2)}) collective-permute-start(bf16[1536,128]{1,0:T(8,128)(2,1)S(1)} %fusion.12), channel_id=1, source_target_pairs={{0,8},{8,0},{1,9},{9,1},{2,10},{10,2},{3,11},{11,3},{4,12},{12,4},... | collective-permute-start | bytes 1179656 | tf_op jit(solution)/shard_map/ppermute | solution.py:48
  110.5 1.9 %convolution_select_fusion = f32[128,512]{1,0:T(8,128)S(1)} fusion(bf16[4096,512]{1,0:T(8,128)(2,1)S(1)} %copy-done.3, bf16[128,4224]{1,0:T(8,128)(2,1)} %bitcast.8, s32[512]{0:T(512)S(1)} %fusion.28, s32[128]{0:T(128)S(1)} %convert_reduce_fusion.2), kind=kOutput, calls=%fused_computation.1 | convolution fusion | flops 537001984 | bytes 5507584 | tf_op jit(solution)/shard_map/dot_general | solution.py:22
  112.5 1.6 collective-permute-start.8
  114.6 7.2 %collective-permute-done.8 = f32[128,512]{1,0:T(8,128)S(1)} collective-permute-done((f32[128,512]{1,0:T(8,128)S(1)}, f32[128,512]{1,0:T(8,128)S(1)}, u32[]{:S(2)}, u32[]{:S(2)}) %collective-permute-start.8) | collective-permute-done | bytes 262176 | tf_op jit(solution)/shard_map/ppermute | solution.py:31
  121.8 1.7 collective-permute-done.6
  123.5 2.4 %collective-permute-done.7 = bf16[1536,128]{1,0:T(8,128)(2,1)S(1)} collective-permute-done((bf16[1536,128]{1,0:T(8,128)(2,1)S(1)}, bf16[1536,128]{1,0:T(8,128)(2,1)S(1)}, u32[]{:S(2)}, u32[]{:S(2)}) %collective-permute-start.7) | collective-permute-done | bytes 393248 | tf_op jit(solution)/shard_map/ppermute | solution.py:48
  125.9 1.3 add_add_fusion.1
  127.3 1.2 slice_add_fusion.5
  128.5 3.1 %collective-permute-start.9 = (bf16[1536,128]{1,0:T(8,128)(2,1)S(1)}, bf16[1536,128]{1,0:T(8,128)(2,1)S(1)}, u32[]{:S(2)}, u32[]{:S(2)}) collective-permute-start(bf16[1536,128]{1,0:T(8,128)(2,1)S(1)} %slice_add_fusion.5), channel_id=1, source_target_pairs={{0,4},{4,0},{1,5},{5,1},{2,6},{6,2},{3,7},{7,3},{8,12},{12,8},{9,1... | collective-permute-start | bytes 1179656 | tf_op jit(solution)/shard_map/ppermute | solution.py:48
  131.6 1.5 fusion.5
  133.1 1.5 convolution_add_fusion.3
  134.6 1.5 convolution_add_fusion.2
  136.1 5.4 %collective-permute-done.11 = f32[512,512]{1,0:T(8,128)S(1)} collective-permute-done((f32[512,512]{1,0:T(8,128)S(1)}, f32[512,512]{1,0:T(8,128)S(1)}, u32[]{:S(2)}, u32[]{:S(2)}) %collective-permute-start.11) | collective-permute-done | bytes 1048608 | tf_op jit(solution)/shard_map/ppermute | solution.py:48
  141.5 4.0 %collective-permute-done.9 = bf16[1536,128]{1,0:T(8,128)(2,1)S(1)} collective-permute-done((bf16[1536,128]{1,0:T(8,128)(2,1)S(1)}, bf16[1536,128]{1,0:T(8,128)(2,1)S(1)}, u32[]{:S(2)}, u32[]{:S(2)}) %collective-permute-start.9) | collective-permute-done | bytes 393248 | tf_op jit(solution)/shard_map/ppermute | solution.py:48
  145.5 1.2 add_add_fusion.2.first_ref
  146.7 1.2 collective-permute-start.12
  148.8 3.9 %all-to-all-start.2 = ((bf16[16,8,512]{2,1,0:T(8,128)(2,1)}), bf16[16,8,512]{2,1,0:T(8,128)(2,1)S(1)}, u32[]{:S(2)}, u32[]{:S(2)}) async-start(bf16[16,8,512]{2,1,0:T(8,128)(2,1)} %fusion), calls=%async_computation.2 | async-start | bytes 262144 | tf_op jit(solution)/shard_map/all_to_all | solution.py:374
  152.7 1.3 fusion.9
  154.0 1.5 fusion.1
  155.5 11.0 %collective-permute-done.12.second_ref = bf16[1536,128]{1,0:T(8,128)(2,1)S(1)} collective-permute-done((bf16[1536,128]{1,0:T(8,128)(2,1)S(1)}, bf16[1536,128]{1,0:T(8,128)(2,1)S(1)}, u32[]{:S(2)}, u32[]{:S(2)}) %collective-permute-start.12) | collective-permute-done | bytes 393248 | tf_op jit(solution)/shard_map/ppermute | solution.py:48
  166.5 1.3 convolution_add_fusion
  167.9 1.2 collective-permute-start.13
  169.2 3.0 %collective-permute-done.13.got_ref = f32[128,128]{1,0:T(8,128)S(1)} collective-permute-done((f32[128,128]{1,0:T(8,128)S(1)}, f32[128,128]{1,0:T(8,128)S(1)}, u32[]{:S(2)}, u32[]{:S(2)}) %collective-permute-start.13) | collective-permute-done | bytes 65568 | tf_op jit(solution)/shard_map/ppermute | solution.py:422
  173.2 3.4 %all-to-all-start.3 = ((bf16[8,32,512]{2,1,0:T(8,128)(2,1)}), bf16[8,32,512]{2,1,0:T(8,128)(2,1)S(1)}, u32[]{:S(2)}, u32[]{:S(2)}) async-start(bf16[8,32,512]{2,1,0:T(8,128)(2,1)} %bitcast.17), calls=%async_computation.3 | async-start | bytes 524288 | tf_op jit(solution)/shard_map/all_to_all | solution.py:427
  177.0 1.5 add_add_fusion.partial_ref
  178.5 4.1 %all-to-all-done.3 = bf16[8,32,512]{2,1,0:T(8,128)(2,1)S(1)} async-done(((bf16[8,32,512]{2,1,0:T(8,128)(2,1)}), bf16[8,32,512]{2,1,0:T(8,128)(2,1)S(1)}, u32[]{:S(2)}, u32[]{:S(2)}) %all-to-all-start.3) | async-done | bytes 262176 | tf_op jit(solution)/shard_map/all_to_all | solution.py:427
  182.6 1.1 shard_map.77
  (86 shorter events, 12.3 us)
Async XLA Ops:
  4.6 2.2 %copy-start = (bf16[4,128,4096]{2,1,0:T(8,128)(2,1)S(1)}, bf16[4,128,4096]{2,1,0:T(8,128)(2,1)}, u32[]{:S(2)}) copy-start(bf16[4,128,4096]{2,1,0:T(8,128)(2,1)} %param.7) | copy-start | bytes 12582916
  6.8 3.3 %copy-start.2 = (bf16[4096,512]{1,0:T(8,128)(2,1)S(1)}, bf16[4096,512]{1,0:T(8,128)(2,1)}, u32[]{:S(2)}) copy-start(bf16[4096,512]{1,0:T(8,128)(2,1)} %store_ref) | copy-start | bytes 12582916
  6.8 3.3 %copy-start.5 = (bf16[512,512]{1,0:T(8,128)(2,1)S(1)}, bf16[512,512]{1,0:T(8,128)(2,1)}, u32[]{:S(2)}) copy-start(bf16[512,512]{1,0:T(8,128)(2,1)} %expand_ref.1) | copy-start | bytes 1572868
  16.3 2.1 %copy-start.4 = (bf16[4608,512]{1,0:T(8,128)(2,1)}, bf16[4608,512]{1,0:T(8,128)(2,1)S(1)}, u32[]{:S(2)}) copy-start(bf16[4608,512]{1,0:T(8,128)(2,1)S(1)} %get-tuple-element.72) | copy-start | bytes 14155780
  18.4 1.8 copy-start.6
  20.2 8.4 %collective-permute-start = (bf16[1536,512]{1,0:T(8,128)(2,1)S(1)}, bf16[1536,512]{1,0:T(8,128)(2,1)}, u32[]{:S(2)}, u32[]{:S(2)}) collective-permute-start(bf16[1536,512]{1,0:T(8,128)(2,1)S(1)} %get-tuple-element.52), channel_id=1, source_target_pairs={{0,1},{1,0},{2,3},{3,2},{4,5},{5,4},{6,7},{7,6},{8,9},{9,8},{10,11... | collective-permute-start | bytes 4718600 | tf_op jit(solution)/shard_map/ppermute | solution.py:48
  20.7 33.7 %all-to-all-start = ((bf16[8,32,4096]{2,1,0:T(8,128)(2,1)}), bf16[8,32,4096]{2,1,0:T(8,128)(2,1)}, u32[]{:S(2)}, u32[]{:S(2)}) async-start(bf16[8,32,4096]{2,1,0:T(8,128)(2,1)} %bitcast.4), calls=%async_computation | async-start | bytes 4194304 | tf_op jit(solution)/shard_map/all_to_all | solution.py:281
  28.1 3.7 %copy-start.10 = (s32[4,128]{1,0:T(4,128)S(1)}, s32[4,128]{1,0:T(4,128)}, u32[]{:S(2)}) copy-start(s32[4,128]{1,0:T(4,128)} %param.12) | copy-start | bytes 6148
  28.1 3.7 %copy-start.11 = (s32[128]{0:T(128)S(1)}, s32[128]{0:T(128)}, u32[]{:S(2)}) copy-start(s32[128]{0:T(128)} %param.11) | copy-start | bytes 1540
  28.1 48.8 %collective-permute-start.2 = (bf16[3072,512]{1,0:T(8,128)(2,1)}, bf16[3072,512]{1,0:T(8,128)(2,1)}, u32[]{:S(2)}, u32[]{:S(2)}) collective-permute-start(bf16[3072,512]{1,0:T(8,128)(2,1)} %copy-done.6), channel_id=1, source_target_pairs={{0,1},{1,0},{2,3},{3,2},{4,5},{5,4},{6,7},{7,6},{8,9},{9,8},{10,11... | collective-permute-start | bytes 9437192 | tf_op jit(solution)/shard_map/ppermute | solution.py:48
  30.0 46.8 %collective-permute-start.1 = (bf16[1536,256]{1,0:T(8,128)(2,1)S(1)}, bf16[1536,256]{1,0:T(8,128)(2,1)S(1)}, u32[]{:S(2)}, u32[]{:S(2)}) collective-permute-start(bf16[1536,256]{1,0:T(8,128)(2,1)S(1)} %slice_add_fusion), channel_id=1, source_target_pairs={{0,2},{2,0},{1,3},{3,1},{4,6},{6,4},{5,7},{7,5},{8,10},{10,8},{9,1... | collective-permute-start | bytes 2359304 | tf_op jit(solution)/shard_map/ppermute | solution.py:48
  54.4 39.4 %all-to-all-start.1 = ((bf16[16,8,4224]{2,1,0:T(8,128)(2,1)}), bf16[16,8,4224]{2,1,0:T(8,128)(2,1)}, u32[]{:S(2)}, u32[]{:S(2)}) async-start(bf16[16,8,4224]{2,1,0:T(8,128)(2,1)} %maximum_bitcast_fusion), calls=%async_computation.1 | async-start | bytes 2162688 | tf_op jit(solution)/shard_map/all_to_all | solution.py:343
  76.9 4.8 %copy-start.8 = (bf16[1536,256]{1,0:T(8,128)(2,1)}, bf16[1536,256]{1,0:T(8,128)(2,1)S(1)}, u32[]{:S(2)}) copy-start(bf16[1536,256]{1,0:T(8,128)(2,1)S(1)} %collective-permute-done.1) | copy-start | bytes 2359300
  78.6 21.4 %collective-permute-start.3 = (bf16[1536,256]{1,0:T(8,128)(2,1)S(1)}, bf16[1536,256]{1,0:T(8,128)(2,1)}, u32[]{:S(2)}, u32[]{:S(2)}) collective-permute-start(bf16[1536,256]{1,0:T(8,128)(2,1)S(1)} %slice_add_fusion.2), channel_id=1, source_target_pairs={{0,2},{2,0},{1,3},{3,1},{4,6},{6,4},{5,7},{7,5},{8,10},{10,8},{9,1... | collective-permute-start | bytes 2359304 | tf_op jit(solution)/shard_map/ppermute | solution.py:48
  80.7 13.1 %collective-permute-start.4 = (bf16[1536,128]{1,0:T(8,128)(2,1)}, bf16[1536,128]{1,0:T(8,128)(2,1)}, u32[]{:S(2)}, u32[]{:S(2)}) collective-permute-start(bf16[1536,128]{1,0:T(8,128)(2,1)} %fusion.13), channel_id=1, source_target_pairs={{0,4},{4,0},{1,5},{5,1},{2,6},{6,2},{3,7},{7,3},{8,12},{12,8},{9,1... | collective-permute-start | bytes 1179656 | tf_op jit(solution)/shard_map/ppermute | solution.py:48
  81.7 2.2 %copy-start.1 = (bf16[4,128,4096]{2,1,0:T(8,128)(2,1)S(1)}, bf16[4,128,4096]{2,1,0:T(8,128)(2,1)}, u32[]{:S(2)}) copy-start(bf16[4,128,4096]{2,1,0:T(8,128)(2,1)} %param.7) | copy-start | bytes 12582916
  93.8 7.9 %copy-start.9 = (bf16[1536,256]{1,0:T(8,128)(2,1)S(1)}, bf16[1536,256]{1,0:T(8,128)(2,1)}, u32[]{:S(2)}) copy-start(bf16[1536,256]{1,0:T(8,128)(2,1)} %copy-done.8) | copy-start | bytes 2359300
  100.0 10.5 %copy-start.3 = (bf16[4096,512]{1,0:T(8,128)(2,1)S(1)}, bf16[4096,512]{1,0:T(8,128)(2,1)}, u32[]{:S(2)}) copy-start(bf16[4096,512]{1,0:T(8,128)(2,1)} %store_ref) | copy-start | bytes 12582916
  101.6 24.3 %collective-permute-start.5 = (bf16[1536,256]{1,0:T(8,128)(2,1)S(1)}, bf16[1536,256]{1,0:T(8,128)(2,1)S(1)}, u32[]{:S(2)}, u32[]{:S(2)}) collective-permute-start(bf16[1536,256]{1,0:T(8,128)(2,1)S(1)} %slice_add_fusion.1), channel_id=1, source_target_pairs={{0,2},{2,0},{1,3},{3,1},{4,6},{6,4},{5,7},{7,5},{8,10},{10,8},{9,1... | collective-permute-start | bytes 2359304 | tf_op jit(solution)/shard_map/ppermute | solution.py:48
  104.4 19.1 %collective-permute-start.6 = (bf16[1536,128]{1,0:T(8,128)(2,1)S(1)}, bf16[1536,128]{1,0:T(8,128)(2,1)S(1)}, u32[]{:S(2)}, u32[]{:S(2)}) collective-permute-start(bf16[1536,128]{1,0:T(8,128)(2,1)S(1)} %slice_add_fusion.6), channel_id=1, source_target_pairs={{0,4},{4,0},{1,5},{5,1},{2,6},{6,2},{3,7},{7,3},{8,12},{12,8},{9,1... | collective-permute-start | bytes 1179656 | tf_op jit(solution)/shard_map/ppermute | solution.py:48
  105.6 20.3 %collective-permute-start.7 = (bf16[1536,128]{1,0:T(8,128)(2,1)S(1)}, bf16[1536,128]{1,0:T(8,128)(2,1)S(1)}, u32[]{:S(2)}, u32[]{:S(2)}) collective-permute-start(bf16[1536,128]{1,0:T(8,128)(2,1)S(1)} %fusion.12), channel_id=1, source_target_pairs={{0,8},{8,0},{1,9},{9,1},{2,10},{10,2},{3,11},{11,3},{4,12},{12,4},... | collective-permute-start | bytes 1179656 | tf_op jit(solution)/shard_map/ppermute | solution.py:48
  112.5 9.3 %collective-permute-start.8 = (f32[128,512]{1,0:T(8,128)S(1)}, f32[128,512]{1,0:T(8,128)S(1)}, u32[]{:S(2)}, u32[]{:S(2)}) collective-permute-start(f32[128,512]{1,0:T(8,128)S(1)} %convolution_select_fusion), channel_id=1, source_target_pairs={{0,16},{16,0},{1,17},{17,1},{2,18},{18,2},{3,19},{19,3},{4,20},{20... | collective-permute-start | bytes 786440 | tf_op jit(solution)/shard_map/ppermute | solution.py:31
  114.1 27.4 %collective-permute-start.11 = (f32[512,512]{1,0:T(8,128)S(1)}, f32[512,512]{1,0:T(8,128)S(1)}, u32[]{:S(2)}, u32[]{:S(2)}) collective-permute-start(f32[512,512]{1,0:T(8,128)S(1)} %get-tuple-element.79), channel_id=1, source_target_pairs={{0,16},{16,0},{1,17},{17,1},{2,18},{18,2},{3,19},{19,3},{4,20},{20... | collective-permute-start | bytes 3145736 | tf_op jit(solution)/shard_map/ppermute | solution.py:48
  127.3 18.2 %collective-permute-start.10 = (bf16[1536,128]{1,0:T(8,128)(2,1)S(1)}, bf16[1536,128]{1,0:T(8,128)(2,1)S(1)}, u32[]{:S(2)}, u32[]{:S(2)}) collective-permute-start(bf16[1536,128]{1,0:T(8,128)(2,1)S(1)} %add_add_fusion.1), channel_id=1, source_target_pairs={{0,8},{8,0},{1,9},{9,1},{2,10},{10,2},{3,11},{11,3},{4,12},{12,4},... | collective-permute-start | bytes 1179656 | tf_op jit(solution)/shard_map/ppermute | solution.py:48
  128.5 16.9 %collective-permute-start.9 = (bf16[1536,128]{1,0:T(8,128)(2,1)S(1)}, bf16[1536,128]{1,0:T(8,128)(2,1)S(1)}, u32[]{:S(2)}, u32[]{:S(2)}) collective-permute-start(bf16[1536,128]{1,0:T(8,128)(2,1)S(1)} %slice_add_fusion.5), channel_id=1, source_target_pairs={{0,4},{4,0},{1,5},{5,1},{2,6},{6,2},{3,7},{7,3},{8,12},{12,8},{9,1... | collective-permute-start | bytes 1179656 | tf_op jit(solution)/shard_map/ppermute | solution.py:48
  141.5 4.0 %copy-start.7 = (f32[512,512]{1,0:T(8,128)}, f32[512,512]{1,0:T(8,128)S(1)}, u32[]{:S(2)}) copy-start(f32[512,512]{1,0:T(8,128)S(1)} %collective-permute-done.11) | copy-start | bytes 3145732
  146.7 19.8 %collective-permute-start.12 = (bf16[1536,128]{1,0:T(8,128)(2,1)S(1)}, bf16[1536,128]{1,0:T(8,128)(2,1)S(1)}, u32[]{:S(2)}, u32[]{:S(2)}) collective-permute-start(bf16[1536,128]{1,0:T(8,128)(2,1)S(1)} %add_add_fusion.2.first_ref), channel_id=1, source_target_pairs={{0,8},{8,0},{1,9},{9,1},{2,10},{10,2},{3,11},{11,3},{4,12},{12,4},... | collective-permute-start | bytes 1179656 | tf_op jit(solution)/shard_map/ppermute | solution.py:48
  148.8 24.4 %all-to-all-start.2 = ((bf16[16,8,512]{2,1,0:T(8,128)(2,1)}), bf16[16,8,512]{2,1,0:T(8,128)(2,1)S(1)}, u32[]{:S(2)}, u32[]{:S(2)}) async-start(bf16[16,8,512]{2,1,0:T(8,128)(2,1)} %fusion), calls=%async_computation.2 | async-start | bytes 262144 | tf_op jit(solution)/shard_map/all_to_all | solution.py:374
  167.9 4.3 %collective-permute-start.13 = (f32[128,128]{1,0:T(8,128)S(1)}, f32[128,128]{1,0:T(8,128)S(1)}, u32[]{:S(2)}, u32[]{:S(2)}) collective-permute-start(f32[128,128]{1,0:T(8,128)S(1)} %fusion.21.own_ref), channel_id=1, source_target_pairs={{0,16},{16,0},{1,17},{17,1},{2,18},{18,2},{3,19},{19,3},{4,20},{20... | collective-permute-start | bytes 196616 | tf_op jit(solution)/shard_map/ppermute | solution.py:422
  173.2 9.4 %all-to-all-start.3 = ((bf16[8,32,512]{2,1,0:T(8,128)(2,1)}), bf16[8,32,512]{2,1,0:T(8,128)(2,1)S(1)}, u32[]{:S(2)}, u32[]{:S(2)}) async-start(bf16[8,32,512]{2,1,0:T(8,128)(2,1)} %bitcast.17), calls=%async_computation.3 | async-start | bytes 524288 | tf_op jit(solution)/shard_map/all_to_all | solution.py:427

commit v16 on v14

--- a/solution.py
+++ b/solution.py
@@ -140,7 +140,7 @@
     blocks = 4
     width = depth // blocks
 
-    def kernel(hot_at, cold_at, tag_at, rows_ref, early_ref, late_ref, cold_ref, place_hot, place_cold):
+    def kernel(hot_at, cold_at, tag_at, rows_ref, hot_ref, cold_ref, place_hot, place_cold):
         step = pl.program_id(0)
 
         @pl.when(step == 0)
@@ -153,16 +153,8 @@
             cold_ref[:, depth:] = jnp.broadcast_to(tags, (cold_rows, TAG)).astype(jnp.bfloat16)
 
         block = rows_ref[...]
-        placed = narrow(place_hot[...], block)
+        hot_ref[...] = narrow(place_hot[...], block)
         cold_ref[:, pl.ds(pl.multiple_of(step * width, 128), width)] = narrow(place_cold[...], block)
-
-        @pl.when(step < blocks - 1)
-        def _():
-            early_ref[...] = placed
-
-        @pl.when(step == blocks - 1)
-        def _():
-            late_ref[...] = placed
 
     index = pl.BlockSpec((1, count), lambda j: (0, 0))
     return pl.pallas_call(
@@ -170,13 +162,11 @@
         grid=(blocks,),
         in_specs=[index, index, index, pl.BlockSpec((count, width), lambda j: (0, j))],
         out_specs=[
-            pl.BlockSpec((hot_rows, width), lambda j: (0, jnp.minimum(j, blocks - 2))),
-            pl.BlockSpec((hot_rows, width), lambda j: (0, 0)),
+            pl.BlockSpec((hot_rows, width), lambda j: (0, j)),
             pl.BlockSpec((cold_rows, depth + TAG), lambda j: (0, 0)),
         ],
         out_shape=[
-            jax.ShapeDtypeStruct((hot_rows, depth - width), jnp.bfloat16),
-            jax.ShapeDtypeStruct((hot_rows, width), jnp.bfloat16),
+            jax.ShapeDtypeStruct((hot_rows, depth), jnp.bfloat16),
             jax.ShapeDtypeStruct((cold_rows, depth + TAG), jnp.bfloat16),
         ],
         scratch_shapes=[pltpu.VMEM((hot_rows, count), jnp.bfloat16), pltpu.VMEM((cold_rows, count), jnp.bfloat16)],
@@ -306,16 +296,11 @@
     hot_target = jnp.where(is_hot, hot_target, -1).reshape(-1)
     cold_target = jnp.where(is_cold, cold_target, -1).reshape(-1)
 
-    early = 3 * depth // 4
-
-    def exchange(block):
-        block = chain.hold(block.reshape(group_count, near * HCAP, -1))
-        return lax.all_to_all(block, GROUP, split_axis=0, concat_axis=0, tiled=True).reshape(hot_rows, -1)
-
-    hot_first_part, hot_last_part, packet = place_rows(
+    hot_out, packet = place_rows(
         rows, hot_target, cold_target, (cold_row % per_dev + 1).reshape(-1), hot_rows, cold_rows
     )
-    hot_early = exchange(hot_first_part)
+    hot_out = chain.hold(hot_out.reshape(group_count, near * HCAP, depth))
+    done = {"hot_in": lax.all_to_all(hot_out, GROUP, split_axis=0, concat_axis=0, tiled=True)}
 
     hot_row = jnp.sum(jnp.where(hot_ids[:, :, None] == names, adapter_row, 0), axis=-1)
     hot_first = jnp.where(hot_row // per_dev == me, (hot_row % per_dev) * R, -R * per_dev)
@@ -362,9 +347,7 @@
     )
     mine[0], swapped[0] = mine_all[:part], chain.permute(other_first, "core", SWAP)
     rest_swapped = chain.permute(other_rest, "core", SWAP)
-    first, hot_early = lax.optimization_barrier((operand(0, 0), hot_early))
-    got[0, 0] = chain.permute(first, *hops[0])
-    done = {"hot_late": exchange(hot_last_part)}
+    send(0, 0)
 
     def cold_tokens_out():
         sent = chain.hold(packet.reshape(dp_count, step_count * CAP, depth + TAG))
@@ -413,10 +396,9 @@
         0: [cold_tokens_out],
         1: [base_product],
         2: [cold_shrink, cold_over_tp, base_over_tp],
-        3: [cold_expand, cold_back],
-        4: [all_but_hot],
+        4: [cold_expand, cold_back, all_but_hot],
     }
-    awaited = {0: ["hot_late"], 1: ["packet", "base_own", "base_other"], 2: ["z_cold"], 3: ["base_got"]}
+    awaited = {0: ["hot_in"], 1: ["packet", "base_own", "base_other"], 2: ["z_cold"], 3: ["base_got"]}
     for slot in range(chunk_count + len(hops) - 1):
         if slot > 0:
             if slot < chunk_count:
@@ -437,12 +419,12 @@
         done.update(zip(names_here, arrived[1 + len(here):]))
     partial = done["partial"]
 
+    hot_in = done["hot_in"].reshape(hot_rows, depth)
     dense = None
     for c in range(chunk_count):
         last = min((c + 1) * part, depth)
-        hot_in = hot_early[:, c * part:last] if last <= early else done["hot_late"]
         for piece in (held[c], got[c, len(hops) - 1]):
-            product = matmul(hot_in, piece[:last - c * part])
+            product = matmul(hot_in[:, c * part:last], piece[:last - c * part])
             dense = product if dense is None else dense + product
     dense = dense.reshape(group_count, near, HCAP, kept)
     at_step = jnp.arange(kept) // R

time: 185 us -> 171 us (0.924)
  Pallas kernels: 26 us -> 21.3 us
  waiting for transfers between devices: 79.2 us -> 75.2 us
  other arithmetic: 21.1 us -> 18.7 us
    pallas_call x1, Pallas kernels: 9.57 us -> 5.44 us  [pick_columns(): pl.pallas_call(kernel, grid_spec=pltpu.PrefetchScalarGridSpec(num_scalar_...]
    all_to_all x2 -> x1, starting transfers between devices: 8.72 us -> 5.37 us  [on_device(): lax.all_to_all(hot_out, GROUP, split_axis=0, concat_axis=0, tiled=True)]
    all_to_all x2 -> x1, waiting for transfers between devices: 7.19 us -> 4.54 us  [on_device(): lax.all_to_all(hot_out, GROUP, split_axis=0, concat_axis=0, tiled=True)]
    unnamed x32 -> x28, local copies, waits for them, and re-layouts: 8.93 us -> 7.62 us
  transfers between devices with their start and end apart: 19 -> 18, of which waited for: 11 -> 12; matrix products, arithmetic and copies ran while one was open for 15% -> 13% of each run, Pallas kernels for 11% -> 10%
where the time goes in v16:
time: 171 us; the launch traced here: 169 us
  waiting for transfers between devices  75.2 us (44%)
  starting transfers between devices  36.9 us (22%)
  Pallas kernels  21.3 us (12%)
  other arithmetic  18.7 us (11%)
  local copies, waits for them, and re-layouts  8.45 us (5%)
  matrix products  8.45 us (5%)
    ppermute x12, waiting for transfers between devices, permute(): return lax.ppermute(self.hold(value), axis, pairs)  56.7 us
    ppermute x12, starting transfers between devices, permute(): return lax.ppermute(self.hold(value), axis, pairs)  15.4 us
    pallas_call x1, Pallas kernels, base_halves(): pl.pallas_call(kernel, grid_spec=pltpu.PrefetchScalarGridSpec(num_scalar_...  9.89 us
    dot_general x8, matrix products, matmul(): return jnp.dot(a, b, preferred_element_type=jnp.float32)  8.1 us
    unnamed x28, local copies, waits for them, and re-layouts  7.62 us
    ppermute x1, waiting for transfers between devices, sum_over_tp(): return part + lax.ppermute(part, 'tp', SWAP)  7.21 us
    pallas_call x1, Pallas kernels, pick_columns(): pl.pallas_call(kernel, grid_spec=pltpu.PrefetchScalarGridSpec(num_scalar_...  5.44 us
    all_to_all x1, starting transfers between devices, on_device(): lax.all_to_all(hot_out, GROUP, split_axis=0, concat_axis=0, tiled=True)  5.37 us
  transfers between devices with their start and end apart: 18, of which 12 were waited for; matrix products, arithmetic and copies ran while one was open for 13% of the time, Pallas kernels for 10%

profile of v16, /device:TPU:0, one launch (start us, length us, event | category | flops | bytes accessed | tf_op | source)
XLA Modules:
  0.0 169.3 jit_solution(10305608272808842199)
XLA Ops:
  0.7 0.9 select_reduce_fusion
  3.3 2.2 %copy-done = bf16[4,128,4096]{2,1,0:T(8,128)(2,1)S(1)} copy-done((bf16[4,128,4096]{2,1,0:T(8,128)(2,1)S(1)}, bf16[4,128,4096]{2,1,0:T(8,128)(2,1)}, u32[]{:S(2)}) %copy-start) | copy-done | bytes 4194328
  5.5 3.9 %shard_map.73 = (bf16[256,4096]{1,0:T(8,128)(2,1)}, bf16[128,4224]{1,0:T(8,128)(2,1)}) custom-call(s32[1,512]{1,0:T(1,128)S(1)} %bitcast.46, s32[1,512]{1,0:T(1,128)S(1)} %bitcast.44, s32[1,512]{1,0:T(1,128)S(1)} %fusion.28.tag_at, bf16[512,4096]{1,0:T(8,128)(2,1)S(1)} %bitcast.41), custom_call_target="tpu_custom_call" | custom-call | flops 1 | bytes 1 | tf_op jit(solution)/shard_map/pallas_call | solution.py:160
  9.4 5.4 %all-to-all-start = ((bf16[8,32,4096]{2,1,0:T(8,128)(2,1)}), bf16[8,32,4096]{2,1,0:T(8,128)(2,1)S(1)}, u32[]{:S(2)}, u32[]{:S(2)}) async-start(bf16[8,32,4096]{2,1,0:T(8,128)(2,1)} %bitcast.7), calls=%async_computation | async-start | bytes 4194304 | tf_op jit(solution)/shard_map/all_to_all | solution.py:303
  17.0 2.2 %copy-done.2 = bf16[4096,512]{1,0:T(8,128)(2,1)S(1)} copy-done((bf16[4096,512]{1,0:T(8,128)(2,1)S(1)}, bf16[4096,512]{1,0:T(8,128)(2,1)}, u32[]{:S(2)}) %copy-start.2) | copy-done | bytes 4194328
  19.2 5.4 %shard_map.74 = (bf16[4608,512]{1,0:T(8,128)(2,1)S(1)}, bf16[1536,512]{1,0:T(8,128)(2,1)S(1)}, bf16[3072,512]{1,0:T(8,128)(2,1)}) custom-call(s32[4]{0:T(128)S(1)} %convert_element_type.18.mine_held, s32[4]{0:T(128)S(1)} %convert_element_type.19.other_held, s32[1,512]{1,0:T(1,128)S(1)} %bitcast.48, s32[1,512]{1,0:T(1,128)S(1)} %bitcast.49, ...), custom_call_target="tpu_custom_call" | custom-call | flops 1 | bytes 1 | tf_op jit(solution)/shard_map/pallas_call | solution.py:108
  25.1 7.4 %collective-permute-done = bf16[1536,512]{1,0:T(8,128)(2,1)S(1)} collective-permute-done((bf16[1536,512]{1,0:T(8,128)(2,1)S(1)}, bf16[1536,512]{1,0:T(8,128)(2,1)S(1)}, u32[]{:S(2)}, u32[]{:S(2)}) %collective-permute-start) | collective-permute-done | bytes 1572896 | tf_op jit(solution)/shard_map/ppermute | solution.py:48
  32.6 3.8 %collective-permute-start.1 = (bf16[1536,256]{1,0:T(8,128)(2,1)S(1)}, bf16[1536,256]{1,0:T(8,128)(2,1)}, u32[]{:S(2)}, u32[]{:S(2)}) collective-permute-start(bf16[1536,256]{1,0:T(8,128)(2,1)S(1)} %slice_add_fusion), channel_id=1, source_target_pairs={{0,2},{2,0},{1,3},{3,1},{4,6},{6,4},{5,7},{7,5},{8,10},{10,8},{9,1... | collective-permute-start | bytes 2359304 | tf_op jit(solution)/shard_map/ppermute | solution.py:48
  36.4 4.5 %all-to-all-done = bf16[8,32,4096]{2,1,0:T(8,128)(2,1)S(1)} async-done(((bf16[8,32,4096]{2,1,0:T(8,128)(2,1)}), bf16[8,32,4096]{2,1,0:T(8,128)(2,1)S(1)}, u32[]{:S(2)}, u32[]{:S(2)}) %all-to-all-start) | async-done | bytes 2097184 | tf_op jit(solution)/shard_map/all_to_all | solution.py:303
  41.0 4.9 %all-to-all-start.1 = ((bf16[16,8,4224]{2,1,0:T(8,128)(2,1)}), bf16[16,8,4224]{2,1,0:T(8,128)(2,1)}, u32[]{:S(2)}, u32[]{:S(2)}) async-start(bf16[16,8,4224]{2,1,0:T(8,128)(2,1)} %bitcast.8), calls=%async_computation.1 | async-start | bytes 2162688 | tf_op jit(solution)/shard_map/all_to_all | solution.py:354
  45.9 17.8 %collective-permute-done.1 = bf16[1536,256]{1,0:T(8,128)(2,1)} collective-permute-done((bf16[1536,256]{1,0:T(8,128)(2,1)S(1)}, bf16[1536,256]{1,0:T(8,128)(2,1)}, u32[]{:S(2)}, u32[]{:S(2)}) %collective-permute-start.1) | collective-permute-done | bytes 786464 | tf_op jit(solution)/shard_map/ppermute | solution.py:48
  63.7 1.5 slice_add_fusion.2
  65.2 1.6 collective-permute-start.3
  66.8 2.0 %fusion.13 = bf16[1536,128]{1,0:T(8,128)(2,1)} fusion(bf16[1536,512]{1,0:T(8,128)(2,1)} %copy-done.10, bf16[1536,256]{1,0:T(8,128)(2,1)} %collective-permute-done.1, bf16[4608,512]{1,0:T(8,128)(2,1)} %copy-done.4), kind=kLoop, calls=%fused_computation.25 | loop fusion | flops 393216 | bytes 1572864 | tf_op jit(solution)/shard_map/add | solution.py:335
  68.9 2.2 %copy-done.1 = bf16[4,128,4096]{2,1,0:T(8,128)(2,1)S(1)} copy-done((bf16[4,128,4096]{2,1,0:T(8,128)(2,1)S(1)}, bf16[4,128,4096]{2,1,0:T(8,128)(2,1)}, u32[]{:S(2)}) %copy-start.1) | copy-done | bytes 4194328
  71.0 9.9 %shard_map.75 = (f32[512,512]{1,0:T(8,128)S(1)}, f32[512,512]{1,0:T(8,128)S(1)}) custom-call(s32[1]{0:T(128)} %bitcast.10.tp_at, bf16[512,4096]{1,0:T(8,128)(2,1)S(1)} %bitcast.42, bf16[4096,1024]{1,0:T(8,128)(2,1)} %weight_ref), custom_call_target="tpu_custom_call" | custom-call | flops 1 | bytes 1 | tf_op jit(solution)/shard_map/pallas_call | solution.py:204
  80.9 1.0 copy-done.6
  82.0 4.6 %collective-permute-done.3 = bf16[1536,256]{1,0:T(8,128)(2,1)} collective-permute-done((bf16[1536,256]{1,0:T(8,128)(2,1)S(1)}, bf16[1536,256]{1,0:T(8,128)(2,1)}, u32[]{:S(2)}, u32[]{:S(2)}) %collective-permute-start.3) | collective-permute-done | bytes 786464 | tf_op jit(solution)/shard_map/ppermute | solution.py:48
  86.6 1.5 slice_add_fusion.1
  88.1 1.4 fusion.12
  89.5 1.3 slice_add_fusion.6
  90.9 1.4 collective-permute-start.6
  92.3 3.3 %collective-permute-start.7 = (bf16[1536,128]{1,0:T(8,128)(2,1)S(1)}, bf16[1536,128]{1,0:T(8,128)(2,1)S(1)}, u32[]{:S(2)}, u32[]{:S(2)}) collective-permute-start(bf16[1536,128]{1,0:T(8,128)(2,1)S(1)} %fusion.12), channel_id=1, source_target_pairs={{0,8},{8,0},{1,9},{9,1},{2,10},{10,2},{3,11},{11,3},{4,12},{12,4},... | collective-permute-start | bytes 1179656 | tf_op jit(solution)/shard_map/ppermute | solution.py:48
  96.4 2.0 %convolution_select_fusion = f32[128,512]{1,0:T(8,128)S(1)} fusion(bf16[4096,512]{1,0:T(8,128)(2,1)S(1)} %copy-done.3, bf16[128,4224]{1,0:T(8,128)(2,1)} %bitcast.9, s32[512]{0:T(512)S(1)} %fusion.25, s32[128]{0:T(128)S(1)} %convert_reduce_fusion.1), kind=kOutput, calls=%fused_computation | convolution fusion | flops 537001984 | bytes 5507584 | tf_op jit(solution)/shard_map/dot_general | solution.py:22
  98.5 1.6 collective-permute-start.8
  100.6 7.2 %collective-permute-done.8 = f32[128,512]{1,0:T(8,128)S(1)} collective-permute-done((f32[128,512]{1,0:T(8,128)S(1)}, f32[128,512]{1,0:T(8,128)S(1)}, u32[]{:S(2)}, u32[]{:S(2)}) %collective-permute-start.8) | collective-permute-done | bytes 262176 | tf_op jit(solution)/shard_map/ppermute | solution.py:31
  107.8 2.3 %collective-permute-done.6 = bf16[1536,128]{1,0:T(8,128)(2,1)S(1)} collective-permute-done((bf16[1536,128]{1,0:T(8,128)(2,1)S(1)}, bf16[1536,128]{1,0:T(8,128)(2,1)S(1)}, u32[]{:S(2)}, u32[]{:S(2)}) %collective-permute-start.6) | collective-permute-done | bytes 393248 | tf_op jit(solution)/shard_map/ppermute | solution.py:48
  110.1 1.9 %collective-permute-done.7 = bf16[1536,128]{1,0:T(8,128)(2,1)S(1)} collective-permute-done((bf16[1536,128]{1,0:T(8,128)(2,1)S(1)}, bf16[1536,128]{1,0:T(8,128)(2,1)S(1)}, u32[]{:S(2)}, u32[]{:S(2)}) %collective-permute-start.7) | collective-permute-done | bytes 393248 | tf_op jit(solution)/shard_map/ppermute | solution.py:48
  112.0 1.4 add_add_fusion.1
  113.7 1.2 slice_add_fusion.5
  114.9 2.8 %collective-permute-start.9 = (bf16[1536,128]{1,0:T(8,128)(2,1)S(1)}, bf16[1536,128]{1,0:T(8,128)(2,1)S(1)}, u32[]{:S(2)}, u32[]{:S(2)}) collective-permute-start(bf16[1536,128]{1,0:T(8,128)(2,1)S(1)} %slice_add_fusion.5), channel_id=1, source_target_pairs={{0,4},{4,0},{1,5},{5,1},{2,6},{6,2},{3,7},{7,3},{8,12},{12,8},{9,1... | collective-permute-start | bytes 1179656 | tf_op jit(solution)/shard_map/ppermute | solution.py:48
  118.8 8.1 %collective-permute-done.11 = f32[512,512]{1,0:T(8,128)S(1)} collective-permute-done((f32[512,512]{1,0:T(8,128)S(1)}, f32[512,512]{1,0:T(8,128)S(1)}, u32[]{:S(2)}, u32[]{:S(2)}) %collective-permute-start.11) | collective-permute-done | bytes 1048608 | tf_op jit(solution)/shard_map/ppermute | solution.py:48
  126.9 4.7 %collective-permute-done.9 = bf16[1536,128]{1,0:T(8,128)(2,1)S(1)} collective-permute-done((bf16[1536,128]{1,0:T(8,128)(2,1)S(1)}, bf16[1536,128]{1,0:T(8,128)(2,1)S(1)}, u32[]{:S(2)}, u32[]{:S(2)}) %collective-permute-start.9) | collective-permute-done | bytes 393248 | tf_op jit(solution)/shard_map/ppermute | solution.py:48
  131.6 1.2 add_add_fusion.2.first_ref
  132.8 1.0 collective-permute-start.12
  133.8 0.9 fusion
  134.7 4.6 %all-to-all-start.2 = ((bf16[16,8,512]{2,1,0:T(8,128)(2,1)}), bf16[16,8,512]{2,1,0:T(8,128)(2,1)S(1)}, u32[]{:S(2)}, u32[]{:S(2)}) async-start(bf16[16,8,512]{2,1,0:T(8,128)(2,1)} %fusion), calls=%async_computation.2 | async-start | bytes 262144 | tf_op jit(solution)/shard_map/all_to_all | solution.py:385
  139.3 1.3 fusion.9
  140.7 1.5 fusion.1
  142.1 10.0 %collective-permute-done.12.second_ref = bf16[1536,128]{1,0:T(8,128)(2,1)S(1)} collective-permute-done((bf16[1536,128]{1,0:T(8,128)(2,1)S(1)}, bf16[1536,128]{1,0:T(8,128)(2,1)S(1)}, u32[]{:S(2)}, u32[]{:S(2)}) %collective-permute-start.12) | collective-permute-done | bytes 393248 | tf_op jit(solution)/shard_map/ppermute | solution.py:48
  152.2 1.3 convolution_add_fusion
  153.5 1.6 collective-permute-start.13
  155.3 2.6 %collective-permute-done.13.got_ref = f32[128,128]{1,0:T(8,128)S(1)} collective-permute-done((f32[128,128]{1,0:T(8,128)S(1)}, f32[128,128]{1,0:T(8,128)S(1)}, u32[]{:S(2)}, u32[]{:S(2)}) %collective-permute-start.13) | collective-permute-done | bytes 65568 | tf_op jit(solution)/shard_map/ppermute | solution.py:433
  157.9 0.9 shard_map.76
  158.8 3.4 %all-to-all-start.3 = ((bf16[8,32,512]{2,1,0:T(8,128)(2,1)}), bf16[8,32,512]{2,1,0:T(8,128)(2,1)S(1)}, u32[]{:S(2)}, u32[]{:S(2)}) async-start(bf16[8,32,512]{2,1,0:T(8,128)(2,1)} %bitcast.18), calls=%async_computation.3 | async-start | bytes 524288 | tf_op jit(solution)/shard_map/all_to_all | solution.py:438
  162.6 1.5 add_add_fusion.partial_ref
  164.1 4.1 %all-to-all-done.3 = bf16[8,32,512]{2,1,0:T(8,128)(2,1)S(1)} async-done(((bf16[8,32,512]{2,1,0:T(8,128)(2,1)}), bf16[8,32,512]{2,1,0:T(8,128)(2,1)S(1)}, u32[]{:S(2)}, u32[]{:S(2)}) %all-to-all-start.3) | async-done | bytes 262176 | tf_op jit(solution)/shard_map/all_to_all | solution.py:438
  168.2 1.1 shard_map.77
  (83 shorter events, 8.6 us)
Async XLA Ops:
  3.3 2.2 %copy-start = (bf16[4,128,4096]{2,1,0:T(8,128)(2,1)S(1)}, bf16[4,128,4096]{2,1,0:T(8,128)(2,1)}, u32[]{:S(2)}) copy-start(bf16[4,128,4096]{2,1,0:T(8,128)(2,1)} %param.7) | copy-start | bytes 12582916
  9.4 5.4 %copy-start.12 = (s32[128]{0:T(128)S(1)}, s32[128]{0:T(128)}, u32[]{:S(2)}) copy-start(s32[128]{0:T(128)} %param.11) | copy-start | bytes 1540
  9.4 5.5 %copy-start.13 = (s32[4,4]{1,0:T(4,128)S(1)}, s32[4,4]{1,0:T(4,128)}, u32[]{:S(2)}) copy-start(s32[4,4]{1,0:T(4,128)} %param.13) | copy-start | bytes 196
  9.4 7.5 %copy-start.5 = (bf16[512,512]{1,0:T(8,128)(2,1)S(1)}, bf16[512,512]{1,0:T(8,128)(2,1)}, u32[]{:S(2)}) copy-start(bf16[512,512]{1,0:T(8,128)(2,1)} %expand_ref.1) | copy-start | bytes 1572868
  9.4 31.5 %all-to-all-start = ((bf16[8,32,4096]{2,1,0:T(8,128)(2,1)}), bf16[8,32,4096]{2,1,0:T(8,128)(2,1)S(1)}, u32[]{:S(2)}, u32[]{:S(2)}) async-start(bf16[8,32,4096]{2,1,0:T(8,128)(2,1)} %bitcast.7), calls=%async_computation | async-start | bytes 4194304 | tf_op jit(solution)/shard_map/all_to_all | solution.py:303
  17.0 2.2 %copy-start.2 = (bf16[4096,512]{1,0:T(8,128)(2,1)S(1)}, bf16[4096,512]{1,0:T(8,128)(2,1)}, u32[]{:S(2)}) copy-start(bf16[4096,512]{1,0:T(8,128)(2,1)} %store_ref) | copy-start | bytes 12582916
  24.6 7.9 %copy-start.4 = (bf16[4608,512]{1,0:T(8,128)(2,1)}, bf16[4608,512]{1,0:T(8,128)(2,1)S(1)}, u32[]{:S(2)}) copy-start(bf16[4608,512]{1,0:T(8,128)(2,1)S(1)} %get-tuple-element.74) | copy-start | bytes 14155780
  24.6 39.1 %collective-permute-start.2 = (bf16[3072,512]{1,0:T(8,128)(2,1)}, bf16[3072,512]{1,0:T(8,128)(2,1)}, u32[]{:S(2)}, u32[]{:S(2)}) collective-permute-start(bf16[3072,512]{1,0:T(8,128)(2,1)} %get-tuple-element.57), channel_id=1, source_target_pairs={{0,1},{1,0},{2,3},{3,2},{4,5},{5,4},{6,7},{7,6},{8,9},{9,8},{10,11... | collective-permute-start | bytes 9437192 | tf_op jit(solution)/shard_map/ppermute | solution.py:48
  25.1 7.4 %collective-permute-start = (bf16[1536,512]{1,0:T(8,128)(2,1)S(1)}, bf16[1536,512]{1,0:T(8,128)(2,1)S(1)}, u32[]{:S(2)}, u32[]{:S(2)}) collective-permute-start(bf16[1536,512]{1,0:T(8,128)(2,1)S(1)} %get-tuple-element.54), channel_id=1, source_target_pairs={{0,1},{1,0},{2,3},{3,2},{4,5},{5,4},{6,7},{7,6},{8,9},{9,8},{10,11... | collective-permute-start | bytes 4718600 | tf_op jit(solution)/shard_map/ppermute | solution.py:48
  32.5 3.9 %copy-start.10 = (bf16[1536,512]{1,0:T(8,128)(2,1)}, bf16[1536,512]{1,0:T(8,128)(2,1)S(1)}, u32[]{:S(2)}) copy-start(bf16[1536,512]{1,0:T(8,128)(2,1)S(1)} %collective-permute-done) | copy-start | bytes 4718596
  32.6 31.1 %collective-permute-start.1 = (bf16[1536,256]{1,0:T(8,128)(2,1)S(1)}, bf16[1536,256]{1,0:T(8,128)(2,1)}, u32[]{:S(2)}, u32[]{:S(2)}) collective-permute-start(bf16[1536,256]{1,0:T(8,128)(2,1)S(1)} %slice_add_fusion), channel_id=1, source_target_pairs={{0,2},{2,0},{1,3},{3,1},{4,6},{6,4},{5,7},{7,5},{8,10},{10,8},{9,1... | collective-permute-start | bytes 2359304 | tf_op jit(solution)/shard_map/ppermute | solution.py:48
  41.0 27.9 %copy-start.8 = (bf16[8,32,4096]{2,1,0:T(8,128)(2,1)}, bf16[8,32,4096]{2,1,0:T(8,128)(2,1)S(1)}, u32[]{:S(2)}) copy-start(bf16[8,32,4096]{2,1,0:T(8,128)(2,1)S(1)} %all-to-all-done) | copy-start | bytes 6291460
  41.0 41.0 %all-to-all-start.1 = ((bf16[16,8,4224]{2,1,0:T(8,128)(2,1)}), bf16[16,8,4224]{2,1,0:T(8,128)(2,1)}, u32[]{:S(2)}, u32[]{:S(2)}) async-start(bf16[16,8,4224]{2,1,0:T(8,128)(2,1)} %bitcast.8), calls=%async_computation.1 | async-start | bytes 2162688 | tf_op jit(solution)/shard_map/all_to_all | solution.py:354
  65.2 21.4 %collective-permute-start.3 = (bf16[1536,256]{1,0:T(8,128)(2,1)S(1)}, bf16[1536,256]{1,0:T(8,128)(2,1)}, u32[]{:S(2)}, u32[]{:S(2)}) collective-permute-start(bf16[1536,256]{1,0:T(8,128)(2,1)S(1)} %slice_add_fusion.2), channel_id=1, source_target_pairs={{0,2},{2,0},{1,3},{3,1},{4,6},{6,4},{5,7},{7,5},{8,10},{10,8},{9,1... | collective-permute-start | bytes 2359304 | tf_op jit(solution)/shard_map/ppermute | solution.py:48
  68.8 13.1 %collective-permute-start.4 = (bf16[1536,128]{1,0:T(8,128)(2,1)}, bf16[1536,128]{1,0:T(8,128)(2,1)}, u32[]{:S(2)}, u32[]{:S(2)}) collective-permute-start(bf16[1536,128]{1,0:T(8,128)(2,1)} %fusion.13), channel_id=1, source_target_pairs={{0,4},{4,0},{1,5},{5,1},{2,6},{6,2},{3,7},{7,3},{8,12},{12,8},{9,1... | collective-permute-start | bytes 1179656 | tf_op jit(solution)/shard_map/ppermute | solution.py:48
  68.8 2.2 %copy-start.1 = (bf16[4,128,4096]{2,1,0:T(8,128)(2,1)S(1)}, bf16[4,128,4096]{2,1,0:T(8,128)(2,1)}, u32[]{:S(2)}) copy-start(bf16[4,128,4096]{2,1,0:T(8,128)(2,1)} %param.7) | copy-start | bytes 12582916
  80.9 1.0 copy-start.6
  82.0 14.5 %copy-start.3 = (bf16[4096,512]{1,0:T(8,128)(2,1)S(1)}, bf16[4096,512]{1,0:T(8,128)(2,1)}, u32[]{:S(2)}) copy-start(bf16[4096,512]{1,0:T(8,128)(2,1)} %store_ref) | copy-start | bytes 12582916
  88.0 23.9 %collective-permute-start.5 = (bf16[1536,256]{1,0:T(8,128)(2,1)S(1)}, bf16[1536,256]{1,0:T(8,128)(2,1)S(1)}, u32[]{:S(2)}, u32[]{:S(2)}) collective-permute-start(bf16[1536,256]{1,0:T(8,128)(2,1)S(1)} %slice_add_fusion.1), channel_id=1, source_target_pairs={{0,2},{2,0},{1,3},{3,1},{4,6},{6,4},{5,7},{7,5},{8,10},{10,8},{9,1... | collective-permute-start | bytes 2359304 | tf_op jit(solution)/shard_map/ppermute | solution.py:48
  90.8 9.2 %copy-start.7 = (f32[512,512]{1,0:T(8,128)S(1)}, f32[512,512]{1,0:T(8,128)}, u32[]{:S(2)}) copy-start(f32[512,512]{1,0:T(8,128)} %copy-done.6) | copy-start | bytes 3145732
  90.9 19.2 %collective-permute-start.6 = (bf16[1536,128]{1,0:T(8,128)(2,1)S(1)}, bf16[1536,128]{1,0:T(8,128)(2,1)S(1)}, u32[]{:S(2)}, u32[]{:S(2)}) collective-permute-start(bf16[1536,128]{1,0:T(8,128)(2,1)S(1)} %slice_add_fusion.6), channel_id=1, source_target_pairs={{0,4},{4,0},{1,5},{5,1},{2,6},{6,2},{3,7},{7,3},{8,12},{12,8},{9,1... | collective-permute-start | bytes 1179656 | tf_op jit(solution)/shard_map/ppermute | solution.py:48
  92.3 19.7 %collective-permute-start.7 = (bf16[1536,128]{1,0:T(8,128)(2,1)S(1)}, bf16[1536,128]{1,0:T(8,128)(2,1)S(1)}, u32[]{:S(2)}, u32[]{:S(2)}) collective-permute-start(bf16[1536,128]{1,0:T(8,128)(2,1)S(1)} %fusion.12), channel_id=1, source_target_pairs={{0,8},{8,0},{1,9},{9,1},{2,10},{10,2},{3,11},{11,3},{4,12},{12,4},... | collective-permute-start | bytes 1179656 | tf_op jit(solution)/shard_map/ppermute | solution.py:48
  98.4 19.3 %copy-start.9 = (bf16[8,32,4096]{2,1,0:T(8,128)(2,1)S(1)}, bf16[8,32,4096]{2,1,0:T(8,128)(2,1)}, u32[]{:S(2)}) copy-start(bf16[8,32,4096]{2,1,0:T(8,128)(2,1)} %copy-done.8) | copy-start | bytes 6291460
  98.5 9.3 %collective-permute-start.8 = (f32[128,512]{1,0:T(8,128)S(1)}, f32[128,512]{1,0:T(8,128)S(1)}, u32[]{:S(2)}, u32[]{:S(2)}) collective-permute-start(f32[128,512]{1,0:T(8,128)S(1)} %convolution_select_fusion), channel_id=1, source_target_pairs={{0,16},{16,0},{1,17},{17,1},{2,18},{18,2},{3,19},{19,3},{4,20},{20... | collective-permute-start | bytes 786440 | tf_op jit(solution)/shard_map/ppermute | solution.py:31
  100.1 26.8 %collective-permute-start.11 = (f32[512,512]{1,0:T(8,128)S(1)}, f32[512,512]{1,0:T(8,128)S(1)}, u32[]{:S(2)}, u32[]{:S(2)}) collective-permute-start(f32[512,512]{1,0:T(8,128)S(1)} %copy-done.7), channel_id=1, source_target_pairs={{0,16},{16,0},{1,17},{17,1},{2,18},{18,2},{3,19},{19,3},{4,20},{20... | collective-permute-start | bytes 3145736 | tf_op jit(solution)/shard_map/ppermute | solution.py:48
  113.3 18.2 %collective-permute-start.10 = (bf16[1536,128]{1,0:T(8,128)(2,1)S(1)}, bf16[1536,128]{1,0:T(8,128)(2,1)S(1)}, u32[]{:S(2)}, u32[]{:S(2)}) collective-permute-start(bf16[1536,128]{1,0:T(8,128)(2,1)S(1)} %add_add_fusion.1), channel_id=1, source_target_pairs={{0,8},{8,0},{1,9},{9,1},{2,10},{10,2},{3,11},{11,3},{4,12},{12,4},... | collective-permute-start | bytes 1179656 | tf_op jit(solution)/shard_map/ppermute | solution.py:48
  114.9 16.6 %collective-permute-start.9 = (bf16[1536,128]{1,0:T(8,128)(2,1)S(1)}, bf16[1536,128]{1,0:T(8,128)(2,1)S(1)}, u32[]{:S(2)}, u32[]{:S(2)}) collective-permute-start(bf16[1536,128]{1,0:T(8,128)(2,1)S(1)} %slice_add_fusion.5), channel_id=1, source_target_pairs={{0,4},{4,0},{1,5},{5,1},{2,6},{6,2},{3,7},{7,3},{8,12},{12,8},{9,1... | collective-permute-start | bytes 1179656 | tf_op jit(solution)/shard_map/ppermute | solution.py:48
  126.9 4.7 %copy-start.11 = (f32[512,512]{1,0:T(8,128)}, f32[512,512]{1,0:T(8,128)S(1)}, u32[]{:S(2)}) copy-start(f32[512,512]{1,0:T(8,128)S(1)} %collective-permute-done.11) | copy-start | bytes 3145732
  132.8 19.4 %collective-permute-start.12 = (bf16[1536,128]{1,0:T(8,128)(2,1)S(1)}, bf16[1536,128]{1,0:T(8,128)(2,1)S(1)}, u32[]{:S(2)}, u32[]{:S(2)}) collective-permute-start(bf16[1536,128]{1,0:T(8,128)(2,1)S(1)} %add_add_fusion.2.first_ref), channel_id=1, source_target_pairs={{0,8},{8,0},{1,9},{9,1},{2,10},{10,2},{3,11},{11,3},{4,12},{12,4},... | collective-permute-start | bytes 1179656 | tf_op jit(solution)/shard_map/ppermute | solution.py:48
  134.7 24.1 %all-to-all-start.2 = ((bf16[16,8,512]{2,1,0:T(8,128)(2,1)}), bf16[16,8,512]{2,1,0:T(8,128)(2,1)S(1)}, u32[]{:S(2)}, u32[]{:S(2)}) async-start(bf16[16,8,512]{2,1,0:T(8,128)(2,1)} %fusion), calls=%async_computation.2 | async-start | bytes 262144 | tf_op jit(solution)/shard_map/all_to_all | solution.py:385
  153.5 4.3 %collective-permute-start.13 = (f32[128,128]{1,0:T(8,128)S(1)}, f32[128,128]{1,0:T(8,128)S(1)}, u32[]{:S(2)}, u32[]{:S(2)}) collective-permute-start(f32[128,128]{1,0:T(8,128)S(1)} %fusion.20.own_ref), channel_id=1, source_target_pairs={{0,16},{16,0},{1,17},{17,1},{2,18},{18,2},{3,19},{19,3},{4,20},{20... | collective-permute-start | bytes 196616 | tf_op jit(solution)/shard_map/ppermute | solution.py:433
  158.8 9.4 %all-to-all-start.3 = ((bf16[8,32,512]{2,1,0:T(8,128)(2,1)}), bf16[8,32,512]{2,1,0:T(8,128)(2,1)S(1)}, u32[]{:S(2)}, u32[]{:S(2)}) async-start(bf16[8,32,512]{2,1,0:T(8,128)(2,1)} %bitcast.18), calls=%async_computation.3 | async-start | bytes 524288 | tf_op jit(solution)/shard_map/all_to_all | solution.py:438

commit v17 on v16

--- a/solution.py
+++ b/solution.py
@@ -218,45 +218,55 @@
     )(lax.axis_index("tp").astype(jnp.int32)[None], rows, weight)
 
 
-def hot_expand(z_own, z_got, factors, head):
+def hot_expand(z_pieces, factors, head, cold=None):
     kept = factors[0].shape[1]
     near = kept // R
-    count = z_own.shape[0] // HCAP
-
-    def kernel(own_ref, got_ref, first_ref, second_ref, out_ref):
-        z = (own_ref[...] + got_ref[...]).astype(jnp.bfloat16).astype(jnp.float32).reshape(count, 1, HCAP, kept)
+    count = z_pieces[0].shape[0] // HCAP
+    served = near * HCAP
+    more = () if cold is None else (cold,)
+    block = served + 16 * len(more)
+
+    def kernel(*refs):
+        first_ref, second_ref = refs[len(z_pieces):len(z_pieces) + 2]
+        out_ref = refs[-1]
+        z = sum(ref[...] for ref in refs[:len(z_pieces)])
+        z = z.astype(jnp.bfloat16).astype(jnp.float32).reshape(count, 1, HCAP, kept)
         shape = (count, near, HCAP, kept)
         same = lax.broadcasted_iota(jnp.int32, shape, 3) // R == lax.broadcasted_iota(jnp.int32, shape, 1)
         spread = jnp.where(same, jnp.broadcast_to(z, shape), 0.0).astype(jnp.bfloat16)
         product = lax.dot_general(
-            spread.reshape(count * near * HCAP, kept),
+            spread.reshape(count * served, kept),
             first_ref[-head:] + second_ref[-head:],
             (((1,), (1,)), ((), ())),
             preferred_element_type=jnp.float32,
-        )
-        out_ref[...] = product.astype(jnp.bfloat16)
+        ).astype(jnp.bfloat16)
+        for k in range(count):
+            out_ref[k * block:k * block + served] = product[k * served:(k + 1) * served]
+            if more:
+                out_ref[k * block + served:(k + 1) * block] = refs[-2][16 * k:16 * (k + 1)]
 
     return pl.pallas_call(
         kernel,
-        out_shape=jax.ShapeDtypeStruct((count * near * HCAP, head), jnp.bfloat16),
+        out_shape=jax.ShapeDtypeStruct((count * block, head), jnp.bfloat16),
         **kernel_params(),
-    )(z_own, z_got, *factors)
-
-
-def add_hot(partial, target, delta):
-    count = partial.shape[0]
-    hot_rows = delta.shape[0]
-
-    def kernel(partial_ref, target_ref, delta_ref, out_ref):
-        hit = lax.broadcasted_iota(jnp.int32, (count, hot_rows), 1) == target_ref[...]
+    )(*z_pieces, *factors, *more)
+
+
+def add_rows(bases, target, delta):
+    count = bases[0].shape[0]
+    placed = delta.shape[0]
+
+    def kernel(target_ref, delta_ref, *refs):
+        hit = lax.broadcasted_iota(jnp.int32, (count, placed), 1) == target_ref[...]
         place = hit.astype(jnp.float32).astype(jnp.bfloat16)
-        out_ref[...] = (partial_ref[...] + matmul(place, delta_ref[...])).astype(jnp.bfloat16)
+        base = sum(ref[...] for ref in refs[:-1])
+        refs[-1][...] = (base + matmul(place, delta_ref[...])).astype(jnp.bfloat16)
 
     return pl.pallas_call(
         kernel,
-        out_shape=jax.ShapeDtypeStruct(partial.shape, jnp.bfloat16),
+        out_shape=jax.ShapeDtypeStruct(bases[0].shape, jnp.bfloat16),
         **kernel_params(),
-    )(partial, target[:, None], delta)
+    )(target[:, None], delta, *bases)
 
 
 def on_device(
@@ -273,6 +283,7 @@
     me = lax.axis_index(DP)
     z_at, x_at, core_at = lax.axis_index("z_low"), lax.axis_index("x"), lax.axis_index("core")
     none_code = adapter_count + hot_count
+    paired = far_count == 2 and lax.axis_size("tp") == 2
     rows = activations.reshape(step_count * token_count, depth)
 
     near = step_count // 2
@@ -380,6 +391,16 @@
     def cold_expand():
         done["delta"] = narrow(done["z_cold"].astype(jnp.bfloat16), after(expand_store, chain.last))
 
+    def cold_far_out():
+        far_at = lax.axis_index("z_high")
+        halves = done["delta"].reshape(2, group_count * step_count * CAP, head_part)
+        done["cold_near"] = jnp.where(far_at == 0, halves[0], halves[1])
+        done["cold_far"] = chain.permute(jnp.where(far_at == 0, halves[1], halves[0]), "z_high", SWAP)
+
+    def far_rows_out():
+        last_rows = done["hot_in"].reshape(hot_rows, depth)[:, (chunk_count - 1) * part:]
+        done["far_rows"] = chain.permute(last_rows, "z_high", SWAP)
+
     def cold_back():
         delta = chain.hold(done["delta"].reshape(dp_count, step_count * CAP, head_part))
         delta = lax.all_to_all(delta, DP, split_axis=0, concat_axis=0, tiled=True)
@@ -392,14 +413,30 @@
         )
         done["partial"] = partial + done["base_own"] + done["base_got"]
 
-    between = {
-        0: [cold_tokens_out],
-        1: [base_product],
-        2: [cold_shrink, cold_over_tp, base_over_tp],
-        4: [cold_expand, cold_back, all_but_hot],
-    }
-    awaited = {0: ["hot_in"], 1: ["packet", "base_own", "base_other"], 2: ["z_cold"], 3: ["base_got"]}
-    for slot in range(chunk_count + len(hops) - 1):
+    if paired:
+        slots = chunk_count + 1
+        between = {
+            0: [cold_tokens_out],
+            1: [far_rows_out, base_product],
+            2: [cold_shrink, cold_over_tp, base_over_tp],
+            3: [cold_expand, cold_far_out],
+        }
+        awaited = {
+            0: ["hot_in"],
+            1: ["packet", "base_own", "base_other", "far_rows"],
+            2: ["z_cold"],
+            3: ["base_got", "cold_far"],
+        }
+    else:
+        slots = chunk_count + len(hops) - 1
+        between = {
+            0: [cold_tokens_out],
+            1: [base_product],
+            2: [cold_shrink, cold_over_tp, base_over_tp],
+            4: [cold_expand, cold_back, all_but_hot],
+        }
+        awaited = {0: ["hot_in"], 1: ["packet", "base_own", "base_other"], 2: ["z_cold"], 3: ["base_got"]}
+    for slot in range(slots):
         if slot > 0:
             if slot < chunk_count:
                 mine[slot] = after(mine_all, chain.last)[slot * part:(slot + 1) * part]
@@ -417,26 +454,56 @@
         chain.last = arrived[0]
         got.update(zip(here, arrived[1:]))
         done.update(zip(names_here, arrived[1 + len(here):]))
-    partial = done["partial"]
 
     hot_in = done["hot_in"].reshape(hot_rows, depth)
+    at_step = jnp.arange(kept) // R
+
+    def own_columns(dense):
+        dense = dense.reshape(group_count, near, HCAP, kept)
+        return sum(jnp.where(at_step == i, dense[:, i], 0.0) for i in range(near)).reshape(group_count * HCAP, kept)
+
     dense = None
-    for c in range(chunk_count):
+    for c in range(chunk_count - 1 if paired else chunk_count):
         last = min((c + 1) * part, depth)
         for piece in (held[c], got[c, len(hops) - 1]):
             product = matmul(hot_in[:, c * part:last], piece[:last - c * part])
             dense = product if dense is None else dense + product
-    dense = dense.reshape(group_count, near, HCAP, kept)
-    at_step = jnp.arange(kept) // R
-    z_part = sum(jnp.where(at_step == i, dense[:, i], 0.0) for i in range(near)).reshape(group_count * HCAP, kept)
-    if lax.axis_size("tp") == 2:
-        z_got = lax.ppermute(z_part, "tp", SWAP)
+    final = chunk_count - 1
+    if paired:
+        operand(final, 2)
+        held[final] = chain.hold(held[final])
+        expand_got = lax.ppermute(held[final][-head_part:], "z_high", SWAP)
+        both = jnp.concatenate([hot_in[:, final * part:], done["far_rows"]], axis=0)
+        products = matmul(both, held[final][:depth - final * part])
+        z_own, z_far = own_columns(dense + products[:hot_rows]), own_columns(products[hot_rows:])
+        z_pieces = (
+            z_own,
+            lax.ppermute(z_own, "tp", SWAP),
+            lax.ppermute(z_far, "z_high", SWAP),
+            lax.ppermute(z_far, ("tp", "z_high"), [(i, 3 - i) for i in range(4)]),
+        )
+        cold = jnp.concatenate(
+            [done[name].reshape(group_count, step_count * CAP, head_part) for name in ("cold_near", "cold_far")], axis=1
+        )
+        delta = hot_expand(z_pieces, (held[final], expand_got), head_part, cold.reshape(-1, head_part))
+        far_off = (owner // group_count != lax.axis_index("z_high")).astype(jnp.int32)
+        cold_place = (far_off * step_count + step_at) * CAP + rank
+        block = near * HCAP + 2 * step_count * CAP
+        target = jnp.where(
+            is_hot,
+            server * block + (step_at % near) * HCAP + rank,
+            owner % group_count * block + near * HCAP + cold_place,
+        )
+        target = jnp.where(is_hot | is_cold, target, -1).reshape(-1)
+        bases = (done["base_own"], done["base_got"])
     else:
-        z_part = lax.psum(z_part, "tp")
-        z_got = jnp.zeros_like(z_part)
-    delta_hot = hot_expand(z_part, z_got, (held[c], got[c, len(hops) - 1]), head_part).reshape(group_count, near * HCAP, head_part)
-    delta_hot = lax.all_to_all(delta_hot, GROUP, split_axis=0, concat_axis=0, tiled=True)
-    added = add_hot(partial, hot_target, delta_hot.reshape(hot_rows, head_part))
+        z_pieces = (lax.psum(own_columns(dense), "tp"),)
+        delta = hot_expand(z_pieces, (held[final], got[final, len(hops) - 1]), head_part)
+        target = hot_target
+        bases = (done["partial"],)
+    delta = delta.reshape(group_count, -1, head_part)
+    delta = lax.all_to_all(delta, GROUP, split_axis=0, concat_axis=0, tiled=True)
+    added = add_rows(bases, target, delta.reshape(-1, head_part))
     return added.reshape(step_count, token_count, head_part)
 
 

time: 171 us -> 176 us (1.029)
  waiting for transfers between devices: 75.2 us -> 80.1 us
  Pallas kernels: 21.3 us -> 23.5 us
  starting transfers between devices: 36.9 us -> 35 us
    all_to_all x2 -> x1, starting transfers between devices: 8 us -> 3.45 us  [on_device(): lax.all_to_all(delta, GROUP, split_axis=0, concat_axis=0, tiled=True)]
    ppermute x1 -> x4, waiting for transfers between devices: 2.59 us -> 6.69 us  [the longest x1 3.75 us: on_device(): lax.ppermute(z_own, 'tp', SWAP)]
    all_to_all x2 -> x1, waiting for transfers between devices: 4.12 us -> 7.25 us  [on_device(): lax.all_to_all(delta, GROUP, split_axis=0, concat_axis=0, tiled=True)]
    ppermute x1 -> x4, starting transfers between devices: 1.59 us -> 4.58 us  [the longest x1 2.97 us: on_device(): lax.ppermute(z_far, 'z_high', SWAP)]
    ppermute x12 -> x13, waiting for transfers between devices: 56.7 us -> 54.4 us  [permute(): return lax.ppermute(self.hold(value), axis, pairs)]
    pallas_call x1, Pallas kernels: 5.44 us -> 7.41 us  [pick_columns(): pl.pallas_call(kernel, grid_spec=pltpu.PrefetchScalarGridSpec(num_scalar_...]
    dot_general x8 -> x7, matrix products: 8.1 us -> 7.27 us  [matmul(): return jnp.dot(a, b, preferred_element_type=jnp.float32)]
    ppermute x12 -> x13, starting transfers between devices: 15.4 us -> 15.1 us  [permute(): return lax.ppermute(self.hold(value), axis, pairs)]
  transfers between devices with their start and end apart: 18 -> 21, of which waited for: 12 -> 13; matrix products, arithmetic and copies ran while one was open for 13% -> 11% of each run, Pallas kernels for 10% -> 10%
where the time goes in v17:
time: 176 us; the launch traced here: 175 us
  waiting for transfers between devices  80.1 us (46%)
  starting transfers between devices  35 us (20%)
  Pallas kernels  23.5 us (13%)
  other arithmetic  19.1 us (11%)
  local copies, waits for them, and re-layouts  9.3 us (5%)
  matrix products  7.27 us (4%)
    ppermute x13, waiting for transfers between devices, permute(): return lax.ppermute(self.hold(value), axis, pairs)  54.4 us
    ppermute x13, starting transfers between devices, permute(): return lax.ppermute(self.hold(value), axis, pairs)  15.1 us
    pallas_call x1, Pallas kernels, base_halves(): pl.pallas_call(kernel, grid_spec=pltpu.PrefetchScalarGridSpec(num_scalar_...  9.89 us
    unnamed x24, local copies, waits for them, and re-layouts  7.61 us
    pallas_call x1, Pallas kernels, pick_columns(): pl.pallas_call(kernel, grid_spec=pltpu.PrefetchScalarGridSpec(num_scalar_...  7.41 us
    dot_general x7, matrix products, matmul(): return jnp.dot(a, b, preferred_element_type=jnp.float32)  7.27 us
    all_to_all x1, waiting for transfers between devices, on_device(): lax.all_to_all(delta, GROUP, split_axis=0, concat_axis=0, tiled=True)  7.25 us
    ppermute x1, waiting for transfers between devices, sum_over_tp(): return part + lax.ppermute(part, 'tp', SWAP)  7.21 us
  transfers between devices with their start and end apart: 21, of which 13 were waited for; matrix products, arithmetic and copies ran while one was open for 11% of the time, Pallas kernels for 10%

profile of v17, /device:TPU:0, one launch (start us, length us, event | category | flops | bytes accessed | tf_op | source)
XLA Modules:
  0.0 174.6 jit_solution(15657277824148654376)
XLA Ops:
  3.4 2.2 %copy-done = bf16[4,128,4096]{2,1,0:T(8,128)(2,1)S(1)} copy-done((bf16[4,128,4096]{2,1,0:T(8,128)(2,1)S(1)}, bf16[4,128,4096]{2,1,0:T(8,128)(2,1)}, u32[]{:S(2)}) %copy-start) | copy-done | bytes 4194328
  5.5 3.9 %shard_map.73 = (bf16[256,4096]{1,0:T(8,128)(2,1)}, bf16[128,4224]{1,0:T(8,128)(2,1)}) custom-call(s32[1,512]{1,0:T(1,128)S(1)} %bitcast.57, s32[1,512]{1,0:T(1,128)S(1)} %bitcast.56, s32[1,512]{1,0:T(1,128)S(1)} %fusion.31.tag_at, bf16[512,4096]{1,0:T(8,128)(2,1)S(1)} %bitcast.52), custom_call_target="tpu_custom_call" | custom-call | flops 1 | bytes 1 | tf_op jit(solution)/shard_map/pallas_call | solution.py:160
  9.5 5.4 %all-to-all-start = ((bf16[8,32,4096]{2,1,0:T(8,128)(2,1)}), bf16[8,32,4096]{2,1,0:T(8,128)(2,1)S(1)}, u32[]{:S(2)}, u32[]{:S(2)}) async-start(bf16[8,32,4096]{2,1,0:T(8,128)(2,1)} %bitcast.8), calls=%async_computation | async-start | bytes 4194304 | tf_op jit(solution)/shard_map/all_to_all | solution.py:314
  17.0 2.2 %copy-done.2 = bf16[4096,512]{1,0:T(8,128)(2,1)S(1)} copy-done((bf16[4096,512]{1,0:T(8,128)(2,1)S(1)}, bf16[4096,512]{1,0:T(8,128)(2,1)}, u32[]{:S(2)}) %copy-start.2) | copy-done | bytes 4194328
  19.2 7.4 %shard_map.74 = (bf16[4608,512]{1,0:T(8,128)(2,1)S(1)}, bf16[1536,512]{1,0:T(8,128)(2,1)S(1)}, bf16[3072,512]{1,0:T(8,128)(2,1)}) custom-call(s32[4]{0:T(128)S(1)} %convert_element_type.18.mine_held, s32[4]{0:T(128)S(1)} %convert_element_type.19.other_held, s32[1,512]{1,0:T(1,128)S(1)} %bitcast.58, s32[1,512]{1,0:T(1,128)S(1)} %bitcast.59, ...), custom_call_target="tpu_custom_call" | custom-call | flops 1 | bytes 1 | tf_op jit(solution)/shard_map/pallas_call | solution.py:108
  27.1 7.4 %collective-permute-done = bf16[1536,512]{1,0:T(8,128)(2,1)S(1)} collective-permute-done((bf16[1536,512]{1,0:T(8,128)(2,1)S(1)}, bf16[1536,512]{1,0:T(8,128)(2,1)S(1)}, u32[]{:S(2)}, u32[]{:S(2)}) %collective-permute-start) | collective-permute-done | bytes 1572896 | tf_op jit(solution)/shard_map/ppermute | solution.py:48
  34.6 1.9 %collective-permute-start.1 = (bf16[1536,256]{1,0:T(8,128)(2,1)S(1)}, bf16[1536,256]{1,0:T(8,128)(2,1)}, u32[]{:S(2)}, u32[]{:S(2)}) collective-permute-start(bf16[1536,256]{1,0:T(8,128)(2,1)S(1)} %slice_add_fusion), channel_id=1, source_target_pairs={{0,2},{2,0},{1,3},{3,1},{4,6},{6,4},{5,7},{7,5},{8,10},{10,8},{9,1... | collective-permute-start | bytes 2359304 | tf_op jit(solution)/shard_map/ppermute | solution.py:48
  36.5 4.5 %all-to-all-done = bf16[8,32,4096]{2,1,0:T(8,128)(2,1)S(1)} async-done(((bf16[8,32,4096]{2,1,0:T(8,128)(2,1)}), bf16[8,32,4096]{2,1,0:T(8,128)(2,1)S(1)}, u32[]{:S(2)}, u32[]{:S(2)}) %all-to-all-start) | async-done | bytes 2097184 | tf_op jit(solution)/shard_map/all_to_all | solution.py:314
  41.0 4.9 %all-to-all-start.1 = ((bf16[16,8,4224]{2,1,0:T(8,128)(2,1)}), bf16[16,8,4224]{2,1,0:T(8,128)(2,1)}, u32[]{:S(2)}, u32[]{:S(2)}) async-start(bf16[16,8,4224]{2,1,0:T(8,128)(2,1)} %bitcast.5), calls=%async_computation.1 | async-start | bytes 2162688 | tf_op jit(solution)/shard_map/all_to_all | solution.py:365
  46.0 17.8 %collective-permute-done.1 = bf16[1536,256]{1,0:T(8,128)(2,1)} collective-permute-done((bf16[1536,256]{1,0:T(8,128)(2,1)S(1)}, bf16[1536,256]{1,0:T(8,128)(2,1)}, u32[]{:S(2)}, u32[]{:S(2)}) %collective-permute-start.1) | collective-permute-done | bytes 786464 | tf_op jit(solution)/shard_map/ppermute | solution.py:48
  64.6 1.5 slice_add_fusion.2
  66.1 1.6 collective-permute-start.3
  67.7 2.0 %fusion.11 = bf16[1536,128]{1,0:T(8,128)(2,1)} fusion(bf16[1536,512]{1,0:T(8,128)(2,1)} %copy-done.9, bf16[1536,256]{1,0:T(8,128)(2,1)} %collective-permute-done.1, bf16[4608,512]{1,0:T(8,128)(2,1)} %copy-done.4), kind=kLoop, calls=%fused_computation.20 | loop fusion | flops 393216 | bytes 1572864 | tf_op jit(solution)/shard_map/add | solution.py:346
  69.7 2.0 %collective-permute-start.5 = (bf16[256,1024]{1,0:T(8,128)(2,1)}, bf16[256,1024]{1,0:T(8,128)(2,1)}, u32[]{:S(2)}, u32[]{:S(2)}) collective-permute-start(bf16[256,1024]{1,0:T(8,128)(2,1)} %slice.226), channel_id=1, source_target_pairs={{0,8},{8,0},{1,9},{9,1},{2,10},{10,2},{3,11},{11,3},{4,12},{12,4},... | collective-permute-start | bytes 1572872 | tf_op jit(solution)/shard_map/ppermute | solution.py:48
  71.7 2.0 %collective-permute-start.4 = (bf16[1536,128]{1,0:T(8,128)(2,1)}, bf16[1536,128]{1,0:T(8,128)(2,1)S(1)}, u32[]{:S(2)}, u32[]{:S(2)}) collective-permute-start(bf16[1536,128]{1,0:T(8,128)(2,1)} %fusion.11), channel_id=1, source_target_pairs={{0,4},{4,0},{1,5},{5,1},{2,6},{6,2},{3,7},{7,3},{8,12},{12,8},{9,1... | collective-permute-start | bytes 1179656 | tf_op jit(solution)/shard_map/ppermute | solution.py:48
  73.7 2.2 %copy-done.1 = bf16[4,128,4096]{2,1,0:T(8,128)(2,1)S(1)} copy-done((bf16[4,128,4096]{2,1,0:T(8,128)(2,1)S(1)}, bf16[4,128,4096]{2,1,0:T(8,128)(2,1)}, u32[]{:S(2)}) %copy-start.1) | copy-done | bytes 4194328
  75.9 9.9 %shard_map.75 = (f32[512,512]{1,0:T(8,128)S(1)}, f32[512,512]{1,0:T(8,128)S(1)}) custom-call(s32[1]{0:T(128)} %bitcast.11.tp_at, bf16[512,4096]{1,0:T(8,128)(2,1)S(1)} %bitcast.53, bf16[4096,1024]{1,0:T(8,128)(2,1)} %weight_ref), custom_call_target="tpu_custom_call" | custom-call | flops 1 | bytes 1 | tf_op jit(solution)/shard_map/pallas_call | solution.py:204
  85.8 1.0 copy-done.6
  86.8 2.3 %collective-permute-done.4 = bf16[1536,128]{1,0:T(8,128)(2,1)S(1)} collective-permute-done((bf16[1536,128]{1,0:T(8,128)(2,1)}, bf16[1536,128]{1,0:T(8,128)(2,1)S(1)}, u32[]{:S(2)}, u32[]{:S(2)}) %collective-permute-start.4) | collective-permute-done | bytes 393248 | tf_op jit(solution)/shard_map/ppermute | solution.py:48
  89.1 6.6 %collective-permute-done.5 = bf16[256,1024]{1,0:T(8,128)(2,1)} collective-permute-done((bf16[256,1024]{1,0:T(8,128)(2,1)}, bf16[256,1024]{1,0:T(8,128)(2,1)}, u32[]{:S(2)}, u32[]{:S(2)}) %collective-permute-start.5) | collective-permute-done | bytes 524320 | tf_op jit(solution)/shard_map/ppermute | solution.py:48
  95.8 2.3 %slice_add_fusion.1 = bf16[1536,256]{1,0:T(8,128)(2,1)} fusion(bf16[3072,512]{1,0:T(8,128)(2,1)} %collective-permute-done.2, bf16[4608,512]{1,0:T(8,128)(2,1)} %copy-done.4), kind=kLoop, calls=%fused_computation.12 | loop fusion | flops 393216 | bytes 2359296 | tf_op jit(solution)/shard_map/add | solution.py:344
  98.1 1.5 collective-permute-start.6
  99.6 2.1 %fusion.13 = bf16[1536,128]{1,0:T(8,128)(2,1)} fusion(bf16[1536,128]{1,0:T(8,128)(2,1)S(1)} %collective-permute-done.4, bf16[1536,512]{1,0:T(8,128)(2,1)} %copy-done.9, bf16[1536,256]{1,0:T(8,128)(2,1)} %collective-permute-done.1, bf16[4608,512]{1,0:T(8,128)(2,1)} %copy-done.4), kind=kLoop, calls=%fused_computation.23 | loop fusion | flops 589824 | bytes 1966080 | tf_op jit(solution)/shard_map/add | solution.py:348
  101.7 1.3 slice_add_fusion.6
  103.1 1.9 %collective-permute-start.8 = (bf16[1536,128]{1,0:T(8,128)(2,1)}, bf16[1536,128]{1,0:T(8,128)(2,1)}, u32[]{:S(2)}, u32[]{:S(2)}) collective-permute-start(bf16[1536,128]{1,0:T(8,128)(2,1)} %fusion.13), channel_id=1, source_target_pairs={{0,8},{8,0},{1,9},{9,1},{2,10},{10,2},{3,11},{11,3},{4,12},{12,4},... | collective-permute-start | bytes 1179656 | tf_op jit(solution)/shard_map/ppermute | solution.py:48
  105.9 2.0 %convolution_select_fusion = f32[128,512]{1,0:T(8,128)S(1)} fusion(bf16[4096,512]{1,0:T(8,128)(2,1)S(1)} %copy-done.3, bf16[128,4224]{1,0:T(8,128)(2,1)} %bitcast.10, s32[512]{0:T(512)S(1)} %fusion.28, s32[128]{0:T(128)S(1)} %convert_reduce_fusion.1), kind=kOutput, calls=%fused_computation | convolution fusion | flops 537001984 | bytes 5507584 | tf_op jit(solution)/shard_map/dot_general | solution.py:22
  107.9 1.6 collective-permute-start.9
  110.0 7.2 %collective-permute-done.9 = f32[128,512]{1,0:T(8,128)S(1)} collective-permute-done((f32[128,512]{1,0:T(8,128)S(1)}, f32[128,512]{1,0:T(8,128)S(1)}, u32[]{:S(2)}, u32[]{:S(2)}) %collective-permute-start.9) | collective-permute-done | bytes 262176 | tf_op jit(solution)/shard_map/ppermute | solution.py:31
  117.3 3.2 %collective-permute-done.7 = bf16[1536,128]{1,0:T(8,128)(2,1)} collective-permute-done((bf16[1536,128]{1,0:T(8,128)(2,1)S(1)}, bf16[1536,128]{1,0:T(8,128)(2,1)}, u32[]{:S(2)}, u32[]{:S(2)}) %collective-permute-start.7) | collective-permute-done | bytes 393248 | tf_op jit(solution)/shard_map/ppermute | solution.py:48
  120.5 2.7 %collective-permute-done.8 = bf16[1536,128]{1,0:T(8,128)(2,1)} collective-permute-done((bf16[1536,128]{1,0:T(8,128)(2,1)}, bf16[1536,128]{1,0:T(8,128)(2,1)}, u32[]{:S(2)}, u32[]{:S(2)}) %collective-permute-start.8) | collective-permute-done | bytes 393248 | tf_op jit(solution)/shard_map/ppermute | solution.py:48
  123.2 1.3 slice_add_fusion.5
  124.5 1.4 add_add_fusion.1
  126.1 1.9 %collective-permute-start.11 = (bf16[1536,128]{1,0:T(8,128)(2,1)S(1)}, bf16[1536,128]{1,0:T(8,128)(2,1)S(1)}, u32[]{:S(2)}, u32[]{:S(2)}) collective-permute-start(bf16[1536,128]{1,0:T(8,128)(2,1)S(1)} %add_add_fusion.1), channel_id=1, source_target_pairs={{0,8},{8,0},{1,9},{9,1},{2,10},{10,2},{3,11},{11,3},{4,12},{12,4},... | collective-permute-start | bytes 1179656 | tf_op jit(solution)/shard_map/ppermute | solution.py:48
  128.3 1.1 collective-permute-start.13
  129.4 1.3 fusion.8
  130.7 1.3 convolution_add_fusion.2
  132.5 14.3 %collective-permute-done.13 = bf16[64,512]{1,0:T(8,128)(2,1)S(1)} collective-permute-done((bf16[64,512]{1,0:T(8,128)(2,1)S(1)}, bf16[64,512]{1,0:T(8,128)(2,1)S(1)}, u32[]{:S(2)}, u32[]{:S(2)}) %collective-permute-start.13) | collective-permute-done | bytes 65568 | tf_op jit(solution)/shard_map/ppermute | solution.py:48
  146.7 1.3 add_add_fusion.refs_4_
  148.1 1.6 fusion.1
  150.2 3.0 %collective-permute-start.15 = (f32[128,128]{1,0:T(8,128)S(1)}, f32[128,128]{1,0:T(8,128)S(1)}, u32[]{:S(2)}, u32[]{:S(2)}) collective-permute-start(f32[128,128]{1,0:T(8,128)S(1)} %get-tuple-element.116), channel_id=1, source_target_pairs={{0,8},{8,0},{1,9},{9,1},{2,10},{10,2},{3,11},{11,3},{4,12},{12,4},... | collective-permute-start | bytes 196616 | tf_op jit(solution)/shard_map/ppermute | solution.py:482
  153.2 1.0 collective-permute-start.16
  154.8 3.7 %collective-permute-done.14.refs_1_ = f32[128,128]{1,0:T(8,128)S(1)} collective-permute-done((f32[128,128]{1,0:T(8,128)S(1)}, f32[128,128]{1,0:T(8,128)S(1)}, u32[]{:S(2)}, u32[]{:S(2)}) %collective-permute-start.14) | collective-permute-done | bytes 65568 | tf_op jit(solution)/shard_map/ppermute | solution.py:481
  158.5 1.3 collective-permute-done.15.refs_2_
  159.8 1.6 collective-permute-done.16.refs_3_
  161.5 1.0 shard_map.76
  162.5 3.5 %all-to-all-start.2 = ((bf16[8,48,512]{2,1,0:T(8,128)(2,1)}), bf16[8,48,512]{2,1,0:T(8,128)(2,1)S(1)}, u32[]{:S(2)}, u32[]{:S(2)}) async-start(bf16[8,48,512]{2,1,0:T(8,128)(2,1)} %bitcast.21), calls=%async_computation.2 | async-start | bytes 786432 | tf_op jit(solution)/shard_map/all_to_all | solution.py:505
  166.1 7.3 %all-to-all-done.2 = bf16[8,48,512]{2,1,0:T(8,128)(2,1)S(1)} async-done(((bf16[8,48,512]{2,1,0:T(8,128)(2,1)}), bf16[8,48,512]{2,1,0:T(8,128)(2,1)S(1)}, u32[]{:S(2)}, u32[]{:S(2)}) %all-to-all-start.2) | async-done | bytes 393248 | tf_op jit(solution)/shard_map/all_to_all | solution.py:505
  173.3 1.3 shard_map.77
  (89 shorter events, 10.2 us)
Async XLA Ops:
  3.4 2.2 %copy-start = (bf16[4,128,4096]{2,1,0:T(8,128)(2,1)S(1)}, bf16[4,128,4096]{2,1,0:T(8,128)(2,1)}, u32[]{:S(2)}) copy-start(bf16[4,128,4096]{2,1,0:T(8,128)(2,1)} %param.7) | copy-start | bytes 12582916
  9.5 5.4 %copy-start.10 = (s32[128]{0:T(128)S(1)}, s32[128]{0:T(128)}, u32[]{:S(2)}) copy-start(s32[128]{0:T(128)} %param.11) | copy-start | bytes 1540
  9.5 5.5 %copy-start.11 = (s32[4,4]{1,0:T(4,128)S(1)}, s32[4,4]{1,0:T(4,128)}, u32[]{:S(2)}) copy-start(s32[4,4]{1,0:T(4,128)} %param.13) | copy-start | bytes 196
  9.5 7.5 %copy-start.5 = (bf16[512,512]{1,0:T(8,128)(2,1)S(1)}, bf16[512,512]{1,0:T(8,128)(2,1)}, u32[]{:S(2)}) copy-start(bf16[512,512]{1,0:T(8,128)(2,1)} %expand_ref.1) | copy-start | bytes 1572868
  9.5 31.5 %all-to-all-start = ((bf16[8,32,4096]{2,1,0:T(8,128)(2,1)}), bf16[8,32,4096]{2,1,0:T(8,128)(2,1)S(1)}, u32[]{:S(2)}, u32[]{:S(2)}) async-start(bf16[8,32,4096]{2,1,0:T(8,128)(2,1)} %bitcast.8), calls=%async_computation | async-start | bytes 4194304 | tf_op jit(solution)/shard_map/all_to_all | solution.py:314
  17.0 2.2 %copy-start.2 = (bf16[4096,512]{1,0:T(8,128)(2,1)S(1)}, bf16[4096,512]{1,0:T(8,128)(2,1)}, u32[]{:S(2)}) copy-start(bf16[4096,512]{1,0:T(8,128)(2,1)} %store_ref) | copy-start | bytes 12582916
  26.6 7.9 %copy-start.4 = (bf16[4608,512]{1,0:T(8,128)(2,1)}, bf16[4608,512]{1,0:T(8,128)(2,1)S(1)}, u32[]{:S(2)}) copy-start(bf16[4608,512]{1,0:T(8,128)(2,1)S(1)} %get-tuple-element.78) | copy-start | bytes 14155780
  26.6 38.0 %collective-permute-start.2 = (bf16[3072,512]{1,0:T(8,128)(2,1)}, bf16[3072,512]{1,0:T(8,128)(2,1)}, u32[]{:S(2)}, u32[]{:S(2)}) collective-permute-start(bf16[3072,512]{1,0:T(8,128)(2,1)} %get-tuple-element.59), channel_id=1, source_target_pairs={{0,1},{1,0},{2,3},{3,2},{4,5},{5,4},{6,7},{7,6},{8,9},{9,8},{10,11... | collective-permute-start | bytes 9437192 | tf_op jit(solution)/shard_map/ppermute | solution.py:48
  27.1 7.4 %collective-permute-start = (bf16[1536,512]{1,0:T(8,128)(2,1)S(1)}, bf16[1536,512]{1,0:T(8,128)(2,1)S(1)}, u32[]{:S(2)}, u32[]{:S(2)}) collective-permute-start(bf16[1536,512]{1,0:T(8,128)(2,1)S(1)} %get-tuple-element.57), channel_id=1, source_target_pairs={{0,1},{1,0},{2,3},{3,2},{4,5},{5,4},{6,7},{7,6},{8,9},{9,8},{10,11... | collective-permute-start | bytes 4718600 | tf_op jit(solution)/shard_map/ppermute | solution.py:48
  34.5 2.0 %copy-start.9 = (bf16[1536,512]{1,0:T(8,128)(2,1)}, bf16[1536,512]{1,0:T(8,128)(2,1)S(1)}, u32[]{:S(2)}) copy-start(bf16[1536,512]{1,0:T(8,128)(2,1)S(1)} %collective-permute-done) | copy-start | bytes 4718596
  34.6 29.2 %collective-permute-start.1 = (bf16[1536,256]{1,0:T(8,128)(2,1)S(1)}, bf16[1536,256]{1,0:T(8,128)(2,1)}, u32[]{:S(2)}, u32[]{:S(2)}) collective-permute-start(bf16[1536,256]{1,0:T(8,128)(2,1)S(1)} %slice_add_fusion), channel_id=1, source_target_pairs={{0,2},{2,0},{1,3},{3,1},{4,6},{6,4},{5,7},{7,5},{8,10},{10,8},{9,1... | collective-permute-start | bytes 2359304 | tf_op jit(solution)/shard_map/ppermute | solution.py:48
  41.0 28.7 %copy-start.7 = (bf16[8,32,4096]{2,1,0:T(8,128)(2,1)}, bf16[8,32,4096]{2,1,0:T(8,128)(2,1)S(1)}, u32[]{:S(2)}) copy-start(bf16[8,32,4096]{2,1,0:T(8,128)(2,1)S(1)} %all-to-all-done) | copy-start | bytes 6291460
  41.0 45.8 %all-to-all-start.1 = ((bf16[16,8,4224]{2,1,0:T(8,128)(2,1)}), bf16[16,8,4224]{2,1,0:T(8,128)(2,1)}, u32[]{:S(2)}, u32[]{:S(2)}) async-start(bf16[16,8,4224]{2,1,0:T(8,128)(2,1)} %bitcast.5), calls=%async_computation.1 | async-start | bytes 2162688 | tf_op jit(solution)/shard_map/all_to_all | solution.py:365
  66.1 29.7 %collective-permute-start.3 = (bf16[1536,256]{1,0:T(8,128)(2,1)S(1)}, bf16[1536,256]{1,0:T(8,128)(2,1)}, u32[]{:S(2)}, u32[]{:S(2)}) collective-permute-start(bf16[1536,256]{1,0:T(8,128)(2,1)S(1)} %slice_add_fusion.2), channel_id=1, source_target_pairs={{0,2},{2,0},{1,3},{3,1},{4,6},{6,4},{5,7},{7,5},{8,10},{10,8},{9,1... | collective-permute-start | bytes 2359304 | tf_op jit(solution)/shard_map/ppermute | solution.py:48
  69.7 26.1 %collective-permute-start.5 = (bf16[256,1024]{1,0:T(8,128)(2,1)}, bf16[256,1024]{1,0:T(8,128)(2,1)}, u32[]{:S(2)}, u32[]{:S(2)}) collective-permute-start(bf16[256,1024]{1,0:T(8,128)(2,1)} %slice.226), channel_id=1, source_target_pairs={{0,8},{8,0},{1,9},{9,1},{2,10},{10,2},{3,11},{11,3},{4,12},{12,4},... | collective-permute-start | bytes 1572872 | tf_op jit(solution)/shard_map/ppermute | solution.py:48
  71.7 17.4 %collective-permute-start.4 = (bf16[1536,128]{1,0:T(8,128)(2,1)}, bf16[1536,128]{1,0:T(8,128)(2,1)S(1)}, u32[]{:S(2)}, u32[]{:S(2)}) collective-permute-start(bf16[1536,128]{1,0:T(8,128)(2,1)} %fusion.11), channel_id=1, source_target_pairs={{0,4},{4,0},{1,5},{5,1},{2,6},{6,2},{3,7},{7,3},{8,12},{12,8},{9,1... | collective-permute-start | bytes 1179656 | tf_op jit(solution)/shard_map/ppermute | solution.py:48
  73.7 2.2 %copy-start.1 = (bf16[4,128,4096]{2,1,0:T(8,128)(2,1)S(1)}, bf16[4,128,4096]{2,1,0:T(8,128)(2,1)}, u32[]{:S(2)}) copy-start(bf16[4,128,4096]{2,1,0:T(8,128)(2,1)} %param.7) | copy-start | bytes 12582916
  85.8 1.0 copy-start.6
  86.8 19.1 %copy-start.3 = (bf16[4096,512]{1,0:T(8,128)(2,1)S(1)}, bf16[4096,512]{1,0:T(8,128)(2,1)}, u32[]{:S(2)}) copy-start(bf16[4096,512]{1,0:T(8,128)(2,1)} %store_ref) | copy-start | bytes 12582916
  98.1 25.1 %collective-permute-start.6 = (bf16[1536,256]{1,0:T(8,128)(2,1)}, bf16[1536,256]{1,0:T(8,128)(2,1)}, u32[]{:S(2)}, u32[]{:S(2)}) collective-permute-start(bf16[1536,256]{1,0:T(8,128)(2,1)} %slice_add_fusion.1), channel_id=1, source_target_pairs={{0,2},{2,0},{1,3},{3,1},{4,6},{6,4},{5,7},{7,5},{8,10},{10,8},{9,1... | collective-permute-start | bytes 2359304 | tf_op jit(solution)/shard_map/ppermute | solution.py:48
  103.0 17.5 %collective-permute-start.7 = (bf16[1536,128]{1,0:T(8,128)(2,1)S(1)}, bf16[1536,128]{1,0:T(8,128)(2,1)}, u32[]{:S(2)}, u32[]{:S(2)}) collective-permute-start(bf16[1536,128]{1,0:T(8,128)(2,1)S(1)} %slice_add_fusion.6), channel_id=1, source_target_pairs={{0,4},{4,0},{1,5},{5,1},{2,6},{6,2},{3,7},{7,3},{8,12},{12,8},{9,1... | collective-permute-start | bytes 1179656 | tf_op jit(solution)/shard_map/ppermute | solution.py:48
  103.1 20.1 %collective-permute-start.8 = (bf16[1536,128]{1,0:T(8,128)(2,1)}, bf16[1536,128]{1,0:T(8,128)(2,1)}, u32[]{:S(2)}, u32[]{:S(2)}) collective-permute-start(bf16[1536,128]{1,0:T(8,128)(2,1)} %fusion.13), channel_id=1, source_target_pairs={{0,8},{8,0},{1,9},{9,1},{2,10},{10,2},{3,11},{11,3},{4,12},{12,4},... | collective-permute-start | bytes 1179656 | tf_op jit(solution)/shard_map/ppermute | solution.py:48
  107.9 9.3 %collective-permute-start.9 = (f32[128,512]{1,0:T(8,128)S(1)}, f32[128,512]{1,0:T(8,128)S(1)}, u32[]{:S(2)}, u32[]{:S(2)}) collective-permute-start(f32[128,512]{1,0:T(8,128)S(1)} %convolution_select_fusion), channel_id=1, source_target_pairs={{0,16},{16,0},{1,17},{17,1},{2,18},{18,2},{3,19},{19,3},{4,20},{20... | collective-permute-start | bytes 786440 | tf_op jit(solution)/shard_map/ppermute | solution.py:31
  109.5 19.9 %copy-start.8 = (bf16[8,32,4096]{2,1,0:T(8,128)(2,1)S(1)}, bf16[8,32,4096]{2,1,0:T(8,128)(2,1)}, u32[]{:S(2)}) copy-start(bf16[8,32,4096]{2,1,0:T(8,128)(2,1)} %copy-done.7) | copy-start | bytes 6291460
  109.5 37.2 %collective-permute-start.12 = (f32[512,512]{1,0:T(8,128)}, f32[512,512]{1,0:T(8,128)S(1)}, u32[]{:S(2)}, u32[]{:S(2)}) collective-permute-start(f32[512,512]{1,0:T(8,128)} %copy-done.6), channel_id=1, source_target_pairs={{0,16},{16,0},{1,17},{17,1},{2,18},{18,2},{3,19},{19,3},{4,20},{20... | collective-permute-start | bytes 3145736 | tf_op jit(solution)/shard_map/ppermute | solution.py:48
  126.0 20.7 %collective-permute-start.10 = (bf16[1536,128]{1,0:T(8,128)(2,1)S(1)}, bf16[1536,128]{1,0:T(8,128)(2,1)S(1)}, u32[]{:S(2)}, u32[]{:S(2)}) collective-permute-start(bf16[1536,128]{1,0:T(8,128)(2,1)S(1)} %slice_add_fusion.5), channel_id=1, source_target_pairs={{0,4},{4,0},{1,5},{5,1},{2,6},{6,2},{3,7},{7,3},{8,12},{12,8},{9,1... | collective-permute-start | bytes 1179656 | tf_op jit(solution)/shard_map/ppermute | solution.py:48
  126.1 20.7 %collective-permute-start.11 = (bf16[1536,128]{1,0:T(8,128)(2,1)S(1)}, bf16[1536,128]{1,0:T(8,128)(2,1)S(1)}, u32[]{:S(2)}, u32[]{:S(2)}) collective-permute-start(bf16[1536,128]{1,0:T(8,128)(2,1)S(1)} %add_add_fusion.1), channel_id=1, source_target_pairs={{0,8},{8,0},{1,9},{9,1},{2,10},{10,2},{3,11},{11,3},{4,12},{12,4},... | collective-permute-start | bytes 1179656 | tf_op jit(solution)/shard_map/ppermute | solution.py:48
  128.3 18.5 %collective-permute-start.13 = (bf16[64,512]{1,0:T(8,128)(2,1)S(1)}, bf16[64,512]{1,0:T(8,128)(2,1)S(1)}, u32[]{:S(2)}, u32[]{:S(2)}) collective-permute-start(bf16[64,512]{1,0:T(8,128)(2,1)S(1)} %get-tuple-element.92), channel_id=1, source_target_pairs={{0,8},{8,0},{1,9},{9,1},{2,10},{10,2},{3,11},{11,3},{4,12},{12,4},... | collective-permute-start | bytes 196616 | tf_op jit(solution)/shard_map/ppermute | solution.py:48
  150.1 11.3 %collective-permute-start.17 = (bf16[512,128]{1,0:T(8,128)(2,1)S(1)}, bf16[512,128]{1,0:T(8,128)(2,1)S(1)}, u32[]{:S(2)}, u32[]{:S(2)}) collective-permute-start(bf16[512,128]{1,0:T(8,128)(2,1)S(1)} %slice.238), channel_id=1, source_target_pairs={{0,8},{8,0},{1,9},{9,1},{2,10},{10,2},{3,11},{11,3},{4,12},{12,4},... | collective-permute-start | bytes 393224 | tf_op jit(solution)/shard_map/ppermute | solution.py:475
  150.2 9.6 %collective-permute-start.15 = (f32[128,128]{1,0:T(8,128)S(1)}, f32[128,128]{1,0:T(8,128)S(1)}, u32[]{:S(2)}, u32[]{:S(2)}) collective-permute-start(f32[128,128]{1,0:T(8,128)S(1)} %get-tuple-element.116), channel_id=1, source_target_pairs={{0,8},{8,0},{1,9},{9,1},{2,10},{10,2},{3,11},{11,3},{4,12},{12,4},... | collective-permute-start | bytes 196616 | tf_op jit(solution)/shard_map/ppermute | solution.py:482
  153.2 8.2 %collective-permute-start.16 = (f32[128,128]{1,0:T(8,128)S(1)}, f32[128,128]{1,0:T(8,128)S(1)}, u32[]{:S(2)}, u32[]{:S(2)}) collective-permute-start(f32[128,128]{1,0:T(8,128)S(1)} %get-tuple-element.116), channel_id=1, source_target_pairs={{0,24},{8,16},{16,8},{24,0},{1,25},{9,17},{17,9},{25,1},{2,26},{10... | collective-permute-start | bytes 196616 | tf_op jit(solution)/shard_map/ppermute | solution.py:483
  154.3 4.3 %collective-permute-start.14 = (f32[128,128]{1,0:T(8,128)S(1)}, f32[128,128]{1,0:T(8,128)S(1)}, u32[]{:S(2)}, u32[]{:S(2)}) collective-permute-start(f32[128,128]{1,0:T(8,128)S(1)} %get-tuple-element.117.refs_0_), channel_id=1, source_target_pairs={{0,16},{16,0},{1,17},{17,1},{2,18},{18,2},{3,19},{19,3},{4,20},{20... | collective-permute-start | bytes 196616 | tf_op jit(solution)/shard_map/ppermute | solution.py:481
  162.5 10.9 %all-to-all-start.2 = ((bf16[8,48,512]{2,1,0:T(8,128)(2,1)}), bf16[8,48,512]{2,1,0:T(8,128)(2,1)S(1)}, u32[]{:S(2)}, u32[]{:S(2)}) async-start(bf16[8,48,512]{2,1,0:T(8,128)(2,1)} %bitcast.21), calls=%async_computation.2 | async-start | bytes 786432 | tf_op jit(solution)/shard_map/all_to_all | solution.py:505

commit v18 on v16

--- a/solution.py
+++ b/solution.py
@@ -135,43 +135,33 @@
     )
 
 
-def place_rows(rows, hot_target, cold_target, tag, hot_rows, cold_rows):
+def place_cold(rows, target, tag, placed):
     count, depth = rows.shape
     blocks = 4
     width = depth // blocks
 
-    def kernel(hot_at, cold_at, tag_at, rows_ref, hot_ref, cold_ref, place_hot, place_cold):
+    def kernel(target_at, tag_at, rows_ref, out_ref, place):
         step = pl.program_id(0)
 
         @pl.when(step == 0)
         def _():
-            hot_hit = lax.broadcasted_iota(jnp.int32, (hot_rows, count), 0) == hot_at[...]
-            cold_hit = lax.broadcasted_iota(jnp.int32, (cold_rows, count), 0) == cold_at[...]
-            place_hot[...] = hot_hit.astype(jnp.float32).astype(jnp.bfloat16)
-            place_cold[...] = cold_hit.astype(jnp.float32).astype(jnp.bfloat16)
-            tags = jnp.sum(jnp.where(cold_hit, tag_at[...].astype(jnp.float32), 0.0), axis=1, keepdims=True)
-            cold_ref[:, depth:] = jnp.broadcast_to(tags, (cold_rows, TAG)).astype(jnp.bfloat16)
-
-        block = rows_ref[...]
-        hot_ref[...] = narrow(place_hot[...], block)
-        cold_ref[:, pl.ds(pl.multiple_of(step * width, 128), width)] = narrow(place_cold[...], block)
+            hit = lax.broadcasted_iota(jnp.int32, (placed, count), 0) == target_at[...]
+            place[...] = hit.astype(jnp.float32).astype(jnp.bfloat16)
+            tags = jnp.sum(jnp.where(hit, tag_at[...].astype(jnp.float32), 0.0), axis=1, keepdims=True)
+            out_ref[:, depth:] = jnp.broadcast_to(tags, (placed, TAG)).astype(jnp.bfloat16)
+
+        out_ref[:, pl.ds(pl.multiple_of(step * width, 128), width)] = narrow(place[...], rows_ref[...])
 
     index = pl.BlockSpec((1, count), lambda j: (0, 0))
     return pl.pallas_call(
         kernel,
         grid=(blocks,),
-        in_specs=[index, index, index, pl.BlockSpec((count, width), lambda j: (0, j))],
-        out_specs=[
-            pl.BlockSpec((hot_rows, width), lambda j: (0, j)),
-            pl.BlockSpec((cold_rows, depth + TAG), lambda j: (0, 0)),
-        ],
-        out_shape=[
-            jax.ShapeDtypeStruct((hot_rows, depth), jnp.bfloat16),
-            jax.ShapeDtypeStruct((cold_rows, depth + TAG), jnp.bfloat16),
-        ],
-        scratch_shapes=[pltpu.VMEM((hot_rows, count), jnp.bfloat16), pltpu.VMEM((cold_rows, count), jnp.bfloat16)],
+        in_specs=[index, index, pl.BlockSpec((count, width), lambda j: (0, j))],
+        out_specs=pl.BlockSpec((placed, depth + TAG), lambda j: (0, 0)),
+        out_shape=jax.ShapeDtypeStruct((placed, depth + TAG), jnp.bfloat16),
+        scratch_shapes=[pltpu.VMEM((placed, count), jnp.bfloat16)],
         **kernel_params(),
-    )(hot_target[None], cold_target[None], tag[None], rows)
+    )(target[None], tag[None], rows)
 
 
 def base_halves(rows, weight):
@@ -296,12 +286,13 @@
     hot_target = jnp.where(is_hot, hot_target, -1).reshape(-1)
     cold_target = jnp.where(is_cold, cold_target, -1).reshape(-1)
 
-    hot_out, packet = place_rows(
-        rows, hot_target, cold_target, (cold_row % per_dev + 1).reshape(-1), hot_rows, cold_rows
-    )
+    place_hot = pick(jnp.arange(hot_rows, dtype=jnp.int32)[:, None] == hot_target)
+    quarters = [slice(q * depth // 4, (q + 1) * depth // 4) for q in range(4)]
+    hot_out = jnp.concatenate([narrow(place_hot, rows[:, q]) for q in quarters], axis=1)
     hot_out = chain.hold(hot_out.reshape(group_count, near * HCAP, depth))
     done = {"hot_in": lax.all_to_all(hot_out, GROUP, split_axis=0, concat_axis=0, tiled=True)}
 
+    hot_ids = after(hot_ids, chain.last)
     hot_row = jnp.sum(jnp.where(hot_ids[:, :, None] == names, adapter_row, 0), axis=-1)
     hot_first = jnp.where(hot_row // per_dev == me, (hot_row % per_dev) * R, -R * per_dev)
     column = jnp.arange(per_dev * R, dtype=jnp.int32)
@@ -339,8 +330,15 @@
             held[c] = held[c] + got[c, stage - 1]
         return held[c]
 
+    ready = {}
+
     def send(c, stage):
-        got[c, stage] = chain.permute(operand(c, stage), *hops[stage])
+        value = ready[c] if stage == 0 and c in ready else operand(c, stage)
+        got[c, stage] = chain.permute(value, *hops[stage])
+
+    def view(c):
+        mine[c] = after(mine_all, chain.last)[c * part:(c + 1) * part]
+        swapped[c] = after(rest_swapped, chain.last)[(c - 1) * part:c * part]
 
     mine_all, other_first, other_rest = pick_columns(
         after(shrink_store, chain.last), expand_store, want_mine, want_other
@@ -350,6 +348,8 @@
     send(0, 0)
 
     def cold_tokens_out():
+        tag = (cold_row % per_dev + 1).reshape(-1)
+        packet = place_cold(rows, after(cold_target, chain.last), tag, cold_rows)
         sent = chain.hold(packet.reshape(dp_count, step_count * CAP, depth + TAG))
         sent = lax.all_to_all(sent, DP, split_axis=0, concat_axis=0, tiled=True)
         done["packet"] = sent.reshape(cold_rows, depth + TAG)
@@ -401,12 +401,14 @@
     awaited = {0: ["hot_in"], 1: ["packet", "base_own", "base_other"], 2: ["z_cold"], 3: ["base_got"]}
     for slot in range(chunk_count + len(hops) - 1):
         if slot > 0:
-            if slot < chunk_count:
-                mine[slot] = after(mine_all, chain.last)[slot * part:(slot + 1) * part]
-                swapped[slot] = after(rest_swapped, chain.last)[(slot - 1) * part:slot * part]
+            if slot == 1:
+                view(1)
             for stage in sorted(range(len(hops)), key=lambda stage: stage == 1):
                 if 0 <= slot - stage < chunk_count:
                     send(slot - stage, stage)
+            if slot == 1:
+                view(2)
+                ready[2] = chain.hold(operand(2, 0))
         for work in between.get(slot, []):
             work()
         here = [(slot - stage, stage) for stage in range(len(hops)) if 0 <= slot - stage < chunk_count]

time: 171 us -> 173 us (1.012)
  matrix products: 8.45 us -> 16.4 us
  local copies, waits for them, and re-layouts: 8.45 us -> 5.13 us
  waiting for transfers between devices: 75.2 us -> 72.1 us
  other arithmetic: 18.7 us -> 21.3 us
    dot_general x8 -> x12, matrix products: 8.1 us -> 16 us  [matmul(): return jnp.dot(a, b, preferred_element_type=jnp.float32)]
    unnamed x28 -> x26, local copies, waits for them, and re-layouts: 7.62 us -> 4.3 us
    all_to_all x1, waiting for transfers between devices: 4.54 us -> 1.93 us  [on_device(): lax.all_to_all(hot_out, GROUP, split_axis=0, concat_axis=0, tiled=True)]
  transfers between devices with their start and end apart: 18 -> 18, of which waited for: 12 -> 11; matrix products, arithmetic and copies ran while one was open for 13% -> 15% of each run, Pallas kernels for 10% -> 11%
where the time goes in v18:
time: 173 us; the launch traced here: 172 us
  waiting for transfers between devices  72.1 us (42%)
  starting transfers between devices  36.8 us (21%)
  other arithmetic  21.3 us (12%)
  Pallas kernels  20.1 us (12%)
  matrix products  16.4 us (9%)
  local copies, waits for them, and re-layouts  5.13 us (3%)
    ppermute x12, waiting for transfers between devices, permute(): return lax.ppermute(self.hold(value), axis, pairs)  56.2 us
    dot_general x12, matrix products, matmul(): return jnp.dot(a, b, preferred_element_type=jnp.float32)  16 us
    ppermute x12, starting transfers between devices, permute(): return lax.ppermute(self.hold(value), axis, pairs)  14.4 us
    pallas_call x1, Pallas kernels, base_halves(): pl.pallas_call(kernel, grid_spec=pltpu.PrefetchScalarGridSpec(num_scalar_...  9.89 us
    ppermute x1, waiting for transfers between devices, sum_over_tp(): return part + lax.ppermute(part, 'tp', SWAP)  7.21 us
    pallas_call x1, Pallas kernels, pick_columns(): pl.pallas_call(kernel, grid_spec=pltpu.PrefetchScalarGridSpec(num_scalar_...  5.45 us
    all_to_all x1, starting transfers between devices, cold_tokens_out(): sent = lax.all_to_all(sent, DP, split_axis=0, concat_axis=0, tiled=True)  5.41 us
    all_to_all x1, starting transfers between devices, on_device(): lax.all_to_all(hot_out, GROUP, split_axis=0, concat_axis=0, tiled=True)  5.36 us
  transfers between devices with their start and end apart: 18, of which 11 were waited for; matrix products, arithmetic and copies ran while one was open for 15% of the time, Pallas kernels for 11%

profile of v18, /device:TPU:0, one launch (start us, length us, event | category | flops | bytes accessed | tf_op | source)
XLA Modules:
  0.0 172.2 jit_solution(5001291401006681218)
XLA Ops:
  3.3 1.7 convolution_convert_fusion
  5.0 1.7 convolution_convert_fusion.1
  6.7 1.7 convolution_convert_fusion.2
  8.4 1.7 convolution_convert_fusion.3
  10.0 1.6 pad_maximum_fusion
  11.6 5.4 %all-to-all-start = ((bf16[8,32,4096]{2,1,0:T(8,128)(2,1)}), bf16[8,32,4096]{2,1,0:T(8,128)(2,1)S(1)}, u32[]{:S(2)}, u32[]{:S(2)}) async-start(bf16[8,32,4096]{2,1,0:T(8,128)(2,1)} %bitcast.3), calls=%async_computation | async-start | bytes 4194304 | tf_op jit(solution)/shard_map/all_to_all | solution.py:293
  19.1 2.2 %copy-done.2 = bf16[4096,512]{1,0:T(8,128)(2,1)S(1)} copy-done((bf16[4096,512]{1,0:T(8,128)(2,1)S(1)}, bf16[4096,512]{1,0:T(8,128)(2,1)}, u32[]{:S(2)}) %copy-start.2) | copy-done | bytes 4194328
  21.3 5.4 %shard_map.73 = (bf16[4608,512]{1,0:T(8,128)(2,1)S(1)}, bf16[1536,512]{1,0:T(8,128)(2,1)S(1)}, bf16[3072,512]{1,0:T(8,128)(2,1)}) custom-call(s32[4]{0:T(128)S(1)} %convert_element_type.35.mine_held, s32[4]{0:T(128)S(1)} %convert_element_type.36.other_held, s32[1,512]{1,0:T(1,128)S(1)} %bitcast.50, s32[1,512]{1,0:T(1,128)S(1)} %bitcast.51, ...), custom_call_target="tpu_custom_call" | custom-call | flops 1 | bytes 1 | tf_op jit(solution)/shard_map/pallas_call | solution.py:108
  27.3 7.4 %collective-permute-done = bf16[1536,512]{1,0:T(8,128)(2,1)S(1)} collective-permute-done((bf16[1536,512]{1,0:T(8,128)(2,1)S(1)}, bf16[1536,512]{1,0:T(8,128)(2,1)S(1)}, u32[]{:S(2)}, u32[]{:S(2)}) %collective-permute-start) | collective-permute-done | bytes 1572896 | tf_op jit(solution)/shard_map/ppermute | solution.py:48
  34.8 3.7 %collective-permute-start.1 = (bf16[1536,256]{1,0:T(8,128)(2,1)S(1)}, bf16[1536,256]{1,0:T(8,128)(2,1)}, u32[]{:S(2)}, u32[]{:S(2)}) collective-permute-start(bf16[1536,256]{1,0:T(8,128)(2,1)S(1)} %slice_add_fusion), channel_id=1, source_target_pairs={{0,2},{2,0},{1,3},{3,1},{4,6},{6,4},{5,7},{7,5},{8,10},{10,8},{9,1... | collective-permute-start | bytes 2359304 | tf_op jit(solution)/shard_map/ppermute | solution.py:48
  38.5 2.7 %shard_map.74 = bf16[128,4224]{1,0:T(8,128)(2,1)} custom-call(s32[1,512]{1,0:T(1,128)S(1)} %bitcast.49, s32[1,512]{1,0:T(1,128)S(1)} %fusion.36.tag_at, bf16[512,4096]{1,0:T(8,128)(2,1)S(1)} %bitcast.46), custom_call_target="tpu_custom_call" | custom-call | flops 1 | bytes 1 | tf_op jit(solution)/shard_map/pallas_call | solution.py:156
  41.2 1.9 %all-to-all-done = bf16[8,32,4096]{2,1,0:T(8,128)(2,1)S(1)} async-done(((bf16[8,32,4096]{2,1,0:T(8,128)(2,1)}), bf16[8,32,4096]{2,1,0:T(8,128)(2,1)S(1)}, u32[]{:S(2)}, u32[]{:S(2)}) %all-to-all-start) | async-done | bytes 2097184 | tf_op jit(solution)/shard_map/all_to_all | solution.py:293
  43.1 5.4 %all-to-all-start.1 = ((bf16[16,8,4224]{2,1,0:T(8,128)(2,1)}), bf16[16,8,4224]{2,1,0:T(8,128)(2,1)}, u32[]{:S(2)}, u32[]{:S(2)}) async-start(bf16[16,8,4224]{2,1,0:T(8,128)(2,1)} %bitcast.8), calls=%async_computation.1 | async-start | bytes 2162688 | tf_op jit(solution)/shard_map/all_to_all | solution.py:354
  48.6 17.3 %collective-permute-done.1 = bf16[1536,256]{1,0:T(8,128)(2,1)} collective-permute-done((bf16[1536,256]{1,0:T(8,128)(2,1)S(1)}, bf16[1536,256]{1,0:T(8,128)(2,1)}, u32[]{:S(2)}, u32[]{:S(2)}) %collective-permute-start.1) | collective-permute-done | bytes 786464 | tf_op jit(solution)/shard_map/ppermute | solution.py:48
  65.9 2.4 %slice_add_fusion.2 = bf16[1536,256]{1,0:T(8,128)(2,1)} fusion(bf16[3072,512]{1,0:T(8,128)(2,1)} %collective-permute-done.2, bf16[4608,512]{1,0:T(8,128)(2,1)} %copy-done.3), kind=kLoop, calls=%fused_computation.21 | loop fusion | flops 393216 | bytes 2359296 | tf_op jit(solution)/shard_map/add | solution.py:324
  68.3 2.0 %fusion.17 = bf16[1536,128]{1,0:T(8,128)(2,1)} fusion(bf16[1536,512]{1,0:T(8,128)(2,1)} %copy-done.9, bf16[1536,256]{1,0:T(8,128)(2,1)} %collective-permute-done.1, bf16[4608,512]{1,0:T(8,128)(2,1)} %copy-done.3), kind=kLoop, calls=%fused_computation.35 | loop fusion | flops 393216 | bytes 1572864 | tf_op jit(solution)/shard_map/add | solution.py:326
  70.3 1.1 collective-permute-start.4
  71.4 1.5 slice_add_fusion.1
  72.9 1.0 collective-permute-start.5
  73.9 9.9 %shard_map.75 = (f32[512,512]{1,0:T(8,128)S(1)}, f32[512,512]{1,0:T(8,128)S(1)}) custom-call(s32[1]{0:T(128)} %bitcast.10.tp_at, bf16[512,4096]{1,0:T(8,128)(2,1)S(1)} %bitcast.47, bf16[4096,1024]{1,0:T(8,128)(2,1)} %weight_ref), custom_call_target="tpu_custom_call" | custom-call | flops 1 | bytes 1 | tf_op jit(solution)/shard_map/pallas_call | solution.py:194
  83.8 1.0 copy-done.5
  84.8 4.6 %collective-permute-done.3 = bf16[1536,256]{1,0:T(8,128)(2,1)} collective-permute-done((bf16[1536,256]{1,0:T(8,128)(2,1)}, bf16[1536,256]{1,0:T(8,128)(2,1)}, u32[]{:S(2)}, u32[]{:S(2)}) %collective-permute-start.3) | collective-permute-done | bytes 786464 | tf_op jit(solution)/shard_map/ppermute | solution.py:48
  89.5 1.4 fusion.16
  90.9 1.3 slice_add_fusion.6
  92.2 1.1 collective-permute-start.6
  93.4 3.9 %collective-permute-start.7 = (bf16[1536,128]{1,0:T(8,128)(2,1)S(1)}, bf16[1536,128]{1,0:T(8,128)(2,1)S(1)}, u32[]{:S(2)}, u32[]{:S(2)}) collective-permute-start(bf16[1536,128]{1,0:T(8,128)(2,1)S(1)} %fusion.16), channel_id=1, source_target_pairs={{0,8},{8,0},{1,9},{9,1},{2,10},{10,2},{3,11},{11,3},{4,12},{12,4},... | collective-permute-start | bytes 1179656 | tf_op jit(solution)/shard_map/ppermute | solution.py:48
  98.1 3.2 %convolution_select_fusion = f32[128,512]{1,0:T(8,128)S(1)} fusion(bf16[4096,512]{1,0:T(8,128)(2,1)} %store_ref, bf16[128,4224]{1,0:T(8,128)(2,1)} %bitcast.9, s32[512]{0:T(512)S(1)} %fusion.33, s32[128]{0:T(128)S(1)} %convert_reduce_fusion.1), kind=kOutput, calls=%fused_computation.5 | convolution fusion | flops 537001984 | bytes 5507584 | tf_op jit(solution)/shard_map/dot_general | solution.py:22
  101.3 1.6 collective-permute-start.8
  103.4 7.2 %collective-permute-done.8 = f32[128,512]{1,0:T(8,128)S(1)} collective-permute-done((f32[128,512]{1,0:T(8,128)S(1)}, f32[128,512]{1,0:T(8,128)S(1)}, u32[]{:S(2)}, u32[]{:S(2)}) %collective-permute-start.8) | collective-permute-done | bytes 262176 | tf_op jit(solution)/shard_map/ppermute | solution.py:31
  110.8 1.9 %collective-permute-done.7 = bf16[1536,128]{1,0:T(8,128)(2,1)S(1)} collective-permute-done((bf16[1536,128]{1,0:T(8,128)(2,1)S(1)}, bf16[1536,128]{1,0:T(8,128)(2,1)S(1)}, u32[]{:S(2)}, u32[]{:S(2)}) %collective-permute-start.7) | collective-permute-done | bytes 393248 | tf_op jit(solution)/shard_map/ppermute | solution.py:48
  112.7 1.3 add_add_fusion.1
  114.3 1.3 slice_add_fusion.5
  115.6 2.2 %collective-permute-start.9 = (bf16[1536,128]{1,0:T(8,128)(2,1)S(1)}, bf16[1536,128]{1,0:T(8,128)(2,1)S(1)}, u32[]{:S(2)}, u32[]{:S(2)}) collective-permute-start(bf16[1536,128]{1,0:T(8,128)(2,1)S(1)} %slice_add_fusion.5), channel_id=1, source_target_pairs={{0,4},{4,0},{1,5},{5,1},{2,6},{6,2},{3,7},{7,3},{8,12},{12,8},{9,1... | collective-permute-start | bytes 1179656 | tf_op jit(solution)/shard_map/ppermute | solution.py:48
  118.9 14.0 %collective-permute-done.9 = bf16[1536,128]{1,0:T(8,128)(2,1)S(1)} collective-permute-done((bf16[1536,128]{1,0:T(8,128)(2,1)S(1)}, bf16[1536,128]{1,0:T(8,128)(2,1)S(1)}, u32[]{:S(2)}, u32[]{:S(2)}) %collective-permute-start.9) | collective-permute-done | bytes 393248 | tf_op jit(solution)/shard_map/ppermute | solution.py:48
  132.9 1.0 copy-done.10
  134.0 1.3 add_add_fusion.2.first_ref
  136.3 5.1 %all-to-all-start.2 = ((bf16[16,8,512]{2,1,0:T(8,128)(2,1)}), bf16[16,8,512]{2,1,0:T(8,128)(2,1)S(1)}, u32[]{:S(2)}, u32[]{:S(2)}) async-start(bf16[16,8,512]{2,1,0:T(8,128)(2,1)} %fusion), calls=%async_computation.2 | async-start | bytes 262144 | tf_op jit(solution)/shard_map/all_to_all | solution.py:385
  141.3 1.3 fusion.13
  142.7 1.5 fusion.1
  144.2 10.9 %collective-permute-done.12.second_ref = bf16[1536,128]{1,0:T(8,128)(2,1)S(1)} collective-permute-done((bf16[1536,128]{1,0:T(8,128)(2,1)S(1)}, bf16[1536,128]{1,0:T(8,128)(2,1)S(1)}, u32[]{:S(2)}, u32[]{:S(2)}) %collective-permute-start.12) | collective-permute-done | bytes 393248 | tf_op jit(solution)/shard_map/ppermute | solution.py:48
  155.1 1.3 convolution_add_fusion
  156.4 1.6 collective-permute-start.13
  158.2 2.6 %collective-permute-done.13.got_ref = f32[128,128]{1,0:T(8,128)S(1)} collective-permute-done((f32[128,128]{1,0:T(8,128)S(1)}, f32[128,128]{1,0:T(8,128)S(1)}, u32[]{:S(2)}, u32[]{:S(2)}) %collective-permute-start.13) | collective-permute-done | bytes 65568 | tf_op jit(solution)/shard_map/ppermute | solution.py:435
  160.8 0.9 shard_map.76
  161.7 3.4 %all-to-all-start.3 = ((bf16[8,32,512]{2,1,0:T(8,128)(2,1)}), bf16[8,32,512]{2,1,0:T(8,128)(2,1)S(1)}, u32[]{:S(2)}, u32[]{:S(2)}) async-start(bf16[8,32,512]{2,1,0:T(8,128)(2,1)} %bitcast.18), calls=%async_computation.3 | async-start | bytes 524288 | tf_op jit(solution)/shard_map/all_to_all | solution.py:440
  165.5 1.5 add_add_fusion.partial_ref
  167.0 4.1 %all-to-all-done.3 = bf16[8,32,512]{2,1,0:T(8,128)(2,1)S(1)} async-done(((bf16[8,32,512]{2,1,0:T(8,128)(2,1)}), bf16[8,32,512]{2,1,0:T(8,128)(2,1)S(1)}, u32[]{:S(2)}, u32[]{:S(2)}) %all-to-all-start.3) | async-done | bytes 262176 | tf_op jit(solution)/shard_map/all_to_all | solution.py:440
  171.1 1.1 shard_map.77
  (87 shorter events, 10.4 us)
Async XLA Ops:
  11.6 5.4 %copy-start.11 = (s32[128]{0:T(128)S(1)}, s32[128]{0:T(128)}, u32[]{:S(2)}) copy-start(s32[128]{0:T(128)} %param.11) | copy-start | bytes 1540
  11.6 5.4 %copy-start.12 = (s32[4,4]{1,0:T(4,128)S(1)}, s32[4,4]{1,0:T(4,128)}, u32[]{:S(2)}) copy-start(s32[4,4]{1,0:T(4,128)} %param.13) | copy-start | bytes 196
  11.6 7.5 %copy-start.4 = (bf16[512,512]{1,0:T(8,128)(2,1)S(1)}, bf16[512,512]{1,0:T(8,128)(2,1)}, u32[]{:S(2)}) copy-start(bf16[512,512]{1,0:T(8,128)(2,1)} %expand_ref.1) | copy-start | bytes 1572868
  11.6 31.5 %all-to-all-start = ((bf16[8,32,4096]{2,1,0:T(8,128)(2,1)}), bf16[8,32,4096]{2,1,0:T(8,128)(2,1)S(1)}, u32[]{:S(2)}, u32[]{:S(2)}) async-start(bf16[8,32,4096]{2,1,0:T(8,128)(2,1)} %bitcast.3), calls=%async_computation | async-start | bytes 4194304 | tf_op jit(solution)/shard_map/all_to_all | solution.py:293
  19.1 2.2 %copy-start.2 = (bf16[4096,512]{1,0:T(8,128)(2,1)S(1)}, bf16[4096,512]{1,0:T(8,128)(2,1)}, u32[]{:S(2)}) copy-start(bf16[4096,512]{1,0:T(8,128)(2,1)} %store_ref) | copy-start | bytes 12582916
  21.3 17.2 %copy-start = (bf16[4,128,4096]{2,1,0:T(8,128)(2,1)S(1)}, bf16[4,128,4096]{2,1,0:T(8,128)(2,1)}, u32[]{:S(2)}) copy-start(bf16[4,128,4096]{2,1,0:T(8,128)(2,1)} %param.7) | copy-start | bytes 12582916
  26.8 7.9 %copy-start.3 = (bf16[4608,512]{1,0:T(8,128)(2,1)}, bf16[4608,512]{1,0:T(8,128)(2,1)S(1)}, u32[]{:S(2)}) copy-start(bf16[4608,512]{1,0:T(8,128)(2,1)S(1)} %get-tuple-element.65) | copy-start | bytes 14155780
  26.8 39.1 %collective-permute-start.2 = (bf16[3072,512]{1,0:T(8,128)(2,1)}, bf16[3072,512]{1,0:T(8,128)(2,1)}, u32[]{:S(2)}, u32[]{:S(2)}) collective-permute-start(bf16[3072,512]{1,0:T(8,128)(2,1)} %get-tuple-element.55), channel_id=1, source_target_pairs={{0,1},{1,0},{2,3},{3,2},{4,5},{5,4},{6,7},{7,6},{8,9},{9,8},{10,11... | collective-permute-start | bytes 9437192 | tf_op jit(solution)/shard_map/ppermute | solution.py:48
  27.3 7.4 %collective-permute-start = (bf16[1536,512]{1,0:T(8,128)(2,1)S(1)}, bf16[1536,512]{1,0:T(8,128)(2,1)S(1)}, u32[]{:S(2)}, u32[]{:S(2)}) collective-permute-start(bf16[1536,512]{1,0:T(8,128)(2,1)S(1)} %get-tuple-element.53), channel_id=1, source_target_pairs={{0,1},{1,0},{2,3},{3,2},{4,5},{5,4},{6,7},{7,6},{8,9},{9,8},{10,11... | collective-permute-start | bytes 4718600 | tf_op jit(solution)/shard_map/ppermute | solution.py:48
  34.7 6.5 %copy-start.9 = (bf16[1536,512]{1,0:T(8,128)(2,1)}, bf16[1536,512]{1,0:T(8,128)(2,1)S(1)}, u32[]{:S(2)}) copy-start(bf16[1536,512]{1,0:T(8,128)(2,1)S(1)} %collective-permute-done) | copy-start | bytes 4718596
  34.8 31.1 %collective-permute-start.1 = (bf16[1536,256]{1,0:T(8,128)(2,1)S(1)}, bf16[1536,256]{1,0:T(8,128)(2,1)}, u32[]{:S(2)}, u32[]{:S(2)}) collective-permute-start(bf16[1536,256]{1,0:T(8,128)(2,1)S(1)} %slice_add_fusion), channel_id=1, source_target_pairs={{0,2},{2,0},{1,3},{3,1},{4,6},{6,4},{5,7},{7,5},{8,10},{10,8},{9,1... | collective-permute-start | bytes 2359304 | tf_op jit(solution)/shard_map/ppermute | solution.py:48
  43.1 29.8 %copy-start.7 = (bf16[8,32,4096]{2,1,0:T(8,128)(2,1)}, bf16[8,32,4096]{2,1,0:T(8,128)(2,1)S(1)}, u32[]{:S(2)}) copy-start(bf16[8,32,4096]{2,1,0:T(8,128)(2,1)S(1)} %all-to-all-done) | copy-start | bytes 6291460
  43.1 41.7 %all-to-all-start.1 = ((bf16[16,8,4224]{2,1,0:T(8,128)(2,1)}), bf16[16,8,4224]{2,1,0:T(8,128)(2,1)}, u32[]{:S(2)}, u32[]{:S(2)}) async-start(bf16[16,8,4224]{2,1,0:T(8,128)(2,1)} %bitcast.8), calls=%async_computation.1 | async-start | bytes 2162688 | tf_op jit(solution)/shard_map/all_to_all | solution.py:354
  48.6 25.3 %copy-start.1 = (bf16[4,128,4096]{2,1,0:T(8,128)(2,1)S(1)}, bf16[4,128,4096]{2,1,0:T(8,128)(2,1)}, u32[]{:S(2)}) copy-start(bf16[4,128,4096]{2,1,0:T(8,128)(2,1)} %param.7) | copy-start | bytes 12582916
  68.3 21.2 %collective-permute-start.3 = (bf16[1536,256]{1,0:T(8,128)(2,1)}, bf16[1536,256]{1,0:T(8,128)(2,1)}, u32[]{:S(2)}, u32[]{:S(2)}) collective-permute-start(bf16[1536,256]{1,0:T(8,128)(2,1)} %slice_add_fusion.2), channel_id=1, source_target_pairs={{0,2},{2,0},{1,3},{3,1},{4,6},{6,4},{5,7},{7,5},{8,10},{10,8},{9,1... | collective-permute-start | bytes 2359304 | tf_op jit(solution)/shard_map/ppermute | solution.py:48
  70.3 14.5 %collective-permute-start.4 = (bf16[1536,128]{1,0:T(8,128)(2,1)}, bf16[1536,128]{1,0:T(8,128)(2,1)}, u32[]{:S(2)}, u32[]{:S(2)}) collective-permute-start(bf16[1536,128]{1,0:T(8,128)(2,1)} %fusion.17), channel_id=1, source_target_pairs={{0,4},{4,0},{1,5},{5,1},{2,6},{6,2},{3,7},{7,3},{8,12},{12,8},{9,1... | collective-permute-start | bytes 1179656 | tf_op jit(solution)/shard_map/ppermute | solution.py:48
  72.9 37.8 %collective-permute-start.5 = (bf16[1536,256]{1,0:T(8,128)(2,1)S(1)}, bf16[1536,256]{1,0:T(8,128)(2,1)}, u32[]{:S(2)}, u32[]{:S(2)}) collective-permute-start(bf16[1536,256]{1,0:T(8,128)(2,1)S(1)} %slice_add_fusion.1), channel_id=1, source_target_pairs={{0,2},{2,0},{1,3},{3,1},{4,6},{6,4},{5,7},{7,5},{8,10},{10,8},{9,1... | collective-permute-start | bytes 2359304 | tf_op jit(solution)/shard_map/ppermute | solution.py:48
  83.8 1.0 copy-start.5
  92.2 10.7 %copy-start.6 = (f32[512,512]{1,0:T(8,128)S(1)}, f32[512,512]{1,0:T(8,128)}, u32[]{:S(2)}) copy-start(f32[512,512]{1,0:T(8,128)} %copy-done.5) | copy-start | bytes 3145732
  92.2 18.6 %collective-permute-start.6 = (bf16[1536,128]{1,0:T(8,128)(2,1)S(1)}, bf16[1536,128]{1,0:T(8,128)(2,1)S(1)}, u32[]{:S(2)}, u32[]{:S(2)}) collective-permute-start(bf16[1536,128]{1,0:T(8,128)(2,1)S(1)} %slice_add_fusion.6), channel_id=1, source_target_pairs={{0,4},{4,0},{1,5},{5,1},{2,6},{6,2},{3,7},{7,3},{8,12},{12,8},{9,1... | collective-permute-start | bytes 1179656 | tf_op jit(solution)/shard_map/ppermute | solution.py:48
  93.4 19.3 %collective-permute-start.7 = (bf16[1536,128]{1,0:T(8,128)(2,1)S(1)}, bf16[1536,128]{1,0:T(8,128)(2,1)S(1)}, u32[]{:S(2)}, u32[]{:S(2)}) collective-permute-start(bf16[1536,128]{1,0:T(8,128)(2,1)S(1)} %fusion.16), channel_id=1, source_target_pairs={{0,8},{8,0},{1,9},{9,1},{2,10},{10,2},{3,11},{11,3},{4,12},{12,4},... | collective-permute-start | bytes 1179656 | tf_op jit(solution)/shard_map/ppermute | solution.py:48
  101.3 16.5 %copy-start.8 = (bf16[8,32,4096]{2,1,0:T(8,128)(2,1)S(1)}, bf16[8,32,4096]{2,1,0:T(8,128)(2,1)}, u32[]{:S(2)}) copy-start(bf16[8,32,4096]{2,1,0:T(8,128)(2,1)} %copy-done.7) | copy-start | bytes 6291460
  101.3 9.3 %collective-permute-start.8 = (f32[128,512]{1,0:T(8,128)S(1)}, f32[128,512]{1,0:T(8,128)S(1)}, u32[]{:S(2)}, u32[]{:S(2)}) collective-permute-start(f32[128,512]{1,0:T(8,128)S(1)} %convolution_select_fusion), channel_id=1, source_target_pairs={{0,16},{16,0},{1,17},{17,1},{2,18},{18,2},{3,19},{19,3},{4,20},{20... | collective-permute-start | bytes 786440 | tf_op jit(solution)/shard_map/ppermute | solution.py:31
  102.9 30.0 %collective-permute-start.11 = (f32[512,512]{1,0:T(8,128)S(1)}, f32[512,512]{1,0:T(8,128)S(1)}, u32[]{:S(2)}, u32[]{:S(2)}) collective-permute-start(f32[512,512]{1,0:T(8,128)S(1)} %copy-done.6), channel_id=1, source_target_pairs={{0,16},{16,0},{1,17},{17,1},{2,18},{18,2},{3,19},{19,3},{4,20},{20... | collective-permute-start | bytes 3145736 | tf_op jit(solution)/shard_map/ppermute | solution.py:48
  114.0 18.9 %collective-permute-start.10 = (bf16[1536,128]{1,0:T(8,128)(2,1)S(1)}, bf16[1536,128]{1,0:T(8,128)(2,1)S(1)}, u32[]{:S(2)}, u32[]{:S(2)}) collective-permute-start(bf16[1536,128]{1,0:T(8,128)(2,1)S(1)} %add_add_fusion.1), channel_id=1, source_target_pairs={{0,8},{8,0},{1,9},{9,1},{2,10},{10,2},{3,11},{11,3},{4,12},{12,4},... | collective-permute-start | bytes 1179656 | tf_op jit(solution)/shard_map/ppermute | solution.py:48
  115.6 17.3 %collective-permute-start.9 = (bf16[1536,128]{1,0:T(8,128)(2,1)S(1)}, bf16[1536,128]{1,0:T(8,128)(2,1)S(1)}, u32[]{:S(2)}, u32[]{:S(2)}) collective-permute-start(bf16[1536,128]{1,0:T(8,128)(2,1)S(1)} %slice_add_fusion.5), channel_id=1, source_target_pairs={{0,4},{4,0},{1,5},{5,1},{2,6},{6,2},{3,7},{7,3},{8,12},{12,8},{9,1... | collective-permute-start | bytes 1179656 | tf_op jit(solution)/shard_map/ppermute | solution.py:48
  132.9 1.0 copy-start.10
  135.3 19.8 %collective-permute-start.12 = (bf16[1536,128]{1,0:T(8,128)(2,1)S(1)}, bf16[1536,128]{1,0:T(8,128)(2,1)S(1)}, u32[]{:S(2)}, u32[]{:S(2)}) collective-permute-start(bf16[1536,128]{1,0:T(8,128)(2,1)S(1)} %add_add_fusion.2.first_ref), channel_id=1, source_target_pairs={{0,8},{8,0},{1,9},{9,1},{2,10},{10,2},{3,11},{11,3},{4,12},{12,4},... | collective-permute-start | bytes 1179656 | tf_op jit(solution)/shard_map/ppermute | solution.py:48
  136.3 25.5 %all-to-all-start.2 = ((bf16[16,8,512]{2,1,0:T(8,128)(2,1)}), bf16[16,8,512]{2,1,0:T(8,128)(2,1)S(1)}, u32[]{:S(2)}, u32[]{:S(2)}) async-start(bf16[16,8,512]{2,1,0:T(8,128)(2,1)} %fusion), calls=%async_computation.2 | async-start | bytes 262144 | tf_op jit(solution)/shard_map/all_to_all | solution.py:385
  156.4 4.3 %collective-permute-start.13 = (f32[128,128]{1,0:T(8,128)S(1)}, f32[128,128]{1,0:T(8,128)S(1)}, u32[]{:S(2)}, u32[]{:S(2)}) collective-permute-start(f32[128,128]{1,0:T(8,128)S(1)} %fusion.28.own_ref), channel_id=1, source_target_pairs={{0,16},{16,0},{1,17},{17,1},{2,18},{18,2},{3,19},{19,3},{4,20},{20... | collective-permute-start | bytes 196616 | tf_op jit(solution)/shard_map/ppermute | solution.py:435
  161.7 9.4 %all-to-all-start.3 = ((bf16[8,32,512]{2,1,0:T(8,128)(2,1)}), bf16[8,32,512]{2,1,0:T(8,128)(2,1)S(1)}, u32[]{:S(2)}, u32[]{:S(2)}) async-start(bf16[8,32,512]{2,1,0:T(8,128)(2,1)} %bitcast.18), calls=%async_computation.3 | async-start | bytes 524288 | tf_op jit(solution)/shard_map/all_to_all | solution.py:440

commit v19 on v16

--- a/solution.py
+++ b/solution.py
@@ -24,12 +24,6 @@
 
 def narrow(a, b):
     return matmul(a, b).astype(jnp.bfloat16)
-
-
-def sum_over_tp(part):
-    if lax.axis_size("tp") == 2:
-        return part + lax.ppermute(part, "tp", SWAP)
-    return lax.psum(part, "tp")
 
 
 def after(value, *others):
@@ -342,6 +336,10 @@
     def send(c, stage):
         got[c, stage] = chain.permute(operand(c, stage), *hops[stage])
 
+    def view(c):
+        mine[c] = after(mine_all, chain.last)[c * part:(c + 1) * part]
+        swapped[c] = after(rest_swapped, chain.last)[(c - 1) * part:c * part]
+
     mine_all, other_first, other_rest = pick_columns(
         after(shrink_store, chain.last), expand_store, want_mine, want_other
     )
@@ -375,10 +373,15 @@
         done["z_part"] = jnp.where(chosen, product, 0.0)
 
     def cold_over_tp():
-        done["z_cold"] = sum_over_tp(chain.hold(done["z_part"]))
+        z_part = chain.hold(done["z_part"])
+        if lax.axis_size("tp") == 2:
+            done["z_got"] = lax.ppermute(z_part, "tp", SWAP)
+        else:
+            done["z_part"], done["z_got"] = jnp.zeros_like(z_part), lax.psum(z_part, "tp")
 
     def cold_expand():
-        done["delta"] = narrow(done["z_cold"].astype(jnp.bfloat16), after(expand_store, chain.last))
+        z_cold = (done["z_part"] + done["z_got"]).astype(jnp.bfloat16)
+        done["delta"] = narrow(z_cold, after(expand_store, chain.last))
 
     def cold_back():
         delta = chain.hold(done["delta"].reshape(dp_count, step_count * CAP, head_part))
@@ -392,31 +395,39 @@
         )
         done["partial"] = partial + done["base_own"] + done["base_got"]
 
-    between = {
-        0: [cold_tokens_out],
-        1: [base_product],
-        2: [cold_shrink, cold_over_tp, base_over_tp],
-        4: [cold_expand, cold_back, all_but_hot],
-    }
-    awaited = {0: ["hot_in"], 1: ["packet", "base_own", "base_other"], 2: ["z_cold"], 3: ["base_got"]}
-    for slot in range(chunk_count + len(hops) - 1):
-        if slot > 0:
-            if slot < chunk_count:
-                mine[slot] = after(mine_all, chain.last)[slot * part:(slot + 1) * part]
-                swapped[slot] = after(rest_swapped, chain.last)[(slot - 1) * part:slot * part]
-            for stage in sorted(range(len(hops)), key=lambda stage: stage == 1):
-                if 0 <= slot - stage < chunk_count:
-                    send(slot - stage, stage)
-        for work in between.get(slot, []):
-            work()
-        here = [(slot - stage, stage) for stage in range(len(hops)) if 0 <= slot - stage < chunk_count]
-        names_here = awaited.get(slot, [])
-        arrived = lax.optimization_barrier(
-            (chain.last, *[got[at] for at in here], *[done[name] for name in names_here])
-        )
-        chain.last = arrived[0]
-        got.update(zip(here, arrived[1:]))
-        done.update(zip(names_here, arrived[1 + len(here):]))
+    cold_tokens_out()
+    chain.last, got[0, 0], done["hot_in"] = lax.optimization_barrier((chain.last, got[0, 0], done["hot_in"]))
+    view(1)
+    send(1, 0)
+    send(0, 1)
+    view(2)
+    send(2, 0)
+    if far_count == 2:
+        send(0, 2)
+        base_product()
+        send(1, 1)
+        chain.wait(got[0, 2], done["packet"], done["base_own"], done["base_other"])
+        cold_shrink()
+        cold_over_tp()
+        base_over_tp()
+        send(1, 2)
+        send(2, 1)
+        chain.last, _, done["z_got"] = lax.optimization_barrier((chain.last, got[1, 2], done["z_got"]))
+        cold_expand()
+        send(2, 2)
+        cold_back()
+    else:
+        base_product()
+        for c in range(chunk_count):
+            for stage in range(1, len(hops)):
+                if (c, stage) != (0, 1):
+                    send(c, stage)
+        base_over_tp()
+        cold_shrink()
+        cold_over_tp()
+        cold_expand()
+        cold_back()
+    all_but_hot()
     partial = done["partial"]
 
     hot_in = done["hot_in"].reshape(hot_rows, depth)

time: 171 us -> 214 us (1.25)
  blocking collectives: 0 us -> 36.6 us
  waiting for transfers between devices: 75.2 us -> 92.7 us
  starting transfers between devices: 36.9 us -> 25.7 us
  matrix products: 8.45 us -> 12.6 us
  local copies, waits for them, and re-layouts: 8.45 us -> 4.49 us
    all_to_all x0 -> x1, blocking collectives: none -> 36.6 us  [cold_tokens_out(): sent = lax.all_to_all(sent, DP, split_axis=0, concat_axis=0, tiled=True)]
    ppermute x12, waiting for transfers between devices: 56.7 us -> 84.7 us  [permute(): return lax.ppermute(self.hold(value), axis, pairs)]
    ppermute x1, waiting for transfers between devices: 7.21 us -> 1.07 us  [cold_over_tp(): done['z_got'] = lax.ppermute(z_part, 'tp', SWAP)]
    all_to_all x1 -> x0, starting transfers between devices: 4.92 us -> none  [cold_tokens_out(): sent = lax.all_to_all(sent, DP, split_axis=0, concat_axis=0, tiled=True)]
    ppermute x12, starting transfers between devices: 15.4 us -> 10.7 us  [permute(): return lax.ppermute(self.hold(value), axis, pairs)]
    all_to_all x1, waiting for transfers between devices: 4.54 us -> 0.01 us  [on_device(): lax.all_to_all(hot_out, GROUP, split_axis=0, concat_axis=0, tiled=True)]
    unnamed x28 -> x22, local copies, waits for them, and re-layouts: 7.62 us -> 3.66 us
    dot_general x8, matrix products: 8.1 us -> 11 us  [matmul(): return jnp.dot(a, b, preferred_element_type=jnp.float32)]
  transfers between devices with their start and end apart: 18 -> 17, of which waited for: 12 -> 9; matrix products, arithmetic and copies ran while one was open for 13% -> 10% of each run, Pallas kernels for 10% -> 5%
where the time goes in v19:
time: 214 us; the launch traced here: 213 us
  waiting for transfers between devices  92.7 us (43%)
  blocking collectives  36.6 us (17%)
  starting transfers between devices  25.7 us (12%)
  Pallas kernels  21.9 us (10%)
  other arithmetic  18.3 us (9%)
  matrix products  12.6 us (6%)
  local copies, waits for them, and re-layouts  4.49 us (2%)
    ppermute x12, waiting for transfers between devices, permute(): return lax.ppermute(self.hold(value), axis, pairs)  84.7 us
    all_to_all x1, blocking collectives, cold_tokens_out(): sent = lax.all_to_all(sent, DP, split_axis=0, concat_axis=0, tiled=True)  36.6 us
    dot_general x8, matrix products, matmul(): return jnp.dot(a, b, preferred_element_type=jnp.float32)  11 us
    ppermute x12, starting transfers between devices, permute(): return lax.ppermute(self.hold(value), axis, pairs)  10.7 us
    pallas_call x1, Pallas kernels, base_halves(): pl.pallas_call(kernel, grid_spec=pltpu.PrefetchScalarGridSpec(num_scalar_...  10 us
    pallas_call x1, Pallas kernels, pick_columns(): pl.pallas_call(kernel, grid_spec=pltpu.PrefetchScalarGridSpec(num_scalar_...  6.19 us
    all_to_all x1, starting transfers between devices, on_device(): lax.all_to_all(hot_out, GROUP, split_axis=0, concat_axis=0, tiled=True)  4.53 us
  transfers between devices with their start and end apart: 17, of which 9 were waited for; matrix products, arithmetic and copies ran while one was open for 10% of the time, Pallas kernels for 5%

profile of v19, /device:TPU:0, one launch (start us, length us, event | category | flops | bytes accessed | tf_op | source)
XLA Modules:
  0.0 212.7 jit_solution(16305921615177244059)
XLA Ops:
  0.1 0.9 select_reduce_fusion.1
  3.6 0.9 select_reduce_fusion
  5.4 0.8 add_select_fusion.5
  6.2 2.2 %copy-done = bf16[4,128,4096]{2,1,0:T(8,128)(2,1)S(1)} copy-done((bf16[4,128,4096]{2,1,0:T(8,128)(2,1)S(1)}, bf16[4,128,4096]{2,1,0:T(8,128)(2,1)}, u32[]{:S(2)}) %copy-start) | copy-done | bytes 4194328
  8.4 3.6 %shard_map.73 = (bf16[256,4096]{1,0:T(8,128)(2,1)}, bf16[128,4224]{1,0:T(8,128)(2,1)S(1)}) custom-call(s32[1,512]{1,0:T(1,128)S(1)} %bitcast.44, s32[1,512]{1,0:T(1,128)S(1)} %bitcast.46, s32[1,512]{1,0:T(1,128)S(1)} %fusion.35.tag_at, bf16[512,4096]{1,0:T(8,128)(2,1)S(1)} %bitcast.40), custom_call_target="tpu_custom_call" | custom-call | flops 1 | bytes 1 | tf_op jit(solution)/shard_map/pallas_call | solution.py:154
  12.0 1.0 copy-done.5
  13.0 6.2 %shard_map.74 = (bf16[4608,512]{1,0:T(8,128)(2,1)S(1)}, bf16[1536,512]{1,0:T(8,128)(2,1)S(1)}, bf16[3072,512]{1,0:T(8,128)(2,1)S(1)}) custom-call(s32[4]{0:T(128)S(1)} %convert_element_type.18.mine_held, s32[4]{0:T(128)S(1)} %convert_element_type.19.other_held, s32[1,512]{1,0:T(1,128)S(1)} %bitcast.49, s32[1,512]{1,0:T(1,128)S(1)} %bitcast.48, ...), custom_call_target="tpu_custom_call" | custom-call | flops 1 | bytes 1 | tf_op jit(solution)/shard_map/pallas_call | solution.py:102
  19.7 3.0 %collective-permute-done = bf16[1536,512]{1,0:T(8,128)(2,1)S(1)} collective-permute-done((bf16[1536,512]{1,0:T(8,128)(2,1)S(1)}, bf16[1536,512]{1,0:T(8,128)(2,1)S(1)}, u32[]{:S(2)}, u32[]{:S(2)}) %collective-permute-start) | collective-permute-done | bytes 1572896 | tf_op jit(solution)/shard_map/ppermute | solution.py:42
  22.8 1.1 slice_add_fusion
  24.3 36.6 %all_to_all.20 = bf16[16,8,4224]{2,1,0:T(8,128)(2,1)} all-to-all(bf16[16,8,4224]{2,1,0:T(8,128)(2,1)S(1)} %bitcast.42), channel_id=1, replica_groups=mesh['tp'=2,'z_high'=2,'z_low'=2,'x'=2,'core'=2] {'z_high','z_low','x','..., dimensions={0} | all-to-all | bytes 2162688 | tf_op jit(solution)/shard_map/all_to_all | solution.py:352
  60.9 4.5 %all-to-all-start.1 = ((bf16[8,32,4096]{2,1,0:T(8,128)(2,1)}), bf16[8,32,4096]{2,1,0:T(8,128)(2,1)}, u32[]{:S(2)}, u32[]{:S(2)}) async-start(bf16[8,32,4096]{2,1,0:T(8,128)(2,1)} %bitcast.8), calls=%async_computation.1 | async-start | bytes 4194304 | tf_op jit(solution)/shard_map/all_to_all | solution.py:297
  65.6 1.7 collective-permute-start.1
  67.3 0.9 convert_reduce_fusion.1
  68.2 39.6 %collective-permute-done.1 = bf16[1536,256]{1,0:T(8,128)(2,1)} collective-permute-done((bf16[1536,256]{1,0:T(8,128)(2,1)}, bf16[1536,256]{1,0:T(8,128)(2,1)}, u32[]{:S(2)}, u32[]{:S(2)}) %collective-permute-start.1) | collective-permute-done | bytes 786464 | tf_op jit(solution)/shard_map/ppermute | solution.py:42
  107.8 1.5 slice_add_fusion.2
  109.3 1.5 fusion.20
  110.7 1.6 collective-permute-start.4
  112.8 1.5 slice_add_fusion.1
  114.3 1.5 collective-permute-start.6
  115.8 5.6 %collective-permute-done.4 = bf16[1536,128]{1,0:T(8,128)(2,1)S(1)} collective-permute-done((bf16[1536,128]{1,0:T(8,128)(2,1)S(1)}, bf16[1536,128]{1,0:T(8,128)(2,1)S(1)}, u32[]{:S(2)}, u32[]{:S(2)}) %collective-permute-start.4) | collective-permute-done | bytes 393248 | tf_op jit(solution)/shard_map/ppermute | solution.py:42
  121.4 1.4 fusion.22
  122.8 0.7 collective-permute-start.5
  123.6 10.0 %shard_map.75 = (f32[512,512]{1,0:T(8,128)S(1)}, f32[512,512]{1,0:T(8,128)S(1)}) custom-call(s32[1]{0:T(128)} %bitcast.10.tp_at, bf16[512,4096]{1,0:T(8,128)(2,1)S(1)} %bitcast.41, bf16[4096,1024]{1,0:T(8,128)(2,1)} %weight_ref), custom_call_target="tpu_custom_call" | custom-call | flops 1 | bytes 1 | tf_op jit(solution)/shard_map/pallas_call | solution.py:198
  133.6 1.3 slice_add_fusion.8
  134.9 1.6 collective-permute-start.7
  136.5 11.4 %collective-permute-done.6 = bf16[1536,256]{1,0:T(8,128)(2,1)S(1)} collective-permute-done((bf16[1536,256]{1,0:T(8,128)(2,1)S(1)}, bf16[1536,256]{1,0:T(8,128)(2,1)S(1)}, u32[]{:S(2)}, u32[]{:S(2)}) %collective-permute-start.6) | collective-permute-done | bytes 786464 | tf_op jit(solution)/shard_map/ppermute | solution.py:42
  147.9 1.2 slice_add_fusion.5
  149.9 1.6 collective-permute-start.9
  152.0 1.3 fusion.19
  154.5 1.5 fusion.11
  156.0 2.1 %fusion.9 = f32[256,128]{1,0:T(8,128)} fusion(bf16[1536,128]{1,0:T(8,128)(2,1)S(1)} %fusion.19, bf16[256,4096]{1,0:T(8,128)(2,1)} %bitcast.14), kind=kOutput, calls=%fused_computation.16 | convolution fusion | flops 100663296 | bytes 1310720 | tf_op jit(solution)/shard_map/dot_general | solution.py:22
  158.2 1.1 collective-permute-done.9
  159.2 12.3 %collective-permute-done.8 = bf16[1536,128]{1,0:T(8,128)(2,1)S(1)} collective-permute-done((bf16[1536,128]{1,0:T(8,128)(2,1)S(1)}, bf16[1536,128]{1,0:T(8,128)(2,1)S(1)}, u32[]{:S(2)}, u32[]{:S(2)}) %collective-permute-start.8) | collective-permute-done | bytes 393248 | tf_op jit(solution)/shard_map/ppermute | solution.py:42
  171.5 1.4 fusion.18.first_ref
  173.4 0.9 fusion.1
  174.3 4.0 %all-to-all-start.2 = ((bf16[16,8,512]{2,1,0:T(8,128)(2,1)}), bf16[16,8,512]{2,1,0:T(8,128)(2,1)S(1)}, u32[]{:S(2)}, u32[]{:S(2)}) async-start(bf16[16,8,512]{2,1,0:T(8,128)(2,1)} %fusion.1), calls=%async_computation.2 | async-start | bytes 262144 | tf_op jit(solution)/shard_map/all_to_all | solution.py:388
  178.3 1.4 fusion.16
  179.7 1.6 fusion.7
  181.3 12.7 %collective-permute-done.12.second_ref = bf16[1536,128]{1,0:T(8,128)(2,1)S(1)} collective-permute-done((bf16[1536,128]{1,0:T(8,128)(2,1)S(1)}, bf16[1536,128]{1,0:T(8,128)(2,1)S(1)}, u32[]{:S(2)}, u32[]{:S(2)}) %collective-permute-start.12) | collective-permute-done | bytes 393248 | tf_op jit(solution)/shard_map/ppermute | solution.py:42
  194.0 1.3 fusion.14
  195.3 1.5 fusion.5
  196.9 1.6 collective-permute-start.13
  198.4 2.7 %collective-permute-done.13.got_ref = f32[128,128]{1,0:T(8,128)S(1)} collective-permute-done((f32[128,128]{1,0:T(8,128)S(1)}, f32[128,128]{1,0:T(8,128)S(1)}, u32[]{:S(2)}, u32[]{:S(2)}) %collective-permute-start.13) | collective-permute-done | bytes 65568 | tf_op jit(solution)/shard_map/ppermute | solution.py:444
  201.2 0.9 shard_map.76
  202.1 3.4 %all-to-all-start.3 = ((bf16[8,32,512]{2,1,0:T(8,128)(2,1)}), bf16[8,32,512]{2,1,0:T(8,128)(2,1)S(1)}, u32[]{:S(2)}, u32[]{:S(2)}) async-start(bf16[8,32,512]{2,1,0:T(8,128)(2,1)} %bitcast.18), calls=%async_computation.3 | async-start | bytes 524288 | tf_op jit(solution)/shard_map/all_to_all | solution.py:449
  205.7 1.6 fusion.partial_ref
  207.3 4.2 %all-to-all-done.3 = bf16[8,32,512]{2,1,0:T(8,128)(2,1)S(1)} async-done(((bf16[8,32,512]{2,1,0:T(8,128)(2,1)}), bf16[8,32,512]{2,1,0:T(8,128)(2,1)S(1)}, u32[]{:S(2)}, u32[]{:S(2)}) %all-to-all-start.3) | async-done | bytes 262176 | tf_op jit(solution)/shard_map/all_to_all | solution.py:449
  211.5 1.1 shard_map.77
  (74 shorter events, 8.4 us)
Async XLA Ops:
  6.2 2.2 %copy-start = (bf16[4,128,4096]{2,1,0:T(8,128)(2,1)S(1)}, bf16[4,128,4096]{2,1,0:T(8,128)(2,1)}, u32[]{:S(2)}) copy-start(bf16[4,128,4096]{2,1,0:T(8,128)(2,1)} %param.7) | copy-start | bytes 12582916
  8.4 3.6 %copy-start.2 = (bf16[4096,512]{1,0:T(8,128)(2,1)S(1)}, bf16[4096,512]{1,0:T(8,128)(2,1)}, u32[]{:S(2)}) copy-start(bf16[4096,512]{1,0:T(8,128)(2,1)} %store_ref) | copy-start | bytes 12582916
  12.0 1.0 copy-start.5
  19.2 3.6 %copy-start.4 = (bf16[4608,512]{1,0:T(8,128)(2,1)}, bf16[4608,512]{1,0:T(8,128)(2,1)S(1)}, u32[]{:S(2)}) copy-start(bf16[4608,512]{1,0:T(8,128)(2,1)S(1)} %get-tuple-element.57) | copy-start | bytes 14155780
  19.2 3.5 %collective-permute-start = (bf16[1536,512]{1,0:T(8,128)(2,1)S(1)}, bf16[1536,512]{1,0:T(8,128)(2,1)S(1)}, u32[]{:S(2)}, u32[]{:S(2)}) collective-permute-start(bf16[1536,512]{1,0:T(8,128)(2,1)S(1)} %get-tuple-element.46), channel_id=1, source_target_pairs={{0,1},{1,0},{2,3},{3,2},{4,5},{5,4},{6,7},{7,6},{8,9},{9,8},{10,11... | collective-permute-start | bytes 4718600 | tf_op jit(solution)/shard_map/ppermute | solution.py:42
  22.8 1.5 copy-start.8
  60.9 46.9 %all-to-all-start.1 = ((bf16[8,32,4096]{2,1,0:T(8,128)(2,1)}), bf16[8,32,4096]{2,1,0:T(8,128)(2,1)}, u32[]{:S(2)}, u32[]{:S(2)}) async-start(bf16[8,32,4096]{2,1,0:T(8,128)(2,1)} %bitcast.8), calls=%async_computation.1 | async-start | bytes 4194304 | tf_op jit(solution)/shard_map/all_to_all | solution.py:297
  65.4 42.4 %collective-permute-start.2 = (bf16[3072,512]{1,0:T(8,128)(2,1)S(1)}, bf16[3072,512]{1,0:T(8,128)(2,1)}, u32[]{:S(2)}, u32[]{:S(2)}) collective-permute-start(bf16[3072,512]{1,0:T(8,128)(2,1)S(1)} %get-tuple-element.48), channel_id=1, source_target_pairs={{0,1},{1,0},{2,3},{3,2},{4,5},{5,4},{6,7},{7,6},{8,9},{9,8},{10,11... | collective-permute-start | bytes 9437192 | tf_op jit(solution)/shard_map/ppermute | solution.py:42
  65.6 42.2 %collective-permute-start.1 = (bf16[1536,256]{1,0:T(8,128)(2,1)}, bf16[1536,256]{1,0:T(8,128)(2,1)}, u32[]{:S(2)}, u32[]{:S(2)}) collective-permute-start(bf16[1536,256]{1,0:T(8,128)(2,1)} %slice_add_fusion), channel_id=1, source_target_pairs={{0,2},{2,0},{1,3},{3,1},{4,6},{6,4},{5,7},{7,5},{8,10},{10,8},{9,1... | collective-permute-start | bytes 2359304 | tf_op jit(solution)/shard_map/ppermute | solution.py:42
  109.2 14.3 %copy-start.1 = (bf16[4,128,4096]{2,1,0:T(8,128)(2,1)S(1)}, bf16[4,128,4096]{2,1,0:T(8,128)(2,1)}, u32[]{:S(2)}) copy-start(bf16[4,128,4096]{2,1,0:T(8,128)(2,1)} %param.7) | copy-start | bytes 12582916
  110.7 10.7 %collective-permute-start.4 = (bf16[1536,128]{1,0:T(8,128)(2,1)S(1)}, bf16[1536,128]{1,0:T(8,128)(2,1)S(1)}, u32[]{:S(2)}, u32[]{:S(2)}) collective-permute-start(bf16[1536,128]{1,0:T(8,128)(2,1)S(1)} %fusion.20), channel_id=1, source_target_pairs={{0,4},{4,0},{1,5},{5,1},{2,6},{6,2},{3,7},{7,3},{8,12},{12,8},{9,1... | collective-permute-start | bytes 1179656 | tf_op jit(solution)/shard_map/ppermute | solution.py:42
  112.3 21.3 %collective-permute-start.3 = (bf16[1536,256]{1,0:T(8,128)(2,1)S(1)}, bf16[1536,256]{1,0:T(8,128)(2,1)S(1)}, u32[]{:S(2)}, u32[]{:S(2)}) collective-permute-start(bf16[1536,256]{1,0:T(8,128)(2,1)S(1)} %slice_add_fusion.2), channel_id=1, source_target_pairs={{0,2},{2,0},{1,3},{3,1},{4,6},{6,4},{5,7},{7,5},{8,10},{10,8},{9,1... | collective-permute-start | bytes 2359304 | tf_op jit(solution)/shard_map/ppermute | solution.py:42
  114.3 33.7 %collective-permute-start.6 = (bf16[1536,256]{1,0:T(8,128)(2,1)S(1)}, bf16[1536,256]{1,0:T(8,128)(2,1)S(1)}, u32[]{:S(2)}, u32[]{:S(2)}) collective-permute-start(bf16[1536,256]{1,0:T(8,128)(2,1)S(1)} %slice_add_fusion.1), channel_id=1, source_target_pairs={{0,2},{2,0},{1,3},{3,1},{4,6},{6,4},{5,7},{7,5},{8,10},{10,8},{9,1... | collective-permute-start | bytes 2359304 | tf_op jit(solution)/shard_map/ppermute | solution.py:42
  122.8 26.4 %collective-permute-start.5 = (bf16[1536,128]{1,0:T(8,128)(2,1)S(1)}, bf16[1536,128]{1,0:T(8,128)(2,1)S(1)}, u32[]{:S(2)}, u32[]{:S(2)}) collective-permute-start(bf16[1536,128]{1,0:T(8,128)(2,1)S(1)} %fusion.22), channel_id=1, source_target_pairs={{0,8},{8,0},{1,9},{9,1},{2,10},{10,2},{3,11},{11,3},{4,12},{12,4},... | collective-permute-start | bytes 1179656 | tf_op jit(solution)/shard_map/ppermute | solution.py:42
  123.6 25.6 %copy-start.3 = (bf16[4096,512]{1,0:T(8,128)(2,1)S(1)}, bf16[4096,512]{1,0:T(8,128)(2,1)}, u32[]{:S(2)}) copy-start(bf16[4096,512]{1,0:T(8,128)(2,1)} %store_ref) | copy-start | bytes 12582916
  133.6 15.6 %copy-start.7 = (bf16[16,8,4224]{2,1,0:T(8,128)(2,1)S(1)}, bf16[16,8,4224]{2,1,0:T(8,128)(2,1)}, u32[]{:S(2)}) copy-start(bf16[16,8,4224]{2,1,0:T(8,128)(2,1)} %all_to_all.20) | copy-start | bytes 3244036
  134.9 17.1 %collective-permute-start.7 = (bf16[1536,128]{1,0:T(8,128)(2,1)S(1)}, bf16[1536,128]{1,0:T(8,128)(2,1)S(1)}, u32[]{:S(2)}, u32[]{:S(2)}) collective-permute-start(bf16[1536,128]{1,0:T(8,128)(2,1)S(1)} %slice_add_fusion.8), channel_id=1, source_target_pairs={{0,4},{4,0},{1,5},{5,1},{2,6},{6,2},{3,7},{7,3},{8,12},{12,8},{9,1... | collective-permute-start | bytes 1179656 | tf_op jit(solution)/shard_map/ppermute | solution.py:42
  149.9 23.5 %copy-start.6 = (bf16[512,512]{1,0:T(8,128)(2,1)S(1)}, bf16[512,512]{1,0:T(8,128)(2,1)}, u32[]{:S(2)}) copy-start(bf16[512,512]{1,0:T(8,128)(2,1)} %expand_ref.1) | copy-start | bytes 1572868
  149.9 9.3 %collective-permute-start.9 = (f32[128,512]{1,0:T(8,128)S(1)}, f32[128,512]{1,0:T(8,128)S(1)}, u32[]{:S(2)}, u32[]{:S(2)}) collective-permute-start(f32[128,512]{1,0:T(8,128)S(1)} %convolution_select_fusion), channel_id=1, source_target_pairs={{0,16},{16,0},{1,17},{17,1},{2,18},{18,2},{3,19},{19,3},{4,20},{20... | collective-permute-start | bytes 786440 | tf_op jit(solution)/shard_map/ppermute | solution.py:378
  151.5 54.2 %collective-permute-start.11 = (f32[512,512]{1,0:T(8,128)S(1)}, f32[512,512]{1,0:T(8,128)}, u32[]{:S(2)}, u32[]{:S(2)}) collective-permute-start(f32[512,512]{1,0:T(8,128)S(1)} %get-tuple-element.68), channel_id=1, source_target_pairs={{0,16},{16,0},{1,17},{17,1},{2,18},{18,2},{3,19},{19,3},{4,20},{20... | collective-permute-start | bytes 3145736 | tf_op jit(solution)/shard_map/ppermute | solution.py:42
  153.3 18.2 %collective-permute-start.8 = (bf16[1536,128]{1,0:T(8,128)(2,1)S(1)}, bf16[1536,128]{1,0:T(8,128)(2,1)S(1)}, u32[]{:S(2)}, u32[]{:S(2)}) collective-permute-start(bf16[1536,128]{1,0:T(8,128)(2,1)S(1)} %fusion.19), channel_id=1, source_target_pairs={{0,8},{8,0},{1,9},{9,1},{2,10},{10,2},{3,11},{11,3},{4,12},{12,4},... | collective-permute-start | bytes 1179656 | tf_op jit(solution)/shard_map/ppermute | solution.py:42
  154.0 17.5 %collective-permute-start.10 = (bf16[1536,128]{1,0:T(8,128)(2,1)S(1)}, bf16[1536,128]{1,0:T(8,128)(2,1)S(1)}, u32[]{:S(2)}, u32[]{:S(2)}) collective-permute-start(bf16[1536,128]{1,0:T(8,128)(2,1)S(1)} %slice_add_fusion.5), channel_id=1, source_target_pairs={{0,4},{4,0},{1,5},{5,1},{2,6},{6,2},{3,7},{7,3},{8,12},{12,8},{9,1... | collective-permute-start | bytes 1179656 | tf_op jit(solution)/shard_map/ppermute | solution.py:42
  171.5 1.4 copy-start.10
  172.9 21.1 %collective-permute-start.12 = (bf16[1536,128]{1,0:T(8,128)(2,1)S(1)}, bf16[1536,128]{1,0:T(8,128)(2,1)S(1)}, u32[]{:S(2)}, u32[]{:S(2)}) collective-permute-start(bf16[1536,128]{1,0:T(8,128)(2,1)S(1)} %fusion.18.first_ref), channel_id=1, source_target_pairs={{0,8},{8,0},{1,9},{9,1},{2,10},{10,2},{3,11},{11,3},{4,12},{12,4},... | collective-permute-start | bytes 1179656 | tf_op jit(solution)/shard_map/ppermute | solution.py:42
  174.3 27.8 %all-to-all-start.2 = ((bf16[16,8,512]{2,1,0:T(8,128)(2,1)}), bf16[16,8,512]{2,1,0:T(8,128)(2,1)S(1)}, u32[]{:S(2)}, u32[]{:S(2)}) async-start(bf16[16,8,512]{2,1,0:T(8,128)(2,1)} %fusion.1), calls=%async_computation.2 | async-start | bytes 262144 | tf_op jit(solution)/shard_map/all_to_all | solution.py:388
  178.3 17.0 %copy-start.9 = (f32[256,128]{1,0:T(8,128)S(1)}, f32[256,128]{1,0:T(8,128)}, u32[]{:S(2)}) copy-start(f32[256,128]{1,0:T(8,128)} %fusion.9) | copy-start | bytes 393220
  196.9 4.3 %collective-permute-start.13 = (f32[128,128]{1,0:T(8,128)S(1)}, f32[128,128]{1,0:T(8,128)S(1)}, u32[]{:S(2)}, u32[]{:S(2)}) collective-permute-start(f32[128,128]{1,0:T(8,128)S(1)} %fusion.27.own_ref), channel_id=1, source_target_pairs={{0,16},{16,0},{1,17},{17,1},{2,18},{18,2},{3,19},{19,3},{4,20},{20... | collective-permute-start | bytes 196616 | tf_op jit(solution)/shard_map/ppermute | solution.py:444
  202.1 9.4 %all-to-all-start.3 = ((bf16[8,32,512]{2,1,0:T(8,128)(2,1)}), bf16[8,32,512]{2,1,0:T(8,128)(2,1)S(1)}, u32[]{:S(2)}, u32[]{:S(2)}) async-start(bf16[8,32,512]{2,1,0:T(8,128)(2,1)} %bitcast.18), calls=%async_computation.3 | async-start | bytes 524288 | tf_op jit(solution)/shard_map/all_to_all | solution.py:449

commit v20 on v19

--- a/solution.py
+++ b/solution.py
@@ -405,12 +405,17 @@
     if far_count == 2:
         send(0, 2)
         base_product()
+        names_here = ["packet", "base_own", "base_other"]
+        arrived = lax.optimization_barrier((chain.last, got[1, 0], *[done[name] for name in names_here]))
+        chain.last, got[1, 0] = arrived[:2]
+        done.update(zip(names_here, arrived[2:]))
         send(1, 1)
-        chain.wait(got[0, 2], done["packet"], done["base_own"], done["base_other"])
+        chain.wait(got[0, 2])
         cold_shrink()
         cold_over_tp()
         base_over_tp()
         send(1, 2)
+        got[2, 0] = after(got[2, 0], chain.last)
         send(2, 1)
         chain.last, _, done["z_got"] = lax.optimization_barrier((chain.last, got[1, 2], done["z_got"]))
         cold_expand()

time: 214 us -> 174 us (0.81)
  blocking collectives: 36.6 us -> 0 us
  waiting for transfers between devices: 92.7 us -> 70.6 us
  starting transfers between devices: 25.7 us -> 41.2 us
    all_to_all x1 -> x0, blocking collectives: 36.6 us -> none  [cold_tokens_out(): sent = lax.all_to_all(sent, DP, split_axis=0, concat_axis=0, tiled=True)]
    ppermute x12, waiting for transfers between devices: 84.7 us -> 63.4 us  [permute(): return lax.ppermute(self.hold(value), axis, pairs)]
    ppermute x12, starting transfers between devices: 10.7 us -> 19.3 us  [permute(): return lax.ppermute(self.hold(value), axis, pairs)]
    all_to_all x0 -> x1, starting transfers between devices: none -> 5.39 us  [cold_tokens_out(): sent = lax.all_to_all(sent, DP, split_axis=0, concat_axis=0, tiled=True)]
    unnamed x22 -> x24, local copies, waits for them, and re-layouts: 3.66 us -> 5.45 us
  transfers between devices with their start and end apart: 17 -> 18, of which waited for: 9 -> 11; matrix products, arithmetic and copies ran while one was open for 10% -> 17% of each run, Pallas kernels for 5% -> 10%
where the time goes in v20:
time: 174 us; the launch traced here: 172 us
  waiting for transfers between devices  70.6 us (41%)
  starting transfers between devices  41.2 us (24%)
  Pallas kernels  22.3 us (13%)
  other arithmetic  19.7 us (11%)
  matrix products  11.9 us (7%)
  local copies, waits for them, and re-layouts  6.28 us (4%)
    ppermute x12, waiting for transfers between devices, permute(): return lax.ppermute(self.hold(value), axis, pairs)  63.4 us
    ppermute x12, starting transfers between devices, permute(): return lax.ppermute(self.hold(value), axis, pairs)  19.3 us
    dot_general x8, matrix products, matmul(): return jnp.dot(a, b, preferred_element_type=jnp.float32)  11.6 us
    pallas_call x1, Pallas kernels, base_halves(): pl.pallas_call(kernel, grid_spec=pltpu.PrefetchScalarGridSpec(num_scalar_...  10.8 us
    pallas_call x1, Pallas kernels, pick_columns(): pl.pallas_call(kernel, grid_spec=pltpu.PrefetchScalarGridSpec(num_scalar_...  5.47 us
    unnamed x24, local copies, waits for them, and re-layouts  5.45 us
    all_to_all x1, starting transfers between devices, cold_tokens_out(): sent = lax.all_to_all(sent, DP, split_axis=0, concat_axis=0, tiled=True)  5.39 us
    all_to_all x1, starting transfers between devices, on_device(): lax.all_to_all(hot_out, GROUP, split_axis=0, concat_axis=0, tiled=True)  5.37 us
  transfers between devices with their start and end apart: 18, of which 11 were waited for; matrix products, arithmetic and copies ran while one was open for 17% of the time, Pallas kernels for 10%

profile of v20, /device:TPU:0, one launch (start us, length us, event | category | flops | bytes accessed | tf_op | source)
XLA Modules:
  0.0 172.2 jit_solution(9105969285524626059)
XLA Ops:
  0.7 0.9 select_reduce_fusion
  3.3 2.2 %copy-done = bf16[4,128,4096]{2,1,0:T(8,128)(2,1)S(1)} copy-done((bf16[4,128,4096]{2,1,0:T(8,128)(2,1)S(1)}, bf16[4,128,4096]{2,1,0:T(8,128)(2,1)}, u32[]{:S(2)}) %copy-start) | copy-done | bytes 4194328
  5.5 3.9 %shard_map.73 = (bf16[256,4096]{1,0:T(8,128)(2,1)}, bf16[128,4224]{1,0:T(8,128)(2,1)}) custom-call(s32[1,512]{1,0:T(1,128)S(1)} %bitcast.45, s32[1,512]{1,0:T(1,128)S(1)} %bitcast.43, s32[1,512]{1,0:T(1,128)S(1)} %fusion.33.tag_at, bf16[512,4096]{1,0:T(8,128)(2,1)S(1)} %bitcast.40), custom_call_target="tpu_custom_call" | custom-call | flops 1 | bytes 1 | tf_op jit(solution)/shard_map/pallas_call | solution.py:154
  9.4 5.4 %all-to-all-start = ((bf16[8,32,4096]{2,1,0:T(8,128)(2,1)}), bf16[8,32,4096]{2,1,0:T(8,128)(2,1)S(1)}, u32[]{:S(2)}, u32[]{:S(2)}) async-start(bf16[8,32,4096]{2,1,0:T(8,128)(2,1)} %bitcast.7), calls=%async_computation | async-start | bytes 4194304 | tf_op jit(solution)/shard_map/all_to_all | solution.py:297
  17.0 2.2 %copy-done.2 = bf16[4096,512]{1,0:T(8,128)(2,1)S(1)} copy-done((bf16[4096,512]{1,0:T(8,128)(2,1)S(1)}, bf16[4096,512]{1,0:T(8,128)(2,1)}, u32[]{:S(2)}) %copy-start.2) | copy-done | bytes 4194328
  19.1 5.5 %shard_map.74 = (bf16[4608,512]{1,0:T(8,128)(2,1)S(1)}, bf16[1536,512]{1,0:T(8,128)(2,1)S(1)}, bf16[3072,512]{1,0:T(8,128)(2,1)}) custom-call(s32[4]{0:T(128)S(1)} %convert_element_type.18.mine_held, s32[4]{0:T(128)S(1)} %convert_element_type.19.other_held, s32[1,512]{1,0:T(1,128)S(1)} %bitcast.48, s32[1,512]{1,0:T(1,128)S(1)} %bitcast.47, ...), custom_call_target="tpu_custom_call" | custom-call | flops 1 | bytes 1 | tf_op jit(solution)/shard_map/pallas_call | solution.py:102
  24.6 2.4 %collective-permute-start.2 = (bf16[3072,512]{1,0:T(8,128)(2,1)}, bf16[3072,512]{1,0:T(8,128)(2,1)}, u32[]{:S(2)}, u32[]{:S(2)}) collective-permute-start(bf16[3072,512]{1,0:T(8,128)(2,1)} %get-tuple-element.52), channel_id=1, source_target_pairs={{0,1},{1,0},{2,3},{3,2},{4,5},{5,4},{6,7},{7,6},{8,9},{9,8},{10,11... | collective-permute-start | bytes 9437192 | tf_op jit(solution)/shard_map/ppermute | solution.py:42
  27.0 7.4 %collective-permute-done = bf16[1536,512]{1,0:T(8,128)(2,1)S(1)} collective-permute-done((bf16[1536,512]{1,0:T(8,128)(2,1)S(1)}, bf16[1536,512]{1,0:T(8,128)(2,1)S(1)}, u32[]{:S(2)}, u32[]{:S(2)}) %collective-permute-start) | collective-permute-done | bytes 1572896 | tf_op jit(solution)/shard_map/ppermute | solution.py:42
  34.6 1.0 copy-done.7
  35.6 3.9 %collective-permute-start.1 = (bf16[1536,256]{1,0:T(8,128)(2,1)S(1)}, bf16[1536,256]{1,0:T(8,128)(2,1)}, u32[]{:S(2)}, u32[]{:S(2)}) collective-permute-start(bf16[1536,256]{1,0:T(8,128)(2,1)S(1)} %slice_add_fusion), channel_id=1, source_target_pairs={{0,2},{2,0},{1,3},{3,1},{4,6},{6,4},{5,7},{7,5},{8,10},{10,8},{9,1... | collective-permute-start | bytes 2359304 | tf_op jit(solution)/shard_map/ppermute | solution.py:42
  40.5 5.4 %all-to-all-start.1 = ((bf16[16,8,4224]{2,1,0:T(8,128)(2,1)}), bf16[16,8,4224]{2,1,0:T(8,128)(2,1)}, u32[]{:S(2)}, u32[]{:S(2)}) async-start(bf16[16,8,4224]{2,1,0:T(8,128)(2,1)} %bitcast.8), calls=%async_computation.1 | async-start | bytes 2162688 | tf_op jit(solution)/shard_map/all_to_all | solution.py:352
  45.9 18.8 %collective-permute-done.1 = bf16[1536,256]{1,0:T(8,128)(2,1)} collective-permute-done((bf16[1536,256]{1,0:T(8,128)(2,1)S(1)}, bf16[1536,256]{1,0:T(8,128)(2,1)}, u32[]{:S(2)}, u32[]{:S(2)}) %collective-permute-start.1) | collective-permute-done | bytes 786464 | tf_op jit(solution)/shard_map/ppermute | solution.py:42
  64.7 2.4 %slice_add_fusion.2 = bf16[1536,256]{1,0:T(8,128)(2,1)} fusion(bf16[3072,512]{1,0:T(8,128)(2,1)} %collective-permute-done.2, bf16[4608,512]{1,0:T(8,128)(2,1)} %copy-done.3), kind=kLoop, calls=%fused_computation.12 | loop fusion | flops 393216 | bytes 2359296 | tf_op jit(solution)/shard_map/add | solution.py:327
  67.1 1.5 fusion.17
  69.1 2.1 %collective-permute-start.4 = (bf16[1536,256]{1,0:T(8,128)(2,1)}, bf16[1536,256]{1,0:T(8,128)(2,1)}, u32[]{:S(2)}, u32[]{:S(2)}) collective-permute-start(bf16[1536,256]{1,0:T(8,128)(2,1)} %slice_add_fusion.2), channel_id=1, source_target_pairs={{0,2},{2,0},{1,3},{3,1},{4,6},{6,4},{5,7},{7,5},{8,10},{10,8},{9,1... | collective-permute-start | bytes 2359304 | tf_op jit(solution)/shard_map/ppermute | solution.py:42
  71.2 1.5 slice_add_fusion.1
  72.8 6.1 %collective-permute-done.3 = bf16[1536,128]{1,0:T(8,128)(2,1)S(1)} collective-permute-done((bf16[1536,128]{1,0:T(8,128)(2,1)S(1)}, bf16[1536,128]{1,0:T(8,128)(2,1)S(1)}, u32[]{:S(2)}, u32[]{:S(2)}) %collective-permute-start.3) | collective-permute-done | bytes 393248 | tf_op jit(solution)/shard_map/ppermute | solution.py:42
  78.9 1.4 fusion.19
  80.2 2.8 %collective-permute-start.5 = (bf16[1536,128]{1,0:T(8,128)(2,1)S(1)}, bf16[1536,128]{1,0:T(8,128)(2,1)}, u32[]{:S(2)}, u32[]{:S(2)}) collective-permute-start(bf16[1536,128]{1,0:T(8,128)(2,1)S(1)} %fusion.19), channel_id=1, source_target_pairs={{0,8},{8,0},{1,9},{9,1},{2,10},{10,2},{3,11},{11,3},{4,12},{12,4},... | collective-permute-start | bytes 1179656 | tf_op jit(solution)/shard_map/ppermute | solution.py:42
  83.0 10.8 %shard_map.75 = (f32[512,512]{1,0:T(8,128)S(1)}, f32[512,512]{1,0:T(8,128)}) custom-call(s32[1]{0:T(128)} %bitcast.10.tp_at, bf16[512,4096]{1,0:T(8,128)(2,1)S(1)} %bitcast.41, bf16[4096,1024]{1,0:T(8,128)(2,1)} %weight_ref), custom_call_target="tpu_custom_call" | custom-call | flops 1 | bytes 1 | tf_op jit(solution)/shard_map/pallas_call | solution.py:198
  93.9 1.3 slice_add_fusion.6
  95.2 2.0 %collective-permute-start.7 = (bf16[1536,128]{1,0:T(8,128)(2,1)S(1)}, bf16[1536,128]{1,0:T(8,128)(2,1)S(1)}, u32[]{:S(2)}, u32[]{:S(2)}) collective-permute-start(bf16[1536,128]{1,0:T(8,128)(2,1)S(1)} %slice_add_fusion.6), channel_id=1, source_target_pairs={{0,4},{4,0},{1,5},{5,1},{2,6},{6,2},{3,7},{7,3},{8,12},{12,8},{9,1... | collective-permute-start | bytes 1179656 | tf_op jit(solution)/shard_map/ppermute | solution.py:42
  98.1 1.5 collective-permute-done.5
  99.6 3.2 %convolution_select_fusion = f32[128,512]{1,0:T(8,128)S(1)} fusion(bf16[4096,512]{1,0:T(8,128)(2,1)} %store_ref, bf16[128,4224]{1,0:T(8,128)(2,1)} %bitcast.9, s32[512]{0:T(512)S(1)} %fusion.27, s32[128]{0:T(128)S(1)} %convert_reduce_fusion.1), kind=kOutput, calls=%fused_computation | convolution fusion | flops 537001984 | bytes 5507584 | tf_op jit(solution)/shard_map/dot_general | solution.py:22
  102.8 1.6 collective-permute-start.9
  104.9 2.9 %collective-permute-done.7 = bf16[1536,128]{1,0:T(8,128)(2,1)S(1)} collective-permute-done((bf16[1536,128]{1,0:T(8,128)(2,1)S(1)}, bf16[1536,128]{1,0:T(8,128)(2,1)S(1)}, u32[]{:S(2)}, u32[]{:S(2)}) %collective-permute-start.7) | collective-permute-done | bytes 393248 | tf_op jit(solution)/shard_map/ppermute | solution.py:42
  107.8 1.4 add_add_fusion.2
  109.2 1.7 collective-permute-start.8
  110.8 1.3 slice_add_fusion.5
  112.1 2.5 %collective-permute-start.10 = (bf16[1536,128]{1,0:T(8,128)(2,1)S(1)}, bf16[1536,128]{1,0:T(8,128)(2,1)S(1)}, u32[]{:S(2)}, u32[]{:S(2)}) collective-permute-start(bf16[1536,128]{1,0:T(8,128)(2,1)S(1)} %slice_add_fusion.5), channel_id=1, source_target_pairs={{0,4},{4,0},{1,5},{5,1},{2,6},{6,2},{3,7},{7,3},{8,12},{12,8},{9,1... | collective-permute-start | bytes 1179656 | tf_op jit(solution)/shard_map/ppermute | solution.py:42
  114.7 1.4 fusion.10
  116.4 13.3 %collective-permute-done.8 = bf16[1536,128]{1,0:T(8,128)(2,1)S(1)} collective-permute-done((bf16[1536,128]{1,0:T(8,128)(2,1)S(1)}, bf16[1536,128]{1,0:T(8,128)(2,1)S(1)}, u32[]{:S(2)}, u32[]{:S(2)}) %collective-permute-start.8) | collective-permute-done | bytes 393248 | tf_op jit(solution)/shard_map/ppermute | solution.py:42
  129.7 1.5 collective-permute-done.10
  131.1 1.4 add_add_fusion.1.first_ref
  133.1 0.9 fusion
  134.0 4.5 %all-to-all-start.2 = ((bf16[16,8,512]{2,1,0:T(8,128)(2,1)}), bf16[16,8,512]{2,1,0:T(8,128)(2,1)S(1)}, u32[]{:S(2)}, u32[]{:S(2)}) async-start(bf16[16,8,512]{2,1,0:T(8,128)(2,1)} %fusion), calls=%async_computation.2 | async-start | bytes 262144 | tf_op jit(solution)/shard_map/all_to_all | solution.py:388
  138.5 1.3 fusion.15
  139.8 1.6 fusion.6
  141.4 12.1 %collective-permute-done.12.second_ref = bf16[1536,128]{1,0:T(8,128)(2,1)S(1)} collective-permute-done((bf16[1536,128]{1,0:T(8,128)(2,1)S(1)}, bf16[1536,128]{1,0:T(8,128)(2,1)S(1)}, u32[]{:S(2)}, u32[]{:S(2)}) %collective-permute-start.12) | collective-permute-done | bytes 393248 | tf_op jit(solution)/shard_map/ppermute | solution.py:42
  153.5 1.3 fusion.13
  154.9 1.5 fusion.4
  156.4 1.6 collective-permute-start.13
  158.2 2.6 %collective-permute-done.13.got_ref = f32[128,128]{1,0:T(8,128)S(1)} collective-permute-done((f32[128,128]{1,0:T(8,128)S(1)}, f32[128,128]{1,0:T(8,128)S(1)}, u32[]{:S(2)}, u32[]{:S(2)}) %collective-permute-start.13) | collective-permute-done | bytes 65568 | tf_op jit(solution)/shard_map/ppermute | solution.py:449
  160.7 0.9 shard_map.76
  161.7 3.4 %all-to-all-start.3 = ((bf16[8,32,512]{2,1,0:T(8,128)(2,1)}), bf16[8,32,512]{2,1,0:T(8,128)(2,1)S(1)}, u32[]{:S(2)}, u32[]{:S(2)}) async-start(bf16[8,32,512]{2,1,0:T(8,128)(2,1)} %bitcast.18), calls=%async_computation.3 | async-start | bytes 524288 | tf_op jit(solution)/shard_map/all_to_all | solution.py:454
  165.5 1.5 add_add_fusion.partial_ref
  167.0 4.1 %all-to-all-done.3 = bf16[8,32,512]{2,1,0:T(8,128)(2,1)S(1)} async-done(((bf16[8,32,512]{2,1,0:T(8,128)(2,1)}), bf16[8,32,512]{2,1,0:T(8,128)(2,1)S(1)}, u32[]{:S(2)}, u32[]{:S(2)}) %all-to-all-start.3) | async-done | bytes 262176 | tf_op jit(solution)/shard_map/all_to_all | solution.py:454
  171.1 1.1 shard_map.77
  (78 shorter events, 9.1 us)
Async XLA Ops:
  3.3 2.2 %copy-start = (bf16[4,128,4096]{2,1,0:T(8,128)(2,1)S(1)}, bf16[4,128,4096]{2,1,0:T(8,128)(2,1)}, u32[]{:S(2)}) copy-start(bf16[4,128,4096]{2,1,0:T(8,128)(2,1)} %param.7) | copy-start | bytes 12582916
  9.4 5.4 %copy-start.8 = (s32[128]{0:T(128)S(1)}, s32[128]{0:T(128)}, u32[]{:S(2)}) copy-start(s32[128]{0:T(128)} %param.11) | copy-start | bytes 1540
  9.4 5.5 %copy-start.9 = (s32[4,4]{1,0:T(4,128)S(1)}, s32[4,4]{1,0:T(4,128)}, u32[]{:S(2)}) copy-start(s32[4,4]{1,0:T(4,128)} %param.13) | copy-start | bytes 196
  9.4 7.5 %copy-start.4 = (bf16[512,512]{1,0:T(8,128)(2,1)S(1)}, bf16[512,512]{1,0:T(8,128)(2,1)}, u32[]{:S(2)}) copy-start(bf16[512,512]{1,0:T(8,128)(2,1)} %expand_ref.1) | copy-start | bytes 1572868
  9.4 31.1 %all-to-all-start = ((bf16[8,32,4096]{2,1,0:T(8,128)(2,1)}), bf16[8,32,4096]{2,1,0:T(8,128)(2,1)S(1)}, u32[]{:S(2)}, u32[]{:S(2)}) async-start(bf16[8,32,4096]{2,1,0:T(8,128)(2,1)} %bitcast.7), calls=%async_computation | async-start | bytes 4194304 | tf_op jit(solution)/shard_map/all_to_all | solution.py:297
  16.9 2.2 %copy-start.2 = (bf16[4096,512]{1,0:T(8,128)(2,1)S(1)}, bf16[4096,512]{1,0:T(8,128)(2,1)}, u32[]{:S(2)}) copy-start(bf16[4096,512]{1,0:T(8,128)(2,1)} %store_ref) | copy-start | bytes 12582916
  24.6 9.8 %copy-start.3 = (bf16[4608,512]{1,0:T(8,128)(2,1)}, bf16[4608,512]{1,0:T(8,128)(2,1)S(1)}, u32[]{:S(2)}) copy-start(bf16[4608,512]{1,0:T(8,128)(2,1)S(1)} %get-tuple-element.61) | copy-start | bytes 14155780
  24.6 40.1 %collective-permute-start.2 = (bf16[3072,512]{1,0:T(8,128)(2,1)}, bf16[3072,512]{1,0:T(8,128)(2,1)}, u32[]{:S(2)}, u32[]{:S(2)}) collective-permute-start(bf16[3072,512]{1,0:T(8,128)(2,1)} %get-tuple-element.52), channel_id=1, source_target_pairs={{0,1},{1,0},{2,3},{3,2},{4,5},{5,4},{6,7},{7,6},{8,9},{9,8},{10,11... | collective-permute-start | bytes 9437192 | tf_op jit(solution)/shard_map/ppermute | solution.py:42
  27.0 7.4 %collective-permute-start = (bf16[1536,512]{1,0:T(8,128)(2,1)S(1)}, bf16[1536,512]{1,0:T(8,128)(2,1)S(1)}, u32[]{:S(2)}, u32[]{:S(2)}) collective-permute-start(bf16[1536,512]{1,0:T(8,128)(2,1)S(1)} %get-tuple-element.49), channel_id=1, source_target_pairs={{0,1},{1,0},{2,3},{3,2},{4,5},{5,4},{6,7},{7,6},{8,9},{9,8},{10,11... | collective-permute-start | bytes 4718600 | tf_op jit(solution)/shard_map/ppermute | solution.py:42
  34.4 1.2 copy-start.7
  35.6 29.1 %collective-permute-start.1 = (bf16[1536,256]{1,0:T(8,128)(2,1)S(1)}, bf16[1536,256]{1,0:T(8,128)(2,1)}, u32[]{:S(2)}, u32[]{:S(2)}) collective-permute-start(bf16[1536,256]{1,0:T(8,128)(2,1)S(1)} %slice_add_fusion), channel_id=1, source_target_pairs={{0,2},{2,0},{1,3},{3,1},{4,6},{6,4},{5,7},{7,5},{8,10},{10,8},{9,1... | collective-permute-start | bytes 2359304 | tf_op jit(solution)/shard_map/ppermute | solution.py:42
  40.5 32.2 %copy-start.5 = (bf16[8,32,4096]{2,1,0:T(8,128)(2,1)}, bf16[8,32,4096]{2,1,0:T(8,128)(2,1)S(1)}, u32[]{:S(2)}) copy-start(bf16[8,32,4096]{2,1,0:T(8,128)(2,1)S(1)} %all-to-all-done) | copy-start | bytes 6291460
  40.5 53.4 %all-to-all-start.1 = ((bf16[16,8,4224]{2,1,0:T(8,128)(2,1)}), bf16[16,8,4224]{2,1,0:T(8,128)(2,1)}, u32[]{:S(2)}, u32[]{:S(2)}) async-start(bf16[16,8,4224]{2,1,0:T(8,128)(2,1)} %bitcast.8), calls=%async_computation.1 | async-start | bytes 2162688 | tf_op jit(solution)/shard_map/all_to_all | solution.py:352
  67.1 16.0 %copy-start.1 = (bf16[4,128,4096]{2,1,0:T(8,128)(2,1)S(1)}, bf16[4,128,4096]{2,1,0:T(8,128)(2,1)}, u32[]{:S(2)}) copy-start(bf16[4,128,4096]{2,1,0:T(8,128)(2,1)} %param.7) | copy-start | bytes 12582916
  68.5 10.4 %collective-permute-start.3 = (bf16[1536,128]{1,0:T(8,128)(2,1)S(1)}, bf16[1536,128]{1,0:T(8,128)(2,1)S(1)}, u32[]{:S(2)}, u32[]{:S(2)}) collective-permute-start(bf16[1536,128]{1,0:T(8,128)(2,1)S(1)} %fusion.17), channel_id=1, source_target_pairs={{0,4},{4,0},{1,5},{5,1},{2,6},{6,2},{3,7},{7,3},{8,12},{12,8},{9,1... | collective-permute-start | bytes 1179656 | tf_op jit(solution)/shard_map/ppermute | solution.py:42
  69.1 24.8 %collective-permute-start.4 = (bf16[1536,256]{1,0:T(8,128)(2,1)}, bf16[1536,256]{1,0:T(8,128)(2,1)}, u32[]{:S(2)}, u32[]{:S(2)}) collective-permute-start(bf16[1536,256]{1,0:T(8,128)(2,1)} %slice_add_fusion.2), channel_id=1, source_target_pairs={{0,2},{2,0},{1,3},{3,1},{4,6},{6,4},{5,7},{7,5},{8,10},{10,8},{9,1... | collective-permute-start | bytes 2359304 | tf_op jit(solution)/shard_map/ppermute | solution.py:42
  72.7 38.1 %collective-permute-start.6 = (bf16[1536,256]{1,0:T(8,128)(2,1)S(1)}, bf16[1536,256]{1,0:T(8,128)(2,1)}, u32[]{:S(2)}, u32[]{:S(2)}) collective-permute-start(bf16[1536,256]{1,0:T(8,128)(2,1)S(1)} %slice_add_fusion.1), channel_id=1, source_target_pairs={{0,2},{2,0},{1,3},{3,1},{4,6},{6,4},{5,7},{7,5},{8,10},{10,8},{9,1... | collective-permute-start | bytes 2359304 | tf_op jit(solution)/shard_map/ppermute | solution.py:42
  80.2 19.3 %collective-permute-start.5 = (bf16[1536,128]{1,0:T(8,128)(2,1)S(1)}, bf16[1536,128]{1,0:T(8,128)(2,1)}, u32[]{:S(2)}, u32[]{:S(2)}) collective-permute-start(bf16[1536,128]{1,0:T(8,128)(2,1)S(1)} %fusion.19), channel_id=1, source_target_pairs={{0,8},{8,0},{1,9},{9,1},{2,10},{10,2},{3,11},{11,3},{4,12},{12,4},... | collective-permute-start | bytes 1179656 | tf_op jit(solution)/shard_map/ppermute | solution.py:42
  95.2 12.6 %collective-permute-start.7 = (bf16[1536,128]{1,0:T(8,128)(2,1)S(1)}, bf16[1536,128]{1,0:T(8,128)(2,1)S(1)}, u32[]{:S(2)}, u32[]{:S(2)}) collective-permute-start(bf16[1536,128]{1,0:T(8,128)(2,1)S(1)} %slice_add_fusion.6), channel_id=1, source_target_pairs={{0,4},{4,0},{1,5},{5,1},{2,6},{6,2},{3,7},{7,3},{8,12},{12,8},{9,1... | collective-permute-start | bytes 1179656 | tf_op jit(solution)/shard_map/ppermute | solution.py:42
  102.8 11.9 %copy-start.6 = (bf16[8,32,4096]{2,1,0:T(8,128)(2,1)S(1)}, bf16[8,32,4096]{2,1,0:T(8,128)(2,1)}, u32[]{:S(2)}) copy-start(bf16[8,32,4096]{2,1,0:T(8,128)(2,1)} %copy-done.5) | copy-start | bytes 6291460
  102.8 13.6 %collective-permute-start.9 = (f32[128,512]{1,0:T(8,128)S(1)}, f32[128,512]{1,0:T(8,128)S(1)}, u32[]{:S(2)}, u32[]{:S(2)}) collective-permute-start(f32[128,512]{1,0:T(8,128)S(1)} %convolution_select_fusion), channel_id=1, source_target_pairs={{0,16},{16,0},{1,17},{17,1},{2,18},{18,2},{3,19},{19,3},{4,20},{20... | collective-permute-start | bytes 786440 | tf_op jit(solution)/shard_map/ppermute | solution.py:378
  104.4 61.0 %collective-permute-start.11 = (f32[512,512]{1,0:T(8,128)}, f32[512,512]{1,0:T(8,128)}, u32[]{:S(2)}, u32[]{:S(2)}) collective-permute-start(f32[512,512]{1,0:T(8,128)} %get-tuple-element.74), channel_id=1, source_target_pairs={{0,16},{16,0},{1,17},{17,1},{2,18},{18,2},{3,19},{19,3},{4,20},{20... | collective-permute-start | bytes 3145736 | tf_op jit(solution)/shard_map/ppermute | solution.py:42
  109.2 20.5 %collective-permute-start.8 = (bf16[1536,128]{1,0:T(8,128)(2,1)S(1)}, bf16[1536,128]{1,0:T(8,128)(2,1)S(1)}, u32[]{:S(2)}, u32[]{:S(2)}) collective-permute-start(bf16[1536,128]{1,0:T(8,128)(2,1)S(1)} %add_add_fusion.2), channel_id=1, source_target_pairs={{0,8},{8,0},{1,9},{9,1},{2,10},{10,2},{3,11},{11,3},{4,12},{12,4},... | collective-permute-start | bytes 1179656 | tf_op jit(solution)/shard_map/ppermute | solution.py:42
  112.1 19.0 %collective-permute-start.10 = (bf16[1536,128]{1,0:T(8,128)(2,1)S(1)}, bf16[1536,128]{1,0:T(8,128)(2,1)S(1)}, u32[]{:S(2)}, u32[]{:S(2)}) collective-permute-start(bf16[1536,128]{1,0:T(8,128)(2,1)S(1)} %slice_add_fusion.5), channel_id=1, source_target_pairs={{0,4},{4,0},{1,5},{5,1},{2,6},{6,2},{3,7},{7,3},{8,12},{12,8},{9,1... | collective-permute-start | bytes 1179656 | tf_op jit(solution)/shard_map/ppermute | solution.py:42
  129.7 3.4 %copy-start.11 = (bf16[1536,128]{1,0:T(8,128)(2,1)}, bf16[1536,128]{1,0:T(8,128)(2,1)S(1)}, u32[]{:S(2)}) copy-start(bf16[1536,128]{1,0:T(8,128)(2,1)S(1)} %collective-permute-done.8) | copy-start | bytes 1179652
  132.5 21.0 %collective-permute-start.12 = (bf16[1536,128]{1,0:T(8,128)(2,1)S(1)}, bf16[1536,128]{1,0:T(8,128)(2,1)S(1)}, u32[]{:S(2)}, u32[]{:S(2)}) collective-permute-start(bf16[1536,128]{1,0:T(8,128)(2,1)S(1)} %add_add_fusion.1.first_ref), channel_id=1, source_target_pairs={{0,8},{8,0},{1,9},{9,1},{2,10},{10,2},{3,11},{11,3},{4,12},{12,4},... | collective-permute-start | bytes 1179656 | tf_op jit(solution)/shard_map/ppermute | solution.py:42
  134.0 22.4 %copy-start.10 = (pred[128]{0:T(512)(128)(4,1)S(1)}, pred[128]{0:T(512)(128)(4,1)}, u32[]{:S(2)}) copy-start(pred[128]{0:T(512)(128)(4,1)} %get-tuple-element.112) | copy-start | bytes 388
  134.0 27.7 %all-to-all-start.2 = ((bf16[16,8,512]{2,1,0:T(8,128)(2,1)}), bf16[16,8,512]{2,1,0:T(8,128)(2,1)S(1)}, u32[]{:S(2)}, u32[]{:S(2)}) async-start(bf16[16,8,512]{2,1,0:T(8,128)(2,1)} %fusion), calls=%async_computation.2 | async-start | bytes 262144 | tf_op jit(solution)/shard_map/all_to_all | solution.py:388
  156.4 4.3 %collective-permute-start.13 = (f32[128,128]{1,0:T(8,128)S(1)}, f32[128,128]{1,0:T(8,128)S(1)}, u32[]{:S(2)}, u32[]{:S(2)}) collective-permute-start(f32[128,128]{1,0:T(8,128)S(1)} %fusion.25.own_ref), channel_id=1, source_target_pairs={{0,16},{16,0},{1,17},{17,1},{2,18},{18,2},{3,19},{19,3},{4,20},{20... | collective-permute-start | bytes 196616 | tf_op jit(solution)/shard_map/ppermute | solution.py:449
  161.7 9.4 %all-to-all-start.3 = ((bf16[8,32,512]{2,1,0:T(8,128)(2,1)}), bf16[8,32,512]{2,1,0:T(8,128)(2,1)S(1)}, u32[]{:S(2)}, u32[]{:S(2)}) async-start(bf16[8,32,512]{2,1,0:T(8,128)(2,1)} %bitcast.18), calls=%async_computation.3 | async-start | bytes 524288 | tf_op jit(solution)/shard_map/all_to_all | solution.py:454

commit v21 on v19

--- a/solution.py
+++ b/solution.py
@@ -404,17 +404,22 @@
     send(2, 0)
     if far_count == 2:
         send(0, 2)
-        base_product()
+        chain.last, got[1, 0], done["packet"] = lax.optimization_barrier((chain.last, got[1, 0], done["packet"]))
         send(1, 1)
-        chain.wait(got[0, 2], done["packet"], done["base_own"], done["base_other"])
+        chain.wait(got[0, 2])
         cold_shrink()
         cold_over_tp()
-        base_over_tp()
         send(1, 2)
+        got[2, 0] = after(got[2, 0], chain.last)
         send(2, 1)
-        chain.last, _, done["z_got"] = lax.optimization_barrier((chain.last, got[1, 2], done["z_got"]))
+        base_product()
+        names_here = ["z_got", "base_own", "base_other"]
+        arrived = lax.optimization_barrier((chain.last, got[1, 2], *[done[name] for name in names_here]))
+        chain.last = arrived[0]
+        done.update(zip(names_here, arrived[2:]))
         cold_expand()
         send(2, 2)
+        base_over_tp()
         cold_back()
     else:
         base_product()

time: 214 us -> 169 us (0.79)
  blocking collectives: 36.6 us -> 0 us
  waiting for transfers between devices: 92.7 us -> 62.3 us
  starting transfers between devices: 25.7 us -> 45 us
  local copies, waits for them, and re-layouts: 4.49 us -> 7.69 us
    all_to_all x1 -> x0, blocking collectives: 36.6 us -> none  [cold_tokens_out(): sent = lax.all_to_all(sent, DP, split_axis=0, concat_axis=0, tiled=True)]
    ppermute x12, waiting for transfers between devices: 84.7 us -> 55.4 us  [permute(): return lax.ppermute(self.hold(value), axis, pairs)]
    ppermute x12, starting transfers between devices: 10.7 us -> 23.4 us  [permute(): return lax.ppermute(self.hold(value), axis, pairs)]
    all_to_all x0 -> x1, starting transfers between devices: none -> 3.88 us  [cold_tokens_out(): sent = lax.all_to_all(sent, DP, split_axis=0, concat_axis=0, tiled=True)]
    unnamed x22 -> x24, local copies, waits for them, and re-layouts: 3.66 us -> 6.86 us
  transfers between devices with their start and end apart: 17 -> 18, of which waited for: 9 -> 10; matrix products, arithmetic and copies ran while one was open for 10% -> 16% of each run, Pallas kernels for 5% -> 10%
where the time goes in v21:
time: 169 us; the launch traced here: 168 us
  waiting for transfers between devices  62.3 us (37%)
  starting transfers between devices  45 us (27%)
  Pallas kernels  22.4 us (13%)
  other arithmetic  18.8 us (11%)
  matrix products  11.7 us (7%)
  local copies, waits for them, and re-layouts  7.69 us (5%)
    ppermute x12, waiting for transfers between devices, permute(): return lax.ppermute(self.hold(value), axis, pairs)  55.4 us
    ppermute x12, starting transfers between devices, permute(): return lax.ppermute(self.hold(value), axis, pairs)  23.4 us
    dot_general x8, matrix products, matmul(): return jnp.dot(a, b, preferred_element_type=jnp.float32)  11.4 us
    pallas_call x1, Pallas kernels, base_halves(): pl.pallas_call(kernel, grid_spec=pltpu.PrefetchScalarGridSpec(num_scalar_...  10.9 us
    unnamed x24, local copies, waits for them, and re-layouts  6.86 us
    pallas_call x1, Pallas kernels, pick_columns(): pl.pallas_call(kernel, grid_spec=pltpu.PrefetchScalarGridSpec(num_scalar_...  5.47 us
    all_to_all x1, starting transfers between devices, on_device(): lax.all_to_all(hot_out, GROUP, split_axis=0, concat_axis=0, tiled=True)  5.37 us
    all_to_all x1, starting transfers between devices, cold_back(): delta = lax.all_to_all(delta, DP, split_axis=0, concat_axis=0, tiled=True)  4.79 us
  transfers between devices with their start and end apart: 18, of which 10 were waited for; matrix products, arithmetic and copies ran while one was open for 16% of the time, Pallas kernels for 10%

profile of v21, /device:TPU:0, one launch (start us, length us, event | category | flops | bytes accessed | tf_op | source)
XLA Modules:
  0.0 168.2 jit_solution(10612965971293185789)
XLA Ops:
  3.3 2.2 %copy-done.1 = bf16[4,128,4096]{2,1,0:T(8,128)(2,1)S(1)} copy-done((bf16[4,128,4096]{2,1,0:T(8,128)(2,1)S(1)}, bf16[4,128,4096]{2,1,0:T(8,128)(2,1)}, u32[]{:S(2)}) %copy-start.1) | copy-done | bytes 4194328
  5.5 3.9 %shard_map.73 = (bf16[256,4096]{1,0:T(8,128)(2,1)}, bf16[128,4224]{1,0:T(8,128)(2,1)}) custom-call(s32[1,512]{1,0:T(1,128)S(1)} %bitcast.45, s32[1,512]{1,0:T(1,128)S(1)} %bitcast.43, s32[1,512]{1,0:T(1,128)S(1)} %fusion.33.tag_at, bf16[512,4096]{1,0:T(8,128)(2,1)S(1)} %bitcast.40), custom_call_target="tpu_custom_call" | custom-call | flops 1 | bytes 1 | tf_op jit(solution)/shard_map/pallas_call | solution.py:154
  9.4 5.4 %all-to-all-start = ((bf16[8,32,4096]{2,1,0:T(8,128)(2,1)}), bf16[8,32,4096]{2,1,0:T(8,128)(2,1)S(1)}, u32[]{:S(2)}, u32[]{:S(2)}) async-start(bf16[8,32,4096]{2,1,0:T(8,128)(2,1)} %bitcast.7), calls=%async_computation | async-start | bytes 4194304 | tf_op jit(solution)/shard_map/all_to_all | solution.py:297
  17.0 2.2 %copy-done = bf16[4096,512]{1,0:T(8,128)(2,1)S(1)} copy-done((bf16[4096,512]{1,0:T(8,128)(2,1)S(1)}, bf16[4096,512]{1,0:T(8,128)(2,1)}, u32[]{:S(2)}) %copy-start) | copy-done | bytes 4194328
  19.1 5.5 %shard_map.74 = (bf16[4608,512]{1,0:T(8,128)(2,1)S(1)}, bf16[1536,512]{1,0:T(8,128)(2,1)S(1)}, bf16[3072,512]{1,0:T(8,128)(2,1)}) custom-call(s32[4]{0:T(128)S(1)} %convert_element_type.18.mine_held, s32[4]{0:T(128)S(1)} %convert_element_type.19.other_held, s32[1,512]{1,0:T(1,128)S(1)} %bitcast.48, s32[1,512]{1,0:T(1,128)S(1)} %bitcast.47, ...), custom_call_target="tpu_custom_call" | custom-call | flops 1 | bytes 1 | tf_op jit(solution)/shard_map/pallas_call | solution.py:102
  25.1 7.4 %collective-permute-done = bf16[1536,512]{1,0:T(8,128)(2,1)S(1)} collective-permute-done((bf16[1536,512]{1,0:T(8,128)(2,1)S(1)}, bf16[1536,512]{1,0:T(8,128)(2,1)S(1)}, u32[]{:S(2)}, u32[]{:S(2)}) %collective-permute-start) | collective-permute-done | bytes 1572896 | tf_op jit(solution)/shard_map/ppermute | solution.py:42
  32.6 1.0 copy-done.7
  33.7 8.2 %collective-permute-start.1 = (bf16[1536,256]{1,0:T(8,128)(2,1)S(1)}, bf16[1536,256]{1,0:T(8,128)(2,1)}, u32[]{:S(2)}, u32[]{:S(2)}) collective-permute-start(bf16[1536,256]{1,0:T(8,128)(2,1)S(1)} %slice_add_fusion), channel_id=1, source_target_pairs={{0,2},{2,0},{1,3},{3,1},{4,6},{6,4},{5,7},{7,5},{8,10},{10,8},{9,1... | collective-permute-start | bytes 2359304 | tf_op jit(solution)/shard_map/ppermute | solution.py:42
  42.4 1.4 copy-done.5
  43.8 3.9 %all-to-all-start.1 = ((bf16[16,8,4224]{2,1,0:T(8,128)(2,1)}), bf16[16,8,4224]{2,1,0:T(8,128)(2,1)S(1)}, u32[]{:S(2)}, u32[]{:S(2)}) async-start(bf16[16,8,4224]{2,1,0:T(8,128)(2,1)} %bitcast.8), calls=%async_computation.1 | async-start | bytes 2162688 | tf_op jit(solution)/shard_map/all_to_all | solution.py:352
  47.7 19.3 %collective-permute-done.1 = bf16[1536,256]{1,0:T(8,128)(2,1)} collective-permute-done((bf16[1536,256]{1,0:T(8,128)(2,1)S(1)}, bf16[1536,256]{1,0:T(8,128)(2,1)}, u32[]{:S(2)}, u32[]{:S(2)}) %collective-permute-start.1) | collective-permute-done | bytes 786464 | tf_op jit(solution)/shard_map/ppermute | solution.py:42
  67.0 2.4 %slice_add_fusion.2 = bf16[1536,256]{1,0:T(8,128)(2,1)} fusion(bf16[3072,512]{1,0:T(8,128)(2,1)} %collective-permute-done.2, bf16[4608,512]{1,0:T(8,128)(2,1)} %copy-done.3), kind=kLoop, calls=%fused_computation.12 | loop fusion | flops 393216 | bytes 2359296 | tf_op jit(solution)/shard_map/add | solution.py:327
  69.4 1.3 fusion.17
  70.7 2.8 %collective-permute-start.3 = (bf16[1536,128]{1,0:T(8,128)(2,1)S(1)}, bf16[1536,128]{1,0:T(8,128)(2,1)S(1)}, u32[]{:S(2)}, u32[]{:S(2)}) collective-permute-start(bf16[1536,128]{1,0:T(8,128)(2,1)S(1)} %fusion.17), channel_id=1, source_target_pairs={{0,4},{4,0},{1,5},{5,1},{2,6},{6,2},{3,7},{7,3},{8,12},{12,8},{9,1... | collective-permute-start | bytes 1179656 | tf_op jit(solution)/shard_map/ppermute | solution.py:42
  73.5 1.5 slice_add_fusion.1
  74.9 2.1 %collective-permute-start.6 = (bf16[1536,256]{1,0:T(8,128)(2,1)S(1)}, bf16[1536,256]{1,0:T(8,128)(2,1)}, u32[]{:S(2)}, u32[]{:S(2)}) collective-permute-start(bf16[1536,256]{1,0:T(8,128)(2,1)S(1)} %slice_add_fusion.1), channel_id=1, source_target_pairs={{0,2},{2,0},{1,3},{3,1},{4,6},{6,4},{5,7},{7,5},{8,10},{10,8},{9,1... | collective-permute-start | bytes 2359304 | tf_op jit(solution)/shard_map/ppermute | solution.py:42
  77.0 3.5 %collective-permute-done.3 = bf16[1536,128]{1,0:T(8,128)(2,1)S(1)} collective-permute-done((bf16[1536,128]{1,0:T(8,128)(2,1)S(1)}, bf16[1536,128]{1,0:T(8,128)(2,1)S(1)}, u32[]{:S(2)}, u32[]{:S(2)}) %collective-permute-start.3) | collective-permute-done | bytes 393248 | tf_op jit(solution)/shard_map/ppermute | solution.py:42
  80.5 1.4 fusion.19
  81.9 1.7 %collective-permute-start.5 = (bf16[1536,128]{1,0:T(8,128)(2,1)S(1)}, bf16[1536,128]{1,0:T(8,128)(2,1)}, u32[]{:S(2)}, u32[]{:S(2)}) collective-permute-start(bf16[1536,128]{1,0:T(8,128)(2,1)S(1)} %fusion.19), channel_id=1, source_target_pairs={{0,8},{8,0},{1,9},{9,1},{2,10},{10,2},{3,11},{11,3},{4,12},{12,4},... | collective-permute-start | bytes 1179656 | tf_op jit(solution)/shard_map/ppermute | solution.py:42
  83.6 10.7 %collective-permute-done.4 = bf16[1536,256]{1,0:T(8,128)(2,1)} collective-permute-done((bf16[1536,256]{1,0:T(8,128)(2,1)}, bf16[1536,256]{1,0:T(8,128)(2,1)}, u32[]{:S(2)}, u32[]{:S(2)}) %collective-permute-start.4) | collective-permute-done | bytes 786464 | tf_op jit(solution)/shard_map/ppermute | solution.py:42
  94.3 1.3 slice_add_fusion.6
  95.8 5.1 %collective-permute-done.5 = bf16[1536,128]{1,0:T(8,128)(2,1)} collective-permute-done((bf16[1536,128]{1,0:T(8,128)(2,1)S(1)}, bf16[1536,128]{1,0:T(8,128)(2,1)}, u32[]{:S(2)}, u32[]{:S(2)}) %collective-permute-start.5) | collective-permute-done | bytes 393248 | tf_op jit(solution)/shard_map/ppermute | solution.py:42
  101.0 3.0 %convolution_select_fusion = f32[128,512]{1,0:T(8,128)S(1)} fusion(bf16[4096,512]{1,0:T(8,128)(2,1)} %store_ref, bf16[128,4224]{1,0:T(8,128)(2,1)S(1)} %bitcast.50, s32[512]{0:T(512)S(1)} %fusion.27, s32[128]{0:T(128)S(1)} %convert_reduce_fusion.1), kind=kOutput, calls=%fused_computation | convolution fusion | flops 537001984 | bytes 5507584 | tf_op jit(solution)/shard_map/dot_general | solution.py:22
  104.0 1.6 collective-permute-start.9
  105.6 0.9 collective-permute-done.7
  106.6 1.4 add_add_fusion.2
  107.9 2.1 %collective-permute-start.8 = (bf16[1536,128]{1,0:T(8,128)(2,1)S(1)}, bf16[1536,128]{1,0:T(8,128)(2,1)S(1)}, u32[]{:S(2)}, u32[]{:S(2)}) collective-permute-start(bf16[1536,128]{1,0:T(8,128)(2,1)S(1)} %add_add_fusion.2), channel_id=1, source_target_pairs={{0,8},{8,0},{1,9},{9,1},{2,10},{10,2},{3,11},{11,3},{4,12},{12,4},... | collective-permute-start | bytes 1179656 | tf_op jit(solution)/shard_map/ppermute | solution.py:42
  110.1 1.3 slice_add_fusion.5
  111.4 2.5 %collective-permute-start.10 = (bf16[1536,128]{1,0:T(8,128)(2,1)S(1)}, bf16[1536,128]{1,0:T(8,128)(2,1)S(1)}, u32[]{:S(2)}, u32[]{:S(2)}) collective-permute-start(bf16[1536,128]{1,0:T(8,128)(2,1)S(1)} %slice_add_fusion.5), channel_id=1, source_target_pairs={{0,4},{4,0},{1,5},{5,1},{2,6},{6,2},{3,7},{7,3},{8,12},{12,8},{9,1... | collective-permute-start | bytes 1179656 | tf_op jit(solution)/shard_map/ppermute | solution.py:42
  113.9 1.4 fusion.10
  115.3 10.9 %shard_map.75 = (f32[512,512]{1,0:T(8,128)S(1)}, f32[512,512]{1,0:T(8,128)}) custom-call(s32[1]{0:T(128)} %bitcast.10.tp_at, bf16[512,4096]{1,0:T(8,128)(2,1)S(1)} %bitcast.41, bf16[4096,1024]{1,0:T(8,128)(2,1)} %weight_ref), custom_call_target="tpu_custom_call" | custom-call | flops 1 | bytes 1 | tf_op jit(solution)/shard_map/pallas_call | solution.py:198
  127.3 1.3 add_add_fusion.1.first_ref
  128.6 1.9 %collective-permute-start.12 = (bf16[1536,128]{1,0:T(8,128)(2,1)S(1)}, bf16[1536,128]{1,0:T(8,128)(2,1)S(1)}, u32[]{:S(2)}, u32[]{:S(2)}) collective-permute-start(bf16[1536,128]{1,0:T(8,128)(2,1)S(1)} %add_add_fusion.1.first_ref), channel_id=1, source_target_pairs={{0,8},{8,0},{1,9},{9,1},{2,10},{10,2},{3,11},{11,3},{4,12},{12,4},... | collective-permute-start | bytes 1179656 | tf_op jit(solution)/shard_map/ppermute | solution.py:42
  130.5 1.4 collective-permute-start.11
  132.0 0.9 fusion
  132.9 4.8 %all-to-all-start.2 = ((bf16[16,8,512]{2,1,0:T(8,128)(2,1)}), bf16[16,8,512]{2,1,0:T(8,128)(2,1)S(1)}, u32[]{:S(2)}, u32[]{:S(2)}) async-start(bf16[16,8,512]{2,1,0:T(8,128)(2,1)} %fusion), calls=%async_computation.2 | async-start | bytes 262144 | tf_op jit(solution)/shard_map/all_to_all | solution.py:388
  137.7 1.3 fusion.15
  139.0 1.6 fusion.6
  140.6 7.8 %collective-permute-done.12.second_ref = bf16[1536,128]{1,0:T(8,128)(2,1)S(1)} collective-permute-done((bf16[1536,128]{1,0:T(8,128)(2,1)S(1)}, bf16[1536,128]{1,0:T(8,128)(2,1)S(1)}, u32[]{:S(2)}, u32[]{:S(2)}) %collective-permute-start.12) | collective-permute-done | bytes 393248 | tf_op jit(solution)/shard_map/ppermute | solution.py:42
  148.4 1.3 fusion.13
  149.7 1.5 fusion.4
  151.3 1.5 collective-permute-start.13
  152.9 2.7 %collective-permute-done.13.got_ref = f32[128,128]{1,0:T(8,128)S(1)} collective-permute-done((f32[128,128]{1,0:T(8,128)S(1)}, f32[128,128]{1,0:T(8,128)S(1)}, u32[]{:S(2)}, u32[]{:S(2)}) %collective-permute-start.13) | collective-permute-done | bytes 65568 | tf_op jit(solution)/shard_map/ppermute | solution.py:449
  155.6 0.9 shard_map.76
  156.5 4.4 %all-to-all-start.3 = ((bf16[8,32,512]{2,1,0:T(8,128)(2,1)}), bf16[8,32,512]{2,1,0:T(8,128)(2,1)S(1)}, u32[]{:S(2)}, u32[]{:S(2)}) async-start(bf16[8,32,512]{2,1,0:T(8,128)(2,1)} %bitcast.18), calls=%async_computation.3 | async-start | bytes 524288 | tf_op jit(solution)/shard_map/all_to_all | solution.py:454
  161.3 1.5 add_add_fusion.partial_ref
  162.8 4.2 %all-to-all-done.3 = bf16[8,32,512]{2,1,0:T(8,128)(2,1)S(1)} async-done(((bf16[8,32,512]{2,1,0:T(8,128)(2,1)}), bf16[8,32,512]{2,1,0:T(8,128)(2,1)S(1)}, u32[]{:S(2)}, u32[]{:S(2)}) %all-to-all-start.3) | async-done | bytes 262176 | tf_op jit(solution)/shard_map/all_to_all | solution.py:454
  167.0 1.1 shard_map.77
  (78 shorter events, 8.4 us)
Async XLA Ops:
  3.3 2.2 %copy-start.1 = (bf16[4,128,4096]{2,1,0:T(8,128)(2,1)S(1)}, bf16[4,128,4096]{2,1,0:T(8,128)(2,1)}, u32[]{:S(2)}) copy-start(bf16[4,128,4096]{2,1,0:T(8,128)(2,1)} %param.7) | copy-start | bytes 12582916
  9.4 5.4 %copy-start.8 = (s32[128]{0:T(128)S(1)}, s32[128]{0:T(128)}, u32[]{:S(2)}) copy-start(s32[128]{0:T(128)} %param.11) | copy-start | bytes 1540
  9.4 5.5 %copy-start.9 = (s32[4,4]{1,0:T(4,128)S(1)}, s32[4,4]{1,0:T(4,128)}, u32[]{:S(2)}) copy-start(s32[4,4]{1,0:T(4,128)} %param.13) | copy-start | bytes 196
  9.4 7.5 %copy-start.4 = (bf16[512,512]{1,0:T(8,128)(2,1)S(1)}, bf16[512,512]{1,0:T(8,128)(2,1)}, u32[]{:S(2)}) copy-start(bf16[512,512]{1,0:T(8,128)(2,1)} %expand_ref.1) | copy-start | bytes 1572868
  9.4 33.0 %all-to-all-start = ((bf16[8,32,4096]{2,1,0:T(8,128)(2,1)}), bf16[8,32,4096]{2,1,0:T(8,128)(2,1)S(1)}, u32[]{:S(2)}, u32[]{:S(2)}) async-start(bf16[8,32,4096]{2,1,0:T(8,128)(2,1)} %bitcast.7), calls=%async_computation | async-start | bytes 4194304 | tf_op jit(solution)/shard_map/all_to_all | solution.py:297
  16.9 2.2 %copy-start = (bf16[4096,512]{1,0:T(8,128)(2,1)S(1)}, bf16[4096,512]{1,0:T(8,128)(2,1)}, u32[]{:S(2)}) copy-start(bf16[4096,512]{1,0:T(8,128)(2,1)} %store_ref) | copy-start | bytes 12582916
  24.6 7.9 %copy-start.3 = (bf16[4608,512]{1,0:T(8,128)(2,1)}, bf16[4608,512]{1,0:T(8,128)(2,1)S(1)}, u32[]{:S(2)}) copy-start(bf16[4608,512]{1,0:T(8,128)(2,1)S(1)} %get-tuple-element.61) | copy-start | bytes 14155780
  24.6 42.4 %collective-permute-start.2 = (bf16[3072,512]{1,0:T(8,128)(2,1)}, bf16[3072,512]{1,0:T(8,128)(2,1)}, u32[]{:S(2)}, u32[]{:S(2)}) collective-permute-start(bf16[3072,512]{1,0:T(8,128)(2,1)} %get-tuple-element.52), channel_id=1, source_target_pairs={{0,1},{1,0},{2,3},{3,2},{4,5},{5,4},{6,7},{7,6},{8,9},{9,8},{10,11... | collective-permute-start | bytes 9437192 | tf_op jit(solution)/shard_map/ppermute | solution.py:42
  25.1 7.4 %collective-permute-start = (bf16[1536,512]{1,0:T(8,128)(2,1)S(1)}, bf16[1536,512]{1,0:T(8,128)(2,1)S(1)}, u32[]{:S(2)}, u32[]{:S(2)}) collective-permute-start(bf16[1536,512]{1,0:T(8,128)(2,1)S(1)} %get-tuple-element.49), channel_id=1, source_target_pairs={{0,1},{1,0},{2,3},{3,2},{4,5},{5,4},{6,7},{7,6},{8,9},{9,8},{10,11... | collective-permute-start | bytes 4718600 | tf_op jit(solution)/shard_map/ppermute | solution.py:42
  32.5 1.2 copy-start.7
  33.7 33.3 %collective-permute-start.1 = (bf16[1536,256]{1,0:T(8,128)(2,1)S(1)}, bf16[1536,256]{1,0:T(8,128)(2,1)}, u32[]{:S(2)}, u32[]{:S(2)}) collective-permute-start(bf16[1536,256]{1,0:T(8,128)(2,1)S(1)} %slice_add_fusion), channel_id=1, source_target_pairs={{0,2},{2,0},{1,3},{3,1},{4,6},{6,4},{5,7},{7,5},{8,10},{10,8},{9,1... | collective-permute-start | bytes 2359304 | tf_op jit(solution)/shard_map/ppermute | solution.py:42
  42.4 1.4 copy-start.5
  43.8 39.8 %all-to-all-start.1 = ((bf16[16,8,4224]{2,1,0:T(8,128)(2,1)}), bf16[16,8,4224]{2,1,0:T(8,128)(2,1)S(1)}, u32[]{:S(2)}, u32[]{:S(2)}) async-start(bf16[16,8,4224]{2,1,0:T(8,128)(2,1)} %bitcast.8), calls=%async_computation.1 | async-start | bytes 2162688 | tf_op jit(solution)/shard_map/all_to_all | solution.py:352
  70.7 9.8 %collective-permute-start.3 = (bf16[1536,128]{1,0:T(8,128)(2,1)S(1)}, bf16[1536,128]{1,0:T(8,128)(2,1)S(1)}, u32[]{:S(2)}, u32[]{:S(2)}) collective-permute-start(bf16[1536,128]{1,0:T(8,128)(2,1)S(1)} %fusion.17), channel_id=1, source_target_pairs={{0,4},{4,0},{1,5},{5,1},{2,6},{6,2},{3,7},{7,3},{8,12},{12,8},{9,1... | collective-permute-start | bytes 1179656 | tf_op jit(solution)/shard_map/ppermute | solution.py:42
  73.5 20.8 %collective-permute-start.4 = (bf16[1536,256]{1,0:T(8,128)(2,1)}, bf16[1536,256]{1,0:T(8,128)(2,1)}, u32[]{:S(2)}, u32[]{:S(2)}) collective-permute-start(bf16[1536,256]{1,0:T(8,128)(2,1)} %slice_add_fusion.2), channel_id=1, source_target_pairs={{0,2},{2,0},{1,3},{3,1},{4,6},{6,4},{5,7},{7,5},{8,10},{10,8},{9,1... | collective-permute-start | bytes 2359304 | tf_op jit(solution)/shard_map/ppermute | solution.py:42
  74.9 35.1 %collective-permute-start.6 = (bf16[1536,256]{1,0:T(8,128)(2,1)S(1)}, bf16[1536,256]{1,0:T(8,128)(2,1)}, u32[]{:S(2)}, u32[]{:S(2)}) collective-permute-start(bf16[1536,256]{1,0:T(8,128)(2,1)S(1)} %slice_add_fusion.1), channel_id=1, source_target_pairs={{0,2},{2,0},{1,3},{3,1},{4,6},{6,4},{5,7},{7,5},{8,10},{10,8},{9,1... | collective-permute-start | bytes 2359304 | tf_op jit(solution)/shard_map/ppermute | solution.py:42
  81.9 19.1 %collective-permute-start.5 = (bf16[1536,128]{1,0:T(8,128)(2,1)S(1)}, bf16[1536,128]{1,0:T(8,128)(2,1)}, u32[]{:S(2)}, u32[]{:S(2)}) collective-permute-start(bf16[1536,128]{1,0:T(8,128)(2,1)S(1)} %fusion.19), channel_id=1, source_target_pairs={{0,8},{8,0},{1,9},{9,1},{2,10},{10,2},{3,11},{11,3},{4,12},{12,4},... | collective-permute-start | bytes 1179656 | tf_op jit(solution)/shard_map/ppermute | solution.py:42
  95.6 11.0 %collective-permute-start.7 = (bf16[1536,128]{1,0:T(8,128)(2,1)S(1)}, bf16[1536,128]{1,0:T(8,128)(2,1)S(1)}, u32[]{:S(2)}, u32[]{:S(2)}) collective-permute-start(bf16[1536,128]{1,0:T(8,128)(2,1)S(1)} %slice_add_fusion.6), channel_id=1, source_target_pairs={{0,4},{4,0},{1,5},{5,1},{2,6},{6,2},{3,7},{7,3},{8,12},{12,8},{9,1... | collective-permute-start | bytes 1179656 | tf_op jit(solution)/shard_map/ppermute | solution.py:42
  101.0 13.0 %copy-start.6 = (bf16[8,32,4096]{2,1,0:T(8,128)(2,1)S(1)}, bf16[8,32,4096]{2,1,0:T(8,128)(2,1)}, u32[]{:S(2)}) copy-start(bf16[8,32,4096]{2,1,0:T(8,128)(2,1)} %copy-done.5) | copy-start | bytes 6291460
  104.0 11.3 %copy-start.2 = (bf16[4,128,4096]{2,1,0:T(8,128)(2,1)S(1)}, bf16[4,128,4096]{2,1,0:T(8,128)(2,1)}, u32[]{:S(2)}) copy-start(bf16[4,128,4096]{2,1,0:T(8,128)(2,1)} %param.7) | copy-start | bytes 12582916
  104.0 22.6 %collective-permute-start.9 = (f32[128,512]{1,0:T(8,128)S(1)}, f32[128,512]{1,0:T(8,128)S(1)}, u32[]{:S(2)}, u32[]{:S(2)}) collective-permute-start(f32[128,512]{1,0:T(8,128)S(1)} %convolution_select_fusion), channel_id=1, source_target_pairs={{0,16},{16,0},{1,17},{17,1},{2,18},{18,2},{3,19},{19,3},{4,20},{20... | collective-permute-start | bytes 786440 | tf_op jit(solution)/shard_map/ppermute | solution.py:378
  107.9 18.7 %collective-permute-start.8 = (bf16[1536,128]{1,0:T(8,128)(2,1)S(1)}, bf16[1536,128]{1,0:T(8,128)(2,1)S(1)}, u32[]{:S(2)}, u32[]{:S(2)}) collective-permute-start(bf16[1536,128]{1,0:T(8,128)(2,1)S(1)} %add_add_fusion.2), channel_id=1, source_target_pairs={{0,8},{8,0},{1,9},{9,1},{2,10},{10,2},{3,11},{11,3},{4,12},{12,4},... | collective-permute-start | bytes 1179656 | tf_op jit(solution)/shard_map/ppermute | solution.py:42
  111.4 15.9 %collective-permute-start.10 = (bf16[1536,128]{1,0:T(8,128)(2,1)S(1)}, bf16[1536,128]{1,0:T(8,128)(2,1)S(1)}, u32[]{:S(2)}, u32[]{:S(2)}) collective-permute-start(bf16[1536,128]{1,0:T(8,128)(2,1)S(1)} %slice_add_fusion.5), channel_id=1, source_target_pairs={{0,4},{4,0},{1,5},{5,1},{2,6},{6,2},{3,7},{7,3},{8,12},{12,8},{9,1... | collective-permute-start | bytes 1179656 | tf_op jit(solution)/shard_map/ppermute | solution.py:42
  126.6 5.4 %copy-start.11 = (bf16[1536,128]{1,0:T(8,128)(2,1)}, bf16[1536,128]{1,0:T(8,128)(2,1)S(1)}, u32[]{:S(2)}) copy-start(bf16[1536,128]{1,0:T(8,128)(2,1)S(1)} %collective-permute-done.8) | copy-start | bytes 1179652
  128.6 19.7 %collective-permute-start.12 = (bf16[1536,128]{1,0:T(8,128)(2,1)S(1)}, bf16[1536,128]{1,0:T(8,128)(2,1)S(1)}, u32[]{:S(2)}, u32[]{:S(2)}) collective-permute-start(bf16[1536,128]{1,0:T(8,128)(2,1)S(1)} %add_add_fusion.1.first_ref), channel_id=1, source_target_pairs={{0,8},{8,0},{1,9},{9,1},{2,10},{10,2},{3,11},{11,3},{4,12},{12,4},... | collective-permute-start | bytes 1179656 | tf_op jit(solution)/shard_map/ppermute | solution.py:42
  130.5 30.8 %collective-permute-start.11 = (f32[512,512]{1,0:T(8,128)}, f32[512,512]{1,0:T(8,128)}, u32[]{:S(2)}, u32[]{:S(2)}) collective-permute-start(f32[512,512]{1,0:T(8,128)} %get-tuple-element.81), channel_id=1, source_target_pairs={{0,16},{16,0},{1,17},{17,1},{2,18},{18,2},{3,19},{19,3},{4,20},{20... | collective-permute-start | bytes 3145736 | tf_op jit(solution)/shard_map/ppermute | solution.py:42
  132.9 18.4 %copy-start.10 = (pred[128]{0:T(512)(128)(4,1)S(1)}, pred[128]{0:T(512)(128)(4,1)}, u32[]{:S(2)}) copy-start(pred[128]{0:T(512)(128)(4,1)} %get-tuple-element.112) | copy-start | bytes 388
  132.9 23.7 %all-to-all-start.2 = ((bf16[16,8,512]{2,1,0:T(8,128)(2,1)}), bf16[16,8,512]{2,1,0:T(8,128)(2,1)S(1)}, u32[]{:S(2)}, u32[]{:S(2)}) async-start(bf16[16,8,512]{2,1,0:T(8,128)(2,1)} %fusion), calls=%async_computation.2 | async-start | bytes 262144 | tf_op jit(solution)/shard_map/all_to_all | solution.py:388
  151.3 4.3 %collective-permute-start.13 = (f32[128,128]{1,0:T(8,128)S(1)}, f32[128,128]{1,0:T(8,128)S(1)}, u32[]{:S(2)}, u32[]{:S(2)}) collective-permute-start(f32[128,128]{1,0:T(8,128)S(1)} %fusion.25.own_ref), channel_id=1, source_target_pairs={{0,16},{16,0},{1,17},{17,1},{2,18},{18,2},{3,19},{19,3},{4,20},{20... | collective-permute-start | bytes 196616 | tf_op jit(solution)/shard_map/ppermute | solution.py:449
  156.5 10.5 %all-to-all-start.3 = ((bf16[8,32,512]{2,1,0:T(8,128)(2,1)}), bf16[8,32,512]{2,1,0:T(8,128)(2,1)S(1)}, u32[]{:S(2)}, u32[]{:S(2)}) async-start(bf16[8,32,512]{2,1,0:T(8,128)(2,1)} %bitcast.18), calls=%async_computation.3 | async-start | bytes 524288 | tf_op jit(solution)/shard_map/all_to_all | solution.py:454

commit v22 on v21

--- a/solution.py
+++ b/solution.py
@@ -407,11 +407,11 @@
         chain.last, got[1, 0], done["packet"] = lax.optimization_barrier((chain.last, got[1, 0], done["packet"]))
         send(1, 1)
         chain.wait(got[0, 2])
-        cold_shrink()
-        cold_over_tp()
         send(1, 2)
         got[2, 0] = after(got[2, 0], chain.last)
         send(2, 1)
+        cold_shrink()
+        cold_over_tp()
         base_product()
         names_here = ["z_got", "base_own", "base_other"]
         arrived = lax.optimization_barrier((chain.last, got[1, 2], *[done[name] for name in names_here]))

time: 169 us -> 171 us (1.012)
  waiting for transfers between devices: 62.3 us -> 74 us
  starting transfers between devices: 45 us -> 35.7 us
  Pallas kernels: 22.4 us -> 24.3 us
    ppermute x12, starting transfers between devices: 23.4 us -> 11.6 us  [permute(): return lax.ppermute(self.hold(value), axis, pairs)]
    ppermute x12, waiting for transfers between devices: 55.4 us -> 63.9 us  [permute(): return lax.ppermute(self.hold(value), axis, pairs)]
    all_to_all x1, starting transfers between devices: 4.79 us -> 8.24 us  [cold_back(): delta = lax.all_to_all(delta, DP, split_axis=0, concat_axis=0, tiled=True)]
    all_to_all x1, waiting for transfers between devices: 0.01 us -> 2.44 us  [on_device(): lax.all_to_all(hot_out, GROUP, split_axis=0, concat_axis=0, tiled=True)]
    pallas_call x1, Pallas kernels: 5.47 us -> 7.39 us  [pick_columns(): pl.pallas_call(kernel, grid_spec=pltpu.PrefetchScalarGridSpec(num_scalar_...]
    unnamed x24 -> x22, local copies, waits for them, and re-layouts: 6.86 us -> 5.8 us
  transfers between devices with their start and end apart: 18 -> 18, of which waited for: 10 -> 11; matrix products, arithmetic and copies ran while one was open for 16% -> 14% of each run, Pallas kernels for 10% -> 11%
where the time goes in v22:
time: 171 us; the launch traced here: 170 us
  waiting for transfers between devices  74 us (43%)
  starting transfers between devices  35.7 us (21%)
  Pallas kernels  24.3 us (14%)
  other arithmetic  18.5 us (11%)
  matrix products  10.7 us (6%)
  local copies, waits for them, and re-layouts  6.63 us (4%)
    ppermute x12, waiting for transfers between devices, permute(): return lax.ppermute(self.hold(value), axis, pairs)  63.9 us
    ppermute x12, starting transfers between devices, permute(): return lax.ppermute(self.hold(value), axis, pairs)  11.6 us
    pallas_call x1, Pallas kernels, base_halves(): pl.pallas_call(kernel, grid_spec=pltpu.PrefetchScalarGridSpec(num_scalar_...  10.9 us
    dot_general x8, matrix products, matmul(): return jnp.dot(a, b, preferred_element_type=jnp.float32)  10.4 us
    all_to_all x1, starting transfers between devices, cold_back(): delta = lax.all_to_all(delta, DP, split_axis=0, concat_axis=0, tiled=True)  8.24 us
    pallas_call x1, Pallas kernels, pick_columns(): pl.pallas_call(kernel, grid_spec=pltpu.PrefetchScalarGridSpec(num_scalar_...  7.39 us
    unnamed x22, local copies, waits for them, and re-layouts  5.8 us
    all_to_all x1, starting transfers between devices, on_device(): lax.all_to_all(hot_out, GROUP, split_axis=0, concat_axis=0, tiled=True)  5.37 us
  transfers between devices with their start and end apart: 18, of which 11 were waited for; matrix products, arithmetic and copies ran while one was open for 14% of the time, Pallas kernels for 11%

profile of v22, /device:TPU:0, one launch (start us, length us, event | category | flops | bytes accessed | tf_op | source)
XLA Modules:
  0.0 170.2 jit_solution(3096392725231711138)
XLA Ops:
  0.0 0.7 broadcast_add_fusion
  0.7 0.9 select_reduce_fusion
  1.6 0.7 select_select_fusion
  2.6 0.8 add_select_fusion.5
  3.3 2.2 %copy-done.1 = bf16[4,128,4096]{2,1,0:T(8,128)(2,1)S(1)} copy-done((bf16[4,128,4096]{2,1,0:T(8,128)(2,1)S(1)}, bf16[4,128,4096]{2,1,0:T(8,128)(2,1)}, u32[]{:S(2)}) %copy-start.1) | copy-done | bytes 4194328
  5.5 3.9 %shard_map.73 = (bf16[256,4096]{1,0:T(8,128)(2,1)}, bf16[128,4224]{1,0:T(8,128)(2,1)}) custom-call(s32[1,512]{1,0:T(1,128)S(1)} %bitcast.45, s32[1,512]{1,0:T(1,128)S(1)} %bitcast.43, s32[1,512]{1,0:T(1,128)S(1)} %fusion.33.tag_at, bf16[512,4096]{1,0:T(8,128)(2,1)S(1)} %bitcast.40), custom_call_target="tpu_custom_call" | custom-call | flops 1 | bytes 1 | tf_op jit(solution)/shard_map/pallas_call | solution.py:154
  9.5 5.4 %all-to-all-start = ((bf16[8,32,4096]{2,1,0:T(8,128)(2,1)}), bf16[8,32,4096]{2,1,0:T(8,128)(2,1)S(1)}, u32[]{:S(2)}, u32[]{:S(2)}) async-start(bf16[8,32,4096]{2,1,0:T(8,128)(2,1)} %bitcast.7), calls=%async_computation | async-start | bytes 4194304 | tf_op jit(solution)/shard_map/all_to_all | solution.py:297
  17.0 2.2 %copy-done = bf16[4096,512]{1,0:T(8,128)(2,1)S(1)} copy-done((bf16[4096,512]{1,0:T(8,128)(2,1)S(1)}, bf16[4096,512]{1,0:T(8,128)(2,1)}, u32[]{:S(2)}) %copy-start) | copy-done | bytes 4194328
  19.2 7.4 %shard_map.74 = (bf16[4608,512]{1,0:T(8,128)(2,1)S(1)}, bf16[1536,512]{1,0:T(8,128)(2,1)S(1)}, bf16[3072,512]{1,0:T(8,128)(2,1)}) custom-call(s32[4]{0:T(128)S(1)} %convert_element_type.18.mine_held, s32[4]{0:T(128)S(1)} %convert_element_type.19.other_held, s32[1,512]{1,0:T(1,128)S(1)} %bitcast.48, s32[1,512]{1,0:T(1,128)S(1)} %bitcast.47, ...), custom_call_target="tpu_custom_call" | custom-call | flops 1 | bytes 1 | tf_op jit(solution)/shard_map/pallas_call | solution.py:102
  26.6 2.7 %collective-permute-start.2 = (bf16[3072,512]{1,0:T(8,128)(2,1)}, bf16[3072,512]{1,0:T(8,128)(2,1)}, u32[]{:S(2)}, u32[]{:S(2)}) collective-permute-start(bf16[3072,512]{1,0:T(8,128)(2,1)} %get-tuple-element.50), channel_id=1, source_target_pairs={{0,1},{1,0},{2,3},{3,2},{4,5},{5,4},{6,7},{7,6},{8,9},{9,8},{10,11... | collective-permute-start | bytes 9437192 | tf_op jit(solution)/shard_map/ppermute | solution.py:42
  29.2 7.4 %collective-permute-done = bf16[1536,512]{1,0:T(8,128)(2,1)S(1)} collective-permute-done((bf16[1536,512]{1,0:T(8,128)(2,1)S(1)}, bf16[1536,512]{1,0:T(8,128)(2,1)S(1)}, u32[]{:S(2)}, u32[]{:S(2)}) %collective-permute-start) | collective-permute-done | bytes 1572896 | tf_op jit(solution)/shard_map/ppermute | solution.py:42
  36.7 1.8 %collective-permute-start.1 = (bf16[1536,256]{1,0:T(8,128)(2,1)S(1)}, bf16[1536,256]{1,0:T(8,128)(2,1)}, u32[]{:S(2)}, u32[]{:S(2)}) collective-permute-start(bf16[1536,256]{1,0:T(8,128)(2,1)S(1)} %slice_add_fusion), channel_id=1, source_target_pairs={{0,2},{2,0},{1,3},{3,1},{4,6},{6,4},{5,7},{7,5},{8,10},{10,8},{9,1... | collective-permute-start | bytes 2359304 | tf_op jit(solution)/shard_map/ppermute | solution.py:42
  38.6 2.4 %all-to-all-done = bf16[8,32,4096]{2,1,0:T(8,128)(2,1)S(1)} async-done(((bf16[8,32,4096]{2,1,0:T(8,128)(2,1)}), bf16[8,32,4096]{2,1,0:T(8,128)(2,1)S(1)}, u32[]{:S(2)}, u32[]{:S(2)}) %all-to-all-start) | async-done | bytes 2097184 | tf_op jit(solution)/shard_map/all_to_all | solution.py:297
  41.0 1.4 copy-done.5
  42.4 4.9 %all-to-all-start.1 = ((bf16[16,8,4224]{2,1,0:T(8,128)(2,1)}), bf16[16,8,4224]{2,1,0:T(8,128)(2,1)S(1)}, u32[]{:S(2)}, u32[]{:S(2)}) async-start(bf16[16,8,4224]{2,1,0:T(8,128)(2,1)} %bitcast.8), calls=%async_computation.1 | async-start | bytes 2162688 | tf_op jit(solution)/shard_map/all_to_all | solution.py:352
  47.3 16.5 %collective-permute-done.1 = bf16[1536,256]{1,0:T(8,128)(2,1)} collective-permute-done((bf16[1536,256]{1,0:T(8,128)(2,1)S(1)}, bf16[1536,256]{1,0:T(8,128)(2,1)}, u32[]{:S(2)}, u32[]{:S(2)}) %collective-permute-start.1) | collective-permute-done | bytes 786464 | tf_op jit(solution)/shard_map/ppermute | solution.py:42
  63.7 2.4 %slice_add_fusion.2 = bf16[1536,256]{1,0:T(8,128)(2,1)} fusion(bf16[3072,512]{1,0:T(8,128)(2,1)} %collective-permute-done.2, bf16[4608,512]{1,0:T(8,128)(2,1)} %copy-done.3), kind=kLoop, calls=%fused_computation.12 | loop fusion | flops 393216 | bytes 2359296 | tf_op jit(solution)/shard_map/add | solution.py:327
  66.2 1.3 fusion.17
  68.1 1.5 slice_add_fusion.1
  69.5 10.6 %collective-permute-done.3 = bf16[1536,128]{1,0:T(8,128)(2,1)S(1)} collective-permute-done((bf16[1536,128]{1,0:T(8,128)(2,1)S(1)}, bf16[1536,128]{1,0:T(8,128)(2,1)S(1)}, u32[]{:S(2)}, u32[]{:S(2)}) %collective-permute-start.3) | collective-permute-done | bytes 393248 | tf_op jit(solution)/shard_map/ppermute | solution.py:42
  80.1 1.4 fusion.19
  81.5 6.7 %collective-permute-done.4 = bf16[1536,256]{1,0:T(8,128)(2,1)} collective-permute-done((bf16[1536,256]{1,0:T(8,128)(2,1)}, bf16[1536,256]{1,0:T(8,128)(2,1)}, u32[]{:S(2)}, u32[]{:S(2)}) %collective-permute-start.4) | collective-permute-done | bytes 786464 | tf_op jit(solution)/shard_map/ppermute | solution.py:42
  88.2 1.3 slice_add_fusion.6
  89.5 1.5 collective-permute-start.6
  91.3 2.7 %collective-permute-start.11 = (bf16[1536,128]{1,0:T(8,128)(2,1)S(1)}, bf16[1536,128]{1,0:T(8,128)(2,1)S(1)}, u32[]{:S(2)}, u32[]{:S(2)}) collective-permute-start(bf16[1536,128]{1,0:T(8,128)(2,1)S(1)} %fusion.19), channel_id=1, source_target_pairs={{0,8},{8,0},{1,9},{9,1},{2,10},{10,2},{3,11},{11,3},{4,12},{12,4},... | collective-permute-start | bytes 1179656 | tf_op jit(solution)/shard_map/ppermute | solution.py:42
  94.1 14.8 %collective-permute-done.6 = bf16[1536,128]{1,0:T(8,128)(2,1)} collective-permute-done((bf16[1536,128]{1,0:T(8,128)(2,1)S(1)}, bf16[1536,128]{1,0:T(8,128)(2,1)}, u32[]{:S(2)}, u32[]{:S(2)}) %collective-permute-start.6) | collective-permute-done | bytes 393248 | tf_op jit(solution)/shard_map/ppermute | solution.py:42
  109.0 1.4 add_add_fusion.2
  110.5 1.5 slice_add_fusion.5
  112.3 3.0 %convolution_select_fusion = f32[128,512]{1,0:T(8,128)S(1)} fusion(bf16[4096,512]{1,0:T(8,128)(2,1)} %store_ref, bf16[128,4224]{1,0:T(8,128)(2,1)S(1)} %bitcast.50, s32[512]{0:T(512)S(1)} %fusion.27, s32[128]{0:T(128)S(1)} %convert_reduce_fusion.1), kind=kOutput, calls=%fused_computation | convolution fusion | flops 537001984 | bytes 5507584 | tf_op jit(solution)/shard_map/dot_general | solution.py:22
  115.3 1.6 collective-permute-start.8
  117.3 10.9 %shard_map.75 = (f32[512,512]{1,0:T(8,128)S(1)}, f32[512,512]{1,0:T(8,128)}) custom-call(s32[1]{0:T(128)} %bitcast.10.tp_at, bf16[512,4096]{1,0:T(8,128)(2,1)S(1)} %bitcast.41, bf16[4096,1024]{1,0:T(8,128)(2,1)} %weight_ref), custom_call_target="tpu_custom_call" | custom-call | flops 1 | bytes 1 | tf_op jit(solution)/shard_map/pallas_call | solution.py:198
  128.7 1.6 collective-permute-done.9
  130.4 1.3 add_add_fusion.1.first_ref
  131.7 1.2 collective-permute-start.12
  133.4 0.9 fusion
  134.3 8.2 %all-to-all-start.2 = ((bf16[16,8,512]{2,1,0:T(8,128)(2,1)}), bf16[16,8,512]{2,1,0:T(8,128)(2,1)S(1)}, u32[]{:S(2)}, u32[]{:S(2)}) async-start(bf16[16,8,512]{2,1,0:T(8,128)(2,1)} %fusion), calls=%async_computation.2 | async-start | bytes 262144 | tf_op jit(solution)/shard_map/all_to_all | solution.py:388
  142.5 1.3 fusion.15
  143.8 1.6 fusion.6
  145.4 6.1 %collective-permute-done.12.second_ref = bf16[1536,128]{1,0:T(8,128)(2,1)S(1)} collective-permute-done((bf16[1536,128]{1,0:T(8,128)(2,1)S(1)}, bf16[1536,128]{1,0:T(8,128)(2,1)S(1)}, u32[]{:S(2)}, u32[]{:S(2)}) %collective-permute-start.12) | collective-permute-done | bytes 393248 | tf_op jit(solution)/shard_map/ppermute | solution.py:42
  151.5 1.3 fusion.13
  152.9 1.5 fusion.4
  154.4 0.6 collective-permute-start.13
  155.1 3.6 %collective-permute-done.13.got_ref = f32[128,128]{1,0:T(8,128)S(1)} collective-permute-done((f32[128,128]{1,0:T(8,128)S(1)}, f32[128,128]{1,0:T(8,128)S(1)}, u32[]{:S(2)}, u32[]{:S(2)}) %collective-permute-start.13) | collective-permute-done | bytes 65568 | tf_op jit(solution)/shard_map/ppermute | solution.py:449
  158.7 0.9 shard_map.76
  159.7 3.4 %all-to-all-start.3 = ((bf16[8,32,512]{2,1,0:T(8,128)(2,1)}), bf16[8,32,512]{2,1,0:T(8,128)(2,1)S(1)}, u32[]{:S(2)}, u32[]{:S(2)}) async-start(bf16[8,32,512]{2,1,0:T(8,128)(2,1)} %bitcast.18), calls=%async_computation.3 | async-start | bytes 524288 | tf_op jit(solution)/shard_map/all_to_all | solution.py:454
  163.5 1.5 add_add_fusion.partial_ref
  165.0 4.1 %all-to-all-done.3 = bf16[8,32,512]{2,1,0:T(8,128)(2,1)S(1)} async-done(((bf16[8,32,512]{2,1,0:T(8,128)(2,1)}), bf16[8,32,512]{2,1,0:T(8,128)(2,1)S(1)}, u32[]{:S(2)}, u32[]{:S(2)}) %all-to-all-start.3) | async-done | bytes 262176 | tf_op jit(solution)/shard_map/all_to_all | solution.py:454
  169.1 1.1 shard_map.77
  (76 shorter events, 5.7 us)
Async XLA Ops:
  3.3 2.2 %copy-start.1 = (bf16[4,128,4096]{2,1,0:T(8,128)(2,1)S(1)}, bf16[4,128,4096]{2,1,0:T(8,128)(2,1)}, u32[]{:S(2)}) copy-start(bf16[4,128,4096]{2,1,0:T(8,128)(2,1)} %param.7) | copy-start | bytes 12582916
  9.4 5.4 %copy-start.8 = (s32[128]{0:T(128)S(1)}, s32[128]{0:T(128)}, u32[]{:S(2)}) copy-start(s32[128]{0:T(128)} %param.11) | copy-start | bytes 1540
  9.4 5.5 %copy-start.9 = (s32[4,4]{1,0:T(4,128)S(1)}, s32[4,4]{1,0:T(4,128)}, u32[]{:S(2)}) copy-start(s32[4,4]{1,0:T(4,128)} %param.13) | copy-start | bytes 196
  9.4 7.5 %copy-start.4 = (bf16[512,512]{1,0:T(8,128)(2,1)S(1)}, bf16[512,512]{1,0:T(8,128)(2,1)}, u32[]{:S(2)}) copy-start(bf16[512,512]{1,0:T(8,128)(2,1)} %expand_ref.1) | copy-start | bytes 1572868
  9.5 31.5 %all-to-all-start = ((bf16[8,32,4096]{2,1,0:T(8,128)(2,1)}), bf16[8,32,4096]{2,1,0:T(8,128)(2,1)S(1)}, u32[]{:S(2)}, u32[]{:S(2)}) async-start(bf16[8,32,4096]{2,1,0:T(8,128)(2,1)} %bitcast.7), calls=%async_computation | async-start | bytes 4194304 | tf_op jit(solution)/shard_map/all_to_all | solution.py:297
  17.0 2.2 %copy-start = (bf16[4096,512]{1,0:T(8,128)(2,1)S(1)}, bf16[4096,512]{1,0:T(8,128)(2,1)}, u32[]{:S(2)}) copy-start(bf16[4096,512]{1,0:T(8,128)(2,1)} %store_ref) | copy-start | bytes 12582916
  26.6 10.1 %copy-start.3 = (bf16[4608,512]{1,0:T(8,128)(2,1)}, bf16[4608,512]{1,0:T(8,128)(2,1)S(1)}, u32[]{:S(2)}) copy-start(bf16[4608,512]{1,0:T(8,128)(2,1)S(1)} %get-tuple-element.59) | copy-start | bytes 14155780
  26.6 37.2 %collective-permute-start.2 = (bf16[3072,512]{1,0:T(8,128)(2,1)}, bf16[3072,512]{1,0:T(8,128)(2,1)}, u32[]{:S(2)}, u32[]{:S(2)}) collective-permute-start(bf16[3072,512]{1,0:T(8,128)(2,1)} %get-tuple-element.50), channel_id=1, source_target_pairs={{0,1},{1,0},{2,3},{3,2},{4,5},{5,4},{6,7},{7,6},{8,9},{9,8},{10,11... | collective-permute-start | bytes 9437192 | tf_op jit(solution)/shard_map/ppermute | solution.py:42
  29.2 7.4 %collective-permute-start = (bf16[1536,512]{1,0:T(8,128)(2,1)S(1)}, bf16[1536,512]{1,0:T(8,128)(2,1)S(1)}, u32[]{:S(2)}, u32[]{:S(2)}) collective-permute-start(bf16[1536,512]{1,0:T(8,128)(2,1)S(1)} %get-tuple-element.47), channel_id=1, source_target_pairs={{0,1},{1,0},{2,3},{3,2},{4,5},{5,4},{6,7},{7,6},{8,9},{9,8},{10,11... | collective-permute-start | bytes 4718600 | tf_op jit(solution)/shard_map/ppermute | solution.py:42
  36.6 1.9 %copy-start.7 = (bf16[1536,512]{1,0:T(8,128)(2,1)}, bf16[1536,512]{1,0:T(8,128)(2,1)S(1)}, u32[]{:S(2)}) copy-start(bf16[1536,512]{1,0:T(8,128)(2,1)S(1)} %collective-permute-done) | copy-start | bytes 4718596
  36.7 27.0 %collective-permute-start.1 = (bf16[1536,256]{1,0:T(8,128)(2,1)S(1)}, bf16[1536,256]{1,0:T(8,128)(2,1)}, u32[]{:S(2)}, u32[]{:S(2)}) collective-permute-start(bf16[1536,256]{1,0:T(8,128)(2,1)S(1)} %slice_add_fusion), channel_id=1, source_target_pairs={{0,2},{2,0},{1,3},{3,1},{4,6},{6,4},{5,7},{7,5},{8,10},{10,8},{9,1... | collective-permute-start | bytes 2359304 | tf_op jit(solution)/shard_map/ppermute | solution.py:42
  41.0 1.4 copy-start.5
  42.4 39.1 %all-to-all-start.1 = ((bf16[16,8,4224]{2,1,0:T(8,128)(2,1)}), bf16[16,8,4224]{2,1,0:T(8,128)(2,1)S(1)}, u32[]{:S(2)}, u32[]{:S(2)}) async-start(bf16[16,8,4224]{2,1,0:T(8,128)(2,1)} %bitcast.8), calls=%async_computation.1 | async-start | bytes 2162688 | tf_op jit(solution)/shard_map/all_to_all | solution.py:352
  67.5 12.6 %collective-permute-start.3 = (bf16[1536,128]{1,0:T(8,128)(2,1)S(1)}, bf16[1536,128]{1,0:T(8,128)(2,1)S(1)}, u32[]{:S(2)}, u32[]{:S(2)}) collective-permute-start(bf16[1536,128]{1,0:T(8,128)(2,1)S(1)} %fusion.17), channel_id=1, source_target_pairs={{0,4},{4,0},{1,5},{5,1},{2,6},{6,2},{3,7},{7,3},{8,12},{12,8},{9,1... | collective-permute-start | bytes 1179656 | tf_op jit(solution)/shard_map/ppermute | solution.py:42
  67.5 20.7 %collective-permute-start.4 = (bf16[1536,256]{1,0:T(8,128)(2,1)}, bf16[1536,256]{1,0:T(8,128)(2,1)}, u32[]{:S(2)}, u32[]{:S(2)}) collective-permute-start(bf16[1536,256]{1,0:T(8,128)(2,1)} %slice_add_fusion.2), channel_id=1, source_target_pairs={{0,2},{2,0},{1,3},{3,1},{4,6},{6,4},{5,7},{7,5},{8,10},{10,8},{9,1... | collective-permute-start | bytes 2359304 | tf_op jit(solution)/shard_map/ppermute | solution.py:42
  89.5 19.4 %collective-permute-start.6 = (bf16[1536,128]{1,0:T(8,128)(2,1)S(1)}, bf16[1536,128]{1,0:T(8,128)(2,1)}, u32[]{:S(2)}, u32[]{:S(2)}) collective-permute-start(bf16[1536,128]{1,0:T(8,128)(2,1)S(1)} %slice_add_fusion.6), channel_id=1, source_target_pairs={{0,4},{4,0},{1,5},{5,1},{2,6},{6,2},{3,7},{7,3},{8,12},{12,8},{9,1... | collective-permute-start | bytes 1179656 | tf_op jit(solution)/shard_map/ppermute | solution.py:42
  91.0 19.5 %collective-permute-start.5 = (bf16[1536,256]{1,0:T(8,128)(2,1)S(1)}, bf16[1536,256]{1,0:T(8,128)(2,1)}, u32[]{:S(2)}, u32[]{:S(2)}) collective-permute-start(bf16[1536,256]{1,0:T(8,128)(2,1)S(1)} %slice_add_fusion.1), channel_id=1, source_target_pairs={{0,2},{2,0},{1,3},{3,1},{4,6},{6,4},{5,7},{7,5},{8,10},{10,8},{9,1... | collective-permute-start | bytes 2359304 | tf_op jit(solution)/shard_map/ppermute | solution.py:42
  91.3 25.6 %collective-permute-start.11 = (bf16[1536,128]{1,0:T(8,128)(2,1)S(1)}, bf16[1536,128]{1,0:T(8,128)(2,1)S(1)}, u32[]{:S(2)}, u32[]{:S(2)}) collective-permute-start(bf16[1536,128]{1,0:T(8,128)(2,1)S(1)} %fusion.19), channel_id=1, source_target_pairs={{0,8},{8,0},{1,9},{9,1},{2,10},{10,2},{3,11},{11,3},{4,12},{12,4},... | collective-permute-start | bytes 1179656 | tf_op jit(solution)/shard_map/ppermute | solution.py:42
  110.4 18.3 %collective-permute-start.7 = (bf16[1536,128]{1,0:T(8,128)(2,1)S(1)}, bf16[1536,128]{1,0:T(8,128)(2,1)S(1)}, u32[]{:S(2)}, u32[]{:S(2)}) collective-permute-start(bf16[1536,128]{1,0:T(8,128)(2,1)S(1)} %add_add_fusion.2), channel_id=1, source_target_pairs={{0,8},{8,0},{1,9},{9,1},{2,10},{10,2},{3,11},{11,3},{4,12},{12,4},... | collective-permute-start | bytes 1179656 | tf_op jit(solution)/shard_map/ppermute | solution.py:42
  110.5 6.4 %copy-start.6 = (bf16[8,32,4096]{2,1,0:T(8,128)(2,1)S(1)}, bf16[8,32,4096]{2,1,0:T(8,128)(2,1)}, u32[]{:S(2)}) copy-start(bf16[8,32,4096]{2,1,0:T(8,128)(2,1)} %copy-done.5) | copy-start | bytes 6291460
  112.0 5.3 %copy-start.2 = (bf16[4,128,4096]{2,1,0:T(8,128)(2,1)S(1)}, bf16[4,128,4096]{2,1,0:T(8,128)(2,1)}, u32[]{:S(2)}) copy-start(bf16[4,128,4096]{2,1,0:T(8,128)(2,1)} %param.7) | copy-start | bytes 12582916
  112.0 18.4 %collective-permute-start.9 = (bf16[1536,128]{1,0:T(8,128)(2,1)S(1)}, bf16[1536,128]{1,0:T(8,128)(2,1)S(1)}, u32[]{:S(2)}, u32[]{:S(2)}) collective-permute-start(bf16[1536,128]{1,0:T(8,128)(2,1)S(1)} %slice_add_fusion.5), channel_id=1, source_target_pairs={{0,4},{4,0},{1,5},{5,1},{2,6},{6,2},{3,7},{7,3},{8,12},{12,8},{9,1... | collective-permute-start | bytes 1179656 | tf_op jit(solution)/shard_map/ppermute | solution.py:42
  115.3 13.3 %collective-permute-start.8 = (f32[128,512]{1,0:T(8,128)S(1)}, f32[128,512]{1,0:T(8,128)S(1)}, u32[]{:S(2)}, u32[]{:S(2)}) collective-permute-start(f32[128,512]{1,0:T(8,128)S(1)} %convolution_select_fusion), channel_id=1, source_target_pairs={{0,16},{16,0},{1,17},{17,1},{2,18},{18,2},{3,19},{19,3},{4,20},{20... | collective-permute-start | bytes 786440 | tf_op jit(solution)/shard_map/ppermute | solution.py:378
  128.7 2.9 %copy-start.10 = (bf16[1536,128]{1,0:T(8,128)(2,1)}, bf16[1536,128]{1,0:T(8,128)(2,1)S(1)}, u32[]{:S(2)}) copy-start(bf16[1536,128]{1,0:T(8,128)(2,1)S(1)} %collective-permute-done.7) | copy-start | bytes 1179652
  131.7 19.8 %collective-permute-start.12 = (bf16[1536,128]{1,0:T(8,128)(2,1)S(1)}, bf16[1536,128]{1,0:T(8,128)(2,1)S(1)}, u32[]{:S(2)}, u32[]{:S(2)}) collective-permute-start(bf16[1536,128]{1,0:T(8,128)(2,1)S(1)} %add_add_fusion.1.first_ref), channel_id=1, source_target_pairs={{0,8},{8,0},{1,9},{9,1},{2,10},{10,2},{3,11},{11,3},{4,12},{12,4},... | collective-permute-start | bytes 1179656 | tf_op jit(solution)/shard_map/ppermute | solution.py:42
  132.8 30.6 %collective-permute-start.10 = (f32[512,512]{1,0:T(8,128)}, f32[512,512]{1,0:T(8,128)}, u32[]{:S(2)}, u32[]{:S(2)}) collective-permute-start(f32[512,512]{1,0:T(8,128)} %get-tuple-element.77), channel_id=1, source_target_pairs={{0,16},{16,0},{1,17},{17,1},{2,18},{18,2},{3,19},{19,3},{4,20},{20... | collective-permute-start | bytes 3145736 | tf_op jit(solution)/shard_map/ppermute | solution.py:42
  134.3 25.4 %all-to-all-start.2 = ((bf16[16,8,512]{2,1,0:T(8,128)(2,1)}), bf16[16,8,512]{2,1,0:T(8,128)(2,1)S(1)}, u32[]{:S(2)}, u32[]{:S(2)}) async-start(bf16[16,8,512]{2,1,0:T(8,128)(2,1)} %fusion), calls=%async_computation.2 | async-start | bytes 262144 | tf_op jit(solution)/shard_map/all_to_all | solution.py:388
  154.4 4.3 %collective-permute-start.13 = (f32[128,128]{1,0:T(8,128)S(1)}, f32[128,128]{1,0:T(8,128)S(1)}, u32[]{:S(2)}, u32[]{:S(2)}) collective-permute-start(f32[128,128]{1,0:T(8,128)S(1)} %fusion.25.own_ref), channel_id=1, source_target_pairs={{0,16},{16,0},{1,17},{17,1},{2,18},{18,2},{3,19},{19,3},{4,20},{20... | collective-permute-start | bytes 196616 | tf_op jit(solution)/shard_map/ppermute | solution.py:449
  159.7 9.4 %all-to-all-start.3 = ((bf16[8,32,512]{2,1,0:T(8,128)(2,1)}), bf16[8,32,512]{2,1,0:T(8,128)(2,1)S(1)}, u32[]{:S(2)}, u32[]{:S(2)}) async-start(bf16[8,32,512]{2,1,0:T(8,128)(2,1)} %bitcast.18), calls=%async_computation.3 | async-start | bytes 524288 | tf_op jit(solution)/shard_map/all_to_all | solution.py:454
